TPU v7x, 128 devices: a whole 4x4x4 slice. The times are simulated.
128 devices in a mesh: aux: 16 (over y, z_hi, core), row: 8 (over x, z_lo).
Axes of the slice: x: 4, y: 4, z: 4 (z_hi: 2, z_lo: 2; z = z_hi * 2 + z_lo), core: 2. Of those that a mesh axis runs over, the one named last changes fastest.
Arguments:
- factors: bfloat16 [16, 768, 128, 128], P('aux', 'row'), may hold values from -0.15625 to 0.15625
- block_rows: int32 [16, 768], P('aux', 'row'), may hold values from 0 to 47, as said below
- block_cols: int32 [16, 768], P('aux', 'row'), may hold values from 0 to 47
- block_count: int32 [16, 8], P('aux', 'row'), may hold values from 24 to 96, as said below
- orbitals: bfloat16 [6144, 800], P(('aux', 'row')), may hold values from -6 to 6
- response: bfloat16 [6144, 800], P(('aux', 'row')), may hold values from -6 to 6
Outputs:
- response_fock: float32 [6144, 800], P('row')
Inputs may be any that keep to these rules, and one draw needn't show every extreme that they name: `block_rows`: slot s names a row shell block of its row group, from (s // 96) * 6 up to the next group's first; no (row block, column block) pair repeats within the 96 slots of one auxiliary function and row group. `block_count`: some auxiliary function and row group has all 96 slots live.
All inputs are finite; a program needn't handle non-finite values.
Results may differ from a plain program's by a relative error of at most 0.004.
Values may be sent and summed in bfloat16 or wider, within the bound.
No kernel may reach another device: no remote copies, remote signals or barrier semaphores. Data moves between devices by JAX's collectives and lax.ppermute only.
A program may use at most 128 MiB of HBM per device.

v0:
```python
import itertools

import jax
import jax.numpy as jnp
from jax import lax
from jax.experimental import pallas as pl
from jax.experimental.pallas import tpu as pltpu
from jax.sharding import PartitionSpec as P

Y, ZH, CORE, X, ZL = 4, 2, 2, 4, 2
AXES = ("aux", "row")
BLK = 128
ROW_BLOCKS = 6
ROWS = ROW_BLOCKS * BLK
GROUPS = 2 * ROW_BLOCKS
SLOTS = 96
NB = 6144
NOCC = 800
WIDE = 896
SHARD = WIDE // 8
OWN = 48
STEP = 4
UNROLL = 3
FLIGHT = 5
MAIN = 32
bf16, f32 = jnp.bfloat16, jnp.float32


def permutation(move):
    pairs = []
    for y, zh, c, x, zl in itertools.product(range(Y), range(ZH), range(CORE), range(X), range(ZL)):
        at = dict(y=y, z=zh * ZL + zl, c=c, x=x)
        to = move(dict(at))

        def flat(d):
            return (((d["y"] * ZH + d["z"] // ZL) * CORE + d["c"]) * X + d["x"]) * ZL + d["z"] % ZL

        pairs.append((flat(at), flat(to)))
    return pairs


def around(axes, by, mirror):
    def move(d):
        axis = axes[d["c"]]
        d[axis] = (d[axis] + (-by if mirror and d["c"] else by)) % 4
        return d

    return permutation(move)


def other_core(d):
    d["c"] = 1 - d["c"]
    return d


def other_low(d):
    d["z"] = d["z"] ^ 1
    return d


def other_high(d):
    d["z"] = d["z"] ^ 2
    return d


def send(array, pairs):
    return lax.ppermute(array, AXES, pairs)


def swap_cores(array):
    return send(array, permutation(other_core))


def swap_low(array):
    return send(array, permutation(other_low))


def swap_high(array):
    return send(array, permutation(other_high))


def slab_kernel(place, main, rest, out, sems):
    core, row = place[0], place[1]
    copies = []
    for x in range(X):
        a = jnp.where(core == 0, x, row // ZL)
        b = jnp.where(core == 0, row // ZL, x)
        copies.append(
            pltpu.make_async_copy(main.at[b, row % ZL, :, :, a], out.at[:, x, :, pl.ds(0, MAIN)], sems.at[2 * x])
        )
        copies.append(
            pltpu.make_async_copy(
                rest.at[row % ZL, :, :, a, b], out.at[:, x, :, pl.ds(MAIN, OWN - MAIN)], sems.at[2 * x + 1]
            )
        )
    for copy in copies:
        copy.start()
    for copy in copies:
        copy.wait()


def own_slab(place, main, rest):
    return pl.pallas_call(
        slab_kernel,
        out_shape=jax.ShapeDtypeStruct((CORE, X, ZL, OWN, WIDE), bf16),
        in_specs=[pl.BlockSpec(memory_space=pltpu.SMEM)] + [pl.BlockSpec(memory_space=pl.ANY)] * 2,
        out_specs=pl.BlockSpec(memory_space=pltpu.VMEM),
        scratch_shapes=[pltpu.SemaphoreType.DMA((2 * X,))],
        compiler_params=pltpu.CompilerParams(vmem_limit_bytes=4 * 1024 * 1024),
        name="slab",
    )(place, main, rest)


def multiply_kernel(place, meta, own_blocks, other_blocks, main, rest, out, blocks, held, total, order, counts, steps, sems):
    core = place[0]
    copies = [
        pltpu.make_async_copy(own_blocks, blocks.at[pl.ds(0, SLOTS)], sems.at[0]),
        pltpu.make_async_copy(other_blocks, blocks.at[pl.ds(SLOTS, SLOTS)], sems.at[1]),
    ]
    for a in range(4):
        for b in range(4):
            y, x = jnp.where(core == 0, b, a), jnp.where(core == 0, a, b)
            i = 2 + 2 * (4 * a + b)
            copies.append(
                pltpu.make_async_copy(
                    main.at[b, :, :, :, a], held.at[y, :, :, x, :, pl.ds(0, MAIN)], sems.at[i]
                )
            )
            copies.append(
                pltpu.make_async_copy(
                    rest.at[:, :, :, a, b], held.at[y, :, :, x, :, pl.ds(MAIN, OWN - MAIN)], sems.at[i + 1]
                )
            )
    for copy in copies:
        copy.start()
    blocks[2 * SLOTS] = jnp.zeros((BLK, BLK), bf16)

    def clear(i, carry):
        counts[i] = 0
        total[i] = jnp.zeros((BLK, WIDE), f32)
        return carry

    lax.fori_loop(0, GROUPS + 1, clear, 0)
    for q in range(2):

        def put(s, carry):
            group = q * ROW_BLOCKS + meta[q, s]
            n = counts[group]
            order[group, n] = s + q * SLOTS
            counts[group] = n + 1
            return carry

        lax.fori_loop(0, meta[q, 2 * SLOTS], put, 0)

    def list_group(group, base):
        n = counts[group]
        for i in range(STEP):
            order[group, n + i] = 2 * SLOTS
        many = (n + STEP - 1) // STEP

        def list_step(i, carry):
            steps[base + i, 0] = group
            for k in range(STEP):
                s = order[group, i * STEP + k]
                q = jnp.minimum(s // SLOTS, 1)
                steps[base + i, 1 + k] = s
                steps[base + i, 1 + STEP + k] = jnp.where(s < 2 * SLOTS, meta[q, SLOTS + s - q * SLOTS], 0)
            return carry

        lax.fori_loop(0, many, list_step, 0)
        return base + many

    many = lax.fori_loop(0, GROUPS, list_group, 0)
    for u in range(UNROLL - 1):
        steps[many + u, 0] = GROUPS
        for k in range(STEP):
            steps[many + u, 1 + k] = 2 * SLOTS
            steps[many + u, 1 + STEP + k] = 0
    for copy in copies:
        copy.wait()
    panels = held.reshape(NB, WIDE)

    def some(i, carry):
        products = []
        for u in range(UNROLL):
            left, right = [], []
            for k in range(STEP):
                left.append(blocks[steps[i * UNROLL + u, 1 + k]])
                column = steps[i * UNROLL + u, 1 + STEP + k]
                right.append(panels[pl.ds(pl.multiple_of(column * BLK, BLK), BLK), :])
            products.append(
                jnp.dot(jnp.concatenate(left, axis=1), jnp.concatenate(right, axis=0), preferred_element_type=f32)
            )
        for u in range(UNROLL):
            total[steps[i * UNROLL + u, 0]] += products[u]
        return carry

    lax.fori_loop(0, (many + UNROLL - 1) // UNROLL, some, 0)

    def finish(group, carry):
        q = group // ROW_BLOCKS
        start = pl.multiple_of((group - q * ROW_BLOCKS) * BLK, BLK)
        out[q, pl.ds(start, BLK), :] = total[group].astype(bf16)
        return carry

    lax.fori_loop(0, GROUPS, finish, 0)


def multiply(place, meta, own_blocks, other_blocks, main, rest):
    most = 2 * SLOTS // STEP + GROUPS + UNROLL
    return pl.pallas_call(
        multiply_kernel,
        out_shape=jax.ShapeDtypeStruct((2, ROWS, WIDE), bf16),
        in_specs=[pl.BlockSpec(memory_space=pltpu.SMEM)] * 2 + [pl.BlockSpec(memory_space=pl.ANY)] * 4,
        out_specs=pl.BlockSpec(memory_space=pltpu.VMEM),
        scratch_shapes=[
            pltpu.VMEM((2 * SLOTS + 1, BLK, BLK), bf16),
            pltpu.VMEM((Y, ZH, CORE, X, ZL, OWN, WIDE), bf16),
            pltpu.VMEM((GROUPS + 1, BLK, WIDE), f32),
            pltpu.SMEM((GROUPS, SLOTS + 2 * STEP), jnp.int32),
            pltpu.SMEM((GROUPS + 1,), jnp.int32),
            pltpu.SMEM((most, 1 + 2 * STEP), jnp.int32),
            pltpu.SemaphoreType.DMA((34,)),
        ],
        compiler_params=pltpu.CompilerParams(vmem_limit_bytes=30 * 1024 * 1024),
        cost_estimate=pl.CostEstimate(flops=2 * 96 * 2 * 128 * 128 * 896, bytes_accessed=2**24, transcendentals=0),
        name="multiply",
    )(place, meta, own_blocks, other_blocks, main, rest)


def cross_kernel(q, starts, place, half, slab, theirs, *refs):
    outs, used, product = refs[:-2], refs[-2], refs[-1]
    core, row = place[0], place[1]
    used[...] = jnp.where(core == 0, slab[...], theirs[...])
    product[...] = lax.dot_general(
        half[q], used[...], (((0,), (0,)), ((), ())), preferred_element_type=f32
    ).astype(bf16)
    value = jnp.sum(half[q].astype(f32) * theirs[...].astype(f32), keepdims=True)
    high = value.astype(bf16).astype(f32)
    middle = (value - high).astype(bf16).astype(f32)
    low = value - high - middle
    lane = lax.broadcasted_iota(jnp.int32, (16, WIDE), 1)
    line = lax.broadcasted_iota(jnp.int32, (16, WIDE), 0)
    coded = jnp.where(
        lane == 3 * row, high, jnp.where(lane == 3 * row + 1, middle, jnp.where(lane == 3 * row + 2, low, 0.0))
    )
    product[NOCC : NOCC + 16, :] = jnp.where(line == 0, coded, 0.0).astype(bf16)
    for out, start in zip(outs, starts):
        n = out.shape[0]
        out[...] = product[pl.ds(pl.multiple_of(place[start] * n, n), n), :]


def cross(q, starts, n, place, half, slab, theirs):
    def kernel(*refs):
        cross_kernel(q, starts, *refs)

    return pl.pallas_call(
        kernel,
        out_shape=[jax.ShapeDtypeStruct((n, WIDE), bf16)] * len(starts),
        in_specs=[pl.BlockSpec(memory_space=pltpu.SMEM)] + [pl.BlockSpec(memory_space=pltpu.VMEM)] * 3,
        out_specs=[pl.BlockSpec(memory_space=pltpu.VMEM)] * len(starts),
        scratch_shapes=[pltpu.VMEM((ROWS, WIDE), bf16), pltpu.VMEM((WIDE, WIDE), bf16)],
        compiler_params=pltpu.CompilerParams(vmem_limit_bytes=30 * 1024 * 1024),
        cost_estimate=pl.CostEstimate(flops=2 * 768 * 896 * 896, bytes_accessed=2**23, transcendentals=0),
        name="cross",
    )(place, half, slab, theirs)


def exchange_kernel(place, half, first, second, keep, give, turned):
    core = place[0]
    total = None
    for q, weight in enumerate((first, second)):
        line = lax.broadcasted_iota(jnp.int32, (16, WIDE), 0)
        codes = jnp.where(line < 2, weight[NOCC : NOCC + 16, :].astype(f32), 0.0)
        coulomb = jnp.sum(codes, keepdims=True) * (1.0 / NB)
        factor = jnp.where(core == 0, 2.0 * coulomb, 0.0)
        own = half[q]
        term = factor * own.astype(f32) - jnp.dot(own, weight[...], preferred_element_type=f32)
        total = term if total is None else total + term
    turned[...] = total.T
    n = WIDE // 2
    keep[...] = turned[pl.ds(pl.multiple_of(core * n, n), n), :]
    give[...] = turned[pl.ds(pl.multiple_of((1 - core) * n, n), n), :]


def exchange(place, half, first, second):
    return pl.pallas_call(
        exchange_kernel,
        out_shape=[jax.ShapeDtypeStruct((WIDE // 2, ROWS), f32)] * 2,
        in_specs=[pl.BlockSpec(memory_space=pltpu.SMEM)] + [pl.BlockSpec(memory_space=pltpu.VMEM)] * 3,
        out_specs=[pl.BlockSpec(memory_space=pltpu.VMEM)] * 2,
        scratch_shapes=[pltpu.VMEM((WIDE, ROWS), f32)],
        compiler_params=pltpu.CompilerParams(vmem_limit_bytes=36 * 1024 * 1024),
        cost_estimate=pl.CostEstimate(flops=4 * 768 * 896 * 896, bytes_accessed=2**23, transcendentals=0),
        name="exchange",
    )(place, half, first, second)


def local(factors, block_rows, block_cols, block_count, orbitals, response):
    aux, row = lax.axis_index("aux"), lax.axis_index("row")
    y, zh, c = aux // (ZH * CORE), (aux // CORE) % ZH, aux % CORE
    x, zl = row // ZL, row % ZL
    z = zh * ZL + zl
    sign = 1 - 2 * c
    first = c == 0

    def choose(a, b):
        return jnp.where(first, a, b)

    flying = []

    def send_next(array, pairs):
        if len(flying) >= FLIGHT:
            array, _ = lax.optimization_barrier((array, flying[-FLIGHT]))
        got = send(array, pairs)
        flying.append(got)
        return got

    def put(into, array, **at):
        index = [jnp.int32(0)] * into.ndim
        for dim, i in at.items():
            index[int(dim[1:])] = i
        return lax.dynamic_update_slice(into, array, index)

    lists = jnp.concatenate([block_rows % ROW_BLOCKS, block_cols, jnp.broadcast_to(block_count, (1, SLOTS))])
    tail = jnp.pad(lists.astype(bf16), ((0, OWN - 3), (0, 0)))
    got = send_next(
        jnp.concatenate([choose(response, orbitals), tail], axis=1), permutation(other_core)
    )
    own_blocks = factors[0]
    other_blocks = send_next(own_blocks, permutation(other_core))
    other_lists = got[:3, NOCC:].astype(jnp.int32)
    meta = jnp.stack([jnp.concatenate([a[0], a[1], a[2, :64]]) for a in (lists, other_lists)])
    place = jnp.stack(
        [c, row, x, (x + sign) % 4, (x - sign) % 4, (x + 2) % 4, zl, 1 - zl]
    ).astype(jnp.int32)
    keep = jnp.pad(choose(orbitals, response), ((0, 0), (0, WIDE - NOCC)))
    got = jnp.where(jnp.arange(WIDE)[None] < NOCC, got, jnp.zeros((), bf16))
    both = jnp.stack([choose(keep, got), choose(got, keep)])

    one, two = ("x", "y"), ("y", "x")
    at_one, at_two = choose(x, y), choose(y, x)
    shape = (CORE, 4, OWN, WIDE)
    stage = put(jnp.zeros(shape, bf16), both[:, None], d1=at_one)
    ahead = send_next(both, around(one, 1, False))
    behind = send_next(both, around(one, -1, False))
    far = send_next(both, around(one, 2, False))
    stage = put(stage, ahead[:, None], d1=(at_one - 1) % 4)
    stage = put(stage, behind[:, None], d1=(at_one + 1) % 4)
    stage = put(stage, far[:, None], d1=(at_one + 2) % 4)

    main, rest = stage[:, :, :MAIN], stage[:, :, MAIN:]
    zz = ("z", "z")
    main_ahead = send_next(main, around(zz, 1, True))
    main_behind = send_next(main, around(zz, -1, True))
    rest_ahead = send_next(rest, around(two, 1, False))
    rest_behind = send_next(rest, around(two, -1, False))
    main_far = send_next(main_ahead, around(zz, 1, True))
    rest_far = send_next(rest, around(two, 2, False))

    def by_z(into, array, at):
        return put(into, array, d0=at // ZL, d2=at % ZL)

    into = jnp.zeros((ZH, CORE, ZL, 4, MAIN, WIDE), bf16)
    for array, at in (
        (main, z),
        (main_ahead, (z - sign) % 4),
        (main_behind, (z + sign) % 4),
        (main_far, (z + 2) % 4),
    ):
        into = by_z(into, array[None, :, None], at)
    main = into
    into = jnp.zeros((CORE, 4, 4, OWN - MAIN, WIDE), bf16)
    for array, at in (
        (rest, at_two),
        (rest_ahead, (at_two - 1) % 4),
        (rest_behind, (at_two + 1) % 4),
        (rest_far, (at_two + 2) % 4),
    ):
        into = put(into, array[:, :, None], d2=at)
    rest = into

    main_ahead = send_next(main, around(two, 1, False))
    rest_ahead = send_next(rest, around(zz, 1, True))
    main_behind = send_next(main, around(two, -1, False))
    rest_behind = send_next(rest, around(zz, -1, True))
    main_far = [
        send_next(main_ahead[:1], around(two, 1, False)),
        send_next(main_behind[1:], around(two, -1, False)),
    ]
    rest_far = send_next(rest_ahead, around(zz, 1, True))
    into = jnp.zeros((4, *main.shape), bf16)
    for array, at, part in (
        (main, at_two, 0),
        (main_ahead, (at_two - 1) % 4, 0),
        (main_behind, (at_two + 1) % 4, 0),
        (main_far[0], (at_two + 2) % 4, 0),
        (main_far[1], (at_two + 2) % 4, 1),
    ):
        into = put(into, array[None], d0=at, d1=jnp.int32(part))
    main = into
    into = jnp.zeros((ZH, CORE, ZL, 4, 4, OWN - MAIN, WIDE), bf16)
    for array, at in (
        (rest, z),
        (rest_ahead, (z - sign) % 4),
        (rest_behind, (z + sign) % 4),
        (rest_far, (z + 2) % 4),
    ):
        into = by_z(into, array[None, :, None], at)
    rest = into

    slab = own_slab(place, main, rest).reshape(ROWS, WIDE)
    theirs = swap_cores(slab)
    half = multiply(place, meta, own_blocks, other_blocks, main, rest)

    def add(*arrays):
        return sum(a.astype(f32) for a in arrays)

    def rows_of(array, k, n):
        return lax.dynamic_slice(array, (k * n, 0), (n, array.shape[1]))

    xx = ("x", "x")
    ahead, behind = around(xx, 1, True), around(xx, -1, True)
    opposite = around(xx, 2, True)
    mine, to_ahead, to_behind, to_far = cross(0, (2, 3, 4, 5), WIDE // 4, place, half, slab, theirs)
    mine = add(mine, send(to_ahead, ahead), send(to_behind, behind), send(to_far, opposite)).astype(bf16)
    half_mine, to_low = cross(1, (6, 7), WIDE // 2, place, half, slab, theirs)
    half_mine = add(half_mine, swap_low(to_low)).astype(bf16)
    shards = [
        add(rows_of(mine, zl, SHARD), swap_low(rows_of(mine, 1 - zl, SHARD))),
        add(
            rows_of(half_mine, x, SHARD),
            send(rows_of(half_mine, (x + sign) % 4, SHARD), ahead),
            send(rows_of(half_mine, (x - sign) % 4, SHARD), behind),
            send(rows_of(half_mine, (x + 2) % 4, SHARD), opposite),
        ),
    ]

    last = (x == X - 1) & (zl == ZL - 1)
    at = jnp.arange(SHARD, dtype=jnp.int32)[:, None] + (WIDE - SHARD)
    shards = [jnp.where(last & (at == NOCC), s, s * (1.0 / NB)).astype(bf16) for s in shards]
    code = [s[NOCC - (WIDE - SHARD)] for s in shards]
    other_shards = swap_cores(jnp.stack(shards))
    here = last & (at == NOCC + 1)
    by_x = jnp.where(here, code[1][None], other_shards[0])
    by_low = jnp.where(here, code[0][None], other_shards[1])

    def gather_x(array):
        n = array.shape[0]
        into = jnp.zeros((n * X, WIDE), bf16)
        for k, part in (
            (x, array),
            (x - sign, send(array, ahead)),
            (x + sign, send(array, behind)),
            (x + 2, send(array, opposite)),
        ):
            into = lax.dynamic_update_slice(into, part, ((k % X) * n, 0))
        return into

    def gather_low(array):
        n = array.shape[0]
        into = jnp.zeros((n * ZL, WIDE), bf16)
        into = lax.dynamic_update_slice(into, array, (zl * n, 0))
        return lax.dynamic_update_slice(into, swap_low(array), ((1 - zl) * n, 0))

    keep, give = exchange(place, half, gather_low(gather_x(by_low)), gather_x(gather_low(by_x)))

    yy = ("y", "y")
    ahead, behind, opposite = around(yy, 1, True), around(yy, -1, True), around(yy, 2, True)
    mine = keep + swap_cores(give)

    def quarter(k):
        return rows_of(mine, k % Y, SHARD)

    part = quarter(y) + add(
        send(quarter(y + sign).astype(bf16), ahead),
        send(quarter(y - sign).astype(bf16), behind),
        send(quarter(y + 2).astype(bf16), opposite),
    )
    part = (part + swap_high(part)).astype(bf16)
    into = jnp.zeros((WIDE // 2, ROWS), bf16)
    for k, array in (
        (y, part),
        (y - sign, send(part, ahead)),
        (y + sign, send(part, behind)),
        (y + 2, send(part, opposite)),
    ):
        into = lax.dynamic_update_slice(into, array, ((k % Y) * SHARD, 0))
    others = swap_cores(into)
    return jnp.concatenate([choose(into, others), choose(others, into)])[:NOCC].astype(f32).T


def solution(mesh):
    in_specs = (
        P("aux", "row", None, None),
        P("aux", "row"),
        P("aux", "row"),
        P("aux", "row"),
        P(("aux", "row"), None),
        P(("aux", "row"), None),
    )
    out_specs = P("row", None)
    return jax.shard_map(local, mesh=mesh, in_specs=in_specs, out_specs=out_specs, check_vma=False)
```

profile of v0, /device:TPU:1, one launch (start us, length us, event | category | flops | bytes accessed | tf_op | source)
XLA Modules:
  0.0 261.9 jit_solution(13541144647814270282)
XLA Ops:
  0.0 1.4 collective-permute-start.1
  4.6 2.2 collective-permute-done
  7.5 1.4 collective-permute-start.2
  8.9 1.9 collective-permute-start.3
  12.1 1.5 collective-permute-done.2
  15.1 1.8 collective-permute-done.4
  17.0 3.8 %collective-permute-start.5 = (bf16[2,4,32,896]{3,2,1,0:T(8,128)(2,1)S(1)}, bf16[2,4,32,896]{3,2,1,0:T(8,128)(2,1)S(1)}, u32[]{:S(2)}, u32[]{:S(2)}) collective-permute-start(bf16[2,4,32,896]{3,2,1,0:T(8,128)(2,1)S(1)} %slice.54), channel_id=1, source_target_pairs={{0,1},{1,16},{2,3},{3,18},{4,5},{5,20},{6,7},{7,22},{8,25},{9,8},{... | collective-permute-start | bytes 1376264 | tf_op jit(solution)/shard_map/ppermute | solution.py:67
  20.8 2.2 collective-permute-start.9
  23.0 1.4 broadcast_in_dim.151
  27.0 2.4 collective-permute-done.14
  33.5 3.8 %collective-permute-done.11 = bf16[2,4,16,896]{3,2,1,0:T(8,128)(2,1)S(1)} collective-permute-done((bf16[2,4,16,896]{3,2,1,0:T(8,128)(2,1)S(1)}, bf16[2,4,16,896]{3,2,1,0:T(8,128)(2,1)S(1)}, u32[]{:S(2)}, u32[]{:S(2)}) %collective-permute-start.11) | collective-permute-done | bytes 229408 | tf_op jit(solution)/shard_map/ppermute | solution.py:67
  38.0 7.6 %collective-permute-done.6 = bf16[2,4,32,896]{3,2,1,0:T(8,128)(2,1)S(1)} collective-permute-done((bf16[2,4,32,896]{3,2,1,0:T(8,128)(2,1)S(1)}, bf16[2,4,32,896]{3,2,1,0:T(8,128)(2,1)S(1)}, u32[]{:S(2)}, u32[]{:S(2)}) %collective-permute-start.6) | collective-permute-done | bytes 458784 | tf_op jit(solution)/shard_map/ppermute | solution.py:67
  47.5 2.4 collective-permute-start.10
  49.9 3.5 %collective-permute-done.15 = bf16[2,4,4,16,896]{4,3,2,1,0:T(8,128)(2,1)} collective-permute-done((bf16[2,4,4,16,896]{4,3,2,1,0:T(8,128)(2,1)}, bf16[2,4,4,16,896]{4,3,2,1,0:T(8,128)(2,1)}, u32[]{:S(2)}, u32[]{:S(2)}) %collective-permute-start.15) | collective-permute-done | bytes 917536 | tf_op jit(solution)/shard_map/ppermute | solution.py:67
  55.1 1.3 bitcast_dynamic-update-slice_fusion.5
  56.4 1.3 bitcast_dynamic-update-slice_fusion.4
  57.8 10.9 %collective-permute-done.16 = bf16[2,4,4,16,896]{4,3,2,1,0:T(8,128)(2,1)} collective-permute-done((bf16[2,4,4,16,896]{4,3,2,1,0:T(8,128)(2,1)}, bf16[2,4,4,16,896]{4,3,2,1,0:T(8,128)(2,1)}, u32[]{:S(2)}, u32[]{:S(2)}) %collective-permute-start.16) | collective-permute-done | bytes 917536 | tf_op jit(solution)/shard_map/ppermute | solution.py:67
  68.7 1.3 bitcast_dynamic-update-slice_fusion.3
  70.0 4.2 %collective-permute-done.17 = bf16[2,4,4,16,896]{4,3,2,1,0:T(8,128)(2,1)} collective-permute-done((bf16[2,4,4,16,896]{4,3,2,1,0:T(8,128)(2,1)}, bf16[2,4,4,16,896]{4,3,2,1,0:T(8,128)(2,1)}, u32[]{:S(2)}, u32[]{:S(2)}) %collective-permute-start.17) | collective-permute-done | bytes 917536 | tf_op jit(solution)/shard_map/ppermute | solution.py:67
  74.3 1.3 bitcast_dynamic-update-slice_fusion.6.rest
  78.2 2.7 %collective-permute-start.13 = (bf16[1,2,2,4,32,896]{5,4,3,2,1,0:T(8,128)(2,1)S(1)}, bf16[1,2,2,4,32,896]{5,4,3,2,1,0:T(8,128)(2,1)S(1)}, u32[]{:S(2)}, u32[]{:S(2)}) collective-permute-start(bf16[1,2,2,4,32,896]{5,4,3,2,1,0:T(8,128)(2,1)S(1)} %slice.57), channel_id=1, source_target_pairs={{0,96},{1,97},{2,98},{3,99},{4,100},{5,101},{6,102},{7,103},{8,14}... | collective-permute-start | bytes 2752520 | tf_op jit(solution)/shard_map/ppermute | solution.py:67
  81.9 1.8 bitcast_dynamic-update-slice_fusion.2
  83.7 1.8 bitcast_dynamic-update-slice_fusion.1
  85.5 1.8 bitcast_dynamic-update-slice_fusion
  87.4 3.3 %collective-permute-done.12 = bf16[1,2,2,4,32,896]{5,4,3,2,1,0:T(8,128)(2,1)S(1)} collective-permute-done((bf16[1,2,2,4,32,896]{5,4,3,2,1,0:T(8,128)(2,1)S(1)}, bf16[1,2,2,4,32,896]{5,4,3,2,1,0:T(8,128)(2,1)S(1)}, u32[]{:S(2)}, u32[]{:S(2)}) %collective-permute-start.12) | collective-permute-done | bytes 917536 | tf_op jit(solution)/shard_map/ppermute | solution.py:67
  92.6 3.7 %collective-permute-start.18 = (bf16[768,896]{1,0:T(8,128)(2,1)S(1)}, bf16[768,896]{1,0:T(8,128)(2,1)S(1)}, u32[]{:S(2)}, u32[]{:S(2)}) collective-permute-start(bf16[768,896]{1,0:T(8,128)(2,1)S(1)} %bitcast.110), channel_id=1, source_target_pairs={{0,8},{1,9},{2,10},{3,11},{4,12},{5,13},{6,14},{7,15},{8,0},{9,1},... | collective-permute-start | bytes 4128776 | tf_op jit(solution)/shard_map/ppermute | solution.py:67
  97.1 17.7 %multiply.1.refs_1_.half = bf16[2,768,896]{2,1,0:T(8,128)(2,1)S(1)} custom-call(s32[8]{0:T(128)S(1)} %stack.62.place.refs_0_, s32[2,256]{1,0:T(2,128)S(1)} %pad_add_fusion.meta, bf16[96,128,128]{2,1,0:T(8,128)(2,1)S(1)} %bitcast.114, bf16[96,128,128]{2,1,0:T(8,128)(2,1)S(1)} %copy-done.8, ...), custom_call_target="tpu_custom_call" | custom-call | flops 5637144576 | bytes 16777216 | tf_op jit(solution)/shard_map/multiply/pallas_call | solution.py:211
  115.4 3.2 %cross.3 = (bf16[448,896]{1,0:T(8,128)(2,1)S(1)}, bf16[448,896]{1,0:T(8,128)(2,1)}) custom-call(s32[8]{0:T(128)S(1)} %copy-done.3, bf16[2,768,896]{2,1,0:T(8,128)(2,1)S(1)} %multiply.1.refs_1_.half, bf16[768,896]{1,0:T(8,128)(2,1)S(1)} %bitcast.111, bf16[768,896]{1,0:T(8,128)(2,1)S(1)} %collective-permute-done.18.refs_3_), custom_call_target="tpu_custom_call" | custom-call | flops 1233125376 | bytes 8388608 | tf_op jit(solution)/shard_map/cross/pallas_call | solution.py:257
  118.6 3.3 %cross.2 = (bf16[224,896]{1,0:T(8,128)(2,1)S(1)}, bf16[224,896]{1,0:T(8,128)(2,1)}, bf16[224,896]{1,0:T(8,128)(2,1)}, bf16[224,896]{1,0:T(8,128)(2,1)}) custom-call(s32[8]{0:T(128)S(1)} %copy-done.4, bf16[2,768,896]{2,1,0:T(8,128)(2,1)S(1)} %multiply.1.refs_1_.half, bf16[768,896]{1,0:T(8,128)(2,1)S(1)} %bitcast.112, ...), custom_call_target="tpu_custom_call" | custom-call | flops 1233125376 | bytes 8388608 | tf_op jit(solution)/shard_map/cross/pallas_call | solution.py:257
  123.9 2.4 collective-permute-start.19
  126.3 8.2 %collective-permute-done.21 = bf16[224,896]{1,0:T(8,128)(2,1)} collective-permute-done((bf16[224,896]{1,0:T(8,128)(2,1)}, bf16[224,896]{1,0:T(8,128)(2,1)}, u32[]{:S(2)}, u32[]{:S(2)}) %collective-permute-start.21) | collective-permute-done | bytes 401440 | tf_op jit(solution)/shard_map/ppermute | solution.py:67
  134.6 9.7 %collective-permute-done.20 = bf16[224,896]{1,0:T(8,128)(2,1)} collective-permute-done((bf16[224,896]{1,0:T(8,128)(2,1)}, bf16[224,896]{1,0:T(8,128)(2,1)}, u32[]{:S(2)}, u32[]{:S(2)}) %collective-permute-start.20) | collective-permute-done | bytes 401440 | tf_op jit(solution)/shard_map/ppermute | solution.py:67
  144.3 2.3 add_convert_fusion.1
  146.6 1.6 constant_dynamic-slice_fusion.3
  148.2 1.5 collective-permute-start.22
  149.7 2.2 add_convert_fusion
  151.9 1.8 constant_dynamic-slice_fusion.2
  155.0 2.4 collective-permute-start.24
  157.4 3.8 %collective-permute-done.26 = bf16[112,896]{1,0:T(8,128)(2,1)S(1)} collective-permute-done((bf16[112,896]{1,0:T(8,128)(2,1)}, bf16[112,896]{1,0:T(8,128)(2,1)S(1)}, u32[]{:S(2)}, u32[]{:S(2)}) %collective-permute-start.26) | collective-permute-done | bytes 200736 | tf_op jit(solution)/shard_map/ppermute | solution.py:67
  161.2 4.6 %collective-permute-done.25 = bf16[112,896]{1,0:T(8,128)(2,1)S(1)} collective-permute-done((bf16[112,896]{1,0:T(8,128)(2,1)S(1)}, bf16[112,896]{1,0:T(8,128)(2,1)S(1)}, u32[]{:S(2)}, u32[]{:S(2)}) %collective-permute-start.25) | collective-permute-done | bytes 200736 | tf_op jit(solution)/shard_map/ppermute | solution.py:67
  165.9 1.5 fusion
  167.4 1.5 collective-permute-start.27
  168.9 1.4 collective-permute-done.27
  171.2 1.9 constant_dynamic-update-slice_fusion.9
  174.5 1.8 collective-permute-start.30
  176.4 1.8 collective-permute-done.28
  178.2 7.8 %collective-permute-done.29 = bf16[112,896]{1,0:T(8,128)(2,1)S(1)} collective-permute-done((bf16[112,896]{1,0:T(8,128)(2,1)S(1)}, bf16[112,896]{1,0:T(8,128)(2,1)S(1)}, u32[]{:S(2)}, u32[]{:S(2)}) %collective-permute-start.29) | collective-permute-done | bytes 200736 | tf_op jit(solution)/shard_map/ppermute | solution.py:67
  186.9 1.5 collective-permute-start.34
  190.9 6.1 %collective-permute-done.33 = bf16[224,896]{1,0:T(8,128)(2,1)} collective-permute-done((bf16[224,896]{1,0:T(8,128)(2,1)}, bf16[224,896]{1,0:T(8,128)(2,1)}, u32[]{:S(2)}, u32[]{:S(2)}) %collective-permute-start.33) | collective-permute-done | bytes 401440 | tf_op jit(solution)/shard_map/ppermute | solution.py:67
  199.3 8.1 %collective-permute-done.35 = bf16[224,896]{1,0:T(8,128)(2,1)S(1)} collective-permute-done((bf16[224,896]{1,0:T(8,128)(2,1)}, bf16[224,896]{1,0:T(8,128)(2,1)S(1)}, u32[]{:S(2)}, u32[]{:S(2)}) %collective-permute-start.35) | collective-permute-done | bytes 401440 | tf_op jit(solution)/shard_map/ppermute | solution.py:67
  208.7 5.4 %exchange.1 = (f32[448,768]{1,0:T(8,128)S(1)}, f32[448,768]{1,0:T(8,128)}) custom-call(s32[8]{0:T(128)S(1)} %copy-done.5, bf16[2,768,896]{2,1,0:T(8,128)(2,1)S(1)} %multiply.1.refs_1_.half, bf16[896,896]{1,0:T(8,128)(2,1)S(1)} %constant_dynamic-update-slice_fusion.10.first, bf16[896,896]{1,0:T(8,128)(2,1)S(1)} %constant_dynamic-update-slice_fusion.4.second), custom_call_target="tpu_custom_call" | custom-call | flops 2466250752 | bytes 8388608 | tf_op jit(solution)/shard_map/exchange/pallas_call | solution.py:287
  216.4 3.0 %collective-permute-done.36 = f32[448,768]{1,0:T(8,128)S(1)} collective-permute-done((f32[448,768]{1,0:T(8,128)}, f32[448,768]{1,0:T(8,128)S(1)}, u32[]{:S(2)}, u32[]{:S(2)}) %collective-permute-start.36) | collective-permute-done | bytes 1376288 | tf_op jit(solution)/shard_map/ppermute | solution.py:67
  219.4 1.5 add.408
  221.0 3.6 %collective-permute-start.39 = (bf16[112,768]{1,0:T(8,128)(2,1)S(1)}, bf16[112,768]{1,0:T(8,128)(2,1)S(1)}, u32[]{:S(2)}, u32[]{:S(2)}) collective-permute-start(bf16[112,768]{1,0:T(8,128)(2,1)S(1)} %get-tuple-element.58), channel_id=1, source_target_pairs={{0,64},{1,65},{2,66},{3,67},{4,68},{5,69},{6,70},{7,71},{8,72},{9,... | collective-permute-start | bytes 516104 | tf_op jit(solution)/shard_map/ppermute | solution.py:67
  225.8 1.4 collective-permute-start.37
  227.2 1.8 collective-permute-done.39
  229.0 3.3 %collective-permute-done.38 = bf16[112,768]{1,0:T(8,128)(2,1)S(1)} collective-permute-done((bf16[112,768]{1,0:T(8,128)(2,1)S(1)}, bf16[112,768]{1,0:T(8,128)(2,1)S(1)}, u32[]{:S(2)}, u32[]{:S(2)}) %collective-permute-start.38) | collective-permute-done | bytes 172064 | tf_op jit(solution)/shard_map/ppermute | solution.py:67
  232.3 1.4 collective-permute-done.37
  233.7 3.3 %collective-permute-start.40 = (f32[112,768]{1,0:T(8,128)S(1)}, f32[112,768]{1,0:T(8,128)S(1)}, u32[]{:S(2)}, u32[]{:S(2)}) collective-permute-start(f32[112,768]{1,0:T(8,128)S(1)} %add_add_fusion), channel_id=1, source_target_pairs={{0,16},{1,17},{2,18},{3,19},{4,20},{5,21},{6,22},{7,23},{8,24},{9,... | collective-permute-start | bytes 1032200 | tf_op jit(solution)/shard_map/ppermute | solution.py:67
  237.0 7.2 %collective-permute-done.40 = f32[112,768]{1,0:T(8,128)S(1)} collective-permute-done((f32[112,768]{1,0:T(8,128)S(1)}, f32[112,768]{1,0:T(8,128)S(1)}, u32[]{:S(2)}, u32[]{:S(2)}) %collective-permute-start.40) | collective-permute-done | bytes 344096 | tf_op jit(solution)/shard_map/ppermute | solution.py:67
  244.3 3.7 %collective-permute-start.41 = (bf16[112,768]{1,0:T(8,128)(2,1)S(1)}, bf16[112,768]{1,0:T(8,128)(2,1)S(1)}, u32[]{:S(2)}, u32[]{:S(2)}) collective-permute-start(bf16[112,768]{1,0:T(8,128)(2,1)S(1)} %get-tuple-element.48), channel_id=1, source_target_pairs={{0,32},{1,33},{2,34},{3,35},{4,36},{5,37},{6,38},{7,39},{8,104},{9... | collective-permute-start | bytes 516104 | tf_op jit(solution)/shard_map/ppermute | solution.py:67
  250.3 7.6 %collective-permute-done.42 = bf16[112,768]{1,0:T(8,128)(2,1)S(1)} collective-permute-done((bf16[112,768]{1,0:T(8,128)(2,1)S(1)}, bf16[112,768]{1,0:T(8,128)(2,1)S(1)}, u32[]{:S(2)}, u32[]{:S(2)}) %collective-permute-start.42) | collective-permute-done | bytes 172064 | tf_op jit(solution)/shard_map/ppermute | solution.py:67
  258.5 1.8 collective-permute-done.44
  260.3 1.6 convert_bitcast_fusion
  (134 shorter events, 43.3 us)
Async XLA Ops:
  0.0 32.1 %collective-permute-start.1 = (bf16[96,128,128]{2,1,0:T(8,128)(2,1)}, bf16[96,128,128]{2,1,0:T(8,128)(2,1)S(1)}, u32[]{:S(2)}, u32[]{:S(2)}) collective-permute-start(bf16[96,128,128]{2,1,0:T(8,128)(2,1)} %bitcast.113), channel_id=1, source_target_pairs={{0,8},{1,9},{2,10},{3,11},{4,12},{5,13},{6,14},{7,15},{8,0},{9,1},... | collective-permute-start | bytes 9437192 | tf_op jit(solution)/shard_map/ppermute | solution.py:67
  4.6 2.2 collective-permute-start
  6.8 0.6 copy-start.9
  7.5 6.1 %collective-permute-start.2 = (bf16[2,48,896]{2,1,0:T(8,128)(2,1)S(1)}, bf16[2,48,896]{2,1,0:T(8,128)(2,1)}, u32[]{:S(2)}, u32[]{:S(2)}) collective-permute-start(bf16[2,48,896]{2,1,0:T(8,128)(2,1)S(1)} %pad_maximum_fusion.2), channel_id=1, source_target_pairs={{0,2},{1,3},{2,4},{3,5},{4,6},{5,7},{6,0},{7,1},{8,40},{9,41},{10,... | collective-permute-start | bytes 516104 | tf_op jit(solution)/shard_map/ppermute | solution.py:67
  8.9 6.1 %collective-permute-start.3 = (bf16[2,48,896]{2,1,0:T(8,128)(2,1)S(1)}, bf16[2,48,896]{2,1,0:T(8,128)(2,1)S(1)}, u32[]{:S(2)}, u32[]{:S(2)}) collective-permute-start(bf16[2,48,896]{2,1,0:T(8,128)(2,1)S(1)} %pad_maximum_fusion.2), channel_id=1, source_target_pairs={{0,6},{1,7},{2,0},{3,1},{4,2},{5,3},{6,4},{7,5},{8,104},{9,105},{1... | collective-permute-start | bytes 516104 | tf_op jit(solution)/shard_map/ppermute | solution.py:67
  10.9 6.1 %collective-permute-start.4 = (bf16[2,48,896]{2,1,0:T(8,128)(2,1)S(1)}, bf16[2,48,896]{2,1,0:T(8,128)(2,1)S(1)}, u32[]{:S(2)}, u32[]{:S(2)}) collective-permute-start(bf16[2,48,896]{2,1,0:T(8,128)(2,1)S(1)} %pad_maximum_fusion.2), channel_id=1, source_target_pairs={{0,4},{1,5},{2,6},{3,7},{4,0},{5,1},{6,2},{7,3},{8,72},{9,73},{10,... | collective-permute-start | bytes 516104 | tf_op jit(solution)/shard_map/ppermute | solution.py:67
  17.0 13.8 %collective-permute-start.5 = (bf16[2,4,32,896]{3,2,1,0:T(8,128)(2,1)S(1)}, bf16[2,4,32,896]{3,2,1,0:T(8,128)(2,1)S(1)}, u32[]{:S(2)}, u32[]{:S(2)}) collective-permute-start(bf16[2,4,32,896]{3,2,1,0:T(8,128)(2,1)S(1)} %slice.54), channel_id=1, source_target_pairs={{0,1},{1,16},{2,3},{3,18},{4,5},{5,20},{6,7},{7,22},{8,25},{9,8},{... | collective-permute-start | bytes 1376264 | tf_op jit(solution)/shard_map/ppermute | solution.py:67
  20.8 9.3 %collective-permute-start.9 = (bf16[2,4,16,896]{3,2,1,0:T(8,128)(2,1)S(1)}, bf16[2,4,16,896]{3,2,1,0:T(8,128)(2,1)S(1)}, u32[]{:S(2)}, u32[]{:S(2)}) collective-permute-start(bf16[2,4,16,896]{3,2,1,0:T(8,128)(2,1)S(1)} %slice.55), channel_id=1, source_target_pairs={{0,96},{1,97},{2,98},{3,99},{4,100},{5,101},{6,102},{7,103},{8,14}... | collective-permute-start | bytes 688136 | tf_op jit(solution)/shard_map/ppermute | solution.py:67
  23.0 6.4 %collective-permute-start.14 = (bf16[2,4,16,896]{3,2,1,0:T(8,128)(2,1)S(1)}, bf16[2,4,16,896]{3,2,1,0:T(8,128)(2,1)S(1)}, u32[]{:S(2)}, u32[]{:S(2)}) collective-permute-start(bf16[2,4,16,896]{3,2,1,0:T(8,128)(2,1)S(1)} %slice.55), channel_id=1, source_target_pairs={{0,32},{1,33},{2,34},{3,35},{4,36},{5,37},{6,38},{7,39},{8,10},{9,... | collective-permute-start | bytes 688136 | tf_op jit(solution)/shard_map/ppermute | solution.py:67
  30.9 15.5 %collective-permute-start.7 = (bf16[2,4,32,896]{3,2,1,0:T(8,128)(2,1)S(1)}, bf16[2,4,32,896]{3,2,1,0:T(8,128)(2,1)S(1)}, u32[]{:S(2)}, u32[]{:S(2)}) collective-permute-start(bf16[2,4,32,896]{3,2,1,0:T(8,128)(2,1)S(1)} %collective-permute-done.5), channel_id=1, source_target_pairs={{0,1},{1,16},{2,3},{3,18},{4,5},{5,20},{6,7},{7,22},{8,25},{9,8},{... | collective-permute-start | bytes 1376264 | tf_op jit(solution)/shard_map/ppermute | solution.py:67
  30.9 6.4 %collective-permute-start.11 = (bf16[2,4,16,896]{3,2,1,0:T(8,128)(2,1)S(1)}, bf16[2,4,16,896]{3,2,1,0:T(8,128)(2,1)S(1)}, u32[]{:S(2)}, u32[]{:S(2)}) collective-permute-start(bf16[2,4,16,896]{3,2,1,0:T(8,128)(2,1)S(1)} %slice.55), channel_id=1, source_target_pairs={{0,64},{1,65},{2,66},{3,67},{4,68},{5,69},{6,70},{7,71},{8,12},{9,... | collective-permute-start | bytes 688136 | tf_op jit(solution)/shard_map/ppermute | solution.py:67
  32.1 22.4 %copy-start.7 = (bf16[96,128,128]{2,1,0:T(8,128)(2,1)}, bf16[96,128,128]{2,1,0:T(8,128)(2,1)S(1)}, u32[]{:S(2)}) copy-start(bf16[96,128,128]{2,1,0:T(8,128)(2,1)S(1)} %collective-permute-done.1.other_blocks) | copy-start | bytes 9437188
  32.1 13.5 %collective-permute-start.6 = (bf16[2,4,32,896]{3,2,1,0:T(8,128)(2,1)S(1)}, bf16[2,4,32,896]{3,2,1,0:T(8,128)(2,1)S(1)}, u32[]{:S(2)}, u32[]{:S(2)}) collective-permute-start(bf16[2,4,32,896]{3,2,1,0:T(8,128)(2,1)S(1)} %slice.54), channel_id=1, source_target_pairs={{0,17},{1,0},{2,19},{3,2},{4,21},{5,4},{6,23},{7,6},{8,9},{9,24},{... | collective-permute-start | bytes 1376264 | tf_op jit(solution)/shard_map/ppermute | solution.py:67
  38.0 15.4 %collective-permute-start.15 = (bf16[2,4,4,16,896]{4,3,2,1,0:T(8,128)(2,1)}, bf16[2,4,4,16,896]{4,3,2,1,0:T(8,128)(2,1)}, u32[]{:S(2)}, u32[]{:S(2)}) collective-permute-start(bf16[2,4,4,16,896]{4,3,2,1,0:T(8,128)(2,1)} %bitcast_dynamic-update-slice_fusion.16), channel_id=1, source_target_pairs={{0,1},{1,16},{2,3},{3,18},{4,5},{5,20},{6,7},{7,22},{8,25},{9,8},{... | collective-permute-start | bytes 2752520 | tf_op jit(solution)/shard_map/ppermute | solution.py:67
  47.2 28.4 %collective-permute-start.8 = (bf16[2,2,2,4,32,896]{5,4,3,2,1,0:T(8,128)(2,1)}, bf16[2,2,2,4,32,896]{5,4,3,2,1,0:T(8,128)(2,1)}, u32[]{:S(2)}, u32[]{:S(2)}) collective-permute-start(bf16[2,2,2,4,32,896]{5,4,3,2,1,0:T(8,128)(2,1)} %bitcast_dynamic-update-slice_fusion.9), channel_id=1, source_target_pairs={{0,32},{1,33},{2,34},{3,35},{4,36},{5,37},{6,38},{7,39},{8,10},{9,... | collective-permute-start | bytes 5505032 | tf_op jit(solution)/shard_map/ppermute | solution.py:67
  47.5 29.4 %collective-permute-start.10 = (bf16[2,2,2,4,32,896]{5,4,3,2,1,0:T(8,128)(2,1)}, bf16[2,2,2,4,32,896]{5,4,3,2,1,0:T(8,128)(2,1)}, u32[]{:S(2)}, u32[]{:S(2)}) collective-permute-start(bf16[2,2,2,4,32,896]{5,4,3,2,1,0:T(8,128)(2,1)} %bitcast_dynamic-update-slice_fusion.9), channel_id=1, source_target_pairs={{0,96},{1,97},{2,98},{3,99},{4,100},{5,101},{6,102},{7,103},{8,14}... | collective-permute-start | bytes 5505032 | tf_op jit(solution)/shard_map/ppermute | solution.py:67
  49.9 18.8 %collective-permute-start.16 = (bf16[2,4,4,16,896]{4,3,2,1,0:T(8,128)(2,1)}, bf16[2,4,4,16,896]{4,3,2,1,0:T(8,128)(2,1)}, u32[]{:S(2)}, u32[]{:S(2)}) collective-permute-start(bf16[2,4,4,16,896]{4,3,2,1,0:T(8,128)(2,1)} %bitcast_dynamic-update-slice_fusion.16), channel_id=1, source_target_pairs={{0,17},{1,0},{2,19},{3,2},{4,21},{5,4},{6,23},{7,6},{8,9},{9,24},{... | collective-permute-start | bytes 2752520 | tf_op jit(solution)/shard_map/ppermute | solution.py:67
  53.3 20.9 %collective-permute-start.17 = (bf16[2,4,4,16,896]{4,3,2,1,0:T(8,128)(2,1)}, bf16[2,4,4,16,896]{4,3,2,1,0:T(8,128)(2,1)}, u32[]{:S(2)}, u32[]{:S(2)}) collective-permute-start(bf16[2,4,4,16,896]{4,3,2,1,0:T(8,128)(2,1)} %collective-permute-done.15), channel_id=1, source_target_pairs={{0,1},{1,16},{2,3},{3,18},{4,5},{5,20},{6,7},{7,22},{8,25},{9,8},{... | collective-permute-start | bytes 2752520 | tf_op jit(solution)/shard_map/ppermute | solution.py:67
  54.6 42.4 %copy-start.2 = (s32[8]{0:T(128)}, s32[8]{0:T(128)S(1)}, u32[]{:S(2)}) copy-start(s32[8]{0:T(128)S(1)} %stack.62.place.refs_0_) | copy-start | bytes 100
  76.8 13.8 %collective-permute-start.12 = (bf16[1,2,2,4,32,896]{5,4,3,2,1,0:T(8,128)(2,1)S(1)}, bf16[1,2,2,4,32,896]{5,4,3,2,1,0:T(8,128)(2,1)S(1)}, u32[]{:S(2)}, u32[]{:S(2)}) collective-permute-start(bf16[1,2,2,4,32,896]{5,4,3,2,1,0:T(8,128)(2,1)S(1)} %slice.56), channel_id=1, source_target_pairs={{0,32},{1,33},{2,34},{3,35},{4,36},{5,37},{6,38},{7,39},{8,10},{9,... | collective-permute-start | bytes 2752520 | tf_op jit(solution)/shard_map/ppermute | solution.py:67
  78.2 13.1 %collective-permute-start.13 = (bf16[1,2,2,4,32,896]{5,4,3,2,1,0:T(8,128)(2,1)S(1)}, bf16[1,2,2,4,32,896]{5,4,3,2,1,0:T(8,128)(2,1)S(1)}, u32[]{:S(2)}, u32[]{:S(2)}) collective-permute-start(bf16[1,2,2,4,32,896]{5,4,3,2,1,0:T(8,128)(2,1)S(1)} %slice.57), channel_id=1, source_target_pairs={{0,96},{1,97},{2,98},{3,99},{4,100},{5,101},{6,102},{7,103},{8,14}... | collective-permute-start | bytes 2752520 | tf_op jit(solution)/shard_map/ppermute | solution.py:67
  91.4 5.5 %copy-start.10 = (s32[1,96]{1,0:T(1,128)S(1)}, s32[1,96]{1,0:T(1,128)}, u32[]{:S(2)}) copy-start(s32[1,96]{1,0:T(1,128)} %param.8) | copy-start | bytes 1156
  91.4 5.6 %copy-start.6 = (bf16[1,96,128,128]{3,2,1,0:T(8,128)(2,1)S(1)}, bf16[1,96,128,128]{3,2,1,0:T(8,128)(2,1)}, u32[]{:S(2)}) copy-start(bf16[1,96,128,128]{3,2,1,0:T(8,128)(2,1)} %param.6) | copy-start | bytes 9437188
  91.4 5.6 %copy-start.8 = (bf16[96,128,128]{2,1,0:T(8,128)(2,1)S(1)}, bf16[96,128,128]{2,1,0:T(8,128)(2,1)}, u32[]{:S(2)}) copy-start(bf16[96,128,128]{2,1,0:T(8,128)(2,1)} %copy-done.7) | copy-start | bytes 9437188
  92.6 22.2 %collective-permute-start.18 = (bf16[768,896]{1,0:T(8,128)(2,1)S(1)}, bf16[768,896]{1,0:T(8,128)(2,1)S(1)}, u32[]{:S(2)}, u32[]{:S(2)}) collective-permute-start(bf16[768,896]{1,0:T(8,128)(2,1)S(1)} %bitcast.110), channel_id=1, source_target_pairs={{0,8},{1,9},{2,10},{3,11},{4,12},{5,13},{6,14},{7,15},{8,0},{9,1},... | collective-permute-start | bytes 4128776 | tf_op jit(solution)/shard_map/ppermute | solution.py:67
  114.8 0.6 copy-start.3
  115.4 3.2 %copy-start.4 = (s32[8]{0:T(128)S(1)}, s32[8]{0:T(128)}, u32[]{:S(2)}) copy-start(s32[8]{0:T(128)} %copy-done.2) | copy-start | bytes 100
  118.6 31.1 %collective-permute-start.23 = (bf16[448,896]{1,0:T(8,128)(2,1)}, bf16[448,896]{1,0:T(8,128)(2,1)}, u32[]{:S(2)}, u32[]{:S(2)}) collective-permute-start(bf16[448,896]{1,0:T(8,128)(2,1)} %get-tuple-element.44), channel_id=1, source_target_pairs={{0,1},{1,0},{2,3},{3,2},{4,5},{5,4},{6,7},{7,6},{8,9},{9,8},{10,11... | collective-permute-start | bytes 2408456 | tf_op jit(solution)/shard_map/ppermute | solution.py:67
  121.9 0.8 copy-start.1
  122.6 11.9 %collective-permute-start.21 = (bf16[224,896]{1,0:T(8,128)(2,1)}, bf16[224,896]{1,0:T(8,128)(2,1)}, u32[]{:S(2)}, u32[]{:S(2)}) collective-permute-start(bf16[224,896]{1,0:T(8,128)(2,1)} %get-tuple-element.42), channel_id=1, source_target_pairs={{0,4},{1,5},{2,6},{3,7},{4,0},{5,1},{6,2},{7,3},{8,12},{9,13},{10,... | collective-permute-start | bytes 1204232 | tf_op jit(solution)/shard_map/ppermute | solution.py:67
  122.6 21.6 %collective-permute-start.20 = (bf16[224,896]{1,0:T(8,128)(2,1)}, bf16[224,896]{1,0:T(8,128)(2,1)}, u32[]{:S(2)}, u32[]{:S(2)}) collective-permute-start(bf16[224,896]{1,0:T(8,128)(2,1)} %get-tuple-element.41), channel_id=1, source_target_pairs={{0,6},{1,7},{2,0},{3,1},{4,2},{5,3},{6,4},{7,5},{8,10},{9,11},{10,... | collective-permute-start | bytes 1204232 | tf_op jit(solution)/shard_map/ppermute | solution.py:67
  123.9 20.3 %collective-permute-start.19 = (bf16[224,896]{1,0:T(8,128)(2,1)}, bf16[224,896]{1,0:T(8,128)(2,1)}, u32[]{:S(2)}, u32[]{:S(2)}) collective-permute-start(bf16[224,896]{1,0:T(8,128)(2,1)} %get-tuple-element.40), channel_id=1, source_target_pairs={{0,2},{1,3},{2,4},{3,5},{4,6},{5,7},{6,0},{7,1},{8,14},{9,15},{10,... | collective-permute-start | bytes 1204232 | tf_op jit(solution)/shard_map/ppermute | solution.py:67
  148.2 9.2 %collective-permute-start.22 = (bf16[112,896]{1,0:T(8,128)(2,1)}, bf16[112,896]{1,0:T(8,128)(2,1)}, u32[]{:S(2)}, u32[]{:S(2)}) collective-permute-start(bf16[112,896]{1,0:T(8,128)(2,1)} %constant_dynamic-slice_fusion.3), channel_id=1, source_target_pairs={{0,1},{1,0},{2,3},{3,2},{4,5},{5,4},{6,7},{7,6},{8,9},{9,8},{10,11... | collective-permute-start | bytes 602120 | tf_op jit(solution)/shard_map/ppermute | solution.py:67
  153.7 7.5 %collective-permute-start.26 = (bf16[112,896]{1,0:T(8,128)(2,1)}, bf16[112,896]{1,0:T(8,128)(2,1)S(1)}, u32[]{:S(2)}, u32[]{:S(2)}) collective-permute-start(bf16[112,896]{1,0:T(8,128)(2,1)} %get-tuple-element.61), channel_id=1, source_target_pairs={{0,4},{1,5},{2,6},{3,7},{4,0},{5,1},{6,2},{7,3},{8,12},{9,13},{10,... | collective-permute-start | bytes 602120 | tf_op jit(solution)/shard_map/ppermute | solution.py:67
  154.7 11.1 %collective-permute-start.25 = (bf16[112,896]{1,0:T(8,128)(2,1)S(1)}, bf16[112,896]{1,0:T(8,128)(2,1)S(1)}, u32[]{:S(2)}, u32[]{:S(2)}) collective-permute-start(bf16[112,896]{1,0:T(8,128)(2,1)S(1)} %get-tuple-element.62), channel_id=1, source_target_pairs={{0,6},{1,7},{2,0},{3,1},{4,2},{5,3},{6,4},{7,5},{8,10},{9,11},{10,... | collective-permute-start | bytes 602120 | tf_op jit(solution)/shard_map/ppermute | solution.py:67
  155.0 10.8 %collective-permute-start.24 = (bf16[112,896]{1,0:T(8,128)(2,1)S(1)}, bf16[112,896]{1,0:T(8,128)(2,1)}, u32[]{:S(2)}, u32[]{:S(2)}) collective-permute-start(bf16[112,896]{1,0:T(8,128)(2,1)S(1)} %get-tuple-element.60), channel_id=1, source_target_pairs={{0,2},{1,3},{2,4},{3,5},{4,6},{5,7},{6,0},{7,1},{8,14},{9,15},{10,... | collective-permute-start | bytes 602120 | tf_op jit(solution)/shard_map/ppermute | solution.py:67
  167.4 3.0 %collective-permute-start.27 = (bf16[2,112,896]{2,1,0:T(8,128)(2,1)S(1)}, bf16[2,112,896]{2,1,0:T(8,128)(2,1)}, u32[]{:S(2)}, u32[]{:S(2)}) collective-permute-start(bf16[2,112,896]{2,1,0:T(8,128)(2,1)S(1)} %pad_maximum_fusion.1), channel_id=1, source_target_pairs={{0,8},{1,9},{2,10},{3,11},{4,12},{5,13},{6,14},{7,15},{8,0},{9,1},... | collective-permute-start | bytes 1204232 | tf_op jit(solution)/shard_map/ppermute | solution.py:67
  173.0 5.1 %collective-permute-start.28 = (bf16[112,896]{1,0:T(8,128)(2,1)S(1)}, bf16[112,896]{1,0:T(8,128)(2,1)S(1)}, u32[]{:S(2)}, u32[]{:S(2)}) collective-permute-start(bf16[112,896]{1,0:T(8,128)(2,1)S(1)} %get-tuple-element.64), channel_id=1, source_target_pairs={{0,2},{1,3},{2,4},{3,5},{4,6},{5,7},{6,0},{7,1},{8,14},{9,15},{10,... | collective-permute-start | bytes 602120 | tf_op jit(solution)/shard_map/ppermute | solution.py:67
  173.7 12.3 %collective-permute-start.29 = (bf16[112,896]{1,0:T(8,128)(2,1)S(1)}, bf16[112,896]{1,0:T(8,128)(2,1)S(1)}, u32[]{:S(2)}, u32[]{:S(2)}) collective-permute-start(bf16[112,896]{1,0:T(8,128)(2,1)S(1)} %get-tuple-element.64), channel_id=1, source_target_pairs={{0,6},{1,7},{2,0},{3,1},{4,2},{5,3},{6,4},{7,5},{8,10},{9,11},{10,... | collective-permute-start | bytes 602120 | tf_op jit(solution)/shard_map/ppermute | solution.py:67
  174.5 11.5 %collective-permute-start.30 = (bf16[112,896]{1,0:T(8,128)(2,1)S(1)}, bf16[112,896]{1,0:T(8,128)(2,1)S(1)}, u32[]{:S(2)}, u32[]{:S(2)}) collective-permute-start(bf16[112,896]{1,0:T(8,128)(2,1)S(1)} %get-tuple-element.64), channel_id=1, source_target_pairs={{0,4},{1,5},{2,6},{3,7},{4,0},{5,1},{6,2},{7,3},{8,12},{9,13},{10,... | collective-permute-start | bytes 602120 | tf_op jit(solution)/shard_map/ppermute | solution.py:67
  176.4 9.8 %collective-permute-start.32 = (bf16[112,896]{1,0:T(8,128)(2,1)S(1)}, bf16[112,896]{1,0:T(8,128)(2,1)S(1)}, u32[]{:S(2)}, u32[]{:S(2)}) collective-permute-start(bf16[112,896]{1,0:T(8,128)(2,1)S(1)} %get-tuple-element.50), channel_id=1, source_target_pairs={{0,1},{1,0},{2,3},{3,2},{4,5},{5,4},{6,7},{7,6},{8,9},{9,8},{10,11... | collective-permute-start | bytes 602120 | tf_op jit(solution)/shard_map/ppermute | solution.py:67
  186.1 21.4 %collective-permute-start.31 = (bf16[448,896]{1,0:T(8,128)(2,1)S(1)}, bf16[448,896]{1,0:T(8,128)(2,1)}, u32[]{:S(2)}, u32[]{:S(2)}) collective-permute-start(bf16[448,896]{1,0:T(8,128)(2,1)S(1)} %constant_dynamic-update-slice_fusion.12), channel_id=1, source_target_pairs={{0,1},{1,0},{2,3},{3,2},{4,5},{5,4},{6,7},{7,6},{8,9},{9,8},{10,11... | collective-permute-start | bytes 2408456 | tf_op jit(solution)/shard_map/ppermute | solution.py:67
  186.9 10.2 %collective-permute-start.33 = (bf16[224,896]{1,0:T(8,128)(2,1)}, bf16[224,896]{1,0:T(8,128)(2,1)}, u32[]{:S(2)}, u32[]{:S(2)}) collective-permute-start(bf16[224,896]{1,0:T(8,128)(2,1)} %constant_dynamic-update-slice_fusion.8), channel_id=1, source_target_pairs={{0,2},{1,3},{2,4},{3,5},{4,6},{5,7},{6,0},{7,1},{8,14},{9,15},{10,... | collective-permute-start | bytes 1204232 | tf_op jit(solution)/shard_map/ppermute | solution.py:67
  186.9 11.4 %collective-permute-start.34 = (bf16[224,896]{1,0:T(8,128)(2,1)}, bf16[224,896]{1,0:T(8,128)(2,1)}, u32[]{:S(2)}, u32[]{:S(2)}) collective-permute-start(bf16[224,896]{1,0:T(8,128)(2,1)} %constant_dynamic-update-slice_fusion.8), channel_id=1, source_target_pairs={{0,6},{1,7},{2,0},{3,1},{4,2},{5,3},{6,4},{7,5},{8,10},{9,11},{10,... | collective-permute-start | bytes 1204232 | tf_op jit(solution)/shard_map/ppermute | solution.py:67
  188.3 19.1 %collective-permute-start.35 = (bf16[224,896]{1,0:T(8,128)(2,1)}, bf16[224,896]{1,0:T(8,128)(2,1)S(1)}, u32[]{:S(2)}, u32[]{:S(2)}) collective-permute-start(bf16[224,896]{1,0:T(8,128)(2,1)} %constant_dynamic-update-slice_fusion.8), channel_id=1, source_target_pairs={{0,4},{1,5},{2,6},{3,7},{4,0},{5,1},{6,2},{7,3},{8,12},{9,13},{10,... | collective-permute-start | bytes 1204232 | tf_op jit(solution)/shard_map/ppermute | solution.py:67
  190.9 17.8 %copy-start.5 = (s32[8]{0:T(128)S(1)}, s32[8]{0:T(128)}, u32[]{:S(2)}) copy-start(s32[8]{0:T(128)} %copy-done.2) | copy-start | bytes 100
  214.2 1.1 copy-start
  215.3 4.1 %collective-permute-start.36 = (f32[448,768]{1,0:T(8,128)}, f32[448,768]{1,0:T(8,128)S(1)}, u32[]{:S(2)}, u32[]{:S(2)}) collective-permute-start(f32[448,768]{1,0:T(8,128)} %get-tuple-element.46), channel_id=1, source_target_pairs={{0,8},{1,9},{2,10},{3,11},{4,12},{5,13},{6,14},{7,15},{8,0},{9,1},... | collective-permute-start | bytes 4128776 | tf_op jit(solution)/shard_map/ppermute | solution.py:67
  221.0 8.0 %collective-permute-start.39 = (bf16[112,768]{1,0:T(8,128)(2,1)S(1)}, bf16[112,768]{1,0:T(8,128)(2,1)S(1)}, u32[]{:S(2)}, u32[]{:S(2)}) collective-permute-start(bf16[112,768]{1,0:T(8,128)(2,1)S(1)} %get-tuple-element.58), channel_id=1, source_target_pairs={{0,64},{1,65},{2,66},{3,67},{4,68},{5,69},{6,70},{7,71},{8,72},{9,... | collective-permute-start | bytes 516104 | tf_op jit(solution)/shard_map/ppermute | solution.py:67
  224.6 7.7 %collective-permute-start.38 = (bf16[112,768]{1,0:T(8,128)(2,1)S(1)}, bf16[112,768]{1,0:T(8,128)(2,1)S(1)}, u32[]{:S(2)}, u32[]{:S(2)}) collective-permute-start(bf16[112,768]{1,0:T(8,128)(2,1)S(1)} %get-tuple-element.59), channel_id=1, source_target_pairs={{0,96},{1,97},{2,98},{3,99},{4,100},{5,101},{6,102},{7,103},{8,40}... | collective-permute-start | bytes 516104 | tf_op jit(solution)/shard_map/ppermute | solution.py:67
  225.8 7.9 %collective-permute-start.37 = (bf16[112,768]{1,0:T(8,128)(2,1)S(1)}, bf16[112,768]{1,0:T(8,128)(2,1)S(1)}, u32[]{:S(2)}, u32[]{:S(2)}) collective-permute-start(bf16[112,768]{1,0:T(8,128)(2,1)S(1)} %get-tuple-element.57), channel_id=1, source_target_pairs={{0,32},{1,33},{2,34},{3,35},{4,36},{5,37},{6,38},{7,39},{8,104},{9... | collective-permute-start | bytes 516104 | tf_op jit(solution)/shard_map/ppermute | solution.py:67
  233.7 10.5 %collective-permute-start.40 = (f32[112,768]{1,0:T(8,128)S(1)}, f32[112,768]{1,0:T(8,128)S(1)}, u32[]{:S(2)}, u32[]{:S(2)}) collective-permute-start(f32[112,768]{1,0:T(8,128)S(1)} %add_add_fusion), channel_id=1, source_target_pairs={{0,16},{1,17},{2,18},{3,19},{4,20},{5,21},{6,22},{7,23},{8,24},{9,... | collective-permute-start | bytes 1032200 | tf_op jit(solution)/shard_map/ppermute | solution.py:67
  244.3 6.0 %collective-permute-start.41 = (bf16[112,768]{1,0:T(8,128)(2,1)S(1)}, bf16[112,768]{1,0:T(8,128)(2,1)S(1)}, u32[]{:S(2)}, u32[]{:S(2)}) collective-permute-start(bf16[112,768]{1,0:T(8,128)(2,1)S(1)} %get-tuple-element.48), channel_id=1, source_target_pairs={{0,32},{1,33},{2,34},{3,35},{4,36},{5,37},{6,38},{7,39},{8,104},{9... | collective-permute-start | bytes 516104 | tf_op jit(solution)/shard_map/ppermute | solution.py:67
  248.0 9.9 %collective-permute-start.42 = (bf16[112,768]{1,0:T(8,128)(2,1)S(1)}, bf16[112,768]{1,0:T(8,128)(2,1)S(1)}, u32[]{:S(2)}, u32[]{:S(2)}) collective-permute-start(bf16[112,768]{1,0:T(8,128)(2,1)S(1)} %get-tuple-element.48), channel_id=1, source_target_pairs={{0,96},{1,97},{2,98},{3,99},{4,100},{5,101},{6,102},{7,103},{8,40}... | collective-permute-start | bytes 516104 | tf_op jit(solution)/shard_map/ppermute | solution.py:67
  248.0 9.9 %collective-permute-start.43 = (bf16[112,768]{1,0:T(8,128)(2,1)S(1)}, bf16[112,768]{1,0:T(8,128)(2,1)S(1)}, u32[]{:S(2)}, u32[]{:S(2)}) collective-permute-start(bf16[112,768]{1,0:T(8,128)(2,1)S(1)} %get-tuple-element.48), channel_id=1, source_target_pairs={{0,64},{1,65},{2,66},{3,67},{4,68},{5,69},{6,70},{7,71},{8,72},{9,... | collective-permute-start | bytes 516104 | tf_op jit(solution)/shard_map/ppermute | solution.py:67
  258.0 2.3 collective-permute-start.44
where the time goes:
time: 263 us; the launch traced here: 262 us
  waiting for transfers between devices  121 us (46%)
  starting transfers between devices  56.4 us (21%)
  local copies, waits for them, and re-layouts  38.2 us (15%)
  Pallas kernels  30.7 us (12%)
  other arithmetic  14.5 us (6%)
    ppermute x45, waiting for transfers between devices, send(): return lax.ppermute(array, AXES, pairs)  121 us
    ppermute x45, starting transfers between devices, send(): return lax.ppermute(array, AXES, pairs)  56.4 us
    dynamic_update_slice x20, local copies, waits for them, and re-layouts, put(): return lax.dynamic_update_slice(into, array, index)  18.4 us
    pallas_call x1, Pallas kernels, multiply(): pl.pallas_call(multiply_kernel, out_shape=jax.ShapeDtypeStruct((2, ROWS,...  17.7 us
    pallas_call x2, Pallas kernels, cross(): pl.pallas_call(kernel, out_shape=[jax.ShapeDtypeStruct((n, WIDE), bf16)]...  6.49 us
    pallas_call x1, Pallas kernels, exchange(): pl.pallas_call(exchange_kernel, out_shape=[jax.ShapeDtypeStruct((WIDE //...  5.41 us
  transfers between devices with their start and end apart: 45, of which 30 were waited for; matrix products, arithmetic and copies ran while one was open for 15% of the time, Pallas kernels for 8%

commit v1 on v0

--- a/solution.py
+++ b/solution.py
@@ -79,18 +79,19 @@
     return send(array, permutation(other_high))
 
 
-def slab_kernel(place, main, rest, out, sems):
+def slab_kernel(place, main0, main1, rest, out, sems):
     core, row = place[0], place[1]
     copies = []
     for x in range(X):
         a = jnp.where(core == 0, x, row // ZL)
         b = jnp.where(core == 0, row // ZL, x)
-        copies.append(
-            pltpu.make_async_copy(main.at[b, row % ZL, :, :, a], out.at[:, x, :, pl.ds(0, MAIN)], sems.at[2 * x])
-        )
+        for c, main in enumerate((main0, main1)):
+            copies.append(
+                pltpu.make_async_copy(main.at[b, row % ZL, :, a], out.at[c, x, :, pl.ds(0, MAIN)], sems.at[3 * x + c])
+            )
         copies.append(
             pltpu.make_async_copy(
-                rest.at[row % ZL, :, :, a, b], out.at[:, x, :, pl.ds(MAIN, OWN - MAIN)], sems.at[2 * x + 1]
+                rest.at[row % ZL, :, :, a, b], out.at[:, x, :, pl.ds(MAIN, OWN - MAIN)], sems.at[3 * x + 2]
             )
         )
     for copy in copies:
@@ -99,19 +100,20 @@
         copy.wait()
 
 
-def own_slab(place, main, rest):
+def own_slab(place, main0, main1, rest):
     return pl.pallas_call(
         slab_kernel,
         out_shape=jax.ShapeDtypeStruct((CORE, X, ZL, OWN, WIDE), bf16),
-        in_specs=[pl.BlockSpec(memory_space=pltpu.SMEM)] + [pl.BlockSpec(memory_space=pl.ANY)] * 2,
+        in_specs=[pl.BlockSpec(memory_space=pltpu.SMEM)] + [pl.BlockSpec(memory_space=pl.ANY)] * 3,
         out_specs=pl.BlockSpec(memory_space=pltpu.VMEM),
-        scratch_shapes=[pltpu.SemaphoreType.DMA((2 * X,))],
+        scratch_shapes=[pltpu.SemaphoreType.DMA((3 * X,))],
         compiler_params=pltpu.CompilerParams(vmem_limit_bytes=4 * 1024 * 1024),
         name="slab",
-    )(place, main, rest)
-
-
-def multiply_kernel(place, meta, own_blocks, other_blocks, main, rest, out, blocks, held, total, order, counts, steps, sems):
+    )(place, main0, main1, rest)
+
+
+def multiply_kernel(place, meta, own_blocks, other_blocks, main0, main1, rest, out, *scratch):
+    blocks, held, total, order, counts, steps, sems = scratch
     core = place[0]
     copies = [
         pltpu.make_async_copy(own_blocks, blocks.at[pl.ds(0, SLOTS)], sems.at[0]),
@@ -120,15 +122,16 @@
     for a in range(4):
         for b in range(4):
             y, x = jnp.where(core == 0, b, a), jnp.where(core == 0, a, b)
-            i = 2 + 2 * (4 * a + b)
+            i = 2 + 3 * (4 * a + b)
+            for c, main in enumerate((main0, main1)):
+                copies.append(
+                    pltpu.make_async_copy(
+                        main.at[b, :, :, a], held.at[y, :, c, x, :, pl.ds(0, MAIN)], sems.at[i + c]
+                    )
+                )
             copies.append(
                 pltpu.make_async_copy(
-                    main.at[b, :, :, :, a], held.at[y, :, :, x, :, pl.ds(0, MAIN)], sems.at[i]
-                )
-            )
-            copies.append(
-                pltpu.make_async_copy(
-                    rest.at[:, :, :, a, b], held.at[y, :, :, x, :, pl.ds(MAIN, OWN - MAIN)], sems.at[i + 1]
+                    rest.at[:, :, :, a, b], held.at[y, :, :, x, :, pl.ds(MAIN, OWN - MAIN)], sems.at[i + 2]
                 )
             )
     for copy in copies:
@@ -206,12 +209,12 @@
     lax.fori_loop(0, GROUPS, finish, 0)
 
 
-def multiply(place, meta, own_blocks, other_blocks, main, rest):
+def multiply(place, meta, own_blocks, other_blocks, main0, main1, rest):
     most = 2 * SLOTS // STEP + GROUPS + UNROLL
     return pl.pallas_call(
         multiply_kernel,
         out_shape=jax.ShapeDtypeStruct((2, ROWS, WIDE), bf16),
-        in_specs=[pl.BlockSpec(memory_space=pltpu.SMEM)] * 2 + [pl.BlockSpec(memory_space=pl.ANY)] * 4,
+        in_specs=[pl.BlockSpec(memory_space=pltpu.SMEM)] * 2 + [pl.BlockSpec(memory_space=pl.ANY)] * 5,
         out_specs=pl.BlockSpec(memory_space=pltpu.VMEM),
         scratch_shapes=[
             pltpu.VMEM((2 * SLOTS + 1, BLK, BLK), bf16),
@@ -220,12 +223,12 @@
             pltpu.SMEM((GROUPS, SLOTS + 2 * STEP), jnp.int32),
             pltpu.SMEM((GROUPS + 1,), jnp.int32),
             pltpu.SMEM((most, 1 + 2 * STEP), jnp.int32),
-            pltpu.SemaphoreType.DMA((34,)),
+            pltpu.SemaphoreType.DMA((50,)),
         ],
         compiler_params=pltpu.CompilerParams(vmem_limit_bytes=30 * 1024 * 1024),
         cost_estimate=pl.CostEstimate(flops=2 * 96 * 2 * 128 * 128 * 896, bytes_accessed=2**24, transcendentals=0),
         name="multiply",
-    )(place, meta, own_blocks, other_blocks, main, rest)
+    )(place, meta, own_blocks, other_blocks, main0, main1, rest)
 
 
 def cross_kernel(q, starts, place, half, slab, theirs, *refs):
@@ -322,21 +325,11 @@
             index[int(dim[1:])] = i
         return lax.dynamic_update_slice(into, array, index)
 
-    lists = jnp.concatenate([block_rows % ROW_BLOCKS, block_cols, jnp.broadcast_to(block_count, (1, SLOTS))])
-    tail = jnp.pad(lists.astype(bf16), ((0, OWN - 3), (0, 0)))
-    got = send_next(
-        jnp.concatenate([choose(response, orbitals), tail], axis=1), permutation(other_core)
-    )
+    got = send(choose(response, orbitals), permutation(other_core))
     own_blocks = factors[0]
-    other_blocks = send_next(own_blocks, permutation(other_core))
-    other_lists = got[:3, NOCC:].astype(jnp.int32)
-    meta = jnp.stack([jnp.concatenate([a[0], a[1], a[2, :64]]) for a in (lists, other_lists)])
-    place = jnp.stack(
-        [c, row, x, (x + sign) % 4, (x - sign) % 4, (x + 2) % 4, zl, 1 - zl]
-    ).astype(jnp.int32)
-    keep = jnp.pad(choose(orbitals, response), ((0, 0), (0, WIDE - NOCC)))
-    got = jnp.where(jnp.arange(WIDE)[None] < NOCC, got, jnp.zeros((), bf16))
-    both = jnp.stack([choose(keep, got), choose(got, keep)])
+    other_blocks = swap_cores(own_blocks)
+    both = jnp.stack([choose(orbitals, got), choose(got, response)])
+    both = jnp.pad(both, ((0, 0), (0, 0), (0, WIDE - NOCC)))
 
     one, two = ("x", "y"), ("y", "x")
     at_one, at_two = choose(x, y), choose(y, x)
@@ -345,9 +338,14 @@
     ahead = send_next(both, around(one, 1, False))
     behind = send_next(both, around(one, -1, False))
     far = send_next(both, around(one, 2, False))
+    lists = jnp.concatenate([block_rows[0] % ROW_BLOCKS, block_cols[0], block_count[0]])
+    lists = jnp.pad(lists, (0, 256 - 2 * SLOTS - 1))[None]
+    meta = jnp.concatenate([lists, swap_cores(lists)])
+    place = jnp.stack([c, row, x, (x + sign) % 4, (x - sign) % 4, (x + 2) % 4, zl, 1 - zl]).astype(jnp.int32)
     stage = put(stage, ahead[:, None], d1=(at_one - 1) % 4)
     stage = put(stage, behind[:, None], d1=(at_one + 1) % 4)
     stage = put(stage, far[:, None], d1=(at_one + 2) % 4)
+    stage, other_blocks, meta = lax.optimization_barrier((stage, other_blocks, meta))
 
     main, rest = stage[:, :, :MAIN], stage[:, :, MAIN:]
     zz = ("z", "z")
@@ -358,18 +356,14 @@
     main_far = send_next(main_ahead, around(zz, 1, True))
     rest_far = send_next(rest, around(two, 2, False))
 
-    def by_z(into, array, at):
-        return put(into, array, d0=at // ZL, d2=at % ZL)
-
-    into = jnp.zeros((ZH, CORE, ZL, 4, MAIN, WIDE), bf16)
+    mains = [jnp.zeros((ZH, ZL, 4, MAIN, WIDE), bf16)] * 2
     for array, at in (
         (main, z),
         (main_ahead, (z - sign) % 4),
         (main_behind, (z + sign) % 4),
         (main_far, (z + 2) % 4),
     ):
-        into = by_z(into, array[None, :, None], at)
-    main = into
+        mains = [put(into, array[i][None, None], d0=at // ZL, d1=at % ZL) for i, into in enumerate(mains)]
     into = jnp.zeros((CORE, 4, 4, OWN - MAIN, WIDE), bf16)
     for array, at in (
         (rest, at_two),
@@ -380,25 +374,26 @@
         into = put(into, array[:, :, None], d2=at)
     rest = into
 
-    main_ahead = send_next(main, around(two, 1, False))
+    ahead, behind = around(two, 1, False), around(two, -1, False)
+    ahead_0 = send_next(mains[0], ahead)
+    behind_1 = send_next(mains[1], behind)
     rest_ahead = send_next(rest, around(zz, 1, True))
-    main_behind = send_next(main, around(two, -1, False))
     rest_behind = send_next(rest, around(zz, -1, True))
-    main_far = [
-        send_next(main_ahead[:1], around(two, 1, False)),
-        send_next(main_behind[1:], around(two, -1, False)),
-    ]
+    ahead_1 = send_next(mains[1], ahead)
+    behind_0 = send_next(mains[0], behind)
+    far_0 = send_next(ahead_0, ahead)
+    far_1 = send_next(behind_1, behind)
     rest_far = send_next(rest_ahead, around(zz, 1, True))
-    into = jnp.zeros((4, *main.shape), bf16)
-    for array, at, part in (
-        (main, at_two, 0),
-        (main_ahead, (at_two - 1) % 4, 0),
-        (main_behind, (at_two + 1) % 4, 0),
-        (main_far[0], (at_two + 2) % 4, 0),
-        (main_far[1], (at_two + 2) % 4, 1),
-    ):
-        into = put(into, array[None], d0=at, d1=jnp.int32(part))
-    main = into
+    arrays = (
+        (mains[0], ahead_0, behind_0, far_0),
+        (mains[1], ahead_1, behind_1, far_1),
+    )
+    mains = []
+    for four in arrays:
+        into = jnp.zeros((4, *four[0].shape), bf16)
+        for array, at in zip(four, (at_two, (at_two - 1) % 4, (at_two + 1) % 4, (at_two + 2) % 4)):
+            into = put(into, array[None], d0=at)
+        mains.append(into)
     into = jnp.zeros((ZH, CORE, ZL, 4, 4, OWN - MAIN, WIDE), bf16)
     for array, at in (
         (rest, z),
@@ -406,12 +401,12 @@
         (rest_behind, (z + sign) % 4),
         (rest_far, (z + 2) % 4),
     ):
-        into = by_z(into, array[None, :, None], at)
+        into = put(into, array[None, :, None], d0=at // ZL, d2=at % ZL)
     rest = into
 
-    slab = own_slab(place, main, rest).reshape(ROWS, WIDE)
+    slab = own_slab(place, *mains, rest).reshape(ROWS, WIDE)
     theirs = swap_cores(slab)
-    half = multiply(place, meta, own_blocks, other_blocks, main, rest)
+    half = multiply(place, meta, own_blocks, other_blocks, *mains, rest)
 
     def add(*arrays):
         return sum(a.astype(f32) for a in arrays)
@@ -422,19 +417,20 @@
     xx = ("x", "x")
     ahead, behind = around(xx, 1, True), around(xx, -1, True)
     opposite = around(xx, 2, True)
+    half_mine, to_low = cross(1, (6, 7), WIDE // 2, place, half, slab, theirs)
+    from_low = swap_low(to_low)
     mine, to_ahead, to_behind, to_far = cross(0, (2, 3, 4, 5), WIDE // 4, place, half, slab, theirs)
-    mine = add(mine, send(to_ahead, ahead), send(to_behind, behind), send(to_far, opposite)).astype(bf16)
-    half_mine, to_low = cross(1, (6, 7), WIDE // 2, place, half, slab, theirs)
-    half_mine = add(half_mine, swap_low(to_low)).astype(bf16)
-    shards = [
-        add(rows_of(mine, zl, SHARD), swap_low(rows_of(mine, 1 - zl, SHARD))),
-        add(
-            rows_of(half_mine, x, SHARD),
-            send(rows_of(half_mine, (x + sign) % 4, SHARD), ahead),
-            send(rows_of(half_mine, (x - sign) % 4, SHARD), behind),
-            send(rows_of(half_mine, (x + 2) % 4, SHARD), opposite),
-        ),
-    ]
+    parts = (mine, send(to_ahead, ahead), send(to_behind, behind), send(to_far, opposite))
+    half_mine = add(half_mine, from_low).astype(bf16)
+    second = (
+        rows_of(half_mine, x, SHARD),
+        send(rows_of(half_mine, (x + sign) % 4, SHARD), ahead),
+        send(rows_of(half_mine, (x - sign) % 4, SHARD), behind),
+        send(rows_of(half_mine, (x + 2) % 4, SHARD), opposite),
+    )
+    parts, half_mine = lax.optimization_barrier((parts, half_mine))
+    mine = add(*parts).astype(bf16)
+    shards = [add(rows_of(mine, zl, SHARD), swap_low(rows_of(mine, 1 - zl, SHARD))), add(*second)]
 
     last = (x == X - 1) & (zl == ZL - 1)
     at = jnp.arange(SHARD, dtype=jnp.int32)[:, None] + (WIDE - SHARD)

time: 263 us -> 255 us (0.970)
  local copies, waits for them, and re-layouts: 38.2 us -> 15.3 us
  starting transfers between devices: 56.4 us -> 75.2 us
    ppermute x45 -> x48, starting transfers between devices: 56.4 us -> 75.2 us  [send(): return lax.ppermute(array, AXES, pairs)]
    dynamic_update_slice x20 -> x24, local copies, waits for them, and re-layouts: 18.4 us -> 2.09 us  [put(): return lax.dynamic_update_slice(into, array, index)]
    ppermute x45 -> x48, waiting for transfers between devices: 121 us -> 119 us  [send(): return lax.ppermute(array, AXES, pairs)]
  transfers between devices with their start and end apart: 45 -> 48, of which waited for: 30 -> 31; matrix products, arithmetic and copies ran while one was open for 15% -> 5% of each run, Pallas kernels for 8% -> 8%
where the time goes in v1:
time: 255 us
  waiting for transfers between devices  119 us (47%)
  starting transfers between devices  75.2 us (29%)
  Pallas kernels  30.6 us (12%)
  local copies, waits for them, and re-layouts  15.3 us (6%)
  other arithmetic  13.7 us (5%)
    ppermute x48, waiting for transfers between devices, send(): return lax.ppermute(array, AXES, pairs)  119 us
    ppermute x48, starting transfers between devices, send(): return lax.ppermute(array, AXES, pairs)  75.2 us
    pallas_call x1, Pallas kernels, multiply(): pl.pallas_call(multiply_kernel, out_shape=jax.ShapeDtypeStruct((2, ROWS,...  17.1 us
    pallas_call x2, Pallas kernels, cross(): pl.pallas_call(kernel, out_shape=[jax.ShapeDtypeStruct((n, WIDE), bf16)]...  6.64 us
    pallas_call x1, Pallas kernels, exchange(): pl.pallas_call(exchange_kernel, out_shape=[jax.ShapeDtypeStruct((WIDE //...  5.41 us
  transfers between devices with their start and end apart: 48, of which 31 were waited for; matrix products, arithmetic and copies ran while one was open for 5% of the time, Pallas kernels for 8%

profile of v1, /device:TPU:1, one launch (start us, length us, event | category | flops | bytes accessed | tf_op | source)
XLA Modules:
  0.0 254.6 jit_solution(3189341464309371058)
XLA Ops:
  0.0 1.4 collective-permute-start.4
  5.1 1.8 collective-permute-done
  7.8 1.4 collective-permute-start.1
  9.2 1.5 collective-permute-start.2
  10.8 1.6 collective-permute-start.3
  12.5 1.3 collective-permute-done.1
  13.9 2.9 %collective-permute-done.3 = bf16[2,48,896]{2,1,0:T(8,128)(2,1)S(1)} collective-permute-done((bf16[2,48,896]{2,1,0:T(8,128)(2,1)S(1)}, bf16[2,48,896]{2,1,0:T(8,128)(2,1)S(1)}, u32[]{:S(2)}, u32[]{:S(2)}) %collective-permute-start.3) | collective-permute-done | bytes 172064 | tf_op jit(solution)/shard_map/ppermute | solution.py:67
  16.9 3.8 %collective-permute-start.6 = (bf16[2,4,32,896]{3,2,1,0:T(8,128)(2,1)S(1)}, bf16[2,4,32,896]{3,2,1,0:T(8,128)(2,1)S(1)}, u32[]{:S(2)}, u32[]{:S(2)}) collective-permute-start(bf16[2,4,32,896]{3,2,1,0:T(8,128)(2,1)S(1)} %slice.48), channel_id=1, source_target_pairs={{0,1},{1,16},{2,3},{3,18},{4,5},{5,20},{6,7},{7,22},{8,25},{9,8},{... | collective-permute-start | bytes 1376264 | tf_op jit(solution)/shard_map/ppermute | solution.py:67
  22.0 1.8 collective-permute-start.16
  23.9 3.6 %collective-permute-done.11 = bf16[2,4,16,896]{3,2,1,0:T(8,128)(2,1)S(1)} collective-permute-done((bf16[2,4,16,896]{3,2,1,0:T(8,128)(2,1)S(1)}, bf16[2,4,16,896]{3,2,1,0:T(8,128)(2,1)S(1)}, u32[]{:S(2)}, u32[]{:S(2)}) %collective-permute-start.11) | collective-permute-done | bytes 229408 | tf_op jit(solution)/shard_map/ppermute | solution.py:67
  27.5 1.2 collective-permute-done.6
  28.8 3.4 %collective-permute-start.8 = (bf16[2,4,32,896]{3,2,1,0:T(8,128)(2,1)S(1)}, bf16[2,4,32,896]{3,2,1,0:T(8,128)(2,1)S(1)}, u32[]{:S(2)}, u32[]{:S(2)}) collective-permute-start(bf16[2,4,32,896]{3,2,1,0:T(8,128)(2,1)S(1)} %collective-permute-done.6), channel_id=1, source_target_pairs={{0,1},{1,16},{2,3},{3,18},{4,5},{5,20},{6,7},{7,22},{8,25},{9,8},{... | collective-permute-start | bytes 1376264 | tf_op jit(solution)/shard_map/ppermute | solution.py:67
  32.2 3.4 %collective-permute-start.14 = (bf16[2,4,16,896]{3,2,1,0:T(8,128)(2,1)S(1)}, bf16[2,4,16,896]{3,2,1,0:T(8,128)(2,1)S(1)}, u32[]{:S(2)}, u32[]{:S(2)}) collective-permute-start(bf16[2,4,16,896]{3,2,1,0:T(8,128)(2,1)S(1)} %slice.56), channel_id=1, source_target_pairs={{0,64},{1,65},{2,66},{3,67},{4,68},{5,69},{6,70},{7,71},{8,12},{9,... | collective-permute-start | bytes 688136 | tf_op jit(solution)/shard_map/ppermute | solution.py:67
  35.7 3.6 %collective-permute-done.14 = bf16[2,4,16,896]{3,2,1,0:T(8,128)(2,1)S(1)} collective-permute-done((bf16[2,4,16,896]{3,2,1,0:T(8,128)(2,1)S(1)}, bf16[2,4,16,896]{3,2,1,0:T(8,128)(2,1)S(1)}, u32[]{:S(2)}, u32[]{:S(2)}) %collective-permute-start.14) | collective-permute-done | bytes 229408 | tf_op jit(solution)/shard_map/ppermute | solution.py:67
  40.5 2.4 collective-permute-start.12
  42.9 1.2 collective-permute-start.19
  45.9 8.3 %collective-permute-done.17 = bf16[2,4,4,16,896]{4,3,2,1,0:T(8,128)(2,1)S(1)} collective-permute-done((bf16[2,4,4,16,896]{4,3,2,1,0:T(8,128)(2,1)S(1)}, bf16[2,4,4,16,896]{4,3,2,1,0:T(8,128)(2,1)S(1)}, u32[]{:S(2)}, u32[]{:S(2)}) %collective-permute-start.17) | collective-permute-done | bytes 917536 | tf_op jit(solution)/shard_map/ppermute | solution.py:67
  54.3 5.1 %collective-permute-start.10 = (bf16[2,2,4,32,896]{4,3,2,1,0:T(8,128)(2,1)S(1)}, bf16[2,2,4,32,896]{4,3,2,1,0:T(8,128)(2,1)S(1)}, u32[]{:S(2)}, u32[]{:S(2)}) collective-permute-start(bf16[2,2,4,32,896]{4,3,2,1,0:T(8,128)(2,1)S(1)} %get-tuple-element.38), channel_id=1, source_target_pairs={{0,96},{1,97},{2,98},{3,99},{4,100},{5,101},{6,102},{7,103},{8,14}... | collective-permute-start | bytes 2752520 | tf_op jit(solution)/shard_map/ppermute | solution.py:67
  59.4 2.7 %collective-permute-start.18 = (bf16[2,2,4,32,896]{4,3,2,1,0:T(8,128)(2,1)S(1)}, bf16[2,2,4,32,896]{4,3,2,1,0:T(8,128)(2,1)S(1)}, u32[]{:S(2)}, u32[]{:S(2)}) collective-permute-start(bf16[2,2,4,32,896]{4,3,2,1,0:T(8,128)(2,1)S(1)} %collective-permute-done.12), channel_id=1, source_target_pairs={{0,96},{1,97},{2,98},{3,99},{4,100},{5,101},{6,102},{7,103},{8,14}... | collective-permute-start | bytes 2752520 | tf_op jit(solution)/shard_map/ppermute | solution.py:67
  62.1 3.5 %collective-permute-done.19 = bf16[2,4,4,16,896]{4,3,2,1,0:T(8,128)(2,1)S(1)} collective-permute-done((bf16[2,4,4,16,896]{4,3,2,1,0:T(8,128)(2,1)S(1)}, bf16[2,4,4,16,896]{4,3,2,1,0:T(8,128)(2,1)S(1)}, u32[]{:S(2)}, u32[]{:S(2)}) %collective-permute-start.19) | collective-permute-done | bytes 917536 | tf_op jit(solution)/shard_map/ppermute | solution.py:67
  65.6 1.1 collective-permute-start.20
  67.3 2.4 collective-permute-done.10
  69.9 3.7 %collective-permute-done.13 = bf16[2,2,4,32,896]{4,3,2,1,0:T(8,128)(2,1)S(1)} collective-permute-done((bf16[2,2,4,32,896]{4,3,2,1,0:T(8,128)(2,1)S(1)}, bf16[2,2,4,32,896]{4,3,2,1,0:T(8,128)(2,1)S(1)}, u32[]{:S(2)}, u32[]{:S(2)}) %collective-permute-start.13) | collective-permute-done | bytes 917536 | tf_op jit(solution)/shard_map/ppermute | solution.py:67
  73.7 5.9 %collective-permute-done.18 = bf16[2,2,4,32,896]{4,3,2,1,0:T(8,128)(2,1)S(1)} collective-permute-done((bf16[2,2,4,32,896]{4,3,2,1,0:T(8,128)(2,1)S(1)}, bf16[2,2,4,32,896]{4,3,2,1,0:T(8,128)(2,1)S(1)}, u32[]{:S(2)}, u32[]{:S(2)}) %collective-permute-start.18) | collective-permute-done | bytes 917536 | tf_op jit(solution)/shard_map/ppermute | solution.py:67
  79.9 1.4 slab.1
  81.3 9.4 %collective-permute-start.21 = (bf16[768,896]{1,0:T(8,128)(2,1)S(1)}, bf16[768,896]{1,0:T(8,128)(2,1)S(1)}, u32[]{:S(2)}, u32[]{:S(2)}) collective-permute-start(bf16[768,896]{1,0:T(8,128)(2,1)S(1)} %bitcast.120), channel_id=1, source_target_pairs={{0,8},{1,9},{2,10},{3,11},{4,12},{5,13},{6,14},{7,15},{8,0},{9,1},... | collective-permute-start | bytes 4128776 | tf_op jit(solution)/shard_map/ppermute | solution.py:67
  90.8 17.1 %multiply.1.refs_1_.half = bf16[2,768,896]{2,1,0:T(8,128)(2,1)S(1)} custom-call(s32[8]{0:T(128)S(1)} %stack.53.place.refs_0_, s32[2,256]{1,0:T(2,128)S(1)} %pad_add_fusion.meta, bf16[96,128,128]{2,1,0:T(8,128)(2,1)S(1)} %bitcast.124, bf16[96,128,128]{2,1,0:T(8,128)(2,1)} %collective-permute-done.4.other_blocks, ...), custom_call_target="tpu_custom_call" | custom-call | flops 5637144576 | bytes 16777216 | tf_op jit(solution)/shard_map/multiply/pallas_call | solution.py:214
  108.6 3.3 %cross.3 = (bf16[448,896]{1,0:T(8,128)(2,1)S(1)}, bf16[448,896]{1,0:T(8,128)(2,1)}) custom-call(s32[8]{0:T(128)S(1)} %copy-done.3, bf16[2,768,896]{2,1,0:T(8,128)(2,1)S(1)} %multiply.1.refs_1_.half, bf16[768,896]{1,0:T(8,128)(2,1)S(1)} %bitcast.121, bf16[768,896]{1,0:T(8,128)(2,1)S(1)} %collective-permute-done.21.refs_3_), custom_call_target="tpu_custom_call" | custom-call | flops 1233125376 | bytes 8388608 | tf_op jit(solution)/shard_map/cross/pallas_call | solution.py:260
  111.9 3.4 %cross.2 = (bf16[224,896]{1,0:T(8,128)(2,1)S(1)}, bf16[224,896]{1,0:T(8,128)(2,1)}, bf16[224,896]{1,0:T(8,128)(2,1)}, bf16[224,896]{1,0:T(8,128)(2,1)}) custom-call(s32[8]{0:T(128)S(1)} %copy-done.4, bf16[2,768,896]{2,1,0:T(8,128)(2,1)S(1)} %multiply.1.refs_1_.half, bf16[768,896]{1,0:T(8,128)(2,1)S(1)} %bitcast.122, ...), custom_call_target="tpu_custom_call" | custom-call | flops 1233125376 | bytes 8388608 | tf_op jit(solution)/shard_map/cross/pallas_call | solution.py:260
  116.0 2.3 collective-permute-start.22
  118.4 3.9 %collective-permute-start.24 = (bf16[224,896]{1,0:T(8,128)(2,1)}, bf16[224,896]{1,0:T(8,128)(2,1)}, u32[]{:S(2)}, u32[]{:S(2)}) collective-permute-start(bf16[224,896]{1,0:T(8,128)(2,1)} %get-tuple-element.52), channel_id=1, source_target_pairs={{0,4},{1,5},{2,6},{3,7},{4,0},{5,1},{6,2},{7,3},{8,12},{9,13},{10,... | collective-permute-start | bytes 1204232 | tf_op jit(solution)/shard_map/ppermute | solution.py:67
  122.2 9.4 %collective-permute-done.25 = bf16[448,896]{1,0:T(8,128)(2,1)} collective-permute-done((bf16[448,896]{1,0:T(8,128)(2,1)}, bf16[448,896]{1,0:T(8,128)(2,1)}, u32[]{:S(2)}, u32[]{:S(2)}) %collective-permute-start.25) | collective-permute-done | bytes 802848 | tf_op jit(solution)/shard_map/ppermute | solution.py:67
  131.6 1.3 add_convert_fusion
  133.0 6.6 %collective-permute-done.24 = bf16[224,896]{1,0:T(8,128)(2,1)} collective-permute-done((bf16[224,896]{1,0:T(8,128)(2,1)}, bf16[224,896]{1,0:T(8,128)(2,1)}, u32[]{:S(2)}, u32[]{:S(2)}) %collective-permute-start.24) | collective-permute-done | bytes 401440 | tf_op jit(solution)/shard_map/ppermute | solution.py:67
  139.6 1.6 add_convert_fusion.1
  141.9 1.7 collective-permute-start.26
  144.7 2.7 %collective-permute-start.27 = (bf16[112,896]{1,0:T(8,128)(2,1)}, bf16[112,896]{1,0:T(8,128)(2,1)}, u32[]{:S(2)}, u32[]{:S(2)}) collective-permute-start(bf16[112,896]{1,0:T(8,128)(2,1)} %get-tuple-element.72), channel_id=1, source_target_pairs={{0,2},{1,3},{2,4},{3,5},{4,6},{5,7},{6,0},{7,1},{8,14},{9,15},{10,... | collective-permute-start | bytes 602120 | tf_op jit(solution)/shard_map/ppermute | solution.py:67
  147.4 1.9 collective-permute-done.26
  149.3 3.4 %collective-permute-done.29 = bf16[112,896]{1,0:T(8,128)(2,1)S(1)} collective-permute-done((bf16[112,896]{1,0:T(8,128)(2,1)}, bf16[112,896]{1,0:T(8,128)(2,1)S(1)}, u32[]{:S(2)}, u32[]{:S(2)}) %collective-permute-start.29) | collective-permute-done | bytes 200736 | tf_op jit(solution)/shard_map/ppermute | solution.py:67
  152.7 4.3 %collective-permute-done.28 = bf16[112,896]{1,0:T(8,128)(2,1)} collective-permute-done((bf16[112,896]{1,0:T(8,128)(2,1)}, bf16[112,896]{1,0:T(8,128)(2,1)}, u32[]{:S(2)}, u32[]{:S(2)}) %collective-permute-start.28) | collective-permute-done | bytes 200736 | tf_op jit(solution)/shard_map/ppermute | solution.py:67
  157.0 1.5 fusion
  160.2 1.5 collective-permute-done.30
  163.4 1.9 constant_dynamic-update-slice_fusion.9
  167.4 4.1 %collective-permute-done.31 = bf16[112,896]{1,0:T(8,128)(2,1)S(1)} collective-permute-done((bf16[112,896]{1,0:T(8,128)(2,1)S(1)}, bf16[112,896]{1,0:T(8,128)(2,1)S(1)}, u32[]{:S(2)}, u32[]{:S(2)}) %collective-permute-start.31) | collective-permute-done | bytes 200736 | tf_op jit(solution)/shard_map/ppermute | solution.py:67
  171.5 6.4 %collective-permute-done.32 = bf16[112,896]{1,0:T(8,128)(2,1)S(1)} collective-permute-done((bf16[112,896]{1,0:T(8,128)(2,1)S(1)}, bf16[112,896]{1,0:T(8,128)(2,1)S(1)}, u32[]{:S(2)}, u32[]{:S(2)}) %collective-permute-start.32) | collective-permute-done | bytes 200736 | tf_op jit(solution)/shard_map/ppermute | solution.py:67
  179.0 1.2 collective-permute-start.37
  182.3 6.6 %collective-permute-done.36 = bf16[224,896]{1,0:T(8,128)(2,1)} collective-permute-done((bf16[224,896]{1,0:T(8,128)(2,1)}, bf16[224,896]{1,0:T(8,128)(2,1)}, u32[]{:S(2)}, u32[]{:S(2)}) %collective-permute-start.36) | collective-permute-done | bytes 401440 | tf_op jit(solution)/shard_map/ppermute | solution.py:67
  189.9 2.2 collective-permute-done.37
  193.2 4.8 %collective-permute-done.38 = bf16[224,896]{1,0:T(8,128)(2,1)S(1)} collective-permute-done((bf16[224,896]{1,0:T(8,128)(2,1)}, bf16[224,896]{1,0:T(8,128)(2,1)S(1)}, u32[]{:S(2)}, u32[]{:S(2)}) %collective-permute-start.38) | collective-permute-done | bytes 401440 | tf_op jit(solution)/shard_map/ppermute | solution.py:67
  198.1 1.3 constant_dynamic-update-slice_fusion.10.first
  199.3 5.4 %exchange.1 = (f32[448,768]{1,0:T(8,128)S(1)}, f32[448,768]{1,0:T(8,128)}) custom-call(s32[8]{0:T(128)S(1)} %copy-done.5, bf16[2,768,896]{2,1,0:T(8,128)(2,1)S(1)} %multiply.1.refs_1_.half, bf16[896,896]{1,0:T(8,128)(2,1)S(1)} %constant_dynamic-update-slice_fusion.10.first, bf16[896,896]{1,0:T(8,128)(2,1)S(1)} %constant_dynamic-update-slice_fusion.4.second), custom_call_target="tpu_custom_call" | custom-call | flops 2466250752 | bytes 8388608 | tf_op jit(solution)/shard_map/exchange/pallas_call | solution.py:290
  205.9 5.0 %collective-permute-start.39 = (f32[448,768]{1,0:T(8,128)}, f32[448,768]{1,0:T(8,128)S(1)}, u32[]{:S(2)}, u32[]{:S(2)}) collective-permute-start(f32[448,768]{1,0:T(8,128)} %get-tuple-element.60), channel_id=1, source_target_pairs={{0,8},{1,9},{2,10},{3,11},{4,12},{5,13},{6,14},{7,15},{8,0},{9,1},... | collective-permute-start | bytes 4128776 | tf_op jit(solution)/shard_map/ppermute | solution.py:67
  210.8 3.0 %collective-permute-done.39 = f32[448,768]{1,0:T(8,128)S(1)} collective-permute-done((f32[448,768]{1,0:T(8,128)}, f32[448,768]{1,0:T(8,128)S(1)}, u32[]{:S(2)}, u32[]{:S(2)}) %collective-permute-start.39) | collective-permute-done | bytes 1376288 | tf_op jit(solution)/shard_map/ppermute | solution.py:67
  213.8 1.5 add.426
  215.5 3.3 %collective-permute-start.41 = (bf16[112,768]{1,0:T(8,128)(2,1)S(1)}, bf16[112,768]{1,0:T(8,128)(2,1)S(1)}, u32[]{:S(2)}, u32[]{:S(2)}) collective-permute-start(bf16[112,768]{1,0:T(8,128)(2,1)S(1)} %get-tuple-element.71), channel_id=1, source_target_pairs={{0,96},{1,97},{2,98},{3,99},{4,100},{5,101},{6,102},{7,103},{8,40}... | collective-permute-start | bytes 516104 | tf_op jit(solution)/shard_map/ppermute | solution.py:67
  219.3 3.2 %collective-permute-done.42 = bf16[112,768]{1,0:T(8,128)(2,1)S(1)} collective-permute-done((bf16[112,768]{1,0:T(8,128)(2,1)S(1)}, bf16[112,768]{1,0:T(8,128)(2,1)S(1)}, u32[]{:S(2)}, u32[]{:S(2)}) %collective-permute-start.42) | collective-permute-done | bytes 172064 | tf_op jit(solution)/shard_map/ppermute | solution.py:67
  222.6 3.1 %collective-permute-done.41 = bf16[112,768]{1,0:T(8,128)(2,1)S(1)} collective-permute-done((bf16[112,768]{1,0:T(8,128)(2,1)S(1)}, bf16[112,768]{1,0:T(8,128)(2,1)S(1)}, u32[]{:S(2)}, u32[]{:S(2)}) %collective-permute-start.41) | collective-permute-done | bytes 172064 | tf_op jit(solution)/shard_map/ppermute | solution.py:67
  226.7 1.6 collective-permute-start.43
  228.3 8.4 %collective-permute-done.43 = f32[112,768]{1,0:T(8,128)S(1)} collective-permute-done((f32[112,768]{1,0:T(8,128)S(1)}, f32[112,768]{1,0:T(8,128)S(1)}, u32[]{:S(2)}, u32[]{:S(2)}) %collective-permute-start.43) | collective-permute-done | bytes 344096 | tf_op jit(solution)/shard_map/ppermute | solution.py:67
  236.8 3.9 %collective-permute-start.44 = (bf16[112,768]{1,0:T(8,128)(2,1)S(1)}, bf16[112,768]{1,0:T(8,128)(2,1)S(1)}, u32[]{:S(2)}, u32[]{:S(2)}) collective-permute-start(bf16[112,768]{1,0:T(8,128)(2,1)S(1)} %get-tuple-element.62), channel_id=1, source_target_pairs={{0,32},{1,33},{2,34},{3,35},{4,36},{5,37},{6,38},{7,39},{8,104},{9... | collective-permute-start | bytes 516104 | tf_op jit(solution)/shard_map/ppermute | solution.py:67
  240.7 1.3 collective-permute-start.46
  243.0 7.6 %collective-permute-done.45 = bf16[112,768]{1,0:T(8,128)(2,1)S(1)} collective-permute-done((bf16[112,768]{1,0:T(8,128)(2,1)S(1)}, bf16[112,768]{1,0:T(8,128)(2,1)S(1)}, u32[]{:S(2)}, u32[]{:S(2)}) %collective-permute-start.45) | collective-permute-done | bytes 172064 | tf_op jit(solution)/shard_map/ppermute | solution.py:67
  251.1 1.8 collective-permute-done.47
  253.0 1.6 convert_bitcast_fusion
  (135 shorter events, 28.5 us)
Async XLA Ops:
  0.0 16.9 %collective-permute-start.4 = (bf16[96,128,128]{2,1,0:T(8,128)(2,1)}, bf16[96,128,128]{2,1,0:T(8,128)(2,1)}, u32[]{:S(2)}, u32[]{:S(2)}) collective-permute-start(bf16[96,128,128]{2,1,0:T(8,128)(2,1)} %bitcast.123), channel_id=1, source_target_pairs={{0,8},{1,9},{2,10},{3,11},{4,12},{5,13},{6,14},{7,15},{8,0},{9,1},... | collective-permute-start | bytes 9437192 | tf_op jit(solution)/shard_map/ppermute | solution.py:67
  2.3 4.5 %collective-permute-start = (bf16[48,800]{1,0:T(8,128)(2,1)S(1)}, bf16[48,800]{1,0:T(8,128)(2,1)S(1)}, u32[]{:S(2)}, u32[]{:S(2)}) collective-permute-start(bf16[48,800]{1,0:T(8,128)(2,1)S(1)} %broadcast_select_fusion.2), channel_id=1, source_target_pairs={{0,8},{1,9},{2,10},{3,11},{4,12},{5,13},{6,14},{7,15},{8,0},{9,1},... | collective-permute-start | bytes 230408 | tf_op jit(solution)/shard_map/ppermute | solution.py:67
  4.5 4.8 %collective-permute-start.5 = (s32[1,256]{1,0:T(1,128)S(1)}, s32[1,256]{1,0:T(1,128)S(1)}, u32[]{:S(2)}, u32[]{:S(2)}) collective-permute-start(s32[1,256]{1,0:T(1,128)S(1)} %bitcast.127), channel_id=1, source_target_pairs={{0,8},{1,9},{2,10},{3,11},{4,12},{5,13},{6,14},{7,15},{8,0},{9,1},... | collective-permute-start | bytes 3080 | tf_op jit(solution)/shard_map/ppermute | solution.py:67
  5.1 85.7 %copy-start.2 = (s32[8]{0:T(128)}, s32[8]{0:T(128)S(1)}, u32[]{:S(2)}) copy-start(s32[8]{0:T(128)S(1)} %stack.53.place.refs_0_) | copy-start | bytes 100
  7.8 6.0 %collective-permute-start.1 = (bf16[2,48,896]{2,1,0:T(8,128)(2,1)S(1)}, bf16[2,48,896]{2,1,0:T(8,128)(2,1)S(1)}, u32[]{:S(2)}, u32[]{:S(2)}) collective-permute-start(bf16[2,48,896]{2,1,0:T(8,128)(2,1)S(1)} %fusion.12), channel_id=1, source_target_pairs={{0,2},{1,3},{2,4},{3,5},{4,6},{5,7},{6,0},{7,1},{8,40},{9,41},{10,... | collective-permute-start | bytes 516104 | tf_op jit(solution)/shard_map/ppermute | solution.py:67
  9.2 4.6 %collective-permute-start.2 = (bf16[2,48,896]{2,1,0:T(8,128)(2,1)S(1)}, bf16[2,48,896]{2,1,0:T(8,128)(2,1)S(1)}, u32[]{:S(2)}, u32[]{:S(2)}) collective-permute-start(bf16[2,48,896]{2,1,0:T(8,128)(2,1)S(1)} %fusion.12), channel_id=1, source_target_pairs={{0,6},{1,7},{2,0},{3,1},{4,2},{5,3},{6,4},{7,5},{8,104},{9,105},{1... | collective-permute-start | bytes 516104 | tf_op jit(solution)/shard_map/ppermute | solution.py:67
  10.8 6.1 %collective-permute-start.3 = (bf16[2,48,896]{2,1,0:T(8,128)(2,1)S(1)}, bf16[2,48,896]{2,1,0:T(8,128)(2,1)S(1)}, u32[]{:S(2)}, u32[]{:S(2)}) collective-permute-start(bf16[2,48,896]{2,1,0:T(8,128)(2,1)S(1)} %fusion.12), channel_id=1, source_target_pairs={{0,4},{1,5},{2,6},{3,7},{4,0},{5,1},{6,2},{7,3},{8,72},{9,73},{10,... | collective-permute-start | bytes 516104 | tf_op jit(solution)/shard_map/ppermute | solution.py:67
  16.9 11.8 %collective-permute-start.6 = (bf16[2,4,32,896]{3,2,1,0:T(8,128)(2,1)S(1)}, bf16[2,4,32,896]{3,2,1,0:T(8,128)(2,1)S(1)}, u32[]{:S(2)}, u32[]{:S(2)}) collective-permute-start(bf16[2,4,32,896]{3,2,1,0:T(8,128)(2,1)S(1)} %slice.48), channel_id=1, source_target_pairs={{0,1},{1,16},{2,3},{3,18},{4,5},{5,20},{6,7},{7,22},{8,25},{9,8},{... | collective-permute-start | bytes 1376264 | tf_op jit(solution)/shard_map/ppermute | solution.py:67
  20.7 14.9 %collective-permute-start.7 = (bf16[2,4,32,896]{3,2,1,0:T(8,128)(2,1)S(1)}, bf16[2,4,32,896]{3,2,1,0:T(8,128)(2,1)S(1)}, u32[]{:S(2)}, u32[]{:S(2)}) collective-permute-start(bf16[2,4,32,896]{3,2,1,0:T(8,128)(2,1)S(1)} %slice.48), channel_id=1, source_target_pairs={{0,17},{1,0},{2,19},{3,2},{4,21},{5,4},{6,23},{7,6},{8,9},{9,24},{... | collective-permute-start | bytes 1376264 | tf_op jit(solution)/shard_map/ppermute | solution.py:67
  21.0 6.4 %collective-permute-start.11 = (bf16[2,4,16,896]{3,2,1,0:T(8,128)(2,1)S(1)}, bf16[2,4,16,896]{3,2,1,0:T(8,128)(2,1)S(1)}, u32[]{:S(2)}, u32[]{:S(2)}) collective-permute-start(bf16[2,4,16,896]{3,2,1,0:T(8,128)(2,1)S(1)} %slice.56), channel_id=1, source_target_pairs={{0,32},{1,33},{2,34},{3,35},{4,36},{5,37},{6,38},{7,39},{8,10},{9,... | collective-permute-start | bytes 688136 | tf_op jit(solution)/shard_map/ppermute | solution.py:67
  22.0 5.5 %collective-permute-start.16 = (bf16[2,4,16,896]{3,2,1,0:T(8,128)(2,1)S(1)}, bf16[2,4,16,896]{3,2,1,0:T(8,128)(2,1)S(1)}, u32[]{:S(2)}, u32[]{:S(2)}) collective-permute-start(bf16[2,4,16,896]{3,2,1,0:T(8,128)(2,1)S(1)} %slice.56), channel_id=1, source_target_pairs={{0,96},{1,97},{2,98},{3,99},{4,100},{5,101},{6,102},{7,103},{8,14}... | collective-permute-start | bytes 688136 | tf_op jit(solution)/shard_map/ppermute | solution.py:67
  28.8 10.6 %collective-permute-start.8 = (bf16[2,4,32,896]{3,2,1,0:T(8,128)(2,1)S(1)}, bf16[2,4,32,896]{3,2,1,0:T(8,128)(2,1)S(1)}, u32[]{:S(2)}, u32[]{:S(2)}) collective-permute-start(bf16[2,4,32,896]{3,2,1,0:T(8,128)(2,1)S(1)} %collective-permute-done.6), channel_id=1, source_target_pairs={{0,1},{1,16},{2,3},{3,18},{4,5},{5,20},{6,7},{7,22},{8,25},{9,8},{... | collective-permute-start | bytes 1376264 | tf_op jit(solution)/shard_map/ppermute | solution.py:67
  32.2 7.1 %collective-permute-start.14 = (bf16[2,4,16,896]{3,2,1,0:T(8,128)(2,1)S(1)}, bf16[2,4,16,896]{3,2,1,0:T(8,128)(2,1)S(1)}, u32[]{:S(2)}, u32[]{:S(2)}) collective-permute-start(bf16[2,4,16,896]{3,2,1,0:T(8,128)(2,1)S(1)} %slice.56), channel_id=1, source_target_pairs={{0,64},{1,65},{2,66},{3,67},{4,68},{5,69},{6,70},{7,71},{8,12},{9,... | collective-permute-start | bytes 688136 | tf_op jit(solution)/shard_map/ppermute | solution.py:67
  39.3 14.9 %collective-permute-start.17 = (bf16[2,4,4,16,896]{4,3,2,1,0:T(8,128)(2,1)S(1)}, bf16[2,4,4,16,896]{4,3,2,1,0:T(8,128)(2,1)S(1)}, u32[]{:S(2)}, u32[]{:S(2)}) collective-permute-start(bf16[2,4,4,16,896]{4,3,2,1,0:T(8,128)(2,1)S(1)} %bitcast_dynamic-update-slice_fusion.15), channel_id=1, source_target_pairs={{0,1},{1,16},{2,3},{3,18},{4,5},{5,20},{6,7},{7,22},{8,25},{9,8},{... | collective-permute-start | bytes 2752520 | tf_op jit(solution)/shard_map/ppermute | solution.py:67
  39.5 14.9 %collective-permute-start.9 = (bf16[2,2,4,32,896]{4,3,2,1,0:T(8,128)(2,1)S(1)}, bf16[2,2,4,32,896]{4,3,2,1,0:T(8,128)(2,1)S(1)}, u32[]{:S(2)}, u32[]{:S(2)}) collective-permute-start(bf16[2,2,4,32,896]{4,3,2,1,0:T(8,128)(2,1)S(1)} %get-tuple-element.38), channel_id=1, source_target_pairs={{0,32},{1,33},{2,34},{3,35},{4,36},{5,37},{6,38},{7,39},{8,10},{9,... | collective-permute-start | bytes 2752520 | tf_op jit(solution)/shard_map/ppermute | solution.py:67
  40.5 18.9 %collective-permute-start.12 = (bf16[2,2,4,32,896]{4,3,2,1,0:T(8,128)(2,1)S(1)}, bf16[2,2,4,32,896]{4,3,2,1,0:T(8,128)(2,1)S(1)}, u32[]{:S(2)}, u32[]{:S(2)}) collective-permute-start(bf16[2,2,4,32,896]{4,3,2,1,0:T(8,128)(2,1)S(1)} %get-tuple-element.43), channel_id=1, source_target_pairs={{0,96},{1,97},{2,98},{3,99},{4,100},{5,101},{6,102},{7,103},{8,14}... | collective-permute-start | bytes 2752520 | tf_op jit(solution)/shard_map/ppermute | solution.py:67
  42.9 22.7 %collective-permute-start.19 = (bf16[2,4,4,16,896]{4,3,2,1,0:T(8,128)(2,1)S(1)}, bf16[2,4,4,16,896]{4,3,2,1,0:T(8,128)(2,1)S(1)}, u32[]{:S(2)}, u32[]{:S(2)}) collective-permute-start(bf16[2,4,4,16,896]{4,3,2,1,0:T(8,128)(2,1)S(1)} %bitcast_dynamic-update-slice_fusion.15), channel_id=1, source_target_pairs={{0,17},{1,0},{2,19},{3,2},{4,21},{5,4},{6,23},{7,6},{8,9},{9,24},{... | collective-permute-start | bytes 2752520 | tf_op jit(solution)/shard_map/ppermute | solution.py:67
  44.7 22.2 %collective-permute-start.15 = (bf16[2,2,4,32,896]{4,3,2,1,0:T(8,128)(2,1)S(1)}, bf16[2,2,4,32,896]{4,3,2,1,0:T(8,128)(2,1)S(1)}, u32[]{:S(2)}, u32[]{:S(2)}) collective-permute-start(bf16[2,2,4,32,896]{4,3,2,1,0:T(8,128)(2,1)S(1)} %get-tuple-element.43), channel_id=1, source_target_pairs={{0,32},{1,33},{2,34},{3,35},{4,36},{5,37},{6,38},{7,39},{8,10},{9,... | collective-permute-start | bytes 2752520 | tf_op jit(solution)/shard_map/ppermute | solution.py:67
  54.3 15.4 %collective-permute-start.10 = (bf16[2,2,4,32,896]{4,3,2,1,0:T(8,128)(2,1)S(1)}, bf16[2,2,4,32,896]{4,3,2,1,0:T(8,128)(2,1)S(1)}, u32[]{:S(2)}, u32[]{:S(2)}) collective-permute-start(bf16[2,2,4,32,896]{4,3,2,1,0:T(8,128)(2,1)S(1)} %get-tuple-element.38), channel_id=1, source_target_pairs={{0,96},{1,97},{2,98},{3,99},{4,100},{5,101},{6,102},{7,103},{8,14}... | collective-permute-start | bytes 2752520 | tf_op jit(solution)/shard_map/ppermute | solution.py:67
  59.4 14.2 %collective-permute-start.13 = (bf16[2,2,4,32,896]{4,3,2,1,0:T(8,128)(2,1)S(1)}, bf16[2,2,4,32,896]{4,3,2,1,0:T(8,128)(2,1)S(1)}, u32[]{:S(2)}, u32[]{:S(2)}) collective-permute-start(bf16[2,2,4,32,896]{4,3,2,1,0:T(8,128)(2,1)S(1)} %collective-permute-done.9), channel_id=1, source_target_pairs={{0,32},{1,33},{2,34},{3,35},{4,36},{5,37},{6,38},{7,39},{8,10},{9,... | collective-permute-start | bytes 2752520 | tf_op jit(solution)/shard_map/ppermute | solution.py:67
  59.4 20.2 %collective-permute-start.18 = (bf16[2,2,4,32,896]{4,3,2,1,0:T(8,128)(2,1)S(1)}, bf16[2,2,4,32,896]{4,3,2,1,0:T(8,128)(2,1)S(1)}, u32[]{:S(2)}, u32[]{:S(2)}) collective-permute-start(bf16[2,2,4,32,896]{4,3,2,1,0:T(8,128)(2,1)S(1)} %collective-permute-done.12), channel_id=1, source_target_pairs={{0,96},{1,97},{2,98},{3,99},{4,100},{5,101},{6,102},{7,103},{8,14}... | collective-permute-start | bytes 2752520 | tf_op jit(solution)/shard_map/ppermute | solution.py:67
  65.6 14.1 %collective-permute-start.20 = (bf16[2,4,4,16,896]{4,3,2,1,0:T(8,128)(2,1)S(1)}, bf16[2,4,4,16,896]{4,3,2,1,0:T(8,128)(2,1)S(1)}, u32[]{:S(2)}, u32[]{:S(2)}) collective-permute-start(bf16[2,4,4,16,896]{4,3,2,1,0:T(8,128)(2,1)S(1)} %collective-permute-done.17), channel_id=1, source_target_pairs={{0,1},{1,16},{2,3},{3,18},{4,5},{5,20},{6,7},{7,22},{8,25},{9,8},{... | collective-permute-start | bytes 2752520 | tf_op jit(solution)/shard_map/ppermute | solution.py:67
  79.9 10.9 %copy-start.6 = (bf16[1,96,128,128]{3,2,1,0:T(8,128)(2,1)S(1)}, bf16[1,96,128,128]{3,2,1,0:T(8,128)(2,1)}, u32[]{:S(2)}) copy-start(bf16[1,96,128,128]{3,2,1,0:T(8,128)(2,1)} %param.6) | copy-start | bytes 9437188
  81.3 26.6 %collective-permute-start.21 = (bf16[768,896]{1,0:T(8,128)(2,1)S(1)}, bf16[768,896]{1,0:T(8,128)(2,1)S(1)}, u32[]{:S(2)}, u32[]{:S(2)}) collective-permute-start(bf16[768,896]{1,0:T(8,128)(2,1)S(1)} %bitcast.120), channel_id=1, source_target_pairs={{0,8},{1,9},{2,10},{3,11},{4,12},{5,13},{6,14},{7,15},{8,0},{9,1},... | collective-permute-start | bytes 4128776 | tf_op jit(solution)/shard_map/ppermute | solution.py:67
  108.0 0.7 copy-start.3
  108.6 3.3 %copy-start.4 = (s32[8]{0:T(128)S(1)}, s32[8]{0:T(128)}, u32[]{:S(2)}) copy-start(s32[8]{0:T(128)} %copy-done.2) | copy-start | bytes 100
  111.9 19.8 %collective-permute-start.25 = (bf16[448,896]{1,0:T(8,128)(2,1)}, bf16[448,896]{1,0:T(8,128)(2,1)}, u32[]{:S(2)}, u32[]{:S(2)}) collective-permute-start(bf16[448,896]{1,0:T(8,128)(2,1)} %get-tuple-element.54), channel_id=1, source_target_pairs={{0,1},{1,0},{2,3},{3,2},{4,5},{5,4},{6,7},{7,6},{8,9},{9,8},{10,11... | collective-permute-start | bytes 2408456 | tf_op jit(solution)/shard_map/ppermute | solution.py:67
  115.3 0.7 copy-start.1
  116.0 17.0 %collective-permute-start.22 = (bf16[224,896]{1,0:T(8,128)(2,1)}, bf16[224,896]{1,0:T(8,128)(2,1)}, u32[]{:S(2)}, u32[]{:S(2)}) collective-permute-start(bf16[224,896]{1,0:T(8,128)(2,1)} %get-tuple-element.50), channel_id=1, source_target_pairs={{0,2},{1,3},{2,4},{3,5},{4,6},{5,7},{6,0},{7,1},{8,14},{9,15},{10,... | collective-permute-start | bytes 1204232 | tf_op jit(solution)/shard_map/ppermute | solution.py:67
  118.4 14.6 %collective-permute-start.23 = (bf16[224,896]{1,0:T(8,128)(2,1)}, bf16[224,896]{1,0:T(8,128)(2,1)}, u32[]{:S(2)}, u32[]{:S(2)}) collective-permute-start(bf16[224,896]{1,0:T(8,128)(2,1)} %get-tuple-element.51), channel_id=1, source_target_pairs={{0,6},{1,7},{2,0},{3,1},{4,2},{5,3},{6,4},{7,5},{8,10},{9,11},{10,... | collective-permute-start | bytes 1204232 | tf_op jit(solution)/shard_map/ppermute | solution.py:67
  118.4 21.3 %collective-permute-start.24 = (bf16[224,896]{1,0:T(8,128)(2,1)}, bf16[224,896]{1,0:T(8,128)(2,1)}, u32[]{:S(2)}, u32[]{:S(2)}) collective-permute-start(bf16[224,896]{1,0:T(8,128)(2,1)} %get-tuple-element.52), channel_id=1, source_target_pairs={{0,4},{1,5},{2,6},{3,7},{4,0},{5,1},{6,2},{7,3},{8,12},{9,13},{10,... | collective-permute-start | bytes 1204232 | tf_op jit(solution)/shard_map/ppermute | solution.py:67
  133.0 10.7 %copy-start.7 = (bf16[448,896]{1,0:T(8,128)(2,1)}, bf16[448,896]{1,0:T(8,128)(2,1)S(1)}, u32[]{:S(2)}) copy-start(bf16[448,896]{1,0:T(8,128)(2,1)S(1)} %add_convert_fusion) | copy-start | bytes 2408452
  141.9 7.4 %collective-permute-start.26 = (bf16[112,896]{1,0:T(8,128)(2,1)}, bf16[112,896]{1,0:T(8,128)(2,1)S(1)}, u32[]{:S(2)}, u32[]{:S(2)}) collective-permute-start(bf16[112,896]{1,0:T(8,128)(2,1)} %constant_dynamic-slice_fusion.3), channel_id=1, source_target_pairs={{0,1},{1,0},{2,3},{3,2},{4,5},{5,4},{6,7},{7,6},{8,9},{9,8},{10,11... | collective-permute-start | bytes 602120 | tf_op jit(solution)/shard_map/ppermute | solution.py:67
  144.5 8.2 %collective-permute-start.29 = (bf16[112,896]{1,0:T(8,128)(2,1)}, bf16[112,896]{1,0:T(8,128)(2,1)S(1)}, u32[]{:S(2)}, u32[]{:S(2)}) collective-permute-start(bf16[112,896]{1,0:T(8,128)(2,1)} %get-tuple-element.73), channel_id=1, source_target_pairs={{0,4},{1,5},{2,6},{3,7},{4,0},{5,1},{6,2},{7,3},{8,12},{9,13},{10,... | collective-permute-start | bytes 602120 | tf_op jit(solution)/shard_map/ppermute | solution.py:67
  144.7 12.3 %collective-permute-start.28 = (bf16[112,896]{1,0:T(8,128)(2,1)}, bf16[112,896]{1,0:T(8,128)(2,1)}, u32[]{:S(2)}, u32[]{:S(2)}) collective-permute-start(bf16[112,896]{1,0:T(8,128)(2,1)} %get-tuple-element.74), channel_id=1, source_target_pairs={{0,6},{1,7},{2,0},{3,1},{4,2},{5,3},{6,4},{7,5},{8,10},{9,11},{10,... | collective-permute-start | bytes 602120 | tf_op jit(solution)/shard_map/ppermute | solution.py:67
  144.7 12.3 %collective-permute-start.27 = (bf16[112,896]{1,0:T(8,128)(2,1)}, bf16[112,896]{1,0:T(8,128)(2,1)}, u32[]{:S(2)}, u32[]{:S(2)}) collective-permute-start(bf16[112,896]{1,0:T(8,128)(2,1)} %get-tuple-element.72), channel_id=1, source_target_pairs={{0,2},{1,3},{2,4},{3,5},{4,6},{5,7},{6,0},{7,1},{8,14},{9,15},{10,... | collective-permute-start | bytes 602120 | tf_op jit(solution)/shard_map/ppermute | solution.py:67
  149.3 7.7 %copy-start.9 = (bf16[112,896]{1,0:T(8,128)(2,1)}, bf16[112,896]{1,0:T(8,128)(2,1)S(1)}, u32[]{:S(2)}) copy-start(bf16[112,896]{1,0:T(8,128)(2,1)S(1)} %collective-permute-done.26) | copy-start | bytes 602116
  152.7 4.4 %copy-start.10 = (bf16[112,896]{1,0:T(8,128)(2,1)}, bf16[112,896]{1,0:T(8,128)(2,1)S(1)}, u32[]{:S(2)}) copy-start(bf16[112,896]{1,0:T(8,128)(2,1)S(1)} %collective-permute-done.29) | copy-start | bytes 602116
  159.3 2.4 collective-permute-start.30
  161.8 0.8 copy-start.8
  165.3 6.2 %collective-permute-start.31 = (bf16[112,896]{1,0:T(8,128)(2,1)S(1)}, bf16[112,896]{1,0:T(8,128)(2,1)S(1)}, u32[]{:S(2)}, u32[]{:S(2)}) collective-permute-start(bf16[112,896]{1,0:T(8,128)(2,1)S(1)} %get-tuple-element.82), channel_id=1, source_target_pairs={{0,2},{1,3},{2,4},{3,5},{4,6},{5,7},{6,0},{7,1},{8,14},{9,15},{10,... | collective-permute-start | bytes 602120 | tf_op jit(solution)/shard_map/ppermute | solution.py:67
  165.7 12.2 %collective-permute-start.32 = (bf16[112,896]{1,0:T(8,128)(2,1)S(1)}, bf16[112,896]{1,0:T(8,128)(2,1)S(1)}, u32[]{:S(2)}, u32[]{:S(2)}) collective-permute-start(bf16[112,896]{1,0:T(8,128)(2,1)S(1)} %get-tuple-element.82), channel_id=1, source_target_pairs={{0,6},{1,7},{2,0},{3,1},{4,2},{5,3},{6,4},{7,5},{8,10},{9,11},{10,... | collective-permute-start | bytes 602120 | tf_op jit(solution)/shard_map/ppermute | solution.py:67
  166.7 11.2 %collective-permute-start.33 = (bf16[112,896]{1,0:T(8,128)(2,1)S(1)}, bf16[112,896]{1,0:T(8,128)(2,1)S(1)}, u32[]{:S(2)}, u32[]{:S(2)}) collective-permute-start(bf16[112,896]{1,0:T(8,128)(2,1)S(1)} %get-tuple-element.82), channel_id=1, source_target_pairs={{0,4},{1,5},{2,6},{3,7},{4,0},{5,1},{6,2},{7,3},{8,12},{9,13},{10,... | collective-permute-start | bytes 602120 | tf_op jit(solution)/shard_map/ppermute | solution.py:67
  167.0 11.1 %collective-permute-start.35 = (bf16[112,896]{1,0:T(8,128)(2,1)S(1)}, bf16[112,896]{1,0:T(8,128)(2,1)S(1)}, u32[]{:S(2)}, u32[]{:S(2)}) collective-permute-start(bf16[112,896]{1,0:T(8,128)(2,1)S(1)} %get-tuple-element.64), channel_id=1, source_target_pairs={{0,1},{1,0},{2,3},{3,2},{4,5},{5,4},{6,7},{7,6},{8,9},{9,8},{10,11... | collective-permute-start | bytes 602120 | tf_op jit(solution)/shard_map/ppermute | solution.py:67
  178.0 20.1 %collective-permute-start.34 = (bf16[448,896]{1,0:T(8,128)(2,1)S(1)}, bf16[448,896]{1,0:T(8,128)(2,1)}, u32[]{:S(2)}, u32[]{:S(2)}) collective-permute-start(bf16[448,896]{1,0:T(8,128)(2,1)S(1)} %constant_dynamic-update-slice_fusion.12), channel_id=1, source_target_pairs={{0,1},{1,0},{2,3},{3,2},{4,5},{5,4},{6,7},{7,6},{8,9},{9,8},{10,11... | collective-permute-start | bytes 2408456 | tf_op jit(solution)/shard_map/ppermute | solution.py:67
  178.8 10.1 %collective-permute-start.36 = (bf16[224,896]{1,0:T(8,128)(2,1)}, bf16[224,896]{1,0:T(8,128)(2,1)}, u32[]{:S(2)}, u32[]{:S(2)}) collective-permute-start(bf16[224,896]{1,0:T(8,128)(2,1)} %constant_dynamic-update-slice_fusion.8), channel_id=1, source_target_pairs={{0,2},{1,3},{2,4},{3,5},{4,6},{5,7},{6,0},{7,1},{8,14},{9,15},{10,... | collective-permute-start | bytes 1204232 | tf_op jit(solution)/shard_map/ppermute | solution.py:67
  179.0 13.1 %collective-permute-start.37 = (bf16[224,896]{1,0:T(8,128)(2,1)}, bf16[224,896]{1,0:T(8,128)(2,1)}, u32[]{:S(2)}, u32[]{:S(2)}) collective-permute-start(bf16[224,896]{1,0:T(8,128)(2,1)} %constant_dynamic-update-slice_fusion.8), channel_id=1, source_target_pairs={{0,6},{1,7},{2,0},{3,1},{4,2},{5,3},{6,4},{7,5},{8,10},{9,11},{10,... | collective-permute-start | bytes 1204232 | tf_op jit(solution)/shard_map/ppermute | solution.py:67
  180.3 17.7 %collective-permute-start.38 = (bf16[224,896]{1,0:T(8,128)(2,1)}, bf16[224,896]{1,0:T(8,128)(2,1)S(1)}, u32[]{:S(2)}, u32[]{:S(2)}) collective-permute-start(bf16[224,896]{1,0:T(8,128)(2,1)} %constant_dynamic-update-slice_fusion.8), channel_id=1, source_target_pairs={{0,4},{1,5},{2,6},{3,7},{4,0},{5,1},{6,2},{7,3},{8,12},{9,13},{10,... | collective-permute-start | bytes 1204232 | tf_op jit(solution)/shard_map/ppermute | solution.py:67
  182.2 17.2 %copy-start.5 = (s32[8]{0:T(128)S(1)}, s32[8]{0:T(128)}, u32[]{:S(2)}) copy-start(s32[8]{0:T(128)} %copy-done.2) | copy-start | bytes 100
  204.8 1.1 copy-start
  205.9 7.9 %collective-permute-start.39 = (f32[448,768]{1,0:T(8,128)}, f32[448,768]{1,0:T(8,128)S(1)}, u32[]{:S(2)}, u32[]{:S(2)}) collective-permute-start(f32[448,768]{1,0:T(8,128)} %get-tuple-element.60), channel_id=1, source_target_pairs={{0,8},{1,9},{2,10},{3,11},{4,12},{5,13},{6,14},{7,15},{8,0},{9,1},... | collective-permute-start | bytes 4128776 | tf_op jit(solution)/shard_map/ppermute | solution.py:67
  215.4 7.2 %collective-permute-start.42 = (bf16[112,768]{1,0:T(8,128)(2,1)S(1)}, bf16[112,768]{1,0:T(8,128)(2,1)S(1)}, u32[]{:S(2)}, u32[]{:S(2)}) collective-permute-start(bf16[112,768]{1,0:T(8,128)(2,1)S(1)} %get-tuple-element.70), channel_id=1, source_target_pairs={{0,64},{1,65},{2,66},{3,67},{4,68},{5,69},{6,70},{7,71},{8,72},{9,... | collective-permute-start | bytes 516104 | tf_op jit(solution)/shard_map/ppermute | solution.py:67
  215.5 10.2 %collective-permute-start.41 = (bf16[112,768]{1,0:T(8,128)(2,1)S(1)}, bf16[112,768]{1,0:T(8,128)(2,1)S(1)}, u32[]{:S(2)}, u32[]{:S(2)}) collective-permute-start(bf16[112,768]{1,0:T(8,128)(2,1)S(1)} %get-tuple-element.71), channel_id=1, source_target_pairs={{0,96},{1,97},{2,98},{3,99},{4,100},{5,101},{6,102},{7,103},{8,40}... | collective-permute-start | bytes 516104 | tf_op jit(solution)/shard_map/ppermute | solution.py:67
  218.8 7.9 %collective-permute-start.40 = (bf16[112,768]{1,0:T(8,128)(2,1)S(1)}, bf16[112,768]{1,0:T(8,128)(2,1)S(1)}, u32[]{:S(2)}, u32[]{:S(2)}) collective-permute-start(bf16[112,768]{1,0:T(8,128)(2,1)S(1)} %get-tuple-element.69), channel_id=1, source_target_pairs={{0,32},{1,33},{2,34},{3,35},{4,36},{5,37},{6,38},{7,39},{8,104},{9... | collective-permute-start | bytes 516104 | tf_op jit(solution)/shard_map/ppermute | solution.py:67
  226.7 9.9 %collective-permute-start.43 = (f32[112,768]{1,0:T(8,128)S(1)}, f32[112,768]{1,0:T(8,128)S(1)}, u32[]{:S(2)}, u32[]{:S(2)}) collective-permute-start(f32[112,768]{1,0:T(8,128)S(1)} %add_add_fusion), channel_id=1, source_target_pairs={{0,16},{1,17},{2,18},{3,19},{4,20},{5,21},{6,22},{7,23},{8,24},{9,... | collective-permute-start | bytes 1032200 | tf_op jit(solution)/shard_map/ppermute | solution.py:67
  236.8 6.3 %collective-permute-start.44 = (bf16[112,768]{1,0:T(8,128)(2,1)S(1)}, bf16[112,768]{1,0:T(8,128)(2,1)S(1)}, u32[]{:S(2)}, u32[]{:S(2)}) collective-permute-start(bf16[112,768]{1,0:T(8,128)(2,1)S(1)} %get-tuple-element.62), channel_id=1, source_target_pairs={{0,32},{1,33},{2,34},{3,35},{4,36},{5,37},{6,38},{7,39},{8,104},{9... | collective-permute-start | bytes 516104 | tf_op jit(solution)/shard_map/ppermute | solution.py:67
  240.7 9.9 %collective-permute-start.45 = (bf16[112,768]{1,0:T(8,128)(2,1)S(1)}, bf16[112,768]{1,0:T(8,128)(2,1)S(1)}, u32[]{:S(2)}, u32[]{:S(2)}) collective-permute-start(bf16[112,768]{1,0:T(8,128)(2,1)S(1)} %get-tuple-element.62), channel_id=1, source_target_pairs={{0,96},{1,97},{2,98},{3,99},{4,100},{5,101},{6,102},{7,103},{8,40}... | collective-permute-start | bytes 516104 | tf_op jit(solution)/shard_map/ppermute | solution.py:67
  240.7 9.9 %collective-permute-start.46 = (bf16[112,768]{1,0:T(8,128)(2,1)S(1)}, bf16[112,768]{1,0:T(8,128)(2,1)S(1)}, u32[]{:S(2)}, u32[]{:S(2)}) collective-permute-start(bf16[112,768]{1,0:T(8,128)(2,1)S(1)} %get-tuple-element.62), channel_id=1, source_target_pairs={{0,64},{1,65},{2,66},{3,67},{4,68},{5,69},{6,70},{7,71},{8,72},{9,... | collective-permute-start | bytes 516104 | tf_op jit(solution)/shard_map/ppermute | solution.py:67
  250.6 2.3 collective-permute-start.47

commit v2 on v1

--- a/solution.py
+++ b/solution.py
@@ -17,11 +17,11 @@
 NB = 6144
 NOCC = 800
 WIDE = 896
-SHARD = WIDE // 8
+CROSS = 832
+SHARD = CROSS // 8
 OWN = 48
 STEP = 4
 UNROLL = 3
-FLIGHT = 5
 MAIN = 32
 bf16, f32 = jnp.bfloat16, jnp.float32
 
@@ -79,8 +79,13 @@
     return send(array, permutation(other_high))
 
 
-def slab_kernel(place, main0, main1, rest, out, sems):
-    core, row = place[0], place[1]
+def here():
+    aux, row = lax.axis_index("aux"), lax.axis_index("row")
+    return aux % CORE, row, row // ZL, row % ZL
+
+
+def slab_kernel(main0, main1, rest, out, sems):
+    core, row, _, _ = here()
     copies = []
     for x in range(X):
         a = jnp.where(core == 0, x, row // ZL)
@@ -100,21 +105,21 @@
         copy.wait()
 
 
-def own_slab(place, main0, main1, rest):
+def own_slab(main0, main1, rest):
     return pl.pallas_call(
         slab_kernel,
         out_shape=jax.ShapeDtypeStruct((CORE, X, ZL, OWN, WIDE), bf16),
-        in_specs=[pl.BlockSpec(memory_space=pltpu.SMEM)] + [pl.BlockSpec(memory_space=pl.ANY)] * 3,
+        in_specs=[pl.BlockSpec(memory_space=pl.ANY)] * 3,
         out_specs=pl.BlockSpec(memory_space=pltpu.VMEM),
         scratch_shapes=[pltpu.SemaphoreType.DMA((3 * X,))],
         compiler_params=pltpu.CompilerParams(vmem_limit_bytes=4 * 1024 * 1024),
         name="slab",
-    )(place, main0, main1, rest)
-
-
-def multiply_kernel(place, meta, own_blocks, other_blocks, main0, main1, rest, out, *scratch):
+    )(main0, main1, rest)
+
+
+def multiply_kernel(meta, own_blocks, other_blocks, main0, main1, rest, out, *scratch):
     blocks, held, total, order, counts, steps, sems = scratch
-    core = place[0]
+    core, _, _, _ = here()
     copies = [
         pltpu.make_async_copy(own_blocks, blocks.at[pl.ds(0, SLOTS)], sems.at[0]),
         pltpu.make_async_copy(other_blocks, blocks.at[pl.ds(SLOTS, SLOTS)], sems.at[1]),
@@ -209,12 +214,12 @@
     lax.fori_loop(0, GROUPS, finish, 0)
 
 
-def multiply(place, meta, own_blocks, other_blocks, main0, main1, rest):
+def multiply(meta, own_blocks, other_blocks, main0, main1, rest):
     most = 2 * SLOTS // STEP + GROUPS + UNROLL
     return pl.pallas_call(
         multiply_kernel,
         out_shape=jax.ShapeDtypeStruct((2, ROWS, WIDE), bf16),
-        in_specs=[pl.BlockSpec(memory_space=pltpu.SMEM)] * 2 + [pl.BlockSpec(memory_space=pl.ANY)] * 5,
+        in_specs=[pl.BlockSpec(memory_space=pltpu.SMEM)] + [pl.BlockSpec(memory_space=pl.ANY)] * 5,
         out_specs=pl.BlockSpec(memory_space=pltpu.VMEM),
         scratch_shapes=[
             pltpu.VMEM((2 * SLOTS + 1, BLK, BLK), bf16),
@@ -228,12 +233,12 @@
         compiler_params=pltpu.CompilerParams(vmem_limit_bytes=30 * 1024 * 1024),
         cost_estimate=pl.CostEstimate(flops=2 * 96 * 2 * 128 * 128 * 896, bytes_accessed=2**24, transcendentals=0),
         name="multiply",
-    )(place, meta, own_blocks, other_blocks, main0, main1, rest)
-
-
-def cross_kernel(q, starts, place, half, slab, theirs, *refs):
+    )(meta, own_blocks, other_blocks, main0, main1, rest)
+
+
+def cross_kernel(q, starts, half, slab, theirs, *refs):
     outs, used, product = refs[:-2], refs[-2], refs[-1]
-    core, row = place[0], place[1]
+    core, row, _, _ = here()
     used[...] = jnp.where(core == 0, slab[...], theirs[...])
     product[...] = lax.dot_general(
         half[q], used[...], (((0,), (0,)), ((), ())), preferred_element_type=f32
@@ -248,55 +253,87 @@
         lane == 3 * row, high, jnp.where(lane == 3 * row + 1, middle, jnp.where(lane == 3 * row + 2, low, 0.0))
     )
     product[NOCC : NOCC + 16, :] = jnp.where(line == 0, coded, 0.0).astype(bf16)
-    for out, start in zip(outs, starts):
+    for out, start in zip(outs, starts()):
         n = out.shape[0]
-        out[...] = product[pl.ds(pl.multiple_of(place[start] * n, n), n), :]
-
-
-def cross(q, starts, n, place, half, slab, theirs):
+        out[...] = product[pl.ds(pl.multiple_of(start * n, n), n), :]
+
+
+def chunks_x():
+    core, _, x, _ = here()
+    return x, (x + 1 - 2 * core) % X, (x - 1 + 2 * core) % X, (x + 2) % X
+
+
+def chunks_low():
+    zl = here()[3]
+    return zl, 1 - zl
+
+
+def cross(q, starts, many, half, slab, theirs):
     def kernel(*refs):
         cross_kernel(q, starts, *refs)
 
     return pl.pallas_call(
         kernel,
-        out_shape=[jax.ShapeDtypeStruct((n, WIDE), bf16)] * len(starts),
-        in_specs=[pl.BlockSpec(memory_space=pltpu.SMEM)] + [pl.BlockSpec(memory_space=pltpu.VMEM)] * 3,
-        out_specs=[pl.BlockSpec(memory_space=pltpu.VMEM)] * len(starts),
+        out_shape=[jax.ShapeDtypeStruct((CROSS // many, WIDE), bf16)] * many,
+        in_specs=[pl.BlockSpec(memory_space=pltpu.VMEM)] * 3,
+        out_specs=[pl.BlockSpec(memory_space=pltpu.VMEM)] * many,
         scratch_shapes=[pltpu.VMEM((ROWS, WIDE), bf16), pltpu.VMEM((WIDE, WIDE), bf16)],
         compiler_params=pltpu.CompilerParams(vmem_limit_bytes=30 * 1024 * 1024),
         cost_estimate=pl.CostEstimate(flops=2 * 768 * 896 * 896, bytes_accessed=2**23, transcendentals=0),
         name="cross",
-    )(place, half, slab, theirs)
-
-
-def exchange_kernel(place, half, first, second, keep, give, turned):
-    core = place[0]
+    )(half, slab, theirs)
+
+
+def exchange_kernel(half, *refs):
+    parts, (keep, give, weights, turned, sems) = refs[:6], refs[6:]
+    core, _, _, _ = here()
+    copies = []
+    for i, (q, at) in enumerate([(0, at) for at in chunks_low()] + [(1, at) for at in chunks_arrived()]):
+        n = parts[i].shape[0]
+        into = weights.at[q, pl.ds(pl.multiple_of(at * n, n), n), :]
+        copies.append(pltpu.make_async_copy(parts[i], into, sems.at[i]))
+    for copy in copies:
+        copy.start()
+    for q in range(2):
+        weights[q, CROSS:, :] = jnp.zeros((WIDE - CROSS, WIDE), bf16)
+    for copy in copies:
+        copy.wait()
+    line = lax.broadcasted_iota(jnp.int32, (16, WIDE), 0)
     total = None
-    for q, weight in enumerate((first, second)):
-        line = lax.broadcasted_iota(jnp.int32, (16, WIDE), 0)
-        codes = jnp.where(line < 2, weight[NOCC : NOCC + 16, :].astype(f32), 0.0)
+    for q in range(2):
+        codes = jnp.where(line == 0, weights[q, NOCC : NOCC + 16, :].astype(f32), 0.0)
+        codes = codes + jnp.where(line == 1, weights[1 - q, NOCC : NOCC + 16, :].astype(f32), 0.0)
         coulomb = jnp.sum(codes, keepdims=True) * (1.0 / NB)
         factor = jnp.where(core == 0, 2.0 * coulomb, 0.0)
         own = half[q]
-        term = factor * own.astype(f32) - jnp.dot(own, weight[...], preferred_element_type=f32)
+        term = factor * own.astype(f32) - jnp.dot(own, weights[q], preferred_element_type=f32)
         total = term if total is None else total + term
     turned[...] = total.T
-    n = WIDE // 2
+    n = CROSS // 2
     keep[...] = turned[pl.ds(pl.multiple_of(core * n, n), n), :]
     give[...] = turned[pl.ds(pl.multiple_of((1 - core) * n, n), n), :]
 
 
-def exchange(place, half, first, second):
+def chunks_arrived():
+    x, ahead, behind, far = chunks_x()
+    return x, behind, ahead, far
+
+
+def exchange(half, low_parts, x_parts):
     return pl.pallas_call(
         exchange_kernel,
-        out_shape=[jax.ShapeDtypeStruct((WIDE // 2, ROWS), f32)] * 2,
-        in_specs=[pl.BlockSpec(memory_space=pltpu.SMEM)] + [pl.BlockSpec(memory_space=pltpu.VMEM)] * 3,
+        out_shape=[jax.ShapeDtypeStruct((CROSS // 2, ROWS), f32)] * 2,
+        in_specs=[pl.BlockSpec(memory_space=pltpu.VMEM)] + [pl.BlockSpec(memory_space=pl.ANY)] * 6,
         out_specs=[pl.BlockSpec(memory_space=pltpu.VMEM)] * 2,
-        scratch_shapes=[pltpu.VMEM((WIDE, ROWS), f32)],
+        scratch_shapes=[
+            pltpu.VMEM((2, WIDE, WIDE), bf16),
+            pltpu.VMEM((WIDE, ROWS), f32),
+            pltpu.SemaphoreType.DMA((6,)),
+        ],
         compiler_params=pltpu.CompilerParams(vmem_limit_bytes=36 * 1024 * 1024),
         cost_estimate=pl.CostEstimate(flops=4 * 768 * 896 * 896, bytes_accessed=2**23, transcendentals=0),
         name="exchange",
-    )(place, half, first, second)
+    )(half, *low_parts, *x_parts)
 
 
 def local(factors, block_rows, block_cols, block_count, orbitals, response):
@@ -310,14 +347,8 @@
     def choose(a, b):
         return jnp.where(first, a, b)
 
-    flying = []
-
-    def send_next(array, pairs):
-        if len(flying) >= FLIGHT:
-            array, _ = lax.optimization_barrier((array, flying[-FLIGHT]))
-        got = send(array, pairs)
-        flying.append(got)
-        return got
+    def send_after(array, pairs, *earlier):
+        return send(lax.optimization_barrier((array, *earlier))[0], pairs)
 
     def put(into, array, **at):
         index = [jnp.int32(0)] * into.ndim
@@ -327,7 +358,7 @@
 
     got = send(choose(response, orbitals), permutation(other_core))
     own_blocks = factors[0]
-    other_blocks = swap_cores(own_blocks)
+    other_blocks = send_after(own_blocks, permutation(other_core), got)
     both = jnp.stack([choose(orbitals, got), choose(got, response)])
     both = jnp.pad(both, ((0, 0), (0, 0), (0, WIDE - NOCC)))
 
@@ -335,13 +366,12 @@
     at_one, at_two = choose(x, y), choose(y, x)
     shape = (CORE, 4, OWN, WIDE)
     stage = put(jnp.zeros(shape, bf16), both[:, None], d1=at_one)
-    ahead = send_next(both, around(one, 1, False))
-    behind = send_next(both, around(one, -1, False))
-    far = send_next(both, around(one, 2, False))
+    ahead = send(both, around(one, 1, False))
+    behind = send(both, around(one, -1, False))
+    far = send(both, around(one, 2, False))
     lists = jnp.concatenate([block_rows[0] % ROW_BLOCKS, block_cols[0], block_count[0]])
     lists = jnp.pad(lists, (0, 256 - 2 * SLOTS - 1))[None]
     meta = jnp.concatenate([lists, swap_cores(lists)])
-    place = jnp.stack([c, row, x, (x + sign) % 4, (x - sign) % 4, (x + 2) % 4, zl, 1 - zl]).astype(jnp.int32)
     stage = put(stage, ahead[:, None], d1=(at_one - 1) % 4)
     stage = put(stage, behind[:, None], d1=(at_one + 1) % 4)
     stage = put(stage, far[:, None], d1=(at_one + 2) % 4)
@@ -349,12 +379,12 @@
 
     main, rest = stage[:, :, :MAIN], stage[:, :, MAIN:]
     zz = ("z", "z")
-    main_ahead = send_next(main, around(zz, 1, True))
-    main_behind = send_next(main, around(zz, -1, True))
-    rest_ahead = send_next(rest, around(two, 1, False))
-    rest_behind = send_next(rest, around(two, -1, False))
-    main_far = send_next(main_ahead, around(zz, 1, True))
-    rest_far = send_next(rest, around(two, 2, False))
+    main_ahead = send(main, around(zz, 1, True))
+    rest_ahead = send(rest, around(two, 1, False))
+    rest_behind = send(rest, around(two, -1, False))
+    main_far = send(main_ahead, around(zz, 1, True))
+    main_behind = send_after(main, around(zz, -1, True), main_ahead)
+    rest_far = send_after(rest, around(two, 2, False), rest_ahead)
 
     mains = [jnp.zeros((ZH, ZL, 4, MAIN, WIDE), bf16)] * 2
     for array, at in (
@@ -375,15 +405,16 @@
     rest = into
 
     ahead, behind = around(two, 1, False), around(two, -1, False)
-    ahead_0 = send_next(mains[0], ahead)
-    behind_1 = send_next(mains[1], behind)
-    rest_ahead = send_next(rest, around(zz, 1, True))
-    rest_behind = send_next(rest, around(zz, -1, True))
-    ahead_1 = send_next(mains[1], ahead)
-    behind_0 = send_next(mains[0], behind)
-    far_0 = send_next(ahead_0, ahead)
-    far_1 = send_next(behind_1, behind)
-    rest_far = send_next(rest_ahead, around(zz, 1, True))
+    mains, rest = lax.optimization_barrier((mains, rest))
+    ahead_0 = send(mains[0], ahead)
+    behind_1 = send(mains[1], behind)
+    rest_ahead = send(rest, around(zz, 1, True))
+    rest_behind = send(rest, around(zz, -1, True))
+    ahead_1 = send_after(mains[1], ahead, ahead_0)
+    behind_0 = send_after(mains[0], behind, behind_1)
+    far_0 = send(ahead_0, ahead)
+    far_1 = send_after(behind_1, behind, rest_ahead)
+    rest_far = send_after(rest_ahead, around(zz, 1, True), rest_behind)
     arrays = (
         (mains[0], ahead_0, behind_0, far_0),
         (mains[1], ahead_1, behind_1, far_1),
@@ -404,9 +435,9 @@
         into = put(into, array[None, :, None], d0=at // ZL, d2=at % ZL)
     rest = into
 
-    slab = own_slab(place, *mains, rest).reshape(ROWS, WIDE)
+    slab = own_slab(*mains, rest).reshape(ROWS, WIDE)
     theirs = swap_cores(slab)
-    half = multiply(place, meta, own_blocks, other_blocks, *mains, rest)
+    half = multiply(meta, own_blocks, other_blocks, *mains, rest)
 
     def add(*arrays):
         return sum(a.astype(f32) for a in arrays)
@@ -417,9 +448,9 @@
     xx = ("x", "x")
     ahead, behind = around(xx, 1, True), around(xx, -1, True)
     opposite = around(xx, 2, True)
-    half_mine, to_low = cross(1, (6, 7), WIDE // 2, place, half, slab, theirs)
+    half_mine, to_low = cross(1, chunks_low, 2, half, slab, theirs)
     from_low = swap_low(to_low)
-    mine, to_ahead, to_behind, to_far = cross(0, (2, 3, 4, 5), WIDE // 4, place, half, slab, theirs)
+    mine, to_ahead, to_behind, to_far = cross(0, chunks_x, 4, half, slab, theirs)
     parts = (mine, send(to_ahead, ahead), send(to_behind, behind), send(to_far, opposite))
     half_mine = add(half_mine, from_low).astype(bf16)
     second = (
@@ -430,28 +461,25 @@
     )
     parts, half_mine = lax.optimization_barrier((parts, half_mine))
     mine = add(*parts).astype(bf16)
-    shards = [add(rows_of(mine, zl, SHARD), swap_low(rows_of(mine, 1 - zl, SHARD))), add(*second)]
+    first_shard = add(rows_of(mine, zl, SHARD), swap_low(rows_of(mine, 1 - zl, SHARD)))
+    second_shard = add(*second)
 
     last = (x == X - 1) & (zl == ZL - 1)
-    at = jnp.arange(SHARD, dtype=jnp.int32)[:, None] + (WIDE - SHARD)
-    shards = [jnp.where(last & (at == NOCC), s, s * (1.0 / NB)).astype(bf16) for s in shards]
-    code = [s[NOCC - (WIDE - SHARD)] for s in shards]
-    other_shards = swap_cores(jnp.stack(shards))
-    here = last & (at == NOCC + 1)
-    by_x = jnp.where(here, code[1][None], other_shards[0])
-    by_low = jnp.where(here, code[0][None], other_shards[1])
+    at = jnp.arange(SHARD, dtype=jnp.int32)[:, None] + (CROSS - SHARD)
+
+    def weights_of(shard):
+        own = jnp.where(last & (at == NOCC), shard, shard * (1.0 / NB)).astype(bf16)
+        return jnp.where(last & (at == NOCC + 1), own[NOCC - (CROSS - SHARD)][None], swap_cores(own))
 
     def gather_x(array):
         n = array.shape[0]
         into = jnp.zeros((n * X, WIDE), bf16)
-        for k, part in (
-            (x, array),
-            (x - sign, send(array, ahead)),
-            (x + sign, send(array, behind)),
-            (x + 2, send(array, opposite)),
-        ):
+        for k, part in zip((x, x - sign, x + sign, x + 2), parts_x(array)):
             into = lax.dynamic_update_slice(into, part, ((k % X) * n, 0))
         return into
+
+    def parts_x(array):
+        return array, send(array, ahead), send(array, behind), send(array, opposite)
 
     def gather_low(array):
         n = array.shape[0]
@@ -459,7 +487,9 @@
         into = lax.dynamic_update_slice(into, array, (zl * n, 0))
         return lax.dynamic_update_slice(into, swap_low(array), ((1 - zl) * n, 0))
 
-    keep, give = exchange(place, half, gather_low(gather_x(by_low)), gather_x(gather_low(by_x)))
+    for_second = parts_x(gather_low(weights_of(first_shard)))
+    by_low = gather_x(weights_of(second_shard))
+    keep, give = exchange(half, (by_low, swap_low(by_low)), for_second)
 
     yy = ("y", "y")
     ahead, behind, opposite = around(yy, 1, True), around(yy, -1, True), around(yy, 2, True)
@@ -474,7 +504,7 @@
         send(quarter(y + 2).astype(bf16), opposite),
     )
     part = (part + swap_high(part)).astype(bf16)
-    into = jnp.zeros((WIDE // 2, ROWS), bf16)
+    into = jnp.zeros((CROSS // 2, ROWS), bf16)
     for k, array in (
         (y, part),
         (y - sign, send(part, ahead)),

time: 255 us -> 259 us (1.016)
  waiting for transfers between devices: 119 us -> 147 us
  starting transfers between devices: 75.2 us -> 61.4 us
  local copies, waits for them, and re-layouts: 15.3 us -> 7.35 us
  other arithmetic: 13.7 us -> 11 us
    ppermute x48 -> x49, waiting for transfers between devices: 119 us -> 147 us  [send(): return lax.ppermute(array, AXES, pairs)]
    ppermute x48 -> x49, starting transfers between devices: 75.2 us -> 61.4 us  [send(): return lax.ppermute(array, AXES, pairs)]
    dynamic_update_slice x7 -> x3, local copies, waits for them, and re-layouts: 3.25 us -> 0.07 us  [gather_x(): into = lax.dynamic_update_slice(into, part, (k % X * n, 0))]
  transfers between devices with their start and end apart: 48 -> 49, of which waited for: 31 -> 33; matrix products, arithmetic and copies ran while one was open for 5% -> 3% of each run, Pallas kernels for 8% -> 8%
where the time goes in v2:
time: 259 us; the launch traced here: 258 us
  waiting for transfers between devices  147 us (57%)
  starting transfers between devices  61.4 us (24%)
  Pallas kernels  30.4 us (12%)
  other arithmetic  11 us (4%)
  local copies, waits for them, and re-layouts  7.35 us (3%)
    ppermute x49, waiting for transfers between devices, send(): return lax.ppermute(array, AXES, pairs)  147 us
    ppermute x49, starting transfers between devices, send(): return lax.ppermute(array, AXES, pairs)  61.4 us
    pallas_call x1, Pallas kernels, multiply(): pl.pallas_call(multiply_kernel, out_shape=jax.ShapeDtypeStruct((2, ROWS,...  17.4 us
    pallas_call x1, Pallas kernels, exchange(): pl.pallas_call(exchange_kernel, out_shape=[jax.ShapeDtypeStruct((CROSS //...  6.39 us
    pallas_call x2, Pallas kernels, cross(): pl.pallas_call(kernel, out_shape=[jax.ShapeDtypeStruct((CROSS // many, WI...  5.71 us
  transfers between devices with their start and end apart: 49, of which 33 were waited for; matrix products, arithmetic and copies ran while one was open for 3% of the time, Pallas kernels for 8%

profile of v2, /device:TPU:1, one launch (start us, length us, event | category | flops | bytes accessed | tf_op | source)
XLA Modules:
  0.0 258.2 jit_solution(276732201584806315)
XLA Ops:
  0.9 1.5 collective-permute-start
  2.4 0.9 collective-permute-done
  6.2 0.9 select_bitcast_fusion.1
  7.1 1.4 collective-permute-start.1
  9.0 2.8 %collective-permute-start.2 = (bf16[2,48,896]{2,1,0:T(8,128)(2,1)S(1)}, bf16[2,48,896]{2,1,0:T(8,128)(2,1)S(1)}, u32[]{:S(2)}, u32[]{:S(2)}) collective-permute-start(bf16[2,48,896]{2,1,0:T(8,128)(2,1)S(1)} %fusion.10), channel_id=1, source_target_pairs={{0,6},{1,7},{2,0},{3,1},{4,2},{5,3},{6,4},{7,5},{8,104},{9,105},{1... | collective-permute-start | bytes 516104 | tf_op jit(solution)/shard_map/ppermute | solution.py:67
  13.1 2.9 %collective-permute-done.2 = bf16[2,48,896]{2,1,0:T(8,128)(2,1)S(1)} collective-permute-done((bf16[2,48,896]{2,1,0:T(8,128)(2,1)S(1)}, bf16[2,48,896]{2,1,0:T(8,128)(2,1)S(1)}, u32[]{:S(2)}, u32[]{:S(2)}) %collective-permute-start.2) | collective-permute-done | bytes 172064 | tf_op jit(solution)/shard_map/ppermute | solution.py:67
  16.0 1.8 collective-permute-done.3
  18.0 1.0 collective-permute-start.9
  19.0 1.8 collective-permute-start.10
  20.7 3.8 %collective-permute-start.6 = (bf16[2,4,32,896]{3,2,1,0:T(8,128)(2,1)S(1)}, bf16[2,4,32,896]{3,2,1,0:T(8,128)(2,1)S(1)}, u32[]{:S(2)}, u32[]{:S(2)}) collective-permute-start(bf16[2,4,32,896]{3,2,1,0:T(8,128)(2,1)S(1)} %slice.42), channel_id=1, source_target_pairs={{0,1},{1,16},{2,3},{3,18},{4,5},{5,20},{6,7},{7,22},{8,25},{9,8},{... | collective-permute-start | bytes 1376264 | tf_op jit(solution)/shard_map/ppermute | solution.py:67
  24.9 1.3 collective-permute-start.11
  26.3 3.6 %collective-permute-done.6 = bf16[2,4,32,896]{3,2,1,0:T(8,128)(2,1)S(1)} collective-permute-done((bf16[2,4,32,896]{3,2,1,0:T(8,128)(2,1)S(1)}, bf16[2,4,32,896]{3,2,1,0:T(8,128)(2,1)S(1)}, u32[]{:S(2)}, u32[]{:S(2)}) %collective-permute-start.6) | collective-permute-done | bytes 458784 | tf_op jit(solution)/shard_map/ppermute | solution.py:67
  30.2 2.9 %collective-permute-start.8 = (bf16[2,4,32,896]{3,2,1,0:T(8,128)(2,1)S(1)}, bf16[2,4,32,896]{3,2,1,0:T(8,128)(2,1)S(1)}, u32[]{:S(2)}, u32[]{:S(2)}) collective-permute-start(bf16[2,4,32,896]{3,2,1,0:T(8,128)(2,1)S(1)} %collective-permute-done.6), channel_id=1, source_target_pairs={{0,1},{1,16},{2,3},{3,18},{4,5},{5,20},{6,7},{7,22},{8,25},{9,8},{... | collective-permute-start | bytes 1376264 | tf_op jit(solution)/shard_map/ppermute | solution.py:67
  33.1 5.7 %collective-permute-done.7 = bf16[2,4,32,896]{3,2,1,0:T(8,128)(2,1)S(1)} collective-permute-done((bf16[2,4,32,896]{3,2,1,0:T(8,128)(2,1)S(1)}, bf16[2,4,32,896]{3,2,1,0:T(8,128)(2,1)S(1)}, u32[]{:S(2)}, u32[]{:S(2)}) %collective-permute-start.7) | collective-permute-done | bytes 458784 | tf_op jit(solution)/shard_map/ppermute | solution.py:67
  38.9 2.2 collective-permute-done.8
  41.3 2.7 %collective-permute-start.13 = (bf16[2,2,4,32,896]{4,3,2,1,0:T(8,128)(2,1)S(1)}, bf16[2,2,4,32,896]{4,3,2,1,0:T(8,128)(2,1)S(1)}, u32[]{:S(2)}, u32[]{:S(2)}) collective-permute-start(bf16[2,2,4,32,896]{4,3,2,1,0:T(8,128)(2,1)S(1)} %get-tuple-element.39), channel_id=1, source_target_pairs={{0,96},{1,97},{2,98},{3,99},{4,100},{5,101},{6,102},{7,103},{8,14}... | collective-permute-start | bytes 2752520 | tf_op jit(solution)/shard_map/ppermute | solution.py:67
  43.9 3.4 %collective-permute-start.17 = (bf16[2,4,4,16,896]{4,3,2,1,0:T(8,128)(2,1)S(1)}, bf16[2,4,4,16,896]{4,3,2,1,0:T(8,128)(2,1)S(1)}, u32[]{:S(2)}, u32[]{:S(2)}) collective-permute-start(bf16[2,4,4,16,896]{4,3,2,1,0:T(8,128)(2,1)S(1)} %bitcast_dynamic-update-slice_fusion.15), channel_id=1, source_target_pairs={{0,1},{1,16},{2,3},{3,18},{4,5},{5,20},{6,7},{7,22},{8,25},{9,8},{... | collective-permute-start | bytes 2752520 | tf_op jit(solution)/shard_map/ppermute | solution.py:67
  48.4 6.5 %collective-permute-done.12 = bf16[2,2,4,32,896]{4,3,2,1,0:T(8,128)(2,1)S(1)} collective-permute-done((bf16[2,2,4,32,896]{4,3,2,1,0:T(8,128)(2,1)S(1)}, bf16[2,2,4,32,896]{4,3,2,1,0:T(8,128)(2,1)S(1)}, u32[]{:S(2)}, u32[]{:S(2)}) %collective-permute-start.12) | collective-permute-done | bytes 917536 | tf_op jit(solution)/shard_map/ppermute | solution.py:67
  55.6 2.7 %collective-permute-start.14 = (bf16[2,2,4,32,896]{4,3,2,1,0:T(8,128)(2,1)S(1)}, bf16[2,2,4,32,896]{4,3,2,1,0:T(8,128)(2,1)S(1)}, u32[]{:S(2)}, u32[]{:S(2)}) collective-permute-start(bf16[2,2,4,32,896]{4,3,2,1,0:T(8,128)(2,1)S(1)} %get-tuple-element.38), channel_id=1, source_target_pairs={{0,96},{1,97},{2,98},{3,99},{4,100},{5,101},{6,102},{7,103},{8,14}... | collective-permute-start | bytes 2752520 | tf_op jit(solution)/shard_map/ppermute | solution.py:67
  58.4 5.8 %collective-permute-done.17 = bf16[2,4,4,16,896]{4,3,2,1,0:T(8,128)(2,1)S(1)} collective-permute-done((bf16[2,4,4,16,896]{4,3,2,1,0:T(8,128)(2,1)S(1)}, bf16[2,4,4,16,896]{4,3,2,1,0:T(8,128)(2,1)S(1)}, u32[]{:S(2)}, u32[]{:S(2)}) %collective-permute-start.17) | collective-permute-done | bytes 917536 | tf_op jit(solution)/shard_map/ppermute | solution.py:67
  64.1 5.5 %collective-permute-done.19 = bf16[2,4,4,16,896]{4,3,2,1,0:T(8,128)(2,1)S(1)} collective-permute-done((bf16[2,4,4,16,896]{4,3,2,1,0:T(8,128)(2,1)S(1)}, bf16[2,4,4,16,896]{4,3,2,1,0:T(8,128)(2,1)S(1)}, u32[]{:S(2)}, u32[]{:S(2)}) %collective-permute-start.19) | collective-permute-done | bytes 917536 | tf_op jit(solution)/shard_map/ppermute | solution.py:67
  70.6 12.8 %collective-permute-done.15 = bf16[2,2,4,32,896]{4,3,2,1,0:T(8,128)(2,1)S(1)} collective-permute-done((bf16[2,2,4,32,896]{4,3,2,1,0:T(8,128)(2,1)S(1)}, bf16[2,2,4,32,896]{4,3,2,1,0:T(8,128)(2,1)S(1)}, u32[]{:S(2)}, u32[]{:S(2)}) %collective-permute-start.15) | collective-permute-done | bytes 917536 | tf_op jit(solution)/shard_map/ppermute | solution.py:67
  84.8 4.5 %collective-permute-start.21 = (bf16[768,896]{1,0:T(8,128)(2,1)S(1)}, bf16[768,896]{1,0:T(8,128)(2,1)S(1)}, u32[]{:S(2)}, u32[]{:S(2)}) collective-permute-start(bf16[768,896]{1,0:T(8,128)(2,1)S(1)} %bitcast.100), channel_id=1, source_target_pairs={{0,8},{1,9},{2,10},{3,11},{4,12},{5,13},{6,14},{7,15},{8,0},{9,1},... | collective-permute-start | bytes 4128776 | tf_op jit(solution)/shard_map/ppermute | solution.py:67
  89.3 17.4 %multiply.1.refs_0_.half = bf16[2,768,896]{2,1,0:T(8,128)(2,1)S(1)} custom-call(s32[2,256]{1,0:T(2,128)S(1)} %pad_add_fusion.meta, bf16[96,128,128]{2,1,0:T(8,128)(2,1)S(1)} %bitcast.104, bf16[96,128,128]{2,1,0:T(8,128)(2,1)S(1)} %copy-done.4, bf16[4,2,2,4,32,896]{5,4,3,2,1,0:T(8,128)(2,1)S(1)} %bitcast_dynamic-update-slice_fusion.8.main0, ...), custom_call_target="tpu_custom_call" | custom-call | flops 5637144576 | bytes 16777216 | tf_op jit(solution)/shard_map/multiply/pallas_call | solution.py:219
  106.7 2.9 %cross.2 = (bf16[416,896]{1,0:T(8,128)(2,1)S(1)}, bf16[416,896]{1,0:T(8,128)(2,1)}) custom-call(bf16[2,768,896]{2,1,0:T(8,128)(2,1)S(1)} %multiply.1.refs_0_.half, bf16[768,896]{1,0:T(8,128)(2,1)S(1)} %bitcast.101, bf16[768,896]{1,0:T(8,128)(2,1)S(1)} %collective-permute-done.21.refs_2_), custom_call_target="tpu_custom_call" | custom-call | flops 1233125376 | bytes 8388608 | tf_op jit(solution)/shard_map/cross/pallas_call | solution.py:275
  109.7 2.8 %cross.3 = (bf16[208,896]{1,0:T(8,128)(2,1)S(1)}, bf16[208,896]{1,0:T(8,128)(2,1)}, bf16[208,896]{1,0:T(8,128)(2,1)}, bf16[208,896]{1,0:T(8,128)(2,1)}) custom-call(bf16[2,768,896]{2,1,0:T(8,128)(2,1)S(1)} %multiply.1.refs_0_.half, bf16[768,896]{1,0:T(8,128)(2,1)S(1)} %bitcast.102, bf16[768,896]{1,0:T(8,128)(2,1)S(1)} %collective-permute-done.21.refs_2_), custom_call_target="tpu_custom_call" | custom-call | flops 1233125376 | bytes 8388608 | tf_op jit(solution)/shard_map/cross/pallas_call | solution.py:275
  113.2 1.5 collective-permute-start.32
  114.6 1.2 collective-permute-start.33
  115.9 10.5 %collective-permute-done.22 = bf16[416,896]{1,0:T(8,128)(2,1)} collective-permute-done((bf16[416,896]{1,0:T(8,128)(2,1)}, bf16[416,896]{1,0:T(8,128)(2,1)}, u32[]{:S(2)}, u32[]{:S(2)}) %collective-permute-start.22) | collective-permute-done | bytes 745504 | tf_op jit(solution)/shard_map/ppermute | solution.py:67
  126.3 1.3 add_convert_fusion
  127.7 5.3 %collective-permute-done.33 = bf16[208,896]{1,0:T(8,128)(2,1)} collective-permute-done((bf16[208,896]{1,0:T(8,128)(2,1)}, bf16[208,896]{1,0:T(8,128)(2,1)}, u32[]{:S(2)}, u32[]{:S(2)}) %collective-permute-start.33) | collective-permute-done | bytes 372768 | tf_op jit(solution)/shard_map/ppermute | solution.py:67
  133.0 1.5 add_convert_fusion.1
  136.7 1.4 collective-permute-start.25
  138.1 2.7 %collective-permute-start.23 = (bf16[104,896]{1,0:T(8,128)(2,1)S(1)}, bf16[104,896]{1,0:T(8,128)(2,1)}, u32[]{:S(2)}, u32[]{:S(2)}) collective-permute-start(bf16[104,896]{1,0:T(8,128)(2,1)S(1)} %get-tuple-element.66), channel_id=1, source_target_pairs={{0,2},{1,3},{2,4},{3,5},{4,6},{5,7},{6,0},{7,1},{8,14},{9,15},{10,... | collective-permute-start | bytes 559112 | tf_op jit(solution)/shard_map/ppermute | solution.py:67
  140.8 2.2 collective-permute-done.25
  143.1 5.1 %collective-permute-done.24 = bf16[104,896]{1,0:T(8,128)(2,1)} collective-permute-done((bf16[104,896]{1,0:T(8,128)(2,1)S(1)}, bf16[104,896]{1,0:T(8,128)(2,1)}, u32[]{:S(2)}, u32[]{:S(2)}) %collective-permute-start.24) | collective-permute-done | bytes 186400 | tf_op jit(solution)/shard_map/ppermute | solution.py:67
  148.1 1.5 fusion.1
  149.6 1.6 collective-permute-start.35
  151.3 0.9 collective-permute-done.35
  152.9 1.6 collective-permute-start.27
  154.5 1.3 collective-permute-start.29
  155.7 3.0 %collective-permute-done.27 = bf16[104,896]{1,0:T(8,128)(2,1)S(1)} collective-permute-done((bf16[104,896]{1,0:T(8,128)(2,1)S(1)}, bf16[104,896]{1,0:T(8,128)(2,1)S(1)}, u32[]{:S(2)}, u32[]{:S(2)}) %collective-permute-start.27) | collective-permute-done | bytes 186400 | tf_op jit(solution)/shard_map/ppermute | solution.py:67
  158.7 6.5 %collective-permute-done.28 = bf16[104,896]{1,0:T(8,128)(2,1)S(1)} collective-permute-done((bf16[104,896]{1,0:T(8,128)(2,1)S(1)}, bf16[104,896]{1,0:T(8,128)(2,1)S(1)}, u32[]{:S(2)}, u32[]{:S(2)}) %collective-permute-start.28) | collective-permute-done | bytes 186400 | tf_op jit(solution)/shard_map/ppermute | solution.py:67
  166.9 20.6 %collective-permute-done.36 = bf16[104,896]{1,0:T(8,128)(2,1)S(1)} collective-permute-done((bf16[104,896]{1,0:T(8,128)(2,1)S(1)}, bf16[104,896]{1,0:T(8,128)(2,1)S(1)}, u32[]{:S(2)}, u32[]{:S(2)}) %collective-permute-start.36) | collective-permute-done | bytes 186400 | tf_op jit(solution)/shard_map/ppermute | solution.py:67
  187.6 1.5 collective-permute-start.38
  189.3 7.5 %collective-permute-done.37.refs_3_ = bf16[208,896]{1,0:T(8,128)(2,1)S(1)} collective-permute-done((bf16[208,896]{1,0:T(8,128)(2,1)S(1)}, bf16[208,896]{1,0:T(8,128)(2,1)S(1)}, u32[]{:S(2)}, u32[]{:S(2)}) %collective-permute-start.37) | collective-permute-done | bytes 372768 | tf_op jit(solution)/shard_map/ppermute | solution.py:67
  196.8 2.3 collective-permute-done.38.refs_4_
  199.1 6.3 %collective-permute-done.39.refs_5_ = bf16[208,896]{1,0:T(8,128)(2,1)S(1)} collective-permute-done((bf16[208,896]{1,0:T(8,128)(2,1)S(1)}, bf16[208,896]{1,0:T(8,128)(2,1)S(1)}, u32[]{:S(2)}, u32[]{:S(2)}) %collective-permute-start.39) | collective-permute-done | bytes 372768 | tf_op jit(solution)/shard_map/ppermute | solution.py:67
  205.4 6.4 %exchange.1 = (f32[416,768]{1,0:T(8,128)S(1)}, f32[416,768]{1,0:T(8,128)}) custom-call(bf16[2,768,896]{2,1,0:T(8,128)(2,1)S(1)} %multiply.1.refs_0_.half, bf16[416,896]{1,0:T(8,128)(2,1)S(1)} %constant_dynamic-update-slice_fusion.6.refs_0_, bf16[416,896]{1,0:T(8,128)(2,1)S(1)} %collective-permute-done.30.refs_1_, ...), custom_call_target="tpu_custom_call" | custom-call | flops 2466250752 | bytes 8388608 | tf_op jit(solution)/shard_map/exchange/pallas_call | solution.py:323
  211.8 1.1 copy-done
  212.9 2.6 %collective-permute-start.40 = (f32[416,768]{1,0:T(8,128)}, f32[416,768]{1,0:T(8,128)S(1)}, u32[]{:S(2)}, u32[]{:S(2)}) collective-permute-start(f32[416,768]{1,0:T(8,128)} %get-tuple-element.54), channel_id=1, source_target_pairs={{0,8},{1,9},{2,10},{3,11},{4,12},{5,13},{6,14},{7,15},{8,0},{9,1},... | collective-permute-start | bytes 3833864 | tf_op jit(solution)/shard_map/ppermute | solution.py:67
  215.5 2.8 %collective-permute-done.40 = f32[416,768]{1,0:T(8,128)S(1)} collective-permute-done((f32[416,768]{1,0:T(8,128)}, f32[416,768]{1,0:T(8,128)S(1)}, u32[]{:S(2)}, u32[]{:S(2)}) %collective-permute-start.40) | collective-permute-done | bytes 1277984 | tf_op jit(solution)/shard_map/ppermute | solution.py:67
  218.3 1.5 add.391
  220.6 2.4 collective-permute-start.42
  223.5 3.3 %collective-permute-done.43 = bf16[104,768]{1,0:T(8,128)(2,1)S(1)} collective-permute-done((bf16[104,768]{1,0:T(8,128)(2,1)S(1)}, bf16[104,768]{1,0:T(8,128)(2,1)S(1)}, u32[]{:S(2)}, u32[]{:S(2)}) %collective-permute-start.43) | collective-permute-done | bytes 159776 | tf_op jit(solution)/shard_map/ppermute | solution.py:67
  226.8 2.9 %collective-permute-done.42 = bf16[104,768]{1,0:T(8,128)(2,1)S(1)} collective-permute-done((bf16[104,768]{1,0:T(8,128)(2,1)S(1)}, bf16[104,768]{1,0:T(8,128)(2,1)S(1)}, u32[]{:S(2)}, u32[]{:S(2)}) %collective-permute-start.42) | collective-permute-done | bytes 159776 | tf_op jit(solution)/shard_map/ppermute | solution.py:67
  230.5 4.3 %collective-permute-start.44 = (f32[104,768]{1,0:T(8,128)S(1)}, f32[104,768]{1,0:T(8,128)S(1)}, u32[]{:S(2)}, u32[]{:S(2)}) collective-permute-start(f32[104,768]{1,0:T(8,128)S(1)} %add_add_fusion), channel_id=1, source_target_pairs={{0,16},{1,17},{2,18},{3,19},{4,20},{5,21},{6,22},{7,23},{8,24},{9,... | collective-permute-start | bytes 958472 | tf_op jit(solution)/shard_map/ppermute | solution.py:67
  234.7 7.2 %collective-permute-done.44 = f32[104,768]{1,0:T(8,128)S(1)} collective-permute-done((f32[104,768]{1,0:T(8,128)S(1)}, f32[104,768]{1,0:T(8,128)S(1)}, u32[]{:S(2)}, u32[]{:S(2)}) %collective-permute-start.44) | collective-permute-done | bytes 319520 | tf_op jit(solution)/shard_map/ppermute | solution.py:67
  242.0 2.8 %collective-permute-start.45 = (bf16[104,768]{1,0:T(8,128)(2,1)S(1)}, bf16[104,768]{1,0:T(8,128)(2,1)S(1)}, u32[]{:S(2)}, u32[]{:S(2)}) collective-permute-start(bf16[104,768]{1,0:T(8,128)(2,1)S(1)} %get-tuple-element.56), channel_id=1, source_target_pairs={{0,32},{1,33},{2,34},{3,35},{4,36},{5,37},{6,38},{7,39},{8,104},{9... | collective-permute-start | bytes 479240 | tf_op jit(solution)/shard_map/ppermute | solution.py:67
  244.9 1.3 collective-permute-start.47
  246.1 1.0 collective-permute-done.45
  247.1 7.2 %collective-permute-done.46 = bf16[104,768]{1,0:T(8,128)(2,1)S(1)} collective-permute-done((bf16[104,768]{1,0:T(8,128)(2,1)S(1)}, bf16[104,768]{1,0:T(8,128)(2,1)S(1)}, u32[]{:S(2)}, u32[]{:S(2)}) %collective-permute-start.46) | collective-permute-done | bytes 159776 | tf_op jit(solution)/shard_map/ppermute | solution.py:67
  254.8 1.7 collective-permute-done.48
  256.6 1.6 convert_bitcast_fusion
  (117 shorter events, 18.0 us)
Async XLA Ops:
  0.9 2.4 collective-permute-start
  3.3 14.6 %collective-permute-start.4 = (bf16[96,128,128]{2,1,0:T(8,128)(2,1)}, bf16[96,128,128]{2,1,0:T(8,128)(2,1)S(1)}, u32[]{:S(2)}, u32[]{:S(2)}) collective-permute-start(bf16[96,128,128]{2,1,0:T(8,128)(2,1)} %bitcast.103), channel_id=1, source_target_pairs={{0,8},{1,9},{2,10},{3,11},{4,12},{5,13},{6,14},{7,15},{8,0},{9,1},... | collective-permute-start | bytes 9437192 | tf_op jit(solution)/shard_map/ppermute | solution.py:67
  5.8 3.2 %collective-permute-start.5 = (s32[1,256]{1,0:T(1,128)S(1)}, s32[1,256]{1,0:T(1,128)S(1)}, u32[]{:S(2)}, u32[]{:S(2)}) collective-permute-start(s32[1,256]{1,0:T(1,128)S(1)} %bitcast.105), channel_id=1, source_target_pairs={{0,8},{1,9},{2,10},{3,11},{4,12},{5,13},{6,14},{7,15},{8,0},{9,1},... | collective-permute-start | bytes 3080 | tf_op jit(solution)/shard_map/ppermute | solution.py:67
  7.1 6.0 %collective-permute-start.1 = (bf16[2,48,896]{2,1,0:T(8,128)(2,1)S(1)}, bf16[2,48,896]{2,1,0:T(8,128)(2,1)S(1)}, u32[]{:S(2)}, u32[]{:S(2)}) collective-permute-start(bf16[2,48,896]{2,1,0:T(8,128)(2,1)S(1)} %fusion.10), channel_id=1, source_target_pairs={{0,2},{1,3},{2,4},{3,5},{4,6},{5,7},{6,0},{7,1},{8,40},{9,41},{10,... | collective-permute-start | bytes 516104 | tf_op jit(solution)/shard_map/ppermute | solution.py:67
  9.0 7.0 %collective-permute-start.2 = (bf16[2,48,896]{2,1,0:T(8,128)(2,1)S(1)}, bf16[2,48,896]{2,1,0:T(8,128)(2,1)S(1)}, u32[]{:S(2)}, u32[]{:S(2)}) collective-permute-start(bf16[2,48,896]{2,1,0:T(8,128)(2,1)S(1)} %fusion.10), channel_id=1, source_target_pairs={{0,6},{1,7},{2,0},{3,1},{4,2},{5,3},{6,4},{7,5},{8,104},{9,105},{1... | collective-permute-start | bytes 516104 | tf_op jit(solution)/shard_map/ppermute | solution.py:67
  11.8 6.1 %collective-permute-start.3 = (bf16[2,48,896]{2,1,0:T(8,128)(2,1)S(1)}, bf16[2,48,896]{2,1,0:T(8,128)(2,1)S(1)}, u32[]{:S(2)}, u32[]{:S(2)}) collective-permute-start(bf16[2,48,896]{2,1,0:T(8,128)(2,1)S(1)} %fusion.10), channel_id=1, source_target_pairs={{0,4},{1,5},{2,6},{3,7},{4,0},{5,1},{6,2},{7,3},{8,72},{9,73},{10,... | collective-permute-start | bytes 516104 | tf_op jit(solution)/shard_map/ppermute | solution.py:67
  17.9 15.2 %copy-start.3 = (bf16[96,128,128]{2,1,0:T(8,128)(2,1)}, bf16[96,128,128]{2,1,0:T(8,128)(2,1)S(1)}, u32[]{:S(2)}) copy-start(bf16[96,128,128]{2,1,0:T(8,128)(2,1)S(1)} %collective-permute-done.4.other_blocks) | copy-start | bytes 9437188
  18.0 6.9 %collective-permute-start.9 = (bf16[2,4,16,896]{3,2,1,0:T(8,128)(2,1)S(1)}, bf16[2,4,16,896]{3,2,1,0:T(8,128)(2,1)S(1)}, u32[]{:S(2)}, u32[]{:S(2)}) collective-permute-start(bf16[2,4,16,896]{3,2,1,0:T(8,128)(2,1)S(1)} %slice.50), channel_id=1, source_target_pairs={{0,32},{1,33},{2,34},{3,35},{4,36},{5,37},{6,38},{7,39},{8,10},{9,... | collective-permute-start | bytes 688136 | tf_op jit(solution)/shard_map/ppermute | solution.py:67
  19.0 7.3 %collective-permute-start.10 = (bf16[2,4,16,896]{3,2,1,0:T(8,128)(2,1)S(1)}, bf16[2,4,16,896]{3,2,1,0:T(8,128)(2,1)S(1)}, u32[]{:S(2)}, u32[]{:S(2)}) collective-permute-start(bf16[2,4,16,896]{3,2,1,0:T(8,128)(2,1)S(1)} %slice.50), channel_id=1, source_target_pairs={{0,96},{1,97},{2,98},{3,99},{4,100},{5,101},{6,102},{7,103},{8,14}... | collective-permute-start | bytes 688136 | tf_op jit(solution)/shard_map/ppermute | solution.py:67
  20.7 9.2 %collective-permute-start.6 = (bf16[2,4,32,896]{3,2,1,0:T(8,128)(2,1)S(1)}, bf16[2,4,32,896]{3,2,1,0:T(8,128)(2,1)S(1)}, u32[]{:S(2)}, u32[]{:S(2)}) collective-permute-start(bf16[2,4,32,896]{3,2,1,0:T(8,128)(2,1)S(1)} %slice.42), channel_id=1, source_target_pairs={{0,1},{1,16},{2,3},{3,18},{4,5},{5,20},{6,7},{7,22},{8,25},{9,8},{... | collective-permute-start | bytes 1376264 | tf_op jit(solution)/shard_map/ppermute | solution.py:67
  24.9 8.2 %collective-permute-start.11 = (bf16[2,4,16,896]{3,2,1,0:T(8,128)(2,1)S(1)}, bf16[2,4,16,896]{3,2,1,0:T(8,128)(2,1)S(1)}, u32[]{:S(2)}, u32[]{:S(2)}) collective-permute-start(bf16[2,4,16,896]{3,2,1,0:T(8,128)(2,1)S(1)} %slice.50), channel_id=1, source_target_pairs={{0,64},{1,65},{2,66},{3,67},{4,68},{5,69},{6,70},{7,71},{8,12},{9,... | collective-permute-start | bytes 688136 | tf_op jit(solution)/shard_map/ppermute | solution.py:67
  29.9 9.0 %collective-permute-start.7 = (bf16[2,4,32,896]{3,2,1,0:T(8,128)(2,1)S(1)}, bf16[2,4,32,896]{3,2,1,0:T(8,128)(2,1)S(1)}, u32[]{:S(2)}, u32[]{:S(2)}) collective-permute-start(bf16[2,4,32,896]{3,2,1,0:T(8,128)(2,1)S(1)} %slice.42), channel_id=1, source_target_pairs={{0,17},{1,0},{2,19},{3,2},{4,21},{5,4},{6,23},{7,6},{8,9},{9,24},{... | collective-permute-start | bytes 1376264 | tf_op jit(solution)/shard_map/ppermute | solution.py:67
  30.2 10.9 %collective-permute-start.8 = (bf16[2,4,32,896]{3,2,1,0:T(8,128)(2,1)S(1)}, bf16[2,4,32,896]{3,2,1,0:T(8,128)(2,1)S(1)}, u32[]{:S(2)}, u32[]{:S(2)}) collective-permute-start(bf16[2,4,32,896]{3,2,1,0:T(8,128)(2,1)S(1)} %collective-permute-done.6), channel_id=1, source_target_pairs={{0,1},{1,16},{2,3},{3,18},{4,5},{5,20},{6,7},{7,22},{8,25},{9,8},{... | collective-permute-start | bytes 1376264 | tf_op jit(solution)/shard_map/ppermute | solution.py:67
  41.2 13.8 %collective-permute-start.12 = (bf16[2,2,4,32,896]{4,3,2,1,0:T(8,128)(2,1)S(1)}, bf16[2,2,4,32,896]{4,3,2,1,0:T(8,128)(2,1)S(1)}, u32[]{:S(2)}, u32[]{:S(2)}) collective-permute-start(bf16[2,2,4,32,896]{4,3,2,1,0:T(8,128)(2,1)S(1)} %get-tuple-element.38), channel_id=1, source_target_pairs={{0,32},{1,33},{2,34},{3,35},{4,36},{5,37},{6,38},{7,39},{8,10},{9,... | collective-permute-start | bytes 2752520 | tf_op jit(solution)/shard_map/ppermute | solution.py:67
  41.3 14.4 %collective-permute-start.13 = (bf16[2,2,4,32,896]{4,3,2,1,0:T(8,128)(2,1)S(1)}, bf16[2,2,4,32,896]{4,3,2,1,0:T(8,128)(2,1)S(1)}, u32[]{:S(2)}, u32[]{:S(2)}) collective-permute-start(bf16[2,2,4,32,896]{4,3,2,1,0:T(8,128)(2,1)S(1)} %get-tuple-element.39), channel_id=1, source_target_pairs={{0,96},{1,97},{2,98},{3,99},{4,100},{5,101},{6,102},{7,103},{8,14}... | collective-permute-start | bytes 2752520 | tf_op jit(solution)/shard_map/ppermute | solution.py:67
  43.9 20.2 %collective-permute-start.17 = (bf16[2,4,4,16,896]{4,3,2,1,0:T(8,128)(2,1)S(1)}, bf16[2,4,4,16,896]{4,3,2,1,0:T(8,128)(2,1)S(1)}, u32[]{:S(2)}, u32[]{:S(2)}) collective-permute-start(bf16[2,4,4,16,896]{4,3,2,1,0:T(8,128)(2,1)S(1)} %bitcast_dynamic-update-slice_fusion.15), channel_id=1, source_target_pairs={{0,1},{1,16},{2,3},{3,18},{4,5},{5,20},{6,7},{7,22},{8,25},{9,8},{... | collective-permute-start | bytes 2752520 | tf_op jit(solution)/shard_map/ppermute | solution.py:67
  47.3 22.3 %collective-permute-start.19 = (bf16[2,4,4,16,896]{4,3,2,1,0:T(8,128)(2,1)S(1)}, bf16[2,4,4,16,896]{4,3,2,1,0:T(8,128)(2,1)S(1)}, u32[]{:S(2)}, u32[]{:S(2)}) collective-permute-start(bf16[2,4,4,16,896]{4,3,2,1,0:T(8,128)(2,1)S(1)} %bitcast_dynamic-update-slice_fusion.15), channel_id=1, source_target_pairs={{0,17},{1,0},{2,19},{3,2},{4,21},{5,4},{6,23},{7,6},{8,9},{9,24},{... | collective-permute-start | bytes 2752520 | tf_op jit(solution)/shard_map/ppermute | solution.py:67
  55.0 15.1 %collective-permute-start.16 = (bf16[2,2,4,32,896]{4,3,2,1,0:T(8,128)(2,1)S(1)}, bf16[2,2,4,32,896]{4,3,2,1,0:T(8,128)(2,1)S(1)}, u32[]{:S(2)}, u32[]{:S(2)}) collective-permute-start(bf16[2,2,4,32,896]{4,3,2,1,0:T(8,128)(2,1)S(1)} %get-tuple-element.39), channel_id=1, source_target_pairs={{0,32},{1,33},{2,34},{3,35},{4,36},{5,37},{6,38},{7,39},{8,10},{9,... | collective-permute-start | bytes 2752520 | tf_op jit(solution)/shard_map/ppermute | solution.py:67
  55.6 14.8 %collective-permute-start.14 = (bf16[2,2,4,32,896]{4,3,2,1,0:T(8,128)(2,1)S(1)}, bf16[2,2,4,32,896]{4,3,2,1,0:T(8,128)(2,1)S(1)}, u32[]{:S(2)}, u32[]{:S(2)}) collective-permute-start(bf16[2,2,4,32,896]{4,3,2,1,0:T(8,128)(2,1)S(1)} %get-tuple-element.38), channel_id=1, source_target_pairs={{0,96},{1,97},{2,98},{3,99},{4,100},{5,101},{6,102},{7,103},{8,14}... | collective-permute-start | bytes 2752520 | tf_op jit(solution)/shard_map/ppermute | solution.py:67
  64.1 19.4 %collective-permute-start.18 = (bf16[2,2,4,32,896]{4,3,2,1,0:T(8,128)(2,1)S(1)}, bf16[2,2,4,32,896]{4,3,2,1,0:T(8,128)(2,1)S(1)}, u32[]{:S(2)}, u32[]{:S(2)}) collective-permute-start(bf16[2,2,4,32,896]{4,3,2,1,0:T(8,128)(2,1)S(1)} %collective-permute-done.13), channel_id=1, source_target_pairs={{0,96},{1,97},{2,98},{3,99},{4,100},{5,101},{6,102},{7,103},{8,14}... | collective-permute-start | bytes 2752520 | tf_op jit(solution)/shard_map/ppermute | solution.py:67
  69.7 14.1 %collective-permute-start.20 = (bf16[2,4,4,16,896]{4,3,2,1,0:T(8,128)(2,1)S(1)}, bf16[2,4,4,16,896]{4,3,2,1,0:T(8,128)(2,1)S(1)}, u32[]{:S(2)}, u32[]{:S(2)}) collective-permute-start(bf16[2,4,4,16,896]{4,3,2,1,0:T(8,128)(2,1)S(1)} %collective-permute-done.17), channel_id=1, source_target_pairs={{0,1},{1,16},{2,3},{3,18},{4,5},{5,20},{6,7},{7,22},{8,25},{9,8},{... | collective-permute-start | bytes 2752520 | tf_op jit(solution)/shard_map/ppermute | solution.py:67
  69.7 13.8 %collective-permute-start.15 = (bf16[2,2,4,32,896]{4,3,2,1,0:T(8,128)(2,1)S(1)}, bf16[2,2,4,32,896]{4,3,2,1,0:T(8,128)(2,1)S(1)}, u32[]{:S(2)}, u32[]{:S(2)}) collective-permute-start(bf16[2,2,4,32,896]{4,3,2,1,0:T(8,128)(2,1)S(1)} %collective-permute-done.12), channel_id=1, source_target_pairs={{0,32},{1,33},{2,34},{3,35},{4,36},{5,37},{6,38},{7,39},{8,10},{9,... | collective-permute-start | bytes 2752520 | tf_op jit(solution)/shard_map/ppermute | solution.py:67
  83.9 5.4 %copy-start.2 = (bf16[1,96,128,128]{3,2,1,0:T(8,128)(2,1)S(1)}, bf16[1,96,128,128]{3,2,1,0:T(8,128)(2,1)}, u32[]{:S(2)}) copy-start(bf16[1,96,128,128]{3,2,1,0:T(8,128)(2,1)} %param.6) | copy-start | bytes 9437188
  83.9 5.4 %copy-start.4 = (bf16[96,128,128]{2,1,0:T(8,128)(2,1)S(1)}, bf16[96,128,128]{2,1,0:T(8,128)(2,1)}, u32[]{:S(2)}) copy-start(bf16[96,128,128]{2,1,0:T(8,128)(2,1)} %copy-done.3) | copy-start | bytes 9437188
  84.8 21.9 %collective-permute-start.21 = (bf16[768,896]{1,0:T(8,128)(2,1)S(1)}, bf16[768,896]{1,0:T(8,128)(2,1)S(1)}, u32[]{:S(2)}, u32[]{:S(2)}) collective-permute-start(bf16[768,896]{1,0:T(8,128)(2,1)S(1)} %bitcast.100), channel_id=1, source_target_pairs={{0,8},{1,9},{2,10},{3,11},{4,12},{5,13},{6,14},{7,15},{8,0},{9,1},... | collective-permute-start | bytes 4128776 | tf_op jit(solution)/shard_map/ppermute | solution.py:67
  109.7 16.7 %collective-permute-start.22 = (bf16[416,896]{1,0:T(8,128)(2,1)}, bf16[416,896]{1,0:T(8,128)(2,1)}, u32[]{:S(2)}, u32[]{:S(2)}) collective-permute-start(bf16[416,896]{1,0:T(8,128)(2,1)} %get-tuple-element.44), channel_id=1, source_target_pairs={{0,1},{1,0},{2,3},{3,2},{4,5},{5,4},{6,7},{7,6},{8,9},{9,8},{10,11... | collective-permute-start | bytes 2236424 | tf_op jit(solution)/shard_map/ppermute | solution.py:67
  112.4 0.7 copy-start.1
  113.2 14.5 %collective-permute-start.31 = (bf16[208,896]{1,0:T(8,128)(2,1)}, bf16[208,896]{1,0:T(8,128)(2,1)}, u32[]{:S(2)}, u32[]{:S(2)}) collective-permute-start(bf16[208,896]{1,0:T(8,128)(2,1)} %get-tuple-element.46), channel_id=1, source_target_pairs={{0,2},{1,3},{2,4},{3,5},{4,6},{5,7},{6,0},{7,1},{8,14},{9,15},{10,... | collective-permute-start | bytes 1118216 | tf_op jit(solution)/shard_map/ppermute | solution.py:67
  113.2 14.5 %collective-permute-start.32 = (bf16[208,896]{1,0:T(8,128)(2,1)}, bf16[208,896]{1,0:T(8,128)(2,1)}, u32[]{:S(2)}, u32[]{:S(2)}) collective-permute-start(bf16[208,896]{1,0:T(8,128)(2,1)} %get-tuple-element.47), channel_id=1, source_target_pairs={{0,6},{1,7},{2,0},{3,1},{4,2},{5,3},{6,4},{7,5},{8,10},{9,11},{10,... | collective-permute-start | bytes 1118216 | tf_op jit(solution)/shard_map/ppermute | solution.py:67
  114.6 18.3 %collective-permute-start.33 = (bf16[208,896]{1,0:T(8,128)(2,1)}, bf16[208,896]{1,0:T(8,128)(2,1)}, u32[]{:S(2)}, u32[]{:S(2)}) collective-permute-start(bf16[208,896]{1,0:T(8,128)(2,1)} %get-tuple-element.48), channel_id=1, source_target_pairs={{0,4},{1,5},{2,6},{3,7},{4,0},{5,1},{6,2},{7,3},{8,12},{9,13},{10,... | collective-permute-start | bytes 1118216 | tf_op jit(solution)/shard_map/ppermute | solution.py:67
  127.6 8.3 %copy-start.5 = (bf16[416,896]{1,0:T(8,128)(2,1)}, bf16[416,896]{1,0:T(8,128)(2,1)S(1)}, u32[]{:S(2)}) copy-start(bf16[416,896]{1,0:T(8,128)(2,1)S(1)} %add_convert_fusion) | copy-start | bytes 2236420
  135.2 5.7 %collective-permute-start.34 = (bf16[104,896]{1,0:T(8,128)(2,1)}, bf16[104,896]{1,0:T(8,128)(2,1)}, u32[]{:S(2)}, u32[]{:S(2)}) collective-permute-start(bf16[104,896]{1,0:T(8,128)(2,1)} %constant_dynamic-slice_fusion), channel_id=1, source_target_pairs={{0,1},{1,0},{2,3},{3,2},{4,5},{5,4},{6,7},{7,6},{8,9},{9,8},{10,11... | collective-permute-start | bytes 559112 | tf_op jit(solution)/shard_map/ppermute | solution.py:67
  136.7 6.3 %collective-permute-start.25 = (bf16[104,896]{1,0:T(8,128)(2,1)}, bf16[104,896]{1,0:T(8,128)(2,1)}, u32[]{:S(2)}, u32[]{:S(2)}) collective-permute-start(bf16[104,896]{1,0:T(8,128)(2,1)} %get-tuple-element.67), channel_id=1, source_target_pairs={{0,4},{1,5},{2,6},{3,7},{4,0},{5,1},{6,2},{7,3},{8,12},{9,13},{10,... | collective-permute-start | bytes 559112 | tf_op jit(solution)/shard_map/ppermute | solution.py:67
  138.1 10.0 %collective-permute-start.24 = (bf16[104,896]{1,0:T(8,128)(2,1)S(1)}, bf16[104,896]{1,0:T(8,128)(2,1)}, u32[]{:S(2)}, u32[]{:S(2)}) collective-permute-start(bf16[104,896]{1,0:T(8,128)(2,1)S(1)} %get-tuple-element.68), channel_id=1, source_target_pairs={{0,6},{1,7},{2,0},{3,1},{4,2},{5,3},{6,4},{7,5},{8,10},{9,11},{10,... | collective-permute-start | bytes 559112 | tf_op jit(solution)/shard_map/ppermute | solution.py:67
  138.1 10.0 %collective-permute-start.23 = (bf16[104,896]{1,0:T(8,128)(2,1)S(1)}, bf16[104,896]{1,0:T(8,128)(2,1)}, u32[]{:S(2)}, u32[]{:S(2)}) collective-permute-start(bf16[104,896]{1,0:T(8,128)(2,1)S(1)} %get-tuple-element.66), channel_id=1, source_target_pairs={{0,2},{1,3},{2,4},{3,5},{4,6},{5,7},{6,0},{7,1},{8,14},{9,15},{10,... | collective-permute-start | bytes 559112 | tf_op jit(solution)/shard_map/ppermute | solution.py:67
  149.6 2.6 %collective-permute-start.35 = (bf16[104,896]{1,0:T(8,128)(2,1)S(1)}, bf16[104,896]{1,0:T(8,128)(2,1)S(1)}, u32[]{:S(2)}, u32[]{:S(2)}) collective-permute-start(bf16[104,896]{1,0:T(8,128)(2,1)S(1)} %get-tuple-element.79), channel_id=1, source_target_pairs={{0,8},{1,9},{2,10},{3,11},{4,12},{5,13},{6,14},{7,15},{8,0},{9,1},... | collective-permute-start | bytes 559112 | tf_op jit(solution)/shard_map/ppermute | solution.py:67
  151.2 1.4 collective-permute-start.26
  152.9 5.9 %collective-permute-start.27 = (bf16[104,896]{1,0:T(8,128)(2,1)S(1)}, bf16[104,896]{1,0:T(8,128)(2,1)S(1)}, u32[]{:S(2)}, u32[]{:S(2)}) collective-permute-start(bf16[104,896]{1,0:T(8,128)(2,1)S(1)} %get-tuple-element.78), channel_id=1, source_target_pairs={{0,2},{1,3},{2,4},{3,5},{4,6},{5,7},{6,0},{7,1},{8,14},{9,15},{10,... | collective-permute-start | bytes 559112 | tf_op jit(solution)/shard_map/ppermute | solution.py:67
  154.5 10.8 %collective-permute-start.28 = (bf16[104,896]{1,0:T(8,128)(2,1)S(1)}, bf16[104,896]{1,0:T(8,128)(2,1)S(1)}, u32[]{:S(2)}, u32[]{:S(2)}) collective-permute-start(bf16[104,896]{1,0:T(8,128)(2,1)S(1)} %get-tuple-element.78), channel_id=1, source_target_pairs={{0,6},{1,7},{2,0},{3,1},{4,2},{5,3},{6,4},{7,5},{8,10},{9,11},{10,... | collective-permute-start | bytes 559112 | tf_op jit(solution)/shard_map/ppermute | solution.py:67
  154.5 10.8 %collective-permute-start.29 = (bf16[104,896]{1,0:T(8,128)(2,1)S(1)}, bf16[104,896]{1,0:T(8,128)(2,1)S(1)}, u32[]{:S(2)}, u32[]{:S(2)}) collective-permute-start(bf16[104,896]{1,0:T(8,128)(2,1)S(1)} %get-tuple-element.78), channel_id=1, source_target_pairs={{0,4},{1,5},{2,6},{3,7},{4,0},{5,1},{6,2},{7,3},{8,12},{9,13},{10,... | collective-permute-start | bytes 559112 | tf_op jit(solution)/shard_map/ppermute | solution.py:67
  165.3 40.1 %collective-permute-start.30 = (bf16[416,896]{1,0:T(8,128)(2,1)S(1)}, bf16[416,896]{1,0:T(8,128)(2,1)S(1)}, u32[]{:S(2)}, u32[]{:S(2)}) collective-permute-start(bf16[416,896]{1,0:T(8,128)(2,1)S(1)} %constant_dynamic-update-slice_fusion.6.refs_0_), channel_id=1, source_target_pairs={{0,1},{1,0},{2,3},{3,2},{4,5},{5,4},{6,7},{7,6},{8,9},{9,8},{10,11... | collective-permute-start | bytes 2236424 | tf_op jit(solution)/shard_map/ppermute | solution.py:67
  166.2 21.3 %collective-permute-start.36 = (bf16[104,896]{1,0:T(8,128)(2,1)S(1)}, bf16[104,896]{1,0:T(8,128)(2,1)S(1)}, u32[]{:S(2)}, u32[]{:S(2)}) collective-permute-start(bf16[104,896]{1,0:T(8,128)(2,1)S(1)} %get-tuple-element.58), channel_id=1, source_target_pairs={{0,1},{1,0},{2,3},{3,2},{4,5},{5,4},{6,7},{7,6},{8,9},{9,8},{10,11... | collective-permute-start | bytes 559112 | tf_op jit(solution)/shard_map/ppermute | solution.py:67
  187.6 9.2 %collective-permute-start.37 = (bf16[208,896]{1,0:T(8,128)(2,1)S(1)}, bf16[208,896]{1,0:T(8,128)(2,1)S(1)}, u32[]{:S(2)}, u32[]{:S(2)}) collective-permute-start(bf16[208,896]{1,0:T(8,128)(2,1)S(1)} %constant_dynamic-update-slice_fusion.4.refs_2_), channel_id=1, source_target_pairs={{0,2},{1,3},{2,4},{3,5},{4,6},{5,7},{6,0},{7,1},{8,14},{9,15},{10,... | collective-permute-start | bytes 1118216 | tf_op jit(solution)/shard_map/ppermute | solution.py:67
  187.6 11.4 %collective-permute-start.38 = (bf16[208,896]{1,0:T(8,128)(2,1)S(1)}, bf16[208,896]{1,0:T(8,128)(2,1)S(1)}, u32[]{:S(2)}, u32[]{:S(2)}) collective-permute-start(bf16[208,896]{1,0:T(8,128)(2,1)S(1)} %constant_dynamic-update-slice_fusion.4.refs_2_), channel_id=1, source_target_pairs={{0,6},{1,7},{2,0},{3,1},{4,2},{5,3},{6,4},{7,5},{8,10},{9,11},{10,... | collective-permute-start | bytes 1118216 | tf_op jit(solution)/shard_map/ppermute | solution.py:67
  189.1 16.3 %collective-permute-start.39 = (bf16[208,896]{1,0:T(8,128)(2,1)S(1)}, bf16[208,896]{1,0:T(8,128)(2,1)S(1)}, u32[]{:S(2)}, u32[]{:S(2)}) collective-permute-start(bf16[208,896]{1,0:T(8,128)(2,1)S(1)} %constant_dynamic-update-slice_fusion.4.refs_2_), channel_id=1, source_target_pairs={{0,4},{1,5},{2,6},{3,7},{4,0},{5,1},{6,2},{7,3},{8,12},{9,13},{10,... | collective-permute-start | bytes 1118216 | tf_op jit(solution)/shard_map/ppermute | solution.py:67
  211.8 1.1 copy-start
  212.9 5.4 %collective-permute-start.40 = (f32[416,768]{1,0:T(8,128)}, f32[416,768]{1,0:T(8,128)S(1)}, u32[]{:S(2)}, u32[]{:S(2)}) collective-permute-start(f32[416,768]{1,0:T(8,128)} %get-tuple-element.54), channel_id=1, source_target_pairs={{0,8},{1,9},{2,10},{3,11},{4,12},{5,13},{6,14},{7,15},{8,0},{9,1},... | collective-permute-start | bytes 3833864 | tf_op jit(solution)/shard_map/ppermute | solution.py:67
  219.9 7.0 %collective-permute-start.43 = (bf16[104,768]{1,0:T(8,128)(2,1)S(1)}, bf16[104,768]{1,0:T(8,128)(2,1)S(1)}, u32[]{:S(2)}, u32[]{:S(2)}) collective-permute-start(bf16[104,768]{1,0:T(8,128)(2,1)S(1)} %get-tuple-element.64), channel_id=1, source_target_pairs={{0,64},{1,65},{2,66},{3,67},{4,68},{5,69},{6,70},{7,71},{8,72},{9,... | collective-permute-start | bytes 479240 | tf_op jit(solution)/shard_map/ppermute | solution.py:67
  220.6 9.0 %collective-permute-start.42 = (bf16[104,768]{1,0:T(8,128)(2,1)S(1)}, bf16[104,768]{1,0:T(8,128)(2,1)S(1)}, u32[]{:S(2)}, u32[]{:S(2)}) collective-permute-start(bf16[104,768]{1,0:T(8,128)(2,1)S(1)} %get-tuple-element.65), channel_id=1, source_target_pairs={{0,96},{1,97},{2,98},{3,99},{4,100},{5,101},{6,102},{7,103},{8,40}... | collective-permute-start | bytes 479240 | tf_op jit(solution)/shard_map/ppermute | solution.py:67
  223.1 7.3 %collective-permute-start.41 = (bf16[104,768]{1,0:T(8,128)(2,1)S(1)}, bf16[104,768]{1,0:T(8,128)(2,1)S(1)}, u32[]{:S(2)}, u32[]{:S(2)}) collective-permute-start(bf16[104,768]{1,0:T(8,128)(2,1)S(1)} %get-tuple-element.63), channel_id=1, source_target_pairs={{0,32},{1,33},{2,34},{3,35},{4,36},{5,37},{6,38},{7,39},{8,104},{9... | collective-permute-start | bytes 479240 | tf_op jit(solution)/shard_map/ppermute | solution.py:67
  230.5 11.5 %collective-permute-start.44 = (f32[104,768]{1,0:T(8,128)S(1)}, f32[104,768]{1,0:T(8,128)S(1)}, u32[]{:S(2)}, u32[]{:S(2)}) collective-permute-start(f32[104,768]{1,0:T(8,128)S(1)} %add_add_fusion), channel_id=1, source_target_pairs={{0,16},{1,17},{2,18},{3,19},{4,20},{5,21},{6,22},{7,23},{8,24},{9,... | collective-permute-start | bytes 958472 | tf_op jit(solution)/shard_map/ppermute | solution.py:67
  242.0 5.0 %collective-permute-start.45 = (bf16[104,768]{1,0:T(8,128)(2,1)S(1)}, bf16[104,768]{1,0:T(8,128)(2,1)S(1)}, u32[]{:S(2)}, u32[]{:S(2)}) collective-permute-start(bf16[104,768]{1,0:T(8,128)(2,1)S(1)} %get-tuple-element.56), channel_id=1, source_target_pairs={{0,32},{1,33},{2,34},{3,35},{4,36},{5,37},{6,38},{7,39},{8,104},{9... | collective-permute-start | bytes 479240 | tf_op jit(solution)/shard_map/ppermute | solution.py:67
  244.9 9.5 %collective-permute-start.46 = (bf16[104,768]{1,0:T(8,128)(2,1)S(1)}, bf16[104,768]{1,0:T(8,128)(2,1)S(1)}, u32[]{:S(2)}, u32[]{:S(2)}) collective-permute-start(bf16[104,768]{1,0:T(8,128)(2,1)S(1)} %get-tuple-element.56), channel_id=1, source_target_pairs={{0,96},{1,97},{2,98},{3,99},{4,100},{5,101},{6,102},{7,103},{8,40}... | collective-permute-start | bytes 479240 | tf_op jit(solution)/shard_map/ppermute | solution.py:67
  244.9 9.5 %collective-permute-start.47 = (bf16[104,768]{1,0:T(8,128)(2,1)S(1)}, bf16[104,768]{1,0:T(8,128)(2,1)S(1)}, u32[]{:S(2)}, u32[]{:S(2)}) collective-permute-start(bf16[104,768]{1,0:T(8,128)(2,1)S(1)} %get-tuple-element.56), channel_id=1, source_target_pairs={{0,64},{1,65},{2,66},{3,67},{4,68},{5,69},{6,70},{7,71},{8,72},{9,... | collective-permute-start | bytes 479240 | tf_op jit(solution)/shard_map/ppermute | solution.py:67
  254.4 2.2 collective-permute-start.48

commit v3 on v2

--- a/solution.py
+++ b/solution.py
@@ -12,7 +12,6 @@
 BLK = 128
 ROW_BLOCKS = 6
 ROWS = ROW_BLOCKS * BLK
-GROUPS = 2 * ROW_BLOCKS
 SLOTS = 96
 NB = 6144
 NOCC = 800
@@ -117,17 +116,13 @@
     )(main0, main1, rest)
 
 
-def multiply_kernel(meta, own_blocks, other_blocks, main0, main1, rest, out, *scratch):
-    blocks, held, total, order, counts, steps, sems = scratch
-    core, _, _, _ = here()
-    copies = [
-        pltpu.make_async_copy(own_blocks, blocks.at[pl.ds(0, SLOTS)], sems.at[0]),
-        pltpu.make_async_copy(other_blocks, blocks.at[pl.ds(SLOTS, SLOTS)], sems.at[1]),
-    ]
+def assemble(main0, main1, rest, held, sems):
+    core = here()[0]
+    copies = []
     for a in range(4):
         for b in range(4):
             y, x = jnp.where(core == 0, b, a), jnp.where(core == 0, a, b)
-            i = 2 + 3 * (4 * a + b)
+            i = 3 * (4 * a + b)
             for c, main in enumerate((main0, main1)):
                 copies.append(
                     pltpu.make_async_copy(
@@ -139,51 +134,64 @@
                     rest.at[:, :, :, a, b], held.at[y, :, :, x, :, pl.ds(MAIN, OWN - MAIN)], sems.at[i + 2]
                 )
             )
-    for copy in copies:
-        copy.start()
-    blocks[2 * SLOTS] = jnp.zeros((BLK, BLK), bf16)
-
+    return copies
+
+
+def list_steps(q, meta, order, counts, steps):
     def clear(i, carry):
         counts[i] = 0
-        total[i] = jnp.zeros((BLK, WIDE), f32)
         return carry
 
-    lax.fori_loop(0, GROUPS + 1, clear, 0)
-    for q in range(2):
-
-        def put(s, carry):
-            group = q * ROW_BLOCKS + meta[q, s]
-            n = counts[group]
-            order[group, n] = s + q * SLOTS
-            counts[group] = n + 1
-            return carry
-
-        lax.fori_loop(0, meta[q, 2 * SLOTS], put, 0)
+    lax.fori_loop(0, ROW_BLOCKS, clear, 0)
+
+    def put(s, carry):
+        group = meta[q, s]
+        n = counts[group]
+        order[group, n] = s
+        counts[group] = n + 1
+        return carry
+
+    lax.fori_loop(0, meta[q, 2 * SLOTS], put, 0)
 
     def list_group(group, base):
         n = counts[group]
         for i in range(STEP):
-            order[group, n + i] = 2 * SLOTS
+            order[group, n + i] = SLOTS
         many = (n + STEP - 1) // STEP
 
         def list_step(i, carry):
             steps[base + i, 0] = group
             for k in range(STEP):
                 s = order[group, i * STEP + k]
-                q = jnp.minimum(s // SLOTS, 1)
                 steps[base + i, 1 + k] = s
-                steps[base + i, 1 + STEP + k] = jnp.where(s < 2 * SLOTS, meta[q, SLOTS + s - q * SLOTS], 0)
+                steps[base + i, 1 + STEP + k] = jnp.where(s < SLOTS, meta[q, SLOTS + s], 0)
             return carry
 
         lax.fori_loop(0, many, list_step, 0)
         return base + many
 
-    many = lax.fori_loop(0, GROUPS, list_group, 0)
+    many = lax.fori_loop(0, ROW_BLOCKS, list_group, 0)
     for u in range(UNROLL - 1):
-        steps[many + u, 0] = GROUPS
+        steps[many + u, 0] = ROW_BLOCKS
         for k in range(STEP):
-            steps[many + u, 1 + k] = 2 * SLOTS
+            steps[many + u, 1 + k] = SLOTS
             steps[many + u, 1 + STEP + k] = 0
+    return many
+
+
+def multiply_kernel(q, meta, factors, *refs):
+    if q == 1:
+        *parts, out, held, blocks, total, order, counts, steps, sems = refs
+        copies = assemble(*parts, held, sems)
+    else:
+        held, out, blocks, total, order, counts, steps, sems = refs
+        copies = []
+    copies.append(pltpu.make_async_copy(factors, blocks.at[pl.ds(0, SLOTS)], sems.at[48]))
+    for copy in copies:
+        copy.start()
+    blocks[SLOTS] = jnp.zeros((BLK, BLK), bf16)
+    total[...] = jnp.zeros_like(total)
+    many = list_steps(q, meta, order, counts, steps)
     for copy in copies:
         copy.wait()
     panels = held.reshape(NB, WIDE)
@@ -204,46 +212,46 @@
         return carry
 
     lax.fori_loop(0, (many + UNROLL - 1) // UNROLL, some, 0)
-
-    def finish(group, carry):
-        q = group // ROW_BLOCKS
-        start = pl.multiple_of((group - q * ROW_BLOCKS) * BLK, BLK)
-        out[q, pl.ds(start, BLK), :] = total[group].astype(bf16)
-        return carry
-
-    lax.fori_loop(0, GROUPS, finish, 0)
-
-
-def multiply(meta, own_blocks, other_blocks, main0, main1, rest):
-    most = 2 * SLOTS // STEP + GROUPS + UNROLL
+    for group in range(ROW_BLOCKS):
+        out[group * BLK : (group + 1) * BLK, :] = total[group].astype(bf16)
+
+
+def multiply(q, meta, factors, *panels):
+    most = SLOTS // STEP + ROW_BLOCKS + UNROLL
+    half = jax.ShapeDtypeStruct((ROWS, WIDE), bf16)
+    held = jax.ShapeDtypeStruct((Y, ZH, CORE, X, ZL, OWN, WIDE), bf16)
+    vmem, anywhere = pl.BlockSpec(memory_space=pltpu.VMEM), pl.BlockSpec(memory_space=pl.ANY)
+
+    def kernel(*refs):
+        multiply_kernel(q, *refs)
+
     return pl.pallas_call(
-        multiply_kernel,
-        out_shape=jax.ShapeDtypeStruct((2, ROWS, WIDE), bf16),
-        in_specs=[pl.BlockSpec(memory_space=pltpu.SMEM)] + [pl.BlockSpec(memory_space=pl.ANY)] * 5,
-        out_specs=pl.BlockSpec(memory_space=pltpu.VMEM),
+        kernel,
+        out_shape=[half, held] if q == 1 else half,
+        in_specs=[pl.BlockSpec(memory_space=pltpu.SMEM), anywhere] + ([anywhere] * 3 if q == 1 else [vmem]),
+        out_specs=[vmem, vmem] if q == 1 else vmem,
         scratch_shapes=[
-            pltpu.VMEM((2 * SLOTS + 1, BLK, BLK), bf16),
-            pltpu.VMEM((Y, ZH, CORE, X, ZL, OWN, WIDE), bf16),
-            pltpu.VMEM((GROUPS + 1, BLK, WIDE), f32),
-            pltpu.SMEM((GROUPS, SLOTS + 2 * STEP), jnp.int32),
-            pltpu.SMEM((GROUPS + 1,), jnp.int32),
+            pltpu.VMEM((SLOTS + 1, BLK, BLK), bf16),
+            pltpu.VMEM((ROW_BLOCKS + 1, BLK, WIDE), f32),
+            pltpu.SMEM((ROW_BLOCKS, SLOTS + 2 * STEP), jnp.int32),
+            pltpu.SMEM((ROW_BLOCKS,), jnp.int32),
             pltpu.SMEM((most, 1 + 2 * STEP), jnp.int32),
-            pltpu.SemaphoreType.DMA((50,)),
+            pltpu.SemaphoreType.DMA((49,)),
         ],
-        compiler_params=pltpu.CompilerParams(vmem_limit_bytes=30 * 1024 * 1024),
-        cost_estimate=pl.CostEstimate(flops=2 * 96 * 2 * 128 * 128 * 896, bytes_accessed=2**24, transcendentals=0),
+        compiler_params=pltpu.CompilerParams(vmem_limit_bytes=24 * 1024 * 1024),
+        cost_estimate=pl.CostEstimate(flops=96 * 2 * 128 * 128 * 896, bytes_accessed=2**23, transcendentals=0),
         name="multiply",
-    )(meta, own_blocks, other_blocks, main0, main1, rest)
-
-
-def cross_kernel(q, starts, half, slab, theirs, *refs):
+    )(meta, factors, *panels)
+
+
+def cross_kernel(starts, half, slab, theirs, *refs):
     outs, used, product = refs[:-2], refs[-2], refs[-1]
     core, row, _, _ = here()
     used[...] = jnp.where(core == 0, slab[...], theirs[...])
     product[...] = lax.dot_general(
-        half[q], used[...], (((0,), (0,)), ((), ())), preferred_element_type=f32
+        half[...], used[...], (((0,), (0,)), ((), ())), preferred_element_type=f32
     ).astype(bf16)
-    value = jnp.sum(half[q].astype(f32) * theirs[...].astype(f32), keepdims=True)
+    value = jnp.sum(half[...].astype(f32) * theirs[...].astype(f32), keepdims=True)
     high = value.astype(bf16).astype(f32)
     middle = (value - high).astype(bf16).astype(f32)
     low = value - high - middle
@@ -268,9 +276,9 @@
     return zl, 1 - zl
 
 
-def cross(q, starts, many, half, slab, theirs):
+def cross(starts, many, half, slab, theirs):
     def kernel(*refs):
-        cross_kernel(q, starts, *refs)
+        cross_kernel(starts, *refs)
 
     return pl.pallas_call(
         kernel,
@@ -284,8 +292,8 @@
     )(half, slab, theirs)
 
 
-def exchange_kernel(half, *refs):
-    parts, (keep, give, weights, turned, sems) = refs[:6], refs[6:]
+def exchange_kernel(*refs):
+    halves, parts, (keep, give, weights, turned, sems) = refs[:2], refs[2:8], refs[8:]
     core, _, _, _ = here()
     copies = []
     for i, (q, at) in enumerate([(0, at) for at in chunks_low()] + [(1, at) for at in chunks_arrived()]):
@@ -305,7 +313,7 @@
         codes = codes + jnp.where(line == 1, weights[1 - q, NOCC : NOCC + 16, :].astype(f32), 0.0)
         coulomb = jnp.sum(codes, keepdims=True) * (1.0 / NB)
         factor = jnp.where(core == 0, 2.0 * coulomb, 0.0)
-        own = half[q]
+        own = halves[q][...]
         term = factor * own.astype(f32) - jnp.dot(own, weights[q], preferred_element_type=f32)
         total = term if total is None else total + term
     turned[...] = total.T
@@ -319,11 +327,11 @@
     return x, behind, ahead, far
 
 
-def exchange(half, low_parts, x_parts):
+def exchange(halves, low_parts, x_parts):
     return pl.pallas_call(
         exchange_kernel,
         out_shape=[jax.ShapeDtypeStruct((CROSS // 2, ROWS), f32)] * 2,
-        in_specs=[pl.BlockSpec(memory_space=pltpu.VMEM)] + [pl.BlockSpec(memory_space=pl.ANY)] * 6,
+        in_specs=[pl.BlockSpec(memory_space=pltpu.VMEM)] * 2 + [pl.BlockSpec(memory_space=pl.ANY)] * 6,
         out_specs=[pl.BlockSpec(memory_space=pltpu.VMEM)] * 2,
         scratch_shapes=[
             pltpu.VMEM((2, WIDE, WIDE), bf16),
@@ -333,7 +341,7 @@
         compiler_params=pltpu.CompilerParams(vmem_limit_bytes=36 * 1024 * 1024),
         cost_estimate=pl.CostEstimate(flops=4 * 768 * 896 * 896, bytes_accessed=2**23, transcendentals=0),
         name="exchange",
-    )(half, *low_parts, *x_parts)
+    )(*halves, *low_parts, *x_parts)
 
 
 def local(factors, block_rows, block_cols, block_count, orbitals, response):
@@ -437,7 +445,7 @@
 
     slab = own_slab(*mains, rest).reshape(ROWS, WIDE)
     theirs = swap_cores(slab)
-    half = multiply(meta, own_blocks, other_blocks, *mains, rest)
+    second_half, panels = multiply(1, meta, other_blocks, *mains, rest)
 
     def add(*arrays):
         return sum(a.astype(f32) for a in arrays)
@@ -448,9 +456,11 @@
     xx = ("x", "x")
     ahead, behind = around(xx, 1, True), around(xx, -1, True)
     opposite = around(xx, 2, True)
-    half_mine, to_low = cross(1, chunks_low, 2, half, slab, theirs)
+    half_mine, to_low = cross(chunks_low, 2, second_half, slab, theirs)
     from_low = swap_low(to_low)
-    mine, to_ahead, to_behind, to_far = cross(0, chunks_x, 4, half, slab, theirs)
+    panels, half_mine = lax.optimization_barrier((panels, half_mine))
+    first_half = multiply(0, meta, own_blocks, panels)
+    mine, to_ahead, to_behind, to_far = cross(chunks_x, 4, first_half, slab, theirs)
     parts = (mine, send(to_ahead, ahead), send(to_behind, behind), send(to_far, opposite))
     half_mine = add(half_mine, from_low).astype(bf16)
     second = (
@@ -471,25 +481,22 @@
         own = jnp.where(last & (at == NOCC), shard, shard * (1.0 / NB)).astype(bf16)
         return jnp.where(last & (at == NOCC + 1), own[NOCC - (CROSS - SHARD)][None], swap_cores(own))
 
-    def gather_x(array):
-        n = array.shape[0]
-        into = jnp.zeros((n * X, WIDE), bf16)
-        for k, part in zip((x, x - sign, x + sign, x + 2), parts_x(array)):
-            into = lax.dynamic_update_slice(into, part, ((k % X) * n, 0))
-        return into
-
     def parts_x(array):
         return array, send(array, ahead), send(array, behind), send(array, opposite)
 
-    def gather_low(array):
-        n = array.shape[0]
-        into = jnp.zeros((n * ZL, WIDE), bf16)
-        into = lax.dynamic_update_slice(into, array, (zl * n, 0))
-        return lax.dynamic_update_slice(into, swap_low(array), ((1 - zl) * n, 0))
-
-    for_second = parts_x(gather_low(weights_of(first_shard)))
-    by_low = gather_x(weights_of(second_shard))
-    keep, give = exchange(half, (by_low, swap_low(by_low)), for_second)
+    def joined(parts, places):
+        n = parts[0].shape[0]
+        into = jnp.zeros((n * len(parts), WIDE), bf16)
+        for part, k in zip(parts, places):
+            into = lax.dynamic_update_slice(into, part, ((k % len(parts)) * n, 0))
+        return into
+
+    array = weights_of(first_shard)
+    from_low = swap_low(array)
+    by_x = joined((array, from_low), (zl, 1 - zl))
+    by_low = joined(parts_x(weights_of(second_shard)), (x, x - sign, x + sign, x + 2))
+    by_low, by_x = lax.optimization_barrier((by_low, by_x))
+    keep, give = exchange((first_half, second_half), (by_low, swap_low(by_low)), parts_x(by_x))
 
     yy = ("y", "y")
     ahead, behind, opposite = around(yy, 1, True), around(yy, -1, True), around(yy, 2, True)

time: 259 us -> 237 us (0.915)
  waiting for transfers between devices: 147 us -> 124 us
    ppermute x49, waiting for transfers between devices: 147 us -> 124 us  [send(): return lax.ppermute(array, AXES, pairs)]
    pallas_call x1 -> x2, Pallas kernels: 17.4 us -> 17 us  [multiply(): pl.pallas_call(kernel, out_shape=[half, held] if q == 1 else half, in_spe...]
  transfers between devices with their start and end apart: 49 -> 49, of which waited for: 33 -> 30; matrix products, arithmetic and copies ran while one was open for 3% -> 3% of each run, Pallas kernels for 8% -> 8%
where the time goes in v3:
time: 237 us
  waiting for transfers between devices  124 us (52%)
  starting transfers between devices  63.4 us (27%)
  Pallas kernels  29.1 us (12%)
  other arithmetic  10.8 us (5%)
  local copies, waits for them, and re-layouts  7.93 us (3%)
    ppermute x49, waiting for transfers between devices, send(): return lax.ppermute(array, AXES, pairs)  124 us
    ppermute x49, starting transfers between devices, send(): return lax.ppermute(array, AXES, pairs)  63.4 us
    pallas_call x2, Pallas kernels, multiply(): pl.pallas_call(kernel, out_shape=[half, held] if q == 1 else half, in_spe...  17 us
    pallas_call x1, Pallas kernels, exchange(): pl.pallas_call(exchange_kernel, out_shape=[jax.ShapeDtypeStruct((CROSS //...  6.39 us
    pallas_call x2, Pallas kernels, cross(): pl.pallas_call(kernel, out_shape=[jax.ShapeDtypeStruct((CROSS // many, WI...  4.83 us
  transfers between devices with their start and end apart: 49, of which 30 were waited for; matrix products, arithmetic and copies ran while one was open for 3% of the time, Pallas kernels for 8%

profile of v3, /device:TPU:1, one launch (start us, length us, event | category | flops | bytes accessed | tf_op | source)
XLA Modules:
  0.0 237.2 jit_solution(3959353041785734993)
XLA Ops:
  0.9 1.5 collective-permute-start
  2.4 0.9 collective-permute-done
  6.2 0.9 select_bitcast_fusion.1
  7.1 1.4 collective-permute-start.1
  9.0 2.8 %collective-permute-start.2 = (bf16[2,48,896]{2,1,0:T(8,128)(2,1)S(1)}, bf16[2,48,896]{2,1,0:T(8,128)(2,1)S(1)}, u32[]{:S(2)}, u32[]{:S(2)}) collective-permute-start(bf16[2,48,896]{2,1,0:T(8,128)(2,1)S(1)} %fusion.10), channel_id=1, source_target_pairs={{0,6},{1,7},{2,0},{3,1},{4,2},{5,3},{6,4},{7,5},{8,104},{9,105},{1... | collective-permute-start | bytes 516104 | tf_op jit(solution)/shard_map/ppermute | solution.py:66
  13.1 2.9 %collective-permute-done.2 = bf16[2,48,896]{2,1,0:T(8,128)(2,1)S(1)} collective-permute-done((bf16[2,48,896]{2,1,0:T(8,128)(2,1)S(1)}, bf16[2,48,896]{2,1,0:T(8,128)(2,1)S(1)}, u32[]{:S(2)}, u32[]{:S(2)}) %collective-permute-start.2) | collective-permute-done | bytes 172064 | tf_op jit(solution)/shard_map/ppermute | solution.py:66
  16.0 1.8 collective-permute-done.3
  18.0 1.0 collective-permute-start.9
  19.0 1.8 collective-permute-start.10
  20.7 3.8 %collective-permute-start.6 = (bf16[2,4,32,896]{3,2,1,0:T(8,128)(2,1)S(1)}, bf16[2,4,32,896]{3,2,1,0:T(8,128)(2,1)S(1)}, u32[]{:S(2)}, u32[]{:S(2)}) collective-permute-start(bf16[2,4,32,896]{3,2,1,0:T(8,128)(2,1)S(1)} %slice.42), channel_id=1, source_target_pairs={{0,1},{1,16},{2,3},{3,18},{4,5},{5,20},{6,7},{7,22},{8,25},{9,8},{... | collective-permute-start | bytes 1376264 | tf_op jit(solution)/shard_map/ppermute | solution.py:66
  24.9 1.3 collective-permute-start.11
  26.3 3.6 %collective-permute-done.6 = bf16[2,4,32,896]{3,2,1,0:T(8,128)(2,1)S(1)} collective-permute-done((bf16[2,4,32,896]{3,2,1,0:T(8,128)(2,1)S(1)}, bf16[2,4,32,896]{3,2,1,0:T(8,128)(2,1)S(1)}, u32[]{:S(2)}, u32[]{:S(2)}) %collective-permute-start.6) | collective-permute-done | bytes 458784 | tf_op jit(solution)/shard_map/ppermute | solution.py:66
  30.2 2.9 %collective-permute-start.8 = (bf16[2,4,32,896]{3,2,1,0:T(8,128)(2,1)S(1)}, bf16[2,4,32,896]{3,2,1,0:T(8,128)(2,1)S(1)}, u32[]{:S(2)}, u32[]{:S(2)}) collective-permute-start(bf16[2,4,32,896]{3,2,1,0:T(8,128)(2,1)S(1)} %collective-permute-done.6), channel_id=1, source_target_pairs={{0,1},{1,16},{2,3},{3,18},{4,5},{5,20},{6,7},{7,22},{8,25},{9,8},{... | collective-permute-start | bytes 1376264 | tf_op jit(solution)/shard_map/ppermute | solution.py:66
  33.1 5.8 %collective-permute-done.7 = bf16[2,4,32,896]{3,2,1,0:T(8,128)(2,1)S(1)} collective-permute-done((bf16[2,4,32,896]{3,2,1,0:T(8,128)(2,1)S(1)}, bf16[2,4,32,896]{3,2,1,0:T(8,128)(2,1)S(1)}, u32[]{:S(2)}, u32[]{:S(2)}) %collective-permute-start.7) | collective-permute-done | bytes 458784 | tf_op jit(solution)/shard_map/ppermute | solution.py:66
  38.9 2.2 collective-permute-done.8
  41.2 2.7 %collective-permute-start.13 = (bf16[2,2,4,32,896]{4,3,2,1,0:T(8,128)(2,1)S(1)}, bf16[2,2,4,32,896]{4,3,2,1,0:T(8,128)(2,1)S(1)}, u32[]{:S(2)}, u32[]{:S(2)}) collective-permute-start(bf16[2,2,4,32,896]{4,3,2,1,0:T(8,128)(2,1)S(1)} %get-tuple-element.45), channel_id=1, source_target_pairs={{0,96},{1,97},{2,98},{3,99},{4,100},{5,101},{6,102},{7,103},{8,14}... | collective-permute-start | bytes 2752520 | tf_op jit(solution)/shard_map/ppermute | solution.py:66
  43.9 3.4 %collective-permute-start.17 = (bf16[2,4,4,16,896]{4,3,2,1,0:T(8,128)(2,1)S(1)}, bf16[2,4,4,16,896]{4,3,2,1,0:T(8,128)(2,1)S(1)}, u32[]{:S(2)}, u32[]{:S(2)}) collective-permute-start(bf16[2,4,4,16,896]{4,3,2,1,0:T(8,128)(2,1)S(1)} %bitcast_dynamic-update-slice_fusion.15), channel_id=1, source_target_pairs={{0,1},{1,16},{2,3},{3,18},{4,5},{5,20},{6,7},{7,22},{8,25},{9,8},{... | collective-permute-start | bytes 2752520 | tf_op jit(solution)/shard_map/ppermute | solution.py:66
  48.4 6.5 %collective-permute-done.12 = bf16[2,2,4,32,896]{4,3,2,1,0:T(8,128)(2,1)S(1)} collective-permute-done((bf16[2,2,4,32,896]{4,3,2,1,0:T(8,128)(2,1)S(1)}, bf16[2,2,4,32,896]{4,3,2,1,0:T(8,128)(2,1)S(1)}, u32[]{:S(2)}, u32[]{:S(2)}) %collective-permute-start.12) | collective-permute-done | bytes 917536 | tf_op jit(solution)/shard_map/ppermute | solution.py:66
  55.6 2.7 %collective-permute-start.14 = (bf16[2,2,4,32,896]{4,3,2,1,0:T(8,128)(2,1)S(1)}, bf16[2,2,4,32,896]{4,3,2,1,0:T(8,128)(2,1)S(1)}, u32[]{:S(2)}, u32[]{:S(2)}) collective-permute-start(bf16[2,2,4,32,896]{4,3,2,1,0:T(8,128)(2,1)S(1)} %get-tuple-element.44), channel_id=1, source_target_pairs={{0,96},{1,97},{2,98},{3,99},{4,100},{5,101},{6,102},{7,103},{8,14}... | collective-permute-start | bytes 2752520 | tf_op jit(solution)/shard_map/ppermute | solution.py:66
  58.4 5.8 %collective-permute-done.17 = bf16[2,4,4,16,896]{4,3,2,1,0:T(8,128)(2,1)S(1)} collective-permute-done((bf16[2,4,4,16,896]{4,3,2,1,0:T(8,128)(2,1)S(1)}, bf16[2,4,4,16,896]{4,3,2,1,0:T(8,128)(2,1)S(1)}, u32[]{:S(2)}, u32[]{:S(2)}) %collective-permute-start.17) | collective-permute-done | bytes 917536 | tf_op jit(solution)/shard_map/ppermute | solution.py:66
  64.1 5.5 %collective-permute-done.19 = bf16[2,4,4,16,896]{4,3,2,1,0:T(8,128)(2,1)S(1)} collective-permute-done((bf16[2,4,4,16,896]{4,3,2,1,0:T(8,128)(2,1)S(1)}, bf16[2,4,4,16,896]{4,3,2,1,0:T(8,128)(2,1)S(1)}, u32[]{:S(2)}, u32[]{:S(2)}) %collective-permute-start.19) | collective-permute-done | bytes 917536 | tf_op jit(solution)/shard_map/ppermute | solution.py:66
  70.6 12.8 %collective-permute-done.15 = bf16[2,2,4,32,896]{4,3,2,1,0:T(8,128)(2,1)S(1)} collective-permute-done((bf16[2,2,4,32,896]{4,3,2,1,0:T(8,128)(2,1)S(1)}, bf16[2,2,4,32,896]{4,3,2,1,0:T(8,128)(2,1)S(1)}, u32[]{:S(2)}, u32[]{:S(2)}) %collective-permute-start.15) | collective-permute-done | bytes 917536 | tf_op jit(solution)/shard_map/ppermute | solution.py:66
  84.8 4.5 %collective-permute-start.21 = (bf16[768,896]{1,0:T(8,128)(2,1)S(1)}, bf16[768,896]{1,0:T(8,128)(2,1)S(1)}, u32[]{:S(2)}, u32[]{:S(2)}) collective-permute-start(bf16[768,896]{1,0:T(8,128)(2,1)S(1)} %bitcast.102), channel_id=1, source_target_pairs={{0,8},{1,9},{2,10},{3,11},{4,12},{5,13},{6,14},{7,15},{8,0},{9,1},... | collective-permute-start | bytes 4128776 | tf_op jit(solution)/shard_map/ppermute | solution.py:66
  89.3 9.2 %multiply.2 = (bf16[768,896]{1,0:T(8,128)(2,1)S(1)}, bf16[4,2,2,4,2,48,896]{6,5,4,3,2,1,0:T(8,128)(2,1)S(1)}) custom-call(s32[2,256]{1,0:T(2,128)S(1)} %pad_add_fusion.refs_0_, bf16[96,128,128]{2,1,0:T(8,128)(2,1)S(1)} %collective-permute-done.4.refs_1_, bf16[4,2,2,4,32,896]{5,4,3,2,1,0:T(8,128)(2,1)S(1)} %bitcast_dynamic-update-slice_fusion.8.refs_2_.main0, ...), custom_call_target="tpu_custom_call" | custom-call | flops 2818572288 | bytes 8388608 | tf_op jit(solution)/shard_map/multiply/pallas_call | solution.py:228
  98.5 2.0 cross.2
  100.5 4.1 %collective-permute-start.22 = (bf16[416,896]{1,0:T(8,128)(2,1)S(1)}, bf16[416,896]{1,0:T(8,128)(2,1)}, u32[]{:S(2)}, u32[]{:S(2)}) collective-permute-start(bf16[416,896]{1,0:T(8,128)(2,1)S(1)} %get-tuple-element.54), channel_id=1, source_target_pairs={{0,1},{1,0},{2,3},{3,2},{4,5},{5,4},{6,7},{7,6},{8,9},{9,8},{10,11... | collective-permute-start | bytes 2236424 | tf_op jit(solution)/shard_map/ppermute | solution.py:66
  104.6 7.8 %multiply.3.refs_0_ = bf16[768,896]{1,0:T(8,128)(2,1)S(1)} custom-call(s32[2,256]{1,0:T(2,128)S(1)} %pad_add_fusion.refs_0_, bf16[96,128,128]{2,1,0:T(8,128)(2,1)S(1)} %bitcast.101, bf16[4,2,2,4,2,48,896]{6,5,4,3,2,1,0:T(8,128)(2,1)S(1)} %get-tuple-element.52.refs_2_), custom_call_target="tpu_custom_call" | custom-call | flops 2818572288 | bytes 8388608 | tf_op jit(solution)/shard_map/multiply/pallas_call | solution.py:228
  112.4 2.8 %cross.3 = (bf16[208,896]{1,0:T(8,128)(2,1)S(1)}, bf16[208,896]{1,0:T(8,128)(2,1)}, bf16[208,896]{1,0:T(8,128)(2,1)}, bf16[208,896]{1,0:T(8,128)(2,1)}) custom-call(bf16[768,896]{1,0:T(8,128)(2,1)S(1)} %multiply.3.refs_0_, bf16[768,896]{1,0:T(8,128)(2,1)S(1)} %bitcast.104, bf16[768,896]{1,0:T(8,128)(2,1)S(1)} %collective-permute-done.21.refs_2_), custom_call_target="tpu_custom_call" | custom-call | flops 1233125376 | bytes 8388608 | tf_op jit(solution)/shard_map/cross/pallas_call | solution.py:283
  115.2 1.5 collective-permute-start.31
  116.7 4.9 %collective-permute-done.22 = bf16[416,896]{1,0:T(8,128)(2,1)} collective-permute-done((bf16[416,896]{1,0:T(8,128)(2,1)S(1)}, bf16[416,896]{1,0:T(8,128)(2,1)}, u32[]{:S(2)}, u32[]{:S(2)}) %collective-permute-start.22) | collective-permute-done | bytes 745504 | tf_op jit(solution)/shard_map/ppermute | solution.py:66
  121.6 1.3 add_convert_fusion
  122.9 3.2 %collective-permute-done.30 = bf16[208,896]{1,0:T(8,128)(2,1)} collective-permute-done((bf16[208,896]{1,0:T(8,128)(2,1)}, bf16[208,896]{1,0:T(8,128)(2,1)}, u32[]{:S(2)}, u32[]{:S(2)}) %collective-permute-start.30) | collective-permute-done | bytes 372768 | tf_op jit(solution)/shard_map/ppermute | solution.py:66
  126.1 6.3 %collective-permute-done.31 = bf16[208,896]{1,0:T(8,128)(2,1)} collective-permute-done((bf16[208,896]{1,0:T(8,128)(2,1)}, bf16[208,896]{1,0:T(8,128)(2,1)}, u32[]{:S(2)}, u32[]{:S(2)}) %collective-permute-start.31) | collective-permute-done | bytes 372768 | tf_op jit(solution)/shard_map/ppermute | solution.py:66
  132.5 1.4 add_convert_fusion.1
  134.6 1.9 collective-permute-start.33
  136.5 2.8 %collective-permute-start.25 = (bf16[104,896]{1,0:T(8,128)(2,1)S(1)}, bf16[104,896]{1,0:T(8,128)(2,1)}, u32[]{:S(2)}, u32[]{:S(2)}) collective-permute-start(bf16[104,896]{1,0:T(8,128)(2,1)S(1)} %get-tuple-element.79), channel_id=1, source_target_pairs={{0,4},{1,5},{2,6},{3,7},{4,0},{5,1},{6,2},{7,3},{8,12},{9,13},{10,... | collective-permute-start | bytes 559112 | tf_op jit(solution)/shard_map/ppermute | solution.py:66
  139.4 2.6 %collective-permute-start.23 = (bf16[104,896]{1,0:T(8,128)(2,1)S(1)}, bf16[104,896]{1,0:T(8,128)(2,1)}, u32[]{:S(2)}, u32[]{:S(2)}) collective-permute-start(bf16[104,896]{1,0:T(8,128)(2,1)S(1)} %get-tuple-element.78), channel_id=1, source_target_pairs={{0,2},{1,3},{2,4},{3,5},{4,6},{5,7},{6,0},{7,1},{8,14},{9,15},{10,... | collective-permute-start | bytes 559112 | tf_op jit(solution)/shard_map/ppermute | solution.py:66
  142.7 5.6 %collective-permute-done.24 = bf16[104,896]{1,0:T(8,128)(2,1)} collective-permute-done((bf16[104,896]{1,0:T(8,128)(2,1)S(1)}, bf16[104,896]{1,0:T(8,128)(2,1)}, u32[]{:S(2)}, u32[]{:S(2)}) %collective-permute-start.24) | collective-permute-done | bytes 186400 | tf_op jit(solution)/shard_map/ppermute | solution.py:66
  148.3 1.3 fusion.1
  149.6 1.5 collective-permute-start.34
  151.2 0.9 collective-permute-done.34
  152.8 1.6 collective-permute-start.27
  154.4 1.3 collective-permute-start.29
  155.6 1.7 collective-permute-start.35
  157.7 7.5 %collective-permute-done.28 = bf16[104,896]{1,0:T(8,128)(2,1)S(1)} collective-permute-done((bf16[104,896]{1,0:T(8,128)(2,1)S(1)}, bf16[104,896]{1,0:T(8,128)(2,1)S(1)}, u32[]{:S(2)}, u32[]{:S(2)}) %collective-permute-start.28) | collective-permute-done | bytes 186400 | tf_op jit(solution)/shard_map/ppermute | solution.py:66
  166.1 0.9 collective-permute-start.37
  169.2 5.8 %collective-permute-done.37.refs_5_ = bf16[208,896]{1,0:T(8,128)(2,1)S(1)} collective-permute-done((bf16[208,896]{1,0:T(8,128)(2,1)S(1)}, bf16[208,896]{1,0:T(8,128)(2,1)S(1)}, u32[]{:S(2)}, u32[]{:S(2)}) %collective-permute-start.37) | collective-permute-done | bytes 372768 | tf_op jit(solution)/shard_map/ppermute | solution.py:66
  175.0 11.3 %collective-permute-done.38.refs_6_ = bf16[208,896]{1,0:T(8,128)(2,1)S(1)} collective-permute-done((bf16[208,896]{1,0:T(8,128)(2,1)S(1)}, bf16[208,896]{1,0:T(8,128)(2,1)S(1)}, u32[]{:S(2)}, u32[]{:S(2)}) %collective-permute-start.38) | collective-permute-done | bytes 372768 | tf_op jit(solution)/shard_map/ppermute | solution.py:66
  186.2 1.0 copy-done.2
  187.2 1.3 copy-done.4
  188.6 6.4 %exchange.1 = (f32[416,768]{1,0:T(8,128)S(1)}, f32[416,768]{1,0:T(8,128)}) custom-call(bf16[768,896]{1,0:T(8,128)(2,1)S(1)} %multiply.3.refs_0_, bf16[768,896]{1,0:T(8,128)(2,1)S(1)} %copy-done.4, bf16[416,896]{1,0:T(8,128)(2,1)S(1)} %constant_dynamic-update-slice_fusion.6.refs_2_, bf16[416,896]{1,0:T(8,128)(2,1)S(1)} %collective-permute-done.36.refs_3_, ...), custom_call_target="tpu_custom_call" | custom-call | flops 2466250752 | bytes 8388608 | tf_op jit(solution)/shard_map/exchange/pallas_call | solution.py:331
  195.0 1.2 collective-permute-start.40
  196.2 3.0 %collective-permute-done.40 = f32[416,768]{1,0:T(8,128)} collective-permute-done((f32[416,768]{1,0:T(8,128)}, f32[416,768]{1,0:T(8,128)}, u32[]{:S(2)}, u32[]{:S(2)}) %collective-permute-start.40) | collective-permute-done | bytes 1277984 | tf_op jit(solution)/shard_map/ppermute | solution.py:66
  199.1 1.5 add.405
  201.6 1.9 collective-permute-start.41
  203.5 4.1 %collective-permute-done.43 = bf16[104,768]{1,0:T(8,128)(2,1)S(1)} collective-permute-done((bf16[104,768]{1,0:T(8,128)(2,1)S(1)}, bf16[104,768]{1,0:T(8,128)(2,1)S(1)}, u32[]{:S(2)}, u32[]{:S(2)}) %collective-permute-start.43) | collective-permute-done | bytes 159776 | tf_op jit(solution)/shard_map/ppermute | solution.py:66
  207.6 3.7 %collective-permute-done.42 = bf16[104,768]{1,0:T(8,128)(2,1)S(1)} collective-permute-done((bf16[104,768]{1,0:T(8,128)(2,1)S(1)}, bf16[104,768]{1,0:T(8,128)(2,1)S(1)}, u32[]{:S(2)}, u32[]{:S(2)}) %collective-permute-start.42) | collective-permute-done | bytes 159776 | tf_op jit(solution)/shard_map/ppermute | solution.py:66
  212.2 9.1 %collective-permute-done.44 = f32[104,768]{1,0:T(8,128)S(1)} collective-permute-done((f32[104,768]{1,0:T(8,128)S(1)}, f32[104,768]{1,0:T(8,128)S(1)}, u32[]{:S(2)}, u32[]{:S(2)}) %collective-permute-start.44) | collective-permute-done | bytes 319520 | tf_op jit(solution)/shard_map/ppermute | solution.py:66
  221.4 1.0 collective-permute-start.45
  223.7 1.9 collective-permute-done.45
  225.6 4.9 %collective-permute-done.46 = bf16[104,768]{1,0:T(8,128)(2,1)S(1)} collective-permute-done((bf16[104,768]{1,0:T(8,128)(2,1)S(1)}, bf16[104,768]{1,0:T(8,128)(2,1)S(1)}, u32[]{:S(2)}, u32[]{:S(2)}) %collective-permute-start.46) | collective-permute-done | bytes 159776 | tf_op jit(solution)/shard_map/ppermute | solution.py:66
  230.6 3.2 %collective-permute-start.48 = (bf16[416,768]{1,0:T(8,128)(2,1)S(1)}, bf16[416,768]{1,0:T(8,128)(2,1)S(1)}, u32[]{:S(2)}, u32[]{:S(2)}) collective-permute-start(bf16[416,768]{1,0:T(8,128)(2,1)S(1)} %constant_dynamic-update-slice_fusion), channel_id=1, source_target_pairs={{0,8},{1,9},{2,10},{3,11},{4,12},{5,13},{6,14},{7,15},{8,0},{9,1},... | collective-permute-start | bytes 1916936 | tf_op jit(solution)/shard_map/ppermute | solution.py:66
  233.8 1.7 collective-permute-done.48
  235.6 1.6 convert_bitcast_fusion
  (116 shorter events, 18.7 us)
Async XLA Ops:
  0.9 2.4 %collective-permute-start = (bf16[48,800]{1,0:T(8,128)(2,1)S(1)}, bf16[48,800]{1,0:T(8,128)(2,1)S(1)}, u32[]{:S(2)}, u32[]{:S(2)}) collective-permute-start(bf16[48,800]{1,0:T(8,128)(2,1)S(1)} %broadcast_select_fusion.4), channel_id=1, source_target_pairs={{0,8},{1,9},{2,10},{3,11},{4,12},{5,13},{6,14},{7,15},{8,0},{9,1},... | collective-permute-start | bytes 230408 | tf_op jit(solution)/shard_map/ppermute | solution.py:66
  3.3 14.6 %collective-permute-start.4 = (bf16[96,128,128]{2,1,0:T(8,128)(2,1)}, bf16[96,128,128]{2,1,0:T(8,128)(2,1)S(1)}, u32[]{:S(2)}, u32[]{:S(2)}) collective-permute-start(bf16[96,128,128]{2,1,0:T(8,128)(2,1)} %bitcast.100), channel_id=1, source_target_pairs={{0,8},{1,9},{2,10},{3,11},{4,12},{5,13},{6,14},{7,15},{8,0},{9,1},... | collective-permute-start | bytes 9437192 | tf_op jit(solution)/shard_map/ppermute | solution.py:66
  5.8 3.2 %collective-permute-start.5 = (s32[1,256]{1,0:T(1,128)S(1)}, s32[1,256]{1,0:T(1,128)S(1)}, u32[]{:S(2)}, u32[]{:S(2)}) collective-permute-start(s32[1,256]{1,0:T(1,128)S(1)} %bitcast.105), channel_id=1, source_target_pairs={{0,8},{1,9},{2,10},{3,11},{4,12},{5,13},{6,14},{7,15},{8,0},{9,1},... | collective-permute-start | bytes 3080 | tf_op jit(solution)/shard_map/ppermute | solution.py:66
  7.1 6.0 %collective-permute-start.1 = (bf16[2,48,896]{2,1,0:T(8,128)(2,1)S(1)}, bf16[2,48,896]{2,1,0:T(8,128)(2,1)S(1)}, u32[]{:S(2)}, u32[]{:S(2)}) collective-permute-start(bf16[2,48,896]{2,1,0:T(8,128)(2,1)S(1)} %fusion.10), channel_id=1, source_target_pairs={{0,2},{1,3},{2,4},{3,5},{4,6},{5,7},{6,0},{7,1},{8,40},{9,41},{10,... | collective-permute-start | bytes 516104 | tf_op jit(solution)/shard_map/ppermute | solution.py:66
  9.0 7.0 %collective-permute-start.2 = (bf16[2,48,896]{2,1,0:T(8,128)(2,1)S(1)}, bf16[2,48,896]{2,1,0:T(8,128)(2,1)S(1)}, u32[]{:S(2)}, u32[]{:S(2)}) collective-permute-start(bf16[2,48,896]{2,1,0:T(8,128)(2,1)S(1)} %fusion.10), channel_id=1, source_target_pairs={{0,6},{1,7},{2,0},{3,1},{4,2},{5,3},{6,4},{7,5},{8,104},{9,105},{1... | collective-permute-start | bytes 516104 | tf_op jit(solution)/shard_map/ppermute | solution.py:66
  11.8 6.1 %collective-permute-start.3 = (bf16[2,48,896]{2,1,0:T(8,128)(2,1)S(1)}, bf16[2,48,896]{2,1,0:T(8,128)(2,1)S(1)}, u32[]{:S(2)}, u32[]{:S(2)}) collective-permute-start(bf16[2,48,896]{2,1,0:T(8,128)(2,1)S(1)} %fusion.10), channel_id=1, source_target_pairs={{0,4},{1,5},{2,6},{3,7},{4,0},{5,1},{6,2},{7,3},{8,72},{9,73},{10,... | collective-permute-start | bytes 516104 | tf_op jit(solution)/shard_map/ppermute | solution.py:66
  18.0 6.9 %collective-permute-start.9 = (bf16[2,4,16,896]{3,2,1,0:T(8,128)(2,1)S(1)}, bf16[2,4,16,896]{3,2,1,0:T(8,128)(2,1)S(1)}, u32[]{:S(2)}, u32[]{:S(2)}) collective-permute-start(bf16[2,4,16,896]{3,2,1,0:T(8,128)(2,1)S(1)} %slice.50), channel_id=1, source_target_pairs={{0,32},{1,33},{2,34},{3,35},{4,36},{5,37},{6,38},{7,39},{8,10},{9,... | collective-permute-start | bytes 688136 | tf_op jit(solution)/shard_map/ppermute | solution.py:66
  19.0 7.3 %collective-permute-start.10 = (bf16[2,4,16,896]{3,2,1,0:T(8,128)(2,1)S(1)}, bf16[2,4,16,896]{3,2,1,0:T(8,128)(2,1)S(1)}, u32[]{:S(2)}, u32[]{:S(2)}) collective-permute-start(bf16[2,4,16,896]{3,2,1,0:T(8,128)(2,1)S(1)} %slice.50), channel_id=1, source_target_pairs={{0,96},{1,97},{2,98},{3,99},{4,100},{5,101},{6,102},{7,103},{8,14}... | collective-permute-start | bytes 688136 | tf_op jit(solution)/shard_map/ppermute | solution.py:66
  20.7 9.2 %collective-permute-start.6 = (bf16[2,4,32,896]{3,2,1,0:T(8,128)(2,1)S(1)}, bf16[2,4,32,896]{3,2,1,0:T(8,128)(2,1)S(1)}, u32[]{:S(2)}, u32[]{:S(2)}) collective-permute-start(bf16[2,4,32,896]{3,2,1,0:T(8,128)(2,1)S(1)} %slice.42), channel_id=1, source_target_pairs={{0,1},{1,16},{2,3},{3,18},{4,5},{5,20},{6,7},{7,22},{8,25},{9,8},{... | collective-permute-start | bytes 1376264 | tf_op jit(solution)/shard_map/ppermute | solution.py:66
  24.9 8.2 %collective-permute-start.11 = (bf16[2,4,16,896]{3,2,1,0:T(8,128)(2,1)S(1)}, bf16[2,4,16,896]{3,2,1,0:T(8,128)(2,1)S(1)}, u32[]{:S(2)}, u32[]{:S(2)}) collective-permute-start(bf16[2,4,16,896]{3,2,1,0:T(8,128)(2,1)S(1)} %slice.50), channel_id=1, source_target_pairs={{0,64},{1,65},{2,66},{3,67},{4,68},{5,69},{6,70},{7,71},{8,12},{9,... | collective-permute-start | bytes 688136 | tf_op jit(solution)/shard_map/ppermute | solution.py:66
  29.9 9.0 %collective-permute-start.7 = (bf16[2,4,32,896]{3,2,1,0:T(8,128)(2,1)S(1)}, bf16[2,4,32,896]{3,2,1,0:T(8,128)(2,1)S(1)}, u32[]{:S(2)}, u32[]{:S(2)}) collective-permute-start(bf16[2,4,32,896]{3,2,1,0:T(8,128)(2,1)S(1)} %slice.42), channel_id=1, source_target_pairs={{0,17},{1,0},{2,19},{3,2},{4,21},{5,4},{6,23},{7,6},{8,9},{9,24},{... | collective-permute-start | bytes 1376264 | tf_op jit(solution)/shard_map/ppermute | solution.py:66
  30.2 10.9 %collective-permute-start.8 = (bf16[2,4,32,896]{3,2,1,0:T(8,128)(2,1)S(1)}, bf16[2,4,32,896]{3,2,1,0:T(8,128)(2,1)S(1)}, u32[]{:S(2)}, u32[]{:S(2)}) collective-permute-start(bf16[2,4,32,896]{3,2,1,0:T(8,128)(2,1)S(1)} %collective-permute-done.6), channel_id=1, source_target_pairs={{0,1},{1,16},{2,3},{3,18},{4,5},{5,20},{6,7},{7,22},{8,25},{9,8},{... | collective-permute-start | bytes 1376264 | tf_op jit(solution)/shard_map/ppermute | solution.py:66
  41.2 13.8 %collective-permute-start.12 = (bf16[2,2,4,32,896]{4,3,2,1,0:T(8,128)(2,1)S(1)}, bf16[2,2,4,32,896]{4,3,2,1,0:T(8,128)(2,1)S(1)}, u32[]{:S(2)}, u32[]{:S(2)}) collective-permute-start(bf16[2,2,4,32,896]{4,3,2,1,0:T(8,128)(2,1)S(1)} %get-tuple-element.44), channel_id=1, source_target_pairs={{0,32},{1,33},{2,34},{3,35},{4,36},{5,37},{6,38},{7,39},{8,10},{9,... | collective-permute-start | bytes 2752520 | tf_op jit(solution)/shard_map/ppermute | solution.py:66
  41.2 14.4 %collective-permute-start.13 = (bf16[2,2,4,32,896]{4,3,2,1,0:T(8,128)(2,1)S(1)}, bf16[2,2,4,32,896]{4,3,2,1,0:T(8,128)(2,1)S(1)}, u32[]{:S(2)}, u32[]{:S(2)}) collective-permute-start(bf16[2,2,4,32,896]{4,3,2,1,0:T(8,128)(2,1)S(1)} %get-tuple-element.45), channel_id=1, source_target_pairs={{0,96},{1,97},{2,98},{3,99},{4,100},{5,101},{6,102},{7,103},{8,14}... | collective-permute-start | bytes 2752520 | tf_op jit(solution)/shard_map/ppermute | solution.py:66
  43.9 20.2 %collective-permute-start.17 = (bf16[2,4,4,16,896]{4,3,2,1,0:T(8,128)(2,1)S(1)}, bf16[2,4,4,16,896]{4,3,2,1,0:T(8,128)(2,1)S(1)}, u32[]{:S(2)}, u32[]{:S(2)}) collective-permute-start(bf16[2,4,4,16,896]{4,3,2,1,0:T(8,128)(2,1)S(1)} %bitcast_dynamic-update-slice_fusion.15), channel_id=1, source_target_pairs={{0,1},{1,16},{2,3},{3,18},{4,5},{5,20},{6,7},{7,22},{8,25},{9,8},{... | collective-permute-start | bytes 2752520 | tf_op jit(solution)/shard_map/ppermute | solution.py:66
  47.3 22.3 %collective-permute-start.19 = (bf16[2,4,4,16,896]{4,3,2,1,0:T(8,128)(2,1)S(1)}, bf16[2,4,4,16,896]{4,3,2,1,0:T(8,128)(2,1)S(1)}, u32[]{:S(2)}, u32[]{:S(2)}) collective-permute-start(bf16[2,4,4,16,896]{4,3,2,1,0:T(8,128)(2,1)S(1)} %bitcast_dynamic-update-slice_fusion.15), channel_id=1, source_target_pairs={{0,17},{1,0},{2,19},{3,2},{4,21},{5,4},{6,23},{7,6},{8,9},{9,24},{... | collective-permute-start | bytes 2752520 | tf_op jit(solution)/shard_map/ppermute | solution.py:66
  55.0 15.1 %collective-permute-start.16 = (bf16[2,2,4,32,896]{4,3,2,1,0:T(8,128)(2,1)S(1)}, bf16[2,2,4,32,896]{4,3,2,1,0:T(8,128)(2,1)S(1)}, u32[]{:S(2)}, u32[]{:S(2)}) collective-permute-start(bf16[2,2,4,32,896]{4,3,2,1,0:T(8,128)(2,1)S(1)} %get-tuple-element.45), channel_id=1, source_target_pairs={{0,32},{1,33},{2,34},{3,35},{4,36},{5,37},{6,38},{7,39},{8,10},{9,... | collective-permute-start | bytes 2752520 | tf_op jit(solution)/shard_map/ppermute | solution.py:66
  55.6 14.8 %collective-permute-start.14 = (bf16[2,2,4,32,896]{4,3,2,1,0:T(8,128)(2,1)S(1)}, bf16[2,2,4,32,896]{4,3,2,1,0:T(8,128)(2,1)S(1)}, u32[]{:S(2)}, u32[]{:S(2)}) collective-permute-start(bf16[2,2,4,32,896]{4,3,2,1,0:T(8,128)(2,1)S(1)} %get-tuple-element.44), channel_id=1, source_target_pairs={{0,96},{1,97},{2,98},{3,99},{4,100},{5,101},{6,102},{7,103},{8,14}... | collective-permute-start | bytes 2752520 | tf_op jit(solution)/shard_map/ppermute | solution.py:66
  64.1 19.4 %collective-permute-start.18 = (bf16[2,2,4,32,896]{4,3,2,1,0:T(8,128)(2,1)S(1)}, bf16[2,2,4,32,896]{4,3,2,1,0:T(8,128)(2,1)S(1)}, u32[]{:S(2)}, u32[]{:S(2)}) collective-permute-start(bf16[2,2,4,32,896]{4,3,2,1,0:T(8,128)(2,1)S(1)} %collective-permute-done.13), channel_id=1, source_target_pairs={{0,96},{1,97},{2,98},{3,99},{4,100},{5,101},{6,102},{7,103},{8,14}... | collective-permute-start | bytes 2752520 | tf_op jit(solution)/shard_map/ppermute | solution.py:66
  69.7 14.1 %collective-permute-start.20 = (bf16[2,4,4,16,896]{4,3,2,1,0:T(8,128)(2,1)S(1)}, bf16[2,4,4,16,896]{4,3,2,1,0:T(8,128)(2,1)S(1)}, u32[]{:S(2)}, u32[]{:S(2)}) collective-permute-start(bf16[2,4,4,16,896]{4,3,2,1,0:T(8,128)(2,1)S(1)} %collective-permute-done.17), channel_id=1, source_target_pairs={{0,1},{1,16},{2,3},{3,18},{4,5},{5,20},{6,7},{7,22},{8,25},{9,8},{... | collective-permute-start | bytes 2752520 | tf_op jit(solution)/shard_map/ppermute | solution.py:66
  69.7 13.8 %collective-permute-start.15 = (bf16[2,2,4,32,896]{4,3,2,1,0:T(8,128)(2,1)S(1)}, bf16[2,2,4,32,896]{4,3,2,1,0:T(8,128)(2,1)S(1)}, u32[]{:S(2)}, u32[]{:S(2)}) collective-permute-start(bf16[2,2,4,32,896]{4,3,2,1,0:T(8,128)(2,1)S(1)} %collective-permute-done.12), channel_id=1, source_target_pairs={{0,32},{1,33},{2,34},{3,35},{4,36},{5,37},{6,38},{7,39},{8,10},{9,... | collective-permute-start | bytes 2752520 | tf_op jit(solution)/shard_map/ppermute | solution.py:66
  84.8 13.7 %collective-permute-start.21 = (bf16[768,896]{1,0:T(8,128)(2,1)S(1)}, bf16[768,896]{1,0:T(8,128)(2,1)S(1)}, u32[]{:S(2)}, u32[]{:S(2)}) collective-permute-start(bf16[768,896]{1,0:T(8,128)(2,1)S(1)} %bitcast.102), channel_id=1, source_target_pairs={{0,8},{1,9},{2,10},{3,11},{4,12},{5,13},{6,14},{7,15},{8,0},{9,1},... | collective-permute-start | bytes 4128776 | tf_op jit(solution)/shard_map/ppermute | solution.py:66
  98.5 14.0 %copy-start.3 = (bf16[768,896]{1,0:T(8,128)(2,1)}, bf16[768,896]{1,0:T(8,128)(2,1)S(1)}, u32[]{:S(2)}) copy-start(bf16[768,896]{1,0:T(8,128)(2,1)S(1)} %get-tuple-element.50.refs_0_.refs_1_) | copy-start | bytes 4128772
  98.5 6.1 %copy-start = (bf16[1,96,128,128]{3,2,1,0:T(8,128)(2,1)S(1)}, bf16[1,96,128,128]{3,2,1,0:T(8,128)(2,1)}, u32[]{:S(2)}) copy-start(bf16[1,96,128,128]{3,2,1,0:T(8,128)(2,1)} %param.6) | copy-start | bytes 9437188
  100.5 21.1 %collective-permute-start.22 = (bf16[416,896]{1,0:T(8,128)(2,1)S(1)}, bf16[416,896]{1,0:T(8,128)(2,1)}, u32[]{:S(2)}, u32[]{:S(2)}) collective-permute-start(bf16[416,896]{1,0:T(8,128)(2,1)S(1)} %get-tuple-element.54), channel_id=1, source_target_pairs={{0,1},{1,0},{2,3},{3,2},{4,5},{5,4},{6,7},{7,6},{8,9},{9,8},{10,11... | collective-permute-start | bytes 2236424 | tf_op jit(solution)/shard_map/ppermute | solution.py:66
  115.2 10.9 %collective-permute-start.30 = (bf16[208,896]{1,0:T(8,128)(2,1)}, bf16[208,896]{1,0:T(8,128)(2,1)}, u32[]{:S(2)}, u32[]{:S(2)}) collective-permute-start(bf16[208,896]{1,0:T(8,128)(2,1)} %get-tuple-element.56), channel_id=1, source_target_pairs={{0,2},{1,3},{2,4},{3,5},{4,6},{5,7},{6,0},{7,1},{8,14},{9,15},{10,... | collective-permute-start | bytes 1118216 | tf_op jit(solution)/shard_map/ppermute | solution.py:66
  115.2 17.2 %collective-permute-start.31 = (bf16[208,896]{1,0:T(8,128)(2,1)}, bf16[208,896]{1,0:T(8,128)(2,1)}, u32[]{:S(2)}, u32[]{:S(2)}) collective-permute-start(bf16[208,896]{1,0:T(8,128)(2,1)} %get-tuple-element.57), channel_id=1, source_target_pairs={{0,6},{1,7},{2,0},{3,1},{4,2},{5,3},{6,4},{7,5},{8,10},{9,11},{10,... | collective-permute-start | bytes 1118216 | tf_op jit(solution)/shard_map/ppermute | solution.py:66
  116.7 15.8 %collective-permute-start.32 = (bf16[208,896]{1,0:T(8,128)(2,1)}, bf16[208,896]{1,0:T(8,128)(2,1)}, u32[]{:S(2)}, u32[]{:S(2)}) collective-permute-start(bf16[208,896]{1,0:T(8,128)(2,1)} %get-tuple-element.58), channel_id=1, source_target_pairs={{0,4},{1,5},{2,6},{3,7},{4,0},{5,1},{6,2},{7,3},{8,12},{9,13},{10,... | collective-permute-start | bytes 1118216 | tf_op jit(solution)/shard_map/ppermute | solution.py:66
  134.6 7.4 %collective-permute-start.33 = (bf16[104,896]{1,0:T(8,128)(2,1)}, bf16[104,896]{1,0:T(8,128)(2,1)S(1)}, u32[]{:S(2)}, u32[]{:S(2)}) collective-permute-start(bf16[104,896]{1,0:T(8,128)(2,1)} %constant_dynamic-slice_fusion), channel_id=1, source_target_pairs={{0,1},{1,0},{2,3},{3,2},{4,5},{5,4},{6,7},{7,6},{8,9},{9,8},{10,11... | collective-permute-start | bytes 559112 | tf_op jit(solution)/shard_map/ppermute | solution.py:66
  136.5 6.2 %collective-permute-start.25 = (bf16[104,896]{1,0:T(8,128)(2,1)S(1)}, bf16[104,896]{1,0:T(8,128)(2,1)}, u32[]{:S(2)}, u32[]{:S(2)}) collective-permute-start(bf16[104,896]{1,0:T(8,128)(2,1)S(1)} %get-tuple-element.79), channel_id=1, source_target_pairs={{0,4},{1,5},{2,6},{3,7},{4,0},{5,1},{6,2},{7,3},{8,12},{9,13},{10,... | collective-permute-start | bytes 559112 | tf_op jit(solution)/shard_map/ppermute | solution.py:66
  139.3 9.0 %collective-permute-start.24 = (bf16[104,896]{1,0:T(8,128)(2,1)S(1)}, bf16[104,896]{1,0:T(8,128)(2,1)}, u32[]{:S(2)}, u32[]{:S(2)}) collective-permute-start(bf16[104,896]{1,0:T(8,128)(2,1)S(1)} %get-tuple-element.80), channel_id=1, source_target_pairs={{0,6},{1,7},{2,0},{3,1},{4,2},{5,3},{6,4},{7,5},{8,10},{9,11},{10,... | collective-permute-start | bytes 559112 | tf_op jit(solution)/shard_map/ppermute | solution.py:66
  139.4 8.9 %collective-permute-start.23 = (bf16[104,896]{1,0:T(8,128)(2,1)S(1)}, bf16[104,896]{1,0:T(8,128)(2,1)}, u32[]{:S(2)}, u32[]{:S(2)}) collective-permute-start(bf16[104,896]{1,0:T(8,128)(2,1)S(1)} %get-tuple-element.78), channel_id=1, source_target_pairs={{0,2},{1,3},{2,4},{3,5},{4,6},{5,7},{6,0},{7,1},{8,14},{9,15},{10,... | collective-permute-start | bytes 559112 | tf_op jit(solution)/shard_map/ppermute | solution.py:66
  149.6 2.5 %collective-permute-start.34 = (bf16[104,896]{1,0:T(8,128)(2,1)S(1)}, bf16[104,896]{1,0:T(8,128)(2,1)S(1)}, u32[]{:S(2)}, u32[]{:S(2)}) collective-permute-start(bf16[104,896]{1,0:T(8,128)(2,1)S(1)} %get-tuple-element.91), channel_id=1, source_target_pairs={{0,8},{1,9},{2,10},{3,11},{4,12},{5,13},{6,14},{7,15},{8,0},{9,1},... | collective-permute-start | bytes 559112 | tf_op jit(solution)/shard_map/ppermute | solution.py:66
  151.1 1.4 collective-permute-start.26
  152.8 4.9 %collective-permute-start.27 = (bf16[104,896]{1,0:T(8,128)(2,1)S(1)}, bf16[104,896]{1,0:T(8,128)(2,1)S(1)}, u32[]{:S(2)}, u32[]{:S(2)}) collective-permute-start(bf16[104,896]{1,0:T(8,128)(2,1)S(1)} %get-tuple-element.90), channel_id=1, source_target_pairs={{0,2},{1,3},{2,4},{3,5},{4,6},{5,7},{6,0},{7,1},{8,14},{9,15},{10,... | collective-permute-start | bytes 559112 | tf_op jit(solution)/shard_map/ppermute | solution.py:66
  154.4 10.8 %collective-permute-start.28 = (bf16[104,896]{1,0:T(8,128)(2,1)S(1)}, bf16[104,896]{1,0:T(8,128)(2,1)S(1)}, u32[]{:S(2)}, u32[]{:S(2)}) collective-permute-start(bf16[104,896]{1,0:T(8,128)(2,1)S(1)} %get-tuple-element.90), channel_id=1, source_target_pairs={{0,6},{1,7},{2,0},{3,1},{4,2},{5,3},{6,4},{7,5},{8,10},{9,11},{10,... | collective-permute-start | bytes 559112 | tf_op jit(solution)/shard_map/ppermute | solution.py:66
  154.4 10.8 %collective-permute-start.29 = (bf16[104,896]{1,0:T(8,128)(2,1)S(1)}, bf16[104,896]{1,0:T(8,128)(2,1)S(1)}, u32[]{:S(2)}, u32[]{:S(2)}) collective-permute-start(bf16[104,896]{1,0:T(8,128)(2,1)S(1)} %get-tuple-element.90), channel_id=1, source_target_pairs={{0,4},{1,5},{2,6},{3,7},{4,0},{5,1},{6,2},{7,3},{8,12},{9,13},{10,... | collective-permute-start | bytes 559112 | tf_op jit(solution)/shard_map/ppermute | solution.py:66
  155.6 9.6 %collective-permute-start.35 = (bf16[104,896]{1,0:T(8,128)(2,1)S(1)}, bf16[104,896]{1,0:T(8,128)(2,1)S(1)}, u32[]{:S(2)}, u32[]{:S(2)}) collective-permute-start(bf16[104,896]{1,0:T(8,128)(2,1)S(1)} %get-tuple-element.70), channel_id=1, source_target_pairs={{0,1},{1,0},{2,3},{3,2},{4,5},{5,4},{6,7},{7,6},{8,9},{9,8},{10,11... | collective-permute-start | bytes 559112 | tf_op jit(solution)/shard_map/ppermute | solution.py:66
  165.3 20.9 %collective-permute-start.36 = (bf16[416,896]{1,0:T(8,128)(2,1)S(1)}, bf16[416,896]{1,0:T(8,128)(2,1)S(1)}, u32[]{:S(2)}, u32[]{:S(2)}) collective-permute-start(bf16[416,896]{1,0:T(8,128)(2,1)S(1)} %constant_dynamic-update-slice_fusion.6.refs_2_), channel_id=1, source_target_pairs={{0,1},{1,0},{2,3},{3,2},{4,5},{5,4},{6,7},{7,6},{8,9},{9,8},{10,11... | collective-permute-start | bytes 2236424 | tf_op jit(solution)/shard_map/ppermute | solution.py:66
  166.1 8.8 %collective-permute-start.37 = (bf16[208,896]{1,0:T(8,128)(2,1)S(1)}, bf16[208,896]{1,0:T(8,128)(2,1)S(1)}, u32[]{:S(2)}, u32[]{:S(2)}) collective-permute-start(bf16[208,896]{1,0:T(8,128)(2,1)S(1)} %constant_dynamic-update-slice_fusion.4.refs_4_), channel_id=1, source_target_pairs={{0,2},{1,3},{2,4},{3,5},{4,6},{5,7},{6,0},{7,1},{8,14},{9,15},{10,... | collective-permute-start | bytes 1118216 | tf_op jit(solution)/shard_map/ppermute | solution.py:66
  167.1 19.1 %collective-permute-start.38 = (bf16[208,896]{1,0:T(8,128)(2,1)S(1)}, bf16[208,896]{1,0:T(8,128)(2,1)S(1)}, u32[]{:S(2)}, u32[]{:S(2)}) collective-permute-start(bf16[208,896]{1,0:T(8,128)(2,1)S(1)} %constant_dynamic-update-slice_fusion.4.refs_4_), channel_id=1, source_target_pairs={{0,6},{1,7},{2,0},{3,1},{4,2},{5,3},{6,4},{7,5},{8,10},{9,11},{10,... | collective-permute-start | bytes 1118216 | tf_op jit(solution)/shard_map/ppermute | solution.py:66
  167.6 18.6 %collective-permute-start.39 = (bf16[208,896]{1,0:T(8,128)(2,1)S(1)}, bf16[208,896]{1,0:T(8,128)(2,1)S(1)}, u32[]{:S(2)}, u32[]{:S(2)}) collective-permute-start(bf16[208,896]{1,0:T(8,128)(2,1)S(1)} %constant_dynamic-update-slice_fusion.4.refs_4_), channel_id=1, source_target_pairs={{0,4},{1,5},{2,6},{3,7},{4,0},{5,1},{6,2},{7,3},{8,12},{9,13},{10,... | collective-permute-start | bytes 1118216 | tf_op jit(solution)/shard_map/ppermute | solution.py:66
  168.5 0.7 copy-start.1
  186.2 1.0 copy-start.2
  187.2 1.3 copy-start.4
  195.0 4.2 %collective-permute-start.40 = (f32[416,768]{1,0:T(8,128)}, f32[416,768]{1,0:T(8,128)}, u32[]{:S(2)}, u32[]{:S(2)}) collective-permute-start(f32[416,768]{1,0:T(8,128)} %get-tuple-element.66), channel_id=1, source_target_pairs={{0,8},{1,9},{2,10},{3,11},{4,12},{5,13},{6,14},{7,15},{8,0},{9,1},... | collective-permute-start | bytes 3833864 | tf_op jit(solution)/shard_map/ppermute | solution.py:66
  200.7 7.0 %collective-permute-start.43 = (bf16[104,768]{1,0:T(8,128)(2,1)S(1)}, bf16[104,768]{1,0:T(8,128)(2,1)S(1)}, u32[]{:S(2)}, u32[]{:S(2)}) collective-permute-start(bf16[104,768]{1,0:T(8,128)(2,1)S(1)} %get-tuple-element.76), channel_id=1, source_target_pairs={{0,64},{1,65},{2,66},{3,67},{4,68},{5,69},{6,70},{7,71},{8,72},{9,... | collective-permute-start | bytes 479240 | tf_op jit(solution)/shard_map/ppermute | solution.py:66
  200.8 10.5 %collective-permute-start.42 = (bf16[104,768]{1,0:T(8,128)(2,1)S(1)}, bf16[104,768]{1,0:T(8,128)(2,1)S(1)}, u32[]{:S(2)}, u32[]{:S(2)}) collective-permute-start(bf16[104,768]{1,0:T(8,128)(2,1)S(1)} %get-tuple-element.77), channel_id=1, source_target_pairs={{0,96},{1,97},{2,98},{3,99},{4,100},{5,101},{6,102},{7,103},{8,40}... | collective-permute-start | bytes 479240 | tf_op jit(solution)/shard_map/ppermute | solution.py:66
  201.6 9.6 %collective-permute-start.41 = (bf16[104,768]{1,0:T(8,128)(2,1)S(1)}, bf16[104,768]{1,0:T(8,128)(2,1)S(1)}, u32[]{:S(2)}, u32[]{:S(2)}) collective-permute-start(bf16[104,768]{1,0:T(8,128)(2,1)S(1)} %get-tuple-element.75), channel_id=1, source_target_pairs={{0,32},{1,33},{2,34},{3,35},{4,36},{5,37},{6,38},{7,39},{8,104},{9... | collective-permute-start | bytes 479240 | tf_op jit(solution)/shard_map/ppermute | solution.py:66
  211.4 9.9 %collective-permute-start.44 = (f32[104,768]{1,0:T(8,128)S(1)}, f32[104,768]{1,0:T(8,128)S(1)}, u32[]{:S(2)}, u32[]{:S(2)}) collective-permute-start(f32[104,768]{1,0:T(8,128)S(1)} %add_add_fusion), channel_id=1, source_target_pairs={{0,16},{1,17},{2,18},{3,19},{4,20},{5,21},{6,22},{7,23},{8,24},{9,... | collective-permute-start | bytes 958472 | tf_op jit(solution)/shard_map/ppermute | solution.py:66
  221.4 4.2 %collective-permute-start.45 = (bf16[104,768]{1,0:T(8,128)(2,1)S(1)}, bf16[104,768]{1,0:T(8,128)(2,1)S(1)}, u32[]{:S(2)}, u32[]{:S(2)}) collective-permute-start(bf16[104,768]{1,0:T(8,128)(2,1)S(1)} %get-tuple-element.68), channel_id=1, source_target_pairs={{0,32},{1,33},{2,34},{3,35},{4,36},{5,37},{6,38},{7,39},{8,104},{9... | collective-permute-start | bytes 479240 | tf_op jit(solution)/shard_map/ppermute | solution.py:66
  222.4 8.1 %collective-permute-start.46 = (bf16[104,768]{1,0:T(8,128)(2,1)S(1)}, bf16[104,768]{1,0:T(8,128)(2,1)S(1)}, u32[]{:S(2)}, u32[]{:S(2)}) collective-permute-start(bf16[104,768]{1,0:T(8,128)(2,1)S(1)} %get-tuple-element.68), channel_id=1, source_target_pairs={{0,96},{1,97},{2,98},{3,99},{4,100},{5,101},{6,102},{7,103},{8,40}... | collective-permute-start | bytes 479240 | tf_op jit(solution)/shard_map/ppermute | solution.py:66
  222.9 7.6 %collective-permute-start.47 = (bf16[104,768]{1,0:T(8,128)(2,1)S(1)}, bf16[104,768]{1,0:T(8,128)(2,1)S(1)}, u32[]{:S(2)}, u32[]{:S(2)}) collective-permute-start(bf16[104,768]{1,0:T(8,128)(2,1)S(1)} %get-tuple-element.68), channel_id=1, source_target_pairs={{0,64},{1,65},{2,66},{3,67},{4,68},{5,69},{6,70},{7,71},{8,72},{9,... | collective-permute-start | bytes 479240 | tf_op jit(solution)/shard_map/ppermute | solution.py:66
  230.6 4.9 %collective-permute-start.48 = (bf16[416,768]{1,0:T(8,128)(2,1)S(1)}, bf16[416,768]{1,0:T(8,128)(2,1)S(1)}, u32[]{:S(2)}, u32[]{:S(2)}) collective-permute-start(bf16[416,768]{1,0:T(8,128)(2,1)S(1)} %constant_dynamic-update-slice_fusion), channel_id=1, source_target_pairs={{0,8},{1,9},{2,10},{3,11},{4,12},{5,13},{6,14},{7,15},{8,0},{9,1},... | collective-permute-start | bytes 1916936 | tf_op jit(solution)/shard_map/ppermute | solution.py:66

commit v4 on v3

--- a/solution.py
+++ b/solution.py
@@ -238,7 +238,7 @@
             pltpu.SMEM((most, 1 + 2 * STEP), jnp.int32),
             pltpu.SemaphoreType.DMA((49,)),
         ],
-        compiler_params=pltpu.CompilerParams(vmem_limit_bytes=24 * 1024 * 1024),
+        compiler_params=pltpu.CompilerParams(vmem_limit_bytes=(22 if q == 1 else 12) * 1024 * 1024),
         cost_estimate=pl.CostEstimate(flops=96 * 2 * 128 * 128 * 896, bytes_accessed=2**23, transcendentals=0),
         name="multiply",
     )(meta, factors, *panels)
@@ -286,7 +286,7 @@
         in_specs=[pl.BlockSpec(memory_space=pltpu.VMEM)] * 3,
         out_specs=[pl.BlockSpec(memory_space=pltpu.VMEM)] * many,
         scratch_shapes=[pltpu.VMEM((ROWS, WIDE), bf16), pltpu.VMEM((WIDE, WIDE), bf16)],
-        compiler_params=pltpu.CompilerParams(vmem_limit_bytes=30 * 1024 * 1024),
+        compiler_params=pltpu.CompilerParams(vmem_limit_bytes=14 * 1024 * 1024),
         cost_estimate=pl.CostEstimate(flops=2 * 768 * 896 * 896, bytes_accessed=2**23, transcendentals=0),
         name="cross",
     )(half, slab, theirs)
@@ -338,7 +338,7 @@
             pltpu.VMEM((WIDE, ROWS), f32),
             pltpu.SemaphoreType.DMA((6,)),
         ],
-        compiler_params=pltpu.CompilerParams(vmem_limit_bytes=36 * 1024 * 1024),
+        compiler_params=pltpu.CompilerParams(vmem_limit_bytes=20 * 1024 * 1024),
         cost_estimate=pl.CostEstimate(flops=4 * 768 * 896 * 896, bytes_accessed=2**23, transcendentals=0),
         name="exchange",
     )(*halves, *low_parts, *x_parts)
@@ -377,13 +377,10 @@
     ahead = send(both, around(one, 1, False))
     behind = send(both, around(one, -1, False))
     far = send(both, around(one, 2, False))
-    lists = jnp.concatenate([block_rows[0] % ROW_BLOCKS, block_cols[0], block_count[0]])
-    lists = jnp.pad(lists, (0, 256 - 2 * SLOTS - 1))[None]
-    meta = jnp.concatenate([lists, swap_cores(lists)])
     stage = put(stage, ahead[:, None], d1=(at_one - 1) % 4)
     stage = put(stage, behind[:, None], d1=(at_one + 1) % 4)
     stage = put(stage, far[:, None], d1=(at_one + 2) % 4)
-    stage, other_blocks, meta = lax.optimization_barrier((stage, other_blocks, meta))
+    stage, other_blocks = lax.optimization_barrier((stage, other_blocks))
 
     main, rest = stage[:, :, :MAIN], stage[:, :, MAIN:]
     zz = ("z", "z")
@@ -391,8 +388,8 @@
     rest_ahead = send(rest, around(two, 1, False))
     rest_behind = send(rest, around(two, -1, False))
     main_far = send(main_ahead, around(zz, 1, True))
-    main_behind = send_after(main, around(zz, -1, True), main_ahead)
-    rest_far = send_after(rest, around(two, 2, False), rest_ahead)
+    main_behind = send(main, around(zz, -1, True))
+    rest_far = send_after(rest, around(two, 2, False), rest_ahead, main_ahead)
 
     mains = [jnp.zeros((ZH, ZL, 4, MAIN, WIDE), bf16)] * 2
     for array, at in (
@@ -422,6 +419,10 @@
     behind_0 = send_after(mains[0], behind, behind_1)
     far_0 = send(ahead_0, ahead)
     far_1 = send_after(behind_1, behind, rest_ahead)
+    lists = lax.optimization_barrier((block_rows[0], block_cols[0], block_count[0], ahead_0))
+    lists = jnp.concatenate([lists[0] % ROW_BLOCKS, lists[1], lists[2]])
+    lists = jnp.pad(lists, (0, 256 - 2 * SLOTS - 1))[None]
+    meta = jnp.concatenate([lists, swap_cores(lists)])
     rest_far = send_after(rest_ahead, around(zz, 1, True), rest_behind)
     arrays = (
         (mains[0], ahead_0, behind_0, far_0),
@@ -469,7 +470,8 @@
         send(rows_of(half_mine, (x - sign) % 4, SHARD), behind),
         send(rows_of(half_mine, (x + 2) % 4, SHARD), opposite),
     )
-    parts, half_mine = lax.optimization_barrier((parts, half_mine))
+    parts, second = lax.optimization_barrier((parts, second[:2])), second
+    parts, second = parts[0], (*parts[1], *second[2:])
     mine = add(*parts).astype(bf16)
     first_shard = add(rows_of(mine, zl, SHARD), swap_low(rows_of(mine, 1 - zl, SHARD)))
     second_shard = add(*second)

time: 237 us -> 244 us (1.030)
  local copies, waits for them, and re-layouts: 7.93 us -> 18.1 us
  waiting for transfers between devices: 124 us -> 115 us
  starting transfers between devices: 63.4 us -> 71.1 us
  other arithmetic: 10.8 us -> 8.25 us
    ppermute x49, waiting for transfers between devices: 124 us -> 115 us  [send(): return lax.ppermute(array, AXES, pairs)]
    unnamed x10 -> x34, local copies, waits for them, and re-layouts: 3.08 us -> 12.2 us
    ppermute x49, starting transfers between devices: 63.4 us -> 71.1 us  [send(): return lax.ppermute(array, AXES, pairs)]
  transfers between devices with their start and end apart: 49 -> 49, of which waited for: 30 -> 32; matrix products, arithmetic and copies ran while one was open for 3% -> 3% of each run, Pallas kernels for 8% -> 8%
where the time goes in v4:
time: 244 us; the launch traced here: 242 us
  waiting for transfers between devices  115 us (47%)
  starting transfers between devices  71.1 us (29%)
  Pallas kernels  29.2 us (12%)
  local copies, waits for them, and re-layouts  18.1 us (7%)
  other arithmetic  8.25 us (3%)
    ppermute x49, waiting for transfers between devices, send(): return lax.ppermute(array, AXES, pairs)  115 us
    ppermute x49, starting transfers between devices, send(): return lax.ppermute(array, AXES, pairs)  71.1 us
    pallas_call x2, Pallas kernels, multiply(): pl.pallas_call(kernel, out_shape=[half, held] if q == 1 else half, in_spe...  17.2 us
    unnamed x34, local copies, waits for them, and re-layouts  12.2 us
    pallas_call x1, Pallas kernels, exchange(): pl.pallas_call(exchange_kernel, out_shape=[jax.ShapeDtypeStruct((CROSS //...  6.38 us
  transfers between devices with their start and end apart: 49, of which 32 were waited for; matrix products, arithmetic and copies ran while one was open for 3% of the time, Pallas kernels for 8%

profile of v4, /device:TPU:1, one launch (start us, length us, event | category | flops | bytes accessed | tf_op | source)
XLA Modules:
  0.0 242.4 jit_solution(7303458435855900844)
XLA Ops:
  0.9 1.5 collective-permute-start
  4.6 1.4 collective-permute-start.1
  6.1 1.9 collective-permute-start.2
  8.0 1.2 collective-permute-start.3
  9.3 1.5 collective-permute-done.1
  12.2 1.8 collective-permute-done.3
  14.2 3.8 %collective-permute-start.5 = (bf16[2,4,32,896]{3,2,1,0:T(8,128)(2,1)S(1)}, bf16[2,4,32,896]{3,2,1,0:T(8,128)(2,1)S(1)}, u32[]{:S(2)}, u32[]{:S(2)}) collective-permute-start(bf16[2,4,32,896]{3,2,1,0:T(8,128)(2,1)S(1)} %slice.42), channel_id=1, source_target_pairs={{0,1},{1,16},{2,3},{3,18},{4,5},{5,20},{6,7},{7,22},{8,25},{9,8},{... | collective-permute-start | bytes 1376264 | tf_op jit(solution)/shard_map/ppermute | solution.py:66
  18.0 1.0 collective-permute-start.8
  19.0 1.8 collective-permute-start.9
  21.1 3.3 %collective-permute-done.8 = bf16[2,4,16,896]{3,2,1,0:T(8,128)(2,1)S(1)} collective-permute-done((bf16[2,4,16,896]{3,2,1,0:T(8,128)(2,1)S(1)}, bf16[2,4,16,896]{3,2,1,0:T(8,128)(2,1)S(1)}, u32[]{:S(2)}, u32[]{:S(2)}) %collective-permute-start.8) | collective-permute-done | bytes 229408 | tf_op jit(solution)/shard_map/ppermute | solution.py:66
  24.5 2.1 collective-permute-done.5
  26.7 3.5 %collective-permute-start.10 = (bf16[2,4,16,896]{3,2,1,0:T(8,128)(2,1)S(1)}, bf16[2,4,16,896]{3,2,1,0:T(8,128)(2,1)S(1)}, u32[]{:S(2)}, u32[]{:S(2)}) collective-permute-start(bf16[2,4,16,896]{3,2,1,0:T(8,128)(2,1)S(1)} %slice.50), channel_id=1, source_target_pairs={{0,64},{1,65},{2,66},{3,67},{4,68},{5,69},{6,70},{7,71},{8,12},{9,... | collective-permute-start | bytes 688136 | tf_op jit(solution)/shard_map/ppermute | solution.py:66
  30.2 3.4 %collective-permute-start.7 = (bf16[2,4,32,896]{3,2,1,0:T(8,128)(2,1)S(1)}, bf16[2,4,32,896]{3,2,1,0:T(8,128)(2,1)S(1)}, u32[]{:S(2)}, u32[]{:S(2)}) collective-permute-start(bf16[2,4,32,896]{3,2,1,0:T(8,128)(2,1)S(1)} %collective-permute-done.5), channel_id=1, source_target_pairs={{0,1},{1,16},{2,3},{3,18},{4,5},{5,20},{6,7},{7,22},{8,25},{9,8},{... | collective-permute-start | bytes 1376264 | tf_op jit(solution)/shard_map/ppermute | solution.py:66
  33.8 5.2 %collective-permute-done.7 = bf16[2,4,32,896]{3,2,1,0:T(8,128)(2,1)S(1)} collective-permute-done((bf16[2,4,32,896]{3,2,1,0:T(8,128)(2,1)S(1)}, bf16[2,4,32,896]{3,2,1,0:T(8,128)(2,1)S(1)}, u32[]{:S(2)}, u32[]{:S(2)}) %collective-permute-start.7) | collective-permute-done | bytes 458784 | tf_op jit(solution)/shard_map/ppermute | solution.py:66
  39.4 2.4 collective-permute-start.13
  41.8 3.1 %collective-permute-start.17 = (bf16[2,4,4,16,896]{4,3,2,1,0:T(8,128)(2,1)S(1)}, bf16[2,4,4,16,896]{4,3,2,1,0:T(8,128)(2,1)S(1)}, u32[]{:S(2)}, u32[]{:S(2)}) collective-permute-start(bf16[2,4,4,16,896]{4,3,2,1,0:T(8,128)(2,1)S(1)} %bitcast_dynamic-update-slice_fusion.15), channel_id=1, source_target_pairs={{0,1},{1,16},{2,3},{3,18},{4,5},{5,20},{6,7},{7,22},{8,25},{9,8},{... | collective-permute-start | bytes 2752520 | tf_op jit(solution)/shard_map/ppermute | solution.py:66
  46.0 6.8 %collective-permute-done.11 = bf16[2,2,4,32,896]{4,3,2,1,0:T(8,128)(2,1)S(1)} collective-permute-done((bf16[2,2,4,32,896]{4,3,2,1,0:T(8,128)(2,1)S(1)}, bf16[2,2,4,32,896]{4,3,2,1,0:T(8,128)(2,1)S(1)}, u32[]{:S(2)}, u32[]{:S(2)}) %collective-permute-start.11) | collective-permute-done | bytes 917536 | tf_op jit(solution)/shard_map/ppermute | solution.py:66
  53.5 2.7 %collective-permute-start.14 = (bf16[2,2,4,32,896]{4,3,2,1,0:T(8,128)(2,1)S(1)}, bf16[2,2,4,32,896]{4,3,2,1,0:T(8,128)(2,1)S(1)}, u32[]{:S(2)}, u32[]{:S(2)}) collective-permute-start(bf16[2,2,4,32,896]{4,3,2,1,0:T(8,128)(2,1)S(1)} %get-tuple-element.48), channel_id=1, source_target_pairs={{0,96},{1,97},{2,98},{3,99},{4,100},{5,101},{6,102},{7,103},{8,14}... | collective-permute-start | bytes 2752520 | tf_op jit(solution)/shard_map/ppermute | solution.py:66
  56.2 3.9 %collective-permute-done.17 = bf16[2,4,4,16,896]{4,3,2,1,0:T(8,128)(2,1)S(1)} collective-permute-done((bf16[2,4,4,16,896]{4,3,2,1,0:T(8,128)(2,1)S(1)}, bf16[2,4,4,16,896]{4,3,2,1,0:T(8,128)(2,1)S(1)}, u32[]{:S(2)}, u32[]{:S(2)}) %collective-permute-start.17) | collective-permute-done | bytes 917536 | tf_op jit(solution)/shard_map/ppermute | solution.py:66
  60.2 6.4 %collective-permute-done.19 = bf16[2,4,4,16,896]{4,3,2,1,0:T(8,128)(2,1)S(1)} collective-permute-done((bf16[2,4,4,16,896]{4,3,2,1,0:T(8,128)(2,1)S(1)}, bf16[2,4,4,16,896]{4,3,2,1,0:T(8,128)(2,1)S(1)}, u32[]{:S(2)}, u32[]{:S(2)}) %collective-permute-start.19) | collective-permute-done | bytes 917536 | tf_op jit(solution)/shard_map/ppermute | solution.py:66
  67.5 12.8 %collective-permute-done.15 = bf16[2,2,4,32,896]{4,3,2,1,0:T(8,128)(2,1)S(1)} collective-permute-done((bf16[2,2,4,32,896]{4,3,2,1,0:T(8,128)(2,1)S(1)}, bf16[2,2,4,32,896]{4,3,2,1,0:T(8,128)(2,1)S(1)}, u32[]{:S(2)}, u32[]{:S(2)}) %collective-permute-start.15) | collective-permute-done | bytes 917536 | tf_op jit(solution)/shard_map/ppermute | solution.py:66
  81.7 4.2 %collective-permute-start.21 = (bf16[768,896]{1,0:T(8,128)(2,1)S(1)}, bf16[768,896]{1,0:T(8,128)(2,1)S(1)}, u32[]{:S(2)}, u32[]{:S(2)}) collective-permute-start(bf16[768,896]{1,0:T(8,128)(2,1)S(1)} %bitcast.101), channel_id=1, source_target_pairs={{0,8},{1,9},{2,10},{3,11},{4,12},{5,13},{6,14},{7,15},{8,0},{9,1},... | collective-permute-start | bytes 4128776 | tf_op jit(solution)/shard_map/ppermute | solution.py:66
  86.9 1.7 collective-permute-done.12
  88.7 8.4 %multiply.2 = (bf16[768,896]{1,0:T(8,128)(2,1)S(1)}, bf16[4,2,2,4,2,48,896]{6,5,4,3,2,1,0:T(8,128)(2,1)S(1)}) custom-call(s32[2,256]{1,0:T(2,128)S(1)} %pad_add_fusion.refs_0_, bf16[96,128,128]{2,1,0:T(8,128)(2,1)S(1)} %collective-permute-done.4.refs_1_, bf16[4,2,2,4,32,896]{5,4,3,2,1,0:T(8,128)(2,1)S(1)} %bitcast_dynamic-update-slice_fusion.8.refs_2_.main0, ...), custom_call_target="tpu_custom_call" | custom-call | flops 2818572288 | bytes 8388608 | tf_op jit(solution)/shard_map/multiply/pallas_call | solution.py:228
  97.1 4.1 %copy-done = bf16[4,2,2,4,2,48,896]{6,5,4,3,2,1,0:T(8,128)(2,1)} copy-done((bf16[4,2,2,4,2,48,896]{6,5,4,3,2,1,0:T(8,128)(2,1)}, bf16[4,2,2,4,2,48,896]{6,5,4,3,2,1,0:T(8,128)(2,1)S(1)}, u32[]{:S(2)}) %copy-start) | copy-done | bytes 11010072
  101.2 2.9 %cross.2 = (bf16[416,896]{1,0:T(8,128)(2,1)S(1)}, bf16[416,896]{1,0:T(8,128)(2,1)}) custom-call(bf16[768,896]{1,0:T(8,128)(2,1)S(1)} %get-tuple-element.54.refs_0_.refs_1_, bf16[768,896]{1,0:T(8,128)(2,1)S(1)} %bitcast.102, bf16[768,896]{1,0:T(8,128)(2,1)S(1)} %collective-permute-done.21.refs_2_), custom_call_target="tpu_custom_call" | custom-call | flops 1233125376 | bytes 8388608 | tf_op jit(solution)/shard_map/cross/pallas_call | solution.py:283
  105.0 4.1 %copy-done.1 = bf16[4,2,2,4,2,48,896]{6,5,4,3,2,1,0:T(8,128)(2,1)S(1)} copy-done((bf16[4,2,2,4,2,48,896]{6,5,4,3,2,1,0:T(8,128)(2,1)S(1)}, bf16[4,2,2,4,2,48,896]{6,5,4,3,2,1,0:T(8,128)(2,1)}, u32[]{:S(2)}) %copy-start.1) | copy-done | bytes 11010072
  109.1 8.8 %multiply.3.refs_0_ = bf16[768,896]{1,0:T(8,128)(2,1)S(1)} custom-call(s32[2,256]{1,0:T(2,128)S(1)} %pad_add_fusion.refs_0_, bf16[96,128,128]{2,1,0:T(8,128)(2,1)S(1)} %bitcast.100, bf16[4,2,2,4,2,48,896]{6,5,4,3,2,1,0:T(8,128)(2,1)S(1)} %copy-done.1), custom_call_target="tpu_custom_call" | custom-call | flops 2818572288 | bytes 8388608 | tf_op jit(solution)/shard_map/multiply/pallas_call | solution.py:228
  118.0 1.8 cross.3
  120.3 1.0 collective-permute-start.23
  121.3 1.6 collective-permute-start.24
  122.9 1.3 add_convert_fusion
  125.9 1.6 collective-permute-start.28
  128.3 4.0 %collective-permute-done.23 = bf16[208,896]{1,0:T(8,128)(2,1)S(1)} collective-permute-done((bf16[208,896]{1,0:T(8,128)(2,1)S(1)}, bf16[208,896]{1,0:T(8,128)(2,1)S(1)}, u32[]{:S(2)}, u32[]{:S(2)}) %collective-permute-start.23) | collective-permute-done | bytes 372768 | tf_op jit(solution)/shard_map/ppermute | solution.py:66
  132.3 7.2 %collective-permute-done.24 = bf16[208,896]{1,0:T(8,128)(2,1)S(1)} collective-permute-done((bf16[208,896]{1,0:T(8,128)(2,1)S(1)}, bf16[208,896]{1,0:T(8,128)(2,1)S(1)}, u32[]{:S(2)}, u32[]{:S(2)}) %collective-permute-start.24) | collective-permute-done | bytes 372768 | tf_op jit(solution)/shard_map/ppermute | solution.py:66
  140.6 4.7 %collective-permute-start.33 = (bf16[104,896]{1,0:T(8,128)(2,1)S(1)}, bf16[104,896]{1,0:T(8,128)(2,1)S(1)}, u32[]{:S(2)}, u32[]{:S(2)}) collective-permute-start(bf16[104,896]{1,0:T(8,128)(2,1)S(1)} %constant_dynamic-slice_fusion), channel_id=1, source_target_pairs={{0,1},{1,0},{2,3},{3,2},{4,5},{5,4},{6,7},{7,6},{8,9},{9,8},{10,11... | collective-permute-start | bytes 559112 | tf_op jit(solution)/shard_map/ppermute | solution.py:66
  145.3 2.2 collective-permute-done.27
  148.3 1.3 fusion.1
  149.6 6.0 %collective-permute-start.34 = (bf16[104,896]{1,0:T(8,128)(2,1)S(1)}, bf16[104,896]{1,0:T(8,128)(2,1)S(1)}, u32[]{:S(2)}, u32[]{:S(2)}) collective-permute-start(bf16[104,896]{1,0:T(8,128)(2,1)S(1)} %get-tuple-element.98), channel_id=1, source_target_pairs={{0,8},{1,9},{2,10},{3,11},{4,12},{5,13},{6,14},{7,15},{8,0},{9,1},... | collective-permute-start | bytes 559112 | tf_op jit(solution)/shard_map/ppermute | solution.py:66
  157.3 1.5 collective-permute-start.31
  159.3 1.2 collective-permute-start.35
  160.5 2.7 %collective-permute-done.30 = bf16[104,896]{1,0:T(8,128)(2,1)S(1)} collective-permute-done((bf16[104,896]{1,0:T(8,128)(2,1)S(1)}, bf16[104,896]{1,0:T(8,128)(2,1)S(1)}, u32[]{:S(2)}, u32[]{:S(2)}) %collective-permute-start.30) | collective-permute-done | bytes 186400 | tf_op jit(solution)/shard_map/ppermute | solution.py:66
  163.3 5.5 %collective-permute-done.31 = bf16[104,896]{1,0:T(8,128)(2,1)S(1)} collective-permute-done((bf16[104,896]{1,0:T(8,128)(2,1)S(1)}, bf16[104,896]{1,0:T(8,128)(2,1)S(1)}, u32[]{:S(2)}, u32[]{:S(2)}) %collective-permute-start.31) | collective-permute-done | bytes 186400 | tf_op jit(solution)/shard_map/ppermute | solution.py:66
  168.8 1.8 collective-permute-start.36
  173.8 5.7 %collective-permute-done.37.refs_5_ = bf16[208,896]{1,0:T(8,128)(2,1)S(1)} collective-permute-done((bf16[208,896]{1,0:T(8,128)(2,1)S(1)}, bf16[208,896]{1,0:T(8,128)(2,1)S(1)}, u32[]{:S(2)}, u32[]{:S(2)}) %collective-permute-start.37) | collective-permute-done | bytes 372768 | tf_op jit(solution)/shard_map/ppermute | solution.py:66
  179.5 11.1 %collective-permute-done.38.refs_6_ = bf16[208,896]{1,0:T(8,128)(2,1)S(1)} collective-permute-done((bf16[208,896]{1,0:T(8,128)(2,1)S(1)}, bf16[208,896]{1,0:T(8,128)(2,1)S(1)}, u32[]{:S(2)}, u32[]{:S(2)}) %collective-permute-start.38) | collective-permute-done | bytes 372768 | tf_op jit(solution)/shard_map/ppermute | solution.py:66
  190.6 1.0 copy-done.10
  191.6 1.3 copy-done.12
  193.0 6.4 %exchange.1 = (f32[416,768]{1,0:T(8,128)S(1)}, f32[416,768]{1,0:T(8,128)}) custom-call(bf16[768,896]{1,0:T(8,128)(2,1)S(1)} %copy-done.6, bf16[768,896]{1,0:T(8,128)(2,1)S(1)} %copy-done.12, bf16[416,896]{1,0:T(8,128)(2,1)S(1)} %constant_dynamic-update-slice_fusion.6.refs_2_, bf16[416,896]{1,0:T(8,128)(2,1)S(1)} %collective-permute-done.36.refs_3_, ...), custom_call_target="tpu_custom_call" | custom-call | flops 2466250752 | bytes 8388608 | tf_op jit(solution)/shard_map/exchange/pallas_call | solution.py:331
  199.3 1.3 collective-permute-start.40
  200.7 3.0 %collective-permute-done.40 = f32[416,768]{1,0:T(8,128)} collective-permute-done((f32[416,768]{1,0:T(8,128)}, f32[416,768]{1,0:T(8,128)}, u32[]{:S(2)}, u32[]{:S(2)}) %collective-permute-start.40) | collective-permute-done | bytes 1277984 | tf_op jit(solution)/shard_map/ppermute | solution.py:66
  203.6 1.5 add.405
  206.0 2.0 collective-permute-start.41
  208.0 4.1 %collective-permute-done.43 = bf16[104,768]{1,0:T(8,128)(2,1)S(1)} collective-permute-done((bf16[104,768]{1,0:T(8,128)(2,1)S(1)}, bf16[104,768]{1,0:T(8,128)(2,1)S(1)}, u32[]{:S(2)}, u32[]{:S(2)}) %collective-permute-start.43) | collective-permute-done | bytes 159776 | tf_op jit(solution)/shard_map/ppermute | solution.py:66
  212.1 3.2 %collective-permute-done.42 = bf16[104,768]{1,0:T(8,128)(2,1)S(1)} collective-permute-done((bf16[104,768]{1,0:T(8,128)(2,1)S(1)}, bf16[104,768]{1,0:T(8,128)(2,1)S(1)}, u32[]{:S(2)}, u32[]{:S(2)}) %collective-permute-start.42) | collective-permute-done | bytes 159776 | tf_op jit(solution)/shard_map/ppermute | solution.py:66
  215.4 2.9 %collective-permute-start.44 = (f32[104,768]{1,0:T(8,128)S(1)}, f32[104,768]{1,0:T(8,128)S(1)}, u32[]{:S(2)}, u32[]{:S(2)}) collective-permute-start(f32[104,768]{1,0:T(8,128)S(1)} %add_add_fusion), channel_id=1, source_target_pairs={{0,16},{1,17},{2,18},{3,19},{4,20},{5,21},{6,22},{7,23},{8,24},{9,... | collective-permute-start | bytes 958472 | tf_op jit(solution)/shard_map/ppermute | solution.py:66
  218.3 6.5 %collective-permute-done.44 = f32[104,768]{1,0:T(8,128)S(1)} collective-permute-done((f32[104,768]{1,0:T(8,128)S(1)}, f32[104,768]{1,0:T(8,128)S(1)}, u32[]{:S(2)}, u32[]{:S(2)}) %collective-permute-start.44) | collective-permute-done | bytes 319520 | tf_op jit(solution)/shard_map/ppermute | solution.py:66
  224.9 4.3 %collective-permute-start.45 = (bf16[104,768]{1,0:T(8,128)(2,1)S(1)}, bf16[104,768]{1,0:T(8,128)(2,1)S(1)}, u32[]{:S(2)}, u32[]{:S(2)}) collective-permute-start(bf16[104,768]{1,0:T(8,128)(2,1)S(1)} %get-tuple-element.74), channel_id=1, source_target_pairs={{0,32},{1,33},{2,34},{3,35},{4,36},{5,37},{6,38},{7,39},{8,104},{9... | collective-permute-start | bytes 479240 | tf_op jit(solution)/shard_map/ppermute | solution.py:66
  229.2 1.3 collective-permute-start.47
  231.4 4.4 %collective-permute-done.46 = bf16[104,768]{1,0:T(8,128)(2,1)S(1)} collective-permute-done((bf16[104,768]{1,0:T(8,128)(2,1)S(1)}, bf16[104,768]{1,0:T(8,128)(2,1)S(1)}, u32[]{:S(2)}, u32[]{:S(2)}) %collective-permute-start.46) | collective-permute-done | bytes 159776 | tf_op jit(solution)/shard_map/ppermute | solution.py:66
  235.8 1.4 collective-permute-done.47
  237.2 1.8 collective-permute-start.48
  239.0 1.7 collective-permute-done.48
  240.8 1.6 convert_bitcast_fusion
  (140 shorter events, 23.5 us)
Async XLA Ops:
  0.9 2.4 %collective-permute-start = (bf16[48,800]{1,0:T(8,128)(2,1)S(1)}, bf16[48,800]{1,0:T(8,128)(2,1)S(1)}, u32[]{:S(2)}, u32[]{:S(2)}) collective-permute-start(bf16[48,800]{1,0:T(8,128)(2,1)S(1)} %broadcast_select_fusion.4), channel_id=1, source_target_pairs={{0,8},{1,9},{2,10},{3,11},{4,12},{5,13},{6,14},{7,15},{8,0},{9,1},... | collective-permute-start | bytes 230408 | tf_op jit(solution)/shard_map/ppermute | solution.py:66
  3.3 10.8 %collective-permute-start.4 = (bf16[96,128,128]{2,1,0:T(8,128)(2,1)}, bf16[96,128,128]{2,1,0:T(8,128)(2,1)S(1)}, u32[]{:S(2)}, u32[]{:S(2)}) collective-permute-start(bf16[96,128,128]{2,1,0:T(8,128)(2,1)} %bitcast.99), channel_id=1, source_target_pairs={{0,8},{1,9},{2,10},{3,11},{4,12},{5,13},{6,14},{7,15},{8,0},{9,1},... | collective-permute-start | bytes 9437192 | tf_op jit(solution)/shard_map/ppermute | solution.py:66
  4.6 6.1 %collective-permute-start.1 = (bf16[2,48,896]{2,1,0:T(8,128)(2,1)S(1)}, bf16[2,48,896]{2,1,0:T(8,128)(2,1)}, u32[]{:S(2)}, u32[]{:S(2)}) collective-permute-start(bf16[2,48,896]{2,1,0:T(8,128)(2,1)S(1)} %fusion.10), channel_id=1, source_target_pairs={{0,2},{1,3},{2,4},{3,5},{4,6},{5,7},{6,0},{7,1},{8,40},{9,41},{10,... | collective-permute-start | bytes 516104 | tf_op jit(solution)/shard_map/ppermute | solution.py:66
  6.1 6.1 %collective-permute-start.2 = (bf16[2,48,896]{2,1,0:T(8,128)(2,1)S(1)}, bf16[2,48,896]{2,1,0:T(8,128)(2,1)S(1)}, u32[]{:S(2)}, u32[]{:S(2)}) collective-permute-start(bf16[2,48,896]{2,1,0:T(8,128)(2,1)S(1)} %fusion.10), channel_id=1, source_target_pairs={{0,6},{1,7},{2,0},{3,1},{4,2},{5,3},{6,4},{7,5},{8,104},{9,105},{1... | collective-permute-start | bytes 516104 | tf_op jit(solution)/shard_map/ppermute | solution.py:66
  8.0 6.1 %collective-permute-start.3 = (bf16[2,48,896]{2,1,0:T(8,128)(2,1)S(1)}, bf16[2,48,896]{2,1,0:T(8,128)(2,1)S(1)}, u32[]{:S(2)}, u32[]{:S(2)}) collective-permute-start(bf16[2,48,896]{2,1,0:T(8,128)(2,1)S(1)} %fusion.10), channel_id=1, source_target_pairs={{0,4},{1,5},{2,6},{3,7},{4,0},{5,1},{6,2},{7,3},{8,72},{9,73},{10,... | collective-permute-start | bytes 516104 | tf_op jit(solution)/shard_map/ppermute | solution.py:66
  14.2 12.5 %collective-permute-start.5 = (bf16[2,4,32,896]{3,2,1,0:T(8,128)(2,1)S(1)}, bf16[2,4,32,896]{3,2,1,0:T(8,128)(2,1)S(1)}, u32[]{:S(2)}, u32[]{:S(2)}) collective-permute-start(bf16[2,4,32,896]{3,2,1,0:T(8,128)(2,1)S(1)} %slice.42), channel_id=1, source_target_pairs={{0,1},{1,16},{2,3},{3,18},{4,5},{5,20},{6,7},{7,22},{8,25},{9,8},{... | collective-permute-start | bytes 1376264 | tf_op jit(solution)/shard_map/ppermute | solution.py:66
  18.0 15.6 %collective-permute-start.6 = (bf16[2,4,32,896]{3,2,1,0:T(8,128)(2,1)S(1)}, bf16[2,4,32,896]{3,2,1,0:T(8,128)(2,1)S(1)}, u32[]{:S(2)}, u32[]{:S(2)}) collective-permute-start(bf16[2,4,32,896]{3,2,1,0:T(8,128)(2,1)S(1)} %slice.42), channel_id=1, source_target_pairs={{0,17},{1,0},{2,19},{3,2},{4,21},{5,4},{6,23},{7,6},{8,9},{9,24},{... | collective-permute-start | bytes 1376264 | tf_op jit(solution)/shard_map/ppermute | solution.py:66
  18.0 6.4 %collective-permute-start.8 = (bf16[2,4,16,896]{3,2,1,0:T(8,128)(2,1)S(1)}, bf16[2,4,16,896]{3,2,1,0:T(8,128)(2,1)S(1)}, u32[]{:S(2)}, u32[]{:S(2)}) collective-permute-start(bf16[2,4,16,896]{3,2,1,0:T(8,128)(2,1)S(1)} %slice.50), channel_id=1, source_target_pairs={{0,32},{1,33},{2,34},{3,35},{4,36},{5,37},{6,38},{7,39},{8,10},{9,... | collective-permute-start | bytes 688136 | tf_op jit(solution)/shard_map/ppermute | solution.py:66
  19.0 5.5 %collective-permute-start.9 = (bf16[2,4,16,896]{3,2,1,0:T(8,128)(2,1)S(1)}, bf16[2,4,16,896]{3,2,1,0:T(8,128)(2,1)S(1)}, u32[]{:S(2)}, u32[]{:S(2)}) collective-permute-start(bf16[2,4,16,896]{3,2,1,0:T(8,128)(2,1)S(1)} %slice.50), channel_id=1, source_target_pairs={{0,96},{1,97},{2,98},{3,99},{4,100},{5,101},{6,102},{7,103},{8,14}... | collective-permute-start | bytes 688136 | tf_op jit(solution)/shard_map/ppermute | solution.py:66
  26.7 7.0 %collective-permute-start.10 = (bf16[2,4,16,896]{3,2,1,0:T(8,128)(2,1)S(1)}, bf16[2,4,16,896]{3,2,1,0:T(8,128)(2,1)S(1)}, u32[]{:S(2)}, u32[]{:S(2)}) collective-permute-start(bf16[2,4,16,896]{3,2,1,0:T(8,128)(2,1)S(1)} %slice.50), channel_id=1, source_target_pairs={{0,64},{1,65},{2,66},{3,67},{4,68},{5,69},{6,70},{7,71},{8,12},{9,... | collective-permute-start | bytes 688136 | tf_op jit(solution)/shard_map/ppermute | solution.py:66
  30.2 8.8 %collective-permute-start.7 = (bf16[2,4,32,896]{3,2,1,0:T(8,128)(2,1)S(1)}, bf16[2,4,32,896]{3,2,1,0:T(8,128)(2,1)S(1)}, u32[]{:S(2)}, u32[]{:S(2)}) collective-permute-start(bf16[2,4,32,896]{3,2,1,0:T(8,128)(2,1)S(1)} %collective-permute-done.5), channel_id=1, source_target_pairs={{0,1},{1,16},{2,3},{3,18},{4,5},{5,20},{6,7},{7,22},{8,25},{9,8},{... | collective-permute-start | bytes 1376264 | tf_op jit(solution)/shard_map/ppermute | solution.py:66
  39.0 13.8 %collective-permute-start.11 = (bf16[2,2,4,32,896]{4,3,2,1,0:T(8,128)(2,1)S(1)}, bf16[2,2,4,32,896]{4,3,2,1,0:T(8,128)(2,1)S(1)}, u32[]{:S(2)}, u32[]{:S(2)}) collective-permute-start(bf16[2,2,4,32,896]{4,3,2,1,0:T(8,128)(2,1)S(1)} %get-tuple-element.48), channel_id=1, source_target_pairs={{0,32},{1,33},{2,34},{3,35},{4,36},{5,37},{6,38},{7,39},{8,10},{9,... | collective-permute-start | bytes 2752520 | tf_op jit(solution)/shard_map/ppermute | solution.py:66
  39.4 14.1 %collective-permute-start.13 = (bf16[2,2,4,32,896]{4,3,2,1,0:T(8,128)(2,1)S(1)}, bf16[2,2,4,32,896]{4,3,2,1,0:T(8,128)(2,1)S(1)}, u32[]{:S(2)}, u32[]{:S(2)}) collective-permute-start(bf16[2,2,4,32,896]{4,3,2,1,0:T(8,128)(2,1)S(1)} %get-tuple-element.49), channel_id=1, source_target_pairs={{0,96},{1,97},{2,98},{3,99},{4,100},{5,101},{6,102},{7,103},{8,14}... | collective-permute-start | bytes 2752520 | tf_op jit(solution)/shard_map/ppermute | solution.py:66
  41.8 18.4 %collective-permute-start.17 = (bf16[2,4,4,16,896]{4,3,2,1,0:T(8,128)(2,1)S(1)}, bf16[2,4,4,16,896]{4,3,2,1,0:T(8,128)(2,1)S(1)}, u32[]{:S(2)}, u32[]{:S(2)}) collective-permute-start(bf16[2,4,4,16,896]{4,3,2,1,0:T(8,128)(2,1)S(1)} %bitcast_dynamic-update-slice_fusion.15), channel_id=1, source_target_pairs={{0,1},{1,16},{2,3},{3,18},{4,5},{5,20},{6,7},{7,22},{8,25},{9,8},{... | collective-permute-start | bytes 2752520 | tf_op jit(solution)/shard_map/ppermute | solution.py:66
  44.9 21.6 %collective-permute-start.19 = (bf16[2,4,4,16,896]{4,3,2,1,0:T(8,128)(2,1)S(1)}, bf16[2,4,4,16,896]{4,3,2,1,0:T(8,128)(2,1)S(1)}, u32[]{:S(2)}, u32[]{:S(2)}) collective-permute-start(bf16[2,4,4,16,896]{4,3,2,1,0:T(8,128)(2,1)S(1)} %bitcast_dynamic-update-slice_fusion.15), channel_id=1, source_target_pairs={{0,17},{1,0},{2,19},{3,2},{4,21},{5,4},{6,23},{7,6},{8,9},{9,24},{... | collective-permute-start | bytes 2752520 | tf_op jit(solution)/shard_map/ppermute | solution.py:66
  52.9 14.1 %collective-permute-start.16 = (bf16[2,2,4,32,896]{4,3,2,1,0:T(8,128)(2,1)S(1)}, bf16[2,2,4,32,896]{4,3,2,1,0:T(8,128)(2,1)S(1)}, u32[]{:S(2)}, u32[]{:S(2)}) collective-permute-start(bf16[2,2,4,32,896]{4,3,2,1,0:T(8,128)(2,1)S(1)} %get-tuple-element.49), channel_id=1, source_target_pairs={{0,32},{1,33},{2,34},{3,35},{4,36},{5,37},{6,38},{7,39},{8,10},{9,... | collective-permute-start | bytes 2752520 | tf_op jit(solution)/shard_map/ppermute | solution.py:66
  53.5 13.8 %collective-permute-start.14 = (bf16[2,2,4,32,896]{4,3,2,1,0:T(8,128)(2,1)S(1)}, bf16[2,2,4,32,896]{4,3,2,1,0:T(8,128)(2,1)S(1)}, u32[]{:S(2)}, u32[]{:S(2)}) collective-permute-start(bf16[2,2,4,32,896]{4,3,2,1,0:T(8,128)(2,1)S(1)} %get-tuple-element.48), channel_id=1, source_target_pairs={{0,96},{1,97},{2,98},{3,99},{4,100},{5,101},{6,102},{7,103},{8,14}... | collective-permute-start | bytes 2752520 | tf_op jit(solution)/shard_map/ppermute | solution.py:66
  60.2 20.3 %collective-permute-start.18 = (bf16[2,2,4,32,896]{4,3,2,1,0:T(8,128)(2,1)S(1)}, bf16[2,2,4,32,896]{4,3,2,1,0:T(8,128)(2,1)S(1)}, u32[]{:S(2)}, u32[]{:S(2)}) collective-permute-start(bf16[2,2,4,32,896]{4,3,2,1,0:T(8,128)(2,1)S(1)} %collective-permute-done.13), channel_id=1, source_target_pairs={{0,96},{1,97},{2,98},{3,99},{4,100},{5,101},{6,102},{7,103},{8,14}... | collective-permute-start | bytes 2752520 | tf_op jit(solution)/shard_map/ppermute | solution.py:66
  66.6 14.1 %collective-permute-start.20 = (bf16[2,4,4,16,896]{4,3,2,1,0:T(8,128)(2,1)S(1)}, bf16[2,4,4,16,896]{4,3,2,1,0:T(8,128)(2,1)S(1)}, u32[]{:S(2)}, u32[]{:S(2)}) collective-permute-start(bf16[2,4,4,16,896]{4,3,2,1,0:T(8,128)(2,1)S(1)} %collective-permute-done.17), channel_id=1, source_target_pairs={{0,1},{1,16},{2,3},{3,18},{4,5},{5,20},{6,7},{7,22},{8,25},{9,8},{... | collective-permute-start | bytes 2752520 | tf_op jit(solution)/shard_map/ppermute | solution.py:66
  66.6 13.8 %collective-permute-start.15 = (bf16[2,2,4,32,896]{4,3,2,1,0:T(8,128)(2,1)S(1)}, bf16[2,2,4,32,896]{4,3,2,1,0:T(8,128)(2,1)S(1)}, u32[]{:S(2)}, u32[]{:S(2)}) collective-permute-start(bf16[2,2,4,32,896]{4,3,2,1,0:T(8,128)(2,1)S(1)} %collective-permute-done.11), channel_id=1, source_target_pairs={{0,32},{1,33},{2,34},{3,35},{4,36},{5,37},{6,38},{7,39},{8,10},{9,... | collective-permute-start | bytes 2752520 | tf_op jit(solution)/shard_map/ppermute | solution.py:66
  80.8 5.8 %copy-start.16 = (s32[1,96]{1,0:T(1,128)S(1)}, s32[1,96]{1,0:T(1,128)}, u32[]{:S(2)}) copy-start(s32[1,96]{1,0:T(1,128)} %param.7) | copy-start | bytes 1156
  80.8 5.8 %copy-start.15 = (s32[1,96]{1,0:T(1,128)S(1)}, s32[1,96]{1,0:T(1,128)}, u32[]{:S(2)}) copy-start(s32[1,96]{1,0:T(1,128)} %param.8) | copy-start | bytes 1156
  81.7 19.5 %copy-start.3 = (bf16[2,4,2,48,896]{4,3,2,1,0:T(8,128)(2,1)}, bf16[2,4,2,48,896]{4,3,2,1,0:T(8,128)(2,1)S(1)}, u32[]{:S(2)}) copy-start(bf16[2,4,2,48,896]{4,3,2,1,0:T(8,128)(2,1)S(1)} %slab.1) | copy-start | bytes 4128772
  81.7 19.4 %collective-permute-start.21 = (bf16[768,896]{1,0:T(8,128)(2,1)S(1)}, bf16[768,896]{1,0:T(8,128)(2,1)S(1)}, u32[]{:S(2)}, u32[]{:S(2)}) collective-permute-start(bf16[768,896]{1,0:T(8,128)(2,1)S(1)} %bitcast.101), channel_id=1, source_target_pairs={{0,8},{1,9},{2,10},{3,11},{4,12},{5,13},{6,14},{7,15},{8,0},{9,1},... | collective-permute-start | bytes 4128776 | tf_op jit(solution)/shard_map/ppermute | solution.py:66
  86.7 2.0 collective-permute-start.12
  97.0 4.1 %copy-start = (bf16[4,2,2,4,2,48,896]{6,5,4,3,2,1,0:T(8,128)(2,1)}, bf16[4,2,2,4,2,48,896]{6,5,4,3,2,1,0:T(8,128)(2,1)S(1)}, u32[]{:S(2)}) copy-start(bf16[4,2,2,4,2,48,896]{6,5,4,3,2,1,0:T(8,128)(2,1)S(1)} %get-tuple-element.56.refs_2_) | copy-start | bytes 33030148
  101.2 2.9 %copy-start.11 = (bf16[768,896]{1,0:T(8,128)(2,1)}, bf16[768,896]{1,0:T(8,128)(2,1)S(1)}, u32[]{:S(2)}) copy-start(bf16[768,896]{1,0:T(8,128)(2,1)S(1)} %get-tuple-element.54.refs_0_.refs_1_) | copy-start | bytes 4128772
  101.2 3.8 %copy-start.2 = (bf16[1,96,128,128]{3,2,1,0:T(8,128)(2,1)S(1)}, bf16[1,96,128,128]{3,2,1,0:T(8,128)(2,1)}, u32[]{:S(2)}) copy-start(bf16[1,96,128,128]{3,2,1,0:T(8,128)(2,1)} %param.6) | copy-start | bytes 9437188
  101.2 3.8 %copy-start.13 = (bf16[768,896]{1,0:T(8,128)(2,1)}, bf16[768,896]{1,0:T(8,128)(2,1)S(1)}, u32[]{:S(2)}) copy-start(bf16[768,896]{1,0:T(8,128)(2,1)S(1)} %collective-permute-done.21.refs_2_) | copy-start | bytes 4128772
  105.0 17.9 %collective-permute-start.25 = (bf16[416,896]{1,0:T(8,128)(2,1)}, bf16[416,896]{1,0:T(8,128)(2,1)}, u32[]{:S(2)}, u32[]{:S(2)}) collective-permute-start(bf16[416,896]{1,0:T(8,128)(2,1)} %get-tuple-element.62), channel_id=1, source_target_pairs={{0,1},{1,0},{2,3},{3,2},{4,5},{5,4},{6,7},{7,6},{8,9},{9,8},{10,11... | collective-permute-start | bytes 2236424 | tf_op jit(solution)/shard_map/ppermute | solution.py:66
  105.0 4.1 %copy-start.1 = (bf16[4,2,2,4,2,48,896]{6,5,4,3,2,1,0:T(8,128)(2,1)S(1)}, bf16[4,2,2,4,2,48,896]{6,5,4,3,2,1,0:T(8,128)(2,1)}, u32[]{:S(2)}) copy-start(bf16[4,2,2,4,2,48,896]{6,5,4,3,2,1,0:T(8,128)(2,1)} %copy-done) | copy-start | bytes 33030148
  109.1 8.8 %copy-start.4 = (bf16[2,4,2,48,896]{4,3,2,1,0:T(8,128)(2,1)S(1)}, bf16[2,4,2,48,896]{4,3,2,1,0:T(8,128)(2,1)}, u32[]{:S(2)}) copy-start(bf16[2,4,2,48,896]{4,3,2,1,0:T(8,128)(2,1)} %copy-done.3) | copy-start | bytes 4128772
  109.1 8.8 %copy-start.14 = (bf16[768,896]{1,0:T(8,128)(2,1)S(1)}, bf16[768,896]{1,0:T(8,128)(2,1)}, u32[]{:S(2)}) copy-start(bf16[768,896]{1,0:T(8,128)(2,1)} %copy-done.13) | copy-start | bytes 4128772
  118.0 7.1 %copy-start.5 = (bf16[768,896]{1,0:T(8,128)(2,1)}, bf16[768,896]{1,0:T(8,128)(2,1)S(1)}, u32[]{:S(2)}) copy-start(bf16[768,896]{1,0:T(8,128)(2,1)S(1)} %multiply.3.refs_0_) | copy-start | bytes 4128772
  118.0 4.9 %copy-start.8 = (bf16[416,896]{1,0:T(8,128)(2,1)S(1)}, bf16[416,896]{1,0:T(8,128)(2,1)}, u32[]{:S(2)}) copy-start(bf16[416,896]{1,0:T(8,128)(2,1)} %copy-done.7) | copy-start | bytes 2236420
  119.8 8.5 %collective-permute-start.22 = (bf16[208,896]{1,0:T(8,128)(2,1)S(1)}, bf16[208,896]{1,0:T(8,128)(2,1)S(1)}, u32[]{:S(2)}, u32[]{:S(2)}) collective-permute-start(bf16[208,896]{1,0:T(8,128)(2,1)S(1)} %get-tuple-element.58), channel_id=1, source_target_pairs={{0,2},{1,3},{2,4},{3,5},{4,6},{5,7},{6,0},{7,1},{8,14},{9,15},{10,... | collective-permute-start | bytes 1118216 | tf_op jit(solution)/shard_map/ppermute | solution.py:66
  120.3 12.0 %collective-permute-start.23 = (bf16[208,896]{1,0:T(8,128)(2,1)S(1)}, bf16[208,896]{1,0:T(8,128)(2,1)S(1)}, u32[]{:S(2)}, u32[]{:S(2)}) collective-permute-start(bf16[208,896]{1,0:T(8,128)(2,1)S(1)} %get-tuple-element.59), channel_id=1, source_target_pairs={{0,6},{1,7},{2,0},{3,1},{4,2},{5,3},{6,4},{7,5},{8,10},{9,11},{10,... | collective-permute-start | bytes 1118216 | tf_op jit(solution)/shard_map/ppermute | solution.py:66
  121.3 18.3 %collective-permute-start.24 = (bf16[208,896]{1,0:T(8,128)(2,1)S(1)}, bf16[208,896]{1,0:T(8,128)(2,1)S(1)}, u32[]{:S(2)}, u32[]{:S(2)}) collective-permute-start(bf16[208,896]{1,0:T(8,128)(2,1)S(1)} %get-tuple-element.60), channel_id=1, source_target_pairs={{0,4},{1,5},{2,6},{3,7},{4,0},{5,1},{6,2},{7,3},{8,12},{9,13},{10,... | collective-permute-start | bytes 1118216 | tf_op jit(solution)/shard_map/ppermute | solution.py:66
  125.1 15.3 %collective-permute-start.26 = (bf16[104,896]{1,0:T(8,128)(2,1)S(1)}, bf16[104,896]{1,0:T(8,128)(2,1)}, u32[]{:S(2)}, u32[]{:S(2)}) collective-permute-start(bf16[104,896]{1,0:T(8,128)(2,1)S(1)} %get-tuple-element.84), channel_id=1, source_target_pairs={{0,2},{1,3},{2,4},{3,5},{4,6},{5,7},{6,0},{7,1},{8,14},{9,15},{10,... | collective-permute-start | bytes 559112 | tf_op jit(solution)/shard_map/ppermute | solution.py:66
  125.9 19.4 %collective-permute-start.28 = (bf16[104,896]{1,0:T(8,128)(2,1)}, bf16[104,896]{1,0:T(8,128)(2,1)}, u32[]{:S(2)}, u32[]{:S(2)}) collective-permute-start(bf16[104,896]{1,0:T(8,128)(2,1)} %get-tuple-element.85), channel_id=1, source_target_pairs={{0,4},{1,5},{2,6},{3,7},{4,0},{5,1},{6,2},{7,3},{8,12},{9,13},{10,... | collective-permute-start | bytes 559112 | tf_op jit(solution)/shard_map/ppermute | solution.py:66
  128.3 19.1 %collective-permute-start.27 = (bf16[104,896]{1,0:T(8,128)(2,1)}, bf16[104,896]{1,0:T(8,128)(2,1)}, u32[]{:S(2)}, u32[]{:S(2)}) collective-permute-start(bf16[104,896]{1,0:T(8,128)(2,1)} %get-tuple-element.86), channel_id=1, source_target_pairs={{0,6},{1,7},{2,0},{3,1},{4,2},{5,3},{6,4},{7,5},{8,10},{9,11},{10,... | collective-permute-start | bytes 559112 | tf_op jit(solution)/shard_map/ppermute | solution.py:66
  140.3 50.3 %copy-start.6 = (bf16[768,896]{1,0:T(8,128)(2,1)S(1)}, bf16[768,896]{1,0:T(8,128)(2,1)}, u32[]{:S(2)}) copy-start(bf16[768,896]{1,0:T(8,128)(2,1)} %copy-done.5) | copy-start | bytes 4128772
  140.6 7.7 %collective-permute-start.33 = (bf16[104,896]{1,0:T(8,128)(2,1)S(1)}, bf16[104,896]{1,0:T(8,128)(2,1)S(1)}, u32[]{:S(2)}, u32[]{:S(2)}) collective-permute-start(bf16[104,896]{1,0:T(8,128)(2,1)S(1)} %constant_dynamic-slice_fusion), channel_id=1, source_target_pairs={{0,1},{1,0},{2,3},{3,2},{4,5},{5,4},{6,7},{7,6},{8,9},{9,8},{10,11... | collective-permute-start | bytes 559112 | tf_op jit(solution)/shard_map/ppermute | solution.py:66
  149.6 7.0 %collective-permute-start.34 = (bf16[104,896]{1,0:T(8,128)(2,1)S(1)}, bf16[104,896]{1,0:T(8,128)(2,1)S(1)}, u32[]{:S(2)}, u32[]{:S(2)}) collective-permute-start(bf16[104,896]{1,0:T(8,128)(2,1)S(1)} %get-tuple-element.98), channel_id=1, source_target_pairs={{0,8},{1,9},{2,10},{3,11},{4,12},{5,13},{6,14},{7,15},{8,0},{9,1},... | collective-permute-start | bytes 559112 | tf_op jit(solution)/shard_map/ppermute | solution.py:66
  155.6 1.4 collective-permute-start.29
  157.2 6.0 %collective-permute-start.30 = (bf16[104,896]{1,0:T(8,128)(2,1)S(1)}, bf16[104,896]{1,0:T(8,128)(2,1)S(1)}, u32[]{:S(2)}, u32[]{:S(2)}) collective-permute-start(bf16[104,896]{1,0:T(8,128)(2,1)S(1)} %get-tuple-element.97), channel_id=1, source_target_pairs={{0,2},{1,3},{2,4},{3,5},{4,6},{5,7},{6,0},{7,1},{8,14},{9,15},{10,... | collective-permute-start | bytes 559112 | tf_op jit(solution)/shard_map/ppermute | solution.py:66
  157.3 11.4 %collective-permute-start.31 = (bf16[104,896]{1,0:T(8,128)(2,1)S(1)}, bf16[104,896]{1,0:T(8,128)(2,1)S(1)}, u32[]{:S(2)}, u32[]{:S(2)}) collective-permute-start(bf16[104,896]{1,0:T(8,128)(2,1)S(1)} %get-tuple-element.97), channel_id=1, source_target_pairs={{0,6},{1,7},{2,0},{3,1},{4,2},{5,3},{6,4},{7,5},{8,10},{9,11},{10,... | collective-permute-start | bytes 559112 | tf_op jit(solution)/shard_map/ppermute | solution.py:66
  158.8 10.0 %collective-permute-start.32 = (bf16[104,896]{1,0:T(8,128)(2,1)S(1)}, bf16[104,896]{1,0:T(8,128)(2,1)S(1)}, u32[]{:S(2)}, u32[]{:S(2)}) collective-permute-start(bf16[104,896]{1,0:T(8,128)(2,1)S(1)} %get-tuple-element.97), channel_id=1, source_target_pairs={{0,4},{1,5},{2,6},{3,7},{4,0},{5,1},{6,2},{7,3},{8,12},{9,13},{10,... | collective-permute-start | bytes 559112 | tf_op jit(solution)/shard_map/ppermute | solution.py:66
  159.3 9.5 %collective-permute-start.35 = (bf16[104,896]{1,0:T(8,128)(2,1)S(1)}, bf16[104,896]{1,0:T(8,128)(2,1)S(1)}, u32[]{:S(2)}, u32[]{:S(2)}) collective-permute-start(bf16[104,896]{1,0:T(8,128)(2,1)S(1)} %get-tuple-element.76), channel_id=1, source_target_pairs={{0,1},{1,0},{2,3},{3,2},{4,5},{5,4},{6,7},{7,6},{8,9},{9,8},{10,11... | collective-permute-start | bytes 559112 | tf_op jit(solution)/shard_map/ppermute | solution.py:66
  168.8 21.8 %collective-permute-start.36 = (bf16[416,896]{1,0:T(8,128)(2,1)S(1)}, bf16[416,896]{1,0:T(8,128)(2,1)S(1)}, u32[]{:S(2)}, u32[]{:S(2)}) collective-permute-start(bf16[416,896]{1,0:T(8,128)(2,1)S(1)} %constant_dynamic-update-slice_fusion.6.refs_2_), channel_id=1, source_target_pairs={{0,1},{1,0},{2,3},{3,2},{4,5},{5,4},{6,7},{7,6},{8,9},{9,8},{10,11... | collective-permute-start | bytes 2236424 | tf_op jit(solution)/shard_map/ppermute | solution.py:66
  170.7 8.9 %collective-permute-start.37 = (bf16[208,896]{1,0:T(8,128)(2,1)S(1)}, bf16[208,896]{1,0:T(8,128)(2,1)S(1)}, u32[]{:S(2)}, u32[]{:S(2)}) collective-permute-start(bf16[208,896]{1,0:T(8,128)(2,1)S(1)} %constant_dynamic-update-slice_fusion.4.refs_4_), channel_id=1, source_target_pairs={{0,2},{1,3},{2,4},{3,5},{4,6},{5,7},{6,0},{7,1},{8,14},{9,15},{10,... | collective-permute-start | bytes 1118216 | tf_op jit(solution)/shard_map/ppermute | solution.py:66
  171.6 19.0 %collective-permute-start.38 = (bf16[208,896]{1,0:T(8,128)(2,1)S(1)}, bf16[208,896]{1,0:T(8,128)(2,1)S(1)}, u32[]{:S(2)}, u32[]{:S(2)}) collective-permute-start(bf16[208,896]{1,0:T(8,128)(2,1)S(1)} %constant_dynamic-update-slice_fusion.4.refs_4_), channel_id=1, source_target_pairs={{0,6},{1,7},{2,0},{3,1},{4,2},{5,3},{6,4},{7,5},{8,10},{9,11},{10,... | collective-permute-start | bytes 1118216 | tf_op jit(solution)/shard_map/ppermute | solution.py:66
  172.1 18.5 %collective-permute-start.39 = (bf16[208,896]{1,0:T(8,128)(2,1)S(1)}, bf16[208,896]{1,0:T(8,128)(2,1)S(1)}, u32[]{:S(2)}, u32[]{:S(2)}) collective-permute-start(bf16[208,896]{1,0:T(8,128)(2,1)S(1)} %constant_dynamic-update-slice_fusion.4.refs_4_), channel_id=1, source_target_pairs={{0,4},{1,5},{2,6},{3,7},{4,0},{5,1},{6,2},{7,3},{8,12},{9,13},{10,... | collective-permute-start | bytes 1118216 | tf_op jit(solution)/shard_map/ppermute | solution.py:66
  190.6 1.0 copy-start.10
  191.6 1.3 copy-start.12
  199.3 4.3 %collective-permute-start.40 = (f32[416,768]{1,0:T(8,128)}, f32[416,768]{1,0:T(8,128)}, u32[]{:S(2)}, u32[]{:S(2)}) collective-permute-start(f32[416,768]{1,0:T(8,128)} %get-tuple-element.72), channel_id=1, source_target_pairs={{0,8},{1,9},{2,10},{3,11},{4,12},{5,13},{6,14},{7,15},{8,0},{9,1},... | collective-permute-start | bytes 3833864 | tf_op jit(solution)/shard_map/ppermute | solution.py:66
  205.2 7.0 %collective-permute-start.43 = (bf16[104,768]{1,0:T(8,128)(2,1)S(1)}, bf16[104,768]{1,0:T(8,128)(2,1)S(1)}, u32[]{:S(2)}, u32[]{:S(2)}) collective-permute-start(bf16[104,768]{1,0:T(8,128)(2,1)S(1)} %get-tuple-element.82), channel_id=1, source_target_pairs={{0,64},{1,65},{2,66},{3,67},{4,68},{5,69},{6,70},{7,71},{8,72},{9,... | collective-permute-start | bytes 479240 | tf_op jit(solution)/shard_map/ppermute | solution.py:66
  205.2 10.1 %collective-permute-start.42 = (bf16[104,768]{1,0:T(8,128)(2,1)S(1)}, bf16[104,768]{1,0:T(8,128)(2,1)S(1)}, u32[]{:S(2)}, u32[]{:S(2)}) collective-permute-start(bf16[104,768]{1,0:T(8,128)(2,1)S(1)} %get-tuple-element.83), channel_id=1, source_target_pairs={{0,96},{1,97},{2,98},{3,99},{4,100},{5,101},{6,102},{7,103},{8,40}... | collective-permute-start | bytes 479240 | tf_op jit(solution)/shard_map/ppermute | solution.py:66
  206.0 9.3 %collective-permute-start.41 = (bf16[104,768]{1,0:T(8,128)(2,1)S(1)}, bf16[104,768]{1,0:T(8,128)(2,1)S(1)}, u32[]{:S(2)}, u32[]{:S(2)}) collective-permute-start(bf16[104,768]{1,0:T(8,128)(2,1)S(1)} %get-tuple-element.81), channel_id=1, source_target_pairs={{0,32},{1,33},{2,34},{3,35},{4,36},{5,37},{6,38},{7,39},{8,104},{9... | collective-permute-start | bytes 479240 | tf_op jit(solution)/shard_map/ppermute | solution.py:66
  215.4 9.4 %collective-permute-start.44 = (f32[104,768]{1,0:T(8,128)S(1)}, f32[104,768]{1,0:T(8,128)S(1)}, u32[]{:S(2)}, u32[]{:S(2)}) collective-permute-start(f32[104,768]{1,0:T(8,128)S(1)} %add_add_fusion), channel_id=1, source_target_pairs={{0,16},{1,17},{2,18},{3,19},{4,20},{5,21},{6,22},{7,23},{8,24},{9,... | collective-permute-start | bytes 958472 | tf_op jit(solution)/shard_map/ppermute | solution.py:66
  224.9 6.5 %collective-permute-start.45 = (bf16[104,768]{1,0:T(8,128)(2,1)S(1)}, bf16[104,768]{1,0:T(8,128)(2,1)S(1)}, u32[]{:S(2)}, u32[]{:S(2)}) collective-permute-start(bf16[104,768]{1,0:T(8,128)(2,1)S(1)} %get-tuple-element.74), channel_id=1, source_target_pairs={{0,32},{1,33},{2,34},{3,35},{4,36},{5,37},{6,38},{7,39},{8,104},{9... | collective-permute-start | bytes 479240 | tf_op jit(solution)/shard_map/ppermute | solution.py:66
  229.2 6.6 %collective-permute-start.46 = (bf16[104,768]{1,0:T(8,128)(2,1)S(1)}, bf16[104,768]{1,0:T(8,128)(2,1)S(1)}, u32[]{:S(2)}, u32[]{:S(2)}) collective-permute-start(bf16[104,768]{1,0:T(8,128)(2,1)S(1)} %get-tuple-element.74), channel_id=1, source_target_pairs={{0,96},{1,97},{2,98},{3,99},{4,100},{5,101},{6,102},{7,103},{8,40}... | collective-permute-start | bytes 479240 | tf_op jit(solution)/shard_map/ppermute | solution.py:66
  229.2 8.0 %collective-permute-start.47 = (bf16[104,768]{1,0:T(8,128)(2,1)S(1)}, bf16[104,768]{1,0:T(8,128)(2,1)S(1)}, u32[]{:S(2)}, u32[]{:S(2)}) collective-permute-start(bf16[104,768]{1,0:T(8,128)(2,1)S(1)} %get-tuple-element.74), channel_id=1, source_target_pairs={{0,64},{1,65},{2,66},{3,67},{4,68},{5,69},{6,70},{7,71},{8,72},{9,... | collective-permute-start | bytes 479240 | tf_op jit(solution)/shard_map/ppermute | solution.py:66
  237.2 3.5 %collective-permute-start.48 = (bf16[416,768]{1,0:T(8,128)(2,1)S(1)}, bf16[416,768]{1,0:T(8,128)(2,1)S(1)}, u32[]{:S(2)}, u32[]{:S(2)}) collective-permute-start(bf16[416,768]{1,0:T(8,128)(2,1)S(1)} %constant_dynamic-update-slice_fusion), channel_id=1, source_target_pairs={{0,8},{1,9},{2,10},{3,11},{4,12},{5,13},{6,14},{7,15},{8,0},{9,1},... | collective-permute-start | bytes 1916936 | tf_op jit(solution)/shard_map/ppermute | solution.py:66
  (2 other events, 1.6 us)

commit v5 on v3

--- a/solution.py
+++ b/solution.py
@@ -293,9 +293,9 @@
 
 
 def exchange_kernel(*refs):
-    halves, parts, (keep, give, weights, turned, sems) = refs[:2], refs[2:8], refs[8:]
+    halves, parts, (keep, give, held, weights, turned, sems) = refs[:2], refs[2:8], refs[8:]
     core, _, _, _ = here()
-    copies = []
+    copies = [pltpu.make_async_copy(halves[q], held.at[q], sems.at[6 + q]) for q in range(2)]
     for i, (q, at) in enumerate([(0, at) for at in chunks_low()] + [(1, at) for at in chunks_arrived()]):
         n = parts[i].shape[0]
         into = weights.at[q, pl.ds(pl.multiple_of(at * n, n), n), :]
@@ -313,7 +313,7 @@
         codes = codes + jnp.where(line == 1, weights[1 - q, NOCC : NOCC + 16, :].astype(f32), 0.0)
         coulomb = jnp.sum(codes, keepdims=True) * (1.0 / NB)
         factor = jnp.where(core == 0, 2.0 * coulomb, 0.0)
-        own = halves[q][...]
+        own = held[q]
         term = factor * own.astype(f32) - jnp.dot(own, weights[q], preferred_element_type=f32)
         total = term if total is None else total + term
     turned[...] = total.T
@@ -331,14 +331,15 @@
     return pl.pallas_call(
         exchange_kernel,
         out_shape=[jax.ShapeDtypeStruct((CROSS // 2, ROWS), f32)] * 2,
-        in_specs=[pl.BlockSpec(memory_space=pltpu.VMEM)] * 2 + [pl.BlockSpec(memory_space=pl.ANY)] * 6,
+        in_specs=[pl.BlockSpec(memory_space=pl.ANY)] * 8,
         out_specs=[pl.BlockSpec(memory_space=pltpu.VMEM)] * 2,
         scratch_shapes=[
+            pltpu.VMEM((2, ROWS, WIDE), bf16),
             pltpu.VMEM((2, WIDE, WIDE), bf16),
             pltpu.VMEM((WIDE, ROWS), f32),
-            pltpu.SemaphoreType.DMA((6,)),
+            pltpu.SemaphoreType.DMA((8,)),
         ],
-        compiler_params=pltpu.CompilerParams(vmem_limit_bytes=36 * 1024 * 1024),
+        compiler_params=pltpu.CompilerParams(vmem_limit_bytes=48 * 1024 * 1024),
         cost_estimate=pl.CostEstimate(flops=4 * 768 * 896 * 896, bytes_accessed=2**23, transcendentals=0),
         name="exchange",
     )(*halves, *low_parts, *x_parts)
@@ -377,13 +378,10 @@
     ahead = send(both, around(one, 1, False))
     behind = send(both, around(one, -1, False))
     far = send(both, around(one, 2, False))
-    lists = jnp.concatenate([block_rows[0] % ROW_BLOCKS, block_cols[0], block_count[0]])
-    lists = jnp.pad(lists, (0, 256 - 2 * SLOTS - 1))[None]
-    meta = jnp.concatenate([lists, swap_cores(lists)])
     stage = put(stage, ahead[:, None], d1=(at_one - 1) % 4)
     stage = put(stage, behind[:, None], d1=(at_one + 1) % 4)
     stage = put(stage, far[:, None], d1=(at_one + 2) % 4)
-    stage, other_blocks, meta = lax.optimization_barrier((stage, other_blocks, meta))
+    stage, other_blocks = lax.optimization_barrier((stage, other_blocks))
 
     main, rest = stage[:, :, :MAIN], stage[:, :, MAIN:]
     zz = ("z", "z")
@@ -391,8 +389,13 @@
     rest_ahead = send(rest, around(two, 1, False))
     rest_behind = send(rest, around(two, -1, False))
     main_far = send(main_ahead, around(zz, 1, True))
-    main_behind = send_after(main, around(zz, -1, True), main_ahead)
-    rest_far = send_after(rest, around(two, 2, False), rest_ahead)
+    main_behind = send(main, around(zz, -1, True))
+    rest_far = send_after(rest, around(two, 2, False), rest_ahead, main_ahead)
+
+    lists = lax.optimization_barrier((block_rows[0], block_cols[0], block_count[0], rest_ahead))
+    lists = jnp.concatenate([lists[0] % ROW_BLOCKS, lists[1], lists[2]])
+    lists = jnp.pad(lists, (0, 256 - 2 * SLOTS - 1))[None]
+    meta = jnp.concatenate([lists, swap_cores(lists)])
 
     mains = [jnp.zeros((ZH, ZL, 4, MAIN, WIDE), bf16)] * 2
     for array, at in (
@@ -413,7 +416,7 @@
     rest = into
 
     ahead, behind = around(two, 1, False), around(two, -1, False)
-    mains, rest = lax.optimization_barrier((mains, rest))
+    mains, rest, meta = lax.optimization_barrier((mains, rest, meta))
     ahead_0 = send(mains[0], ahead)
     behind_1 = send(mains[1], behind)
     rest_ahead = send(rest, around(zz, 1, True))

time: 237 us -> 232 us (0.979)
  other arithmetic: 10.8 us -> 8.33 us
  transfers between devices with their start and end apart: 49 -> 49, of which waited for: 30 -> 33; matrix products, arithmetic and copies ran while one was open for 3% -> 3% of each run, Pallas kernels for 8% -> 9%
where the time goes in v5:
time: 232 us
  waiting for transfers between devices  123 us (53%)
  starting transfers between devices  63.7 us (27%)
  Pallas kernels  29.6 us (13%)
  other arithmetic  8.33 us (4%)
  local copies, waits for them, and re-layouts  6.18 us (3%)
    ppermute x49, waiting for transfers between devices, send(): return lax.ppermute(array, AXES, pairs)  123 us
    ppermute x49, starting transfers between devices, send(): return lax.ppermute(array, AXES, pairs)  63.7 us
    pallas_call x2, Pallas kernels, multiply(): pl.pallas_call(kernel, out_shape=[half, held] if q == 1 else half, in_spe...  17.1 us
    pallas_call x1, Pallas kernels, exchange(): pl.pallas_call(exchange_kernel, out_shape=[jax.ShapeDtypeStruct((CROSS //...  6.86 us
    pallas_call x2, Pallas kernels, cross(): pl.pallas_call(kernel, out_shape=[jax.ShapeDtypeStruct((CROSS // many, WI...  4.74 us
  transfers between devices with their start and end apart: 49, of which 33 were waited for; matrix products, arithmetic and copies ran while one was open for 3% of the time, Pallas kernels for 9%

profile of v5, /device:TPU:1, one launch (start us, length us, event | category | flops | bytes accessed | tf_op | source)
XLA Modules:
  0.0 231.9 jit_solution(13819216088057185461)
XLA Ops:
  0.9 1.5 collective-permute-start
  4.6 1.4 collective-permute-start.1
  6.8 1.9 collective-permute-start.2
  8.7 1.3 collective-permute-start.3
  11.7 1.2 collective-permute-done.2
  12.9 1.8 collective-permute-done.3
  14.9 3.8 %collective-permute-start.5 = (bf16[2,4,32,896]{3,2,1,0:T(8,128)(2,1)S(1)}, bf16[2,4,32,896]{3,2,1,0:T(8,128)(2,1)S(1)}, u32[]{:S(2)}, u32[]{:S(2)}) collective-permute-start(bf16[2,4,32,896]{3,2,1,0:T(8,128)(2,1)S(1)} %slice.42), channel_id=1, source_target_pairs={{0,1},{1,16},{2,3},{3,18},{4,5},{5,20},{6,7},{7,22},{8,25},{9,8},{... | collective-permute-start | bytes 1376264 | tf_op jit(solution)/shard_map/ppermute | solution.py:66
  19.6 1.8 collective-permute-start.9
  21.7 3.3 %collective-permute-done.8 = bf16[2,4,16,896]{3,2,1,0:T(8,128)(2,1)S(1)} collective-permute-done((bf16[2,4,16,896]{3,2,1,0:T(8,128)(2,1)S(1)}, bf16[2,4,16,896]{3,2,1,0:T(8,128)(2,1)S(1)}, u32[]{:S(2)}, u32[]{:S(2)}) %collective-permute-start.8) | collective-permute-done | bytes 229408 | tf_op jit(solution)/shard_map/ppermute | solution.py:66
  25.2 2.4 %collective-permute-start.11 = (s32[1,256]{1,0:T(1,128)S(1)}, s32[1,256]{1,0:T(1,128)S(1)}, u32[]{:S(2)}, u32[]{:S(2)}) collective-permute-start(s32[1,256]{1,0:T(1,128)S(1)} %bitcast.104), channel_id=1, source_target_pairs={{0,8},{1,9},{2,10},{3,11},{4,12},{5,13},{6,14},{7,15},{8,0},{9,1},... | collective-permute-start | bytes 3080 | tf_op jit(solution)/shard_map/ppermute | solution.py:66
  28.4 2.3 collective-permute-start.10
  30.7 3.4 %collective-permute-start.7 = (bf16[2,4,32,896]{3,2,1,0:T(8,128)(2,1)S(1)}, bf16[2,4,32,896]{3,2,1,0:T(8,128)(2,1)S(1)}, u32[]{:S(2)}, u32[]{:S(2)}) collective-permute-start(bf16[2,4,32,896]{3,2,1,0:T(8,128)(2,1)S(1)} %collective-permute-done.5), channel_id=1, source_target_pairs={{0,1},{1,16},{2,3},{3,18},{4,5},{5,20},{6,7},{7,22},{8,25},{9,8},{... | collective-permute-start | bytes 1376264 | tf_op jit(solution)/shard_map/ppermute | solution.py:66
  34.9 4.7 %collective-permute-done.7 = bf16[2,4,32,896]{3,2,1,0:T(8,128)(2,1)S(1)} collective-permute-done((bf16[2,4,32,896]{3,2,1,0:T(8,128)(2,1)S(1)}, bf16[2,4,32,896]{3,2,1,0:T(8,128)(2,1)S(1)}, u32[]{:S(2)}, u32[]{:S(2)}) %collective-permute-start.7) | collective-permute-done | bytes 458784 | tf_op jit(solution)/shard_map/ppermute | solution.py:66
  40.0 2.4 %collective-permute-start.13 = (bf16[2,2,4,32,896]{4,3,2,1,0:T(8,128)(2,1)S(1)}, bf16[2,2,4,32,896]{4,3,2,1,0:T(8,128)(2,1)S(1)}, u32[]{:S(2)}, u32[]{:S(2)}) collective-permute-start(bf16[2,2,4,32,896]{4,3,2,1,0:T(8,128)(2,1)S(1)} %get-tuple-element.49), channel_id=1, source_target_pairs={{0,96},{1,97},{2,98},{3,99},{4,100},{5,101},{6,102},{7,103},{8,14}... | collective-permute-start | bytes 2752520 | tf_op jit(solution)/shard_map/ppermute | solution.py:66
  42.3 3.1 %collective-permute-start.17 = (bf16[2,4,4,16,896]{4,3,2,1,0:T(8,128)(2,1)S(1)}, bf16[2,4,4,16,896]{4,3,2,1,0:T(8,128)(2,1)S(1)}, u32[]{:S(2)}, u32[]{:S(2)}) collective-permute-start(bf16[2,4,4,16,896]{4,3,2,1,0:T(8,128)(2,1)S(1)} %bitcast_dynamic-update-slice_fusion.15), channel_id=1, source_target_pairs={{0,1},{1,16},{2,3},{3,18},{4,5},{5,20},{6,7},{7,22},{8,25},{9,8},{... | collective-permute-start | bytes 2752520 | tf_op jit(solution)/shard_map/ppermute | solution.py:66
  46.6 6.8 %collective-permute-done.12 = bf16[2,2,4,32,896]{4,3,2,1,0:T(8,128)(2,1)S(1)} collective-permute-done((bf16[2,2,4,32,896]{4,3,2,1,0:T(8,128)(2,1)S(1)}, bf16[2,2,4,32,896]{4,3,2,1,0:T(8,128)(2,1)S(1)}, u32[]{:S(2)}, u32[]{:S(2)}) %collective-permute-start.12) | collective-permute-done | bytes 917536 | tf_op jit(solution)/shard_map/ppermute | solution.py:66
  54.1 2.7 %collective-permute-start.14 = (bf16[2,2,4,32,896]{4,3,2,1,0:T(8,128)(2,1)S(1)}, bf16[2,2,4,32,896]{4,3,2,1,0:T(8,128)(2,1)S(1)}, u32[]{:S(2)}, u32[]{:S(2)}) collective-permute-start(bf16[2,2,4,32,896]{4,3,2,1,0:T(8,128)(2,1)S(1)} %get-tuple-element.48), channel_id=1, source_target_pairs={{0,96},{1,97},{2,98},{3,99},{4,100},{5,101},{6,102},{7,103},{8,14}... | collective-permute-start | bytes 2752520 | tf_op jit(solution)/shard_map/ppermute | solution.py:66
  56.8 3.7 %collective-permute-done.17 = bf16[2,4,4,16,896]{4,3,2,1,0:T(8,128)(2,1)S(1)} collective-permute-done((bf16[2,4,4,16,896]{4,3,2,1,0:T(8,128)(2,1)S(1)}, bf16[2,4,4,16,896]{4,3,2,1,0:T(8,128)(2,1)S(1)}, u32[]{:S(2)}, u32[]{:S(2)}) %collective-permute-start.17) | collective-permute-done | bytes 917536 | tf_op jit(solution)/shard_map/ppermute | solution.py:66
  60.5 6.4 %collective-permute-done.19 = bf16[2,4,4,16,896]{4,3,2,1,0:T(8,128)(2,1)S(1)} collective-permute-done((bf16[2,4,4,16,896]{4,3,2,1,0:T(8,128)(2,1)S(1)}, bf16[2,4,4,16,896]{4,3,2,1,0:T(8,128)(2,1)S(1)}, u32[]{:S(2)}, u32[]{:S(2)}) %collective-permute-start.19) | collective-permute-done | bytes 917536 | tf_op jit(solution)/shard_map/ppermute | solution.py:66
  67.7 12.8 %collective-permute-done.15 = bf16[2,2,4,32,896]{4,3,2,1,0:T(8,128)(2,1)S(1)} collective-permute-done((bf16[2,2,4,32,896]{4,3,2,1,0:T(8,128)(2,1)S(1)}, bf16[2,2,4,32,896]{4,3,2,1,0:T(8,128)(2,1)S(1)}, u32[]{:S(2)}, u32[]{:S(2)}) %collective-permute-start.15) | collective-permute-done | bytes 917536 | tf_op jit(solution)/shard_map/ppermute | solution.py:66
  82.0 4.6 %collective-permute-start.21 = (bf16[768,896]{1,0:T(8,128)(2,1)S(1)}, bf16[768,896]{1,0:T(8,128)(2,1)S(1)}, u32[]{:S(2)}, u32[]{:S(2)}) collective-permute-start(bf16[768,896]{1,0:T(8,128)(2,1)S(1)} %bitcast.101), channel_id=1, source_target_pairs={{0,8},{1,9},{2,10},{3,11},{4,12},{5,13},{6,14},{7,15},{8,0},{9,1},... | collective-permute-start | bytes 4128776 | tf_op jit(solution)/shard_map/ppermute | solution.py:66
  86.6 10.9 %multiply.2 = (bf16[768,896]{1,0:T(8,128)(2,1)S(1)}, bf16[4,2,2,4,2,48,896]{6,5,4,3,2,1,0:T(8,128)(2,1)S(1)}) custom-call(s32[2,256]{1,0:T(2,128)S(1)} %pad_add_fusion.refs_0_, bf16[96,128,128]{2,1,0:T(8,128)(2,1)S(1)} %collective-permute-done.4.refs_1_, bf16[4,2,2,4,32,896]{5,4,3,2,1,0:T(8,128)(2,1)S(1)} %bitcast_dynamic-update-slice_fusion.8.refs_2_.main0, ...), custom_call_target="tpu_custom_call" | custom-call | flops 2818572288 | bytes 8388608 | tf_op jit(solution)/shard_map/multiply/pallas_call | solution.py:228
  97.5 2.0 cross.2
  100.3 6.2 %multiply.3.refs_0_ = bf16[768,896]{1,0:T(8,128)(2,1)S(1)} custom-call(s32[2,256]{1,0:T(2,128)S(1)} %pad_add_fusion.refs_0_, bf16[96,128,128]{2,1,0:T(8,128)(2,1)S(1)} %bitcast.100, bf16[4,2,2,4,2,48,896]{6,5,4,3,2,1,0:T(8,128)(2,1)S(1)} %get-tuple-element.56.refs_2_), custom_call_target="tpu_custom_call" | custom-call | flops 2818572288 | bytes 8388608 | tf_op jit(solution)/shard_map/multiply/pallas_call | solution.py:228
  106.6 2.8 %cross.3 = (bf16[208,896]{1,0:T(8,128)(2,1)S(1)}, bf16[208,896]{1,0:T(8,128)(2,1)}, bf16[208,896]{1,0:T(8,128)(2,1)}, bf16[208,896]{1,0:T(8,128)(2,1)}) custom-call(bf16[768,896]{1,0:T(8,128)(2,1)S(1)} %multiply.3.refs_0_, bf16[768,896]{1,0:T(8,128)(2,1)S(1)} %bitcast.103, bf16[768,896]{1,0:T(8,128)(2,1)S(1)} %collective-permute-done.21.refs_2_), custom_call_target="tpu_custom_call" | custom-call | flops 1233125376 | bytes 8388608 | tf_op jit(solution)/shard_map/cross/pallas_call | solution.py:283
  109.3 1.5 collective-permute-start.30
  110.9 1.2 collective-permute-start.32
  112.0 5.2 %collective-permute-done.22 = bf16[416,896]{1,0:T(8,128)(2,1)} collective-permute-done((bf16[416,896]{1,0:T(8,128)(2,1)S(1)}, bf16[416,896]{1,0:T(8,128)(2,1)}, u32[]{:S(2)}, u32[]{:S(2)}) %collective-permute-start.22) | collective-permute-done | bytes 745504 | tf_op jit(solution)/shard_map/ppermute | solution.py:66
  117.3 1.3 add_convert_fusion
  118.6 1.3 collective-permute-done.30
  119.9 1.8 collective-permute-done.31
  121.7 7.5 %collective-permute-done.32 = bf16[208,896]{1,0:T(8,128)(2,1)} collective-permute-done((bf16[208,896]{1,0:T(8,128)(2,1)}, bf16[208,896]{1,0:T(8,128)(2,1)}, u32[]{:S(2)}, u32[]{:S(2)}) %collective-permute-start.32) | collective-permute-done | bytes 372768 | tf_op jit(solution)/shard_map/ppermute | solution.py:66
  129.2 1.4 add_convert_fusion.1
  131.4 1.2 collective-permute-start.24
  132.6 1.5 collective-permute-start.23
  134.1 2.0 collective-permute-done.33
  136.1 1.4 collective-permute-done.25
  137.5 4.9 %collective-permute-done.24 = bf16[104,896]{1,0:T(8,128)(2,1)S(1)} collective-permute-done((bf16[104,896]{1,0:T(8,128)(2,1)S(1)}, bf16[104,896]{1,0:T(8,128)(2,1)S(1)}, u32[]{:S(2)}, u32[]{:S(2)}) %collective-permute-start.24) | collective-permute-done | bytes 186400 | tf_op jit(solution)/shard_map/ppermute | solution.py:66
  142.6 1.3 collective-permute-start.34
  145.6 1.1 collective-permute-start.27
  147.9 1.4 collective-permute-start.35
  149.4 2.2 collective-permute-done.27
  151.6 6.4 %collective-permute-done.28 = bf16[104,896]{1,0:T(8,128)(2,1)S(1)} collective-permute-done((bf16[104,896]{1,0:T(8,128)(2,1)S(1)}, bf16[104,896]{1,0:T(8,128)(2,1)S(1)}, u32[]{:S(2)}, u32[]{:S(2)}) %collective-permute-start.28) | collective-permute-done | bytes 186400 | tf_op jit(solution)/shard_map/ppermute | solution.py:66
  158.1 1.4 collective-permute-start.36
  159.5 1.5 collective-permute-start.38
  161.0 8.1 %collective-permute-done.37.refs_5_ = bf16[208,896]{1,0:T(8,128)(2,1)S(1)} collective-permute-done((bf16[208,896]{1,0:T(8,128)(2,1)S(1)}, bf16[208,896]{1,0:T(8,128)(2,1)S(1)}, u32[]{:S(2)}, u32[]{:S(2)}) %collective-permute-start.37) | collective-permute-done | bytes 372768 | tf_op jit(solution)/shard_map/ppermute | solution.py:66
  169.1 9.2 %collective-permute-done.38.refs_6_ = bf16[208,896]{1,0:T(8,128)(2,1)S(1)} collective-permute-done((bf16[208,896]{1,0:T(8,128)(2,1)S(1)}, bf16[208,896]{1,0:T(8,128)(2,1)S(1)}, u32[]{:S(2)}, u32[]{:S(2)}) %collective-permute-start.38) | collective-permute-done | bytes 372768 | tf_op jit(solution)/shard_map/ppermute | solution.py:66
  178.3 6.9 %exchange.1 = (f32[416,768]{1,0:T(8,128)S(1)}, f32[416,768]{1,0:T(8,128)}) custom-call(bf16[768,896]{1,0:T(8,128)(2,1)} %copy-done.1, bf16[768,896]{1,0:T(8,128)(2,1)} %copy-done.2, bf16[416,896]{1,0:T(8,128)(2,1)S(1)} %constant_dynamic-update-slice_fusion.6.refs_2_, bf16[416,896]{1,0:T(8,128)(2,1)S(1)} %collective-permute-done.36.refs_3_, ...), custom_call_target="tpu_custom_call" | custom-call | flops 2466250752 | bytes 8388608 | tf_op jit(solution)/shard_map/exchange/pallas_call | solution.py:331
  185.1 1.6 collective-permute-start.40
  186.7 2.8 %collective-permute-done.40 = f32[416,768]{1,0:T(8,128)S(1)} collective-permute-done((f32[416,768]{1,0:T(8,128)}, f32[416,768]{1,0:T(8,128)S(1)}, u32[]{:S(2)}, u32[]{:S(2)}) %collective-permute-start.40) | collective-permute-done | bytes 1277984 | tf_op jit(solution)/shard_map/ppermute | solution.py:66
  189.6 1.0 copy-done.3
  190.6 1.5 add.405
  192.5 5.1 %collective-permute-start.42 = (bf16[104,768]{1,0:T(8,128)(2,1)S(1)}, bf16[104,768]{1,0:T(8,128)(2,1)S(1)}, u32[]{:S(2)}, u32[]{:S(2)}) collective-permute-start(bf16[104,768]{1,0:T(8,128)(2,1)S(1)} %get-tuple-element.81), channel_id=1, source_target_pairs={{0,96},{1,97},{2,98},{3,99},{4,100},{5,101},{6,102},{7,103},{8,40}... | collective-permute-start | bytes 479240 | tf_op jit(solution)/shard_map/ppermute | solution.py:66
  197.6 1.5 collective-permute-done.43
  199.0 2.2 collective-permute-done.42
  201.3 3.6 %collective-permute-done.41 = bf16[104,768]{1,0:T(8,128)(2,1)S(1)} collective-permute-done((bf16[104,768]{1,0:T(8,128)(2,1)S(1)}, bf16[104,768]{1,0:T(8,128)(2,1)S(1)}, u32[]{:S(2)}, u32[]{:S(2)}) %collective-permute-start.41) | collective-permute-done | bytes 159776 | tf_op jit(solution)/shard_map/ppermute | solution.py:66
  204.9 1.4 collective-permute-start.44
  206.4 8.0 %collective-permute-done.44 = f32[104,768]{1,0:T(8,128)S(1)} collective-permute-done((f32[104,768]{1,0:T(8,128)S(1)}, f32[104,768]{1,0:T(8,128)S(1)}, u32[]{:S(2)}, u32[]{:S(2)}) %collective-permute-start.44) | collective-permute-done | bytes 319520 | tf_op jit(solution)/shard_map/ppermute | solution.py:66
  214.5 4.0 %collective-permute-start.45 = (bf16[104,768]{1,0:T(8,128)(2,1)S(1)}, bf16[104,768]{1,0:T(8,128)(2,1)S(1)}, u32[]{:S(2)}, u32[]{:S(2)}) collective-permute-start(bf16[104,768]{1,0:T(8,128)(2,1)S(1)} %get-tuple-element.72), channel_id=1, source_target_pairs={{0,32},{1,33},{2,34},{3,35},{4,36},{5,37},{6,38},{7,39},{8,104},{9... | collective-permute-start | bytes 479240 | tf_op jit(solution)/shard_map/ppermute | solution.py:66
  218.5 1.3 collective-permute-start.47
  219.8 1.0 collective-permute-done.45
  220.7 7.2 %collective-permute-done.46 = bf16[104,768]{1,0:T(8,128)(2,1)S(1)} collective-permute-done((bf16[104,768]{1,0:T(8,128)(2,1)S(1)}, bf16[104,768]{1,0:T(8,128)(2,1)S(1)}, u32[]{:S(2)}, u32[]{:S(2)}) %collective-permute-start.46) | collective-permute-done | bytes 159776 | tf_op jit(solution)/shard_map/ppermute | solution.py:66
  228.5 1.7 collective-permute-done.48
  230.2 1.6 convert_bitcast_fusion
  (118 shorter events, 18.3 us)
Async XLA Ops:
  0.9 2.4 %collective-permute-start = (bf16[48,800]{1,0:T(8,128)(2,1)S(1)}, bf16[48,800]{1,0:T(8,128)(2,1)S(1)}, u32[]{:S(2)}, u32[]{:S(2)}) collective-permute-start(bf16[48,800]{1,0:T(8,128)(2,1)S(1)} %broadcast_select_fusion.4), channel_id=1, source_target_pairs={{0,8},{1,9},{2,10},{3,11},{4,12},{5,13},{6,14},{7,15},{8,0},{9,1},... | collective-permute-start | bytes 230408 | tf_op jit(solution)/shard_map/ppermute | solution.py:66
  3.3 11.4 %collective-permute-start.4 = (bf16[96,128,128]{2,1,0:T(8,128)(2,1)}, bf16[96,128,128]{2,1,0:T(8,128)(2,1)S(1)}, u32[]{:S(2)}, u32[]{:S(2)}) collective-permute-start(bf16[96,128,128]{2,1,0:T(8,128)(2,1)} %bitcast.99), channel_id=1, source_target_pairs={{0,8},{1,9},{2,10},{3,11},{4,12},{5,13},{6,14},{7,15},{8,0},{9,1},... | collective-permute-start | bytes 9437192 | tf_op jit(solution)/shard_map/ppermute | solution.py:66
  4.6 6.1 %collective-permute-start.1 = (bf16[2,48,896]{2,1,0:T(8,128)(2,1)S(1)}, bf16[2,48,896]{2,1,0:T(8,128)(2,1)}, u32[]{:S(2)}, u32[]{:S(2)}) collective-permute-start(bf16[2,48,896]{2,1,0:T(8,128)(2,1)S(1)} %fusion.10), channel_id=1, source_target_pairs={{0,2},{1,3},{2,4},{3,5},{4,6},{5,7},{6,0},{7,1},{8,40},{9,41},{10,... | collective-permute-start | bytes 516104 | tf_op jit(solution)/shard_map/ppermute | solution.py:66
  6.8 18.3 %copy-start.5 = (s32[1,96]{1,0:T(1,128)S(1)}, s32[1,96]{1,0:T(1,128)}, u32[]{:S(2)}) copy-start(s32[1,96]{1,0:T(1,128)} %param.7) | copy-start | bytes 1156
  6.8 18.3 %copy-start.4 = (s32[1,96]{1,0:T(1,128)S(1)}, s32[1,96]{1,0:T(1,128)}, u32[]{:S(2)}) copy-start(s32[1,96]{1,0:T(1,128)} %param.8) | copy-start | bytes 1156
  6.8 6.1 %collective-permute-start.2 = (bf16[2,48,896]{2,1,0:T(8,128)(2,1)S(1)}, bf16[2,48,896]{2,1,0:T(8,128)(2,1)S(1)}, u32[]{:S(2)}, u32[]{:S(2)}) collective-permute-start(bf16[2,48,896]{2,1,0:T(8,128)(2,1)S(1)} %fusion.10), channel_id=1, source_target_pairs={{0,6},{1,7},{2,0},{3,1},{4,2},{5,3},{6,4},{7,5},{8,104},{9,105},{1... | collective-permute-start | bytes 516104 | tf_op jit(solution)/shard_map/ppermute | solution.py:66
  8.7 6.1 %collective-permute-start.3 = (bf16[2,48,896]{2,1,0:T(8,128)(2,1)S(1)}, bf16[2,48,896]{2,1,0:T(8,128)(2,1)S(1)}, u32[]{:S(2)}, u32[]{:S(2)}) collective-permute-start(bf16[2,48,896]{2,1,0:T(8,128)(2,1)S(1)} %fusion.10), channel_id=1, source_target_pairs={{0,4},{1,5},{2,6},{3,7},{4,0},{5,1},{6,2},{7,3},{8,72},{9,73},{10,... | collective-permute-start | bytes 516104 | tf_op jit(solution)/shard_map/ppermute | solution.py:66
  14.9 13.5 %collective-permute-start.5 = (bf16[2,4,32,896]{3,2,1,0:T(8,128)(2,1)S(1)}, bf16[2,4,32,896]{3,2,1,0:T(8,128)(2,1)S(1)}, u32[]{:S(2)}, u32[]{:S(2)}) collective-permute-start(bf16[2,4,32,896]{3,2,1,0:T(8,128)(2,1)S(1)} %slice.42), channel_id=1, source_target_pairs={{0,1},{1,16},{2,3},{3,18},{4,5},{5,20},{6,7},{7,22},{8,25},{9,8},{... | collective-permute-start | bytes 1376264 | tf_op jit(solution)/shard_map/ppermute | solution.py:66
  18.7 15.5 %collective-permute-start.6 = (bf16[2,4,32,896]{3,2,1,0:T(8,128)(2,1)S(1)}, bf16[2,4,32,896]{3,2,1,0:T(8,128)(2,1)S(1)}, u32[]{:S(2)}, u32[]{:S(2)}) collective-permute-start(bf16[2,4,32,896]{3,2,1,0:T(8,128)(2,1)S(1)} %slice.42), channel_id=1, source_target_pairs={{0,17},{1,0},{2,19},{3,2},{4,21},{5,4},{6,23},{7,6},{8,9},{9,24},{... | collective-permute-start | bytes 1376264 | tf_op jit(solution)/shard_map/ppermute | solution.py:66
  18.7 6.4 %collective-permute-start.8 = (bf16[2,4,16,896]{3,2,1,0:T(8,128)(2,1)S(1)}, bf16[2,4,16,896]{3,2,1,0:T(8,128)(2,1)S(1)}, u32[]{:S(2)}, u32[]{:S(2)}) collective-permute-start(bf16[2,4,16,896]{3,2,1,0:T(8,128)(2,1)S(1)} %slice.50), channel_id=1, source_target_pairs={{0,32},{1,33},{2,34},{3,35},{4,36},{5,37},{6,38},{7,39},{8,10},{9,... | collective-permute-start | bytes 688136 | tf_op jit(solution)/shard_map/ppermute | solution.py:66
  19.6 8.0 %collective-permute-start.9 = (bf16[2,4,16,896]{3,2,1,0:T(8,128)(2,1)S(1)}, bf16[2,4,16,896]{3,2,1,0:T(8,128)(2,1)S(1)}, u32[]{:S(2)}, u32[]{:S(2)}) collective-permute-start(bf16[2,4,16,896]{3,2,1,0:T(8,128)(2,1)S(1)} %slice.50), channel_id=1, source_target_pairs={{0,96},{1,97},{2,98},{3,99},{4,100},{5,101},{6,102},{7,103},{8,14}... | collective-permute-start | bytes 688136 | tf_op jit(solution)/shard_map/ppermute | solution.py:66
  25.2 3.2 %collective-permute-start.11 = (s32[1,256]{1,0:T(1,128)S(1)}, s32[1,256]{1,0:T(1,128)S(1)}, u32[]{:S(2)}, u32[]{:S(2)}) collective-permute-start(s32[1,256]{1,0:T(1,128)S(1)} %bitcast.104), channel_id=1, source_target_pairs={{0,8},{1,9},{2,10},{3,11},{4,12},{5,13},{6,14},{7,15},{8,0},{9,1},... | collective-permute-start | bytes 3080 | tf_op jit(solution)/shard_map/ppermute | solution.py:66
  28.4 6.5 %collective-permute-start.10 = (bf16[2,4,16,896]{3,2,1,0:T(8,128)(2,1)S(1)}, bf16[2,4,16,896]{3,2,1,0:T(8,128)(2,1)S(1)}, u32[]{:S(2)}, u32[]{:S(2)}) collective-permute-start(bf16[2,4,16,896]{3,2,1,0:T(8,128)(2,1)S(1)} %slice.50), channel_id=1, source_target_pairs={{0,64},{1,65},{2,66},{3,67},{4,68},{5,69},{6,70},{7,71},{8,12},{9,... | collective-permute-start | bytes 688136 | tf_op jit(solution)/shard_map/ppermute | solution.py:66
  30.7 8.8 %collective-permute-start.7 = (bf16[2,4,32,896]{3,2,1,0:T(8,128)(2,1)S(1)}, bf16[2,4,32,896]{3,2,1,0:T(8,128)(2,1)S(1)}, u32[]{:S(2)}, u32[]{:S(2)}) collective-permute-start(bf16[2,4,32,896]{3,2,1,0:T(8,128)(2,1)S(1)} %collective-permute-done.5), channel_id=1, source_target_pairs={{0,1},{1,16},{2,3},{3,18},{4,5},{5,20},{6,7},{7,22},{8,25},{9,8},{... | collective-permute-start | bytes 1376264 | tf_op jit(solution)/shard_map/ppermute | solution.py:66
  39.6 13.8 %collective-permute-start.12 = (bf16[2,2,4,32,896]{4,3,2,1,0:T(8,128)(2,1)S(1)}, bf16[2,2,4,32,896]{4,3,2,1,0:T(8,128)(2,1)S(1)}, u32[]{:S(2)}, u32[]{:S(2)}) collective-permute-start(bf16[2,2,4,32,896]{4,3,2,1,0:T(8,128)(2,1)S(1)} %get-tuple-element.48), channel_id=1, source_target_pairs={{0,32},{1,33},{2,34},{3,35},{4,36},{5,37},{6,38},{7,39},{8,10},{9,... | collective-permute-start | bytes 2752520 | tf_op jit(solution)/shard_map/ppermute | solution.py:66
  40.0 14.1 %collective-permute-start.13 = (bf16[2,2,4,32,896]{4,3,2,1,0:T(8,128)(2,1)S(1)}, bf16[2,2,4,32,896]{4,3,2,1,0:T(8,128)(2,1)S(1)}, u32[]{:S(2)}, u32[]{:S(2)}) collective-permute-start(bf16[2,2,4,32,896]{4,3,2,1,0:T(8,128)(2,1)S(1)} %get-tuple-element.49), channel_id=1, source_target_pairs={{0,96},{1,97},{2,98},{3,99},{4,100},{5,101},{6,102},{7,103},{8,14}... | collective-permute-start | bytes 2752520 | tf_op jit(solution)/shard_map/ppermute | solution.py:66
  42.3 18.1 %collective-permute-start.17 = (bf16[2,4,4,16,896]{4,3,2,1,0:T(8,128)(2,1)S(1)}, bf16[2,4,4,16,896]{4,3,2,1,0:T(8,128)(2,1)S(1)}, u32[]{:S(2)}, u32[]{:S(2)}) collective-permute-start(bf16[2,4,4,16,896]{4,3,2,1,0:T(8,128)(2,1)S(1)} %bitcast_dynamic-update-slice_fusion.15), channel_id=1, source_target_pairs={{0,1},{1,16},{2,3},{3,18},{4,5},{5,20},{6,7},{7,22},{8,25},{9,8},{... | collective-permute-start | bytes 2752520 | tf_op jit(solution)/shard_map/ppermute | solution.py:66
  45.5 21.4 %collective-permute-start.19 = (bf16[2,4,4,16,896]{4,3,2,1,0:T(8,128)(2,1)S(1)}, bf16[2,4,4,16,896]{4,3,2,1,0:T(8,128)(2,1)S(1)}, u32[]{:S(2)}, u32[]{:S(2)}) collective-permute-start(bf16[2,4,4,16,896]{4,3,2,1,0:T(8,128)(2,1)S(1)} %bitcast_dynamic-update-slice_fusion.15), channel_id=1, source_target_pairs={{0,17},{1,0},{2,19},{3,2},{4,21},{5,4},{6,23},{7,6},{8,9},{9,24},{... | collective-permute-start | bytes 2752520 | tf_op jit(solution)/shard_map/ppermute | solution.py:66
  53.4 13.9 %collective-permute-start.16 = (bf16[2,2,4,32,896]{4,3,2,1,0:T(8,128)(2,1)S(1)}, bf16[2,2,4,32,896]{4,3,2,1,0:T(8,128)(2,1)S(1)}, u32[]{:S(2)}, u32[]{:S(2)}) collective-permute-start(bf16[2,2,4,32,896]{4,3,2,1,0:T(8,128)(2,1)S(1)} %get-tuple-element.49), channel_id=1, source_target_pairs={{0,32},{1,33},{2,34},{3,35},{4,36},{5,37},{6,38},{7,39},{8,10},{9,... | collective-permute-start | bytes 2752520 | tf_op jit(solution)/shard_map/ppermute | solution.py:66
  54.1 13.5 %collective-permute-start.14 = (bf16[2,2,4,32,896]{4,3,2,1,0:T(8,128)(2,1)S(1)}, bf16[2,2,4,32,896]{4,3,2,1,0:T(8,128)(2,1)S(1)}, u32[]{:S(2)}, u32[]{:S(2)}) collective-permute-start(bf16[2,2,4,32,896]{4,3,2,1,0:T(8,128)(2,1)S(1)} %get-tuple-element.48), channel_id=1, source_target_pairs={{0,96},{1,97},{2,98},{3,99},{4,100},{5,101},{6,102},{7,103},{8,14}... | collective-permute-start | bytes 2752520 | tf_op jit(solution)/shard_map/ppermute | solution.py:66
  60.5 20.3 %collective-permute-start.18 = (bf16[2,2,4,32,896]{4,3,2,1,0:T(8,128)(2,1)S(1)}, bf16[2,2,4,32,896]{4,3,2,1,0:T(8,128)(2,1)S(1)}, u32[]{:S(2)}, u32[]{:S(2)}) collective-permute-start(bf16[2,2,4,32,896]{4,3,2,1,0:T(8,128)(2,1)S(1)} %collective-permute-done.13), channel_id=1, source_target_pairs={{0,96},{1,97},{2,98},{3,99},{4,100},{5,101},{6,102},{7,103},{8,14}... | collective-permute-start | bytes 2752520 | tf_op jit(solution)/shard_map/ppermute | solution.py:66
  66.8 14.1 %collective-permute-start.20 = (bf16[2,4,4,16,896]{4,3,2,1,0:T(8,128)(2,1)S(1)}, bf16[2,4,4,16,896]{4,3,2,1,0:T(8,128)(2,1)S(1)}, u32[]{:S(2)}, u32[]{:S(2)}) collective-permute-start(bf16[2,4,4,16,896]{4,3,2,1,0:T(8,128)(2,1)S(1)} %collective-permute-done.17), channel_id=1, source_target_pairs={{0,1},{1,16},{2,3},{3,18},{4,5},{5,20},{6,7},{7,22},{8,25},{9,8},{... | collective-permute-start | bytes 2752520 | tf_op jit(solution)/shard_map/ppermute | solution.py:66
  66.8 13.8 %collective-permute-start.15 = (bf16[2,2,4,32,896]{4,3,2,1,0:T(8,128)(2,1)S(1)}, bf16[2,2,4,32,896]{4,3,2,1,0:T(8,128)(2,1)S(1)}, u32[]{:S(2)}, u32[]{:S(2)}) collective-permute-start(bf16[2,2,4,32,896]{4,3,2,1,0:T(8,128)(2,1)S(1)} %collective-permute-done.12), channel_id=1, source_target_pairs={{0,32},{1,33},{2,34},{3,35},{4,36},{5,37},{6,38},{7,39},{8,10},{9,... | collective-permute-start | bytes 2752520 | tf_op jit(solution)/shard_map/ppermute | solution.py:66
  82.0 15.6 %collective-permute-start.21 = (bf16[768,896]{1,0:T(8,128)(2,1)S(1)}, bf16[768,896]{1,0:T(8,128)(2,1)S(1)}, u32[]{:S(2)}, u32[]{:S(2)}) collective-permute-start(bf16[768,896]{1,0:T(8,128)(2,1)S(1)} %bitcast.101), channel_id=1, source_target_pairs={{0,8},{1,9},{2,10},{3,11},{4,12},{5,13},{6,14},{7,15},{8,0},{9,1},... | collective-permute-start | bytes 4128776 | tf_op jit(solution)/shard_map/ppermute | solution.py:66
  97.5 9.0 %copy-start.2 = (bf16[768,896]{1,0:T(8,128)(2,1)}, bf16[768,896]{1,0:T(8,128)(2,1)S(1)}, u32[]{:S(2)}) copy-start(bf16[768,896]{1,0:T(8,128)(2,1)S(1)} %get-tuple-element.54.refs_0_.refs_1_) | copy-start | bytes 4128772
  97.5 2.8 %copy-start = (bf16[1,96,128,128]{3,2,1,0:T(8,128)(2,1)S(1)}, bf16[1,96,128,128]{3,2,1,0:T(8,128)(2,1)}, u32[]{:S(2)}) copy-start(bf16[1,96,128,128]{3,2,1,0:T(8,128)(2,1)} %param.6) | copy-start | bytes 9437188
  99.5 17.8 %collective-permute-start.22 = (bf16[416,896]{1,0:T(8,128)(2,1)S(1)}, bf16[416,896]{1,0:T(8,128)(2,1)}, u32[]{:S(2)}, u32[]{:S(2)}) collective-permute-start(bf16[416,896]{1,0:T(8,128)(2,1)S(1)} %get-tuple-element.58), channel_id=1, source_target_pairs={{0,1},{1,0},{2,3},{3,2},{4,5},{5,4},{6,7},{7,6},{8,9},{9,8},{10,11... | collective-permute-start | bytes 2236424 | tf_op jit(solution)/shard_map/ppermute | solution.py:66
  106.6 24.0 %copy-start.1 = (bf16[768,896]{1,0:T(8,128)(2,1)}, bf16[768,896]{1,0:T(8,128)(2,1)S(1)}, u32[]{:S(2)}) copy-start(bf16[768,896]{1,0:T(8,128)(2,1)S(1)} %multiply.3.refs_0_) | copy-start | bytes 4128772
  109.3 10.6 %collective-permute-start.30 = (bf16[208,896]{1,0:T(8,128)(2,1)}, bf16[208,896]{1,0:T(8,128)(2,1)}, u32[]{:S(2)}, u32[]{:S(2)}) collective-permute-start(bf16[208,896]{1,0:T(8,128)(2,1)} %get-tuple-element.60), channel_id=1, source_target_pairs={{0,2},{1,3},{2,4},{3,5},{4,6},{5,7},{6,0},{7,1},{8,14},{9,15},{10,... | collective-permute-start | bytes 1118216 | tf_op jit(solution)/shard_map/ppermute | solution.py:66
  110.9 10.8 %collective-permute-start.31 = (bf16[208,896]{1,0:T(8,128)(2,1)}, bf16[208,896]{1,0:T(8,128)(2,1)}, u32[]{:S(2)}, u32[]{:S(2)}) collective-permute-start(bf16[208,896]{1,0:T(8,128)(2,1)} %get-tuple-element.61), channel_id=1, source_target_pairs={{0,6},{1,7},{2,0},{3,1},{4,2},{5,3},{6,4},{7,5},{8,10},{9,11},{10,... | collective-permute-start | bytes 1118216 | tf_op jit(solution)/shard_map/ppermute | solution.py:66
  110.9 18.3 %collective-permute-start.32 = (bf16[208,896]{1,0:T(8,128)(2,1)}, bf16[208,896]{1,0:T(8,128)(2,1)}, u32[]{:S(2)}, u32[]{:S(2)}) collective-permute-start(bf16[208,896]{1,0:T(8,128)(2,1)} %get-tuple-element.62), channel_id=1, source_target_pairs={{0,4},{1,5},{2,6},{3,7},{4,0},{5,1},{6,2},{7,3},{8,12},{9,13},{10,... | collective-permute-start | bytes 1118216 | tf_op jit(solution)/shard_map/ppermute | solution.py:66
  130.6 5.5 %collective-permute-start.33 = (bf16[104,896]{1,0:T(8,128)(2,1)S(1)}, bf16[104,896]{1,0:T(8,128)(2,1)S(1)}, u32[]{:S(2)}, u32[]{:S(2)}) collective-permute-start(bf16[104,896]{1,0:T(8,128)(2,1)S(1)} %constant_dynamic-slice_fusion), channel_id=1, source_target_pairs={{0,1},{1,0},{2,3},{3,2},{4,5},{5,4},{6,7},{7,6},{8,9},{9,8},{10,11... | collective-permute-start | bytes 559112 | tf_op jit(solution)/shard_map/ppermute | solution.py:66
  130.9 6.6 %collective-permute-start.25 = (bf16[104,896]{1,0:T(8,128)(2,1)S(1)}, bf16[104,896]{1,0:T(8,128)(2,1)S(1)}, u32[]{:S(2)}, u32[]{:S(2)}) collective-permute-start(bf16[104,896]{1,0:T(8,128)(2,1)S(1)} %get-tuple-element.83), channel_id=1, source_target_pairs={{0,4},{1,5},{2,6},{3,7},{4,0},{5,1},{6,2},{7,3},{8,12},{9,13},{10,... | collective-permute-start | bytes 559112 | tf_op jit(solution)/shard_map/ppermute | solution.py:66
  131.4 10.9 %collective-permute-start.24 = (bf16[104,896]{1,0:T(8,128)(2,1)S(1)}, bf16[104,896]{1,0:T(8,128)(2,1)S(1)}, u32[]{:S(2)}, u32[]{:S(2)}) collective-permute-start(bf16[104,896]{1,0:T(8,128)(2,1)S(1)} %get-tuple-element.84), channel_id=1, source_target_pairs={{0,6},{1,7},{2,0},{3,1},{4,2},{5,3},{6,4},{7,5},{8,10},{9,11},{10,... | collective-permute-start | bytes 559112 | tf_op jit(solution)/shard_map/ppermute | solution.py:66
  132.6 9.7 %collective-permute-start.23 = (bf16[104,896]{1,0:T(8,128)(2,1)S(1)}, bf16[104,896]{1,0:T(8,128)(2,1)S(1)}, u32[]{:S(2)}, u32[]{:S(2)}) collective-permute-start(bf16[104,896]{1,0:T(8,128)(2,1)S(1)} %get-tuple-element.82), channel_id=1, source_target_pairs={{0,2},{1,3},{2,4},{3,5},{4,6},{5,7},{6,0},{7,1},{8,14},{9,15},{10,... | collective-permute-start | bytes 559112 | tf_op jit(solution)/shard_map/ppermute | solution.py:66
  142.6 2.4 %collective-permute-start.34 = (bf16[104,896]{1,0:T(8,128)(2,1)S(1)}, bf16[104,896]{1,0:T(8,128)(2,1)S(1)}, u32[]{:S(2)}, u32[]{:S(2)}) collective-permute-start(bf16[104,896]{1,0:T(8,128)(2,1)S(1)} %get-tuple-element.95), channel_id=1, source_target_pairs={{0,8},{1,9},{2,10},{3,11},{4,12},{5,13},{6,14},{7,15},{8,0},{9,1},... | collective-permute-start | bytes 559112 | tf_op jit(solution)/shard_map/ppermute | solution.py:66
  143.9 1.4 collective-permute-start.26
  145.6 6.0 %collective-permute-start.27 = (bf16[104,896]{1,0:T(8,128)(2,1)S(1)}, bf16[104,896]{1,0:T(8,128)(2,1)S(1)}, u32[]{:S(2)}, u32[]{:S(2)}) collective-permute-start(bf16[104,896]{1,0:T(8,128)(2,1)S(1)} %get-tuple-element.94), channel_id=1, source_target_pairs={{0,2},{1,3},{2,4},{3,5},{4,6},{5,7},{6,0},{7,1},{8,14},{9,15},{10,... | collective-permute-start | bytes 559112 | tf_op jit(solution)/shard_map/ppermute | solution.py:66
  146.7 11.3 %collective-permute-start.28 = (bf16[104,896]{1,0:T(8,128)(2,1)S(1)}, bf16[104,896]{1,0:T(8,128)(2,1)S(1)}, u32[]{:S(2)}, u32[]{:S(2)}) collective-permute-start(bf16[104,896]{1,0:T(8,128)(2,1)S(1)} %get-tuple-element.94), channel_id=1, source_target_pairs={{0,6},{1,7},{2,0},{3,1},{4,2},{5,3},{6,4},{7,5},{8,10},{9,11},{10,... | collective-permute-start | bytes 559112 | tf_op jit(solution)/shard_map/ppermute | solution.py:66
  147.1 10.9 %collective-permute-start.29 = (bf16[104,896]{1,0:T(8,128)(2,1)S(1)}, bf16[104,896]{1,0:T(8,128)(2,1)S(1)}, u32[]{:S(2)}, u32[]{:S(2)}) collective-permute-start(bf16[104,896]{1,0:T(8,128)(2,1)S(1)} %get-tuple-element.94), channel_id=1, source_target_pairs={{0,4},{1,5},{2,6},{3,7},{4,0},{5,1},{6,2},{7,3},{8,12},{9,13},{10,... | collective-permute-start | bytes 559112 | tf_op jit(solution)/shard_map/ppermute | solution.py:66
  147.9 10.1 %collective-permute-start.35 = (bf16[104,896]{1,0:T(8,128)(2,1)S(1)}, bf16[104,896]{1,0:T(8,128)(2,1)S(1)}, u32[]{:S(2)}, u32[]{:S(2)}) collective-permute-start(bf16[104,896]{1,0:T(8,128)(2,1)S(1)} %get-tuple-element.74), channel_id=1, source_target_pairs={{0,1},{1,0},{2,3},{3,2},{4,5},{5,4},{6,7},{7,6},{8,9},{9,8},{10,11... | collective-permute-start | bytes 559112 | tf_op jit(solution)/shard_map/ppermute | solution.py:66
  158.1 20.2 %collective-permute-start.36 = (bf16[416,896]{1,0:T(8,128)(2,1)S(1)}, bf16[416,896]{1,0:T(8,128)(2,1)S(1)}, u32[]{:S(2)}, u32[]{:S(2)}) collective-permute-start(bf16[416,896]{1,0:T(8,128)(2,1)S(1)} %constant_dynamic-update-slice_fusion.6.refs_2_), channel_id=1, source_target_pairs={{0,1},{1,0},{2,3},{3,2},{4,5},{5,4},{6,7},{7,6},{8,9},{9,8},{10,11... | collective-permute-start | bytes 2236424 | tf_op jit(solution)/shard_map/ppermute | solution.py:66
  159.5 9.6 %collective-permute-start.37 = (bf16[208,896]{1,0:T(8,128)(2,1)S(1)}, bf16[208,896]{1,0:T(8,128)(2,1)S(1)}, u32[]{:S(2)}, u32[]{:S(2)}) collective-permute-start(bf16[208,896]{1,0:T(8,128)(2,1)S(1)} %constant_dynamic-update-slice_fusion.4.refs_4_), channel_id=1, source_target_pairs={{0,2},{1,3},{2,4},{3,5},{4,6},{5,7},{6,0},{7,1},{8,14},{9,15},{10,... | collective-permute-start | bytes 1118216 | tf_op jit(solution)/shard_map/ppermute | solution.py:66
  159.5 18.8 %collective-permute-start.38 = (bf16[208,896]{1,0:T(8,128)(2,1)S(1)}, bf16[208,896]{1,0:T(8,128)(2,1)S(1)}, u32[]{:S(2)}, u32[]{:S(2)}) collective-permute-start(bf16[208,896]{1,0:T(8,128)(2,1)S(1)} %constant_dynamic-update-slice_fusion.4.refs_4_), channel_id=1, source_target_pairs={{0,6},{1,7},{2,0},{3,1},{4,2},{5,3},{6,4},{7,5},{8,10},{9,11},{10,... | collective-permute-start | bytes 1118216 | tf_op jit(solution)/shard_map/ppermute | solution.py:66
  161.0 17.3 %collective-permute-start.39 = (bf16[208,896]{1,0:T(8,128)(2,1)S(1)}, bf16[208,896]{1,0:T(8,128)(2,1)S(1)}, u32[]{:S(2)}, u32[]{:S(2)}) collective-permute-start(bf16[208,896]{1,0:T(8,128)(2,1)S(1)} %constant_dynamic-update-slice_fusion.4.refs_4_), channel_id=1, source_target_pairs={{0,4},{1,5},{2,6},{3,7},{4,0},{5,1},{6,2},{7,3},{8,12},{9,13},{10,... | collective-permute-start | bytes 1118216 | tf_op jit(solution)/shard_map/ppermute | solution.py:66
  185.1 4.4 %collective-permute-start.40 = (f32[416,768]{1,0:T(8,128)}, f32[416,768]{1,0:T(8,128)S(1)}, u32[]{:S(2)}, u32[]{:S(2)}) collective-permute-start(f32[416,768]{1,0:T(8,128)} %get-tuple-element.70), channel_id=1, source_target_pairs={{0,8},{1,9},{2,10},{3,11},{4,12},{5,13},{6,14},{7,15},{8,0},{9,1},... | collective-permute-start | bytes 3833864 | tf_op jit(solution)/shard_map/ppermute | solution.py:66
  189.6 1.0 copy-start.3
  192.1 6.9 %collective-permute-start.43 = (bf16[104,768]{1,0:T(8,128)(2,1)S(1)}, bf16[104,768]{1,0:T(8,128)(2,1)S(1)}, u32[]{:S(2)}, u32[]{:S(2)}) collective-permute-start(bf16[104,768]{1,0:T(8,128)(2,1)S(1)} %get-tuple-element.80), channel_id=1, source_target_pairs={{0,64},{1,65},{2,66},{3,67},{4,68},{5,69},{6,70},{7,71},{8,72},{9,... | collective-permute-start | bytes 479240 | tf_op jit(solution)/shard_map/ppermute | solution.py:66
  192.5 8.8 %collective-permute-start.42 = (bf16[104,768]{1,0:T(8,128)(2,1)S(1)}, bf16[104,768]{1,0:T(8,128)(2,1)S(1)}, u32[]{:S(2)}, u32[]{:S(2)}) collective-permute-start(bf16[104,768]{1,0:T(8,128)(2,1)S(1)} %get-tuple-element.81), channel_id=1, source_target_pairs={{0,96},{1,97},{2,98},{3,99},{4,100},{5,101},{6,102},{7,103},{8,40}... | collective-permute-start | bytes 479240 | tf_op jit(solution)/shard_map/ppermute | solution.py:66
  197.5 7.3 %collective-permute-start.41 = (bf16[104,768]{1,0:T(8,128)(2,1)S(1)}, bf16[104,768]{1,0:T(8,128)(2,1)S(1)}, u32[]{:S(2)}, u32[]{:S(2)}) collective-permute-start(bf16[104,768]{1,0:T(8,128)(2,1)S(1)} %get-tuple-element.79), channel_id=1, source_target_pairs={{0,32},{1,33},{2,34},{3,35},{4,36},{5,37},{6,38},{7,39},{8,104},{9... | collective-permute-start | bytes 479240 | tf_op jit(solution)/shard_map/ppermute | solution.py:66
  204.9 9.4 %collective-permute-start.44 = (f32[104,768]{1,0:T(8,128)S(1)}, f32[104,768]{1,0:T(8,128)S(1)}, u32[]{:S(2)}, u32[]{:S(2)}) collective-permute-start(f32[104,768]{1,0:T(8,128)S(1)} %add_add_fusion), channel_id=1, source_target_pairs={{0,16},{1,17},{2,18},{3,19},{4,20},{5,21},{6,22},{7,23},{8,24},{9,... | collective-permute-start | bytes 958472 | tf_op jit(solution)/shard_map/ppermute | solution.py:66
  214.5 6.3 %collective-permute-start.45 = (bf16[104,768]{1,0:T(8,128)(2,1)S(1)}, bf16[104,768]{1,0:T(8,128)(2,1)S(1)}, u32[]{:S(2)}, u32[]{:S(2)}) collective-permute-start(bf16[104,768]{1,0:T(8,128)(2,1)S(1)} %get-tuple-element.72), channel_id=1, source_target_pairs={{0,32},{1,33},{2,34},{3,35},{4,36},{5,37},{6,38},{7,39},{8,104},{9... | collective-permute-start | bytes 479240 | tf_op jit(solution)/shard_map/ppermute | solution.py:66
  218.5 9.4 %collective-permute-start.46 = (bf16[104,768]{1,0:T(8,128)(2,1)S(1)}, bf16[104,768]{1,0:T(8,128)(2,1)S(1)}, u32[]{:S(2)}, u32[]{:S(2)}) collective-permute-start(bf16[104,768]{1,0:T(8,128)(2,1)S(1)} %get-tuple-element.72), channel_id=1, source_target_pairs={{0,96},{1,97},{2,98},{3,99},{4,100},{5,101},{6,102},{7,103},{8,40}... | collective-permute-start | bytes 479240 | tf_op jit(solution)/shard_map/ppermute | solution.py:66
  218.5 9.4 %collective-permute-start.47 = (bf16[104,768]{1,0:T(8,128)(2,1)S(1)}, bf16[104,768]{1,0:T(8,128)(2,1)S(1)}, u32[]{:S(2)}, u32[]{:S(2)}) collective-permute-start(bf16[104,768]{1,0:T(8,128)(2,1)S(1)} %get-tuple-element.72), channel_id=1, source_target_pairs={{0,64},{1,65},{2,66},{3,67},{4,68},{5,69},{6,70},{7,71},{8,72},{9,... | collective-permute-start | bytes 479240 | tf_op jit(solution)/shard_map/ppermute | solution.py:66
  228.0 2.2 collective-permute-start.48

commit v6 on v5

--- a/solution.py
+++ b/solution.py
@@ -290,6 +290,39 @@
         cost_estimate=pl.CostEstimate(flops=2 * 768 * 896 * 896, bytes_accessed=2**23, transcendentals=0),
         name="cross",
     )(half, slab, theirs)
+
+
+def sum_kernel(starts, many, *refs):
+    arrays, outs, total = refs[:many], refs[many:-1], refs[-1]
+    total[...] = sum(array[...].astype(f32) for array in arrays)
+    for out, start in zip(outs, starts()):
+        n = out.shape[0]
+        out[...] = total[pl.ds(pl.multiple_of(start * n, n), n), :].astype(out.dtype)
+
+
+def sum_chunks(starts, pieces, *arrays):
+    n, width = arrays[0].shape
+    own = jax.ShapeDtypeStruct((n // pieces, width), f32)
+    sent = jax.ShapeDtypeStruct((n // pieces, width), bf16)
+
+    def kernel(*refs):
+        sum_kernel(starts, len(arrays), *refs)
+
+    return pl.pallas_call(
+        kernel,
+        out_shape=[own] + [sent] * (pieces - 1),
+        in_specs=[pl.BlockSpec(memory_space=pltpu.VMEM)] * len(arrays),
+        out_specs=[pl.BlockSpec(memory_space=pltpu.VMEM)] * pieces,
+        scratch_shapes=[pltpu.VMEM((n, width), f32)],
+        compiler_params=pltpu.CompilerParams(vmem_limit_bytes=24 * 1024 * 1024),
+        cost_estimate=pl.CostEstimate(flops=n * width, bytes_accessed=2**21, transcendentals=0),
+        name="sum_chunks",
+    )(*arrays)
+
+
+def chunks_y():
+    y, c = lax.axis_index("aux") // (ZH * CORE), here()[0]
+    return y, (y + 1 - 2 * c) % Y, (y - 1 + 2 * c) % Y, (y + 2) % Y
 
 
 def exchange_kernel(*refs):
@@ -390,12 +423,11 @@
     rest_behind = send(rest, around(two, -1, False))
     main_far = send(main_ahead, around(zz, 1, True))
     main_behind = send(main, around(zz, -1, True))
-    rest_far = send_after(rest, around(two, 2, False), rest_ahead, main_ahead)
+    rest_far = send(rest, around(two, 2, False))
 
     lists = lax.optimization_barrier((block_rows[0], block_cols[0], block_count[0], rest_ahead))
     lists = jnp.concatenate([lists[0] % ROW_BLOCKS, lists[1], lists[2]])
     lists = jnp.pad(lists, (0, 256 - 2 * SLOTS - 1))[None]
-    meta = jnp.concatenate([lists, swap_cores(lists)])
 
     mains = [jnp.zeros((ZH, ZL, 4, MAIN, WIDE), bf16)] * 2
     for array, at in (
@@ -416,13 +448,14 @@
     rest = into
 
     ahead, behind = around(two, 1, False), around(two, -1, False)
-    mains, rest, meta = lax.optimization_barrier((mains, rest, meta))
+    mains, rest, lists = lax.optimization_barrier((mains, rest, lists))
     ahead_0 = send(mains[0], ahead)
     behind_1 = send(mains[1], behind)
     rest_ahead = send(rest, around(zz, 1, True))
     rest_behind = send(rest, around(zz, -1, True))
-    ahead_1 = send_after(mains[1], ahead, ahead_0)
-    behind_0 = send_after(mains[0], behind, behind_1)
+    meta = jnp.concatenate([lists, swap_cores(lists)])
+    ahead_1 = send_after(mains[1], ahead, ahead_0, meta)
+    behind_0 = send_after(mains[0], behind, behind_1, meta)
     far_0 = send(ahead_0, ahead)
     far_1 = send_after(behind_1, behind, rest_ahead)
     rest_far = send_after(rest_ahead, around(zz, 1, True), rest_behind)
@@ -453,9 +486,6 @@
     def add(*arrays):
         return sum(a.astype(f32) for a in arrays)
 
-    def rows_of(array, k, n):
-        return lax.dynamic_slice(array, (k * n, 0), (n, array.shape[1]))
-
     xx = ("x", "x")
     ahead, behind = around(xx, 1, True), around(xx, -1, True)
     opposite = around(xx, 2, True)
@@ -465,16 +495,11 @@
     first_half = multiply(0, meta, own_blocks, panels)
     mine, to_ahead, to_behind, to_far = cross(chunks_x, 4, first_half, slab, theirs)
     parts = (mine, send(to_ahead, ahead), send(to_behind, behind), send(to_far, opposite))
-    half_mine = add(half_mine, from_low).astype(bf16)
-    second = (
-        rows_of(half_mine, x, SHARD),
-        send(rows_of(half_mine, (x + sign) % 4, SHARD), ahead),
-        send(rows_of(half_mine, (x - sign) % 4, SHARD), behind),
-        send(rows_of(half_mine, (x + 2) % 4, SHARD), opposite),
-    )
-    parts, half_mine = lax.optimization_barrier((parts, half_mine))
-    mine = add(*parts).astype(bf16)
-    first_shard = add(rows_of(mine, zl, SHARD), swap_low(rows_of(mine, 1 - zl, SHARD)))
+    own, *sent = sum_chunks(chunks_x, 4, half_mine, from_low)
+    second = (own, send(sent[0], ahead), send(sent[1], behind), send(sent[2], opposite))
+    parts, _ = lax.optimization_barrier((parts, sent))
+    own, sent = sum_chunks(chunks_low, 2, *parts)
+    first_shard = add(own, swap_low(sent))
     second_shard = add(*second)
 
     last = (x == X - 1) & (zl == ZL - 1)
@@ -503,16 +528,8 @@
 
     yy = ("y", "y")
     ahead, behind, opposite = around(yy, 1, True), around(yy, -1, True), around(yy, 2, True)
-    mine = keep + swap_cores(give)
-
-    def quarter(k):
-        return rows_of(mine, k % Y, SHARD)
-
-    part = quarter(y) + add(
-        send(quarter(y + sign).astype(bf16), ahead),
-        send(quarter(y - sign).astype(bf16), behind),
-        send(quarter(y + 2).astype(bf16), opposite),
-    )
+    own, *sent = sum_chunks(chunks_y, 4, keep, swap_cores(give))
+    part = own + add(send(sent[0], ahead), send(sent[1], behind), send(sent[2], opposite))
     part = (part + swap_high(part)).astype(bf16)
     into = jnp.zeros((CROSS // 2, ROWS), bf16)
     for k, array in (

time: 232 us -> 224 us (0.966)
  waiting for transfers between devices: 123 us -> 116 us
  starting transfers between devices: 63.7 us -> 70.1 us
  other arithmetic: 8.33 us -> 4.25 us
    ppermute x49, waiting for transfers between devices: 123 us -> 116 us  [send(): return lax.ppermute(array, AXES, pairs)]
    ppermute x49, starting transfers between devices: 63.7 us -> 70.1 us  [send(): return lax.ppermute(array, AXES, pairs)]
    convert_element_type x2 -> x0, other arithmetic: 2.69 us -> none  [the longest x1 1.4 us: local(): mine = add(*parts).astype(bf16)]
  transfers between devices with their start and end apart: 49 -> 49, of which waited for: 33 -> 33; matrix products, arithmetic and copies ran while one was open for 3% -> 2% of each run, Pallas kernels for 9% -> 8%
where the time goes in v6:
time: 224 us; the launch traced here: 225 us
  waiting for transfers between devices  116 us (52%)
  starting transfers between devices  70.1 us (31%)
  Pallas kernels  27.7 us (12%)
  local copies, waits for them, and re-layouts  5.19 us (2%)
  other arithmetic  4.25 us (2%)
    ppermute x49, waiting for transfers between devices, send(): return lax.ppermute(array, AXES, pairs)  116 us
    ppermute x49, starting transfers between devices, send(): return lax.ppermute(array, AXES, pairs)  70.1 us
    pallas_call x2, Pallas kernels, multiply(): pl.pallas_call(kernel, out_shape=[half, held] if q == 1 else half, in_spe...  16.2 us
    pallas_call x1, Pallas kernels, exchange(): pl.pallas_call(exchange_kernel, out_shape=[jax.ShapeDtypeStruct((CROSS //...  5.79 us
  transfers between devices with their start and end apart: 49, of which 33 were waited for; matrix products, arithmetic and copies ran while one was open for 2% of the time, Pallas kernels for 8%

profile of v6, /device:TPU:1, one launch (start us, length us, event | category | flops | bytes accessed | tf_op | source)
XLA Modules:
  0.0 224.7 jit_solution(10432304724571154164)
XLA Ops:
  0.9 1.5 collective-permute-start
  4.6 1.4 collective-permute-start.1
  6.8 1.9 collective-permute-start.2
  8.7 1.3 collective-permute-start.3
  10.7 0.9 bitcast_dynamic-update-slice_fusion.19
  11.7 1.2 collective-permute-done.2
  12.9 1.8 collective-permute-done.3
  14.9 3.8 %collective-permute-start.5 = (bf16[2,4,32,896]{3,2,1,0:T(8,128)(2,1)S(1)}, bf16[2,4,32,896]{3,2,1,0:T(8,128)(2,1)S(1)}, u32[]{:S(2)}, u32[]{:S(2)}) collective-permute-start(bf16[2,4,32,896]{3,2,1,0:T(8,128)(2,1)S(1)} %slice.42), channel_id=1, source_target_pairs={{0,1},{1,16},{2,3},{3,18},{4,5},{5,20},{6,7},{7,22},{8,25},{9,8},{... | collective-permute-start | bytes 1376264 | tf_op jit(solution)/shard_map/ppermute | solution.py:66
  19.6 1.8 collective-permute-start.9
  21.4 1.2 collective-permute-start.10
  23.0 2.1 collective-permute-done.8
  25.2 1.6 collective-permute-done.9
  26.8 1.1 collective-permute-done.10
  28.0 3.0 %collective-permute-start.7 = (bf16[2,4,32,896]{3,2,1,0:T(8,128)(2,1)S(1)}, bf16[2,4,32,896]{3,2,1,0:T(8,128)(2,1)S(1)}, u32[]{:S(2)}, u32[]{:S(2)}) collective-permute-start(bf16[2,4,32,896]{3,2,1,0:T(8,128)(2,1)S(1)} %collective-permute-done.5), channel_id=1, source_target_pairs={{0,1},{1,16},{2,3},{3,18},{4,5},{5,20},{6,7},{7,22},{8,25},{9,8},{... | collective-permute-start | bytes 1376264 | tf_op jit(solution)/shard_map/ppermute | solution.py:66
  31.1 5.3 %collective-permute-done.7 = bf16[2,4,32,896]{3,2,1,0:T(8,128)(2,1)S(1)} collective-permute-done((bf16[2,4,32,896]{3,2,1,0:T(8,128)(2,1)S(1)}, bf16[2,4,32,896]{3,2,1,0:T(8,128)(2,1)S(1)}, u32[]{:S(2)}, u32[]{:S(2)}) %collective-permute-start.7) | collective-permute-done | bytes 458784 | tf_op jit(solution)/shard_map/ppermute | solution.py:66
  36.5 1.2 collective-permute-start.12
  37.6 3.1 %collective-permute-start.17 = (bf16[2,4,4,16,896]{4,3,2,1,0:T(8,128)(2,1)S(1)}, bf16[2,4,4,16,896]{4,3,2,1,0:T(8,128)(2,1)S(1)}, u32[]{:S(2)}, u32[]{:S(2)}) collective-permute-start(bf16[2,4,4,16,896]{4,3,2,1,0:T(8,128)(2,1)S(1)} %bitcast_dynamic-update-slice_fusion.15), channel_id=1, source_target_pairs={{0,1},{1,16},{2,3},{3,18},{4,5},{5,20},{6,7},{7,22},{8,25},{9,8},{... | collective-permute-start | bytes 2752520 | tf_op jit(solution)/shard_map/ppermute | solution.py:66
  40.8 5.0 %collective-permute-start.11 = (s32[1,256]{1,0:T(1,128)S(1)}, s32[1,256]{1,0:T(1,128)S(1)}, u32[]{:S(2)}, u32[]{:S(2)}) collective-permute-start(s32[1,256]{1,0:T(1,128)S(1)} %bitcast.104), channel_id=1, source_target_pairs={{0,8},{1,9},{2,10},{3,11},{4,12},{5,13},{6,14},{7,15},{8,0},{9,1},... | collective-permute-start | bytes 3080 | tf_op jit(solution)/shard_map/ppermute | solution.py:66
  45.7 1.3 collective-permute-start.13
  48.1 2.3 %collective-permute-done.12 = bf16[2,2,4,32,896]{4,3,2,1,0:T(8,128)(2,1)S(1)} collective-permute-done((bf16[2,2,4,32,896]{4,3,2,1,0:T(8,128)(2,1)S(1)}, bf16[2,2,4,32,896]{4,3,2,1,0:T(8,128)(2,1)S(1)}, u32[]{:S(2)}, u32[]{:S(2)}) %collective-permute-start.12) | collective-permute-done | bytes 917536 | tf_op jit(solution)/shard_map/ppermute | solution.py:66
  51.1 7.2 %collective-permute-done.13 = bf16[2,2,4,32,896]{4,3,2,1,0:T(8,128)(2,1)S(1)} collective-permute-done((bf16[2,2,4,32,896]{4,3,2,1,0:T(8,128)(2,1)S(1)}, bf16[2,2,4,32,896]{4,3,2,1,0:T(8,128)(2,1)S(1)}, u32[]{:S(2)}, u32[]{:S(2)}) %collective-permute-start.13) | collective-permute-done | bytes 917536 | tf_op jit(solution)/shard_map/ppermute | solution.py:66
  58.3 2.5 %collective-permute-start.14 = (bf16[2,2,4,32,896]{4,3,2,1,0:T(8,128)(2,1)S(1)}, bf16[2,2,4,32,896]{4,3,2,1,0:T(8,128)(2,1)S(1)}, u32[]{:S(2)}, u32[]{:S(2)}) collective-permute-start(bf16[2,2,4,32,896]{4,3,2,1,0:T(8,128)(2,1)S(1)} %get-tuple-element.56), channel_id=1, source_target_pairs={{0,96},{1,97},{2,98},{3,99},{4,100},{5,101},{6,102},{7,103},{8,14}... | collective-permute-start | bytes 2752520 | tf_op jit(solution)/shard_map/ppermute | solution.py:66
  60.8 1.3 collective-permute-done.19
  62.1 3.1 %collective-permute-start.15 = (bf16[2,2,4,32,896]{4,3,2,1,0:T(8,128)(2,1)S(1)}, bf16[2,2,4,32,896]{4,3,2,1,0:T(8,128)(2,1)S(1)}, u32[]{:S(2)}, u32[]{:S(2)}) collective-permute-start(bf16[2,2,4,32,896]{4,3,2,1,0:T(8,128)(2,1)S(1)} %collective-permute-done.12), channel_id=1, source_target_pairs={{0,32},{1,33},{2,34},{3,35},{4,36},{5,37},{6,38},{7,39},{8,10},{9,... | collective-permute-start | bytes 2752520 | tf_op jit(solution)/shard_map/ppermute | solution.py:66
  65.9 5.2 %collective-permute-done.14 = bf16[2,2,4,32,896]{4,3,2,1,0:T(8,128)(2,1)S(1)} collective-permute-done((bf16[2,2,4,32,896]{4,3,2,1,0:T(8,128)(2,1)S(1)}, bf16[2,2,4,32,896]{4,3,2,1,0:T(8,128)(2,1)S(1)}, u32[]{:S(2)}, u32[]{:S(2)}) %collective-permute-start.14) | collective-permute-done | bytes 917536 | tf_op jit(solution)/shard_map/ppermute | solution.py:66
  71.2 4.6 %collective-permute-done.15 = bf16[2,2,4,32,896]{4,3,2,1,0:T(8,128)(2,1)S(1)} collective-permute-done((bf16[2,2,4,32,896]{4,3,2,1,0:T(8,128)(2,1)S(1)}, bf16[2,2,4,32,896]{4,3,2,1,0:T(8,128)(2,1)S(1)}, u32[]{:S(2)}, u32[]{:S(2)}) %collective-permute-start.15) | collective-permute-done | bytes 917536 | tf_op jit(solution)/shard_map/ppermute | solution.py:66
  76.0 4.9 %collective-permute-done.18 = bf16[2,2,4,32,896]{4,3,2,1,0:T(8,128)(2,1)S(1)} collective-permute-done((bf16[2,2,4,32,896]{4,3,2,1,0:T(8,128)(2,1)S(1)}, bf16[2,2,4,32,896]{4,3,2,1,0:T(8,128)(2,1)S(1)}, u32[]{:S(2)}, u32[]{:S(2)}) %collective-permute-start.18) | collective-permute-done | bytes 917536 | tf_op jit(solution)/shard_map/ppermute | solution.py:66
  82.1 2.2 collective-permute-start.21
  84.4 11.9 %multiply.2 = (bf16[768,896]{1,0:T(8,128)(2,1)S(1)}, bf16[4,2,2,4,2,48,896]{6,5,4,3,2,1,0:T(8,128)(2,1)S(1)}) custom-call(s32[2,256]{1,0:T(2,128)S(1)} %pad_add_fusion.refs_0_, bf16[96,128,128]{2,1,0:T(8,128)(2,1)S(1)} %collective-permute-done.4.refs_1_, bf16[4,2,2,4,32,896]{5,4,3,2,1,0:T(8,128)(2,1)S(1)} %bitcast_dynamic-update-slice_fusion.8.refs_2_.main0, ...), custom_call_target="tpu_custom_call" | custom-call | flops 2818572288 | bytes 8388608 | tf_op jit(solution)/shard_map/multiply/pallas_call | solution.py:228
  96.3 2.0 cross.2
  98.7 4.3 %multiply.3.refs_0_ = bf16[768,896]{1,0:T(8,128)(2,1)S(1)} custom-call(s32[2,256]{1,0:T(2,128)S(1)} %pad_add_fusion.refs_0_, bf16[96,128,128]{2,1,0:T(8,128)(2,1)S(1)} %bitcast.100, bf16[4,2,2,4,2,48,896]{6,5,4,3,2,1,0:T(8,128)(2,1)S(1)} %get-tuple-element.64.refs_2_), custom_call_target="tpu_custom_call" | custom-call | flops 2818572288 | bytes 8388608 | tf_op jit(solution)/shard_map/multiply/pallas_call | solution.py:228
  103.0 1.8 cross.3
  105.2 1.2 collective-permute-start.31
  106.5 8.8 %collective-permute-done.22.refs_1_ = bf16[416,896]{1,0:T(8,128)(2,1)S(1)} collective-permute-done((bf16[416,896]{1,0:T(8,128)(2,1)S(1)}, bf16[416,896]{1,0:T(8,128)(2,1)S(1)}, u32[]{:S(2)}, u32[]{:S(2)}) %collective-permute-start.22) | collective-permute-done | bytes 745504 | tf_op jit(solution)/shard_map/ppermute | solution.py:66
  115.6 5.4 %collective-permute-done.32.refs_3_ = bf16[208,896]{1,0:T(8,128)(2,1)S(1)} collective-permute-done((bf16[208,896]{1,0:T(8,128)(2,1)S(1)}, bf16[208,896]{1,0:T(8,128)(2,1)S(1)}, u32[]{:S(2)}, u32[]{:S(2)}) %collective-permute-start.32) | collective-permute-done | bytes 372768 | tf_op jit(solution)/shard_map/ppermute | solution.py:66
  121.4 6.2 %collective-permute-start.33 = (bf16[104,896]{1,0:T(8,128)(2,1)S(1)}, bf16[104,896]{1,0:T(8,128)(2,1)S(1)}, u32[]{:S(2)}, u32[]{:S(2)}) collective-permute-start(bf16[104,896]{1,0:T(8,128)(2,1)S(1)} %get-tuple-element.80), channel_id=1, source_target_pairs={{0,1},{1,0},{2,3},{3,2},{4,5},{5,4},{6,7},{7,6},{8,9},{9,8},{10,11... | collective-permute-start | bytes 559112 | tf_op jit(solution)/shard_map/ppermute | solution.py:66
  127.6 1.2 collective-permute-start.25
  128.8 1.3 collective-permute-start.24
  130.1 1.4 collective-permute-start.23
  131.5 1.1 collective-permute-done.33
  132.5 3.2 %collective-permute-done.25 = bf16[104,896]{1,0:T(8,128)(2,1)S(1)} collective-permute-done((bf16[104,896]{1,0:T(8,128)(2,1)S(1)}, bf16[104,896]{1,0:T(8,128)(2,1)S(1)}, u32[]{:S(2)}, u32[]{:S(2)}) %collective-permute-start.25) | collective-permute-done | bytes 186400 | tf_op jit(solution)/shard_map/ppermute | solution.py:66
  135.8 3.4 %collective-permute-done.24 = bf16[104,896]{1,0:T(8,128)(2,1)S(1)} collective-permute-done((bf16[104,896]{1,0:T(8,128)(2,1)S(1)}, bf16[104,896]{1,0:T(8,128)(2,1)S(1)}, u32[]{:S(2)}, u32[]{:S(2)}) %collective-permute-start.24) | collective-permute-done | bytes 186400 | tf_op jit(solution)/shard_map/ppermute | solution.py:66
  139.5 1.1 collective-permute-start.34
  142.2 1.1 collective-permute-start.27
  145.6 2.2 collective-permute-done.27
  147.8 6.8 %collective-permute-done.28 = bf16[104,896]{1,0:T(8,128)(2,1)S(1)} collective-permute-done((bf16[104,896]{1,0:T(8,128)(2,1)S(1)}, bf16[104,896]{1,0:T(8,128)(2,1)S(1)}, u32[]{:S(2)}, u32[]{:S(2)}) %collective-permute-start.28) | collective-permute-done | bytes 186400 | tf_op jit(solution)/shard_map/ppermute | solution.py:66
  155.7 1.1 collective-permute-start.38
  157.1 7.7 %collective-permute-done.37.refs_5_ = bf16[208,896]{1,0:T(8,128)(2,1)S(1)} collective-permute-done((bf16[208,896]{1,0:T(8,128)(2,1)S(1)}, bf16[208,896]{1,0:T(8,128)(2,1)S(1)}, u32[]{:S(2)}, u32[]{:S(2)}) %collective-permute-start.37) | collective-permute-done | bytes 372768 | tf_op jit(solution)/shard_map/ppermute | solution.py:66
  164.8 10.1 %collective-permute-done.38.refs_6_ = bf16[208,896]{1,0:T(8,128)(2,1)S(1)} collective-permute-done((bf16[208,896]{1,0:T(8,128)(2,1)S(1)}, bf16[208,896]{1,0:T(8,128)(2,1)S(1)}, u32[]{:S(2)}, u32[]{:S(2)}) %collective-permute-start.38) | collective-permute-done | bytes 372768 | tf_op jit(solution)/shard_map/ppermute | solution.py:66
  174.9 5.8 %exchange.1 = (f32[416,768]{1,0:T(8,128)S(1)}, f32[416,768]{1,0:T(8,128)S(1)}) custom-call(bf16[768,896]{1,0:T(8,128)(2,1)} %copy-done.1, bf16[768,896]{1,0:T(8,128)(2,1)} %copy-done.2, bf16[416,896]{1,0:T(8,128)(2,1)S(1)} %constant_dynamic-update-slice_fusion.6.refs_2_, bf16[416,896]{1,0:T(8,128)(2,1)S(1)} %collective-permute-done.36.refs_3_, ...), custom_call_target="tpu_custom_call" | custom-call | flops 2466250752 | bytes 8388608 | tf_op jit(solution)/shard_map/exchange/pallas_call | solution.py:364
  180.7 1.2 collective-permute-start.40
  181.9 2.6 %collective-permute-done.40.refs_1_ = f32[416,768]{1,0:T(8,128)S(1)} collective-permute-done((f32[416,768]{1,0:T(8,128)S(1)}, f32[416,768]{1,0:T(8,128)S(1)}, u32[]{:S(2)}, u32[]{:S(2)}) %collective-permute-start.40) | collective-permute-done | bytes 1277984 | tf_op jit(solution)/shard_map/ppermute | solution.py:66
  184.7 4.4 %collective-permute-start.43 = (bf16[104,768]{1,0:T(8,128)(2,1)S(1)}, bf16[104,768]{1,0:T(8,128)(2,1)S(1)}, u32[]{:S(2)}, u32[]{:S(2)}) collective-permute-start(bf16[104,768]{1,0:T(8,128)(2,1)S(1)} %get-tuple-element.88), channel_id=1, source_target_pairs={{0,64},{1,65},{2,66},{3,67},{4,68},{5,69},{6,70},{7,71},{8,72},{9,... | collective-permute-start | bytes 479240 | tf_op jit(solution)/shard_map/ppermute | solution.py:66
  189.6 2.2 collective-permute-start.41
  191.7 1.5 collective-permute-done.43
  193.2 3.5 %collective-permute-done.42 = bf16[104,768]{1,0:T(8,128)(2,1)S(1)} collective-permute-done((bf16[104,768]{1,0:T(8,128)(2,1)S(1)}, bf16[104,768]{1,0:T(8,128)(2,1)S(1)}, u32[]{:S(2)}, u32[]{:S(2)}) %collective-permute-start.42) | collective-permute-done | bytes 159776 | tf_op jit(solution)/shard_map/ppermute | solution.py:66
  197.0 4.1 %collective-permute-start.44 = (f32[104,768]{1,0:T(8,128)S(1)}, f32[104,768]{1,0:T(8,128)S(1)}, u32[]{:S(2)}, u32[]{:S(2)}) collective-permute-start(f32[104,768]{1,0:T(8,128)S(1)} %add_add_fusion), channel_id=1, source_target_pairs={{0,16},{1,17},{2,18},{3,19},{4,20},{5,21},{6,22},{7,23},{8,24},{9,... | collective-permute-start | bytes 958472 | tf_op jit(solution)/shard_map/ppermute | solution.py:66
  201.1 7.5 %collective-permute-done.44 = f32[104,768]{1,0:T(8,128)S(1)} collective-permute-done((f32[104,768]{1,0:T(8,128)S(1)}, f32[104,768]{1,0:T(8,128)S(1)}, u32[]{:S(2)}, u32[]{:S(2)}) %collective-permute-start.44) | collective-permute-done | bytes 319520 | tf_op jit(solution)/shard_map/ppermute | solution.py:66
  208.7 1.8 collective-permute-start.45
  210.5 1.3 collective-permute-start.47
  211.8 1.4 collective-permute-done.45
  213.2 7.5 %collective-permute-done.46 = bf16[104,768]{1,0:T(8,128)(2,1)S(1)} collective-permute-done((bf16[104,768]{1,0:T(8,128)(2,1)S(1)}, bf16[104,768]{1,0:T(8,128)(2,1)S(1)}, u32[]{:S(2)}, u32[]{:S(2)}) %collective-permute-start.46) | collective-permute-done | bytes 159776 | tf_op jit(solution)/shard_map/ppermute | solution.py:66
  221.3 1.7 collective-permute-done.48
  223.1 1.6 convert_bitcast_fusion
  (113 shorter events, 18.2 us)
Async XLA Ops:
  0.9 2.4 %collective-permute-start = (bf16[48,800]{1,0:T(8,128)(2,1)S(1)}, bf16[48,800]{1,0:T(8,128)(2,1)S(1)}, u32[]{:S(2)}, u32[]{:S(2)}) collective-permute-start(bf16[48,800]{1,0:T(8,128)(2,1)S(1)} %broadcast_select_fusion.4), channel_id=1, source_target_pairs={{0,8},{1,9},{2,10},{3,11},{4,12},{5,13},{6,14},{7,15},{8,0},{9,1},... | collective-permute-start | bytes 230408 | tf_op jit(solution)/shard_map/ppermute | solution.py:66
  3.3 11.4 %collective-permute-start.4 = (bf16[96,128,128]{2,1,0:T(8,128)(2,1)}, bf16[96,128,128]{2,1,0:T(8,128)(2,1)S(1)}, u32[]{:S(2)}, u32[]{:S(2)}) collective-permute-start(bf16[96,128,128]{2,1,0:T(8,128)(2,1)} %bitcast.99), channel_id=1, source_target_pairs={{0,8},{1,9},{2,10},{3,11},{4,12},{5,13},{6,14},{7,15},{8,0},{9,1},... | collective-permute-start | bytes 9437192 | tf_op jit(solution)/shard_map/ppermute | solution.py:66
  4.6 6.1 %collective-permute-start.1 = (bf16[2,48,896]{2,1,0:T(8,128)(2,1)S(1)}, bf16[2,48,896]{2,1,0:T(8,128)(2,1)}, u32[]{:S(2)}, u32[]{:S(2)}) collective-permute-start(bf16[2,48,896]{2,1,0:T(8,128)(2,1)S(1)} %fusion.10), channel_id=1, source_target_pairs={{0,2},{1,3},{2,4},{3,5},{4,6},{5,7},{6,0},{7,1},{8,40},{9,41},{10,... | collective-permute-start | bytes 516104 | tf_op jit(solution)/shard_map/ppermute | solution.py:66
  6.8 18.3 %copy-start.4 = (s32[1,96]{1,0:T(1,128)S(1)}, s32[1,96]{1,0:T(1,128)}, u32[]{:S(2)}) copy-start(s32[1,96]{1,0:T(1,128)} %param.7) | copy-start | bytes 1156
  6.8 18.3 %copy-start.3 = (s32[1,96]{1,0:T(1,128)S(1)}, s32[1,96]{1,0:T(1,128)}, u32[]{:S(2)}) copy-start(s32[1,96]{1,0:T(1,128)} %param.8) | copy-start | bytes 1156
  6.8 6.1 %collective-permute-start.2 = (bf16[2,48,896]{2,1,0:T(8,128)(2,1)S(1)}, bf16[2,48,896]{2,1,0:T(8,128)(2,1)S(1)}, u32[]{:S(2)}, u32[]{:S(2)}) collective-permute-start(bf16[2,48,896]{2,1,0:T(8,128)(2,1)S(1)} %fusion.10), channel_id=1, source_target_pairs={{0,6},{1,7},{2,0},{3,1},{4,2},{5,3},{6,4},{7,5},{8,104},{9,105},{1... | collective-permute-start | bytes 516104 | tf_op jit(solution)/shard_map/ppermute | solution.py:66
  8.7 6.1 %collective-permute-start.3 = (bf16[2,48,896]{2,1,0:T(8,128)(2,1)S(1)}, bf16[2,48,896]{2,1,0:T(8,128)(2,1)S(1)}, u32[]{:S(2)}, u32[]{:S(2)}) collective-permute-start(bf16[2,48,896]{2,1,0:T(8,128)(2,1)S(1)} %fusion.10), channel_id=1, source_target_pairs={{0,4},{1,5},{2,6},{3,7},{4,0},{5,1},{6,2},{7,3},{8,72},{9,73},{10,... | collective-permute-start | bytes 516104 | tf_op jit(solution)/shard_map/ppermute | solution.py:66
  14.9 13.1 %collective-permute-start.5 = (bf16[2,4,32,896]{3,2,1,0:T(8,128)(2,1)S(1)}, bf16[2,4,32,896]{3,2,1,0:T(8,128)(2,1)S(1)}, u32[]{:S(2)}, u32[]{:S(2)}) collective-permute-start(bf16[2,4,32,896]{3,2,1,0:T(8,128)(2,1)S(1)} %slice.42), channel_id=1, source_target_pairs={{0,1},{1,16},{2,3},{3,18},{4,5},{5,20},{6,7},{7,22},{8,25},{9,8},{... | collective-permute-start | bytes 1376264 | tf_op jit(solution)/shard_map/ppermute | solution.py:66
  18.7 12.4 %collective-permute-start.6 = (bf16[2,4,32,896]{3,2,1,0:T(8,128)(2,1)S(1)}, bf16[2,4,32,896]{3,2,1,0:T(8,128)(2,1)S(1)}, u32[]{:S(2)}, u32[]{:S(2)}) collective-permute-start(bf16[2,4,32,896]{3,2,1,0:T(8,128)(2,1)S(1)} %slice.42), channel_id=1, source_target_pairs={{0,17},{1,0},{2,19},{3,2},{4,21},{5,4},{6,23},{7,6},{8,9},{9,24},{... | collective-permute-start | bytes 1376264 | tf_op jit(solution)/shard_map/ppermute | solution.py:66
  18.7 6.4 %collective-permute-start.8 = (bf16[2,4,16,896]{3,2,1,0:T(8,128)(2,1)S(1)}, bf16[2,4,16,896]{3,2,1,0:T(8,128)(2,1)S(1)}, u32[]{:S(2)}, u32[]{:S(2)}) collective-permute-start(bf16[2,4,16,896]{3,2,1,0:T(8,128)(2,1)S(1)} %slice.50), channel_id=1, source_target_pairs={{0,32},{1,33},{2,34},{3,35},{4,36},{5,37},{6,38},{7,39},{8,10},{9,... | collective-permute-start | bytes 688136 | tf_op jit(solution)/shard_map/ppermute | solution.py:66
  19.6 7.2 %collective-permute-start.9 = (bf16[2,4,16,896]{3,2,1,0:T(8,128)(2,1)S(1)}, bf16[2,4,16,896]{3,2,1,0:T(8,128)(2,1)S(1)}, u32[]{:S(2)}, u32[]{:S(2)}) collective-permute-start(bf16[2,4,16,896]{3,2,1,0:T(8,128)(2,1)S(1)} %slice.50), channel_id=1, source_target_pairs={{0,96},{1,97},{2,98},{3,99},{4,100},{5,101},{6,102},{7,103},{8,14}... | collective-permute-start | bytes 688136 | tf_op jit(solution)/shard_map/ppermute | solution.py:66
  21.4 6.6 %collective-permute-start.10 = (bf16[2,4,16,896]{3,2,1,0:T(8,128)(2,1)S(1)}, bf16[2,4,16,896]{3,2,1,0:T(8,128)(2,1)S(1)}, u32[]{:S(2)}, u32[]{:S(2)}) collective-permute-start(bf16[2,4,16,896]{3,2,1,0:T(8,128)(2,1)S(1)} %slice.50), channel_id=1, source_target_pairs={{0,64},{1,65},{2,66},{3,67},{4,68},{5,69},{6,70},{7,71},{8,12},{9,... | collective-permute-start | bytes 688136 | tf_op jit(solution)/shard_map/ppermute | solution.py:66
  28.0 8.5 %collective-permute-start.7 = (bf16[2,4,32,896]{3,2,1,0:T(8,128)(2,1)S(1)}, bf16[2,4,32,896]{3,2,1,0:T(8,128)(2,1)S(1)}, u32[]{:S(2)}, u32[]{:S(2)}) collective-permute-start(bf16[2,4,32,896]{3,2,1,0:T(8,128)(2,1)S(1)} %collective-permute-done.5), channel_id=1, source_target_pairs={{0,1},{1,16},{2,3},{3,18},{4,5},{5,20},{6,7},{7,22},{8,25},{9,8},{... | collective-permute-start | bytes 1376264 | tf_op jit(solution)/shard_map/ppermute | solution.py:66
  36.5 14.0 %collective-permute-start.12 = (bf16[2,2,4,32,896]{4,3,2,1,0:T(8,128)(2,1)S(1)}, bf16[2,2,4,32,896]{4,3,2,1,0:T(8,128)(2,1)S(1)}, u32[]{:S(2)}, u32[]{:S(2)}) collective-permute-start(bf16[2,2,4,32,896]{4,3,2,1,0:T(8,128)(2,1)S(1)} %get-tuple-element.56), channel_id=1, source_target_pairs={{0,32},{1,33},{2,34},{3,35},{4,36},{5,37},{6,38},{7,39},{8,10},{9,... | collective-permute-start | bytes 2752520 | tf_op jit(solution)/shard_map/ppermute | solution.py:66
  37.6 23.1 %collective-permute-start.17 = (bf16[2,4,4,16,896]{4,3,2,1,0:T(8,128)(2,1)S(1)}, bf16[2,4,4,16,896]{4,3,2,1,0:T(8,128)(2,1)S(1)}, u32[]{:S(2)}, u32[]{:S(2)}) collective-permute-start(bf16[2,4,4,16,896]{4,3,2,1,0:T(8,128)(2,1)S(1)} %bitcast_dynamic-update-slice_fusion.15), channel_id=1, source_target_pairs={{0,1},{1,16},{2,3},{3,18},{4,5},{5,20},{6,7},{7,22},{8,25},{9,8},{... | collective-permute-start | bytes 2752520 | tf_op jit(solution)/shard_map/ppermute | solution.py:66
  40.8 21.3 %collective-permute-start.19 = (bf16[2,4,4,16,896]{4,3,2,1,0:T(8,128)(2,1)S(1)}, bf16[2,4,4,16,896]{4,3,2,1,0:T(8,128)(2,1)S(1)}, u32[]{:S(2)}, u32[]{:S(2)}) collective-permute-start(bf16[2,4,4,16,896]{4,3,2,1,0:T(8,128)(2,1)S(1)} %bitcast_dynamic-update-slice_fusion.15), channel_id=1, source_target_pairs={{0,17},{1,0},{2,19},{3,2},{4,21},{5,4},{6,23},{7,6},{8,9},{9,24},{... | collective-permute-start | bytes 2752520 | tf_op jit(solution)/shard_map/ppermute | solution.py:66
  40.8 7.4 %collective-permute-start.11 = (s32[1,256]{1,0:T(1,128)S(1)}, s32[1,256]{1,0:T(1,128)S(1)}, u32[]{:S(2)}, u32[]{:S(2)}) collective-permute-start(s32[1,256]{1,0:T(1,128)S(1)} %bitcast.104), channel_id=1, source_target_pairs={{0,8},{1,9},{2,10},{3,11},{4,12},{5,13},{6,14},{7,15},{8,0},{9,1},... | collective-permute-start | bytes 3080 | tf_op jit(solution)/shard_map/ppermute | solution.py:66
  45.7 12.5 %collective-permute-start.13 = (bf16[2,2,4,32,896]{4,3,2,1,0:T(8,128)(2,1)S(1)}, bf16[2,2,4,32,896]{4,3,2,1,0:T(8,128)(2,1)S(1)}, u32[]{:S(2)}, u32[]{:S(2)}) collective-permute-start(bf16[2,2,4,32,896]{4,3,2,1,0:T(8,128)(2,1)S(1)} %get-tuple-element.57), channel_id=1, source_target_pairs={{0,96},{1,97},{2,98},{3,99},{4,100},{5,101},{6,102},{7,103},{8,14}... | collective-permute-start | bytes 2752520 | tf_op jit(solution)/shard_map/ppermute | solution.py:66
  50.5 15.1 %collective-permute-start.16 = (bf16[2,2,4,32,896]{4,3,2,1,0:T(8,128)(2,1)S(1)}, bf16[2,2,4,32,896]{4,3,2,1,0:T(8,128)(2,1)S(1)}, u32[]{:S(2)}, u32[]{:S(2)}) collective-permute-start(bf16[2,2,4,32,896]{4,3,2,1,0:T(8,128)(2,1)S(1)} %get-tuple-element.57), channel_id=1, source_target_pairs={{0,32},{1,33},{2,34},{3,35},{4,36},{5,37},{6,38},{7,39},{8,10},{9,... | collective-permute-start | bytes 2752520 | tf_op jit(solution)/shard_map/ppermute | solution.py:66
  58.3 12.8 %collective-permute-start.14 = (bf16[2,2,4,32,896]{4,3,2,1,0:T(8,128)(2,1)S(1)}, bf16[2,2,4,32,896]{4,3,2,1,0:T(8,128)(2,1)S(1)}, u32[]{:S(2)}, u32[]{:S(2)}) collective-permute-start(bf16[2,2,4,32,896]{4,3,2,1,0:T(8,128)(2,1)S(1)} %get-tuple-element.56), channel_id=1, source_target_pairs={{0,96},{1,97},{2,98},{3,99},{4,100},{5,101},{6,102},{7,103},{8,14}... | collective-permute-start | bytes 2752520 | tf_op jit(solution)/shard_map/ppermute | solution.py:66
  60.7 20.2 %collective-permute-start.18 = (bf16[2,2,4,32,896]{4,3,2,1,0:T(8,128)(2,1)S(1)}, bf16[2,2,4,32,896]{4,3,2,1,0:T(8,128)(2,1)S(1)}, u32[]{:S(2)}, u32[]{:S(2)}) collective-permute-start(bf16[2,2,4,32,896]{4,3,2,1,0:T(8,128)(2,1)S(1)} %collective-permute-done.13), channel_id=1, source_target_pairs={{0,96},{1,97},{2,98},{3,99},{4,100},{5,101},{6,102},{7,103},{8,14}... | collective-permute-start | bytes 2752520 | tf_op jit(solution)/shard_map/ppermute | solution.py:66
  62.1 19.0 %collective-permute-start.20 = (bf16[2,4,4,16,896]{4,3,2,1,0:T(8,128)(2,1)S(1)}, bf16[2,4,4,16,896]{4,3,2,1,0:T(8,128)(2,1)S(1)}, u32[]{:S(2)}, u32[]{:S(2)}) collective-permute-start(bf16[2,4,4,16,896]{4,3,2,1,0:T(8,128)(2,1)S(1)} %collective-permute-done.17), channel_id=1, source_target_pairs={{0,1},{1,16},{2,3},{3,18},{4,5},{5,20},{6,7},{7,22},{8,25},{9,8},{... | collective-permute-start | bytes 2752520 | tf_op jit(solution)/shard_map/ppermute | solution.py:66
  62.1 13.8 %collective-permute-start.15 = (bf16[2,2,4,32,896]{4,3,2,1,0:T(8,128)(2,1)S(1)}, bf16[2,2,4,32,896]{4,3,2,1,0:T(8,128)(2,1)S(1)}, u32[]{:S(2)}, u32[]{:S(2)}) collective-permute-start(bf16[2,2,4,32,896]{4,3,2,1,0:T(8,128)(2,1)S(1)} %collective-permute-done.12), channel_id=1, source_target_pairs={{0,32},{1,33},{2,34},{3,35},{4,36},{5,37},{6,38},{7,39},{8,10},{9,... | collective-permute-start | bytes 2752520 | tf_op jit(solution)/shard_map/ppermute | solution.py:66
  82.1 14.2 %collective-permute-start.21 = (bf16[768,896]{1,0:T(8,128)(2,1)S(1)}, bf16[768,896]{1,0:T(8,128)(2,1)S(1)}, u32[]{:S(2)}, u32[]{:S(2)}) collective-permute-start(bf16[768,896]{1,0:T(8,128)(2,1)S(1)} %bitcast.101), channel_id=1, source_target_pairs={{0,8},{1,9},{2,10},{3,11},{4,12},{5,13},{6,14},{7,15},{8,0},{9,1},... | collective-permute-start | bytes 4128776 | tf_op jit(solution)/shard_map/ppermute | solution.py:66
  96.3 6.8 %copy-start.2 = (bf16[768,896]{1,0:T(8,128)(2,1)}, bf16[768,896]{1,0:T(8,128)(2,1)S(1)}, u32[]{:S(2)}) copy-start(bf16[768,896]{1,0:T(8,128)(2,1)S(1)} %get-tuple-element.62.refs_0_.refs_1_) | copy-start | bytes 4128772
  96.3 2.4 %copy-start = (bf16[1,96,128,128]{3,2,1,0:T(8,128)(2,1)S(1)}, bf16[1,96,128,128]{3,2,1,0:T(8,128)(2,1)}, u32[]{:S(2)}) copy-start(bf16[1,96,128,128]{3,2,1,0:T(8,128)(2,1)} %param.6) | copy-start | bytes 9437188
  98.3 16.9 %collective-permute-start.22 = (bf16[416,896]{1,0:T(8,128)(2,1)S(1)}, bf16[416,896]{1,0:T(8,128)(2,1)S(1)}, u32[]{:S(2)}, u32[]{:S(2)}) collective-permute-start(bf16[416,896]{1,0:T(8,128)(2,1)S(1)} %get-tuple-element.66), channel_id=1, source_target_pairs={{0,1},{1,0},{2,3},{3,2},{4,5},{5,4},{6,7},{7,6},{8,9},{9,8},{10,11... | collective-permute-start | bytes 2236424 | tf_op jit(solution)/shard_map/ppermute | solution.py:66
  103.0 18.4 %copy-start.1 = (bf16[768,896]{1,0:T(8,128)(2,1)}, bf16[768,896]{1,0:T(8,128)(2,1)S(1)}, u32[]{:S(2)}) copy-start(bf16[768,896]{1,0:T(8,128)(2,1)S(1)} %multiply.3.refs_0_) | copy-start | bytes 4128772
  104.9 10.7 %collective-permute-start.30 = (bf16[208,896]{1,0:T(8,128)(2,1)S(1)}, bf16[208,896]{1,0:T(8,128)(2,1)S(1)}, u32[]{:S(2)}, u32[]{:S(2)}) collective-permute-start(bf16[208,896]{1,0:T(8,128)(2,1)S(1)} %get-tuple-element.72), channel_id=1, source_target_pairs={{0,2},{1,3},{2,4},{3,5},{4,6},{5,7},{6,0},{7,1},{8,14},{9,15},{10,... | collective-permute-start | bytes 1118216 | tf_op jit(solution)/shard_map/ppermute | solution.py:66
  105.2 10.4 %collective-permute-start.31 = (bf16[208,896]{1,0:T(8,128)(2,1)S(1)}, bf16[208,896]{1,0:T(8,128)(2,1)S(1)}, u32[]{:S(2)}, u32[]{:S(2)}) collective-permute-start(bf16[208,896]{1,0:T(8,128)(2,1)S(1)} %get-tuple-element.73), channel_id=1, source_target_pairs={{0,6},{1,7},{2,0},{3,1},{4,2},{5,3},{6,4},{7,5},{8,10},{9,11},{10,... | collective-permute-start | bytes 1118216 | tf_op jit(solution)/shard_map/ppermute | solution.py:66
  106.4 14.6 %collective-permute-start.32 = (bf16[208,896]{1,0:T(8,128)(2,1)S(1)}, bf16[208,896]{1,0:T(8,128)(2,1)S(1)}, u32[]{:S(2)}, u32[]{:S(2)}) collective-permute-start(bf16[208,896]{1,0:T(8,128)(2,1)S(1)} %get-tuple-element.74), channel_id=1, source_target_pairs={{0,4},{1,5},{2,6},{3,7},{4,0},{5,1},{6,2},{7,3},{8,12},{9,13},{10,... | collective-permute-start | bytes 1118216 | tf_op jit(solution)/shard_map/ppermute | solution.py:66
  121.4 11.1 %collective-permute-start.33 = (bf16[104,896]{1,0:T(8,128)(2,1)S(1)}, bf16[104,896]{1,0:T(8,128)(2,1)S(1)}, u32[]{:S(2)}, u32[]{:S(2)}) collective-permute-start(bf16[104,896]{1,0:T(8,128)(2,1)S(1)} %get-tuple-element.80), channel_id=1, source_target_pairs={{0,1},{1,0},{2,3},{3,2},{4,5},{5,4},{6,7},{7,6},{8,9},{9,8},{10,11... | collective-permute-start | bytes 559112 | tf_op jit(solution)/shard_map/ppermute | solution.py:66
  127.6 8.2 %collective-permute-start.25 = (bf16[104,896]{1,0:T(8,128)(2,1)S(1)}, bf16[104,896]{1,0:T(8,128)(2,1)S(1)}, u32[]{:S(2)}, u32[]{:S(2)}) collective-permute-start(bf16[104,896]{1,0:T(8,128)(2,1)S(1)} %get-tuple-element.70), channel_id=1, source_target_pairs={{0,4},{1,5},{2,6},{3,7},{4,0},{5,1},{6,2},{7,3},{8,12},{9,13},{10,... | collective-permute-start | bytes 559112 | tf_op jit(solution)/shard_map/ppermute | solution.py:66
  128.8 10.4 %collective-permute-start.24 = (bf16[104,896]{1,0:T(8,128)(2,1)S(1)}, bf16[104,896]{1,0:T(8,128)(2,1)S(1)}, u32[]{:S(2)}, u32[]{:S(2)}) collective-permute-start(bf16[104,896]{1,0:T(8,128)(2,1)S(1)} %get-tuple-element.69), channel_id=1, source_target_pairs={{0,6},{1,7},{2,0},{3,1},{4,2},{5,3},{6,4},{7,5},{8,10},{9,11},{10,... | collective-permute-start | bytes 559112 | tf_op jit(solution)/shard_map/ppermute | solution.py:66
  130.1 9.1 %collective-permute-start.23 = (bf16[104,896]{1,0:T(8,128)(2,1)S(1)}, bf16[104,896]{1,0:T(8,128)(2,1)S(1)}, u32[]{:S(2)}, u32[]{:S(2)}) collective-permute-start(bf16[104,896]{1,0:T(8,128)(2,1)S(1)} %get-tuple-element.68), channel_id=1, source_target_pairs={{0,2},{1,3},{2,4},{3,5},{4,6},{5,7},{6,0},{7,1},{8,14},{9,15},{10,... | collective-permute-start | bytes 559112 | tf_op jit(solution)/shard_map/ppermute | solution.py:66
  139.5 2.1 collective-permute-start.34
  140.5 1.4 collective-permute-start.26
  142.2 5.6 %collective-permute-start.27 = (bf16[104,896]{1,0:T(8,128)(2,1)S(1)}, bf16[104,896]{1,0:T(8,128)(2,1)S(1)}, u32[]{:S(2)}, u32[]{:S(2)}) collective-permute-start(bf16[104,896]{1,0:T(8,128)(2,1)S(1)} %get-tuple-element.106), channel_id=1, source_target_pairs={{0,2},{1,3},{2,4},{3,5},{4,6},{5,7},{6,0},{7,1},{8,14},{9,15},{10,... | collective-permute-start | bytes 559112 | tf_op jit(solution)/shard_map/ppermute | solution.py:66
  143.3 11.4 %collective-permute-start.28 = (bf16[104,896]{1,0:T(8,128)(2,1)S(1)}, bf16[104,896]{1,0:T(8,128)(2,1)S(1)}, u32[]{:S(2)}, u32[]{:S(2)}) collective-permute-start(bf16[104,896]{1,0:T(8,128)(2,1)S(1)} %get-tuple-element.106), channel_id=1, source_target_pairs={{0,6},{1,7},{2,0},{3,1},{4,2},{5,3},{6,4},{7,5},{8,10},{9,11},{10,... | collective-permute-start | bytes 559112 | tf_op jit(solution)/shard_map/ppermute | solution.py:66
  143.7 10.9 %collective-permute-start.29 = (bf16[104,896]{1,0:T(8,128)(2,1)S(1)}, bf16[104,896]{1,0:T(8,128)(2,1)S(1)}, u32[]{:S(2)}, u32[]{:S(2)}) collective-permute-start(bf16[104,896]{1,0:T(8,128)(2,1)S(1)} %get-tuple-element.106), channel_id=1, source_target_pairs={{0,4},{1,5},{2,6},{3,7},{4,0},{5,1},{6,2},{7,3},{8,12},{9,13},{10,... | collective-permute-start | bytes 559112 | tf_op jit(solution)/shard_map/ppermute | solution.py:66
  144.6 10.1 %collective-permute-start.35 = (bf16[104,896]{1,0:T(8,128)(2,1)S(1)}, bf16[104,896]{1,0:T(8,128)(2,1)S(1)}, u32[]{:S(2)}, u32[]{:S(2)}) collective-permute-start(bf16[104,896]{1,0:T(8,128)(2,1)S(1)} %get-tuple-element.92), channel_id=1, source_target_pairs={{0,1},{1,0},{2,3},{3,2},{4,5},{5,4},{6,7},{7,6},{8,9},{9,8},{10,11... | collective-permute-start | bytes 559112 | tf_op jit(solution)/shard_map/ppermute | solution.py:66
  154.8 20.1 %collective-permute-start.36 = (bf16[416,896]{1,0:T(8,128)(2,1)S(1)}, bf16[416,896]{1,0:T(8,128)(2,1)S(1)}, u32[]{:S(2)}, u32[]{:S(2)}) collective-permute-start(bf16[416,896]{1,0:T(8,128)(2,1)S(1)} %constant_dynamic-update-slice_fusion.6.refs_2_), channel_id=1, source_target_pairs={{0,1},{1,0},{2,3},{3,2},{4,5},{5,4},{6,7},{7,6},{8,9},{9,8},{10,11... | collective-permute-start | bytes 2236424 | tf_op jit(solution)/shard_map/ppermute | solution.py:66
  155.3 9.5 %collective-permute-start.37 = (bf16[208,896]{1,0:T(8,128)(2,1)S(1)}, bf16[208,896]{1,0:T(8,128)(2,1)S(1)}, u32[]{:S(2)}, u32[]{:S(2)}) collective-permute-start(bf16[208,896]{1,0:T(8,128)(2,1)S(1)} %constant_dynamic-update-slice_fusion.4.refs_4_), channel_id=1, source_target_pairs={{0,2},{1,3},{2,4},{3,5},{4,6},{5,7},{6,0},{7,1},{8,14},{9,15},{10,... | collective-permute-start | bytes 1118216 | tf_op jit(solution)/shard_map/ppermute | solution.py:66
  155.7 19.2 %collective-permute-start.38 = (bf16[208,896]{1,0:T(8,128)(2,1)S(1)}, bf16[208,896]{1,0:T(8,128)(2,1)S(1)}, u32[]{:S(2)}, u32[]{:S(2)}) collective-permute-start(bf16[208,896]{1,0:T(8,128)(2,1)S(1)} %constant_dynamic-update-slice_fusion.4.refs_4_), channel_id=1, source_target_pairs={{0,6},{1,7},{2,0},{3,1},{4,2},{5,3},{6,4},{7,5},{8,10},{9,11},{10,... | collective-permute-start | bytes 1118216 | tf_op jit(solution)/shard_map/ppermute | solution.py:66
  156.7 18.1 %collective-permute-start.39 = (bf16[208,896]{1,0:T(8,128)(2,1)S(1)}, bf16[208,896]{1,0:T(8,128)(2,1)S(1)}, u32[]{:S(2)}, u32[]{:S(2)}) collective-permute-start(bf16[208,896]{1,0:T(8,128)(2,1)S(1)} %constant_dynamic-update-slice_fusion.4.refs_4_), channel_id=1, source_target_pairs={{0,4},{1,5},{2,6},{3,7},{4,0},{5,1},{6,2},{7,3},{8,12},{9,13},{10,... | collective-permute-start | bytes 1118216 | tf_op jit(solution)/shard_map/ppermute | solution.py:66
  180.7 3.8 %collective-permute-start.40 = (f32[416,768]{1,0:T(8,128)S(1)}, f32[416,768]{1,0:T(8,128)S(1)}, u32[]{:S(2)}, u32[]{:S(2)}) collective-permute-start(f32[416,768]{1,0:T(8,128)S(1)} %get-tuple-element.84), channel_id=1, source_target_pairs={{0,8},{1,9},{2,10},{3,11},{4,12},{5,13},{6,14},{7,15},{8,0},{9,1},... | collective-permute-start | bytes 3833864 | tf_op jit(solution)/shard_map/ppermute | solution.py:66
  184.7 8.6 %collective-permute-start.43 = (bf16[104,768]{1,0:T(8,128)(2,1)S(1)}, bf16[104,768]{1,0:T(8,128)(2,1)S(1)}, u32[]{:S(2)}, u32[]{:S(2)}) collective-permute-start(bf16[104,768]{1,0:T(8,128)(2,1)S(1)} %get-tuple-element.88), channel_id=1, source_target_pairs={{0,64},{1,65},{2,66},{3,67},{4,68},{5,69},{6,70},{7,71},{8,72},{9,... | collective-permute-start | bytes 479240 | tf_op jit(solution)/shard_map/ppermute | solution.py:66
  189.1 7.6 %collective-permute-start.42 = (bf16[104,768]{1,0:T(8,128)(2,1)S(1)}, bf16[104,768]{1,0:T(8,128)(2,1)S(1)}, u32[]{:S(2)}, u32[]{:S(2)}) collective-permute-start(bf16[104,768]{1,0:T(8,128)(2,1)S(1)} %get-tuple-element.87), channel_id=1, source_target_pairs={{0,96},{1,97},{2,98},{3,99},{4,100},{5,101},{6,102},{7,103},{8,40}... | collective-permute-start | bytes 479240 | tf_op jit(solution)/shard_map/ppermute | solution.py:66
  189.6 7.3 %collective-permute-start.41 = (bf16[104,768]{1,0:T(8,128)(2,1)S(1)}, bf16[104,768]{1,0:T(8,128)(2,1)S(1)}, u32[]{:S(2)}, u32[]{:S(2)}) collective-permute-start(bf16[104,768]{1,0:T(8,128)(2,1)S(1)} %get-tuple-element.86), channel_id=1, source_target_pairs={{0,32},{1,33},{2,34},{3,35},{4,36},{5,37},{6,38},{7,39},{8,104},{9... | collective-permute-start | bytes 479240 | tf_op jit(solution)/shard_map/ppermute | solution.py:66
  197.0 11.6 %collective-permute-start.44 = (f32[104,768]{1,0:T(8,128)S(1)}, f32[104,768]{1,0:T(8,128)S(1)}, u32[]{:S(2)}, u32[]{:S(2)}) collective-permute-start(f32[104,768]{1,0:T(8,128)S(1)} %add_add_fusion), channel_id=1, source_target_pairs={{0,16},{1,17},{2,18},{3,19},{4,20},{5,21},{6,22},{7,23},{8,24},{9,... | collective-permute-start | bytes 958472 | tf_op jit(solution)/shard_map/ppermute | solution.py:66
  208.7 4.5 %collective-permute-start.45 = (bf16[104,768]{1,0:T(8,128)(2,1)S(1)}, bf16[104,768]{1,0:T(8,128)(2,1)S(1)}, u32[]{:S(2)}, u32[]{:S(2)}) collective-permute-start(bf16[104,768]{1,0:T(8,128)(2,1)S(1)} %get-tuple-element.90), channel_id=1, source_target_pairs={{0,32},{1,33},{2,34},{3,35},{4,36},{5,37},{6,38},{7,39},{8,104},{9... | collective-permute-start | bytes 479240 | tf_op jit(solution)/shard_map/ppermute | solution.py:66
  210.5 10.2 %collective-permute-start.46 = (bf16[104,768]{1,0:T(8,128)(2,1)S(1)}, bf16[104,768]{1,0:T(8,128)(2,1)S(1)}, u32[]{:S(2)}, u32[]{:S(2)}) collective-permute-start(bf16[104,768]{1,0:T(8,128)(2,1)S(1)} %get-tuple-element.90), channel_id=1, source_target_pairs={{0,96},{1,97},{2,98},{3,99},{4,100},{5,101},{6,102},{7,103},{8,40}... | collective-permute-start | bytes 479240 | tf_op jit(solution)/shard_map/ppermute | solution.py:66
  210.5 10.3 %collective-permute-start.47 = (bf16[104,768]{1,0:T(8,128)(2,1)S(1)}, bf16[104,768]{1,0:T(8,128)(2,1)S(1)}, u32[]{:S(2)}, u32[]{:S(2)}) collective-permute-start(bf16[104,768]{1,0:T(8,128)(2,1)S(1)} %get-tuple-element.90), channel_id=1, source_target_pairs={{0,64},{1,65},{2,66},{3,67},{4,68},{5,69},{6,70},{7,71},{8,72},{9,... | collective-permute-start | bytes 479240 | tf_op jit(solution)/shard_map/ppermute | solution.py:66
  220.8 2.2 collective-permute-start.48

commit v7 on v6

--- a/solution.py
+++ b/solution.py
@@ -22,6 +22,7 @@
 STEP = 4
 UNROLL = 3
 MAIN = 32
+PARTS = 24
 bf16, f32 = jnp.bfloat16, jnp.float32
 
 
@@ -83,58 +84,75 @@
     return aux % CORE, row, row // ZL, row % ZL
 
 
-def slab_kernel(main0, main1, rest, out, sems):
-    core, row, _, _ = here()
+def place_parts(main0, main1, rest, at_two, at_z, held, sems):
+    core = here()[0]
     copies = []
-    for x in range(X):
-        a = jnp.where(core == 0, x, row // ZL)
-        b = jnp.where(core == 0, row // ZL, x)
+    for a in range(4):
+        y, x = jnp.where(core == 0, at_two, a), jnp.where(core == 0, a, at_two)
         for c, main in enumerate((main0, main1)):
-            copies.append(
-                pltpu.make_async_copy(main.at[b, row % ZL, :, a], out.at[c, x, :, pl.ds(0, MAIN)], sems.at[3 * x + c])
-            )
-        copies.append(
-            pltpu.make_async_copy(
-                rest.at[row % ZL, :, :, a, b], out.at[:, x, :, pl.ds(MAIN, OWN - MAIN)], sems.at[3 * x + 2]
-            )
-        )
+            copies.append((main.at[:, :, a], held.at[y, :, c, x, :, pl.ds(0, MAIN)]))
+        for b in range(4):
+            y, x = jnp.where(core == 0, b, a), jnp.where(core == 0, a, b)
+            into = held.at[y, at_z // ZL, :, x, at_z % ZL, pl.ds(MAIN, OWN - MAIN)]
+            copies.append((rest.at[:, a, b], into))
+    return [pltpu.make_async_copy(*copy, sems.at[i]) for i, copy in enumerate(copies)]
+
+
+def positions():
+    aux = lax.axis_index("aux")
+    core, _, x, zl = here()
+    y, z = aux // (ZH * CORE), aux // CORE % ZH * ZL + zl
+    return jnp.where(core == 0, y, x), z, 1 - 2 * core
+
+
+def near_kernel(*refs):
+    parts, held, sems = refs[:9], refs[9], refs[10]
+    at_two, z, sign = positions()
+    copies = []
+    for k, (two, along) in enumerate(((0, 0), (3, 4 - sign), (1, 4 + sign))):
+        where = ((at_two + two) % 4, (z + along) % 4)
+        copies += place_parts(*parts[3 * k : 3 * k + 3], *where, held, sems.at[k])
     for copy in copies:
         copy.start()
     for copy in copies:
         copy.wait()
 
 
-def own_slab(main0, main1, rest):
+def far_kernel(main0, main1, rest, near, held, slab, sems):
+    at_two, z, _ = positions()
+    row = here()[1]
+    copies = place_parts(main0, main1, rest, (at_two + 2) % 4, (z + 2) % 4, held, sems)
+    for copy in copies:
+        copy.start()
+    for copy in copies:
+        copy.wait()
+    copy = pltpu.make_async_copy(held.at[row // ZL, row % ZL], slab, sems.at[PARTS])
+    copy.start()
+    copy.wait()
+
+
+def panels_and_slab(near, far):
+    anywhere = pl.BlockSpec(memory_space=pl.ANY)
+    held = jax.ShapeDtypeStruct((Y, ZH, CORE, X, ZL, OWN, WIDE), bf16)
+    panels = pl.pallas_call(
+        near_kernel,
+        out_shape=held,
+        in_specs=[anywhere] * 9,
+        out_specs=anywhere,
+        scratch_shapes=[pltpu.SemaphoreType.DMA((3, PARTS))],
+        compiler_params=pltpu.CompilerParams(vmem_limit_bytes=4 * 1024 * 1024),
+        name="near",
+    )(*near)
     return pl.pallas_call(
-        slab_kernel,
-        out_shape=jax.ShapeDtypeStruct((CORE, X, ZL, OWN, WIDE), bf16),
-        in_specs=[pl.BlockSpec(memory_space=pl.ANY)] * 3,
-        out_specs=pl.BlockSpec(memory_space=pltpu.VMEM),
-        scratch_shapes=[pltpu.SemaphoreType.DMA((3 * X,))],
+        far_kernel,
+        out_shape=[held, jax.ShapeDtypeStruct((CORE, X, ZL, OWN, WIDE), bf16)],
+        in_specs=[anywhere] * 4,
+        out_specs=[anywhere] * 2,
+        input_output_aliases={3: 0},
+        scratch_shapes=[pltpu.SemaphoreType.DMA((PARTS + 1,))],
         compiler_params=pltpu.CompilerParams(vmem_limit_bytes=4 * 1024 * 1024),
-        name="slab",
-    )(main0, main1, rest)
-
-
-def assemble(main0, main1, rest, held, sems):
-    core = here()[0]
-    copies = []
-    for a in range(4):
-        for b in range(4):
-            y, x = jnp.where(core == 0, b, a), jnp.where(core == 0, a, b)
-            i = 3 * (4 * a + b)
-            for c, main in enumerate((main0, main1)):
-                copies.append(
-                    pltpu.make_async_copy(
-                        main.at[b, :, :, a], held.at[y, :, c, x, :, pl.ds(0, MAIN)], sems.at[i + c]
-                    )
-                )
-            copies.append(
-                pltpu.make_async_copy(
-                    rest.at[:, :, :, a, b], held.at[y, :, :, x, :, pl.ds(MAIN, OWN - MAIN)], sems.at[i + 2]
-                )
-            )
-    return copies
+        name="far",
+    )(*far, panels)
 
 
 def list_steps(q, meta, order, counts, steps):
@@ -179,21 +197,9 @@
     return many
 
 
-def multiply_kernel(q, meta, factors, *refs):
-    if q == 1:
-        *parts, out, held, blocks, total, order, counts, steps, sems = refs
-        copies = assemble(*parts, held, sems)
-    else:
-        held, out, blocks, total, order, counts, steps, sems = refs
-        copies = []
-    copies.append(pltpu.make_async_copy(factors, blocks.at[pl.ds(0, SLOTS)], sems.at[48]))
-    for copy in copies:
-        copy.start()
-    blocks[SLOTS] = jnp.zeros((BLK, BLK), bf16)
+def multiply_kernel(q, meta, factors, held, out, total, order, counts, steps):
     total[...] = jnp.zeros_like(total)
     many = list_steps(q, meta, order, counts, steps)
-    for copy in copies:
-        copy.wait()
     panels = held.reshape(NB, WIDE)
 
     def some(i, carry):
@@ -201,7 +207,9 @@
         for u in range(UNROLL):
             left, right = [], []
             for k in range(STEP):
-                left.append(blocks[steps[i * UNROLL + u, 1 + k]])
+                slot = steps[i * UNROLL + u, 1 + k]
+                block = factors[jnp.minimum(slot, SLOTS - 1)]
+                left.append(jnp.where(slot < SLOTS, block, jnp.zeros_like(block)))
                 column = steps[i * UNROLL + u, 1 + STEP + k]
                 right.append(panels[pl.ds(pl.multiple_of(column * BLK, BLK), BLK), :])
             products.append(
@@ -216,32 +224,28 @@
         out[group * BLK : (group + 1) * BLK, :] = total[group].astype(bf16)
 
 
-def multiply(q, meta, factors, *panels):
+def multiply(q, meta, factors, panels):
     most = SLOTS // STEP + ROW_BLOCKS + UNROLL
-    half = jax.ShapeDtypeStruct((ROWS, WIDE), bf16)
-    held = jax.ShapeDtypeStruct((Y, ZH, CORE, X, ZL, OWN, WIDE), bf16)
-    vmem, anywhere = pl.BlockSpec(memory_space=pltpu.VMEM), pl.BlockSpec(memory_space=pl.ANY)
+    vmem = pl.BlockSpec(memory_space=pltpu.VMEM)
 
     def kernel(*refs):
         multiply_kernel(q, *refs)
 
     return pl.pallas_call(
         kernel,
-        out_shape=[half, held] if q == 1 else half,
-        in_specs=[pl.BlockSpec(memory_space=pltpu.SMEM), anywhere] + ([anywhere] * 3 if q == 1 else [vmem]),
-        out_specs=[vmem, vmem] if q == 1 else vmem,
+        out_shape=jax.ShapeDtypeStruct((ROWS, WIDE), bf16),
+        in_specs=[pl.BlockSpec(memory_space=pltpu.SMEM), vmem, vmem],
+        out_specs=vmem,
         scratch_shapes=[
-            pltpu.VMEM((SLOTS + 1, BLK, BLK), bf16),
             pltpu.VMEM((ROW_BLOCKS + 1, BLK, WIDE), f32),
             pltpu.SMEM((ROW_BLOCKS, SLOTS + 2 * STEP), jnp.int32),
             pltpu.SMEM((ROW_BLOCKS,), jnp.int32),
             pltpu.SMEM((most, 1 + 2 * STEP), jnp.int32),
-            pltpu.SemaphoreType.DMA((49,)),
         ],
         compiler_params=pltpu.CompilerParams(vmem_limit_bytes=24 * 1024 * 1024),
         cost_estimate=pl.CostEstimate(flops=96 * 2 * 128 * 128 * 896, bytes_accessed=2**23, transcendentals=0),
         name="multiply",
-    )(meta, factors, *panels)
+    )(meta, factors, panels)
 
 
 def cross_kernel(starts, half, slab, theirs, *refs):
@@ -378,6 +382,23 @@
     )(*halves, *low_parts, *x_parts)
 
 
+def widen_kernel(own, others, out):
+    core, n = here()[0], CROSS // 2
+    out[:n, :] = jnp.where(core == 0, own[...], others[...]).astype(f32)
+    out[n:, :] = jnp.where(core == 0, others[...], own[...])[: NOCC - n].astype(f32)
+
+
+def widen(own, others):
+    return pl.pallas_call(
+        widen_kernel,
+        out_shape=jax.ShapeDtypeStruct((NOCC, ROWS), f32),
+        in_specs=[pl.BlockSpec(memory_space=pltpu.VMEM)] * 2,
+        out_specs=pl.BlockSpec(memory_space=pltpu.VMEM),
+        compiler_params=pltpu.CompilerParams(vmem_limit_bytes=16 * 1024 * 1024),
+        name="widen",
+    )(own, others)
+
+
 def local(factors, block_rows, block_cols, block_count, orbitals, response):
     aux, row = lax.axis_index("aux"), lax.axis_index("row")
     y, zh, c = aux // (ZH * CORE), (aux // CORE) % ZH, aux % CORE
@@ -459,29 +480,11 @@
     far_0 = send(ahead_0, ahead)
     far_1 = send_after(behind_1, behind, rest_ahead)
     rest_far = send_after(rest_ahead, around(zz, 1, True), rest_behind)
-    arrays = (
-        (mains[0], ahead_0, behind_0, far_0),
-        (mains[1], ahead_1, behind_1, far_1),
-    )
-    mains = []
-    for four in arrays:
-        into = jnp.zeros((4, *four[0].shape), bf16)
-        for array, at in zip(four, (at_two, (at_two - 1) % 4, (at_two + 1) % 4, (at_two + 2) % 4)):
-            into = put(into, array[None], d0=at)
-        mains.append(into)
-    into = jnp.zeros((ZH, CORE, ZL, 4, 4, OWN - MAIN, WIDE), bf16)
-    for array, at in (
-        (rest, z),
-        (rest_ahead, (z - sign) % 4),
-        (rest_behind, (z + sign) % 4),
-        (rest_far, (z + 2) % 4),
-    ):
-        into = put(into, array[None, :, None], d0=at // ZL, d2=at % ZL)
-    rest = into
-
-    slab = own_slab(*mains, rest).reshape(ROWS, WIDE)
+    near = [mains[0], mains[1], rest, ahead_0, ahead_1, rest_ahead, behind_0, behind_1, rest_behind]
+    panels, slab = panels_and_slab(near, (far_0, far_1, rest_far))
+    slab = slab.reshape(ROWS, WIDE)
     theirs = swap_cores(slab)
-    second_half, panels = multiply(1, meta, other_blocks, *mains, rest)
+    second_half = multiply(1, meta, other_blocks, panels)
 
     def add(*arrays):
         return sum(a.astype(f32) for a in arrays)
@@ -539,8 +542,7 @@
         (y + 2, send(part, opposite)),
     ):
         into = lax.dynamic_update_slice(into, array, ((k % Y) * SHARD, 0))
-    others = swap_cores(into)
-    return jnp.concatenate([choose(into, others), choose(others, into)])[:NOCC].astype(f32).T
+    return widen(into, swap_cores(into)).T
 
 
 def solution(mesh):

time: 224 us -> 223 us (level)
  waiting for transfers between devices: 116 us -> 106 us
  starting transfers between devices: 70.1 us -> 78.6 us
  Pallas kernels: 27.7 us -> 30.4 us
  local copies, waits for them, and re-layouts: 5.19 us -> 2.63 us
    ppermute x49, waiting for transfers between devices: 116 us -> 106 us  [send(): return lax.ppermute(array, AXES, pairs)]
    ppermute x49, starting transfers between devices: 70.1 us -> 78.6 us  [send(): return lax.ppermute(array, AXES, pairs)]
    pallas_call x3 -> x5, Pallas kernels: 17.1 us -> 20 us  [the longest x2 11.6 us: multiply(): pl.pallas_call(kernel, out_shape=jax.ShapeDtypeStruct((ROWS, WIDE), bf16)...]
  transfers between devices with their start and end apart: 49 -> 49, of which waited for: 33 -> 38; matrix products, arithmetic and copies ran while one was open for 2% -> 1% of each run, Pallas kernels for 8% -> 8%
where the time goes in v7:
time: 223 us; the launch traced here: 222 us
  waiting for transfers between devices  106 us (48%)
  starting transfers between devices  78.6 us (35%)
  Pallas kernels  30.4 us (14%)
  local copies, waits for them, and re-layouts  2.63 us (1%)
  other arithmetic  2.54 us (1%)
    ppermute x49, waiting for transfers between devices, send(): return lax.ppermute(array, AXES, pairs)  106 us
    ppermute x49, starting transfers between devices, send(): return lax.ppermute(array, AXES, pairs)  78.6 us
    pallas_call x2, Pallas kernels, multiply(): pl.pallas_call(kernel, out_shape=jax.ShapeDtypeStruct((ROWS, WIDE), bf16)...  11.6 us
    pallas_call x1, Pallas kernels, exchange(): pl.pallas_call(exchange_kernel, out_shape=[jax.ShapeDtypeStruct((CROSS //...  5.8 us
    pallas_call x1, Pallas kernels, panels_and_slab(): pl.pallas_call(near_kernel, out_shape=held, in_specs=[anywhere] * 9, out_...  5.02 us
  transfers between devices with their start and end apart: 49, of which 38 were waited for; matrix products, arithmetic and copies ran while one was open for 1% of the time, Pallas kernels for 8%

profile of v7, /device:TPU:1, one launch (start us, length us, event | category | flops | bytes accessed | tf_op | source)
XLA Modules:
  0.0 221.7 jit_solution(14345591596481036143)
XLA Ops:
  0.9 1.5 collective-permute-start
  4.6 1.4 collective-permute-start.1
  6.8 1.9 collective-permute-start.2
  8.7 1.3 collective-permute-start.3
  11.7 1.2 collective-permute-done.2
  12.9 1.8 collective-permute-done.3
  15.8 1.8 collective-permute-start.9
  17.5 1.2 collective-permute-start.10
  18.8 3.8 %collective-permute-start.5 = (bf16[2,4,32,896]{3,2,1,0:T(8,128)(2,1)S(1)}, bf16[2,4,32,896]{3,2,1,0:T(8,128)(2,1)S(1)}, u32[]{:S(2)}, u32[]{:S(2)}) collective-permute-start(bf16[2,4,32,896]{3,2,1,0:T(8,128)(2,1)S(1)} %slice.39), channel_id=1, source_target_pairs={{0,1},{1,16},{2,3},{3,18},{4,5},{5,20},{6,7},{7,22},{8,25},{9,8},{... | collective-permute-start | bytes 1376264 | tf_op jit(solution)/shard_map/ppermute | solution.py:67
  24.4 5.5 %collective-permute-done.5 = bf16[2,4,32,896]{3,2,1,0:T(8,128)(2,1)S(1)} collective-permute-done((bf16[2,4,32,896]{3,2,1,0:T(8,128)(2,1)S(1)}, bf16[2,4,32,896]{3,2,1,0:T(8,128)(2,1)S(1)}, u32[]{:S(2)}, u32[]{:S(2)}) %collective-permute-start.5) | collective-permute-done | bytes 458784 | tf_op jit(solution)/shard_map/ppermute | solution.py:67
  29.9 3.4 %collective-permute-start.7 = (bf16[2,4,32,896]{3,2,1,0:T(8,128)(2,1)S(1)}, bf16[2,4,32,896]{3,2,1,0:T(8,128)(2,1)S(1)}, u32[]{:S(2)}, u32[]{:S(2)}) collective-permute-start(bf16[2,4,32,896]{3,2,1,0:T(8,128)(2,1)S(1)} %collective-permute-done.5), channel_id=1, source_target_pairs={{0,1},{1,16},{2,3},{3,18},{4,5},{5,20},{6,7},{7,22},{8,25},{9,8},{... | collective-permute-start | bytes 1376264 | tf_op jit(solution)/shard_map/ppermute | solution.py:67
  33.4 3.0 %collective-permute-done.6 = bf16[2,4,32,896]{3,2,1,0:T(8,128)(2,1)S(1)} collective-permute-done((bf16[2,4,32,896]{3,2,1,0:T(8,128)(2,1)S(1)}, bf16[2,4,32,896]{3,2,1,0:T(8,128)(2,1)S(1)}, u32[]{:S(2)}, u32[]{:S(2)}) %collective-permute-start.6) | collective-permute-done | bytes 458784 | tf_op jit(solution)/shard_map/ppermute | solution.py:67
  36.4 2.3 %collective-permute-done.7 = bf16[2,4,32,896]{3,2,1,0:T(8,128)(2,1)S(1)} collective-permute-done((bf16[2,4,32,896]{3,2,1,0:T(8,128)(2,1)S(1)}, bf16[2,4,32,896]{3,2,1,0:T(8,128)(2,1)S(1)}, u32[]{:S(2)}, u32[]{:S(2)}) %collective-permute-start.7) | collective-permute-done | bytes 458784 | tf_op jit(solution)/shard_map/ppermute | solution.py:67
  40.3 3.1 %collective-permute-start.15 = (bf16[2,4,4,16,896]{4,3,2,1,0:T(8,128)(2,1)S(1)}, bf16[2,4,4,16,896]{4,3,2,1,0:T(8,128)(2,1)S(1)}, u32[]{:S(2)}, u32[]{:S(2)}) collective-permute-start(bf16[2,4,4,16,896]{4,3,2,1,0:T(8,128)(2,1)S(1)} %bitcast_dynamic-update-slice_fusion.3.refs_2_), channel_id=1, source_target_pairs={{0,1},{1,16},{2,3},{3,18},{4,5},{5,20},{6,7},{7,22},{8,25},{9,8},{... | collective-permute-start | bytes 2752520 | tf_op jit(solution)/shard_map/ppermute | solution.py:67
  43.5 8.4 %collective-permute-start.11 = (s32[1,256]{1,0:T(1,128)S(1)}, s32[1,256]{1,0:T(1,128)S(1)}, u32[]{:S(2)}, u32[]{:S(2)}) collective-permute-start(s32[1,256]{1,0:T(1,128)S(1)} %bitcast.73), channel_id=1, source_target_pairs={{0,8},{1,9},{2,10},{3,11},{4,12},{5,13},{6,14},{7,15},{8,0},{9,1},... | collective-permute-start | bytes 3080 | tf_op jit(solution)/shard_map/ppermute | solution.py:67
  55.0 6.4 %collective-permute-done.17.refs_8_ = bf16[2,4,4,16,896]{4,3,2,1,0:T(8,128)(2,1)S(1)} collective-permute-done((bf16[2,4,4,16,896]{4,3,2,1,0:T(8,128)(2,1)S(1)}, bf16[2,4,4,16,896]{4,3,2,1,0:T(8,128)(2,1)S(1)}, u32[]{:S(2)}, u32[]{:S(2)}) %collective-permute-start.17) | collective-permute-done | bytes 917536 | tf_op jit(solution)/shard_map/ppermute | solution.py:67
  61.4 2.4 %collective-permute-start.16 = (bf16[2,2,4,32,896]{4,3,2,1,0:T(8,128)(2,1)S(1)}, bf16[2,2,4,32,896]{4,3,2,1,0:T(8,128)(2,1)S(1)}, u32[]{:S(2)}, u32[]{:S(2)}) collective-permute-start(bf16[2,2,4,32,896]{4,3,2,1,0:T(8,128)(2,1)S(1)} %collective-permute-done.14.refs_7_), channel_id=1, source_target_pairs={{0,96},{1,97},{2,98},{3,99},{4,100},{5,101},{6,102},{7,103},{8,14}... | collective-permute-start | bytes 2752520 | tf_op jit(solution)/shard_map/ppermute | solution.py:67
  63.8 1.5 collective-permute-done.20.refs_6_
  65.3 2.1 collective-permute-done.19.refs_4_
  67.4 5.0 %near.1 = bf16[4,2,2,4,2,48,896]{6,5,4,3,2,1,0:T(8,128)(2,1)S(1)} custom-call(bf16[2,2,4,32,896]{4,3,2,1,0:T(8,128)(2,1)S(1)} %get-tuple-element.59.refs_0_, bf16[2,2,4,32,896]{4,3,2,1,0:T(8,128)(2,1)S(1)} %get-tuple-element.58.refs_1_, bf16[2,4,4,16,896]{4,3,2,1,0:T(8,128)(2,1)S(1)} %bitcast_dynamic-update-slice_fusion.3.refs_2_, ...), custom_call_target="tpu_custom_call" | custom-call | tf_op jit(solution)/shard_map/near/pallas_call | solution.py:137
  72.4 1.5 collective-permute-done.18.rest
  73.9 1.2 collective-permute-done.16.main1
  75.1 2.5 %collective-permute-done.13.main0 = bf16[2,2,4,32,896]{4,3,2,1,0:T(8,128)(2,1)S(1)} collective-permute-done((bf16[2,2,4,32,896]{4,3,2,1,0:T(8,128)(2,1)S(1)}, bf16[2,2,4,32,896]{4,3,2,1,0:T(8,128)(2,1)S(1)}, u32[]{:S(2)}, u32[]{:S(2)}) %collective-permute-start.13) | collective-permute-done | bytes 917536 | tf_op jit(solution)/shard_map/ppermute | solution.py:67
  77.5 1.7 far.1
  79.3 8.2 %collective-permute-start.21 = (bf16[768,896]{1,0:T(8,128)(2,1)S(1)}, bf16[768,896]{1,0:T(8,128)(2,1)S(1)}, u32[]{:S(2)}, u32[]{:S(2)}) collective-permute-start(bf16[768,896]{1,0:T(8,128)(2,1)S(1)} %bitcast.70), channel_id=1, source_target_pairs={{0,8},{1,9},{2,10},{3,11},{4,12},{5,13},{6,14},{7,15},{8,0},{9,1},... | collective-permute-start | bytes 4128776 | tf_op jit(solution)/shard_map/ppermute | solution.py:67
  87.5 7.2 %multiply.2.refs_0_.refs_1_ = bf16[768,896]{1,0:T(8,128)(2,1)S(1)} custom-call(s32[2,256]{1,0:T(2,128)S(1)} %pad_add_fusion.refs_0_, bf16[96,128,128]{2,1,0:T(8,128)(2,1)S(1)} %collective-permute-done.4.refs_1_, bf16[4,2,2,4,2,48,896]{6,5,4,3,2,1,0:T(8,128)(2,1)S(1)} %get-tuple-element.64.refs_2_), custom_call_target="tpu_custom_call" | custom-call | flops 2818572288 | bytes 8388608 | tf_op jit(solution)/shard_map/multiply/pallas_call | solution.py:234
  94.8 2.0 cross.2
  97.1 4.4 %multiply.3.refs_0_ = bf16[768,896]{1,0:T(8,128)(2,1)S(1)} custom-call(s32[2,256]{1,0:T(2,128)S(1)} %pad_add_fusion.refs_0_, bf16[96,128,128]{2,1,0:T(8,128)(2,1)S(1)} %bitcast.69, bf16[4,2,2,4,2,48,896]{6,5,4,3,2,1,0:T(8,128)(2,1)S(1)} %get-tuple-element.64.refs_2_), custom_call_target="tpu_custom_call" | custom-call | flops 2818572288 | bytes 8388608 | tf_op jit(solution)/shard_map/multiply/pallas_call | solution.py:234
  101.6 1.8 cross.3
  104.3 2.2 collective-permute-start.31
  106.5 3.6 %collective-permute-start.32 = (bf16[208,896]{1,0:T(8,128)(2,1)S(1)}, bf16[208,896]{1,0:T(8,128)(2,1)S(1)}, u32[]{:S(2)}, u32[]{:S(2)}) collective-permute-start(bf16[208,896]{1,0:T(8,128)(2,1)S(1)} %get-tuple-element.74), channel_id=1, source_target_pairs={{0,4},{1,5},{2,6},{3,7},{4,0},{5,1},{6,2},{7,3},{8,12},{9,13},{10,... | collective-permute-start | bytes 1118216 | tf_op jit(solution)/shard_map/ppermute | solution.py:67
  110.1 4.2 %collective-permute-done.22.refs_1_ = bf16[416,896]{1,0:T(8,128)(2,1)S(1)} collective-permute-done((bf16[416,896]{1,0:T(8,128)(2,1)S(1)}, bf16[416,896]{1,0:T(8,128)(2,1)S(1)}, u32[]{:S(2)}, u32[]{:S(2)}) %collective-permute-start.22) | collective-permute-done | bytes 745504 | tf_op jit(solution)/shard_map/ppermute | solution.py:67
  114.7 4.4 %collective-permute-done.31.refs_2_ = bf16[208,896]{1,0:T(8,128)(2,1)S(1)} collective-permute-done((bf16[208,896]{1,0:T(8,128)(2,1)S(1)}, bf16[208,896]{1,0:T(8,128)(2,1)S(1)}, u32[]{:S(2)}, u32[]{:S(2)}) %collective-permute-start.31) | collective-permute-done | bytes 372768 | tf_op jit(solution)/shard_map/ppermute | solution.py:67
  119.1 6.8 %collective-permute-done.32.refs_3_ = bf16[208,896]{1,0:T(8,128)(2,1)S(1)} collective-permute-done((bf16[208,896]{1,0:T(8,128)(2,1)S(1)}, bf16[208,896]{1,0:T(8,128)(2,1)S(1)}, u32[]{:S(2)}, u32[]{:S(2)}) %collective-permute-start.32) | collective-permute-done | bytes 372768 | tf_op jit(solution)/shard_map/ppermute | solution.py:67
  126.3 1.8 collective-permute-start.23
  128.4 2.8 %collective-permute-start.25 = (bf16[104,896]{1,0:T(8,128)(2,1)S(1)}, bf16[104,896]{1,0:T(8,128)(2,1)S(1)}, u32[]{:S(2)}, u32[]{:S(2)}) collective-permute-start(bf16[104,896]{1,0:T(8,128)(2,1)S(1)} %get-tuple-element.70), channel_id=1, source_target_pairs={{0,4},{1,5},{2,6},{3,7},{4,0},{5,1},{6,2},{7,3},{8,12},{9,13},{10,... | collective-permute-start | bytes 559112 | tf_op jit(solution)/shard_map/ppermute | solution.py:67
  131.8 3.8 %collective-permute-done.24 = bf16[104,896]{1,0:T(8,128)(2,1)S(1)} collective-permute-done((bf16[104,896]{1,0:T(8,128)(2,1)S(1)}, bf16[104,896]{1,0:T(8,128)(2,1)S(1)}, u32[]{:S(2)}, u32[]{:S(2)}) %collective-permute-start.24) | collective-permute-done | bytes 186400 | tf_op jit(solution)/shard_map/ppermute | solution.py:67
  135.6 3.9 %collective-permute-done.25 = bf16[104,896]{1,0:T(8,128)(2,1)S(1)} collective-permute-done((bf16[104,896]{1,0:T(8,128)(2,1)S(1)}, bf16[104,896]{1,0:T(8,128)(2,1)S(1)}, u32[]{:S(2)}, u32[]{:S(2)}) %collective-permute-start.25) | collective-permute-done | bytes 186400 | tf_op jit(solution)/shard_map/ppermute | solution.py:67
  139.8 1.3 collective-permute-start.26
  143.0 1.1 collective-permute-start.27
  145.4 3.5 %collective-permute-done.35 = bf16[104,896]{1,0:T(8,128)(2,1)S(1)} collective-permute-done((bf16[104,896]{1,0:T(8,128)(2,1)S(1)}, bf16[104,896]{1,0:T(8,128)(2,1)S(1)}, u32[]{:S(2)}, u32[]{:S(2)}) %collective-permute-start.35) | collective-permute-done | bytes 186400 | tf_op jit(solution)/shard_map/ppermute | solution.py:67
  149.0 6.9 %collective-permute-done.28 = bf16[104,896]{1,0:T(8,128)(2,1)S(1)} collective-permute-done((bf16[104,896]{1,0:T(8,128)(2,1)S(1)}, bf16[104,896]{1,0:T(8,128)(2,1)S(1)}, u32[]{:S(2)}, u32[]{:S(2)}) %collective-permute-start.28) | collective-permute-done | bytes 186400 | tf_op jit(solution)/shard_map/ppermute | solution.py:67
  156.6 1.4 collective-permute-start.38
  158.5 7.0 %collective-permute-done.37.refs_5_ = bf16[208,896]{1,0:T(8,128)(2,1)S(1)} collective-permute-done((bf16[208,896]{1,0:T(8,128)(2,1)S(1)}, bf16[208,896]{1,0:T(8,128)(2,1)S(1)}, u32[]{:S(2)}, u32[]{:S(2)}) %collective-permute-start.37) | collective-permute-done | bytes 372768 | tf_op jit(solution)/shard_map/ppermute | solution.py:67
  165.5 2.7 %collective-permute-done.38.refs_6_ = bf16[208,896]{1,0:T(8,128)(2,1)S(1)} collective-permute-done((bf16[208,896]{1,0:T(8,128)(2,1)S(1)}, bf16[208,896]{1,0:T(8,128)(2,1)S(1)}, u32[]{:S(2)}, u32[]{:S(2)}) %collective-permute-start.38) | collective-permute-done | bytes 372768 | tf_op jit(solution)/shard_map/ppermute | solution.py:67
  168.2 6.1 %collective-permute-done.39.refs_7_ = bf16[208,896]{1,0:T(8,128)(2,1)S(1)} collective-permute-done((bf16[208,896]{1,0:T(8,128)(2,1)S(1)}, bf16[208,896]{1,0:T(8,128)(2,1)S(1)}, u32[]{:S(2)}, u32[]{:S(2)}) %collective-permute-start.39) | collective-permute-done | bytes 372768 | tf_op jit(solution)/shard_map/ppermute | solution.py:67
  174.3 5.8 %exchange.1 = (f32[416,768]{1,0:T(8,128)S(1)}, f32[416,768]{1,0:T(8,128)S(1)}) custom-call(bf16[768,896]{1,0:T(8,128)(2,1)} %copy-done.2, bf16[768,896]{1,0:T(8,128)(2,1)} %copy-done.1, bf16[416,896]{1,0:T(8,128)(2,1)S(1)} %constant_dynamic-update-slice_fusion.6.refs_2_, bf16[416,896]{1,0:T(8,128)(2,1)S(1)} %collective-permute-done.36.refs_3_, ...), custom_call_target="tpu_custom_call" | custom-call | flops 2466250752 | bytes 8388608 | tf_op jit(solution)/shard_map/exchange/pallas_call | solution.py:368
  180.1 2.6 %collective-permute-start.40 = (f32[416,768]{1,0:T(8,128)S(1)}, f32[416,768]{1,0:T(8,128)S(1)}, u32[]{:S(2)}, u32[]{:S(2)}) collective-permute-start(f32[416,768]{1,0:T(8,128)S(1)} %get-tuple-element.84), channel_id=1, source_target_pairs={{0,8},{1,9},{2,10},{3,11},{4,12},{5,13},{6,14},{7,15},{8,0},{9,1},... | collective-permute-start | bytes 3833864 | tf_op jit(solution)/shard_map/ppermute | solution.py:67
  182.8 2.6 %collective-permute-done.40.refs_1_ = f32[416,768]{1,0:T(8,128)S(1)} collective-permute-done((f32[416,768]{1,0:T(8,128)S(1)}, f32[416,768]{1,0:T(8,128)S(1)}, u32[]{:S(2)}, u32[]{:S(2)}) %collective-permute-start.40) | collective-permute-done | bytes 1277984 | tf_op jit(solution)/shard_map/ppermute | solution.py:67
  185.6 2.2 collective-permute-start.42
  187.8 1.7 collective-permute-start.43
  189.5 1.2 collective-permute-done.41
  190.7 1.6 collective-permute-done.42
  192.3 2.2 collective-permute-done.43
  194.6 5.1 %collective-permute-start.44 = (f32[104,768]{1,0:T(8,128)S(1)}, f32[104,768]{1,0:T(8,128)S(1)}, u32[]{:S(2)}, u32[]{:S(2)}) collective-permute-start(f32[104,768]{1,0:T(8,128)S(1)} %add_add_fusion), channel_id=1, source_target_pairs={{0,16},{1,17},{2,18},{3,19},{4,20},{5,21},{6,22},{7,23},{8,24},{9,... | collective-permute-start | bytes 958472 | tf_op jit(solution)/shard_map/ppermute | solution.py:67
  199.7 6.8 %collective-permute-done.44 = f32[104,768]{1,0:T(8,128)S(1)} collective-permute-done((f32[104,768]{1,0:T(8,128)S(1)}, f32[104,768]{1,0:T(8,128)S(1)}, u32[]{:S(2)}, u32[]{:S(2)}) %collective-permute-start.44) | collective-permute-done | bytes 319520 | tf_op jit(solution)/shard_map/ppermute | solution.py:67
  206.6 1.5 collective-permute-start.46
  208.1 1.3 collective-permute-start.47
  209.4 1.3 collective-permute-done.45
  210.7 1.3 collective-permute-done.46
  212.0 3.6 %collective-permute-done.47 = bf16[104,768]{1,0:T(8,128)(2,1)S(1)} collective-permute-done((bf16[104,768]{1,0:T(8,128)(2,1)S(1)}, bf16[104,768]{1,0:T(8,128)(2,1)S(1)}, u32[]{:S(2)}, u32[]{:S(2)}) %collective-permute-start.47) | collective-permute-done | bytes 159776 | tf_op jit(solution)/shard_map/ppermute | solution.py:67
  215.6 2.8 %collective-permute-start.48 = (bf16[416,768]{1,0:T(8,128)(2,1)S(1)}, bf16[416,768]{1,0:T(8,128)(2,1)S(1)}, u32[]{:S(2)}, u32[]{:S(2)}) collective-permute-start(bf16[416,768]{1,0:T(8,128)(2,1)S(1)} %constant_dynamic-update-slice_fusion.own), channel_id=1, source_target_pairs={{0,8},{1,9},{2,10},{3,11},{4,12},{5,13},{6,14},{7,15},{8,0},{9,1},... | collective-permute-start | bytes 1916936 | tf_op jit(solution)/shard_map/ppermute | solution.py:67
  218.4 1.7 collective-permute-done.48.others
  220.1 1.6 widen.1
  (98 shorter events, 21.0 us)
Async XLA Ops:
  0.9 2.4 %collective-permute-start = (bf16[48,800]{1,0:T(8,128)(2,1)S(1)}, bf16[48,800]{1,0:T(8,128)(2,1)S(1)}, u32[]{:S(2)}, u32[]{:S(2)}) collective-permute-start(bf16[48,800]{1,0:T(8,128)(2,1)S(1)} %broadcast_select_fusion.2), channel_id=1, source_target_pairs={{0,8},{1,9},{2,10},{3,11},{4,12},{5,13},{6,14},{7,15},{8,0},{9,1},... | collective-permute-start | bytes 230408 | tf_op jit(solution)/shard_map/ppermute | solution.py:67
  3.3 11.4 %collective-permute-start.4 = (bf16[96,128,128]{2,1,0:T(8,128)(2,1)}, bf16[96,128,128]{2,1,0:T(8,128)(2,1)S(1)}, u32[]{:S(2)}, u32[]{:S(2)}) collective-permute-start(bf16[96,128,128]{2,1,0:T(8,128)(2,1)} %bitcast.68), channel_id=1, source_target_pairs={{0,8},{1,9},{2,10},{3,11},{4,12},{5,13},{6,14},{7,15},{8,0},{9,1},... | collective-permute-start | bytes 9437192 | tf_op jit(solution)/shard_map/ppermute | solution.py:67
  4.6 6.1 %collective-permute-start.1 = (bf16[2,48,896]{2,1,0:T(8,128)(2,1)S(1)}, bf16[2,48,896]{2,1,0:T(8,128)(2,1)}, u32[]{:S(2)}, u32[]{:S(2)}) collective-permute-start(bf16[2,48,896]{2,1,0:T(8,128)(2,1)S(1)} %fusion.10), channel_id=1, source_target_pairs={{0,2},{1,3},{2,4},{3,5},{4,6},{5,7},{6,0},{7,1},{8,40},{9,41},{10,... | collective-permute-start | bytes 516104 | tf_op jit(solution)/shard_map/ppermute | solution.py:67
  6.8 6.1 %collective-permute-start.2 = (bf16[2,48,896]{2,1,0:T(8,128)(2,1)S(1)}, bf16[2,48,896]{2,1,0:T(8,128)(2,1)S(1)}, u32[]{:S(2)}, u32[]{:S(2)}) collective-permute-start(bf16[2,48,896]{2,1,0:T(8,128)(2,1)S(1)} %fusion.10), channel_id=1, source_target_pairs={{0,6},{1,7},{2,0},{3,1},{4,2},{5,3},{6,4},{7,5},{8,104},{9,105},{1... | collective-permute-start | bytes 516104 | tf_op jit(solution)/shard_map/ppermute | solution.py:67
  8.7 6.1 %collective-permute-start.3 = (bf16[2,48,896]{2,1,0:T(8,128)(2,1)S(1)}, bf16[2,48,896]{2,1,0:T(8,128)(2,1)S(1)}, u32[]{:S(2)}, u32[]{:S(2)}) collective-permute-start(bf16[2,48,896]{2,1,0:T(8,128)(2,1)S(1)} %fusion.10), channel_id=1, source_target_pairs={{0,4},{1,5},{2,6},{3,7},{4,0},{5,1},{6,2},{7,3},{8,72},{9,73},{10,... | collective-permute-start | bytes 516104 | tf_op jit(solution)/shard_map/ppermute | solution.py:67
  14.8 8.3 %collective-permute-start.8 = (bf16[2,4,16,896]{3,2,1,0:T(8,128)(2,1)S(1)}, bf16[2,4,16,896]{3,2,1,0:T(8,128)(2,1)S(1)}, u32[]{:S(2)}, u32[]{:S(2)}) collective-permute-start(bf16[2,4,16,896]{3,2,1,0:T(8,128)(2,1)S(1)} %slice.47), channel_id=1, source_target_pairs={{0,32},{1,33},{2,34},{3,35},{4,36},{5,37},{6,38},{7,39},{8,10},{9,... | collective-permute-start | bytes 688136 | tf_op jit(solution)/shard_map/ppermute | solution.py:67
  15.8 7.8 %collective-permute-start.9 = (bf16[2,4,16,896]{3,2,1,0:T(8,128)(2,1)S(1)}, bf16[2,4,16,896]{3,2,1,0:T(8,128)(2,1)S(1)}, u32[]{:S(2)}, u32[]{:S(2)}) collective-permute-start(bf16[2,4,16,896]{3,2,1,0:T(8,128)(2,1)S(1)} %slice.47), channel_id=1, source_target_pairs={{0,96},{1,97},{2,98},{3,99},{4,100},{5,101},{6,102},{7,103},{8,14}... | collective-permute-start | bytes 688136 | tf_op jit(solution)/shard_map/ppermute | solution.py:67
  17.5 6.8 %collective-permute-start.10 = (bf16[2,4,16,896]{3,2,1,0:T(8,128)(2,1)S(1)}, bf16[2,4,16,896]{3,2,1,0:T(8,128)(2,1)S(1)}, u32[]{:S(2)}, u32[]{:S(2)}) collective-permute-start(bf16[2,4,16,896]{3,2,1,0:T(8,128)(2,1)S(1)} %slice.47), channel_id=1, source_target_pairs={{0,64},{1,65},{2,66},{3,67},{4,68},{5,69},{6,70},{7,71},{8,12},{9,... | collective-permute-start | bytes 688136 | tf_op jit(solution)/shard_map/ppermute | solution.py:67
  18.8 11.1 %collective-permute-start.5 = (bf16[2,4,32,896]{3,2,1,0:T(8,128)(2,1)S(1)}, bf16[2,4,32,896]{3,2,1,0:T(8,128)(2,1)S(1)}, u32[]{:S(2)}, u32[]{:S(2)}) collective-permute-start(bf16[2,4,32,896]{3,2,1,0:T(8,128)(2,1)S(1)} %slice.39), channel_id=1, source_target_pairs={{0,1},{1,16},{2,3},{3,18},{4,5},{5,20},{6,7},{7,22},{8,25},{9,8},{... | collective-permute-start | bytes 1376264 | tf_op jit(solution)/shard_map/ppermute | solution.py:67
  22.6 13.7 %collective-permute-start.6 = (bf16[2,4,32,896]{3,2,1,0:T(8,128)(2,1)S(1)}, bf16[2,4,32,896]{3,2,1,0:T(8,128)(2,1)S(1)}, u32[]{:S(2)}, u32[]{:S(2)}) collective-permute-start(bf16[2,4,32,896]{3,2,1,0:T(8,128)(2,1)S(1)} %slice.39), channel_id=1, source_target_pairs={{0,17},{1,0},{2,19},{3,2},{4,21},{5,4},{6,23},{7,6},{8,9},{9,24},{... | collective-permute-start | bytes 1376264 | tf_op jit(solution)/shard_map/ppermute | solution.py:67
  22.8 0.7 copy-start.4
  22.8 0.7 copy-start.3
  29.9 8.8 %collective-permute-start.7 = (bf16[2,4,32,896]{3,2,1,0:T(8,128)(2,1)S(1)}, bf16[2,4,32,896]{3,2,1,0:T(8,128)(2,1)S(1)}, u32[]{:S(2)}, u32[]{:S(2)}) collective-permute-start(bf16[2,4,32,896]{3,2,1,0:T(8,128)(2,1)S(1)} %collective-permute-done.5), channel_id=1, source_target_pairs={{0,1},{1,16},{2,3},{3,18},{4,5},{5,20},{6,7},{7,22},{8,25},{9,8},{... | collective-permute-start | bytes 1376264 | tf_op jit(solution)/shard_map/ppermute | solution.py:67
  38.8 13.8 %collective-permute-start.14 = (bf16[2,2,4,32,896]{4,3,2,1,0:T(8,128)(2,1)S(1)}, bf16[2,2,4,32,896]{4,3,2,1,0:T(8,128)(2,1)S(1)}, u32[]{:S(2)}, u32[]{:S(2)}) collective-permute-start(bf16[2,2,4,32,896]{4,3,2,1,0:T(8,128)(2,1)S(1)} %get-tuple-element.58.refs_1_), channel_id=1, source_target_pairs={{0,96},{1,97},{2,98},{3,99},{4,100},{5,101},{6,102},{7,103},{8,14}... | collective-permute-start | bytes 2752520 | tf_op jit(solution)/shard_map/ppermute | solution.py:67
  39.3 14.3 %collective-permute-start.12 = (bf16[2,2,4,32,896]{4,3,2,1,0:T(8,128)(2,1)S(1)}, bf16[2,2,4,32,896]{4,3,2,1,0:T(8,128)(2,1)S(1)}, u32[]{:S(2)}, u32[]{:S(2)}) collective-permute-start(bf16[2,2,4,32,896]{4,3,2,1,0:T(8,128)(2,1)S(1)} %get-tuple-element.59.refs_0_), channel_id=1, source_target_pairs={{0,32},{1,33},{2,34},{3,35},{4,36},{5,37},{6,38},{7,39},{8,10},{9,... | collective-permute-start | bytes 2752520 | tf_op jit(solution)/shard_map/ppermute | solution.py:67
  40.3 14.7 %collective-permute-start.15 = (bf16[2,4,4,16,896]{4,3,2,1,0:T(8,128)(2,1)S(1)}, bf16[2,4,4,16,896]{4,3,2,1,0:T(8,128)(2,1)S(1)}, u32[]{:S(2)}, u32[]{:S(2)}) collective-permute-start(bf16[2,4,4,16,896]{4,3,2,1,0:T(8,128)(2,1)S(1)} %bitcast_dynamic-update-slice_fusion.3.refs_2_), channel_id=1, source_target_pairs={{0,1},{1,16},{2,3},{3,18},{4,5},{5,20},{6,7},{7,22},{8,25},{9,8},{... | collective-permute-start | bytes 2752520 | tf_op jit(solution)/shard_map/ppermute | solution.py:67
  43.5 17.9 %collective-permute-start.17 = (bf16[2,4,4,16,896]{4,3,2,1,0:T(8,128)(2,1)S(1)}, bf16[2,4,4,16,896]{4,3,2,1,0:T(8,128)(2,1)S(1)}, u32[]{:S(2)}, u32[]{:S(2)}) collective-permute-start(bf16[2,4,4,16,896]{4,3,2,1,0:T(8,128)(2,1)S(1)} %bitcast_dynamic-update-slice_fusion.3.refs_2_), channel_id=1, source_target_pairs={{0,17},{1,0},{2,19},{3,2},{4,21},{5,4},{6,23},{7,6},{8,9},{9,24},{... | collective-permute-start | bytes 2752520 | tf_op jit(solution)/shard_map/ppermute | solution.py:67
  43.5 9.2 %collective-permute-start.11 = (s32[1,256]{1,0:T(1,128)S(1)}, s32[1,256]{1,0:T(1,128)S(1)}, u32[]{:S(2)}, u32[]{:S(2)}) collective-permute-start(s32[1,256]{1,0:T(1,128)S(1)} %bitcast.73), channel_id=1, source_target_pairs={{0,8},{1,9},{2,10},{3,11},{4,12},{5,13},{6,14},{7,15},{8,0},{9,1},... | collective-permute-start | bytes 3080 | tf_op jit(solution)/shard_map/ppermute | solution.py:67
  52.6 12.6 %collective-permute-start.20 = (bf16[2,2,4,32,896]{4,3,2,1,0:T(8,128)(2,1)S(1)}, bf16[2,2,4,32,896]{4,3,2,1,0:T(8,128)(2,1)S(1)}, u32[]{:S(2)}, u32[]{:S(2)}) collective-permute-start(bf16[2,2,4,32,896]{4,3,2,1,0:T(8,128)(2,1)S(1)} %get-tuple-element.59.refs_0_), channel_id=1, source_target_pairs={{0,96},{1,97},{2,98},{3,99},{4,100},{5,101},{6,102},{7,103},{8,14}... | collective-permute-start | bytes 2752520 | tf_op jit(solution)/shard_map/ppermute | solution.py:67
  53.6 13.8 %collective-permute-start.19 = (bf16[2,2,4,32,896]{4,3,2,1,0:T(8,128)(2,1)S(1)}, bf16[2,2,4,32,896]{4,3,2,1,0:T(8,128)(2,1)S(1)}, u32[]{:S(2)}, u32[]{:S(2)}) collective-permute-start(bf16[2,2,4,32,896]{4,3,2,1,0:T(8,128)(2,1)S(1)} %get-tuple-element.58.refs_1_), channel_id=1, source_target_pairs={{0,32},{1,33},{2,34},{3,35},{4,36},{5,37},{6,38},{7,39},{8,10},{9,... | collective-permute-start | bytes 2752520 | tf_op jit(solution)/shard_map/ppermute | solution.py:67
  61.4 12.5 %collective-permute-start.18 = (bf16[2,4,4,16,896]{4,3,2,1,0:T(8,128)(2,1)S(1)}, bf16[2,4,4,16,896]{4,3,2,1,0:T(8,128)(2,1)S(1)}, u32[]{:S(2)}, u32[]{:S(2)}) collective-permute-start(bf16[2,4,4,16,896]{4,3,2,1,0:T(8,128)(2,1)S(1)} %collective-permute-done.15.refs_5_), channel_id=1, source_target_pairs={{0,1},{1,16},{2,3},{3,18},{4,5},{5,20},{6,7},{7,22},{8,25},{9,8},{... | collective-permute-start | bytes 2752520 | tf_op jit(solution)/shard_map/ppermute | solution.py:67
  61.4 13.7 %collective-permute-start.16 = (bf16[2,2,4,32,896]{4,3,2,1,0:T(8,128)(2,1)S(1)}, bf16[2,2,4,32,896]{4,3,2,1,0:T(8,128)(2,1)S(1)}, u32[]{:S(2)}, u32[]{:S(2)}) collective-permute-start(bf16[2,2,4,32,896]{4,3,2,1,0:T(8,128)(2,1)S(1)} %collective-permute-done.14.refs_7_), channel_id=1, source_target_pairs={{0,96},{1,97},{2,98},{3,99},{4,100},{5,101},{6,102},{7,103},{8,14}... | collective-permute-start | bytes 2752520 | tf_op jit(solution)/shard_map/ppermute | solution.py:67
  63.8 13.8 %collective-permute-start.13 = (bf16[2,2,4,32,896]{4,3,2,1,0:T(8,128)(2,1)S(1)}, bf16[2,2,4,32,896]{4,3,2,1,0:T(8,128)(2,1)S(1)}, u32[]{:S(2)}, u32[]{:S(2)}) collective-permute-start(bf16[2,2,4,32,896]{4,3,2,1,0:T(8,128)(2,1)S(1)} %collective-permute-done.12.refs_3_), channel_id=1, source_target_pairs={{0,32},{1,33},{2,34},{3,35},{4,36},{5,37},{6,38},{7,39},{8,10},{9,... | collective-permute-start | bytes 2752520 | tf_op jit(solution)/shard_map/ppermute | solution.py:67
  79.3 15.5 %collective-permute-start.21 = (bf16[768,896]{1,0:T(8,128)(2,1)S(1)}, bf16[768,896]{1,0:T(8,128)(2,1)S(1)}, u32[]{:S(2)}, u32[]{:S(2)}) collective-permute-start(bf16[768,896]{1,0:T(8,128)(2,1)S(1)} %bitcast.70), channel_id=1, source_target_pairs={{0,8},{1,9},{2,10},{3,11},{4,12},{5,13},{6,14},{7,15},{8,0},{9,1},... | collective-permute-start | bytes 4128776 | tf_op jit(solution)/shard_map/ppermute | solution.py:67
  94.7 2.1 copy-start.1
  94.8 2.4 %copy-start = (bf16[1,96,128,128]{3,2,1,0:T(8,128)(2,1)S(1)}, bf16[1,96,128,128]{3,2,1,0:T(8,128)(2,1)}, u32[]{:S(2)}) copy-start(bf16[1,96,128,128]{3,2,1,0:T(8,128)(2,1)} %param.6) | copy-start | bytes 9437188
  96.8 17.5 %collective-permute-start.22 = (bf16[416,896]{1,0:T(8,128)(2,1)S(1)}, bf16[416,896]{1,0:T(8,128)(2,1)S(1)}, u32[]{:S(2)}, u32[]{:S(2)}) collective-permute-start(bf16[416,896]{1,0:T(8,128)(2,1)S(1)} %get-tuple-element.66), channel_id=1, source_target_pairs={{0,1},{1,0},{2,3},{3,2},{4,5},{5,4},{6,7},{7,6},{8,9},{9,8},{10,11... | collective-permute-start | bytes 2236424 | tf_op jit(solution)/shard_map/ppermute | solution.py:67
  101.5 1.8 copy-start.2
  103.4 11.3 %collective-permute-start.30 = (bf16[208,896]{1,0:T(8,128)(2,1)S(1)}, bf16[208,896]{1,0:T(8,128)(2,1)S(1)}, u32[]{:S(2)}, u32[]{:S(2)}) collective-permute-start(bf16[208,896]{1,0:T(8,128)(2,1)S(1)} %get-tuple-element.72), channel_id=1, source_target_pairs={{0,2},{1,3},{2,4},{3,5},{4,6},{5,7},{6,0},{7,1},{8,14},{9,15},{10,... | collective-permute-start | bytes 1118216 | tf_op jit(solution)/shard_map/ppermute | solution.py:67
  104.3 14.7 %collective-permute-start.31 = (bf16[208,896]{1,0:T(8,128)(2,1)S(1)}, bf16[208,896]{1,0:T(8,128)(2,1)S(1)}, u32[]{:S(2)}, u32[]{:S(2)}) collective-permute-start(bf16[208,896]{1,0:T(8,128)(2,1)S(1)} %get-tuple-element.73), channel_id=1, source_target_pairs={{0,6},{1,7},{2,0},{3,1},{4,2},{5,3},{6,4},{7,5},{8,10},{9,11},{10,... | collective-permute-start | bytes 1118216 | tf_op jit(solution)/shard_map/ppermute | solution.py:67
  106.5 19.3 %collective-permute-start.32 = (bf16[208,896]{1,0:T(8,128)(2,1)S(1)}, bf16[208,896]{1,0:T(8,128)(2,1)S(1)}, u32[]{:S(2)}, u32[]{:S(2)}) collective-permute-start(bf16[208,896]{1,0:T(8,128)(2,1)S(1)} %get-tuple-element.74), channel_id=1, source_target_pairs={{0,4},{1,5},{2,6},{3,7},{4,0},{5,1},{6,2},{7,3},{8,12},{9,13},{10,... | collective-permute-start | bytes 1118216 | tf_op jit(solution)/shard_map/ppermute | solution.py:67
  126.2 5.6 %collective-permute-start.33 = (bf16[104,896]{1,0:T(8,128)(2,1)S(1)}, bf16[104,896]{1,0:T(8,128)(2,1)S(1)}, u32[]{:S(2)}, u32[]{:S(2)}) collective-permute-start(bf16[104,896]{1,0:T(8,128)(2,1)S(1)} %get-tuple-element.80), channel_id=1, source_target_pairs={{0,1},{1,0},{2,3},{3,2},{4,5},{5,4},{6,7},{7,6},{8,9},{9,8},{10,11... | collective-permute-start | bytes 559112 | tf_op jit(solution)/shard_map/ppermute | solution.py:67
  126.3 5.5 %collective-permute-start.23 = (bf16[104,896]{1,0:T(8,128)(2,1)S(1)}, bf16[104,896]{1,0:T(8,128)(2,1)S(1)}, u32[]{:S(2)}, u32[]{:S(2)}) collective-permute-start(bf16[104,896]{1,0:T(8,128)(2,1)S(1)} %get-tuple-element.68), channel_id=1, source_target_pairs={{0,2},{1,3},{2,4},{3,5},{4,6},{5,7},{6,0},{7,1},{8,14},{9,15},{10,... | collective-permute-start | bytes 559112 | tf_op jit(solution)/shard_map/ppermute | solution.py:67
  128.1 7.5 %collective-permute-start.24 = (bf16[104,896]{1,0:T(8,128)(2,1)S(1)}, bf16[104,896]{1,0:T(8,128)(2,1)S(1)}, u32[]{:S(2)}, u32[]{:S(2)}) collective-permute-start(bf16[104,896]{1,0:T(8,128)(2,1)S(1)} %get-tuple-element.69), channel_id=1, source_target_pairs={{0,6},{1,7},{2,0},{3,1},{4,2},{5,3},{6,4},{7,5},{8,10},{9,11},{10,... | collective-permute-start | bytes 559112 | tf_op jit(solution)/shard_map/ppermute | solution.py:67
  128.4 11.2 %collective-permute-start.25 = (bf16[104,896]{1,0:T(8,128)(2,1)S(1)}, bf16[104,896]{1,0:T(8,128)(2,1)S(1)}, u32[]{:S(2)}, u32[]{:S(2)}) collective-permute-start(bf16[104,896]{1,0:T(8,128)(2,1)S(1)} %get-tuple-element.70), channel_id=1, source_target_pairs={{0,4},{1,5},{2,6},{3,7},{4,0},{5,1},{6,2},{7,3},{8,12},{9,13},{10,... | collective-permute-start | bytes 559112 | tf_op jit(solution)/shard_map/ppermute | solution.py:67
  139.8 2.3 %collective-permute-start.26 = (bf16[104,896]{1,0:T(8,128)(2,1)S(1)}, bf16[104,896]{1,0:T(8,128)(2,1)S(1)}, u32[]{:S(2)}, u32[]{:S(2)}) collective-permute-start(bf16[104,896]{1,0:T(8,128)(2,1)S(1)} %get-tuple-element.106), channel_id=1, source_target_pairs={{0,8},{1,9},{2,10},{3,11},{4,12},{5,13},{6,14},{7,15},{8,0},{9,1},... | collective-permute-start | bytes 559112 | tf_op jit(solution)/shard_map/ppermute | solution.py:67
  141.1 1.4 collective-permute-start.34
  142.8 6.1 %collective-permute-start.35 = (bf16[104,896]{1,0:T(8,128)(2,1)S(1)}, bf16[104,896]{1,0:T(8,128)(2,1)S(1)}, u32[]{:S(2)}, u32[]{:S(2)}) collective-permute-start(bf16[104,896]{1,0:T(8,128)(2,1)S(1)} %get-tuple-element.92), channel_id=1, source_target_pairs={{0,1},{1,0},{2,3},{3,2},{4,5},{5,4},{6,7},{7,6},{8,9},{9,8},{10,11... | collective-permute-start | bytes 559112 | tf_op jit(solution)/shard_map/ppermute | solution.py:67
  143.0 5.9 %collective-permute-start.27 = (bf16[104,896]{1,0:T(8,128)(2,1)S(1)}, bf16[104,896]{1,0:T(8,128)(2,1)S(1)}, u32[]{:S(2)}, u32[]{:S(2)}) collective-permute-start(bf16[104,896]{1,0:T(8,128)(2,1)S(1)} %get-tuple-element.104), channel_id=1, source_target_pairs={{0,2},{1,3},{2,4},{3,5},{4,6},{5,7},{6,0},{7,1},{8,14},{9,15},{10,... | collective-permute-start | bytes 559112 | tf_op jit(solution)/shard_map/ppermute | solution.py:67
  144.0 11.8 %collective-permute-start.28 = (bf16[104,896]{1,0:T(8,128)(2,1)S(1)}, bf16[104,896]{1,0:T(8,128)(2,1)S(1)}, u32[]{:S(2)}, u32[]{:S(2)}) collective-permute-start(bf16[104,896]{1,0:T(8,128)(2,1)S(1)} %get-tuple-element.104), channel_id=1, source_target_pairs={{0,6},{1,7},{2,0},{3,1},{4,2},{5,3},{6,4},{7,5},{8,10},{9,11},{10,... | collective-permute-start | bytes 559112 | tf_op jit(solution)/shard_map/ppermute | solution.py:67
  144.4 11.4 %collective-permute-start.29 = (bf16[104,896]{1,0:T(8,128)(2,1)S(1)}, bf16[104,896]{1,0:T(8,128)(2,1)S(1)}, u32[]{:S(2)}, u32[]{:S(2)}) collective-permute-start(bf16[104,896]{1,0:T(8,128)(2,1)S(1)} %get-tuple-element.104), channel_id=1, source_target_pairs={{0,4},{1,5},{2,6},{3,7},{4,0},{5,1},{6,2},{7,3},{8,12},{9,13},{10,... | collective-permute-start | bytes 559112 | tf_op jit(solution)/shard_map/ppermute | solution.py:67
  155.9 18.4 %collective-permute-start.36 = (bf16[416,896]{1,0:T(8,128)(2,1)S(1)}, bf16[416,896]{1,0:T(8,128)(2,1)S(1)}, u32[]{:S(2)}, u32[]{:S(2)}) collective-permute-start(bf16[416,896]{1,0:T(8,128)(2,1)S(1)} %constant_dynamic-update-slice_fusion.6.refs_2_), channel_id=1, source_target_pairs={{0,1},{1,0},{2,3},{3,2},{4,5},{5,4},{6,7},{7,6},{8,9},{9,8},{10,11... | collective-permute-start | bytes 2236424 | tf_op jit(solution)/shard_map/ppermute | solution.py:67
  156.5 9.0 %collective-permute-start.37 = (bf16[208,896]{1,0:T(8,128)(2,1)S(1)}, bf16[208,896]{1,0:T(8,128)(2,1)S(1)}, u32[]{:S(2)}, u32[]{:S(2)}) collective-permute-start(bf16[208,896]{1,0:T(8,128)(2,1)S(1)} %constant_dynamic-update-slice_fusion.4.refs_4_), channel_id=1, source_target_pairs={{0,2},{1,3},{2,4},{3,5},{4,6},{5,7},{6,0},{7,1},{8,14},{9,15},{10,... | collective-permute-start | bytes 1118216 | tf_op jit(solution)/shard_map/ppermute | solution.py:67
  156.6 11.6 %collective-permute-start.38 = (bf16[208,896]{1,0:T(8,128)(2,1)S(1)}, bf16[208,896]{1,0:T(8,128)(2,1)S(1)}, u32[]{:S(2)}, u32[]{:S(2)}) collective-permute-start(bf16[208,896]{1,0:T(8,128)(2,1)S(1)} %constant_dynamic-update-slice_fusion.4.refs_4_), channel_id=1, source_target_pairs={{0,6},{1,7},{2,0},{3,1},{4,2},{5,3},{6,4},{7,5},{8,10},{9,11},{10,... | collective-permute-start | bytes 1118216 | tf_op jit(solution)/shard_map/ppermute | solution.py:67
  158.0 16.4 %collective-permute-start.39 = (bf16[208,896]{1,0:T(8,128)(2,1)S(1)}, bf16[208,896]{1,0:T(8,128)(2,1)S(1)}, u32[]{:S(2)}, u32[]{:S(2)}) collective-permute-start(bf16[208,896]{1,0:T(8,128)(2,1)S(1)} %constant_dynamic-update-slice_fusion.4.refs_4_), channel_id=1, source_target_pairs={{0,4},{1,5},{2,6},{3,7},{4,0},{5,1},{6,2},{7,3},{8,12},{9,13},{10,... | collective-permute-start | bytes 1118216 | tf_op jit(solution)/shard_map/ppermute | solution.py:67
  180.1 5.2 %collective-permute-start.40 = (f32[416,768]{1,0:T(8,128)S(1)}, f32[416,768]{1,0:T(8,128)S(1)}, u32[]{:S(2)}, u32[]{:S(2)}) collective-permute-start(f32[416,768]{1,0:T(8,128)S(1)} %get-tuple-element.84), channel_id=1, source_target_pairs={{0,8},{1,9},{2,10},{3,11},{4,12},{5,13},{6,14},{7,15},{8,0},{9,1},... | collective-permute-start | bytes 3833864 | tf_op jit(solution)/shard_map/ppermute | solution.py:67
  185.6 5.1 %collective-permute-start.41 = (bf16[104,768]{1,0:T(8,128)(2,1)S(1)}, bf16[104,768]{1,0:T(8,128)(2,1)S(1)}, u32[]{:S(2)}, u32[]{:S(2)}) collective-permute-start(bf16[104,768]{1,0:T(8,128)(2,1)S(1)} %get-tuple-element.86), channel_id=1, source_target_pairs={{0,32},{1,33},{2,34},{3,35},{4,36},{5,37},{6,38},{7,39},{8,104},{9... | collective-permute-start | bytes 479240 | tf_op jit(solution)/shard_map/ppermute | solution.py:67
  185.6 6.7 %collective-permute-start.42 = (bf16[104,768]{1,0:T(8,128)(2,1)S(1)}, bf16[104,768]{1,0:T(8,128)(2,1)S(1)}, u32[]{:S(2)}, u32[]{:S(2)}) collective-permute-start(bf16[104,768]{1,0:T(8,128)(2,1)S(1)} %get-tuple-element.87), channel_id=1, source_target_pairs={{0,96},{1,97},{2,98},{3,99},{4,100},{5,101},{6,102},{7,103},{8,40}... | collective-permute-start | bytes 479240 | tf_op jit(solution)/shard_map/ppermute | solution.py:67
  187.8 6.7 %collective-permute-start.43 = (bf16[104,768]{1,0:T(8,128)(2,1)S(1)}, bf16[104,768]{1,0:T(8,128)(2,1)S(1)}, u32[]{:S(2)}, u32[]{:S(2)}) collective-permute-start(bf16[104,768]{1,0:T(8,128)(2,1)S(1)} %get-tuple-element.88), channel_id=1, source_target_pairs={{0,64},{1,65},{2,66},{3,67},{4,68},{5,69},{6,70},{7,71},{8,72},{9,... | collective-permute-start | bytes 479240 | tf_op jit(solution)/shard_map/ppermute | solution.py:67
  194.6 11.8 %collective-permute-start.44 = (f32[104,768]{1,0:T(8,128)S(1)}, f32[104,768]{1,0:T(8,128)S(1)}, u32[]{:S(2)}, u32[]{:S(2)}) collective-permute-start(f32[104,768]{1,0:T(8,128)S(1)} %add_add_fusion), channel_id=1, source_target_pairs={{0,16},{1,17},{2,18},{3,19},{4,20},{5,21},{6,22},{7,23},{8,24},{9,... | collective-permute-start | bytes 958472 | tf_op jit(solution)/shard_map/ppermute | solution.py:67
  206.5 4.2 %collective-permute-start.45 = (bf16[104,768]{1,0:T(8,128)(2,1)S(1)}, bf16[104,768]{1,0:T(8,128)(2,1)S(1)}, u32[]{:S(2)}, u32[]{:S(2)}) collective-permute-start(bf16[104,768]{1,0:T(8,128)(2,1)S(1)} %get-tuple-element.90), channel_id=1, source_target_pairs={{0,32},{1,33},{2,34},{3,35},{4,36},{5,37},{6,38},{7,39},{8,104},{9... | collective-permute-start | bytes 479240 | tf_op jit(solution)/shard_map/ppermute | solution.py:67
  206.6 5.4 %collective-permute-start.46 = (bf16[104,768]{1,0:T(8,128)(2,1)S(1)}, bf16[104,768]{1,0:T(8,128)(2,1)S(1)}, u32[]{:S(2)}, u32[]{:S(2)}) collective-permute-start(bf16[104,768]{1,0:T(8,128)(2,1)S(1)} %get-tuple-element.90), channel_id=1, source_target_pairs={{0,96},{1,97},{2,98},{3,99},{4,100},{5,101},{6,102},{7,103},{8,40}... | collective-permute-start | bytes 479240 | tf_op jit(solution)/shard_map/ppermute | solution.py:67
  208.1 7.5 %collective-permute-start.47 = (bf16[104,768]{1,0:T(8,128)(2,1)S(1)}, bf16[104,768]{1,0:T(8,128)(2,1)S(1)}, u32[]{:S(2)}, u32[]{:S(2)}) collective-permute-start(bf16[104,768]{1,0:T(8,128)(2,1)S(1)} %get-tuple-element.90), channel_id=1, source_target_pairs={{0,64},{1,65},{2,66},{3,67},{4,68},{5,69},{6,70},{7,71},{8,72},{9,... | collective-permute-start | bytes 479240 | tf_op jit(solution)/shard_map/ppermute | solution.py:67
  215.6 4.5 %collective-permute-start.48 = (bf16[416,768]{1,0:T(8,128)(2,1)S(1)}, bf16[416,768]{1,0:T(8,128)(2,1)S(1)}, u32[]{:S(2)}, u32[]{:S(2)}) collective-permute-start(bf16[416,768]{1,0:T(8,128)(2,1)S(1)} %constant_dynamic-update-slice_fusion.own), channel_id=1, source_target_pairs={{0,8},{1,9},{2,10},{3,11},{4,12},{5,13},{6,14},{7,15},{8,0},{9,1},... | collective-permute-start | bytes 1916936 | tf_op jit(solution)/shard_map/ppermute | solution.py:67

commit v8 on v7

--- a/solution.py
+++ b/solution.py
@@ -332,17 +332,19 @@
 def exchange_kernel(*refs):
     halves, parts, (keep, give, held, weights, turned, sems) = refs[:2], refs[2:8], refs[8:]
     core, _, _, _ = here()
-    copies = [pltpu.make_async_copy(halves[q], held.at[q], sems.at[6 + q]) for q in range(2)]
+    copies = [[pltpu.make_async_copy(halves[q], held.at[q], sems.at[6 + q])] for q in range(2)]
     for i, (q, at) in enumerate([(0, at) for at in chunks_low()] + [(1, at) for at in chunks_arrived()]):
         n = parts[i].shape[0]
         into = weights.at[q, pl.ds(pl.multiple_of(at * n, n), n), :]
-        copies.append(pltpu.make_async_copy(parts[i], into, sems.at[i]))
-    for copy in copies:
+        copies[q].append(pltpu.make_async_copy(parts[i], into, sems.at[i]))
+    for copy in copies[0] + copies[1]:
         copy.start()
+    exchanged = []
     for q in range(2):
         weights[q, CROSS:, :] = jnp.zeros((WIDE - CROSS, WIDE), bf16)
-    for copy in copies:
-        copy.wait()
+        for copy in copies[q]:
+            copy.wait()
+        exchanged.append(jnp.dot(held[q], weights[q], preferred_element_type=f32))
     line = lax.broadcasted_iota(jnp.int32, (16, WIDE), 0)
     total = None
     for q in range(2):
@@ -350,8 +352,7 @@
         codes = codes + jnp.where(line == 1, weights[1 - q, NOCC : NOCC + 16, :].astype(f32), 0.0)
         coulomb = jnp.sum(codes, keepdims=True) * (1.0 / NB)
         factor = jnp.where(core == 0, 2.0 * coulomb, 0.0)
-        own = held[q]
-        term = factor * own.astype(f32) - jnp.dot(own, weights[q], preferred_element_type=f32)
+        term = factor * held[q].astype(f32) - exchanged[q]
         total = term if total is None else total + term
     turned[...] = total.T
     n = CROSS // 2
@@ -440,15 +441,16 @@
     main, rest = stage[:, :, :MAIN], stage[:, :, MAIN:]
     zz = ("z", "z")
     main_ahead = send(main, around(zz, 1, True))
+    main_far = send(main_ahead, around(zz, 1, True))
+    main_behind = send_after(main, around(zz, -1, True), main_ahead)
+    lists = lax.optimization_barrier((block_rows[0], block_cols[0], block_count[0], ahead))
+    lists = jnp.concatenate([lists[0] % ROW_BLOCKS, lists[1], lists[2]])
+    lists = jnp.pad(lists, (0, 256 - 2 * SLOTS - 1))[None]
+    meta = jnp.concatenate([lists, send_after(lists, permutation(other_core), main_ahead)])
+    rest, meta = lax.optimization_barrier((rest, meta))
     rest_ahead = send(rest, around(two, 1, False))
     rest_behind = send(rest, around(two, -1, False))
-    main_far = send(main_ahead, around(zz, 1, True))
-    main_behind = send(main, around(zz, -1, True))
     rest_far = send(rest, around(two, 2, False))
-
-    lists = lax.optimization_barrier((block_rows[0], block_cols[0], block_count[0], rest_ahead))
-    lists = jnp.concatenate([lists[0] % ROW_BLOCKS, lists[1], lists[2]])
-    lists = jnp.pad(lists, (0, 256 - 2 * SLOTS - 1))[None]
 
     mains = [jnp.zeros((ZH, ZL, 4, MAIN, WIDE), bf16)] * 2
     for array, at in (
@@ -469,14 +471,13 @@
     rest = into
 
     ahead, behind = around(two, 1, False), around(two, -1, False)
-    mains, rest, lists = lax.optimization_barrier((mains, rest, lists))
+    mains, rest = lax.optimization_barrier((mains, rest))
     ahead_0 = send(mains[0], ahead)
     behind_1 = send(mains[1], behind)
     rest_ahead = send(rest, around(zz, 1, True))
     rest_behind = send(rest, around(zz, -1, True))
-    meta = jnp.concatenate([lists, swap_cores(lists)])
-    ahead_1 = send_after(mains[1], ahead, ahead_0, meta)
-    behind_0 = send_after(mains[0], behind, behind_1, meta)
+    ahead_1 = send_after(mains[1], ahead, ahead_0)
+    behind_0 = send_after(mains[0], behind, behind_1)
     far_0 = send(ahead_0, ahead)
     far_1 = send_after(behind_1, behind, rest_ahead)
     rest_far = send_after(rest_ahead, around(zz, 1, True), rest_behind)

time: 223 us -> 224 us (level)
  waiting for transfers between devices: 106 us -> 122 us
  starting transfers between devices: 78.6 us -> 67.5 us
    ppermute x49, waiting for transfers between devices: 106 us -> 122 us  [send(): return lax.ppermute(array, AXES, pairs)]
    ppermute x49, starting transfers between devices: 78.6 us -> 67.5 us  [send(): return lax.ppermute(array, AXES, pairs)]
  transfers between devices with their start and end apart: 49 -> 49, of which waited for: 38 -> 36; matrix products, arithmetic and copies ran while one was open for 1% -> 1% of each run, Pallas kernels for 8% -> 8%
where the time goes in v8:
time: 224 us
  waiting for transfers between devices  122 us (54%)
  starting transfers between devices  67.5 us (30%)
  Pallas kernels  28.8 us (13%)
  other arithmetic  2.57 us (1%)
    ppermute x49, waiting for transfers between devices, send(): return lax.ppermute(array, AXES, pairs)  122 us
    ppermute x49, starting transfers between devices, send(): return lax.ppermute(array, AXES, pairs)  67.5 us
    pallas_call x2, Pallas kernels, multiply(): pl.pallas_call(kernel, out_shape=jax.ShapeDtypeStruct((ROWS, WIDE), bf16)...  9.92 us
    pallas_call x1, Pallas kernels, exchange(): pl.pallas_call(exchange_kernel, out_shape=[jax.ShapeDtypeStruct((CROSS //...  5.74 us
    pallas_call x1, Pallas kernels, panels_and_slab(): pl.pallas_call(near_kernel, out_shape=held, in_specs=[anywhere] * 9, out_...  5.12 us
  transfers between devices with their start and end apart: 49, of which 36 were waited for; matrix products, arithmetic and copies ran while one was open for 1% of the time, Pallas kernels for 8%

profile of v8, /device:TPU:1, one launch (start us, length us, event | category | flops | bytes accessed | tf_op | source)
XLA Modules:
  0.0 223.7 jit_solution(5523977425311732735)
XLA Ops:
  0.9 1.5 collective-permute-start
  4.7 1.4 collective-permute-start.1
  6.8 1.9 collective-permute-start.2
  8.7 1.3 collective-permute-start.3
  12.9 1.8 collective-permute-done.3
  14.9 3.8 %collective-permute-start.5 = (bf16[2,4,32,896]{3,2,1,0:T(8,128)(2,1)S(1)}, bf16[2,4,32,896]{3,2,1,0:T(8,128)(2,1)S(1)}, u32[]{:S(2)}, u32[]{:S(2)}) collective-permute-start(bf16[2,4,32,896]{3,2,1,0:T(8,128)(2,1)S(1)} %slice.39), channel_id=1, source_target_pairs={{0,1},{1,16},{2,3},{3,18},{4,5},{5,20},{6,7},{7,22},{8,25},{9,8},{... | collective-permute-start | bytes 1376264 | tf_op jit(solution)/shard_map/ppermute | solution.py:67
  18.9 5.2 %collective-permute-done.5 = bf16[2,4,32,896]{3,2,1,0:T(8,128)(2,1)S(1)} collective-permute-done((bf16[2,4,32,896]{3,2,1,0:T(8,128)(2,1)S(1)}, bf16[2,4,32,896]{3,2,1,0:T(8,128)(2,1)S(1)}, u32[]{:S(2)}, u32[]{:S(2)}) %collective-permute-start.5) | collective-permute-done | bytes 458784 | tf_op jit(solution)/shard_map/ppermute | solution.py:67
  24.1 2.5 %collective-permute-start.6 = (s32[1,256]{1,0:T(1,128)S(1)}, s32[1,256]{1,0:T(1,128)S(1)}, u32[]{:S(2)}, u32[]{:S(2)}) collective-permute-start(s32[1,256]{1,0:T(1,128)S(1)} %bitcast.73), channel_id=1, source_target_pairs={{0,8},{1,9},{2,10},{3,11},{4,12},{5,13},{6,14},{7,15},{8,0},{9,1},... | collective-permute-start | bytes 3080 | tf_op jit(solution)/shard_map/ppermute | solution.py:67
  26.6 2.7 %collective-permute-start.8 = (bf16[2,4,32,896]{3,2,1,0:T(8,128)(2,1)S(1)}, bf16[2,4,32,896]{3,2,1,0:T(8,128)(2,1)S(1)}, u32[]{:S(2)}, u32[]{:S(2)}) collective-permute-start(bf16[2,4,32,896]{3,2,1,0:T(8,128)(2,1)S(1)} %collective-permute-done.5), channel_id=1, source_target_pairs={{0,1},{1,16},{2,3},{3,18},{4,5},{5,20},{6,7},{7,22},{8,25},{9,8},{... | collective-permute-start | bytes 1376264 | tf_op jit(solution)/shard_map/ppermute | solution.py:67
  29.9 2.2 %collective-permute-start.10 = (bf16[2,4,16,896]{3,2,1,0:T(8,128)(2,1)S(1)}, bf16[2,4,16,896]{3,2,1,0:T(8,128)(2,1)S(1)}, u32[]{:S(2)}, u32[]{:S(2)}) collective-permute-start(bf16[2,4,16,896]{3,2,1,0:T(8,128)(2,1)S(1)} %slice.38), channel_id=1, source_target_pairs={{0,96},{1,97},{2,98},{3,99},{4,100},{5,101},{6,102},{7,103},{8,14}... | collective-permute-start | bytes 688136 | tf_op jit(solution)/shard_map/ppermute | solution.py:67
  32.5 3.3 %collective-permute-done.9 = bf16[2,4,16,896]{3,2,1,0:T(8,128)(2,1)S(1)} collective-permute-done((bf16[2,4,16,896]{3,2,1,0:T(8,128)(2,1)S(1)}, bf16[2,4,16,896]{3,2,1,0:T(8,128)(2,1)S(1)}, u32[]{:S(2)}, u32[]{:S(2)}) %collective-permute-start.9) | collective-permute-done | bytes 229408 | tf_op jit(solution)/shard_map/ppermute | solution.py:67
  35.8 1.7 collective-permute-done.10
  37.6 1.2 collective-permute-done.11
  39.2 2.1 collective-permute-start.14
  41.2 2.9 %collective-permute-start.15 = (bf16[2,4,4,16,896]{4,3,2,1,0:T(8,128)(2,1)S(1)}, bf16[2,4,4,16,896]{4,3,2,1,0:T(8,128)(2,1)S(1)}, u32[]{:S(2)}, u32[]{:S(2)}) collective-permute-start(bf16[2,4,4,16,896]{4,3,2,1,0:T(8,128)(2,1)S(1)} %bitcast_dynamic-update-slice_fusion.3.refs_2_), channel_id=1, source_target_pairs={{0,1},{1,16},{2,3},{3,18},{4,5},{5,20},{6,7},{7,22},{8,25},{9,8},{... | collective-permute-start | bytes 2752520 | tf_op jit(solution)/shard_map/ppermute | solution.py:67
  44.1 7.7 %collective-permute-done.14.refs_7_ = bf16[2,2,4,32,896]{4,3,2,1,0:T(8,128)(2,1)S(1)} collective-permute-done((bf16[2,2,4,32,896]{4,3,2,1,0:T(8,128)(2,1)S(1)}, bf16[2,2,4,32,896]{4,3,2,1,0:T(8,128)(2,1)S(1)}, u32[]{:S(2)}, u32[]{:S(2)}) %collective-permute-start.14) | collective-permute-done | bytes 917536 | tf_op jit(solution)/shard_map/ppermute | solution.py:67
  51.8 3.2 %collective-permute-start.20 = (bf16[2,2,4,32,896]{4,3,2,1,0:T(8,128)(2,1)S(1)}, bf16[2,2,4,32,896]{4,3,2,1,0:T(8,128)(2,1)S(1)}, u32[]{:S(2)}, u32[]{:S(2)}) collective-permute-start(bf16[2,2,4,32,896]{4,3,2,1,0:T(8,128)(2,1)S(1)} %get-tuple-element.65.refs_0_), channel_id=1, source_target_pairs={{0,96},{1,97},{2,98},{3,99},{4,100},{5,101},{6,102},{7,103},{8,14}... | collective-permute-start | bytes 2752520 | tf_op jit(solution)/shard_map/ppermute | solution.py:67
  55.0 6.0 %collective-permute-done.15.refs_5_ = bf16[2,4,4,16,896]{4,3,2,1,0:T(8,128)(2,1)S(1)} collective-permute-done((bf16[2,4,4,16,896]{4,3,2,1,0:T(8,128)(2,1)S(1)}, bf16[2,4,4,16,896]{4,3,2,1,0:T(8,128)(2,1)S(1)}, u32[]{:S(2)}, u32[]{:S(2)}) %collective-permute-start.15) | collective-permute-done | bytes 917536 | tf_op jit(solution)/shard_map/ppermute | solution.py:67
  61.0 6.4 %collective-permute-done.17.refs_8_ = bf16[2,4,4,16,896]{4,3,2,1,0:T(8,128)(2,1)S(1)} collective-permute-done((bf16[2,4,4,16,896]{4,3,2,1,0:T(8,128)(2,1)S(1)}, bf16[2,4,4,16,896]{4,3,2,1,0:T(8,128)(2,1)S(1)}, u32[]{:S(2)}, u32[]{:S(2)}) %collective-permute-start.17) | collective-permute-done | bytes 917536 | tf_op jit(solution)/shard_map/ppermute | solution.py:67
  67.5 1.7 collective-permute-start.16
  69.2 5.1 %near.1 = bf16[4,2,2,4,2,48,896]{6,5,4,3,2,1,0:T(8,128)(2,1)S(1)} custom-call(bf16[2,2,4,32,896]{4,3,2,1,0:T(8,128)(2,1)S(1)} %get-tuple-element.65.refs_0_, bf16[2,2,4,32,896]{4,3,2,1,0:T(8,128)(2,1)S(1)} %get-tuple-element.64.refs_1_, bf16[2,4,4,16,896]{4,3,2,1,0:T(8,128)(2,1)S(1)} %bitcast_dynamic-update-slice_fusion.3.refs_2_, ...), custom_call_target="tpu_custom_call" | custom-call | tf_op jit(solution)/shard_map/near/pallas_call | solution.py:137
  74.3 5.7 %collective-permute-done.18.rest = bf16[2,4,4,16,896]{4,3,2,1,0:T(8,128)(2,1)S(1)} collective-permute-done((bf16[2,4,4,16,896]{4,3,2,1,0:T(8,128)(2,1)S(1)}, bf16[2,4,4,16,896]{4,3,2,1,0:T(8,128)(2,1)S(1)}, u32[]{:S(2)}, u32[]{:S(2)}) %collective-permute-start.18) | collective-permute-done | bytes 917536 | tf_op jit(solution)/shard_map/ppermute | solution.py:67
  80.0 2.9 %collective-permute-done.13.main0 = bf16[2,2,4,32,896]{4,3,2,1,0:T(8,128)(2,1)S(1)} collective-permute-done((bf16[2,2,4,32,896]{4,3,2,1,0:T(8,128)(2,1)S(1)}, bf16[2,2,4,32,896]{4,3,2,1,0:T(8,128)(2,1)S(1)}, u32[]{:S(2)}, u32[]{:S(2)}) %collective-permute-start.13) | collective-permute-done | bytes 917536 | tf_op jit(solution)/shard_map/ppermute | solution.py:67
  82.9 1.7 far.1
  84.7 2.6 %collective-permute-start.21 = (bf16[768,896]{1,0:T(8,128)(2,1)S(1)}, bf16[768,896]{1,0:T(8,128)(2,1)S(1)}, u32[]{:S(2)}, u32[]{:S(2)}) collective-permute-start(bf16[768,896]{1,0:T(8,128)(2,1)S(1)} %bitcast.70), channel_id=1, source_target_pairs={{0,8},{1,9},{2,10},{3,11},{4,12},{5,13},{6,14},{7,15},{8,0},{9,1},... | collective-permute-start | bytes 4128776 | tf_op jit(solution)/shard_map/ppermute | solution.py:67
  87.2 5.4 %multiply.2.refs_0_.refs_1_ = bf16[768,896]{1,0:T(8,128)(2,1)S(1)} custom-call(s32[2,256]{1,0:T(2,128)S(1)} %pad_add_fusion.refs_0_, bf16[96,128,128]{2,1,0:T(8,128)(2,1)S(1)} %collective-permute-done.4.refs_1_, bf16[4,2,2,4,2,48,896]{6,5,4,3,2,1,0:T(8,128)(2,1)S(1)} %get-tuple-element.70.refs_2_), custom_call_target="tpu_custom_call" | custom-call | flops 2818572288 | bytes 8388608 | tf_op jit(solution)/shard_map/multiply/pallas_call | solution.py:234
  92.6 2.0 cross.2
  94.7 2.4 %collective-permute-start.22 = (bf16[416,896]{1,0:T(8,128)(2,1)S(1)}, bf16[416,896]{1,0:T(8,128)(2,1)S(1)}, u32[]{:S(2)}, u32[]{:S(2)}) collective-permute-start(bf16[416,896]{1,0:T(8,128)(2,1)S(1)} %get-tuple-element.72), channel_id=1, source_target_pairs={{0,1},{1,0},{2,3},{3,2},{4,5},{5,4},{6,7},{7,6},{8,9},{9,8},{10,11... | collective-permute-start | bytes 2236424 | tf_op jit(solution)/shard_map/ppermute | solution.py:67
  97.1 4.5 %multiply.3.refs_0_ = bf16[768,896]{1,0:T(8,128)(2,1)S(1)} custom-call(s32[2,256]{1,0:T(2,128)S(1)} %pad_add_fusion.refs_0_, bf16[96,128,128]{2,1,0:T(8,128)(2,1)S(1)} %bitcast.69, bf16[4,2,2,4,2,48,896]{6,5,4,3,2,1,0:T(8,128)(2,1)S(1)} %get-tuple-element.70.refs_2_), custom_call_target="tpu_custom_call" | custom-call | flops 2818572288 | bytes 8388608 | tf_op jit(solution)/shard_map/multiply/pallas_call | solution.py:234
  101.7 1.8 cross.3
  103.6 3.6 %collective-permute-start.31 = (bf16[208,896]{1,0:T(8,128)(2,1)S(1)}, bf16[208,896]{1,0:T(8,128)(2,1)S(1)}, u32[]{:S(2)}, u32[]{:S(2)}) collective-permute-start(bf16[208,896]{1,0:T(8,128)(2,1)S(1)} %get-tuple-element.79), channel_id=1, source_target_pairs={{0,6},{1,7},{2,0},{3,1},{4,2},{5,3},{6,4},{7,5},{8,10},{9,11},{10,... | collective-permute-start | bytes 1118216 | tf_op jit(solution)/shard_map/ppermute | solution.py:67
  107.2 2.1 collective-permute-start.32
  109.3 4.0 %collective-permute-done.22.refs_1_ = bf16[416,896]{1,0:T(8,128)(2,1)S(1)} collective-permute-done((bf16[416,896]{1,0:T(8,128)(2,1)S(1)}, bf16[416,896]{1,0:T(8,128)(2,1)S(1)}, u32[]{:S(2)}, u32[]{:S(2)}) %collective-permute-start.22) | collective-permute-done | bytes 745504 | tf_op jit(solution)/shard_map/ppermute | solution.py:67
  114.0 2.2 collective-permute-done.31.refs_2_
  116.3 7.4 %collective-permute-done.32.refs_3_ = bf16[208,896]{1,0:T(8,128)(2,1)S(1)} collective-permute-done((bf16[208,896]{1,0:T(8,128)(2,1)S(1)}, bf16[208,896]{1,0:T(8,128)(2,1)S(1)}, u32[]{:S(2)}, u32[]{:S(2)}) %collective-permute-start.32) | collective-permute-done | bytes 372768 | tf_op jit(solution)/shard_map/ppermute | solution.py:67
  124.0 4.5 %collective-permute-start.33 = (bf16[104,896]{1,0:T(8,128)(2,1)S(1)}, bf16[104,896]{1,0:T(8,128)(2,1)S(1)}, u32[]{:S(2)}, u32[]{:S(2)}) collective-permute-start(bf16[104,896]{1,0:T(8,128)(2,1)S(1)} %get-tuple-element.86), channel_id=1, source_target_pairs={{0,1},{1,0},{2,3},{3,2},{4,5},{5,4},{6,7},{7,6},{8,9},{9,8},{10,11... | collective-permute-start | bytes 559112 | tf_op jit(solution)/shard_map/ppermute | solution.py:67
  128.6 1.5 collective-permute-start.24
  131.2 2.0 collective-permute-done.33
  134.1 1.2 collective-permute-done.24
  135.3 4.4 %collective-permute-done.25 = bf16[104,896]{1,0:T(8,128)(2,1)S(1)} collective-permute-done((bf16[104,896]{1,0:T(8,128)(2,1)S(1)}, bf16[104,896]{1,0:T(8,128)(2,1)S(1)}, u32[]{:S(2)}, u32[]{:S(2)}) %collective-permute-start.25) | collective-permute-done | bytes 186400 | tf_op jit(solution)/shard_map/ppermute | solution.py:67
  139.9 1.3 collective-permute-start.26
  143.1 2.0 collective-permute-start.27
  145.1 1.4 collective-permute-start.29
  146.5 2.5 %collective-permute-done.35 = bf16[104,896]{1,0:T(8,128)(2,1)S(1)} collective-permute-done((bf16[104,896]{1,0:T(8,128)(2,1)S(1)}, bf16[104,896]{1,0:T(8,128)(2,1)S(1)}, u32[]{:S(2)}, u32[]{:S(2)}) %collective-permute-start.35) | collective-permute-done | bytes 186400 | tf_op jit(solution)/shard_map/ppermute | solution.py:67
  149.0 6.7 %collective-permute-done.28 = bf16[104,896]{1,0:T(8,128)(2,1)S(1)} collective-permute-done((bf16[104,896]{1,0:T(8,128)(2,1)S(1)}, bf16[104,896]{1,0:T(8,128)(2,1)S(1)}, u32[]{:S(2)}, u32[]{:S(2)}) %collective-permute-start.28) | collective-permute-done | bytes 186400 | tf_op jit(solution)/shard_map/ppermute | solution.py:67
  155.8 1.4 collective-permute-start.36
  158.8 7.8 %collective-permute-done.37.refs_5_ = bf16[208,896]{1,0:T(8,128)(2,1)S(1)} collective-permute-done((bf16[208,896]{1,0:T(8,128)(2,1)S(1)}, bf16[208,896]{1,0:T(8,128)(2,1)S(1)}, u32[]{:S(2)}, u32[]{:S(2)}) %collective-permute-start.37) | collective-permute-done | bytes 372768 | tf_op jit(solution)/shard_map/ppermute | solution.py:67
  166.6 10.0 %collective-permute-done.38.refs_6_ = bf16[208,896]{1,0:T(8,128)(2,1)S(1)} collective-permute-done((bf16[208,896]{1,0:T(8,128)(2,1)S(1)}, bf16[208,896]{1,0:T(8,128)(2,1)S(1)}, u32[]{:S(2)}, u32[]{:S(2)}) %collective-permute-start.38) | collective-permute-done | bytes 372768 | tf_op jit(solution)/shard_map/ppermute | solution.py:67
  176.6 5.7 %exchange.1 = (f32[416,768]{1,0:T(8,128)S(1)}, f32[416,768]{1,0:T(8,128)S(1)}) custom-call(bf16[768,896]{1,0:T(8,128)(2,1)} %copy-done.2, bf16[768,896]{1,0:T(8,128)(2,1)} %copy-done.1, bf16[416,896]{1,0:T(8,128)(2,1)S(1)} %constant_dynamic-update-slice_fusion.6.refs_2_, bf16[416,896]{1,0:T(8,128)(2,1)S(1)} %collective-permute-done.36.refs_3_, ...), custom_call_target="tpu_custom_call" | custom-call | flops 2466250752 | bytes 8388608 | tf_op jit(solution)/shard_map/exchange/pallas_call | solution.py:369
  182.4 1.2 collective-permute-start.40
  183.6 2.6 %collective-permute-done.40.refs_1_ = f32[416,768]{1,0:T(8,128)S(1)} collective-permute-done((f32[416,768]{1,0:T(8,128)S(1)}, f32[416,768]{1,0:T(8,128)S(1)}, u32[]{:S(2)}, u32[]{:S(2)}) %collective-permute-start.40) | collective-permute-done | bytes 1277984 | tf_op jit(solution)/shard_map/ppermute | solution.py:67
  186.4 1.8 collective-permute-start.41
  188.2 1.3 collective-permute-start.43
  189.5 2.2 collective-permute-done.41
  191.7 6.1 %collective-permute-done.42 = bf16[104,768]{1,0:T(8,128)(2,1)S(1)} collective-permute-done((bf16[104,768]{1,0:T(8,128)(2,1)S(1)}, bf16[104,768]{1,0:T(8,128)(2,1)S(1)}, u32[]{:S(2)}, u32[]{:S(2)}) %collective-permute-start.42) | collective-permute-done | bytes 159776 | tf_op jit(solution)/shard_map/ppermute | solution.py:67
  197.9 3.4 %collective-permute-start.44 = (f32[104,768]{1,0:T(8,128)S(1)}, f32[104,768]{1,0:T(8,128)S(1)}, u32[]{:S(2)}, u32[]{:S(2)}) collective-permute-start(f32[104,768]{1,0:T(8,128)S(1)} %add_add_fusion), channel_id=1, source_target_pairs={{0,16},{1,17},{2,18},{3,19},{4,20},{5,21},{6,22},{7,23},{8,24},{9,... | collective-permute-start | bytes 958472 | tf_op jit(solution)/shard_map/ppermute | solution.py:67
  201.2 6.8 %collective-permute-done.44 = f32[104,768]{1,0:T(8,128)S(1)} collective-permute-done((f32[104,768]{1,0:T(8,128)S(1)}, f32[104,768]{1,0:T(8,128)S(1)}, u32[]{:S(2)}, u32[]{:S(2)}) %collective-permute-start.44) | collective-permute-done | bytes 319520 | tf_op jit(solution)/shard_map/ppermute | solution.py:67
  208.2 1.5 collective-permute-start.46
  209.6 2.2 collective-permute-start.47
  212.3 1.3 collective-permute-done.46
  213.6 4.9 %collective-permute-done.47 = bf16[104,768]{1,0:T(8,128)(2,1)S(1)} collective-permute-done((bf16[104,768]{1,0:T(8,128)(2,1)S(1)}, bf16[104,768]{1,0:T(8,128)(2,1)S(1)}, u32[]{:S(2)}, u32[]{:S(2)}) %collective-permute-start.47) | collective-permute-done | bytes 159776 | tf_op jit(solution)/shard_map/ppermute | solution.py:67
  218.5 1.9 collective-permute-start.48
  220.4 1.7 collective-permute-done.48.others
  222.1 1.6 widen.1
  (98 shorter events, 16.0 us)
Async XLA Ops:
  0.0 10.8 %copy-start.4 = (s32[1,96]{1,0:T(1,128)S(1)}, s32[1,96]{1,0:T(1,128)}, u32[]{:S(2)}) copy-start(s32[1,96]{1,0:T(1,128)} %param.7) | copy-start | bytes 1156
  0.0 10.8 %copy-start.3 = (s32[1,96]{1,0:T(1,128)S(1)}, s32[1,96]{1,0:T(1,128)}, u32[]{:S(2)}) copy-start(s32[1,96]{1,0:T(1,128)} %param.8) | copy-start | bytes 1156
  0.9 2.4 %collective-permute-start = (bf16[48,800]{1,0:T(8,128)(2,1)S(1)}, bf16[48,800]{1,0:T(8,128)(2,1)S(1)}, u32[]{:S(2)}, u32[]{:S(2)}) collective-permute-start(bf16[48,800]{1,0:T(8,128)(2,1)S(1)} %broadcast_select_fusion.2), channel_id=1, source_target_pairs={{0,8},{1,9},{2,10},{3,11},{4,12},{5,13},{6,14},{7,15},{8,0},{9,1},... | collective-permute-start | bytes 230408 | tf_op jit(solution)/shard_map/ppermute | solution.py:67
  3.4 11.4 %collective-permute-start.4 = (bf16[96,128,128]{2,1,0:T(8,128)(2,1)}, bf16[96,128,128]{2,1,0:T(8,128)(2,1)S(1)}, u32[]{:S(2)}, u32[]{:S(2)}) collective-permute-start(bf16[96,128,128]{2,1,0:T(8,128)(2,1)} %bitcast.68), channel_id=1, source_target_pairs={{0,8},{1,9},{2,10},{3,11},{4,12},{5,13},{6,14},{7,15},{8,0},{9,1},... | collective-permute-start | bytes 9437192 | tf_op jit(solution)/shard_map/ppermute | solution.py:67
  4.7 6.1 %collective-permute-start.1 = (bf16[2,48,896]{2,1,0:T(8,128)(2,1)S(1)}, bf16[2,48,896]{2,1,0:T(8,128)(2,1)}, u32[]{:S(2)}, u32[]{:S(2)}) collective-permute-start(bf16[2,48,896]{2,1,0:T(8,128)(2,1)S(1)} %fusion.10), channel_id=1, source_target_pairs={{0,2},{1,3},{2,4},{3,5},{4,6},{5,7},{6,0},{7,1},{8,40},{9,41},{10,... | collective-permute-start | bytes 516104 | tf_op jit(solution)/shard_map/ppermute | solution.py:67
  6.8 6.1 %collective-permute-start.2 = (bf16[2,48,896]{2,1,0:T(8,128)(2,1)S(1)}, bf16[2,48,896]{2,1,0:T(8,128)(2,1)S(1)}, u32[]{:S(2)}, u32[]{:S(2)}) collective-permute-start(bf16[2,48,896]{2,1,0:T(8,128)(2,1)S(1)} %fusion.10), channel_id=1, source_target_pairs={{0,6},{1,7},{2,0},{3,1},{4,2},{5,3},{6,4},{7,5},{8,104},{9,105},{1... | collective-permute-start | bytes 516104 | tf_op jit(solution)/shard_map/ppermute | solution.py:67
  8.7 6.1 %collective-permute-start.3 = (bf16[2,48,896]{2,1,0:T(8,128)(2,1)S(1)}, bf16[2,48,896]{2,1,0:T(8,128)(2,1)S(1)}, u32[]{:S(2)}, u32[]{:S(2)}) collective-permute-start(bf16[2,48,896]{2,1,0:T(8,128)(2,1)S(1)} %fusion.10), channel_id=1, source_target_pairs={{0,4},{1,5},{2,6},{3,7},{4,0},{5,1},{6,2},{7,3},{8,72},{9,73},{10,... | collective-permute-start | bytes 516104 | tf_op jit(solution)/shard_map/ppermute | solution.py:67
  14.9 9.2 %collective-permute-start.5 = (bf16[2,4,32,896]{3,2,1,0:T(8,128)(2,1)S(1)}, bf16[2,4,32,896]{3,2,1,0:T(8,128)(2,1)S(1)}, u32[]{:S(2)}, u32[]{:S(2)}) collective-permute-start(bf16[2,4,32,896]{3,2,1,0:T(8,128)(2,1)S(1)} %slice.39), channel_id=1, source_target_pairs={{0,1},{1,16},{2,3},{3,18},{4,5},{5,20},{6,7},{7,22},{8,25},{9,8},{... | collective-permute-start | bytes 1376264 | tf_op jit(solution)/shard_map/ppermute | solution.py:67
  24.1 5.2 %collective-permute-start.6 = (s32[1,256]{1,0:T(1,128)S(1)}, s32[1,256]{1,0:T(1,128)S(1)}, u32[]{:S(2)}, u32[]{:S(2)}) collective-permute-start(s32[1,256]{1,0:T(1,128)S(1)} %bitcast.73), channel_id=1, source_target_pairs={{0,8},{1,9},{2,10},{3,11},{4,12},{5,13},{6,14},{7,15},{8,0},{9,1},... | collective-permute-start | bytes 3080 | tf_op jit(solution)/shard_map/ppermute | solution.py:67
  26.6 12.2 %collective-permute-start.7 = (bf16[2,4,32,896]{3,2,1,0:T(8,128)(2,1)S(1)}, bf16[2,4,32,896]{3,2,1,0:T(8,128)(2,1)S(1)}, u32[]{:S(2)}, u32[]{:S(2)}) collective-permute-start(bf16[2,4,32,896]{3,2,1,0:T(8,128)(2,1)S(1)} %slice.39), channel_id=1, source_target_pairs={{0,17},{1,0},{2,19},{3,2},{4,21},{5,4},{6,23},{7,6},{8,9},{9,24},{... | collective-permute-start | bytes 1376264 | tf_op jit(solution)/shard_map/ppermute | solution.py:67
  26.6 12.5 %collective-permute-start.8 = (bf16[2,4,32,896]{3,2,1,0:T(8,128)(2,1)S(1)}, bf16[2,4,32,896]{3,2,1,0:T(8,128)(2,1)S(1)}, u32[]{:S(2)}, u32[]{:S(2)}) collective-permute-start(bf16[2,4,32,896]{3,2,1,0:T(8,128)(2,1)S(1)} %collective-permute-done.5), channel_id=1, source_target_pairs={{0,1},{1,16},{2,3},{3,18},{4,5},{5,20},{6,7},{7,22},{8,25},{9,8},{... | collective-permute-start | bytes 1376264 | tf_op jit(solution)/shard_map/ppermute | solution.py:67
  29.3 6.4 %collective-permute-start.9 = (bf16[2,4,16,896]{3,2,1,0:T(8,128)(2,1)S(1)}, bf16[2,4,16,896]{3,2,1,0:T(8,128)(2,1)S(1)}, u32[]{:S(2)}, u32[]{:S(2)}) collective-permute-start(bf16[2,4,16,896]{3,2,1,0:T(8,128)(2,1)S(1)} %slice.38), channel_id=1, source_target_pairs={{0,32},{1,33},{2,34},{3,35},{4,36},{5,37},{6,38},{7,39},{8,10},{9,... | collective-permute-start | bytes 688136 | tf_op jit(solution)/shard_map/ppermute | solution.py:67
  29.9 7.7 %collective-permute-start.10 = (bf16[2,4,16,896]{3,2,1,0:T(8,128)(2,1)S(1)}, bf16[2,4,16,896]{3,2,1,0:T(8,128)(2,1)S(1)}, u32[]{:S(2)}, u32[]{:S(2)}) collective-permute-start(bf16[2,4,16,896]{3,2,1,0:T(8,128)(2,1)S(1)} %slice.38), channel_id=1, source_target_pairs={{0,96},{1,97},{2,98},{3,99},{4,100},{5,101},{6,102},{7,103},{8,14}... | collective-permute-start | bytes 688136 | tf_op jit(solution)/shard_map/ppermute | solution.py:67
  32.1 6.7 %collective-permute-start.11 = (bf16[2,4,16,896]{3,2,1,0:T(8,128)(2,1)S(1)}, bf16[2,4,16,896]{3,2,1,0:T(8,128)(2,1)S(1)}, u32[]{:S(2)}, u32[]{:S(2)}) collective-permute-start(bf16[2,4,16,896]{3,2,1,0:T(8,128)(2,1)S(1)} %slice.38), channel_id=1, source_target_pairs={{0,64},{1,65},{2,66},{3,67},{4,68},{5,69},{6,70},{7,71},{8,12},{9,... | collective-permute-start | bytes 688136 | tf_op jit(solution)/shard_map/ppermute | solution.py:67
  39.2 12.6 %collective-permute-start.14 = (bf16[2,2,4,32,896]{4,3,2,1,0:T(8,128)(2,1)S(1)}, bf16[2,2,4,32,896]{4,3,2,1,0:T(8,128)(2,1)S(1)}, u32[]{:S(2)}, u32[]{:S(2)}) collective-permute-start(bf16[2,2,4,32,896]{4,3,2,1,0:T(8,128)(2,1)S(1)} %get-tuple-element.64.refs_1_), channel_id=1, source_target_pairs={{0,96},{1,97},{2,98},{3,99},{4,100},{5,101},{6,102},{7,103},{8,14}... | collective-permute-start | bytes 2752520 | tf_op jit(solution)/shard_map/ppermute | solution.py:67
  41.2 13.8 %collective-permute-start.12 = (bf16[2,2,4,32,896]{4,3,2,1,0:T(8,128)(2,1)S(1)}, bf16[2,2,4,32,896]{4,3,2,1,0:T(8,128)(2,1)S(1)}, u32[]{:S(2)}, u32[]{:S(2)}) collective-permute-start(bf16[2,2,4,32,896]{4,3,2,1,0:T(8,128)(2,1)S(1)} %get-tuple-element.65.refs_0_), channel_id=1, source_target_pairs={{0,32},{1,33},{2,34},{3,35},{4,36},{5,37},{6,38},{7,39},{8,10},{9,... | collective-permute-start | bytes 2752520 | tf_op jit(solution)/shard_map/ppermute | solution.py:67
  41.2 19.8 %collective-permute-start.15 = (bf16[2,4,4,16,896]{4,3,2,1,0:T(8,128)(2,1)S(1)}, bf16[2,4,4,16,896]{4,3,2,1,0:T(8,128)(2,1)S(1)}, u32[]{:S(2)}, u32[]{:S(2)}) collective-permute-start(bf16[2,4,4,16,896]{4,3,2,1,0:T(8,128)(2,1)S(1)} %bitcast_dynamic-update-slice_fusion.3.refs_2_), channel_id=1, source_target_pairs={{0,1},{1,16},{2,3},{3,18},{4,5},{5,20},{6,7},{7,22},{8,25},{9,8},{... | collective-permute-start | bytes 2752520 | tf_op jit(solution)/shard_map/ppermute | solution.py:67
  44.1 23.4 %collective-permute-start.17 = (bf16[2,4,4,16,896]{4,3,2,1,0:T(8,128)(2,1)S(1)}, bf16[2,4,4,16,896]{4,3,2,1,0:T(8,128)(2,1)S(1)}, u32[]{:S(2)}, u32[]{:S(2)}) collective-permute-start(bf16[2,4,4,16,896]{4,3,2,1,0:T(8,128)(2,1)S(1)} %bitcast_dynamic-update-slice_fusion.3.refs_2_), channel_id=1, source_target_pairs={{0,17},{1,0},{2,19},{3,2},{4,21},{5,4},{6,23},{7,6},{8,9},{9,24},{... | collective-permute-start | bytes 2752520 | tf_op jit(solution)/shard_map/ppermute | solution.py:67
  51.8 17.4 %collective-permute-start.20 = (bf16[2,2,4,32,896]{4,3,2,1,0:T(8,128)(2,1)S(1)}, bf16[2,2,4,32,896]{4,3,2,1,0:T(8,128)(2,1)S(1)}, u32[]{:S(2)}, u32[]{:S(2)}) collective-permute-start(bf16[2,2,4,32,896]{4,3,2,1,0:T(8,128)(2,1)S(1)} %get-tuple-element.65.refs_0_), channel_id=1, source_target_pairs={{0,96},{1,97},{2,98},{3,99},{4,100},{5,101},{6,102},{7,103},{8,14}... | collective-permute-start | bytes 2752520 | tf_op jit(solution)/shard_map/ppermute | solution.py:67
  55.0 14.2 %collective-permute-start.19 = (bf16[2,2,4,32,896]{4,3,2,1,0:T(8,128)(2,1)S(1)}, bf16[2,2,4,32,896]{4,3,2,1,0:T(8,128)(2,1)S(1)}, u32[]{:S(2)}, u32[]{:S(2)}) collective-permute-start(bf16[2,2,4,32,896]{4,3,2,1,0:T(8,128)(2,1)S(1)} %get-tuple-element.64.refs_1_), channel_id=1, source_target_pairs={{0,32},{1,33},{2,34},{3,35},{4,36},{5,37},{6,38},{7,39},{8,10},{9,... | collective-permute-start | bytes 2752520 | tf_op jit(solution)/shard_map/ppermute | solution.py:67
  67.5 12.5 %collective-permute-start.18 = (bf16[2,4,4,16,896]{4,3,2,1,0:T(8,128)(2,1)S(1)}, bf16[2,4,4,16,896]{4,3,2,1,0:T(8,128)(2,1)S(1)}, u32[]{:S(2)}, u32[]{:S(2)}) collective-permute-start(bf16[2,4,4,16,896]{4,3,2,1,0:T(8,128)(2,1)S(1)} %collective-permute-done.15.refs_5_), channel_id=1, source_target_pairs={{0,1},{1,16},{2,3},{3,18},{4,5},{5,20},{6,7},{7,22},{8,25},{9,8},{... | collective-permute-start | bytes 2752520 | tf_op jit(solution)/shard_map/ppermute | solution.py:67
  67.5 12.5 %collective-permute-start.16 = (bf16[2,2,4,32,896]{4,3,2,1,0:T(8,128)(2,1)S(1)}, bf16[2,2,4,32,896]{4,3,2,1,0:T(8,128)(2,1)S(1)}, u32[]{:S(2)}, u32[]{:S(2)}) collective-permute-start(bf16[2,2,4,32,896]{4,3,2,1,0:T(8,128)(2,1)S(1)} %collective-permute-done.14.refs_7_), channel_id=1, source_target_pairs={{0,96},{1,97},{2,98},{3,99},{4,100},{5,101},{6,102},{7,103},{8,14}... | collective-permute-start | bytes 2752520 | tf_op jit(solution)/shard_map/ppermute | solution.py:67
  69.2 13.8 %collective-permute-start.13 = (bf16[2,2,4,32,896]{4,3,2,1,0:T(8,128)(2,1)S(1)}, bf16[2,2,4,32,896]{4,3,2,1,0:T(8,128)(2,1)S(1)}, u32[]{:S(2)}, u32[]{:S(2)}) collective-permute-start(bf16[2,2,4,32,896]{4,3,2,1,0:T(8,128)(2,1)S(1)} %collective-permute-done.12.refs_3_), channel_id=1, source_target_pairs={{0,32},{1,33},{2,34},{3,35},{4,36},{5,37},{6,38},{7,39},{8,10},{9,... | collective-permute-start | bytes 2752520 | tf_op jit(solution)/shard_map/ppermute | solution.py:67
  84.7 8.0 %collective-permute-start.21 = (bf16[768,896]{1,0:T(8,128)(2,1)S(1)}, bf16[768,896]{1,0:T(8,128)(2,1)S(1)}, u32[]{:S(2)}, u32[]{:S(2)}) collective-permute-start(bf16[768,896]{1,0:T(8,128)(2,1)S(1)} %bitcast.70), channel_id=1, source_target_pairs={{0,8},{1,9},{2,10},{3,11},{4,12},{5,13},{6,14},{7,15},{8,0},{9,1},... | collective-permute-start | bytes 4128776 | tf_op jit(solution)/shard_map/ppermute | solution.py:67
  92.6 2.1 copy-start.1
  92.6 4.5 %copy-start = (bf16[1,96,128,128]{3,2,1,0:T(8,128)(2,1)S(1)}, bf16[1,96,128,128]{3,2,1,0:T(8,128)(2,1)}, u32[]{:S(2)}) copy-start(bf16[1,96,128,128]{3,2,1,0:T(8,128)(2,1)} %param.6) | copy-start | bytes 9437188
  94.7 18.6 %collective-permute-start.22 = (bf16[416,896]{1,0:T(8,128)(2,1)S(1)}, bf16[416,896]{1,0:T(8,128)(2,1)S(1)}, u32[]{:S(2)}, u32[]{:S(2)}) collective-permute-start(bf16[416,896]{1,0:T(8,128)(2,1)S(1)} %get-tuple-element.72), channel_id=1, source_target_pairs={{0,1},{1,0},{2,3},{3,2},{4,5},{5,4},{6,7},{7,6},{8,9},{9,8},{10,11... | collective-permute-start | bytes 2236424 | tf_op jit(solution)/shard_map/ppermute | solution.py:67
  101.7 1.8 copy-start.2
  103.5 10.5 %collective-permute-start.30 = (bf16[208,896]{1,0:T(8,128)(2,1)S(1)}, bf16[208,896]{1,0:T(8,128)(2,1)S(1)}, u32[]{:S(2)}, u32[]{:S(2)}) collective-permute-start(bf16[208,896]{1,0:T(8,128)(2,1)S(1)} %get-tuple-element.78), channel_id=1, source_target_pairs={{0,2},{1,3},{2,4},{3,5},{4,6},{5,7},{6,0},{7,1},{8,14},{9,15},{10,... | collective-permute-start | bytes 1118216 | tf_op jit(solution)/shard_map/ppermute | solution.py:67
  103.6 12.7 %collective-permute-start.31 = (bf16[208,896]{1,0:T(8,128)(2,1)S(1)}, bf16[208,896]{1,0:T(8,128)(2,1)S(1)}, u32[]{:S(2)}, u32[]{:S(2)}) collective-permute-start(bf16[208,896]{1,0:T(8,128)(2,1)S(1)} %get-tuple-element.79), channel_id=1, source_target_pairs={{0,6},{1,7},{2,0},{3,1},{4,2},{5,3},{6,4},{7,5},{8,10},{9,11},{10,... | collective-permute-start | bytes 1118216 | tf_op jit(solution)/shard_map/ppermute | solution.py:67
  107.2 16.5 %collective-permute-start.32 = (bf16[208,896]{1,0:T(8,128)(2,1)S(1)}, bf16[208,896]{1,0:T(8,128)(2,1)S(1)}, u32[]{:S(2)}, u32[]{:S(2)}) collective-permute-start(bf16[208,896]{1,0:T(8,128)(2,1)S(1)} %get-tuple-element.80), channel_id=1, source_target_pairs={{0,4},{1,5},{2,6},{3,7},{4,0},{5,1},{6,2},{7,3},{8,12},{9,13},{10,... | collective-permute-start | bytes 1118216 | tf_op jit(solution)/shard_map/ppermute | solution.py:67
  124.0 9.2 %collective-permute-start.33 = (bf16[104,896]{1,0:T(8,128)(2,1)S(1)}, bf16[104,896]{1,0:T(8,128)(2,1)S(1)}, u32[]{:S(2)}, u32[]{:S(2)}) collective-permute-start(bf16[104,896]{1,0:T(8,128)(2,1)S(1)} %get-tuple-element.86), channel_id=1, source_target_pairs={{0,1},{1,0},{2,3},{3,2},{4,5},{5,4},{6,7},{7,6},{8,9},{9,8},{10,11... | collective-permute-start | bytes 559112 | tf_op jit(solution)/shard_map/ppermute | solution.py:67
  128.5 5.5 %collective-permute-start.23 = (bf16[104,896]{1,0:T(8,128)(2,1)S(1)}, bf16[104,896]{1,0:T(8,128)(2,1)S(1)}, u32[]{:S(2)}, u32[]{:S(2)}) collective-permute-start(bf16[104,896]{1,0:T(8,128)(2,1)S(1)} %get-tuple-element.74), channel_id=1, source_target_pairs={{0,2},{1,3},{2,4},{3,5},{4,6},{5,7},{6,0},{7,1},{8,14},{9,15},{10,... | collective-permute-start | bytes 559112 | tf_op jit(solution)/shard_map/ppermute | solution.py:67
  128.6 6.7 %collective-permute-start.24 = (bf16[104,896]{1,0:T(8,128)(2,1)S(1)}, bf16[104,896]{1,0:T(8,128)(2,1)S(1)}, u32[]{:S(2)}, u32[]{:S(2)}) collective-permute-start(bf16[104,896]{1,0:T(8,128)(2,1)S(1)} %get-tuple-element.75), channel_id=1, source_target_pairs={{0,6},{1,7},{2,0},{3,1},{4,2},{5,3},{6,4},{7,5},{8,10},{9,11},{10,... | collective-permute-start | bytes 559112 | tf_op jit(solution)/shard_map/ppermute | solution.py:67
  130.0 9.6 %collective-permute-start.25 = (bf16[104,896]{1,0:T(8,128)(2,1)S(1)}, bf16[104,896]{1,0:T(8,128)(2,1)S(1)}, u32[]{:S(2)}, u32[]{:S(2)}) collective-permute-start(bf16[104,896]{1,0:T(8,128)(2,1)S(1)} %get-tuple-element.76), channel_id=1, source_target_pairs={{0,4},{1,5},{2,6},{3,7},{4,0},{5,1},{6,2},{7,3},{8,12},{9,13},{10,... | collective-permute-start | bytes 559112 | tf_op jit(solution)/shard_map/ppermute | solution.py:67
  139.9 2.3 %collective-permute-start.26 = (bf16[104,896]{1,0:T(8,128)(2,1)S(1)}, bf16[104,896]{1,0:T(8,128)(2,1)S(1)}, u32[]{:S(2)}, u32[]{:S(2)}) collective-permute-start(bf16[104,896]{1,0:T(8,128)(2,1)S(1)} %get-tuple-element.112), channel_id=1, source_target_pairs={{0,8},{1,9},{2,10},{3,11},{4,12},{5,13},{6,14},{7,15},{8,0},{9,1},... | collective-permute-start | bytes 559112 | tf_op jit(solution)/shard_map/ppermute | solution.py:67
  141.2 1.4 collective-permute-start.34
  142.9 6.1 %collective-permute-start.35 = (bf16[104,896]{1,0:T(8,128)(2,1)S(1)}, bf16[104,896]{1,0:T(8,128)(2,1)S(1)}, u32[]{:S(2)}, u32[]{:S(2)}) collective-permute-start(bf16[104,896]{1,0:T(8,128)(2,1)S(1)} %get-tuple-element.98), channel_id=1, source_target_pairs={{0,1},{1,0},{2,3},{3,2},{4,5},{5,4},{6,7},{7,6},{8,9},{9,8},{10,11... | collective-permute-start | bytes 559112 | tf_op jit(solution)/shard_map/ppermute | solution.py:67
  143.1 5.9 %collective-permute-start.27 = (bf16[104,896]{1,0:T(8,128)(2,1)S(1)}, bf16[104,896]{1,0:T(8,128)(2,1)S(1)}, u32[]{:S(2)}, u32[]{:S(2)}) collective-permute-start(bf16[104,896]{1,0:T(8,128)(2,1)S(1)} %get-tuple-element.110), channel_id=1, source_target_pairs={{0,2},{1,3},{2,4},{3,5},{4,6},{5,7},{6,0},{7,1},{8,14},{9,15},{10,... | collective-permute-start | bytes 559112 | tf_op jit(solution)/shard_map/ppermute | solution.py:67
  145.1 10.6 %collective-permute-start.28 = (bf16[104,896]{1,0:T(8,128)(2,1)S(1)}, bf16[104,896]{1,0:T(8,128)(2,1)S(1)}, u32[]{:S(2)}, u32[]{:S(2)}) collective-permute-start(bf16[104,896]{1,0:T(8,128)(2,1)S(1)} %get-tuple-element.110), channel_id=1, source_target_pairs={{0,6},{1,7},{2,0},{3,1},{4,2},{5,3},{6,4},{7,5},{8,10},{9,11},{10,... | collective-permute-start | bytes 559112 | tf_op jit(solution)/shard_map/ppermute | solution.py:67
  145.1 10.7 %collective-permute-start.29 = (bf16[104,896]{1,0:T(8,128)(2,1)S(1)}, bf16[104,896]{1,0:T(8,128)(2,1)S(1)}, u32[]{:S(2)}, u32[]{:S(2)}) collective-permute-start(bf16[104,896]{1,0:T(8,128)(2,1)S(1)} %get-tuple-element.110), channel_id=1, source_target_pairs={{0,4},{1,5},{2,6},{3,7},{4,0},{5,1},{6,2},{7,3},{8,12},{9,13},{10,... | collective-permute-start | bytes 559112 | tf_op jit(solution)/shard_map/ppermute | solution.py:67
  155.8 20.8 %collective-permute-start.36 = (bf16[416,896]{1,0:T(8,128)(2,1)S(1)}, bf16[416,896]{1,0:T(8,128)(2,1)S(1)}, u32[]{:S(2)}, u32[]{:S(2)}) collective-permute-start(bf16[416,896]{1,0:T(8,128)(2,1)S(1)} %constant_dynamic-update-slice_fusion.6.refs_2_), channel_id=1, source_target_pairs={{0,1},{1,0},{2,3},{3,2},{4,5},{5,4},{6,7},{7,6},{8,9},{9,8},{10,11... | collective-permute-start | bytes 2236424 | tf_op jit(solution)/shard_map/ppermute | solution.py:67
  157.2 9.4 %collective-permute-start.37 = (bf16[208,896]{1,0:T(8,128)(2,1)S(1)}, bf16[208,896]{1,0:T(8,128)(2,1)S(1)}, u32[]{:S(2)}, u32[]{:S(2)}) collective-permute-start(bf16[208,896]{1,0:T(8,128)(2,1)S(1)} %constant_dynamic-update-slice_fusion.4.refs_4_), channel_id=1, source_target_pairs={{0,2},{1,3},{2,4},{3,5},{4,6},{5,7},{6,0},{7,1},{8,14},{9,15},{10,... | collective-permute-start | bytes 1118216 | tf_op jit(solution)/shard_map/ppermute | solution.py:67
  157.5 19.1 %collective-permute-start.38 = (bf16[208,896]{1,0:T(8,128)(2,1)S(1)}, bf16[208,896]{1,0:T(8,128)(2,1)S(1)}, u32[]{:S(2)}, u32[]{:S(2)}) collective-permute-start(bf16[208,896]{1,0:T(8,128)(2,1)S(1)} %constant_dynamic-update-slice_fusion.4.refs_4_), channel_id=1, source_target_pairs={{0,6},{1,7},{2,0},{3,1},{4,2},{5,3},{6,4},{7,5},{8,10},{9,11},{10,... | collective-permute-start | bytes 1118216 | tf_op jit(solution)/shard_map/ppermute | solution.py:67
  158.7 17.9 %collective-permute-start.39 = (bf16[208,896]{1,0:T(8,128)(2,1)S(1)}, bf16[208,896]{1,0:T(8,128)(2,1)S(1)}, u32[]{:S(2)}, u32[]{:S(2)}) collective-permute-start(bf16[208,896]{1,0:T(8,128)(2,1)S(1)} %constant_dynamic-update-slice_fusion.4.refs_4_), channel_id=1, source_target_pairs={{0,4},{1,5},{2,6},{3,7},{4,0},{5,1},{6,2},{7,3},{8,12},{9,13},{10,... | collective-permute-start | bytes 1118216 | tf_op jit(solution)/shard_map/ppermute | solution.py:67
  182.4 3.9 %collective-permute-start.40 = (f32[416,768]{1,0:T(8,128)S(1)}, f32[416,768]{1,0:T(8,128)S(1)}, u32[]{:S(2)}, u32[]{:S(2)}) collective-permute-start(f32[416,768]{1,0:T(8,128)S(1)} %get-tuple-element.90), channel_id=1, source_target_pairs={{0,8},{1,9},{2,10},{3,11},{4,12},{5,13},{6,14},{7,15},{8,0},{9,1},... | collective-permute-start | bytes 3833864 | tf_op jit(solution)/shard_map/ppermute | solution.py:67
  186.4 5.3 %collective-permute-start.41 = (bf16[104,768]{1,0:T(8,128)(2,1)S(1)}, bf16[104,768]{1,0:T(8,128)(2,1)S(1)}, u32[]{:S(2)}, u32[]{:S(2)}) collective-permute-start(bf16[104,768]{1,0:T(8,128)(2,1)S(1)} %get-tuple-element.92), channel_id=1, source_target_pairs={{0,32},{1,33},{2,34},{3,35},{4,36},{5,37},{6,38},{7,39},{8,104},{9... | collective-permute-start | bytes 479240 | tf_op jit(solution)/shard_map/ppermute | solution.py:67
  188.2 9.6 %collective-permute-start.42 = (bf16[104,768]{1,0:T(8,128)(2,1)S(1)}, bf16[104,768]{1,0:T(8,128)(2,1)S(1)}, u32[]{:S(2)}, u32[]{:S(2)}) collective-permute-start(bf16[104,768]{1,0:T(8,128)(2,1)S(1)} %get-tuple-element.93), channel_id=1, source_target_pairs={{0,96},{1,97},{2,98},{3,99},{4,100},{5,101},{6,102},{7,103},{8,40}... | collective-permute-start | bytes 479240 | tf_op jit(solution)/shard_map/ppermute | solution.py:67
  188.2 9.6 %collective-permute-start.43 = (bf16[104,768]{1,0:T(8,128)(2,1)S(1)}, bf16[104,768]{1,0:T(8,128)(2,1)S(1)}, u32[]{:S(2)}, u32[]{:S(2)}) collective-permute-start(bf16[104,768]{1,0:T(8,128)(2,1)S(1)} %get-tuple-element.94), channel_id=1, source_target_pairs={{0,64},{1,65},{2,66},{3,67},{4,68},{5,69},{6,70},{7,71},{8,72},{9,... | collective-permute-start | bytes 479240 | tf_op jit(solution)/shard_map/ppermute | solution.py:67
  197.9 10.1 %collective-permute-start.44 = (f32[104,768]{1,0:T(8,128)S(1)}, f32[104,768]{1,0:T(8,128)S(1)}, u32[]{:S(2)}, u32[]{:S(2)}) collective-permute-start(f32[104,768]{1,0:T(8,128)S(1)} %add_add_fusion), channel_id=1, source_target_pairs={{0,16},{1,17},{2,18},{3,19},{4,20},{5,21},{6,22},{7,23},{8,24},{9,... | collective-permute-start | bytes 958472 | tf_op jit(solution)/shard_map/ppermute | solution.py:67
  208.1 4.2 %collective-permute-start.45 = (bf16[104,768]{1,0:T(8,128)(2,1)S(1)}, bf16[104,768]{1,0:T(8,128)(2,1)S(1)}, u32[]{:S(2)}, u32[]{:S(2)}) collective-permute-start(bf16[104,768]{1,0:T(8,128)(2,1)S(1)} %get-tuple-element.96), channel_id=1, source_target_pairs={{0,32},{1,33},{2,34},{3,35},{4,36},{5,37},{6,38},{7,39},{8,104},{9... | collective-permute-start | bytes 479240 | tf_op jit(solution)/shard_map/ppermute | solution.py:67
  208.2 5.4 %collective-permute-start.46 = (bf16[104,768]{1,0:T(8,128)(2,1)S(1)}, bf16[104,768]{1,0:T(8,128)(2,1)S(1)}, u32[]{:S(2)}, u32[]{:S(2)}) collective-permute-start(bf16[104,768]{1,0:T(8,128)(2,1)S(1)} %get-tuple-element.96), channel_id=1, source_target_pairs={{0,96},{1,97},{2,98},{3,99},{4,100},{5,101},{6,102},{7,103},{8,40}... | collective-permute-start | bytes 479240 | tf_op jit(solution)/shard_map/ppermute | solution.py:67
  209.6 8.9 %collective-permute-start.47 = (bf16[104,768]{1,0:T(8,128)(2,1)S(1)}, bf16[104,768]{1,0:T(8,128)(2,1)S(1)}, u32[]{:S(2)}, u32[]{:S(2)}) collective-permute-start(bf16[104,768]{1,0:T(8,128)(2,1)S(1)} %get-tuple-element.96), channel_id=1, source_target_pairs={{0,64},{1,65},{2,66},{3,67},{4,68},{5,69},{6,70},{7,71},{8,72},{9,... | collective-permute-start | bytes 479240 | tf_op jit(solution)/shard_map/ppermute | solution.py:67
  218.5 3.6 %collective-permute-start.48 = (bf16[416,768]{1,0:T(8,128)(2,1)S(1)}, bf16[416,768]{1,0:T(8,128)(2,1)S(1)}, u32[]{:S(2)}, u32[]{:S(2)}) collective-permute-start(bf16[416,768]{1,0:T(8,128)(2,1)S(1)} %constant_dynamic-update-slice_fusion.own), channel_id=1, source_target_pairs={{0,8},{1,9},{2,10},{3,11},{4,12},{5,13},{6,14},{7,15},{8,0},{9,1},... | collective-permute-start | bytes 1916936 | tf_op jit(solution)/shard_map/ppermute | solution.py:67

commit v9 on v8

--- a/solution.py
+++ b/solution.py
@@ -21,6 +21,8 @@
 OWN = 48
 STEP = 4
 UNROLL = 3
+FIELDS = 1 + 2 * STEP
+MOST = SLOTS // STEP + ROW_BLOCKS + UNROLL
 MAIN = 32
 PARTS = 24
 bf16, f32 = jnp.bfloat16, jnp.float32
@@ -155,51 +157,72 @@
     )(*far, panels)
 
 
-def list_steps(q, meta, order, counts, steps):
-    def clear(i, carry):
-        counts[i] = 0
-        return carry
-
-    lax.fori_loop(0, ROW_BLOCKS, clear, 0)
-
-    def put(s, carry):
-        group = meta[q, s]
-        n = counts[group]
-        order[group, n] = s
-        counts[group] = n + 1
-        return carry
-
-    lax.fori_loop(0, meta[q, 2 * SLOTS], put, 0)
-
-    def list_group(group, base):
-        n = counts[group]
-        for i in range(STEP):
-            order[group, n + i] = SLOTS
-        many = (n + STEP - 1) // STEP
-
-        def list_step(i, carry):
-            steps[base + i, 0] = group
+def plan_kernel(meta, steps, order, counts):
+    for q in range(2):
+
+        def clear(i, carry):
+            counts[i] = 0
+            return carry
+
+        lax.fori_loop(0, ROW_BLOCKS, clear, 0)
+
+        def put(s, carry):
+            group = meta[q, s]
+            n = counts[group]
+            order[group, n] = s
+            counts[group] = n + 1
+            return carry
+
+        lax.fori_loop(0, meta[q, 2 * SLOTS], put, 0)
+
+        def list_group(group, base):
+            n = counts[group]
+            for i in range(STEP):
+                order[group, n + i] = SLOTS
+            many = (n + STEP - 1) // STEP
+
+            def list_step(i, carry):
+                at = (base + i) * FIELDS
+                steps[q, at] = group
+                for k in range(STEP):
+                    s = order[group, i * STEP + k]
+                    steps[q, at + 1 + k] = s
+                    steps[q, at + 1 + STEP + k] = jnp.where(s < SLOTS, meta[q, SLOTS + s], 0)
+                return carry
+
+            lax.fori_loop(0, many, list_step, 0)
+            return base + many
+
+        many = lax.fori_loop(0, ROW_BLOCKS, list_group, 0)
+        for u in range(UNROLL - 1):
+            at = (many + u) * FIELDS
+            steps[q, at] = ROW_BLOCKS
             for k in range(STEP):
-                s = order[group, i * STEP + k]
-                steps[base + i, 1 + k] = s
-                steps[base + i, 1 + STEP + k] = jnp.where(s < SLOTS, meta[q, SLOTS + s], 0)
-            return carry
-
-        lax.fori_loop(0, many, list_step, 0)
-        return base + many
-
-    many = lax.fori_loop(0, ROW_BLOCKS, list_group, 0)
-    for u in range(UNROLL - 1):
-        steps[many + u, 0] = ROW_BLOCKS
-        for k in range(STEP):
-            steps[many + u, 1 + k] = SLOTS
-            steps[many + u, 1 + STEP + k] = 0
-    return many
-
-
-def multiply_kernel(q, meta, factors, held, out, total, order, counts, steps):
+                steps[q, at + 1 + k] = SLOTS
+                steps[q, at + 1 + STEP + k] = 0
+        steps[q, MOST * FIELDS] = many
+
+
+def plan(meta):
+    smem = pl.BlockSpec(memory_space=pltpu.SMEM)
+    return pl.pallas_call(
+        plan_kernel,
+        out_shape=jax.ShapeDtypeStruct((2, MOST * FIELDS + 1), jnp.int32),
+        in_specs=[smem],
+        out_specs=smem,
+        scratch_shapes=[
+            pltpu.SMEM((ROW_BLOCKS, SLOTS + 2 * STEP), jnp.int32),
+            pltpu.SMEM((ROW_BLOCKS,), jnp.int32),
+        ],
+        compiler_params=pltpu.CompilerParams(vmem_limit_bytes=2**20),
+        cost_estimate=pl.CostEstimate(flops=2**31, bytes_accessed=2**12, transcendentals=0),
+        name="plan",
+    )(meta)
+
+
+def multiply_kernel(q, steps, factors, held, out, total):
     total[...] = jnp.zeros_like(total)
-    many = list_steps(q, meta, order, counts, steps)
+    many = steps[q, MOST * FIELDS]
     panels = held.reshape(NB, WIDE)
 
     def some(i, carry):
@@ -207,16 +230,16 @@
         for u in range(UNROLL):
             left, right = [], []
             for k in range(STEP):
-                slot = steps[i * UNROLL + u, 1 + k]
+                slot = steps[q, (i * UNROLL + u) * FIELDS + 1 + k]
                 block = factors[jnp.minimum(slot, SLOTS - 1)]
                 left.append(jnp.where(slot < SLOTS, block, jnp.zeros_like(block)))
-                column = steps[i * UNROLL + u, 1 + STEP + k]
+                column = steps[q, (i * UNROLL + u) * FIELDS + 1 + STEP + k]
                 right.append(panels[pl.ds(pl.multiple_of(column * BLK, BLK), BLK), :])
             products.append(
                 jnp.dot(jnp.concatenate(left, axis=1), jnp.concatenate(right, axis=0), preferred_element_type=f32)
             )
         for u in range(UNROLL):
-            total[steps[i * UNROLL + u, 0]] += products[u]
+            total[steps[q, (i * UNROLL + u) * FIELDS]] += products[u]
         return carry
 
     lax.fori_loop(0, (many + UNROLL - 1) // UNROLL, some, 0)
@@ -224,8 +247,7 @@
         out[group * BLK : (group + 1) * BLK, :] = total[group].astype(bf16)
 
 
-def multiply(q, meta, factors, panels):
-    most = SLOTS // STEP + ROW_BLOCKS + UNROLL
+def multiply(q, steps, factors, panels):
     vmem = pl.BlockSpec(memory_space=pltpu.VMEM)
 
     def kernel(*refs):
@@ -238,14 +260,11 @@
         out_specs=vmem,
         scratch_shapes=[
             pltpu.VMEM((ROW_BLOCKS + 1, BLK, WIDE), f32),
-            pltpu.SMEM((ROW_BLOCKS, SLOTS + 2 * STEP), jnp.int32),
-            pltpu.SMEM((ROW_BLOCKS,), jnp.int32),
-            pltpu.SMEM((most, 1 + 2 * STEP), jnp.int32),
         ],
         compiler_params=pltpu.CompilerParams(vmem_limit_bytes=24 * 1024 * 1024),
         cost_estimate=pl.CostEstimate(flops=96 * 2 * 128 * 128 * 896, bytes_accessed=2**23, transcendentals=0),
         name="multiply",
-    )(meta, factors, panels)
+    )(steps, factors, panels)
 
 
 def cross_kernel(starts, half, slab, theirs, *refs):
@@ -476,8 +495,9 @@
     behind_1 = send(mains[1], behind)
     rest_ahead = send(rest, around(zz, 1, True))
     rest_behind = send(rest, around(zz, -1, True))
-    ahead_1 = send_after(mains[1], ahead, ahead_0)
-    behind_0 = send_after(mains[0], behind, behind_1)
+    steps = plan(meta)
+    ahead_1 = send_after(mains[1], ahead, ahead_0, steps)
+    behind_0 = send_after(mains[0], behind, behind_1, steps)
     far_0 = send(ahead_0, ahead)
     far_1 = send_after(behind_1, behind, rest_ahead)
     rest_far = send_after(rest_ahead, around(zz, 1, True), rest_behind)
@@ -485,7 +505,7 @@
     panels, slab = panels_and_slab(near, (far_0, far_1, rest_far))
     slab = slab.reshape(ROWS, WIDE)
     theirs = swap_cores(slab)
-    second_half = multiply(1, meta, other_blocks, panels)
+    second_half = multiply(1, steps, other_blocks, panels)
 
     def add(*arrays):
         return sum(a.astype(f32) for a in arrays)
@@ -496,7 +516,7 @@
     half_mine, to_low = cross(chunks_low, 2, second_half, slab, theirs)
     from_low = swap_low(to_low)
     panels, half_mine = lax.optimization_barrier((panels, half_mine))
-    first_half = multiply(0, meta, own_blocks, panels)
+    first_half = multiply(0, steps, own_blocks, panels)
     mine, to_ahead, to_behind, to_far = cross(chunks_x, 4, first_half, slab, theirs)
     parts = (mine, send(to_ahead, ahead), send(to_behind, behind), send(to_far, opposite))
     own, *sent = sum_chunks(chunks_x, 4, half_mine, from_low)

time: 224 us -> 219 us (0.978)
  starting transfers between devices: 67.5 us -> 53.4 us
  Pallas kernels: 28.8 us -> 35 us
    ppermute x49, starting transfers between devices: 67.5 us -> 53.4 us  [send(): return lax.ppermute(array, AXES, pairs)]
    pallas_call x0 -> x1, Pallas kernels: none -> 5.43 us  [plan(): pl.pallas_call(plan_kernel, out_shape=jax.ShapeDtypeStruct((2, MOST * FIE...]
    ppermute x49, waiting for transfers between devices: 122 us -> 124 us  [send(): return lax.ppermute(array, AXES, pairs)]
  transfers between devices with their start and end apart: 49 -> 49, of which waited for: 36 -> 34; matrix products, arithmetic and copies ran while one was open for 1% -> 1% of each run, Pallas kernels for 8% -> 11%
where the time goes in v9:
time: 219 us; the launch traced here: 218 us
  waiting for transfers between devices  124 us (57%)
  starting transfers between devices  53.4 us (24%)
  Pallas kernels  35 us (16%)
  other arithmetic  2.57 us (1%)
  local copies, waits for them, and re-layouts  2.25 us (1%)
    ppermute x49, waiting for transfers between devices, send(): return lax.ppermute(array, AXES, pairs)  124 us
    ppermute x49, starting transfers between devices, send(): return lax.ppermute(array, AXES, pairs)  53.4 us
    pallas_call x2, Pallas kernels, multiply(): pl.pallas_call(kernel, out_shape=jax.ShapeDtypeStruct((ROWS, WIDE), bf16)...  10.8 us
    pallas_call x1, Pallas kernels, exchange(): pl.pallas_call(exchange_kernel, out_shape=[jax.ShapeDtypeStruct((CROSS //...  5.74 us
    pallas_call x1, Pallas kernels, plan(): pl.pallas_call(plan_kernel, out_shape=jax.ShapeDtypeStruct((2, MOST * FIE...  5.43 us
    pallas_call x1, Pallas kernels, panels_and_slab(): pl.pallas_call(near_kernel, out_shape=held, in_specs=[anywhere] * 9, out_...  5.12 us
  transfers between devices with their start and end apart: 49, of which 34 were waited for; matrix products, arithmetic and copies ran while one was open for 1% of the time, Pallas kernels for 11%

profile of v9, /device:TPU:1, one launch (start us, length us, event | category | flops | bytes accessed | tf_op | source)
XLA Modules:
  0.0 218.4 jit_solution(16726381167941731590)
XLA Ops:
  0.0 0.9 broadcast_select_fusion.2
  0.9 1.5 collective-permute-start
  2.4 0.9 collective-permute-done
  4.7 1.4 collective-permute-start.1
  6.8 1.9 collective-permute-start.2
  8.7 1.3 collective-permute-start.3
  10.9 0.9 bitcast_dynamic-update-slice_fusion.7
  11.8 1.1 collective-permute-done.2
  12.9 1.8 collective-permute-done.3
  14.9 3.8 %collective-permute-start.5 = (bf16[2,4,32,896]{3,2,1,0:T(8,128)(2,1)S(1)}, bf16[2,4,32,896]{3,2,1,0:T(8,128)(2,1)S(1)}, u32[]{:S(2)}, u32[]{:S(2)}) collective-permute-start(bf16[2,4,32,896]{3,2,1,0:T(8,128)(2,1)S(1)} %slice.39), channel_id=1, source_target_pairs={{0,1},{1,16},{2,3},{3,18},{4,5},{5,20},{6,7},{7,22},{8,25},{9,8},{... | collective-permute-start | bytes 1376264 | tf_op jit(solution)/shard_map/ppermute | solution.py:69
  18.9 5.2 %collective-permute-done.5 = bf16[2,4,32,896]{3,2,1,0:T(8,128)(2,1)S(1)} collective-permute-done((bf16[2,4,32,896]{3,2,1,0:T(8,128)(2,1)S(1)}, bf16[2,4,32,896]{3,2,1,0:T(8,128)(2,1)S(1)}, u32[]{:S(2)}, u32[]{:S(2)}) %collective-permute-start.5) | collective-permute-done | bytes 458784 | tf_op jit(solution)/shard_map/ppermute | solution.py:69
  24.1 2.5 %collective-permute-start.6 = (s32[1,256]{1,0:T(1,128)S(1)}, s32[1,256]{1,0:T(1,128)S(1)}, u32[]{:S(2)}, u32[]{:S(2)}) collective-permute-start(s32[1,256]{1,0:T(1,128)S(1)} %bitcast.73), channel_id=1, source_target_pairs={{0,8},{1,9},{2,10},{3,11},{4,12},{5,13},{6,14},{7,15},{8,0},{9,1},... | collective-permute-start | bytes 3080 | tf_op jit(solution)/shard_map/ppermute | solution.py:69
  26.6 2.7 %collective-permute-start.8 = (bf16[2,4,32,896]{3,2,1,0:T(8,128)(2,1)S(1)}, bf16[2,4,32,896]{3,2,1,0:T(8,128)(2,1)S(1)}, u32[]{:S(2)}, u32[]{:S(2)}) collective-permute-start(bf16[2,4,32,896]{3,2,1,0:T(8,128)(2,1)S(1)} %collective-permute-done.5), channel_id=1, source_target_pairs={{0,1},{1,16},{2,3},{3,18},{4,5},{5,20},{6,7},{7,22},{8,25},{9,8},{... | collective-permute-start | bytes 1376264 | tf_op jit(solution)/shard_map/ppermute | solution.py:69
  29.9 2.2 %collective-permute-start.10 = (bf16[2,4,16,896]{3,2,1,0:T(8,128)(2,1)S(1)}, bf16[2,4,16,896]{3,2,1,0:T(8,128)(2,1)S(1)}, u32[]{:S(2)}, u32[]{:S(2)}) collective-permute-start(bf16[2,4,16,896]{3,2,1,0:T(8,128)(2,1)S(1)} %slice.38), channel_id=1, source_target_pairs={{0,96},{1,97},{2,98},{3,99},{4,100},{5,101},{6,102},{7,103},{8,14}... | collective-permute-start | bytes 688136 | tf_op jit(solution)/shard_map/ppermute | solution.py:69
  32.5 3.3 %collective-permute-done.9 = bf16[2,4,16,896]{3,2,1,0:T(8,128)(2,1)S(1)} collective-permute-done((bf16[2,4,16,896]{3,2,1,0:T(8,128)(2,1)S(1)}, bf16[2,4,16,896]{3,2,1,0:T(8,128)(2,1)S(1)}, u32[]{:S(2)}, u32[]{:S(2)}) %collective-permute-start.9) | collective-permute-done | bytes 229408 | tf_op jit(solution)/shard_map/ppermute | solution.py:69
  35.8 1.7 collective-permute-done.10
  37.6 1.2 collective-permute-done.11
  39.2 2.1 collective-permute-start.14
  41.2 2.9 %collective-permute-start.15 = (bf16[2,4,4,16,896]{4,3,2,1,0:T(8,128)(2,1)S(1)}, bf16[2,4,4,16,896]{4,3,2,1,0:T(8,128)(2,1)S(1)}, u32[]{:S(2)}, u32[]{:S(2)}) collective-permute-start(bf16[2,4,4,16,896]{4,3,2,1,0:T(8,128)(2,1)S(1)} %bitcast_dynamic-update-slice_fusion.3.refs_2_), channel_id=1, source_target_pairs={{0,1},{1,16},{2,3},{3,18},{4,5},{5,20},{6,7},{7,22},{8,25},{9,8},{... | collective-permute-start | bytes 2752520 | tf_op jit(solution)/shard_map/ppermute | solution.py:69
  44.1 5.4 %plan.1.refs_0_ = s32[2,298]{1,0:T(2,128)S(1)} custom-call(s32[2,256]{1,0:T(2,128)S(1)} %pad_add_fusion.meta), custom_call_target="tpu_custom_call" | custom-call | flops 2147483648 | bytes 4096 | tf_op jit(solution)/shard_map/plan/pallas_call | solution.py:208
  49.6 2.2 %collective-permute-done.14.refs_7_ = bf16[2,2,4,32,896]{4,3,2,1,0:T(8,128)(2,1)S(1)} collective-permute-done((bf16[2,2,4,32,896]{4,3,2,1,0:T(8,128)(2,1)S(1)}, bf16[2,2,4,32,896]{4,3,2,1,0:T(8,128)(2,1)S(1)}, u32[]{:S(2)}, u32[]{:S(2)}) %collective-permute-start.14) | collective-permute-done | bytes 917536 | tf_op jit(solution)/shard_map/ppermute | solution.py:69
  51.8 3.2 %collective-permute-start.20 = (bf16[2,2,4,32,896]{4,3,2,1,0:T(8,128)(2,1)S(1)}, bf16[2,2,4,32,896]{4,3,2,1,0:T(8,128)(2,1)S(1)}, u32[]{:S(2)}, u32[]{:S(2)}) collective-permute-start(bf16[2,2,4,32,896]{4,3,2,1,0:T(8,128)(2,1)S(1)} %get-tuple-element.65.refs_0_), channel_id=1, source_target_pairs={{0,96},{1,97},{2,98},{3,99},{4,100},{5,101},{6,102},{7,103},{8,14}... | collective-permute-start | bytes 2752520 | tf_op jit(solution)/shard_map/ppermute | solution.py:69
  55.0 6.0 %collective-permute-done.15.refs_5_ = bf16[2,4,4,16,896]{4,3,2,1,0:T(8,128)(2,1)S(1)} collective-permute-done((bf16[2,4,4,16,896]{4,3,2,1,0:T(8,128)(2,1)S(1)}, bf16[2,4,4,16,896]{4,3,2,1,0:T(8,128)(2,1)S(1)}, u32[]{:S(2)}, u32[]{:S(2)}) %collective-permute-start.15) | collective-permute-done | bytes 917536 | tf_op jit(solution)/shard_map/ppermute | solution.py:69
  61.0 6.4 %collective-permute-done.17.refs_8_ = bf16[2,4,4,16,896]{4,3,2,1,0:T(8,128)(2,1)S(1)} collective-permute-done((bf16[2,4,4,16,896]{4,3,2,1,0:T(8,128)(2,1)S(1)}, bf16[2,4,4,16,896]{4,3,2,1,0:T(8,128)(2,1)S(1)}, u32[]{:S(2)}, u32[]{:S(2)}) %collective-permute-start.17) | collective-permute-done | bytes 917536 | tf_op jit(solution)/shard_map/ppermute | solution.py:69
  67.5 1.7 collective-permute-start.16
  69.2 5.1 %near.1 = bf16[4,2,2,4,2,48,896]{6,5,4,3,2,1,0:T(8,128)(2,1)S(1)} custom-call(bf16[2,2,4,32,896]{4,3,2,1,0:T(8,128)(2,1)S(1)} %get-tuple-element.65.refs_0_, bf16[2,2,4,32,896]{4,3,2,1,0:T(8,128)(2,1)S(1)} %get-tuple-element.64.refs_1_, bf16[2,4,4,16,896]{4,3,2,1,0:T(8,128)(2,1)S(1)} %bitcast_dynamic-update-slice_fusion.3.refs_2_, ...), custom_call_target="tpu_custom_call" | custom-call | tf_op jit(solution)/shard_map/near/pallas_call | solution.py:139
  74.3 5.7 %collective-permute-done.18.rest = bf16[2,4,4,16,896]{4,3,2,1,0:T(8,128)(2,1)S(1)} collective-permute-done((bf16[2,4,4,16,896]{4,3,2,1,0:T(8,128)(2,1)S(1)}, bf16[2,4,4,16,896]{4,3,2,1,0:T(8,128)(2,1)S(1)}, u32[]{:S(2)}, u32[]{:S(2)}) %collective-permute-start.18) | collective-permute-done | bytes 917536 | tf_op jit(solution)/shard_map/ppermute | solution.py:69
  80.0 2.9 %collective-permute-done.13.main0 = bf16[2,2,4,32,896]{4,3,2,1,0:T(8,128)(2,1)S(1)} collective-permute-done((bf16[2,2,4,32,896]{4,3,2,1,0:T(8,128)(2,1)S(1)}, bf16[2,2,4,32,896]{4,3,2,1,0:T(8,128)(2,1)S(1)}, u32[]{:S(2)}, u32[]{:S(2)}) %collective-permute-start.13) | collective-permute-done | bytes 917536 | tf_op jit(solution)/shard_map/ppermute | solution.py:69
  82.9 1.7 far.1
  84.7 2.6 %collective-permute-start.21 = (bf16[768,896]{1,0:T(8,128)(2,1)S(1)}, bf16[768,896]{1,0:T(8,128)(2,1)S(1)}, u32[]{:S(2)}, u32[]{:S(2)}) collective-permute-start(bf16[768,896]{1,0:T(8,128)(2,1)S(1)} %bitcast.70), channel_id=1, source_target_pairs={{0,8},{1,9},{2,10},{3,11},{4,12},{5,13},{6,14},{7,15},{8,0},{9,1},... | collective-permute-start | bytes 4128776 | tf_op jit(solution)/shard_map/ppermute | solution.py:69
  87.2 5.5 %multiply.2.refs_0_.refs_1_ = bf16[768,896]{1,0:T(8,128)(2,1)S(1)} custom-call(s32[2,298]{1,0:T(2,128)S(1)} %plan.1.refs_0_, bf16[96,128,128]{2,1,0:T(8,128)(2,1)S(1)} %collective-permute-done.4.refs_1_, bf16[4,2,2,4,2,48,896]{6,5,4,3,2,1,0:T(8,128)(2,1)S(1)} %get-tuple-element.70.refs_2_), custom_call_target="tpu_custom_call" | custom-call | flops 2818572288 | bytes 8388608 | tf_op jit(solution)/shard_map/multiply/pallas_call | solution.py:256
  92.8 2.0 cross.2
  95.1 5.3 %multiply.3.refs_0_ = bf16[768,896]{1,0:T(8,128)(2,1)S(1)} custom-call(s32[2,298]{1,0:T(2,128)S(1)} %plan.1.refs_0_, bf16[96,128,128]{2,1,0:T(8,128)(2,1)S(1)} %bitcast.69, bf16[4,2,2,4,2,48,896]{6,5,4,3,2,1,0:T(8,128)(2,1)S(1)} %get-tuple-element.70.refs_2_), custom_call_target="tpu_custom_call" | custom-call | flops 2818572288 | bytes 8388608 | tf_op jit(solution)/shard_map/multiply/pallas_call | solution.py:256
  100.4 1.8 cross.3
  102.6 1.2 collective-permute-start.31
  104.7 8.5 %collective-permute-done.22.refs_1_ = bf16[416,896]{1,0:T(8,128)(2,1)S(1)} collective-permute-done((bf16[416,896]{1,0:T(8,128)(2,1)S(1)}, bf16[416,896]{1,0:T(8,128)(2,1)S(1)}, u32[]{:S(2)}, u32[]{:S(2)}) %collective-permute-start.22) | collective-permute-done | bytes 745504 | tf_op jit(solution)/shard_map/ppermute | solution.py:69
  113.5 8.8 %collective-permute-done.31.refs_2_ = bf16[208,896]{1,0:T(8,128)(2,1)S(1)} collective-permute-done((bf16[208,896]{1,0:T(8,128)(2,1)S(1)}, bf16[208,896]{1,0:T(8,128)(2,1)S(1)}, u32[]{:S(2)}, u32[]{:S(2)}) %collective-permute-start.31) | collective-permute-done | bytes 372768 | tf_op jit(solution)/shard_map/ppermute | solution.py:69
  122.7 1.3 collective-permute-start.33
  124.1 1.3 collective-permute-start.24
  125.4 2.9 %collective-permute-done.33 = bf16[104,896]{1,0:T(8,128)(2,1)S(1)} collective-permute-done((bf16[104,896]{1,0:T(8,128)(2,1)S(1)}, bf16[104,896]{1,0:T(8,128)(2,1)S(1)}, u32[]{:S(2)}, u32[]{:S(2)}) %collective-permute-start.33) | collective-permute-done | bytes 186400 | tf_op jit(solution)/shard_map/ppermute | solution.py:69
  128.4 1.0 collective-permute-done.23
  129.4 5.6 %collective-permute-done.24 = bf16[104,896]{1,0:T(8,128)(2,1)S(1)} collective-permute-done((bf16[104,896]{1,0:T(8,128)(2,1)S(1)}, bf16[104,896]{1,0:T(8,128)(2,1)S(1)}, u32[]{:S(2)}, u32[]{:S(2)}) %collective-permute-start.24) | collective-permute-done | bytes 186400 | tf_op jit(solution)/shard_map/ppermute | solution.py:69
  135.3 1.5 collective-permute-start.26
  139.2 1.5 collective-permute-start.27
  140.7 1.2 collective-permute-start.29
  141.8 2.7 %collective-permute-done.35 = bf16[104,896]{1,0:T(8,128)(2,1)S(1)} collective-permute-done((bf16[104,896]{1,0:T(8,128)(2,1)S(1)}, bf16[104,896]{1,0:T(8,128)(2,1)S(1)}, u32[]{:S(2)}, u32[]{:S(2)}) %collective-permute-start.35) | collective-permute-done | bytes 186400 | tf_op jit(solution)/shard_map/ppermute | solution.py:69
  144.9 6.9 %collective-permute-done.28 = bf16[104,896]{1,0:T(8,128)(2,1)S(1)} collective-permute-done((bf16[104,896]{1,0:T(8,128)(2,1)S(1)}, bf16[104,896]{1,0:T(8,128)(2,1)S(1)}, u32[]{:S(2)}, u32[]{:S(2)}) %collective-permute-start.28) | collective-permute-done | bytes 186400 | tf_op jit(solution)/shard_map/ppermute | solution.py:69
  152.9 1.3 collective-permute-start.38
  154.2 8.1 %collective-permute-done.37.refs_5_ = bf16[208,896]{1,0:T(8,128)(2,1)S(1)} collective-permute-done((bf16[208,896]{1,0:T(8,128)(2,1)S(1)}, bf16[208,896]{1,0:T(8,128)(2,1)S(1)}, u32[]{:S(2)}, u32[]{:S(2)}) %collective-permute-start.37) | collective-permute-done | bytes 372768 | tf_op jit(solution)/shard_map/ppermute | solution.py:69
  162.3 9.9 %collective-permute-done.38.refs_6_ = bf16[208,896]{1,0:T(8,128)(2,1)S(1)} collective-permute-done((bf16[208,896]{1,0:T(8,128)(2,1)S(1)}, bf16[208,896]{1,0:T(8,128)(2,1)S(1)}, u32[]{:S(2)}, u32[]{:S(2)}) %collective-permute-start.38) | collective-permute-done | bytes 372768 | tf_op jit(solution)/shard_map/ppermute | solution.py:69
  172.2 5.7 %exchange.1 = (f32[416,768]{1,0:T(8,128)S(1)}, f32[416,768]{1,0:T(8,128)S(1)}) custom-call(bf16[768,896]{1,0:T(8,128)(2,1)} %copy-done.2, bf16[768,896]{1,0:T(8,128)(2,1)} %copy-done.1, bf16[416,896]{1,0:T(8,128)(2,1)S(1)} %constant_dynamic-update-slice_fusion.6.refs_2_, bf16[416,896]{1,0:T(8,128)(2,1)S(1)} %collective-permute-done.36.refs_3_, ...), custom_call_target="tpu_custom_call" | custom-call | flops 2466250752 | bytes 8388608 | tf_op jit(solution)/shard_map/exchange/pallas_call | solution.py:388
  177.9 1.1 collective-permute-start.40
  179.1 2.6 %collective-permute-done.40.refs_1_ = f32[416,768]{1,0:T(8,128)S(1)} collective-permute-done((f32[416,768]{1,0:T(8,128)S(1)}, f32[416,768]{1,0:T(8,128)S(1)}, u32[]{:S(2)}, u32[]{:S(2)}) %collective-permute-start.40) | collective-permute-done | bytes 1277984 | tf_op jit(solution)/shard_map/ppermute | solution.py:69
  183.9 3.3 %collective-permute-done.41 = bf16[104,768]{1,0:T(8,128)(2,1)S(1)} collective-permute-done((bf16[104,768]{1,0:T(8,128)(2,1)S(1)}, bf16[104,768]{1,0:T(8,128)(2,1)S(1)}, u32[]{:S(2)}, u32[]{:S(2)}) %collective-permute-start.41) | collective-permute-done | bytes 159776 | tf_op jit(solution)/shard_map/ppermute | solution.py:69
  187.2 6.0 %collective-permute-done.42 = bf16[104,768]{1,0:T(8,128)(2,1)S(1)} collective-permute-done((bf16[104,768]{1,0:T(8,128)(2,1)S(1)}, bf16[104,768]{1,0:T(8,128)(2,1)S(1)}, u32[]{:S(2)}, u32[]{:S(2)}) %collective-permute-start.42) | collective-permute-done | bytes 159776 | tf_op jit(solution)/shard_map/ppermute | solution.py:69
  193.3 1.8 collective-permute-start.44
  195.1 8.2 %collective-permute-done.44 = f32[104,768]{1,0:T(8,128)S(1)} collective-permute-done((f32[104,768]{1,0:T(8,128)S(1)}, f32[104,768]{1,0:T(8,128)S(1)}, u32[]{:S(2)}, u32[]{:S(2)}) %collective-permute-start.44) | collective-permute-done | bytes 319520 | tf_op jit(solution)/shard_map/ppermute | solution.py:69
  203.5 1.5 collective-permute-start.46
  205.5 2.2 collective-permute-done.45
  207.7 1.3 collective-permute-done.46
  209.0 3.2 %collective-permute-done.47 = bf16[104,768]{1,0:T(8,128)(2,1)S(1)} collective-permute-done((bf16[104,768]{1,0:T(8,128)(2,1)S(1)}, bf16[104,768]{1,0:T(8,128)(2,1)S(1)}, u32[]{:S(2)}, u32[]{:S(2)}) %collective-permute-start.47) | collective-permute-done | bytes 159776 | tf_op jit(solution)/shard_map/ppermute | solution.py:69
  212.2 2.9 %collective-permute-start.48 = (bf16[416,768]{1,0:T(8,128)(2,1)S(1)}, bf16[416,768]{1,0:T(8,128)(2,1)S(1)}, u32[]{:S(2)}, u32[]{:S(2)}) collective-permute-start(bf16[416,768]{1,0:T(8,128)(2,1)S(1)} %constant_dynamic-update-slice_fusion.own), channel_id=1, source_target_pairs={{0,8},{1,9},{2,10},{3,11},{4,12},{5,13},{6,14},{7,15},{8,0},{9,1},... | collective-permute-start | bytes 1916936 | tf_op jit(solution)/shard_map/ppermute | solution.py:69
  215.1 1.7 collective-permute-done.48.others
  216.8 1.6 widen.1
  (99 shorter events, 13.6 us)
Async XLA Ops:
  0.0 10.8 %copy-start.4 = (s32[1,96]{1,0:T(1,128)S(1)}, s32[1,96]{1,0:T(1,128)}, u32[]{:S(2)}) copy-start(s32[1,96]{1,0:T(1,128)} %param.7) | copy-start | bytes 1156
  0.0 10.8 %copy-start.3 = (s32[1,96]{1,0:T(1,128)S(1)}, s32[1,96]{1,0:T(1,128)}, u32[]{:S(2)}) copy-start(s32[1,96]{1,0:T(1,128)} %param.8) | copy-start | bytes 1156
  0.9 2.4 %collective-permute-start = (bf16[48,800]{1,0:T(8,128)(2,1)S(1)}, bf16[48,800]{1,0:T(8,128)(2,1)S(1)}, u32[]{:S(2)}, u32[]{:S(2)}) collective-permute-start(bf16[48,800]{1,0:T(8,128)(2,1)S(1)} %broadcast_select_fusion.2), channel_id=1, source_target_pairs={{0,8},{1,9},{2,10},{3,11},{4,12},{5,13},{6,14},{7,15},{8,0},{9,1},... | collective-permute-start | bytes 230408 | tf_op jit(solution)/shard_map/ppermute | solution.py:69
  3.4 11.4 %collective-permute-start.4 = (bf16[96,128,128]{2,1,0:T(8,128)(2,1)}, bf16[96,128,128]{2,1,0:T(8,128)(2,1)S(1)}, u32[]{:S(2)}, u32[]{:S(2)}) collective-permute-start(bf16[96,128,128]{2,1,0:T(8,128)(2,1)} %bitcast.68), channel_id=1, source_target_pairs={{0,8},{1,9},{2,10},{3,11},{4,12},{5,13},{6,14},{7,15},{8,0},{9,1},... | collective-permute-start | bytes 9437192 | tf_op jit(solution)/shard_map/ppermute | solution.py:69
  4.7 6.1 %collective-permute-start.1 = (bf16[2,48,896]{2,1,0:T(8,128)(2,1)S(1)}, bf16[2,48,896]{2,1,0:T(8,128)(2,1)}, u32[]{:S(2)}, u32[]{:S(2)}) collective-permute-start(bf16[2,48,896]{2,1,0:T(8,128)(2,1)S(1)} %fusion.10), channel_id=1, source_target_pairs={{0,2},{1,3},{2,4},{3,5},{4,6},{5,7},{6,0},{7,1},{8,40},{9,41},{10,... | collective-permute-start | bytes 516104 | tf_op jit(solution)/shard_map/ppermute | solution.py:69
  6.8 6.1 %collective-permute-start.2 = (bf16[2,48,896]{2,1,0:T(8,128)(2,1)S(1)}, bf16[2,48,896]{2,1,0:T(8,128)(2,1)S(1)}, u32[]{:S(2)}, u32[]{:S(2)}) collective-permute-start(bf16[2,48,896]{2,1,0:T(8,128)(2,1)S(1)} %fusion.10), channel_id=1, source_target_pairs={{0,6},{1,7},{2,0},{3,1},{4,2},{5,3},{6,4},{7,5},{8,104},{9,105},{1... | collective-permute-start | bytes 516104 | tf_op jit(solution)/shard_map/ppermute | solution.py:69
  8.7 6.1 %collective-permute-start.3 = (bf16[2,48,896]{2,1,0:T(8,128)(2,1)S(1)}, bf16[2,48,896]{2,1,0:T(8,128)(2,1)S(1)}, u32[]{:S(2)}, u32[]{:S(2)}) collective-permute-start(bf16[2,48,896]{2,1,0:T(8,128)(2,1)S(1)} %fusion.10), channel_id=1, source_target_pairs={{0,4},{1,5},{2,6},{3,7},{4,0},{5,1},{6,2},{7,3},{8,72},{9,73},{10,... | collective-permute-start | bytes 516104 | tf_op jit(solution)/shard_map/ppermute | solution.py:69
  14.9 9.2 %collective-permute-start.5 = (bf16[2,4,32,896]{3,2,1,0:T(8,128)(2,1)S(1)}, bf16[2,4,32,896]{3,2,1,0:T(8,128)(2,1)S(1)}, u32[]{:S(2)}, u32[]{:S(2)}) collective-permute-start(bf16[2,4,32,896]{3,2,1,0:T(8,128)(2,1)S(1)} %slice.39), channel_id=1, source_target_pairs={{0,1},{1,16},{2,3},{3,18},{4,5},{5,20},{6,7},{7,22},{8,25},{9,8},{... | collective-permute-start | bytes 1376264 | tf_op jit(solution)/shard_map/ppermute | solution.py:69
  24.1 5.2 %collective-permute-start.6 = (s32[1,256]{1,0:T(1,128)S(1)}, s32[1,256]{1,0:T(1,128)S(1)}, u32[]{:S(2)}, u32[]{:S(2)}) collective-permute-start(s32[1,256]{1,0:T(1,128)S(1)} %bitcast.73), channel_id=1, source_target_pairs={{0,8},{1,9},{2,10},{3,11},{4,12},{5,13},{6,14},{7,15},{8,0},{9,1},... | collective-permute-start | bytes 3080 | tf_op jit(solution)/shard_map/ppermute | solution.py:69
  26.6 12.2 %collective-permute-start.7 = (bf16[2,4,32,896]{3,2,1,0:T(8,128)(2,1)S(1)}, bf16[2,4,32,896]{3,2,1,0:T(8,128)(2,1)S(1)}, u32[]{:S(2)}, u32[]{:S(2)}) collective-permute-start(bf16[2,4,32,896]{3,2,1,0:T(8,128)(2,1)S(1)} %slice.39), channel_id=1, source_target_pairs={{0,17},{1,0},{2,19},{3,2},{4,21},{5,4},{6,23},{7,6},{8,9},{9,24},{... | collective-permute-start | bytes 1376264 | tf_op jit(solution)/shard_map/ppermute | solution.py:69
  26.6 12.5 %collective-permute-start.8 = (bf16[2,4,32,896]{3,2,1,0:T(8,128)(2,1)S(1)}, bf16[2,4,32,896]{3,2,1,0:T(8,128)(2,1)S(1)}, u32[]{:S(2)}, u32[]{:S(2)}) collective-permute-start(bf16[2,4,32,896]{3,2,1,0:T(8,128)(2,1)S(1)} %collective-permute-done.5), channel_id=1, source_target_pairs={{0,1},{1,16},{2,3},{3,18},{4,5},{5,20},{6,7},{7,22},{8,25},{9,8},{... | collective-permute-start | bytes 1376264 | tf_op jit(solution)/shard_map/ppermute | solution.py:69
  29.3 6.4 %collective-permute-start.9 = (bf16[2,4,16,896]{3,2,1,0:T(8,128)(2,1)S(1)}, bf16[2,4,16,896]{3,2,1,0:T(8,128)(2,1)S(1)}, u32[]{:S(2)}, u32[]{:S(2)}) collective-permute-start(bf16[2,4,16,896]{3,2,1,0:T(8,128)(2,1)S(1)} %slice.38), channel_id=1, source_target_pairs={{0,32},{1,33},{2,34},{3,35},{4,36},{5,37},{6,38},{7,39},{8,10},{9,... | collective-permute-start | bytes 688136 | tf_op jit(solution)/shard_map/ppermute | solution.py:69
  29.9 7.7 %collective-permute-start.10 = (bf16[2,4,16,896]{3,2,1,0:T(8,128)(2,1)S(1)}, bf16[2,4,16,896]{3,2,1,0:T(8,128)(2,1)S(1)}, u32[]{:S(2)}, u32[]{:S(2)}) collective-permute-start(bf16[2,4,16,896]{3,2,1,0:T(8,128)(2,1)S(1)} %slice.38), channel_id=1, source_target_pairs={{0,96},{1,97},{2,98},{3,99},{4,100},{5,101},{6,102},{7,103},{8,14}... | collective-permute-start | bytes 688136 | tf_op jit(solution)/shard_map/ppermute | solution.py:69
  32.1 6.7 %collective-permute-start.11 = (bf16[2,4,16,896]{3,2,1,0:T(8,128)(2,1)S(1)}, bf16[2,4,16,896]{3,2,1,0:T(8,128)(2,1)S(1)}, u32[]{:S(2)}, u32[]{:S(2)}) collective-permute-start(bf16[2,4,16,896]{3,2,1,0:T(8,128)(2,1)S(1)} %slice.38), channel_id=1, source_target_pairs={{0,64},{1,65},{2,66},{3,67},{4,68},{5,69},{6,70},{7,71},{8,12},{9,... | collective-permute-start | bytes 688136 | tf_op jit(solution)/shard_map/ppermute | solution.py:69
  39.2 12.6 %collective-permute-start.14 = (bf16[2,2,4,32,896]{4,3,2,1,0:T(8,128)(2,1)S(1)}, bf16[2,2,4,32,896]{4,3,2,1,0:T(8,128)(2,1)S(1)}, u32[]{:S(2)}, u32[]{:S(2)}) collective-permute-start(bf16[2,2,4,32,896]{4,3,2,1,0:T(8,128)(2,1)S(1)} %get-tuple-element.64.refs_1_), channel_id=1, source_target_pairs={{0,96},{1,97},{2,98},{3,99},{4,100},{5,101},{6,102},{7,103},{8,14}... | collective-permute-start | bytes 2752520 | tf_op jit(solution)/shard_map/ppermute | solution.py:69
  41.2 13.8 %collective-permute-start.12 = (bf16[2,2,4,32,896]{4,3,2,1,0:T(8,128)(2,1)S(1)}, bf16[2,2,4,32,896]{4,3,2,1,0:T(8,128)(2,1)S(1)}, u32[]{:S(2)}, u32[]{:S(2)}) collective-permute-start(bf16[2,2,4,32,896]{4,3,2,1,0:T(8,128)(2,1)S(1)} %get-tuple-element.65.refs_0_), channel_id=1, source_target_pairs={{0,32},{1,33},{2,34},{3,35},{4,36},{5,37},{6,38},{7,39},{8,10},{9,... | collective-permute-start | bytes 2752520 | tf_op jit(solution)/shard_map/ppermute | solution.py:69
  41.2 19.8 %collective-permute-start.15 = (bf16[2,4,4,16,896]{4,3,2,1,0:T(8,128)(2,1)S(1)}, bf16[2,4,4,16,896]{4,3,2,1,0:T(8,128)(2,1)S(1)}, u32[]{:S(2)}, u32[]{:S(2)}) collective-permute-start(bf16[2,4,4,16,896]{4,3,2,1,0:T(8,128)(2,1)S(1)} %bitcast_dynamic-update-slice_fusion.3.refs_2_), channel_id=1, source_target_pairs={{0,1},{1,16},{2,3},{3,18},{4,5},{5,20},{6,7},{7,22},{8,25},{9,8},{... | collective-permute-start | bytes 2752520 | tf_op jit(solution)/shard_map/ppermute | solution.py:69
  44.1 23.4 %collective-permute-start.17 = (bf16[2,4,4,16,896]{4,3,2,1,0:T(8,128)(2,1)S(1)}, bf16[2,4,4,16,896]{4,3,2,1,0:T(8,128)(2,1)S(1)}, u32[]{:S(2)}, u32[]{:S(2)}) collective-permute-start(bf16[2,4,4,16,896]{4,3,2,1,0:T(8,128)(2,1)S(1)} %bitcast_dynamic-update-slice_fusion.3.refs_2_), channel_id=1, source_target_pairs={{0,17},{1,0},{2,19},{3,2},{4,21},{5,4},{6,23},{7,6},{8,9},{9,24},{... | collective-permute-start | bytes 2752520 | tf_op jit(solution)/shard_map/ppermute | solution.py:69
  51.8 17.4 %collective-permute-start.20 = (bf16[2,2,4,32,896]{4,3,2,1,0:T(8,128)(2,1)S(1)}, bf16[2,2,4,32,896]{4,3,2,1,0:T(8,128)(2,1)S(1)}, u32[]{:S(2)}, u32[]{:S(2)}) collective-permute-start(bf16[2,2,4,32,896]{4,3,2,1,0:T(8,128)(2,1)S(1)} %get-tuple-element.65.refs_0_), channel_id=1, source_target_pairs={{0,96},{1,97},{2,98},{3,99},{4,100},{5,101},{6,102},{7,103},{8,14}... | collective-permute-start | bytes 2752520 | tf_op jit(solution)/shard_map/ppermute | solution.py:69
  55.0 14.2 %collective-permute-start.19 = (bf16[2,2,4,32,896]{4,3,2,1,0:T(8,128)(2,1)S(1)}, bf16[2,2,4,32,896]{4,3,2,1,0:T(8,128)(2,1)S(1)}, u32[]{:S(2)}, u32[]{:S(2)}) collective-permute-start(bf16[2,2,4,32,896]{4,3,2,1,0:T(8,128)(2,1)S(1)} %get-tuple-element.64.refs_1_), channel_id=1, source_target_pairs={{0,32},{1,33},{2,34},{3,35},{4,36},{5,37},{6,38},{7,39},{8,10},{9,... | collective-permute-start | bytes 2752520 | tf_op jit(solution)/shard_map/ppermute | solution.py:69
  67.5 12.5 %collective-permute-start.18 = (bf16[2,4,4,16,896]{4,3,2,1,0:T(8,128)(2,1)S(1)}, bf16[2,4,4,16,896]{4,3,2,1,0:T(8,128)(2,1)S(1)}, u32[]{:S(2)}, u32[]{:S(2)}) collective-permute-start(bf16[2,4,4,16,896]{4,3,2,1,0:T(8,128)(2,1)S(1)} %collective-permute-done.15.refs_5_), channel_id=1, source_target_pairs={{0,1},{1,16},{2,3},{3,18},{4,5},{5,20},{6,7},{7,22},{8,25},{9,8},{... | collective-permute-start | bytes 2752520 | tf_op jit(solution)/shard_map/ppermute | solution.py:69
  67.5 12.5 %collective-permute-start.16 = (bf16[2,2,4,32,896]{4,3,2,1,0:T(8,128)(2,1)S(1)}, bf16[2,2,4,32,896]{4,3,2,1,0:T(8,128)(2,1)S(1)}, u32[]{:S(2)}, u32[]{:S(2)}) collective-permute-start(bf16[2,2,4,32,896]{4,3,2,1,0:T(8,128)(2,1)S(1)} %collective-permute-done.14.refs_7_), channel_id=1, source_target_pairs={{0,96},{1,97},{2,98},{3,99},{4,100},{5,101},{6,102},{7,103},{8,14}... | collective-permute-start | bytes 2752520 | tf_op jit(solution)/shard_map/ppermute | solution.py:69
  69.2 13.8 %collective-permute-start.13 = (bf16[2,2,4,32,896]{4,3,2,1,0:T(8,128)(2,1)S(1)}, bf16[2,2,4,32,896]{4,3,2,1,0:T(8,128)(2,1)S(1)}, u32[]{:S(2)}, u32[]{:S(2)}) collective-permute-start(bf16[2,2,4,32,896]{4,3,2,1,0:T(8,128)(2,1)S(1)} %collective-permute-done.12.refs_3_), channel_id=1, source_target_pairs={{0,32},{1,33},{2,34},{3,35},{4,36},{5,37},{6,38},{7,39},{8,10},{9,... | collective-permute-start | bytes 2752520 | tf_op jit(solution)/shard_map/ppermute | solution.py:69
  84.7 8.1 %collective-permute-start.21 = (bf16[768,896]{1,0:T(8,128)(2,1)S(1)}, bf16[768,896]{1,0:T(8,128)(2,1)S(1)}, u32[]{:S(2)}, u32[]{:S(2)}) collective-permute-start(bf16[768,896]{1,0:T(8,128)(2,1)S(1)} %bitcast.70), channel_id=1, source_target_pairs={{0,8},{1,9},{2,10},{3,11},{4,12},{5,13},{6,14},{7,15},{8,0},{9,1},... | collective-permute-start | bytes 4128776 | tf_op jit(solution)/shard_map/ppermute | solution.py:69
  92.7 2.1 copy-start.1
  92.8 2.4 %copy-start = (bf16[1,96,128,128]{3,2,1,0:T(8,128)(2,1)S(1)}, bf16[1,96,128,128]{3,2,1,0:T(8,128)(2,1)}, u32[]{:S(2)}) copy-start(bf16[1,96,128,128]{3,2,1,0:T(8,128)(2,1)} %param.6) | copy-start | bytes 9437188
  94.8 18.4 %collective-permute-start.22 = (bf16[416,896]{1,0:T(8,128)(2,1)S(1)}, bf16[416,896]{1,0:T(8,128)(2,1)S(1)}, u32[]{:S(2)}, u32[]{:S(2)}) collective-permute-start(bf16[416,896]{1,0:T(8,128)(2,1)S(1)} %get-tuple-element.72), channel_id=1, source_target_pairs={{0,1},{1,0},{2,3},{3,2},{4,5},{5,4},{6,7},{7,6},{8,9},{9,8},{10,11... | collective-permute-start | bytes 2236424 | tf_op jit(solution)/shard_map/ppermute | solution.py:69
  100.4 1.8 copy-start.2
  102.3 11.2 %collective-permute-start.30 = (bf16[208,896]{1,0:T(8,128)(2,1)S(1)}, bf16[208,896]{1,0:T(8,128)(2,1)S(1)}, u32[]{:S(2)}, u32[]{:S(2)}) collective-permute-start(bf16[208,896]{1,0:T(8,128)(2,1)S(1)} %get-tuple-element.78), channel_id=1, source_target_pairs={{0,2},{1,3},{2,4},{3,5},{4,6},{5,7},{6,0},{7,1},{8,14},{9,15},{10,... | collective-permute-start | bytes 1118216 | tf_op jit(solution)/shard_map/ppermute | solution.py:69
  102.6 19.7 %collective-permute-start.31 = (bf16[208,896]{1,0:T(8,128)(2,1)S(1)}, bf16[208,896]{1,0:T(8,128)(2,1)S(1)}, u32[]{:S(2)}, u32[]{:S(2)}) collective-permute-start(bf16[208,896]{1,0:T(8,128)(2,1)S(1)} %get-tuple-element.79), channel_id=1, source_target_pairs={{0,6},{1,7},{2,0},{3,1},{4,2},{5,3},{6,4},{7,5},{8,10},{9,11},{10,... | collective-permute-start | bytes 1118216 | tf_op jit(solution)/shard_map/ppermute | solution.py:69
  103.8 18.5 %collective-permute-start.32 = (bf16[208,896]{1,0:T(8,128)(2,1)S(1)}, bf16[208,896]{1,0:T(8,128)(2,1)S(1)}, u32[]{:S(2)}, u32[]{:S(2)}) collective-permute-start(bf16[208,896]{1,0:T(8,128)(2,1)S(1)} %get-tuple-element.80), channel_id=1, source_target_pairs={{0,4},{1,5},{2,6},{3,7},{4,0},{5,1},{6,2},{7,3},{8,12},{9,13},{10,... | collective-permute-start | bytes 1118216 | tf_op jit(solution)/shard_map/ppermute | solution.py:69
  122.7 5.7 %collective-permute-start.33 = (bf16[104,896]{1,0:T(8,128)(2,1)S(1)}, bf16[104,896]{1,0:T(8,128)(2,1)S(1)}, u32[]{:S(2)}, u32[]{:S(2)}) collective-permute-start(bf16[104,896]{1,0:T(8,128)(2,1)S(1)} %get-tuple-element.86), channel_id=1, source_target_pairs={{0,1},{1,0},{2,3},{3,2},{4,5},{5,4},{6,7},{7,6},{8,9},{9,8},{10,11... | collective-permute-start | bytes 559112 | tf_op jit(solution)/shard_map/ppermute | solution.py:69
  123.9 5.5 %collective-permute-start.23 = (bf16[104,896]{1,0:T(8,128)(2,1)S(1)}, bf16[104,896]{1,0:T(8,128)(2,1)S(1)}, u32[]{:S(2)}, u32[]{:S(2)}) collective-permute-start(bf16[104,896]{1,0:T(8,128)(2,1)S(1)} %get-tuple-element.74), channel_id=1, source_target_pairs={{0,2},{1,3},{2,4},{3,5},{4,6},{5,7},{6,0},{7,1},{8,14},{9,15},{10,... | collective-permute-start | bytes 559112 | tf_op jit(solution)/shard_map/ppermute | solution.py:69
  124.1 10.9 %collective-permute-start.24 = (bf16[104,896]{1,0:T(8,128)(2,1)S(1)}, bf16[104,896]{1,0:T(8,128)(2,1)S(1)}, u32[]{:S(2)}, u32[]{:S(2)}) collective-permute-start(bf16[104,896]{1,0:T(8,128)(2,1)S(1)} %get-tuple-element.75), channel_id=1, source_target_pairs={{0,6},{1,7},{2,0},{3,1},{4,2},{5,3},{6,4},{7,5},{8,10},{9,11},{10,... | collective-permute-start | bytes 559112 | tf_op jit(solution)/shard_map/ppermute | solution.py:69
  125.4 9.6 %collective-permute-start.25 = (bf16[104,896]{1,0:T(8,128)(2,1)S(1)}, bf16[104,896]{1,0:T(8,128)(2,1)S(1)}, u32[]{:S(2)}, u32[]{:S(2)}) collective-permute-start(bf16[104,896]{1,0:T(8,128)(2,1)S(1)} %get-tuple-element.76), channel_id=1, source_target_pairs={{0,4},{1,5},{2,6},{3,7},{4,0},{5,1},{6,2},{7,3},{8,12},{9,13},{10,... | collective-permute-start | bytes 559112 | tf_op jit(solution)/shard_map/ppermute | solution.py:69
  135.3 2.5 %collective-permute-start.26 = (bf16[104,896]{1,0:T(8,128)(2,1)S(1)}, bf16[104,896]{1,0:T(8,128)(2,1)S(1)}, u32[]{:S(2)}, u32[]{:S(2)}) collective-permute-start(bf16[104,896]{1,0:T(8,128)(2,1)S(1)} %get-tuple-element.112), channel_id=1, source_target_pairs={{0,8},{1,9},{2,10},{3,11},{4,12},{5,13},{6,14},{7,15},{8,0},{9,1},... | collective-permute-start | bytes 559112 | tf_op jit(solution)/shard_map/ppermute | solution.py:69
  136.7 1.4 collective-permute-start.34
  138.4 6.1 %collective-permute-start.35 = (bf16[104,896]{1,0:T(8,128)(2,1)S(1)}, bf16[104,896]{1,0:T(8,128)(2,1)S(1)}, u32[]{:S(2)}, u32[]{:S(2)}) collective-permute-start(bf16[104,896]{1,0:T(8,128)(2,1)S(1)} %get-tuple-element.98), channel_id=1, source_target_pairs={{0,1},{1,0},{2,3},{3,2},{4,5},{5,4},{6,7},{7,6},{8,9},{9,8},{10,11... | collective-permute-start | bytes 559112 | tf_op jit(solution)/shard_map/ppermute | solution.py:69
  139.2 5.7 %collective-permute-start.27 = (bf16[104,896]{1,0:T(8,128)(2,1)S(1)}, bf16[104,896]{1,0:T(8,128)(2,1)S(1)}, u32[]{:S(2)}, u32[]{:S(2)}) collective-permute-start(bf16[104,896]{1,0:T(8,128)(2,1)S(1)} %get-tuple-element.110), channel_id=1, source_target_pairs={{0,2},{1,3},{2,4},{3,5},{4,6},{5,7},{6,0},{7,1},{8,14},{9,15},{10,... | collective-permute-start | bytes 559112 | tf_op jit(solution)/shard_map/ppermute | solution.py:69
  140.7 11.1 %collective-permute-start.28 = (bf16[104,896]{1,0:T(8,128)(2,1)S(1)}, bf16[104,896]{1,0:T(8,128)(2,1)S(1)}, u32[]{:S(2)}, u32[]{:S(2)}) collective-permute-start(bf16[104,896]{1,0:T(8,128)(2,1)S(1)} %get-tuple-element.110), channel_id=1, source_target_pairs={{0,6},{1,7},{2,0},{3,1},{4,2},{5,3},{6,4},{7,5},{8,10},{9,11},{10,... | collective-permute-start | bytes 559112 | tf_op jit(solution)/shard_map/ppermute | solution.py:69
  140.7 11.1 %collective-permute-start.29 = (bf16[104,896]{1,0:T(8,128)(2,1)S(1)}, bf16[104,896]{1,0:T(8,128)(2,1)S(1)}, u32[]{:S(2)}, u32[]{:S(2)}) collective-permute-start(bf16[104,896]{1,0:T(8,128)(2,1)S(1)} %get-tuple-element.110), channel_id=1, source_target_pairs={{0,4},{1,5},{2,6},{3,7},{4,0},{5,1},{6,2},{7,3},{8,12},{9,13},{10,... | collective-permute-start | bytes 559112 | tf_op jit(solution)/shard_map/ppermute | solution.py:69
  151.8 20.3 %collective-permute-start.36 = (bf16[416,896]{1,0:T(8,128)(2,1)S(1)}, bf16[416,896]{1,0:T(8,128)(2,1)S(1)}, u32[]{:S(2)}, u32[]{:S(2)}) collective-permute-start(bf16[416,896]{1,0:T(8,128)(2,1)S(1)} %constant_dynamic-update-slice_fusion.6.refs_2_), channel_id=1, source_target_pairs={{0,1},{1,0},{2,3},{3,2},{4,5},{5,4},{6,7},{7,6},{8,9},{9,8},{10,11... | collective-permute-start | bytes 2236424 | tf_op jit(solution)/shard_map/ppermute | solution.py:69
  152.7 9.6 %collective-permute-start.37 = (bf16[208,896]{1,0:T(8,128)(2,1)S(1)}, bf16[208,896]{1,0:T(8,128)(2,1)S(1)}, u32[]{:S(2)}, u32[]{:S(2)}) collective-permute-start(bf16[208,896]{1,0:T(8,128)(2,1)S(1)} %constant_dynamic-update-slice_fusion.4.refs_4_), channel_id=1, source_target_pairs={{0,2},{1,3},{2,4},{3,5},{4,6},{5,7},{6,0},{7,1},{8,14},{9,15},{10,... | collective-permute-start | bytes 1118216 | tf_op jit(solution)/shard_map/ppermute | solution.py:69
  152.9 19.2 %collective-permute-start.38 = (bf16[208,896]{1,0:T(8,128)(2,1)S(1)}, bf16[208,896]{1,0:T(8,128)(2,1)S(1)}, u32[]{:S(2)}, u32[]{:S(2)}) collective-permute-start(bf16[208,896]{1,0:T(8,128)(2,1)S(1)} %constant_dynamic-update-slice_fusion.4.refs_4_), channel_id=1, source_target_pairs={{0,6},{1,7},{2,0},{3,1},{4,2},{5,3},{6,4},{7,5},{8,10},{9,11},{10,... | collective-permute-start | bytes 1118216 | tf_op jit(solution)/shard_map/ppermute | solution.py:69
  154.2 18.0 %collective-permute-start.39 = (bf16[208,896]{1,0:T(8,128)(2,1)S(1)}, bf16[208,896]{1,0:T(8,128)(2,1)S(1)}, u32[]{:S(2)}, u32[]{:S(2)}) collective-permute-start(bf16[208,896]{1,0:T(8,128)(2,1)S(1)} %constant_dynamic-update-slice_fusion.4.refs_4_), channel_id=1, source_target_pairs={{0,4},{1,5},{2,6},{3,7},{4,0},{5,1},{6,2},{7,3},{8,12},{9,13},{10,... | collective-permute-start | bytes 1118216 | tf_op jit(solution)/shard_map/ppermute | solution.py:69
  177.9 3.7 %collective-permute-start.40 = (f32[416,768]{1,0:T(8,128)S(1)}, f32[416,768]{1,0:T(8,128)S(1)}, u32[]{:S(2)}, u32[]{:S(2)}) collective-permute-start(f32[416,768]{1,0:T(8,128)S(1)} %get-tuple-element.90), channel_id=1, source_target_pairs={{0,8},{1,9},{2,10},{3,11},{4,12},{5,13},{6,14},{7,15},{8,0},{9,1},... | collective-permute-start | bytes 3833864 | tf_op jit(solution)/shard_map/ppermute | solution.py:69
  181.9 5.3 %collective-permute-start.41 = (bf16[104,768]{1,0:T(8,128)(2,1)S(1)}, bf16[104,768]{1,0:T(8,128)(2,1)S(1)}, u32[]{:S(2)}, u32[]{:S(2)}) collective-permute-start(bf16[104,768]{1,0:T(8,128)(2,1)S(1)} %get-tuple-element.92), channel_id=1, source_target_pairs={{0,32},{1,33},{2,34},{3,35},{4,36},{5,37},{6,38},{7,39},{8,104},{9... | collective-permute-start | bytes 479240 | tf_op jit(solution)/shard_map/ppermute | solution.py:69
  182.6 10.6 %collective-permute-start.42 = (bf16[104,768]{1,0:T(8,128)(2,1)S(1)}, bf16[104,768]{1,0:T(8,128)(2,1)S(1)}, u32[]{:S(2)}, u32[]{:S(2)}) collective-permute-start(bf16[104,768]{1,0:T(8,128)(2,1)S(1)} %get-tuple-element.93), channel_id=1, source_target_pairs={{0,96},{1,97},{2,98},{3,99},{4,100},{5,101},{6,102},{7,103},{8,40}... | collective-permute-start | bytes 479240 | tf_op jit(solution)/shard_map/ppermute | solution.py:69
  183.4 9.8 %collective-permute-start.43 = (bf16[104,768]{1,0:T(8,128)(2,1)S(1)}, bf16[104,768]{1,0:T(8,128)(2,1)S(1)}, u32[]{:S(2)}, u32[]{:S(2)}) collective-permute-start(bf16[104,768]{1,0:T(8,128)(2,1)S(1)} %get-tuple-element.94), channel_id=1, source_target_pairs={{0,64},{1,65},{2,66},{3,67},{4,68},{5,69},{6,70},{7,71},{8,72},{9,... | collective-permute-start | bytes 479240 | tf_op jit(solution)/shard_map/ppermute | solution.py:69
  193.3 10.1 %collective-permute-start.44 = (f32[104,768]{1,0:T(8,128)S(1)}, f32[104,768]{1,0:T(8,128)S(1)}, u32[]{:S(2)}, u32[]{:S(2)}) collective-permute-start(f32[104,768]{1,0:T(8,128)S(1)} %add_add_fusion), channel_id=1, source_target_pairs={{0,16},{1,17},{2,18},{3,19},{4,20},{5,21},{6,22},{7,23},{8,24},{9,... | collective-permute-start | bytes 958472 | tf_op jit(solution)/shard_map/ppermute | solution.py:69
  203.4 4.2 %collective-permute-start.45 = (bf16[104,768]{1,0:T(8,128)(2,1)S(1)}, bf16[104,768]{1,0:T(8,128)(2,1)S(1)}, u32[]{:S(2)}, u32[]{:S(2)}) collective-permute-start(bf16[104,768]{1,0:T(8,128)(2,1)S(1)} %get-tuple-element.96), channel_id=1, source_target_pairs={{0,32},{1,33},{2,34},{3,35},{4,36},{5,37},{6,38},{7,39},{8,104},{9... | collective-permute-start | bytes 479240 | tf_op jit(solution)/shard_map/ppermute | solution.py:69
  203.5 5.4 %collective-permute-start.46 = (bf16[104,768]{1,0:T(8,128)(2,1)S(1)}, bf16[104,768]{1,0:T(8,128)(2,1)S(1)}, u32[]{:S(2)}, u32[]{:S(2)}) collective-permute-start(bf16[104,768]{1,0:T(8,128)(2,1)S(1)} %get-tuple-element.96), channel_id=1, source_target_pairs={{0,96},{1,97},{2,98},{3,99},{4,100},{5,101},{6,102},{7,103},{8,40}... | collective-permute-start | bytes 479240 | tf_op jit(solution)/shard_map/ppermute | solution.py:69
  205.0 7.2 %collective-permute-start.47 = (bf16[104,768]{1,0:T(8,128)(2,1)S(1)}, bf16[104,768]{1,0:T(8,128)(2,1)S(1)}, u32[]{:S(2)}, u32[]{:S(2)}) collective-permute-start(bf16[104,768]{1,0:T(8,128)(2,1)S(1)} %get-tuple-element.96), channel_id=1, source_target_pairs={{0,64},{1,65},{2,66},{3,67},{4,68},{5,69},{6,70},{7,71},{8,72},{9,... | collective-permute-start | bytes 479240 | tf_op jit(solution)/shard_map/ppermute | solution.py:69
  212.2 4.6 %collective-permute-start.48 = (bf16[416,768]{1,0:T(8,128)(2,1)S(1)}, bf16[416,768]{1,0:T(8,128)(2,1)S(1)}, u32[]{:S(2)}, u32[]{:S(2)}) collective-permute-start(bf16[416,768]{1,0:T(8,128)(2,1)S(1)} %constant_dynamic-update-slice_fusion.own), channel_id=1, source_target_pairs={{0,8},{1,9},{2,10},{3,11},{4,12},{5,13},{6,14},{7,15},{8,0},{9,1},... | collective-permute-start | bytes 1916936 | tf_op jit(solution)/shard_map/ppermute | solution.py:69

commit v10 on v9

--- a/solution.py
+++ b/solution.py
@@ -20,7 +20,7 @@
 SHARD = CROSS // 8
 OWN = 48
 STEP = 4
-UNROLL = 3
+UNROLL = 6
 FIELDS = 1 + 2 * STEP
 MOST = SLOTS // STEP + ROW_BLOCKS + UNROLL
 MAIN = 32
@@ -409,11 +409,13 @@
 
 
 def widen(own, others):
+    part = ROWS // 3
     return pl.pallas_call(
         widen_kernel,
+        grid=(3,),
         out_shape=jax.ShapeDtypeStruct((NOCC, ROWS), f32),
-        in_specs=[pl.BlockSpec(memory_space=pltpu.VMEM)] * 2,
-        out_specs=pl.BlockSpec(memory_space=pltpu.VMEM),
+        in_specs=[pl.BlockSpec((CROSS // 2, part), lambda i: (0, i))] * 2,
+        out_specs=pl.BlockSpec((NOCC, part), lambda i: (0, i)),
         compiler_params=pltpu.CompilerParams(vmem_limit_bytes=16 * 1024 * 1024),
         name="widen",
     )(own, others)

time: 219 us -> 219 us (level); the launches traced: 218 us -> 221 us
  starting transfers between devices: 53.4 us -> 64.6 us
  waiting for transfers between devices: 124 us -> 116 us
    ppermute x49, starting transfers between devices: 53.4 us -> 64.6 us  [send(): return lax.ppermute(array, AXES, pairs)]
    ppermute x49, waiting for transfers between devices: 124 us -> 116 us  [send(): return lax.ppermute(array, AXES, pairs)]
  transfers between devices with their start and end apart: 49 -> 49, of which waited for: 34 -> 37; matrix products, arithmetic and copies ran while one was open for 1% -> 1% of each run, Pallas kernels for 11% -> 10%
where the time goes in v10:
time: 219 us; the launch traced here: 221 us
  waiting for transfers between devices  116 us (53%)
  starting transfers between devices  64.6 us (29%)
  Pallas kernels  34.2 us (16%)
  other arithmetic  2.57 us (1%)
  local copies, waits for them, and re-layouts  2.25 us (1%)
    ppermute x49, waiting for transfers between devices, send(): return lax.ppermute(array, AXES, pairs)  116 us
    ppermute x49, starting transfers between devices, send(): return lax.ppermute(array, AXES, pairs)  64.6 us
    pallas_call x2, Pallas kernels, multiply(): pl.pallas_call(kernel, out_shape=jax.ShapeDtypeStruct((ROWS, WIDE), bf16)...  9.63 us
    pallas_call x1, Pallas kernels, exchange(): pl.pallas_call(exchange_kernel, out_shape=[jax.ShapeDtypeStruct((CROSS //...  5.73 us
    pallas_call x1, Pallas kernels, plan(): pl.pallas_call(plan_kernel, out_shape=jax.ShapeDtypeStruct((2, MOST * FIE...  5.29 us
    pallas_call x1, Pallas kernels, panels_and_slab(): pl.pallas_call(near_kernel, out_shape=held, in_specs=[anywhere] * 9, out_...  5.12 us
  transfers between devices with their start and end apart: 49, of which 37 were waited for; matrix products, arithmetic and copies ran while one was open for 1% of the time, Pallas kernels for 10%

profile of v10, /device:TPU:1, one launch (start us, length us, event | category | flops | bytes accessed | tf_op | source)
XLA Modules:
  0.0 220.6 jit_solution(7543195323305755038)
XLA Ops:
  0.9 1.5 collective-permute-start
  4.7 1.4 collective-permute-start.1
  6.8 1.9 collective-permute-start.2
  8.7 1.3 collective-permute-start.3
  12.9 1.8 collective-permute-done.3
  14.9 3.8 %collective-permute-start.5 = (bf16[2,4,32,896]{3,2,1,0:T(8,128)(2,1)S(1)}, bf16[2,4,32,896]{3,2,1,0:T(8,128)(2,1)S(1)}, u32[]{:S(2)}, u32[]{:S(2)}) collective-permute-start(bf16[2,4,32,896]{3,2,1,0:T(8,128)(2,1)S(1)} %slice.39), channel_id=1, source_target_pairs={{0,1},{1,16},{2,3},{3,18},{4,5},{5,20},{6,7},{7,22},{8,25},{9,8},{... | collective-permute-start | bytes 1376264 | tf_op jit(solution)/shard_map/ppermute | solution.py:69
  18.9 5.2 %collective-permute-done.5 = bf16[2,4,32,896]{3,2,1,0:T(8,128)(2,1)S(1)} collective-permute-done((bf16[2,4,32,896]{3,2,1,0:T(8,128)(2,1)S(1)}, bf16[2,4,32,896]{3,2,1,0:T(8,128)(2,1)S(1)}, u32[]{:S(2)}, u32[]{:S(2)}) %collective-permute-start.5) | collective-permute-done | bytes 458784 | tf_op jit(solution)/shard_map/ppermute | solution.py:69
  24.1 2.5 %collective-permute-start.6 = (s32[1,256]{1,0:T(1,128)S(1)}, s32[1,256]{1,0:T(1,128)S(1)}, u32[]{:S(2)}, u32[]{:S(2)}) collective-permute-start(s32[1,256]{1,0:T(1,128)S(1)} %bitcast.73), channel_id=1, source_target_pairs={{0,8},{1,9},{2,10},{3,11},{4,12},{5,13},{6,14},{7,15},{8,0},{9,1},... | collective-permute-start | bytes 3080 | tf_op jit(solution)/shard_map/ppermute | solution.py:69
  26.6 2.7 %collective-permute-start.8 = (bf16[2,4,32,896]{3,2,1,0:T(8,128)(2,1)S(1)}, bf16[2,4,32,896]{3,2,1,0:T(8,128)(2,1)S(1)}, u32[]{:S(2)}, u32[]{:S(2)}) collective-permute-start(bf16[2,4,32,896]{3,2,1,0:T(8,128)(2,1)S(1)} %collective-permute-done.5), channel_id=1, source_target_pairs={{0,1},{1,16},{2,3},{3,18},{4,5},{5,20},{6,7},{7,22},{8,25},{9,8},{... | collective-permute-start | bytes 1376264 | tf_op jit(solution)/shard_map/ppermute | solution.py:69
  29.9 2.2 %collective-permute-start.10 = (bf16[2,4,16,896]{3,2,1,0:T(8,128)(2,1)S(1)}, bf16[2,4,16,896]{3,2,1,0:T(8,128)(2,1)S(1)}, u32[]{:S(2)}, u32[]{:S(2)}) collective-permute-start(bf16[2,4,16,896]{3,2,1,0:T(8,128)(2,1)S(1)} %slice.38), channel_id=1, source_target_pairs={{0,96},{1,97},{2,98},{3,99},{4,100},{5,101},{6,102},{7,103},{8,14}... | collective-permute-start | bytes 688136 | tf_op jit(solution)/shard_map/ppermute | solution.py:69
  32.5 3.3 %collective-permute-done.9 = bf16[2,4,16,896]{3,2,1,0:T(8,128)(2,1)S(1)} collective-permute-done((bf16[2,4,16,896]{3,2,1,0:T(8,128)(2,1)S(1)}, bf16[2,4,16,896]{3,2,1,0:T(8,128)(2,1)S(1)}, u32[]{:S(2)}, u32[]{:S(2)}) %collective-permute-start.9) | collective-permute-done | bytes 229408 | tf_op jit(solution)/shard_map/ppermute | solution.py:69
  35.8 1.7 collective-permute-done.10
  37.6 1.2 collective-permute-done.11
  39.2 2.1 collective-permute-start.14
  41.2 2.9 %collective-permute-start.15 = (bf16[2,4,4,16,896]{4,3,2,1,0:T(8,128)(2,1)S(1)}, bf16[2,4,4,16,896]{4,3,2,1,0:T(8,128)(2,1)S(1)}, u32[]{:S(2)}, u32[]{:S(2)}) collective-permute-start(bf16[2,4,4,16,896]{4,3,2,1,0:T(8,128)(2,1)S(1)} %bitcast_dynamic-update-slice_fusion.3.refs_2_), channel_id=1, source_target_pairs={{0,1},{1,16},{2,3},{3,18},{4,5},{5,20},{6,7},{7,22},{8,25},{9,8},{... | collective-permute-start | bytes 2752520 | tf_op jit(solution)/shard_map/ppermute | solution.py:69
  44.1 5.3 %plan.1.refs_0_ = s32[2,325]{1,0:T(2,128)S(1)} custom-call(s32[2,256]{1,0:T(2,128)S(1)} %pad_add_fusion.meta), custom_call_target="tpu_custom_call" | custom-call | flops 2147483648 | bytes 4096 | tf_op jit(solution)/shard_map/plan/pallas_call | solution.py:208
  49.4 2.4 %collective-permute-done.14.refs_7_ = bf16[2,2,4,32,896]{4,3,2,1,0:T(8,128)(2,1)S(1)} collective-permute-done((bf16[2,2,4,32,896]{4,3,2,1,0:T(8,128)(2,1)S(1)}, bf16[2,2,4,32,896]{4,3,2,1,0:T(8,128)(2,1)S(1)}, u32[]{:S(2)}, u32[]{:S(2)}) %collective-permute-start.14) | collective-permute-done | bytes 917536 | tf_op jit(solution)/shard_map/ppermute | solution.py:69
  51.8 3.2 %collective-permute-start.20 = (bf16[2,2,4,32,896]{4,3,2,1,0:T(8,128)(2,1)S(1)}, bf16[2,2,4,32,896]{4,3,2,1,0:T(8,128)(2,1)S(1)}, u32[]{:S(2)}, u32[]{:S(2)}) collective-permute-start(bf16[2,2,4,32,896]{4,3,2,1,0:T(8,128)(2,1)S(1)} %get-tuple-element.65.refs_0_), channel_id=1, source_target_pairs={{0,96},{1,97},{2,98},{3,99},{4,100},{5,101},{6,102},{7,103},{8,14}... | collective-permute-start | bytes 2752520 | tf_op jit(solution)/shard_map/ppermute | solution.py:69
  55.0 6.0 %collective-permute-done.15.refs_5_ = bf16[2,4,4,16,896]{4,3,2,1,0:T(8,128)(2,1)S(1)} collective-permute-done((bf16[2,4,4,16,896]{4,3,2,1,0:T(8,128)(2,1)S(1)}, bf16[2,4,4,16,896]{4,3,2,1,0:T(8,128)(2,1)S(1)}, u32[]{:S(2)}, u32[]{:S(2)}) %collective-permute-start.15) | collective-permute-done | bytes 917536 | tf_op jit(solution)/shard_map/ppermute | solution.py:69
  61.0 6.4 %collective-permute-done.17.refs_8_ = bf16[2,4,4,16,896]{4,3,2,1,0:T(8,128)(2,1)S(1)} collective-permute-done((bf16[2,4,4,16,896]{4,3,2,1,0:T(8,128)(2,1)S(1)}, bf16[2,4,4,16,896]{4,3,2,1,0:T(8,128)(2,1)S(1)}, u32[]{:S(2)}, u32[]{:S(2)}) %collective-permute-start.17) | collective-permute-done | bytes 917536 | tf_op jit(solution)/shard_map/ppermute | solution.py:69
  67.5 1.7 collective-permute-start.16
  69.2 5.1 %near.1 = bf16[4,2,2,4,2,48,896]{6,5,4,3,2,1,0:T(8,128)(2,1)S(1)} custom-call(bf16[2,2,4,32,896]{4,3,2,1,0:T(8,128)(2,1)S(1)} %get-tuple-element.65.refs_0_, bf16[2,2,4,32,896]{4,3,2,1,0:T(8,128)(2,1)S(1)} %get-tuple-element.64.refs_1_, bf16[2,4,4,16,896]{4,3,2,1,0:T(8,128)(2,1)S(1)} %bitcast_dynamic-update-slice_fusion.3.refs_2_, ...), custom_call_target="tpu_custom_call" | custom-call | tf_op jit(solution)/shard_map/near/pallas_call | solution.py:139
  74.3 5.7 %collective-permute-done.18.rest = bf16[2,4,4,16,896]{4,3,2,1,0:T(8,128)(2,1)S(1)} collective-permute-done((bf16[2,4,4,16,896]{4,3,2,1,0:T(8,128)(2,1)S(1)}, bf16[2,4,4,16,896]{4,3,2,1,0:T(8,128)(2,1)S(1)}, u32[]{:S(2)}, u32[]{:S(2)}) %collective-permute-start.18) | collective-permute-done | bytes 917536 | tf_op jit(solution)/shard_map/ppermute | solution.py:69
  80.0 2.9 %collective-permute-done.13.main0 = bf16[2,2,4,32,896]{4,3,2,1,0:T(8,128)(2,1)S(1)} collective-permute-done((bf16[2,2,4,32,896]{4,3,2,1,0:T(8,128)(2,1)S(1)}, bf16[2,2,4,32,896]{4,3,2,1,0:T(8,128)(2,1)S(1)}, u32[]{:S(2)}, u32[]{:S(2)}) %collective-permute-start.13) | collective-permute-done | bytes 917536 | tf_op jit(solution)/shard_map/ppermute | solution.py:69
  82.9 1.7 far.1
  84.7 2.6 %collective-permute-start.21 = (bf16[768,896]{1,0:T(8,128)(2,1)S(1)}, bf16[768,896]{1,0:T(8,128)(2,1)S(1)}, u32[]{:S(2)}, u32[]{:S(2)}) collective-permute-start(bf16[768,896]{1,0:T(8,128)(2,1)S(1)} %bitcast.70), channel_id=1, source_target_pairs={{0,8},{1,9},{2,10},{3,11},{4,12},{5,13},{6,14},{7,15},{8,0},{9,1},... | collective-permute-start | bytes 4128776 | tf_op jit(solution)/shard_map/ppermute | solution.py:69
  87.2 4.4 %multiply.2.refs_0_.refs_1_ = bf16[768,896]{1,0:T(8,128)(2,1)S(1)} custom-call(s32[2,325]{1,0:T(2,128)S(1)} %plan.1.refs_0_, bf16[96,128,128]{2,1,0:T(8,128)(2,1)S(1)} %collective-permute-done.4.refs_1_, bf16[4,2,2,4,2,48,896]{6,5,4,3,2,1,0:T(8,128)(2,1)S(1)} %get-tuple-element.70.refs_2_), custom_call_target="tpu_custom_call" | custom-call | flops 2818572288 | bytes 8388608 | tf_op jit(solution)/shard_map/multiply/pallas_call | solution.py:256
  91.7 2.0 cross.2
  94.1 5.2 %multiply.3.refs_0_ = bf16[768,896]{1,0:T(8,128)(2,1)S(1)} custom-call(s32[2,325]{1,0:T(2,128)S(1)} %plan.1.refs_0_, bf16[96,128,128]{2,1,0:T(8,128)(2,1)S(1)} %bitcast.69, bf16[4,2,2,4,2,48,896]{6,5,4,3,2,1,0:T(8,128)(2,1)S(1)} %get-tuple-element.70.refs_2_), custom_call_target="tpu_custom_call" | custom-call | flops 2818572288 | bytes 8388608 | tf_op jit(solution)/shard_map/multiply/pallas_call | solution.py:256
  99.3 1.8 cross.3
  101.1 1.7 collective-permute-start.30
  102.8 2.5 %collective-permute-start.32 = (bf16[208,896]{1,0:T(8,128)(2,1)S(1)}, bf16[208,896]{1,0:T(8,128)(2,1)S(1)}, u32[]{:S(2)}, u32[]{:S(2)}) collective-permute-start(bf16[208,896]{1,0:T(8,128)(2,1)S(1)} %get-tuple-element.80), channel_id=1, source_target_pairs={{0,4},{1,5},{2,6},{3,7},{4,0},{5,1},{6,2},{7,3},{8,12},{9,13},{10,... | collective-permute-start | bytes 1118216 | tf_op jit(solution)/shard_map/ppermute | solution.py:69
  105.3 5.5 %collective-permute-done.22.refs_1_ = bf16[416,896]{1,0:T(8,128)(2,1)S(1)} collective-permute-done((bf16[416,896]{1,0:T(8,128)(2,1)S(1)}, bf16[416,896]{1,0:T(8,128)(2,1)S(1)}, u32[]{:S(2)}, u32[]{:S(2)}) %collective-permute-start.22) | collective-permute-done | bytes 745504 | tf_op jit(solution)/shard_map/ppermute | solution.py:69
  111.2 2.1 collective-permute-done.31.refs_2_
  113.3 8.5 %collective-permute-done.32.refs_3_ = bf16[208,896]{1,0:T(8,128)(2,1)S(1)} collective-permute-done((bf16[208,896]{1,0:T(8,128)(2,1)S(1)}, bf16[208,896]{1,0:T(8,128)(2,1)S(1)}, u32[]{:S(2)}, u32[]{:S(2)}) %collective-permute-start.32) | collective-permute-done | bytes 372768 | tf_op jit(solution)/shard_map/ppermute | solution.py:69
  122.3 3.1 %collective-permute-start.23 = (bf16[104,896]{1,0:T(8,128)(2,1)S(1)}, bf16[104,896]{1,0:T(8,128)(2,1)S(1)}, u32[]{:S(2)}, u32[]{:S(2)}) collective-permute-start(bf16[104,896]{1,0:T(8,128)(2,1)S(1)} %get-tuple-element.74), channel_id=1, source_target_pairs={{0,2},{1,3},{2,4},{3,5},{4,6},{5,7},{6,0},{7,1},{8,14},{9,15},{10,... | collective-permute-start | bytes 559112 | tf_op jit(solution)/shard_map/ppermute | solution.py:69
  125.4 1.2 collective-permute-start.25
  126.6 1.6 collective-permute-done.33
  128.7 3.3 %collective-permute-done.24 = bf16[104,896]{1,0:T(8,128)(2,1)S(1)} collective-permute-done((bf16[104,896]{1,0:T(8,128)(2,1)S(1)}, bf16[104,896]{1,0:T(8,128)(2,1)S(1)}, u32[]{:S(2)}, u32[]{:S(2)}) %collective-permute-start.24) | collective-permute-done | bytes 186400 | tf_op jit(solution)/shard_map/ppermute | solution.py:69
  132.0 2.7 %collective-permute-done.25 = bf16[104,896]{1,0:T(8,128)(2,1)S(1)} collective-permute-done((bf16[104,896]{1,0:T(8,128)(2,1)S(1)}, bf16[104,896]{1,0:T(8,128)(2,1)S(1)}, u32[]{:S(2)}, u32[]{:S(2)}) %collective-permute-start.25) | collective-permute-done | bytes 186400 | tf_op jit(solution)/shard_map/ppermute | solution.py:69
  134.9 1.6 collective-permute-start.26
  138.8 1.4 collective-permute-start.27
  140.3 1.1 collective-permute-start.29
  141.4 2.9 %collective-permute-done.35 = bf16[104,896]{1,0:T(8,128)(2,1)S(1)} collective-permute-done((bf16[104,896]{1,0:T(8,128)(2,1)S(1)}, bf16[104,896]{1,0:T(8,128)(2,1)S(1)}, u32[]{:S(2)}, u32[]{:S(2)}) %collective-permute-start.35) | collective-permute-done | bytes 186400 | tf_op jit(solution)/shard_map/ppermute | solution.py:69
  144.6 6.9 %collective-permute-done.28 = bf16[104,896]{1,0:T(8,128)(2,1)S(1)} collective-permute-done((bf16[104,896]{1,0:T(8,128)(2,1)S(1)}, bf16[104,896]{1,0:T(8,128)(2,1)S(1)}, u32[]{:S(2)}, u32[]{:S(2)}) %collective-permute-start.28) | collective-permute-done | bytes 186400 | tf_op jit(solution)/shard_map/ppermute | solution.py:69
  152.5 1.5 collective-permute-start.38
  154.3 7.8 %collective-permute-done.37.refs_5_ = bf16[208,896]{1,0:T(8,128)(2,1)S(1)} collective-permute-done((bf16[208,896]{1,0:T(8,128)(2,1)S(1)}, bf16[208,896]{1,0:T(8,128)(2,1)S(1)}, u32[]{:S(2)}, u32[]{:S(2)}) %collective-permute-start.37) | collective-permute-done | bytes 372768 | tf_op jit(solution)/shard_map/ppermute | solution.py:69
  162.2 2.9 %collective-permute-done.38.refs_6_ = bf16[208,896]{1,0:T(8,128)(2,1)S(1)} collective-permute-done((bf16[208,896]{1,0:T(8,128)(2,1)S(1)}, bf16[208,896]{1,0:T(8,128)(2,1)S(1)}, u32[]{:S(2)}, u32[]{:S(2)}) %collective-permute-start.38) | collective-permute-done | bytes 372768 | tf_op jit(solution)/shard_map/ppermute | solution.py:69
  165.1 4.7 %collective-permute-done.39.refs_7_ = bf16[208,896]{1,0:T(8,128)(2,1)S(1)} collective-permute-done((bf16[208,896]{1,0:T(8,128)(2,1)S(1)}, bf16[208,896]{1,0:T(8,128)(2,1)S(1)}, u32[]{:S(2)}, u32[]{:S(2)}) %collective-permute-start.39) | collective-permute-done | bytes 372768 | tf_op jit(solution)/shard_map/ppermute | solution.py:69
  169.8 5.7 %exchange.1 = (f32[416,768]{1,0:T(8,128)S(1)}, f32[416,768]{1,0:T(8,128)S(1)}) custom-call(bf16[768,896]{1,0:T(8,128)(2,1)} %copy-done.2, bf16[768,896]{1,0:T(8,128)(2,1)} %copy-done.1, bf16[416,896]{1,0:T(8,128)(2,1)S(1)} %constant_dynamic-update-slice_fusion.6.refs_2_, bf16[416,896]{1,0:T(8,128)(2,1)S(1)} %collective-permute-done.36.refs_3_, ...), custom_call_target="tpu_custom_call" | custom-call | flops 2466250752 | bytes 8388608 | tf_op jit(solution)/shard_map/exchange/pallas_call | solution.py:388
  175.5 3.1 %collective-permute-start.40 = (f32[416,768]{1,0:T(8,128)S(1)}, f32[416,768]{1,0:T(8,128)S(1)}, u32[]{:S(2)}, u32[]{:S(2)}) collective-permute-start(f32[416,768]{1,0:T(8,128)S(1)} %get-tuple-element.90), channel_id=1, source_target_pairs={{0,8},{1,9},{2,10},{3,11},{4,12},{5,13},{6,14},{7,15},{8,0},{9,1},... | collective-permute-start | bytes 3833864 | tf_op jit(solution)/shard_map/ppermute | solution.py:69
  178.7 2.6 %collective-permute-done.40.refs_1_ = f32[416,768]{1,0:T(8,128)S(1)} collective-permute-done((f32[416,768]{1,0:T(8,128)S(1)}, f32[416,768]{1,0:T(8,128)S(1)}, u32[]{:S(2)}, u32[]{:S(2)}) %collective-permute-start.40) | collective-permute-done | bytes 1277984 | tf_op jit(solution)/shard_map/ppermute | solution.py:69
  181.6 1.5 collective-permute-start.42
  184.0 2.6 %collective-permute-done.41 = bf16[104,768]{1,0:T(8,128)(2,1)S(1)} collective-permute-done((bf16[104,768]{1,0:T(8,128)(2,1)S(1)}, bf16[104,768]{1,0:T(8,128)(2,1)S(1)}, u32[]{:S(2)}, u32[]{:S(2)}) %collective-permute-start.41) | collective-permute-done | bytes 159776 | tf_op jit(solution)/shard_map/ppermute | solution.py:69
  186.6 5.0 %collective-permute-done.42 = bf16[104,768]{1,0:T(8,128)(2,1)S(1)} collective-permute-done((bf16[104,768]{1,0:T(8,128)(2,1)S(1)}, bf16[104,768]{1,0:T(8,128)(2,1)S(1)}, u32[]{:S(2)}, u32[]{:S(2)}) %collective-permute-start.42) | collective-permute-done | bytes 159776 | tf_op jit(solution)/shard_map/ppermute | solution.py:69
  191.8 6.0 %collective-permute-start.44 = (f32[104,768]{1,0:T(8,128)S(1)}, f32[104,768]{1,0:T(8,128)S(1)}, u32[]{:S(2)}, u32[]{:S(2)}) collective-permute-start(f32[104,768]{1,0:T(8,128)S(1)} %add_add_fusion), channel_id=1, source_target_pairs={{0,16},{1,17},{2,18},{3,19},{4,20},{5,21},{6,22},{7,23},{8,24},{9,... | collective-permute-start | bytes 958472 | tf_op jit(solution)/shard_map/ppermute | solution.py:69
  197.8 6.8 %collective-permute-done.44 = f32[104,768]{1,0:T(8,128)S(1)} collective-permute-done((f32[104,768]{1,0:T(8,128)S(1)}, f32[104,768]{1,0:T(8,128)S(1)}, u32[]{:S(2)}, u32[]{:S(2)}) %collective-permute-start.44) | collective-permute-done | bytes 319520 | tf_op jit(solution)/shard_map/ppermute | solution.py:69
  204.7 1.5 collective-permute-start.46
  206.2 2.2 collective-permute-start.47
  208.8 1.3 collective-permute-done.46
  210.1 4.9 %collective-permute-done.47 = bf16[104,768]{1,0:T(8,128)(2,1)S(1)} collective-permute-done((bf16[104,768]{1,0:T(8,128)(2,1)S(1)}, bf16[104,768]{1,0:T(8,128)(2,1)S(1)}, u32[]{:S(2)}, u32[]{:S(2)}) %collective-permute-start.47) | collective-permute-done | bytes 159776 | tf_op jit(solution)/shard_map/ppermute | solution.py:69
  215.0 1.9 collective-permute-start.48
  216.9 1.7 collective-permute-done.48.others
  218.6 2.0 widen.1
  (99 shorter events, 15.9 us)
Async XLA Ops:
  0.0 10.8 %copy-start.4 = (s32[1,96]{1,0:T(1,128)S(1)}, s32[1,96]{1,0:T(1,128)}, u32[]{:S(2)}) copy-start(s32[1,96]{1,0:T(1,128)} %param.7) | copy-start | bytes 1156
  0.0 10.8 %copy-start.3 = (s32[1,96]{1,0:T(1,128)S(1)}, s32[1,96]{1,0:T(1,128)}, u32[]{:S(2)}) copy-start(s32[1,96]{1,0:T(1,128)} %param.8) | copy-start | bytes 1156
  0.9 2.4 %collective-permute-start = (bf16[48,800]{1,0:T(8,128)(2,1)S(1)}, bf16[48,800]{1,0:T(8,128)(2,1)S(1)}, u32[]{:S(2)}, u32[]{:S(2)}) collective-permute-start(bf16[48,800]{1,0:T(8,128)(2,1)S(1)} %broadcast_select_fusion.2), channel_id=1, source_target_pairs={{0,8},{1,9},{2,10},{3,11},{4,12},{5,13},{6,14},{7,15},{8,0},{9,1},... | collective-permute-start | bytes 230408 | tf_op jit(solution)/shard_map/ppermute | solution.py:69
  3.4 11.4 %collective-permute-start.4 = (bf16[96,128,128]{2,1,0:T(8,128)(2,1)}, bf16[96,128,128]{2,1,0:T(8,128)(2,1)S(1)}, u32[]{:S(2)}, u32[]{:S(2)}) collective-permute-start(bf16[96,128,128]{2,1,0:T(8,128)(2,1)} %bitcast.68), channel_id=1, source_target_pairs={{0,8},{1,9},{2,10},{3,11},{4,12},{5,13},{6,14},{7,15},{8,0},{9,1},... | collective-permute-start | bytes 9437192 | tf_op jit(solution)/shard_map/ppermute | solution.py:69
  4.7 6.1 %collective-permute-start.1 = (bf16[2,48,896]{2,1,0:T(8,128)(2,1)S(1)}, bf16[2,48,896]{2,1,0:T(8,128)(2,1)}, u32[]{:S(2)}, u32[]{:S(2)}) collective-permute-start(bf16[2,48,896]{2,1,0:T(8,128)(2,1)S(1)} %fusion.10), channel_id=1, source_target_pairs={{0,2},{1,3},{2,4},{3,5},{4,6},{5,7},{6,0},{7,1},{8,40},{9,41},{10,... | collective-permute-start | bytes 516104 | tf_op jit(solution)/shard_map/ppermute | solution.py:69
  6.8 6.1 %collective-permute-start.2 = (bf16[2,48,896]{2,1,0:T(8,128)(2,1)S(1)}, bf16[2,48,896]{2,1,0:T(8,128)(2,1)S(1)}, u32[]{:S(2)}, u32[]{:S(2)}) collective-permute-start(bf16[2,48,896]{2,1,0:T(8,128)(2,1)S(1)} %fusion.10), channel_id=1, source_target_pairs={{0,6},{1,7},{2,0},{3,1},{4,2},{5,3},{6,4},{7,5},{8,104},{9,105},{1... | collective-permute-start | bytes 516104 | tf_op jit(solution)/shard_map/ppermute | solution.py:69
  8.7 6.1 %collective-permute-start.3 = (bf16[2,48,896]{2,1,0:T(8,128)(2,1)S(1)}, bf16[2,48,896]{2,1,0:T(8,128)(2,1)S(1)}, u32[]{:S(2)}, u32[]{:S(2)}) collective-permute-start(bf16[2,48,896]{2,1,0:T(8,128)(2,1)S(1)} %fusion.10), channel_id=1, source_target_pairs={{0,4},{1,5},{2,6},{3,7},{4,0},{5,1},{6,2},{7,3},{8,72},{9,73},{10,... | collective-permute-start | bytes 516104 | tf_op jit(solution)/shard_map/ppermute | solution.py:69
  14.9 9.2 %collective-permute-start.5 = (bf16[2,4,32,896]{3,2,1,0:T(8,128)(2,1)S(1)}, bf16[2,4,32,896]{3,2,1,0:T(8,128)(2,1)S(1)}, u32[]{:S(2)}, u32[]{:S(2)}) collective-permute-start(bf16[2,4,32,896]{3,2,1,0:T(8,128)(2,1)S(1)} %slice.39), channel_id=1, source_target_pairs={{0,1},{1,16},{2,3},{3,18},{4,5},{5,20},{6,7},{7,22},{8,25},{9,8},{... | collective-permute-start | bytes 1376264 | tf_op jit(solution)/shard_map/ppermute | solution.py:69
  24.1 5.2 %collective-permute-start.6 = (s32[1,256]{1,0:T(1,128)S(1)}, s32[1,256]{1,0:T(1,128)S(1)}, u32[]{:S(2)}, u32[]{:S(2)}) collective-permute-start(s32[1,256]{1,0:T(1,128)S(1)} %bitcast.73), channel_id=1, source_target_pairs={{0,8},{1,9},{2,10},{3,11},{4,12},{5,13},{6,14},{7,15},{8,0},{9,1},... | collective-permute-start | bytes 3080 | tf_op jit(solution)/shard_map/ppermute | solution.py:69
  26.6 12.2 %collective-permute-start.7 = (bf16[2,4,32,896]{3,2,1,0:T(8,128)(2,1)S(1)}, bf16[2,4,32,896]{3,2,1,0:T(8,128)(2,1)S(1)}, u32[]{:S(2)}, u32[]{:S(2)}) collective-permute-start(bf16[2,4,32,896]{3,2,1,0:T(8,128)(2,1)S(1)} %slice.39), channel_id=1, source_target_pairs={{0,17},{1,0},{2,19},{3,2},{4,21},{5,4},{6,23},{7,6},{8,9},{9,24},{... | collective-permute-start | bytes 1376264 | tf_op jit(solution)/shard_map/ppermute | solution.py:69
  26.6 12.5 %collective-permute-start.8 = (bf16[2,4,32,896]{3,2,1,0:T(8,128)(2,1)S(1)}, bf16[2,4,32,896]{3,2,1,0:T(8,128)(2,1)S(1)}, u32[]{:S(2)}, u32[]{:S(2)}) collective-permute-start(bf16[2,4,32,896]{3,2,1,0:T(8,128)(2,1)S(1)} %collective-permute-done.5), channel_id=1, source_target_pairs={{0,1},{1,16},{2,3},{3,18},{4,5},{5,20},{6,7},{7,22},{8,25},{9,8},{... | collective-permute-start | bytes 1376264 | tf_op jit(solution)/shard_map/ppermute | solution.py:69
  29.3 6.4 %collective-permute-start.9 = (bf16[2,4,16,896]{3,2,1,0:T(8,128)(2,1)S(1)}, bf16[2,4,16,896]{3,2,1,0:T(8,128)(2,1)S(1)}, u32[]{:S(2)}, u32[]{:S(2)}) collective-permute-start(bf16[2,4,16,896]{3,2,1,0:T(8,128)(2,1)S(1)} %slice.38), channel_id=1, source_target_pairs={{0,32},{1,33},{2,34},{3,35},{4,36},{5,37},{6,38},{7,39},{8,10},{9,... | collective-permute-start | bytes 688136 | tf_op jit(solution)/shard_map/ppermute | solution.py:69
  29.9 7.7 %collective-permute-start.10 = (bf16[2,4,16,896]{3,2,1,0:T(8,128)(2,1)S(1)}, bf16[2,4,16,896]{3,2,1,0:T(8,128)(2,1)S(1)}, u32[]{:S(2)}, u32[]{:S(2)}) collective-permute-start(bf16[2,4,16,896]{3,2,1,0:T(8,128)(2,1)S(1)} %slice.38), channel_id=1, source_target_pairs={{0,96},{1,97},{2,98},{3,99},{4,100},{5,101},{6,102},{7,103},{8,14}... | collective-permute-start | bytes 688136 | tf_op jit(solution)/shard_map/ppermute | solution.py:69
  32.1 6.7 %collective-permute-start.11 = (bf16[2,4,16,896]{3,2,1,0:T(8,128)(2,1)S(1)}, bf16[2,4,16,896]{3,2,1,0:T(8,128)(2,1)S(1)}, u32[]{:S(2)}, u32[]{:S(2)}) collective-permute-start(bf16[2,4,16,896]{3,2,1,0:T(8,128)(2,1)S(1)} %slice.38), channel_id=1, source_target_pairs={{0,64},{1,65},{2,66},{3,67},{4,68},{5,69},{6,70},{7,71},{8,12},{9,... | collective-permute-start | bytes 688136 | tf_op jit(solution)/shard_map/ppermute | solution.py:69
  39.2 12.6 %collective-permute-start.14 = (bf16[2,2,4,32,896]{4,3,2,1,0:T(8,128)(2,1)S(1)}, bf16[2,2,4,32,896]{4,3,2,1,0:T(8,128)(2,1)S(1)}, u32[]{:S(2)}, u32[]{:S(2)}) collective-permute-start(bf16[2,2,4,32,896]{4,3,2,1,0:T(8,128)(2,1)S(1)} %get-tuple-element.64.refs_1_), channel_id=1, source_target_pairs={{0,96},{1,97},{2,98},{3,99},{4,100},{5,101},{6,102},{7,103},{8,14}... | collective-permute-start | bytes 2752520 | tf_op jit(solution)/shard_map/ppermute | solution.py:69
  41.2 13.8 %collective-permute-start.12 = (bf16[2,2,4,32,896]{4,3,2,1,0:T(8,128)(2,1)S(1)}, bf16[2,2,4,32,896]{4,3,2,1,0:T(8,128)(2,1)S(1)}, u32[]{:S(2)}, u32[]{:S(2)}) collective-permute-start(bf16[2,2,4,32,896]{4,3,2,1,0:T(8,128)(2,1)S(1)} %get-tuple-element.65.refs_0_), channel_id=1, source_target_pairs={{0,32},{1,33},{2,34},{3,35},{4,36},{5,37},{6,38},{7,39},{8,10},{9,... | collective-permute-start | bytes 2752520 | tf_op jit(solution)/shard_map/ppermute | solution.py:69
  41.2 19.8 %collective-permute-start.15 = (bf16[2,4,4,16,896]{4,3,2,1,0:T(8,128)(2,1)S(1)}, bf16[2,4,4,16,896]{4,3,2,1,0:T(8,128)(2,1)S(1)}, u32[]{:S(2)}, u32[]{:S(2)}) collective-permute-start(bf16[2,4,4,16,896]{4,3,2,1,0:T(8,128)(2,1)S(1)} %bitcast_dynamic-update-slice_fusion.3.refs_2_), channel_id=1, source_target_pairs={{0,1},{1,16},{2,3},{3,18},{4,5},{5,20},{6,7},{7,22},{8,25},{9,8},{... | collective-permute-start | bytes 2752520 | tf_op jit(solution)/shard_map/ppermute | solution.py:69
  44.1 23.4 %collective-permute-start.17 = (bf16[2,4,4,16,896]{4,3,2,1,0:T(8,128)(2,1)S(1)}, bf16[2,4,4,16,896]{4,3,2,1,0:T(8,128)(2,1)S(1)}, u32[]{:S(2)}, u32[]{:S(2)}) collective-permute-start(bf16[2,4,4,16,896]{4,3,2,1,0:T(8,128)(2,1)S(1)} %bitcast_dynamic-update-slice_fusion.3.refs_2_), channel_id=1, source_target_pairs={{0,17},{1,0},{2,19},{3,2},{4,21},{5,4},{6,23},{7,6},{8,9},{9,24},{... | collective-permute-start | bytes 2752520 | tf_op jit(solution)/shard_map/ppermute | solution.py:69
  51.8 17.4 %collective-permute-start.20 = (bf16[2,2,4,32,896]{4,3,2,1,0:T(8,128)(2,1)S(1)}, bf16[2,2,4,32,896]{4,3,2,1,0:T(8,128)(2,1)S(1)}, u32[]{:S(2)}, u32[]{:S(2)}) collective-permute-start(bf16[2,2,4,32,896]{4,3,2,1,0:T(8,128)(2,1)S(1)} %get-tuple-element.65.refs_0_), channel_id=1, source_target_pairs={{0,96},{1,97},{2,98},{3,99},{4,100},{5,101},{6,102},{7,103},{8,14}... | collective-permute-start | bytes 2752520 | tf_op jit(solution)/shard_map/ppermute | solution.py:69
  55.0 14.2 %collective-permute-start.19 = (bf16[2,2,4,32,896]{4,3,2,1,0:T(8,128)(2,1)S(1)}, bf16[2,2,4,32,896]{4,3,2,1,0:T(8,128)(2,1)S(1)}, u32[]{:S(2)}, u32[]{:S(2)}) collective-permute-start(bf16[2,2,4,32,896]{4,3,2,1,0:T(8,128)(2,1)S(1)} %get-tuple-element.64.refs_1_), channel_id=1, source_target_pairs={{0,32},{1,33},{2,34},{3,35},{4,36},{5,37},{6,38},{7,39},{8,10},{9,... | collective-permute-start | bytes 2752520 | tf_op jit(solution)/shard_map/ppermute | solution.py:69
  67.5 12.5 %collective-permute-start.18 = (bf16[2,4,4,16,896]{4,3,2,1,0:T(8,128)(2,1)S(1)}, bf16[2,4,4,16,896]{4,3,2,1,0:T(8,128)(2,1)S(1)}, u32[]{:S(2)}, u32[]{:S(2)}) collective-permute-start(bf16[2,4,4,16,896]{4,3,2,1,0:T(8,128)(2,1)S(1)} %collective-permute-done.15.refs_5_), channel_id=1, source_target_pairs={{0,1},{1,16},{2,3},{3,18},{4,5},{5,20},{6,7},{7,22},{8,25},{9,8},{... | collective-permute-start | bytes 2752520 | tf_op jit(solution)/shard_map/ppermute | solution.py:69
  67.5 12.5 %collective-permute-start.16 = (bf16[2,2,4,32,896]{4,3,2,1,0:T(8,128)(2,1)S(1)}, bf16[2,2,4,32,896]{4,3,2,1,0:T(8,128)(2,1)S(1)}, u32[]{:S(2)}, u32[]{:S(2)}) collective-permute-start(bf16[2,2,4,32,896]{4,3,2,1,0:T(8,128)(2,1)S(1)} %collective-permute-done.14.refs_7_), channel_id=1, source_target_pairs={{0,96},{1,97},{2,98},{3,99},{4,100},{5,101},{6,102},{7,103},{8,14}... | collective-permute-start | bytes 2752520 | tf_op jit(solution)/shard_map/ppermute | solution.py:69
  69.2 13.8 %collective-permute-start.13 = (bf16[2,2,4,32,896]{4,3,2,1,0:T(8,128)(2,1)S(1)}, bf16[2,2,4,32,896]{4,3,2,1,0:T(8,128)(2,1)S(1)}, u32[]{:S(2)}, u32[]{:S(2)}) collective-permute-start(bf16[2,2,4,32,896]{4,3,2,1,0:T(8,128)(2,1)S(1)} %collective-permute-done.12.refs_3_), channel_id=1, source_target_pairs={{0,32},{1,33},{2,34},{3,35},{4,36},{5,37},{6,38},{7,39},{8,10},{9,... | collective-permute-start | bytes 2752520 | tf_op jit(solution)/shard_map/ppermute | solution.py:69
  84.7 7.0 %collective-permute-start.21 = (bf16[768,896]{1,0:T(8,128)(2,1)S(1)}, bf16[768,896]{1,0:T(8,128)(2,1)S(1)}, u32[]{:S(2)}, u32[]{:S(2)}) collective-permute-start(bf16[768,896]{1,0:T(8,128)(2,1)S(1)} %bitcast.70), channel_id=1, source_target_pairs={{0,8},{1,9},{2,10},{3,11},{4,12},{5,13},{6,14},{7,15},{8,0},{9,1},... | collective-permute-start | bytes 4128776 | tf_op jit(solution)/shard_map/ppermute | solution.py:69
  91.7 2.1 copy-start.1
  91.7 2.4 %copy-start = (bf16[1,96,128,128]{3,2,1,0:T(8,128)(2,1)S(1)}, bf16[1,96,128,128]{3,2,1,0:T(8,128)(2,1)}, u32[]{:S(2)}) copy-start(bf16[1,96,128,128]{3,2,1,0:T(8,128)(2,1)} %param.6) | copy-start | bytes 9437188
  93.7 17.1 %collective-permute-start.22 = (bf16[416,896]{1,0:T(8,128)(2,1)S(1)}, bf16[416,896]{1,0:T(8,128)(2,1)S(1)}, u32[]{:S(2)}, u32[]{:S(2)}) collective-permute-start(bf16[416,896]{1,0:T(8,128)(2,1)S(1)} %get-tuple-element.72), channel_id=1, source_target_pairs={{0,1},{1,0},{2,3},{3,2},{4,5},{5,4},{6,7},{7,6},{8,9},{9,8},{10,11... | collective-permute-start | bytes 2236424 | tf_op jit(solution)/shard_map/ppermute | solution.py:69
  99.3 1.8 copy-start.2
  101.1 10.1 %collective-permute-start.30 = (bf16[208,896]{1,0:T(8,128)(2,1)S(1)}, bf16[208,896]{1,0:T(8,128)(2,1)S(1)}, u32[]{:S(2)}, u32[]{:S(2)}) collective-permute-start(bf16[208,896]{1,0:T(8,128)(2,1)S(1)} %get-tuple-element.78), channel_id=1, source_target_pairs={{0,2},{1,3},{2,4},{3,5},{4,6},{5,7},{6,0},{7,1},{8,14},{9,15},{10,... | collective-permute-start | bytes 1118216 | tf_op jit(solution)/shard_map/ppermute | solution.py:69
  102.8 10.5 %collective-permute-start.31 = (bf16[208,896]{1,0:T(8,128)(2,1)S(1)}, bf16[208,896]{1,0:T(8,128)(2,1)S(1)}, u32[]{:S(2)}, u32[]{:S(2)}) collective-permute-start(bf16[208,896]{1,0:T(8,128)(2,1)S(1)} %get-tuple-element.79), channel_id=1, source_target_pairs={{0,6},{1,7},{2,0},{3,1},{4,2},{5,3},{6,4},{7,5},{8,10},{9,11},{10,... | collective-permute-start | bytes 1118216 | tf_op jit(solution)/shard_map/ppermute | solution.py:69
  102.8 19.0 %collective-permute-start.32 = (bf16[208,896]{1,0:T(8,128)(2,1)S(1)}, bf16[208,896]{1,0:T(8,128)(2,1)S(1)}, u32[]{:S(2)}, u32[]{:S(2)}) collective-permute-start(bf16[208,896]{1,0:T(8,128)(2,1)S(1)} %get-tuple-element.80), channel_id=1, source_target_pairs={{0,4},{1,5},{2,6},{3,7},{4,0},{5,1},{6,2},{7,3},{8,12},{9,13},{10,... | collective-permute-start | bytes 1118216 | tf_op jit(solution)/shard_map/ppermute | solution.py:69
  122.2 6.0 %collective-permute-start.33 = (bf16[104,896]{1,0:T(8,128)(2,1)S(1)}, bf16[104,896]{1,0:T(8,128)(2,1)S(1)}, u32[]{:S(2)}, u32[]{:S(2)}) collective-permute-start(bf16[104,896]{1,0:T(8,128)(2,1)S(1)} %get-tuple-element.86), channel_id=1, source_target_pairs={{0,1},{1,0},{2,3},{3,2},{4,5},{5,4},{6,7},{7,6},{8,9},{9,8},{10,11... | collective-permute-start | bytes 559112 | tf_op jit(solution)/shard_map/ppermute | solution.py:69
  122.3 6.4 %collective-permute-start.23 = (bf16[104,896]{1,0:T(8,128)(2,1)S(1)}, bf16[104,896]{1,0:T(8,128)(2,1)S(1)}, u32[]{:S(2)}, u32[]{:S(2)}) collective-permute-start(bf16[104,896]{1,0:T(8,128)(2,1)S(1)} %get-tuple-element.74), channel_id=1, source_target_pairs={{0,2},{1,3},{2,4},{3,5},{4,6},{5,7},{6,0},{7,1},{8,14},{9,15},{10,... | collective-permute-start | bytes 559112 | tf_op jit(solution)/shard_map/ppermute | solution.py:69
  125.4 6.6 %collective-permute-start.24 = (bf16[104,896]{1,0:T(8,128)(2,1)S(1)}, bf16[104,896]{1,0:T(8,128)(2,1)S(1)}, u32[]{:S(2)}, u32[]{:S(2)}) collective-permute-start(bf16[104,896]{1,0:T(8,128)(2,1)S(1)} %get-tuple-element.75), channel_id=1, source_target_pairs={{0,6},{1,7},{2,0},{3,1},{4,2},{5,3},{6,4},{7,5},{8,10},{9,11},{10,... | collective-permute-start | bytes 559112 | tf_op jit(solution)/shard_map/ppermute | solution.py:69
  125.4 9.3 %collective-permute-start.25 = (bf16[104,896]{1,0:T(8,128)(2,1)S(1)}, bf16[104,896]{1,0:T(8,128)(2,1)S(1)}, u32[]{:S(2)}, u32[]{:S(2)}) collective-permute-start(bf16[104,896]{1,0:T(8,128)(2,1)S(1)} %get-tuple-element.76), channel_id=1, source_target_pairs={{0,4},{1,5},{2,6},{3,7},{4,0},{5,1},{6,2},{7,3},{8,12},{9,13},{10,... | collective-permute-start | bytes 559112 | tf_op jit(solution)/shard_map/ppermute | solution.py:69
  134.9 2.7 %collective-permute-start.26 = (bf16[104,896]{1,0:T(8,128)(2,1)S(1)}, bf16[104,896]{1,0:T(8,128)(2,1)S(1)}, u32[]{:S(2)}, u32[]{:S(2)}) collective-permute-start(bf16[104,896]{1,0:T(8,128)(2,1)S(1)} %get-tuple-element.112), channel_id=1, source_target_pairs={{0,8},{1,9},{2,10},{3,11},{4,12},{5,13},{6,14},{7,15},{8,0},{9,1},... | collective-permute-start | bytes 559112 | tf_op jit(solution)/shard_map/ppermute | solution.py:69
  136.5 1.4 collective-permute-start.34
  138.2 6.1 %collective-permute-start.35 = (bf16[104,896]{1,0:T(8,128)(2,1)S(1)}, bf16[104,896]{1,0:T(8,128)(2,1)S(1)}, u32[]{:S(2)}, u32[]{:S(2)}) collective-permute-start(bf16[104,896]{1,0:T(8,128)(2,1)S(1)} %get-tuple-element.98), channel_id=1, source_target_pairs={{0,1},{1,0},{2,3},{3,2},{4,5},{5,4},{6,7},{7,6},{8,9},{9,8},{10,11... | collective-permute-start | bytes 559112 | tf_op jit(solution)/shard_map/ppermute | solution.py:69
  138.8 5.7 %collective-permute-start.27 = (bf16[104,896]{1,0:T(8,128)(2,1)S(1)}, bf16[104,896]{1,0:T(8,128)(2,1)S(1)}, u32[]{:S(2)}, u32[]{:S(2)}) collective-permute-start(bf16[104,896]{1,0:T(8,128)(2,1)S(1)} %get-tuple-element.110), channel_id=1, source_target_pairs={{0,2},{1,3},{2,4},{3,5},{4,6},{5,7},{6,0},{7,1},{8,14},{9,15},{10,... | collective-permute-start | bytes 559112 | tf_op jit(solution)/shard_map/ppermute | solution.py:69
  140.2 11.2 %collective-permute-start.28 = (bf16[104,896]{1,0:T(8,128)(2,1)S(1)}, bf16[104,896]{1,0:T(8,128)(2,1)S(1)}, u32[]{:S(2)}, u32[]{:S(2)}) collective-permute-start(bf16[104,896]{1,0:T(8,128)(2,1)S(1)} %get-tuple-element.110), channel_id=1, source_target_pairs={{0,6},{1,7},{2,0},{3,1},{4,2},{5,3},{6,4},{7,5},{8,10},{9,11},{10,... | collective-permute-start | bytes 559112 | tf_op jit(solution)/shard_map/ppermute | solution.py:69
  140.3 11.2 %collective-permute-start.29 = (bf16[104,896]{1,0:T(8,128)(2,1)S(1)}, bf16[104,896]{1,0:T(8,128)(2,1)S(1)}, u32[]{:S(2)}, u32[]{:S(2)}) collective-permute-start(bf16[104,896]{1,0:T(8,128)(2,1)S(1)} %get-tuple-element.110), channel_id=1, source_target_pairs={{0,4},{1,5},{2,6},{3,7},{4,0},{5,1},{6,2},{7,3},{8,12},{9,13},{10,... | collective-permute-start | bytes 559112 | tf_op jit(solution)/shard_map/ppermute | solution.py:69
  151.5 18.3 %collective-permute-start.36 = (bf16[416,896]{1,0:T(8,128)(2,1)S(1)}, bf16[416,896]{1,0:T(8,128)(2,1)S(1)}, u32[]{:S(2)}, u32[]{:S(2)}) collective-permute-start(bf16[416,896]{1,0:T(8,128)(2,1)S(1)} %constant_dynamic-update-slice_fusion.6.refs_2_), channel_id=1, source_target_pairs={{0,1},{1,0},{2,3},{3,2},{4,5},{5,4},{6,7},{7,6},{8,9},{9,8},{10,11... | collective-permute-start | bytes 2236424 | tf_op jit(solution)/shard_map/ppermute | solution.py:69
  152.5 9.6 %collective-permute-start.37 = (bf16[208,896]{1,0:T(8,128)(2,1)S(1)}, bf16[208,896]{1,0:T(8,128)(2,1)S(1)}, u32[]{:S(2)}, u32[]{:S(2)}) collective-permute-start(bf16[208,896]{1,0:T(8,128)(2,1)S(1)} %constant_dynamic-update-slice_fusion.4.refs_4_), channel_id=1, source_target_pairs={{0,2},{1,3},{2,4},{3,5},{4,6},{5,7},{6,0},{7,1},{8,14},{9,15},{10,... | collective-permute-start | bytes 1118216 | tf_op jit(solution)/shard_map/ppermute | solution.py:69
  152.5 12.5 %collective-permute-start.38 = (bf16[208,896]{1,0:T(8,128)(2,1)S(1)}, bf16[208,896]{1,0:T(8,128)(2,1)S(1)}, u32[]{:S(2)}, u32[]{:S(2)}) collective-permute-start(bf16[208,896]{1,0:T(8,128)(2,1)S(1)} %constant_dynamic-update-slice_fusion.4.refs_4_), channel_id=1, source_target_pairs={{0,6},{1,7},{2,0},{3,1},{4,2},{5,3},{6,4},{7,5},{8,10},{9,11},{10,... | collective-permute-start | bytes 1118216 | tf_op jit(solution)/shard_map/ppermute | solution.py:69
  154.0 15.8 %collective-permute-start.39 = (bf16[208,896]{1,0:T(8,128)(2,1)S(1)}, bf16[208,896]{1,0:T(8,128)(2,1)S(1)}, u32[]{:S(2)}, u32[]{:S(2)}) collective-permute-start(bf16[208,896]{1,0:T(8,128)(2,1)S(1)} %constant_dynamic-update-slice_fusion.4.refs_4_), channel_id=1, source_target_pairs={{0,4},{1,5},{2,6},{3,7},{4,0},{5,1},{6,2},{7,3},{8,12},{9,13},{10,... | collective-permute-start | bytes 1118216 | tf_op jit(solution)/shard_map/ppermute | solution.py:69
  175.5 5.7 %collective-permute-start.40 = (f32[416,768]{1,0:T(8,128)S(1)}, f32[416,768]{1,0:T(8,128)S(1)}, u32[]{:S(2)}, u32[]{:S(2)}) collective-permute-start(f32[416,768]{1,0:T(8,128)S(1)} %get-tuple-element.90), channel_id=1, source_target_pairs={{0,8},{1,9},{2,10},{3,11},{4,12},{5,13},{6,14},{7,15},{8,0},{9,1},... | collective-permute-start | bytes 3833864 | tf_op jit(solution)/shard_map/ppermute | solution.py:69
  181.5 5.2 %collective-permute-start.41 = (bf16[104,768]{1,0:T(8,128)(2,1)S(1)}, bf16[104,768]{1,0:T(8,128)(2,1)S(1)}, u32[]{:S(2)}, u32[]{:S(2)}) collective-permute-start(bf16[104,768]{1,0:T(8,128)(2,1)S(1)} %get-tuple-element.92), channel_id=1, source_target_pairs={{0,32},{1,33},{2,34},{3,35},{4,36},{5,37},{6,38},{7,39},{8,104},{9... | collective-permute-start | bytes 479240 | tf_op jit(solution)/shard_map/ppermute | solution.py:69
  181.6 10.1 %collective-permute-start.42 = (bf16[104,768]{1,0:T(8,128)(2,1)S(1)}, bf16[104,768]{1,0:T(8,128)(2,1)S(1)}, u32[]{:S(2)}, u32[]{:S(2)}) collective-permute-start(bf16[104,768]{1,0:T(8,128)(2,1)S(1)} %get-tuple-element.93), channel_id=1, source_target_pairs={{0,96},{1,97},{2,98},{3,99},{4,100},{5,101},{6,102},{7,103},{8,40}... | collective-permute-start | bytes 479240 | tf_op jit(solution)/shard_map/ppermute | solution.py:69
  183.0 8.7 %collective-permute-start.43 = (bf16[104,768]{1,0:T(8,128)(2,1)S(1)}, bf16[104,768]{1,0:T(8,128)(2,1)S(1)}, u32[]{:S(2)}, u32[]{:S(2)}) collective-permute-start(bf16[104,768]{1,0:T(8,128)(2,1)S(1)} %get-tuple-element.94), channel_id=1, source_target_pairs={{0,64},{1,65},{2,66},{3,67},{4,68},{5,69},{6,70},{7,71},{8,72},{9,... | collective-permute-start | bytes 479240 | tf_op jit(solution)/shard_map/ppermute | solution.py:69
  191.8 12.8 %collective-permute-start.44 = (f32[104,768]{1,0:T(8,128)S(1)}, f32[104,768]{1,0:T(8,128)S(1)}, u32[]{:S(2)}, u32[]{:S(2)}) collective-permute-start(f32[104,768]{1,0:T(8,128)S(1)} %add_add_fusion), channel_id=1, source_target_pairs={{0,16},{1,17},{2,18},{3,19},{4,20},{5,21},{6,22},{7,23},{8,24},{9,... | collective-permute-start | bytes 958472 | tf_op jit(solution)/shard_map/ppermute | solution.py:69
  204.6 4.2 %collective-permute-start.45 = (bf16[104,768]{1,0:T(8,128)(2,1)S(1)}, bf16[104,768]{1,0:T(8,128)(2,1)S(1)}, u32[]{:S(2)}, u32[]{:S(2)}) collective-permute-start(bf16[104,768]{1,0:T(8,128)(2,1)S(1)} %get-tuple-element.96), channel_id=1, source_target_pairs={{0,32},{1,33},{2,34},{3,35},{4,36},{5,37},{6,38},{7,39},{8,104},{9... | collective-permute-start | bytes 479240 | tf_op jit(solution)/shard_map/ppermute | solution.py:69
  204.7 5.4 %collective-permute-start.46 = (bf16[104,768]{1,0:T(8,128)(2,1)S(1)}, bf16[104,768]{1,0:T(8,128)(2,1)S(1)}, u32[]{:S(2)}, u32[]{:S(2)}) collective-permute-start(bf16[104,768]{1,0:T(8,128)(2,1)S(1)} %get-tuple-element.96), channel_id=1, source_target_pairs={{0,96},{1,97},{2,98},{3,99},{4,100},{5,101},{6,102},{7,103},{8,40}... | collective-permute-start | bytes 479240 | tf_op jit(solution)/shard_map/ppermute | solution.py:69
  206.2 8.9 %collective-permute-start.47 = (bf16[104,768]{1,0:T(8,128)(2,1)S(1)}, bf16[104,768]{1,0:T(8,128)(2,1)S(1)}, u32[]{:S(2)}, u32[]{:S(2)}) collective-permute-start(bf16[104,768]{1,0:T(8,128)(2,1)S(1)} %get-tuple-element.96), channel_id=1, source_target_pairs={{0,64},{1,65},{2,66},{3,67},{4,68},{5,69},{6,70},{7,71},{8,72},{9,... | collective-permute-start | bytes 479240 | tf_op jit(solution)/shard_map/ppermute | solution.py:69
  215.0 3.6 %collective-permute-start.48 = (bf16[416,768]{1,0:T(8,128)(2,1)S(1)}, bf16[416,768]{1,0:T(8,128)(2,1)S(1)}, u32[]{:S(2)}, u32[]{:S(2)}) collective-permute-start(bf16[416,768]{1,0:T(8,128)(2,1)S(1)} %constant_dynamic-update-slice_fusion.own), channel_id=1, source_target_pairs={{0,8},{1,9},{2,10},{3,11},{4,12},{5,13},{6,14},{7,15},{8,0},{9,1},... | collective-permute-start | bytes 1916936 | tf_op jit(solution)/shard_map/ppermute | solution.py:69

commit v11 on v9

--- a/solution.py
+++ b/solution.py
@@ -20,7 +20,7 @@
 SHARD = CROSS // 8
 OWN = 48
 STEP = 4
-UNROLL = 3
+UNROLL = 6
 FIELDS = 1 + 2 * STEP
 MOST = SLOTS // STEP + ROW_BLOCKS + UNROLL
 MAIN = 32
@@ -521,7 +521,7 @@
     parts = (mine, send(to_ahead, ahead), send(to_behind, behind), send(to_far, opposite))
     own, *sent = sum_chunks(chunks_x, 4, half_mine, from_low)
     second = (own, send(sent[0], ahead), send(sent[1], behind), send(sent[2], opposite))
-    parts, _ = lax.optimization_barrier((parts, sent))
+    parts, _ = lax.optimization_barrier((parts, second[1]))
     own, sent = sum_chunks(chunks_low, 2, *parts)
     first_shard = add(own, swap_low(sent))
     second_shard = add(*second)

time: 219 us -> 217 us (level)
  starting transfers between devices: 53.4 us -> 66.9 us
  waiting for transfers between devices: 124 us -> 112 us
  Pallas kernels: 35 us -> 32.2 us
    ppermute x49, starting transfers between devices: 53.4 us -> 66.9 us  [send(): return lax.ppermute(array, AXES, pairs)]
    ppermute x49, waiting for transfers between devices: 124 us -> 112 us  [send(): return lax.ppermute(array, AXES, pairs)]
  transfers between devices with their start and end apart: 49 -> 49, of which waited for: 34 -> 37; matrix products, arithmetic and copies ran while one was open for 1% -> 1% of each run, Pallas kernels for 11% -> 10%
where the time goes in v11:
time: 217 us
  waiting for transfers between devices  112 us (52%)
  starting transfers between devices  66.9 us (31%)
  Pallas kernels  32.2 us (15%)
  other arithmetic  2.57 us (1%)
  local copies, waits for them, and re-layouts  2.25 us (1%)
    ppermute x49, waiting for transfers between devices, send(): return lax.ppermute(array, AXES, pairs)  112 us
    ppermute x49, starting transfers between devices, send(): return lax.ppermute(array, AXES, pairs)  66.9 us
    pallas_call x2, Pallas kernels, multiply(): pl.pallas_call(kernel, out_shape=jax.ShapeDtypeStruct((ROWS, WIDE), bf16)...  8.6 us
    pallas_call x1, Pallas kernels, exchange(): pl.pallas_call(exchange_kernel, out_shape=[jax.ShapeDtypeStruct((CROSS //...  5.74 us
    pallas_call x1, Pallas kernels, panels_and_slab(): pl.pallas_call(near_kernel, out_shape=held, in_specs=[anywhere] * 9, out_...  5.12 us
    pallas_call x1, Pallas kernels, plan(): pl.pallas_call(plan_kernel, out_shape=jax.ShapeDtypeStruct((2, MOST * FIE...  4.72 us
  transfers between devices with their start and end apart: 49, of which 37 were waited for; matrix products, arithmetic and copies ran while one was open for 1% of the time, Pallas kernels for 10%

profile of v11, /device:TPU:1, one launch (start us, length us, event | category | flops | bytes accessed | tf_op | source)
XLA Modules:
  0.0 216.7 jit_solution(11873989960102655522)
XLA Ops:
  0.9 1.5 collective-permute-start
  4.7 1.4 collective-permute-start.1
  6.8 1.9 collective-permute-start.2
  8.7 1.3 collective-permute-start.3
  12.9 1.8 collective-permute-done.3
  14.9 3.8 %collective-permute-start.5 = (bf16[2,4,32,896]{3,2,1,0:T(8,128)(2,1)S(1)}, bf16[2,4,32,896]{3,2,1,0:T(8,128)(2,1)S(1)}, u32[]{:S(2)}, u32[]{:S(2)}) collective-permute-start(bf16[2,4,32,896]{3,2,1,0:T(8,128)(2,1)S(1)} %slice.39), channel_id=1, source_target_pairs={{0,1},{1,16},{2,3},{3,18},{4,5},{5,20},{6,7},{7,22},{8,25},{9,8},{... | collective-permute-start | bytes 1376264 | tf_op jit(solution)/shard_map/ppermute | solution.py:69
  18.9 5.2 %collective-permute-done.5 = bf16[2,4,32,896]{3,2,1,0:T(8,128)(2,1)S(1)} collective-permute-done((bf16[2,4,32,896]{3,2,1,0:T(8,128)(2,1)S(1)}, bf16[2,4,32,896]{3,2,1,0:T(8,128)(2,1)S(1)}, u32[]{:S(2)}, u32[]{:S(2)}) %collective-permute-start.5) | collective-permute-done | bytes 458784 | tf_op jit(solution)/shard_map/ppermute | solution.py:69
  24.1 2.5 %collective-permute-start.6 = (s32[1,256]{1,0:T(1,128)S(1)}, s32[1,256]{1,0:T(1,128)S(1)}, u32[]{:S(2)}, u32[]{:S(2)}) collective-permute-start(s32[1,256]{1,0:T(1,128)S(1)} %bitcast.73), channel_id=1, source_target_pairs={{0,8},{1,9},{2,10},{3,11},{4,12},{5,13},{6,14},{7,15},{8,0},{9,1},... | collective-permute-start | bytes 3080 | tf_op jit(solution)/shard_map/ppermute | solution.py:69
  26.6 2.7 %collective-permute-start.8 = (bf16[2,4,32,896]{3,2,1,0:T(8,128)(2,1)S(1)}, bf16[2,4,32,896]{3,2,1,0:T(8,128)(2,1)S(1)}, u32[]{:S(2)}, u32[]{:S(2)}) collective-permute-start(bf16[2,4,32,896]{3,2,1,0:T(8,128)(2,1)S(1)} %collective-permute-done.5), channel_id=1, source_target_pairs={{0,1},{1,16},{2,3},{3,18},{4,5},{5,20},{6,7},{7,22},{8,25},{9,8},{... | collective-permute-start | bytes 1376264 | tf_op jit(solution)/shard_map/ppermute | solution.py:69
  29.9 2.2 %collective-permute-start.10 = (bf16[2,4,16,896]{3,2,1,0:T(8,128)(2,1)S(1)}, bf16[2,4,16,896]{3,2,1,0:T(8,128)(2,1)S(1)}, u32[]{:S(2)}, u32[]{:S(2)}) collective-permute-start(bf16[2,4,16,896]{3,2,1,0:T(8,128)(2,1)S(1)} %slice.38), channel_id=1, source_target_pairs={{0,96},{1,97},{2,98},{3,99},{4,100},{5,101},{6,102},{7,103},{8,14}... | collective-permute-start | bytes 688136 | tf_op jit(solution)/shard_map/ppermute | solution.py:69
  32.5 3.3 %collective-permute-done.9 = bf16[2,4,16,896]{3,2,1,0:T(8,128)(2,1)S(1)} collective-permute-done((bf16[2,4,16,896]{3,2,1,0:T(8,128)(2,1)S(1)}, bf16[2,4,16,896]{3,2,1,0:T(8,128)(2,1)S(1)}, u32[]{:S(2)}, u32[]{:S(2)}) %collective-permute-start.9) | collective-permute-done | bytes 229408 | tf_op jit(solution)/shard_map/ppermute | solution.py:69
  35.8 1.7 collective-permute-done.10
  37.6 1.2 collective-permute-done.11
  39.2 2.1 collective-permute-start.14
  41.2 2.9 %collective-permute-start.15 = (bf16[2,4,4,16,896]{4,3,2,1,0:T(8,128)(2,1)S(1)}, bf16[2,4,4,16,896]{4,3,2,1,0:T(8,128)(2,1)S(1)}, u32[]{:S(2)}, u32[]{:S(2)}) collective-permute-start(bf16[2,4,4,16,896]{4,3,2,1,0:T(8,128)(2,1)S(1)} %bitcast_dynamic-update-slice_fusion.3.refs_2_), channel_id=1, source_target_pairs={{0,1},{1,16},{2,3},{3,18},{4,5},{5,20},{6,7},{7,22},{8,25},{9,8},{... | collective-permute-start | bytes 2752520 | tf_op jit(solution)/shard_map/ppermute | solution.py:69
  44.1 4.7 %plan.1.refs_0_ = s32[2,325]{1,0:T(2,128)S(1)} custom-call(s32[2,256]{1,0:T(2,128)S(1)} %pad_add_fusion.meta), custom_call_target="tpu_custom_call" | custom-call | flops 2147483648 | bytes 4096 | tf_op jit(solution)/shard_map/plan/pallas_call | solution.py:208
  48.8 3.0 %collective-permute-done.14.refs_7_ = bf16[2,2,4,32,896]{4,3,2,1,0:T(8,128)(2,1)S(1)} collective-permute-done((bf16[2,2,4,32,896]{4,3,2,1,0:T(8,128)(2,1)S(1)}, bf16[2,2,4,32,896]{4,3,2,1,0:T(8,128)(2,1)S(1)}, u32[]{:S(2)}, u32[]{:S(2)}) %collective-permute-start.14) | collective-permute-done | bytes 917536 | tf_op jit(solution)/shard_map/ppermute | solution.py:69
  51.8 3.2 %collective-permute-start.20 = (bf16[2,2,4,32,896]{4,3,2,1,0:T(8,128)(2,1)S(1)}, bf16[2,2,4,32,896]{4,3,2,1,0:T(8,128)(2,1)S(1)}, u32[]{:S(2)}, u32[]{:S(2)}) collective-permute-start(bf16[2,2,4,32,896]{4,3,2,1,0:T(8,128)(2,1)S(1)} %get-tuple-element.65.refs_0_), channel_id=1, source_target_pairs={{0,96},{1,97},{2,98},{3,99},{4,100},{5,101},{6,102},{7,103},{8,14}... | collective-permute-start | bytes 2752520 | tf_op jit(solution)/shard_map/ppermute | solution.py:69
  55.0 6.0 %collective-permute-done.15.refs_5_ = bf16[2,4,4,16,896]{4,3,2,1,0:T(8,128)(2,1)S(1)} collective-permute-done((bf16[2,4,4,16,896]{4,3,2,1,0:T(8,128)(2,1)S(1)}, bf16[2,4,4,16,896]{4,3,2,1,0:T(8,128)(2,1)S(1)}, u32[]{:S(2)}, u32[]{:S(2)}) %collective-permute-start.15) | collective-permute-done | bytes 917536 | tf_op jit(solution)/shard_map/ppermute | solution.py:69
  61.0 6.4 %collective-permute-done.17.refs_8_ = bf16[2,4,4,16,896]{4,3,2,1,0:T(8,128)(2,1)S(1)} collective-permute-done((bf16[2,4,4,16,896]{4,3,2,1,0:T(8,128)(2,1)S(1)}, bf16[2,4,4,16,896]{4,3,2,1,0:T(8,128)(2,1)S(1)}, u32[]{:S(2)}, u32[]{:S(2)}) %collective-permute-start.17) | collective-permute-done | bytes 917536 | tf_op jit(solution)/shard_map/ppermute | solution.py:69
  67.5 1.7 collective-permute-start.16
  69.2 5.1 %near.1 = bf16[4,2,2,4,2,48,896]{6,5,4,3,2,1,0:T(8,128)(2,1)S(1)} custom-call(bf16[2,2,4,32,896]{4,3,2,1,0:T(8,128)(2,1)S(1)} %get-tuple-element.65.refs_0_, bf16[2,2,4,32,896]{4,3,2,1,0:T(8,128)(2,1)S(1)} %get-tuple-element.64.refs_1_, bf16[2,4,4,16,896]{4,3,2,1,0:T(8,128)(2,1)S(1)} %bitcast_dynamic-update-slice_fusion.3.refs_2_, ...), custom_call_target="tpu_custom_call" | custom-call | tf_op jit(solution)/shard_map/near/pallas_call | solution.py:139
  74.3 5.7 %collective-permute-done.18.rest = bf16[2,4,4,16,896]{4,3,2,1,0:T(8,128)(2,1)S(1)} collective-permute-done((bf16[2,4,4,16,896]{4,3,2,1,0:T(8,128)(2,1)S(1)}, bf16[2,4,4,16,896]{4,3,2,1,0:T(8,128)(2,1)S(1)}, u32[]{:S(2)}, u32[]{:S(2)}) %collective-permute-start.18) | collective-permute-done | bytes 917536 | tf_op jit(solution)/shard_map/ppermute | solution.py:69
  80.0 2.9 %collective-permute-done.13.main0 = bf16[2,2,4,32,896]{4,3,2,1,0:T(8,128)(2,1)S(1)} collective-permute-done((bf16[2,2,4,32,896]{4,3,2,1,0:T(8,128)(2,1)S(1)}, bf16[2,2,4,32,896]{4,3,2,1,0:T(8,128)(2,1)S(1)}, u32[]{:S(2)}, u32[]{:S(2)}) %collective-permute-start.13) | collective-permute-done | bytes 917536 | tf_op jit(solution)/shard_map/ppermute | solution.py:69
  82.9 1.7 far.1
  84.7 2.6 %collective-permute-start.21 = (bf16[768,896]{1,0:T(8,128)(2,1)S(1)}, bf16[768,896]{1,0:T(8,128)(2,1)S(1)}, u32[]{:S(2)}, u32[]{:S(2)}) collective-permute-start(bf16[768,896]{1,0:T(8,128)(2,1)S(1)} %bitcast.70), channel_id=1, source_target_pairs={{0,8},{1,9},{2,10},{3,11},{4,12},{5,13},{6,14},{7,15},{8,0},{9,1},... | collective-permute-start | bytes 4128776 | tf_op jit(solution)/shard_map/ppermute | solution.py:69
  87.2 5.5 %multiply.2.refs_0_.refs_1_ = bf16[768,896]{1,0:T(8,128)(2,1)S(1)} custom-call(s32[2,325]{1,0:T(2,128)S(1)} %plan.1.refs_0_, bf16[96,128,128]{2,1,0:T(8,128)(2,1)S(1)} %collective-permute-done.4.refs_1_, bf16[4,2,2,4,2,48,896]{6,5,4,3,2,1,0:T(8,128)(2,1)S(1)} %get-tuple-element.70.refs_2_), custom_call_target="tpu_custom_call" | custom-call | flops 2818572288 | bytes 8388608 | tf_op jit(solution)/shard_map/multiply/pallas_call | solution.py:256
  92.8 2.0 cross.2
  95.2 3.1 %multiply.3.refs_0_ = bf16[768,896]{1,0:T(8,128)(2,1)S(1)} custom-call(s32[2,325]{1,0:T(2,128)S(1)} %plan.1.refs_0_, bf16[96,128,128]{2,1,0:T(8,128)(2,1)S(1)} %bitcast.69, bf16[4,2,2,4,2,48,896]{6,5,4,3,2,1,0:T(8,128)(2,1)S(1)} %get-tuple-element.70.refs_2_), custom_call_target="tpu_custom_call" | custom-call | flops 2818572288 | bytes 8388608 | tf_op jit(solution)/shard_map/multiply/pallas_call | solution.py:256
  98.3 1.8 cross.3
  100.1 1.8 collective-permute-start.30
  101.9 1.5 collective-permute-start.32
  103.4 8.5 %collective-permute-done.22.refs_1_ = bf16[416,896]{1,0:T(8,128)(2,1)S(1)} collective-permute-done((bf16[416,896]{1,0:T(8,128)(2,1)S(1)}, bf16[416,896]{1,0:T(8,128)(2,1)S(1)}, u32[]{:S(2)}, u32[]{:S(2)}) %collective-permute-start.22) | collective-permute-done | bytes 745504 | tf_op jit(solution)/shard_map/ppermute | solution.py:69
  112.2 1.9 collective-permute-start.23
  114.1 1.3 collective-permute-start.25
  115.3 5.2 %collective-permute-done.32.refs_3_ = bf16[208,896]{1,0:T(8,128)(2,1)S(1)} collective-permute-done((bf16[208,896]{1,0:T(8,128)(2,1)S(1)}, bf16[208,896]{1,0:T(8,128)(2,1)S(1)}, u32[]{:S(2)}, u32[]{:S(2)}) %collective-permute-start.32) | collective-permute-done | bytes 372768 | tf_op jit(solution)/shard_map/ppermute | solution.py:69
  120.5 3.3 %collective-permute-done.23 = bf16[104,896]{1,0:T(8,128)(2,1)S(1)} collective-permute-done((bf16[104,896]{1,0:T(8,128)(2,1)S(1)}, bf16[104,896]{1,0:T(8,128)(2,1)S(1)}, u32[]{:S(2)}, u32[]{:S(2)}) %collective-permute-start.23) | collective-permute-done | bytes 186400 | tf_op jit(solution)/shard_map/ppermute | solution.py:69
  124.6 3.9 %collective-permute-done.25 = bf16[104,896]{1,0:T(8,128)(2,1)S(1)} collective-permute-done((bf16[104,896]{1,0:T(8,128)(2,1)S(1)}, bf16[104,896]{1,0:T(8,128)(2,1)S(1)}, u32[]{:S(2)}, u32[]{:S(2)}) %collective-permute-start.25) | collective-permute-done | bytes 186400 | tf_op jit(solution)/shard_map/ppermute | solution.py:69
  128.9 2.9 %collective-permute-start.26 = (bf16[104,896]{1,0:T(8,128)(2,1)S(1)}, bf16[104,896]{1,0:T(8,128)(2,1)S(1)}, u32[]{:S(2)}, u32[]{:S(2)}) collective-permute-start(bf16[104,896]{1,0:T(8,128)(2,1)S(1)} %get-tuple-element.112), channel_id=1, source_target_pairs={{0,8},{1,9},{2,10},{3,11},{4,12},{5,13},{6,14},{7,15},{8,0},{9,1},... | collective-permute-start | bytes 559112 | tf_op jit(solution)/shard_map/ppermute | solution.py:69
  133.6 1.8 collective-permute-start.35
  135.4 2.1 collective-permute-start.27
  137.5 1.2 collective-permute-start.29
  138.7 1.5 collective-permute-done.35
  141.1 6.9 %collective-permute-done.28 = bf16[104,896]{1,0:T(8,128)(2,1)S(1)} collective-permute-done((bf16[104,896]{1,0:T(8,128)(2,1)S(1)}, bf16[104,896]{1,0:T(8,128)(2,1)S(1)}, u32[]{:S(2)}, u32[]{:S(2)}) %collective-permute-start.28) | collective-permute-done | bytes 186400 | tf_op jit(solution)/shard_map/ppermute | solution.py:69
  148.8 1.2 collective-permute-start.38
  151.0 6.4 %collective-permute-done.37.refs_5_ = bf16[208,896]{1,0:T(8,128)(2,1)S(1)} collective-permute-done((bf16[208,896]{1,0:T(8,128)(2,1)S(1)}, bf16[208,896]{1,0:T(8,128)(2,1)S(1)}, u32[]{:S(2)}, u32[]{:S(2)}) %collective-permute-start.37) | collective-permute-done | bytes 372768 | tf_op jit(solution)/shard_map/ppermute | solution.py:69
  157.5 3.2 %collective-permute-done.38.refs_6_ = bf16[208,896]{1,0:T(8,128)(2,1)S(1)} collective-permute-done((bf16[208,896]{1,0:T(8,128)(2,1)S(1)}, bf16[208,896]{1,0:T(8,128)(2,1)S(1)}, u32[]{:S(2)}, u32[]{:S(2)}) %collective-permute-start.38) | collective-permute-done | bytes 372768 | tf_op jit(solution)/shard_map/ppermute | solution.py:69
  160.6 6.2 %collective-permute-done.39.refs_7_ = bf16[208,896]{1,0:T(8,128)(2,1)S(1)} collective-permute-done((bf16[208,896]{1,0:T(8,128)(2,1)S(1)}, bf16[208,896]{1,0:T(8,128)(2,1)S(1)}, u32[]{:S(2)}, u32[]{:S(2)}) %collective-permute-start.39) | collective-permute-done | bytes 372768 | tf_op jit(solution)/shard_map/ppermute | solution.py:69
  166.8 5.7 %exchange.1 = (f32[416,768]{1,0:T(8,128)S(1)}, f32[416,768]{1,0:T(8,128)S(1)}) custom-call(bf16[768,896]{1,0:T(8,128)(2,1)} %copy-done.2, bf16[768,896]{1,0:T(8,128)(2,1)} %copy-done.1, bf16[416,896]{1,0:T(8,128)(2,1)S(1)} %constant_dynamic-update-slice_fusion.6.refs_2_, bf16[416,896]{1,0:T(8,128)(2,1)S(1)} %collective-permute-done.36.refs_3_, ...), custom_call_target="tpu_custom_call" | custom-call | flops 2466250752 | bytes 8388608 | tf_op jit(solution)/shard_map/exchange/pallas_call | solution.py:388
  172.6 2.3 %collective-permute-start.40 = (f32[416,768]{1,0:T(8,128)S(1)}, f32[416,768]{1,0:T(8,128)S(1)}, u32[]{:S(2)}, u32[]{:S(2)}) collective-permute-start(f32[416,768]{1,0:T(8,128)S(1)} %get-tuple-element.90), channel_id=1, source_target_pairs={{0,8},{1,9},{2,10},{3,11},{4,12},{5,13},{6,14},{7,15},{8,0},{9,1},... | collective-permute-start | bytes 3833864 | tf_op jit(solution)/shard_map/ppermute | solution.py:69
  174.9 2.6 %collective-permute-done.40.refs_1_ = f32[416,768]{1,0:T(8,128)S(1)} collective-permute-done((f32[416,768]{1,0:T(8,128)S(1)}, f32[416,768]{1,0:T(8,128)S(1)}, u32[]{:S(2)}, u32[]{:S(2)}) %collective-permute-start.40) | collective-permute-done | bytes 1277984 | tf_op jit(solution)/shard_map/ppermute | solution.py:69
  177.7 3.2 %collective-permute-start.41 = (bf16[104,768]{1,0:T(8,128)(2,1)S(1)}, bf16[104,768]{1,0:T(8,128)(2,1)S(1)}, u32[]{:S(2)}, u32[]{:S(2)}) collective-permute-start(bf16[104,768]{1,0:T(8,128)(2,1)S(1)} %get-tuple-element.92), channel_id=1, source_target_pairs={{0,32},{1,33},{2,34},{3,35},{4,36},{5,37},{6,38},{7,39},{8,104},{9... | collective-permute-start | bytes 479240 | tf_op jit(solution)/shard_map/ppermute | solution.py:69
  181.9 2.1 collective-permute-start.43
  184.5 1.7 collective-permute-done.42
  186.2 4.7 %collective-permute-done.43 = bf16[104,768]{1,0:T(8,128)(2,1)S(1)} collective-permute-done((bf16[104,768]{1,0:T(8,128)(2,1)S(1)}, bf16[104,768]{1,0:T(8,128)(2,1)S(1)}, u32[]{:S(2)}, u32[]{:S(2)}) %collective-permute-start.43) | collective-permute-done | bytes 159776 | tf_op jit(solution)/shard_map/ppermute | solution.py:69
  190.9 3.7 %collective-permute-start.44 = (f32[104,768]{1,0:T(8,128)S(1)}, f32[104,768]{1,0:T(8,128)S(1)}, u32[]{:S(2)}, u32[]{:S(2)}) collective-permute-start(f32[104,768]{1,0:T(8,128)S(1)} %add_add_fusion), channel_id=1, source_target_pairs={{0,16},{1,17},{2,18},{3,19},{4,20},{5,21},{6,22},{7,23},{8,24},{9,... | collective-permute-start | bytes 958472 | tf_op jit(solution)/shard_map/ppermute | solution.py:69
  194.7 6.8 %collective-permute-done.44 = f32[104,768]{1,0:T(8,128)S(1)} collective-permute-done((f32[104,768]{1,0:T(8,128)S(1)}, f32[104,768]{1,0:T(8,128)S(1)}, u32[]{:S(2)}, u32[]{:S(2)}) %collective-permute-start.44) | collective-permute-done | bytes 319520 | tf_op jit(solution)/shard_map/ppermute | solution.py:69
  201.6 1.5 collective-permute-start.46
  203.1 1.8 collective-permute-start.47
  205.7 1.3 collective-permute-done.46
  207.0 3.9 %collective-permute-done.47 = bf16[104,768]{1,0:T(8,128)(2,1)S(1)} collective-permute-done((bf16[104,768]{1,0:T(8,128)(2,1)S(1)}, bf16[104,768]{1,0:T(8,128)(2,1)S(1)}, u32[]{:S(2)}, u32[]{:S(2)}) %collective-permute-start.47) | collective-permute-done | bytes 159776 | tf_op jit(solution)/shard_map/ppermute | solution.py:69
  210.9 2.5 %collective-permute-start.48 = (bf16[416,768]{1,0:T(8,128)(2,1)S(1)}, bf16[416,768]{1,0:T(8,128)(2,1)S(1)}, u32[]{:S(2)}, u32[]{:S(2)}) collective-permute-start(bf16[416,768]{1,0:T(8,128)(2,1)S(1)} %constant_dynamic-update-slice_fusion.own), channel_id=1, source_target_pairs={{0,8},{1,9},{2,10},{3,11},{4,12},{5,13},{6,14},{7,15},{8,0},{9,1},... | collective-permute-start | bytes 1916936 | tf_op jit(solution)/shard_map/ppermute | solution.py:69
  213.4 1.7 collective-permute-done.48.others
  215.1 1.6 widen.1
  (99 shorter events, 17.0 us)
Async XLA Ops:
  0.0 10.8 %copy-start.4 = (s32[1,96]{1,0:T(1,128)S(1)}, s32[1,96]{1,0:T(1,128)}, u32[]{:S(2)}) copy-start(s32[1,96]{1,0:T(1,128)} %param.7) | copy-start | bytes 1156
  0.0 10.8 %copy-start.3 = (s32[1,96]{1,0:T(1,128)S(1)}, s32[1,96]{1,0:T(1,128)}, u32[]{:S(2)}) copy-start(s32[1,96]{1,0:T(1,128)} %param.8) | copy-start | bytes 1156
  0.9 2.4 %collective-permute-start = (bf16[48,800]{1,0:T(8,128)(2,1)S(1)}, bf16[48,800]{1,0:T(8,128)(2,1)S(1)}, u32[]{:S(2)}, u32[]{:S(2)}) collective-permute-start(bf16[48,800]{1,0:T(8,128)(2,1)S(1)} %broadcast_select_fusion.2), channel_id=1, source_target_pairs={{0,8},{1,9},{2,10},{3,11},{4,12},{5,13},{6,14},{7,15},{8,0},{9,1},... | collective-permute-start | bytes 230408 | tf_op jit(solution)/shard_map/ppermute | solution.py:69
  3.4 11.4 %collective-permute-start.4 = (bf16[96,128,128]{2,1,0:T(8,128)(2,1)}, bf16[96,128,128]{2,1,0:T(8,128)(2,1)S(1)}, u32[]{:S(2)}, u32[]{:S(2)}) collective-permute-start(bf16[96,128,128]{2,1,0:T(8,128)(2,1)} %bitcast.68), channel_id=1, source_target_pairs={{0,8},{1,9},{2,10},{3,11},{4,12},{5,13},{6,14},{7,15},{8,0},{9,1},... | collective-permute-start | bytes 9437192 | tf_op jit(solution)/shard_map/ppermute | solution.py:69
  4.7 6.1 %collective-permute-start.1 = (bf16[2,48,896]{2,1,0:T(8,128)(2,1)S(1)}, bf16[2,48,896]{2,1,0:T(8,128)(2,1)}, u32[]{:S(2)}, u32[]{:S(2)}) collective-permute-start(bf16[2,48,896]{2,1,0:T(8,128)(2,1)S(1)} %fusion.10), channel_id=1, source_target_pairs={{0,2},{1,3},{2,4},{3,5},{4,6},{5,7},{6,0},{7,1},{8,40},{9,41},{10,... | collective-permute-start | bytes 516104 | tf_op jit(solution)/shard_map/ppermute | solution.py:69
  6.8 6.1 %collective-permute-start.2 = (bf16[2,48,896]{2,1,0:T(8,128)(2,1)S(1)}, bf16[2,48,896]{2,1,0:T(8,128)(2,1)S(1)}, u32[]{:S(2)}, u32[]{:S(2)}) collective-permute-start(bf16[2,48,896]{2,1,0:T(8,128)(2,1)S(1)} %fusion.10), channel_id=1, source_target_pairs={{0,6},{1,7},{2,0},{3,1},{4,2},{5,3},{6,4},{7,5},{8,104},{9,105},{1... | collective-permute-start | bytes 516104 | tf_op jit(solution)/shard_map/ppermute | solution.py:69
  8.7 6.1 %collective-permute-start.3 = (bf16[2,48,896]{2,1,0:T(8,128)(2,1)S(1)}, bf16[2,48,896]{2,1,0:T(8,128)(2,1)S(1)}, u32[]{:S(2)}, u32[]{:S(2)}) collective-permute-start(bf16[2,48,896]{2,1,0:T(8,128)(2,1)S(1)} %fusion.10), channel_id=1, source_target_pairs={{0,4},{1,5},{2,6},{3,7},{4,0},{5,1},{6,2},{7,3},{8,72},{9,73},{10,... | collective-permute-start | bytes 516104 | tf_op jit(solution)/shard_map/ppermute | solution.py:69
  14.9 9.2 %collective-permute-start.5 = (bf16[2,4,32,896]{3,2,1,0:T(8,128)(2,1)S(1)}, bf16[2,4,32,896]{3,2,1,0:T(8,128)(2,1)S(1)}, u32[]{:S(2)}, u32[]{:S(2)}) collective-permute-start(bf16[2,4,32,896]{3,2,1,0:T(8,128)(2,1)S(1)} %slice.39), channel_id=1, source_target_pairs={{0,1},{1,16},{2,3},{3,18},{4,5},{5,20},{6,7},{7,22},{8,25},{9,8},{... | collective-permute-start | bytes 1376264 | tf_op jit(solution)/shard_map/ppermute | solution.py:69
  24.1 5.2 %collective-permute-start.6 = (s32[1,256]{1,0:T(1,128)S(1)}, s32[1,256]{1,0:T(1,128)S(1)}, u32[]{:S(2)}, u32[]{:S(2)}) collective-permute-start(s32[1,256]{1,0:T(1,128)S(1)} %bitcast.73), channel_id=1, source_target_pairs={{0,8},{1,9},{2,10},{3,11},{4,12},{5,13},{6,14},{7,15},{8,0},{9,1},... | collective-permute-start | bytes 3080 | tf_op jit(solution)/shard_map/ppermute | solution.py:69
  26.6 12.2 %collective-permute-start.7 = (bf16[2,4,32,896]{3,2,1,0:T(8,128)(2,1)S(1)}, bf16[2,4,32,896]{3,2,1,0:T(8,128)(2,1)S(1)}, u32[]{:S(2)}, u32[]{:S(2)}) collective-permute-start(bf16[2,4,32,896]{3,2,1,0:T(8,128)(2,1)S(1)} %slice.39), channel_id=1, source_target_pairs={{0,17},{1,0},{2,19},{3,2},{4,21},{5,4},{6,23},{7,6},{8,9},{9,24},{... | collective-permute-start | bytes 1376264 | tf_op jit(solution)/shard_map/ppermute | solution.py:69
  26.6 12.5 %collective-permute-start.8 = (bf16[2,4,32,896]{3,2,1,0:T(8,128)(2,1)S(1)}, bf16[2,4,32,896]{3,2,1,0:T(8,128)(2,1)S(1)}, u32[]{:S(2)}, u32[]{:S(2)}) collective-permute-start(bf16[2,4,32,896]{3,2,1,0:T(8,128)(2,1)S(1)} %collective-permute-done.5), channel_id=1, source_target_pairs={{0,1},{1,16},{2,3},{3,18},{4,5},{5,20},{6,7},{7,22},{8,25},{9,8},{... | collective-permute-start | bytes 1376264 | tf_op jit(solution)/shard_map/ppermute | solution.py:69
  29.3 6.4 %collective-permute-start.9 = (bf16[2,4,16,896]{3,2,1,0:T(8,128)(2,1)S(1)}, bf16[2,4,16,896]{3,2,1,0:T(8,128)(2,1)S(1)}, u32[]{:S(2)}, u32[]{:S(2)}) collective-permute-start(bf16[2,4,16,896]{3,2,1,0:T(8,128)(2,1)S(1)} %slice.38), channel_id=1, source_target_pairs={{0,32},{1,33},{2,34},{3,35},{4,36},{5,37},{6,38},{7,39},{8,10},{9,... | collective-permute-start | bytes 688136 | tf_op jit(solution)/shard_map/ppermute | solution.py:69
  29.9 7.7 %collective-permute-start.10 = (bf16[2,4,16,896]{3,2,1,0:T(8,128)(2,1)S(1)}, bf16[2,4,16,896]{3,2,1,0:T(8,128)(2,1)S(1)}, u32[]{:S(2)}, u32[]{:S(2)}) collective-permute-start(bf16[2,4,16,896]{3,2,1,0:T(8,128)(2,1)S(1)} %slice.38), channel_id=1, source_target_pairs={{0,96},{1,97},{2,98},{3,99},{4,100},{5,101},{6,102},{7,103},{8,14}... | collective-permute-start | bytes 688136 | tf_op jit(solution)/shard_map/ppermute | solution.py:69
  32.1 6.7 %collective-permute-start.11 = (bf16[2,4,16,896]{3,2,1,0:T(8,128)(2,1)S(1)}, bf16[2,4,16,896]{3,2,1,0:T(8,128)(2,1)S(1)}, u32[]{:S(2)}, u32[]{:S(2)}) collective-permute-start(bf16[2,4,16,896]{3,2,1,0:T(8,128)(2,1)S(1)} %slice.38), channel_id=1, source_target_pairs={{0,64},{1,65},{2,66},{3,67},{4,68},{5,69},{6,70},{7,71},{8,12},{9,... | collective-permute-start | bytes 688136 | tf_op jit(solution)/shard_map/ppermute | solution.py:69
  39.2 12.6 %collective-permute-start.14 = (bf16[2,2,4,32,896]{4,3,2,1,0:T(8,128)(2,1)S(1)}, bf16[2,2,4,32,896]{4,3,2,1,0:T(8,128)(2,1)S(1)}, u32[]{:S(2)}, u32[]{:S(2)}) collective-permute-start(bf16[2,2,4,32,896]{4,3,2,1,0:T(8,128)(2,1)S(1)} %get-tuple-element.64.refs_1_), channel_id=1, source_target_pairs={{0,96},{1,97},{2,98},{3,99},{4,100},{5,101},{6,102},{7,103},{8,14}... | collective-permute-start | bytes 2752520 | tf_op jit(solution)/shard_map/ppermute | solution.py:69
  41.2 13.8 %collective-permute-start.12 = (bf16[2,2,4,32,896]{4,3,2,1,0:T(8,128)(2,1)S(1)}, bf16[2,2,4,32,896]{4,3,2,1,0:T(8,128)(2,1)S(1)}, u32[]{:S(2)}, u32[]{:S(2)}) collective-permute-start(bf16[2,2,4,32,896]{4,3,2,1,0:T(8,128)(2,1)S(1)} %get-tuple-element.65.refs_0_), channel_id=1, source_target_pairs={{0,32},{1,33},{2,34},{3,35},{4,36},{5,37},{6,38},{7,39},{8,10},{9,... | collective-permute-start | bytes 2752520 | tf_op jit(solution)/shard_map/ppermute | solution.py:69
  41.2 19.8 %collective-permute-start.15 = (bf16[2,4,4,16,896]{4,3,2,1,0:T(8,128)(2,1)S(1)}, bf16[2,4,4,16,896]{4,3,2,1,0:T(8,128)(2,1)S(1)}, u32[]{:S(2)}, u32[]{:S(2)}) collective-permute-start(bf16[2,4,4,16,896]{4,3,2,1,0:T(8,128)(2,1)S(1)} %bitcast_dynamic-update-slice_fusion.3.refs_2_), channel_id=1, source_target_pairs={{0,1},{1,16},{2,3},{3,18},{4,5},{5,20},{6,7},{7,22},{8,25},{9,8},{... | collective-permute-start | bytes 2752520 | tf_op jit(solution)/shard_map/ppermute | solution.py:69
  44.1 23.4 %collective-permute-start.17 = (bf16[2,4,4,16,896]{4,3,2,1,0:T(8,128)(2,1)S(1)}, bf16[2,4,4,16,896]{4,3,2,1,0:T(8,128)(2,1)S(1)}, u32[]{:S(2)}, u32[]{:S(2)}) collective-permute-start(bf16[2,4,4,16,896]{4,3,2,1,0:T(8,128)(2,1)S(1)} %bitcast_dynamic-update-slice_fusion.3.refs_2_), channel_id=1, source_target_pairs={{0,17},{1,0},{2,19},{3,2},{4,21},{5,4},{6,23},{7,6},{8,9},{9,24},{... | collective-permute-start | bytes 2752520 | tf_op jit(solution)/shard_map/ppermute | solution.py:69
  51.8 17.4 %collective-permute-start.20 = (bf16[2,2,4,32,896]{4,3,2,1,0:T(8,128)(2,1)S(1)}, bf16[2,2,4,32,896]{4,3,2,1,0:T(8,128)(2,1)S(1)}, u32[]{:S(2)}, u32[]{:S(2)}) collective-permute-start(bf16[2,2,4,32,896]{4,3,2,1,0:T(8,128)(2,1)S(1)} %get-tuple-element.65.refs_0_), channel_id=1, source_target_pairs={{0,96},{1,97},{2,98},{3,99},{4,100},{5,101},{6,102},{7,103},{8,14}... | collective-permute-start | bytes 2752520 | tf_op jit(solution)/shard_map/ppermute | solution.py:69
  55.0 14.2 %collective-permute-start.19 = (bf16[2,2,4,32,896]{4,3,2,1,0:T(8,128)(2,1)S(1)}, bf16[2,2,4,32,896]{4,3,2,1,0:T(8,128)(2,1)S(1)}, u32[]{:S(2)}, u32[]{:S(2)}) collective-permute-start(bf16[2,2,4,32,896]{4,3,2,1,0:T(8,128)(2,1)S(1)} %get-tuple-element.64.refs_1_), channel_id=1, source_target_pairs={{0,32},{1,33},{2,34},{3,35},{4,36},{5,37},{6,38},{7,39},{8,10},{9,... | collective-permute-start | bytes 2752520 | tf_op jit(solution)/shard_map/ppermute | solution.py:69
  67.5 12.5 %collective-permute-start.18 = (bf16[2,4,4,16,896]{4,3,2,1,0:T(8,128)(2,1)S(1)}, bf16[2,4,4,16,896]{4,3,2,1,0:T(8,128)(2,1)S(1)}, u32[]{:S(2)}, u32[]{:S(2)}) collective-permute-start(bf16[2,4,4,16,896]{4,3,2,1,0:T(8,128)(2,1)S(1)} %collective-permute-done.15.refs_5_), channel_id=1, source_target_pairs={{0,1},{1,16},{2,3},{3,18},{4,5},{5,20},{6,7},{7,22},{8,25},{9,8},{... | collective-permute-start | bytes 2752520 | tf_op jit(solution)/shard_map/ppermute | solution.py:69
  67.5 12.5 %collective-permute-start.16 = (bf16[2,2,4,32,896]{4,3,2,1,0:T(8,128)(2,1)S(1)}, bf16[2,2,4,32,896]{4,3,2,1,0:T(8,128)(2,1)S(1)}, u32[]{:S(2)}, u32[]{:S(2)}) collective-permute-start(bf16[2,2,4,32,896]{4,3,2,1,0:T(8,128)(2,1)S(1)} %collective-permute-done.14.refs_7_), channel_id=1, source_target_pairs={{0,96},{1,97},{2,98},{3,99},{4,100},{5,101},{6,102},{7,103},{8,14}... | collective-permute-start | bytes 2752520 | tf_op jit(solution)/shard_map/ppermute | solution.py:69
  69.2 13.8 %collective-permute-start.13 = (bf16[2,2,4,32,896]{4,3,2,1,0:T(8,128)(2,1)S(1)}, bf16[2,2,4,32,896]{4,3,2,1,0:T(8,128)(2,1)S(1)}, u32[]{:S(2)}, u32[]{:S(2)}) collective-permute-start(bf16[2,2,4,32,896]{4,3,2,1,0:T(8,128)(2,1)S(1)} %collective-permute-done.12.refs_3_), channel_id=1, source_target_pairs={{0,32},{1,33},{2,34},{3,35},{4,36},{5,37},{6,38},{7,39},{8,10},{9,... | collective-permute-start | bytes 2752520 | tf_op jit(solution)/shard_map/ppermute | solution.py:69
  84.7 8.1 %collective-permute-start.21 = (bf16[768,896]{1,0:T(8,128)(2,1)S(1)}, bf16[768,896]{1,0:T(8,128)(2,1)S(1)}, u32[]{:S(2)}, u32[]{:S(2)}) collective-permute-start(bf16[768,896]{1,0:T(8,128)(2,1)S(1)} %bitcast.70), channel_id=1, source_target_pairs={{0,8},{1,9},{2,10},{3,11},{4,12},{5,13},{6,14},{7,15},{8,0},{9,1},... | collective-permute-start | bytes 4128776 | tf_op jit(solution)/shard_map/ppermute | solution.py:69
  92.8 2.1 copy-start.1
  92.8 2.4 %copy-start = (bf16[1,96,128,128]{3,2,1,0:T(8,128)(2,1)S(1)}, bf16[1,96,128,128]{3,2,1,0:T(8,128)(2,1)}, u32[]{:S(2)}) copy-start(bf16[1,96,128,128]{3,2,1,0:T(8,128)(2,1)} %param.6) | copy-start | bytes 9437188
  94.8 17.0 %collective-permute-start.22 = (bf16[416,896]{1,0:T(8,128)(2,1)S(1)}, bf16[416,896]{1,0:T(8,128)(2,1)S(1)}, u32[]{:S(2)}, u32[]{:S(2)}) collective-permute-start(bf16[416,896]{1,0:T(8,128)(2,1)S(1)} %get-tuple-element.72), channel_id=1, source_target_pairs={{0,1},{1,0},{2,3},{3,2},{4,5},{5,4},{6,7},{7,6},{8,9},{9,8},{10,11... | collective-permute-start | bytes 2236424 | tf_op jit(solution)/shard_map/ppermute | solution.py:69
  98.2 1.8 copy-start.2
  100.1 14.0 %collective-permute-start.30 = (bf16[208,896]{1,0:T(8,128)(2,1)S(1)}, bf16[208,896]{1,0:T(8,128)(2,1)S(1)}, u32[]{:S(2)}, u32[]{:S(2)}) collective-permute-start(bf16[208,896]{1,0:T(8,128)(2,1)S(1)} %get-tuple-element.78), channel_id=1, source_target_pairs={{0,2},{1,3},{2,4},{3,5},{4,6},{5,7},{6,0},{7,1},{8,14},{9,15},{10,... | collective-permute-start | bytes 1118216 | tf_op jit(solution)/shard_map/ppermute | solution.py:69
  101.9 13.4 %collective-permute-start.31 = (bf16[208,896]{1,0:T(8,128)(2,1)S(1)}, bf16[208,896]{1,0:T(8,128)(2,1)S(1)}, u32[]{:S(2)}, u32[]{:S(2)}) collective-permute-start(bf16[208,896]{1,0:T(8,128)(2,1)S(1)} %get-tuple-element.79), channel_id=1, source_target_pairs={{0,6},{1,7},{2,0},{3,1},{4,2},{5,3},{6,4},{7,5},{8,10},{9,11},{10,... | collective-permute-start | bytes 1118216 | tf_op jit(solution)/shard_map/ppermute | solution.py:69
  101.9 18.6 %collective-permute-start.32 = (bf16[208,896]{1,0:T(8,128)(2,1)S(1)}, bf16[208,896]{1,0:T(8,128)(2,1)S(1)}, u32[]{:S(2)}, u32[]{:S(2)}) collective-permute-start(bf16[208,896]{1,0:T(8,128)(2,1)S(1)} %get-tuple-element.80), channel_id=1, source_target_pairs={{0,4},{1,5},{2,6},{3,7},{4,0},{5,1},{6,2},{7,3},{8,12},{9,13},{10,... | collective-permute-start | bytes 1118216 | tf_op jit(solution)/shard_map/ppermute | solution.py:69
  112.2 11.6 %collective-permute-start.23 = (bf16[104,896]{1,0:T(8,128)(2,1)S(1)}, bf16[104,896]{1,0:T(8,128)(2,1)S(1)}, u32[]{:S(2)}, u32[]{:S(2)}) collective-permute-start(bf16[104,896]{1,0:T(8,128)(2,1)S(1)} %get-tuple-element.74), channel_id=1, source_target_pairs={{0,2},{1,3},{2,4},{3,5},{4,6},{5,7},{6,0},{7,1},{8,14},{9,15},{10,... | collective-permute-start | bytes 559112 | tf_op jit(solution)/shard_map/ppermute | solution.py:69
  114.1 10.5 %collective-permute-start.24 = (bf16[104,896]{1,0:T(8,128)(2,1)S(1)}, bf16[104,896]{1,0:T(8,128)(2,1)S(1)}, u32[]{:S(2)}, u32[]{:S(2)}) collective-permute-start(bf16[104,896]{1,0:T(8,128)(2,1)S(1)} %get-tuple-element.75), channel_id=1, source_target_pairs={{0,6},{1,7},{2,0},{3,1},{4,2},{5,3},{6,4},{7,5},{8,10},{9,11},{10,... | collective-permute-start | bytes 559112 | tf_op jit(solution)/shard_map/ppermute | solution.py:69
  114.1 14.4 %collective-permute-start.25 = (bf16[104,896]{1,0:T(8,128)(2,1)S(1)}, bf16[104,896]{1,0:T(8,128)(2,1)S(1)}, u32[]{:S(2)}, u32[]{:S(2)}) collective-permute-start(bf16[104,896]{1,0:T(8,128)(2,1)S(1)} %get-tuple-element.76), channel_id=1, source_target_pairs={{0,4},{1,5},{2,6},{3,7},{4,0},{5,1},{6,2},{7,3},{8,12},{9,13},{10,... | collective-permute-start | bytes 559112 | tf_op jit(solution)/shard_map/ppermute | solution.py:69
  124.2 4.5 %collective-permute-start.33 = (bf16[104,896]{1,0:T(8,128)(2,1)S(1)}, bf16[104,896]{1,0:T(8,128)(2,1)S(1)}, u32[]{:S(2)}, u32[]{:S(2)}) collective-permute-start(bf16[104,896]{1,0:T(8,128)(2,1)S(1)} %get-tuple-element.86), channel_id=1, source_target_pairs={{0,1},{1,0},{2,3},{3,2},{4,5},{5,4},{6,7},{7,6},{8,9},{9,8},{10,11... | collective-permute-start | bytes 559112 | tf_op jit(solution)/shard_map/ppermute | solution.py:69
  128.9 4.0 %collective-permute-start.26 = (bf16[104,896]{1,0:T(8,128)(2,1)S(1)}, bf16[104,896]{1,0:T(8,128)(2,1)S(1)}, u32[]{:S(2)}, u32[]{:S(2)}) collective-permute-start(bf16[104,896]{1,0:T(8,128)(2,1)S(1)} %get-tuple-element.112), channel_id=1, source_target_pairs={{0,8},{1,9},{2,10},{3,11},{4,12},{5,13},{6,14},{7,15},{8,0},{9,1},... | collective-permute-start | bytes 559112 | tf_op jit(solution)/shard_map/ppermute | solution.py:69
  131.9 1.4 collective-permute-start.34
  133.6 6.7 %collective-permute-start.35 = (bf16[104,896]{1,0:T(8,128)(2,1)S(1)}, bf16[104,896]{1,0:T(8,128)(2,1)S(1)}, u32[]{:S(2)}, u32[]{:S(2)}) collective-permute-start(bf16[104,896]{1,0:T(8,128)(2,1)S(1)} %get-tuple-element.98), channel_id=1, source_target_pairs={{0,1},{1,0},{2,3},{3,2},{4,5},{5,4},{6,7},{7,6},{8,9},{9,8},{10,11... | collective-permute-start | bytes 559112 | tf_op jit(solution)/shard_map/ppermute | solution.py:69
  135.4 5.7 %collective-permute-start.27 = (bf16[104,896]{1,0:T(8,128)(2,1)S(1)}, bf16[104,896]{1,0:T(8,128)(2,1)S(1)}, u32[]{:S(2)}, u32[]{:S(2)}) collective-permute-start(bf16[104,896]{1,0:T(8,128)(2,1)S(1)} %get-tuple-element.110), channel_id=1, source_target_pairs={{0,2},{1,3},{2,4},{3,5},{4,6},{5,7},{6,0},{7,1},{8,14},{9,15},{10,... | collective-permute-start | bytes 559112 | tf_op jit(solution)/shard_map/ppermute | solution.py:69
  137.5 10.5 %collective-permute-start.28 = (bf16[104,896]{1,0:T(8,128)(2,1)S(1)}, bf16[104,896]{1,0:T(8,128)(2,1)S(1)}, u32[]{:S(2)}, u32[]{:S(2)}) collective-permute-start(bf16[104,896]{1,0:T(8,128)(2,1)S(1)} %get-tuple-element.110), channel_id=1, source_target_pairs={{0,6},{1,7},{2,0},{3,1},{4,2},{5,3},{6,4},{7,5},{8,10},{9,11},{10,... | collective-permute-start | bytes 559112 | tf_op jit(solution)/shard_map/ppermute | solution.py:69
  137.5 10.5 %collective-permute-start.29 = (bf16[104,896]{1,0:T(8,128)(2,1)S(1)}, bf16[104,896]{1,0:T(8,128)(2,1)S(1)}, u32[]{:S(2)}, u32[]{:S(2)}) collective-permute-start(bf16[104,896]{1,0:T(8,128)(2,1)S(1)} %get-tuple-element.110), channel_id=1, source_target_pairs={{0,4},{1,5},{2,6},{3,7},{4,0},{5,1},{6,2},{7,3},{8,12},{9,13},{10,... | collective-permute-start | bytes 559112 | tf_op jit(solution)/shard_map/ppermute | solution.py:69
  148.1 18.8 %collective-permute-start.36 = (bf16[416,896]{1,0:T(8,128)(2,1)S(1)}, bf16[416,896]{1,0:T(8,128)(2,1)S(1)}, u32[]{:S(2)}, u32[]{:S(2)}) collective-permute-start(bf16[416,896]{1,0:T(8,128)(2,1)S(1)} %constant_dynamic-update-slice_fusion.6.refs_2_), channel_id=1, source_target_pairs={{0,1},{1,0},{2,3},{3,2},{4,5},{5,4},{6,7},{7,6},{8,9},{9,8},{10,11... | collective-permute-start | bytes 2236424 | tf_op jit(solution)/shard_map/ppermute | solution.py:69
  148.2 9.3 %collective-permute-start.37 = (bf16[208,896]{1,0:T(8,128)(2,1)S(1)}, bf16[208,896]{1,0:T(8,128)(2,1)S(1)}, u32[]{:S(2)}, u32[]{:S(2)}) collective-permute-start(bf16[208,896]{1,0:T(8,128)(2,1)S(1)} %constant_dynamic-update-slice_fusion.4.refs_4_), channel_id=1, source_target_pairs={{0,2},{1,3},{2,4},{3,5},{4,6},{5,7},{6,0},{7,1},{8,14},{9,15},{10,... | collective-permute-start | bytes 1118216 | tf_op jit(solution)/shard_map/ppermute | solution.py:69
  148.8 11.9 %collective-permute-start.38 = (bf16[208,896]{1,0:T(8,128)(2,1)S(1)}, bf16[208,896]{1,0:T(8,128)(2,1)S(1)}, u32[]{:S(2)}, u32[]{:S(2)}) collective-permute-start(bf16[208,896]{1,0:T(8,128)(2,1)S(1)} %constant_dynamic-update-slice_fusion.4.refs_4_), channel_id=1, source_target_pairs={{0,6},{1,7},{2,0},{3,1},{4,2},{5,3},{6,4},{7,5},{8,10},{9,11},{10,... | collective-permute-start | bytes 1118216 | tf_op jit(solution)/shard_map/ppermute | solution.py:69
  149.9 16.9 %collective-permute-start.39 = (bf16[208,896]{1,0:T(8,128)(2,1)S(1)}, bf16[208,896]{1,0:T(8,128)(2,1)S(1)}, u32[]{:S(2)}, u32[]{:S(2)}) collective-permute-start(bf16[208,896]{1,0:T(8,128)(2,1)S(1)} %constant_dynamic-update-slice_fusion.4.refs_4_), channel_id=1, source_target_pairs={{0,4},{1,5},{2,6},{3,7},{4,0},{5,1},{6,2},{7,3},{8,12},{9,13},{10,... | collective-permute-start | bytes 1118216 | tf_op jit(solution)/shard_map/ppermute | solution.py:69
  172.6 4.9 %collective-permute-start.40 = (f32[416,768]{1,0:T(8,128)S(1)}, f32[416,768]{1,0:T(8,128)S(1)}, u32[]{:S(2)}, u32[]{:S(2)}) collective-permute-start(f32[416,768]{1,0:T(8,128)S(1)} %get-tuple-element.90), channel_id=1, source_target_pairs={{0,8},{1,9},{2,10},{3,11},{4,12},{5,13},{6,14},{7,15},{8,0},{9,1},... | collective-permute-start | bytes 3833864 | tf_op jit(solution)/shard_map/ppermute | solution.py:69
  177.7 6.8 %collective-permute-start.41 = (bf16[104,768]{1,0:T(8,128)(2,1)S(1)}, bf16[104,768]{1,0:T(8,128)(2,1)S(1)}, u32[]{:S(2)}, u32[]{:S(2)}) collective-permute-start(bf16[104,768]{1,0:T(8,128)(2,1)S(1)} %get-tuple-element.92), channel_id=1, source_target_pairs={{0,32},{1,33},{2,34},{3,35},{4,36},{5,37},{6,38},{7,39},{8,104},{9... | collective-permute-start | bytes 479240 | tf_op jit(solution)/shard_map/ppermute | solution.py:69
  180.9 5.3 %collective-permute-start.42 = (bf16[104,768]{1,0:T(8,128)(2,1)S(1)}, bf16[104,768]{1,0:T(8,128)(2,1)S(1)}, u32[]{:S(2)}, u32[]{:S(2)}) collective-permute-start(bf16[104,768]{1,0:T(8,128)(2,1)S(1)} %get-tuple-element.93), channel_id=1, source_target_pairs={{0,96},{1,97},{2,98},{3,99},{4,100},{5,101},{6,102},{7,103},{8,40}... | collective-permute-start | bytes 479240 | tf_op jit(solution)/shard_map/ppermute | solution.py:69
  181.9 9.0 %collective-permute-start.43 = (bf16[104,768]{1,0:T(8,128)(2,1)S(1)}, bf16[104,768]{1,0:T(8,128)(2,1)S(1)}, u32[]{:S(2)}, u32[]{:S(2)}) collective-permute-start(bf16[104,768]{1,0:T(8,128)(2,1)S(1)} %get-tuple-element.94), channel_id=1, source_target_pairs={{0,64},{1,65},{2,66},{3,67},{4,68},{5,69},{6,70},{7,71},{8,72},{9,... | collective-permute-start | bytes 479240 | tf_op jit(solution)/shard_map/ppermute | solution.py:69
  190.9 10.5 %collective-permute-start.44 = (f32[104,768]{1,0:T(8,128)S(1)}, f32[104,768]{1,0:T(8,128)S(1)}, u32[]{:S(2)}, u32[]{:S(2)}) collective-permute-start(f32[104,768]{1,0:T(8,128)S(1)} %add_add_fusion), channel_id=1, source_target_pairs={{0,16},{1,17},{2,18},{3,19},{4,20},{5,21},{6,22},{7,23},{8,24},{9,... | collective-permute-start | bytes 958472 | tf_op jit(solution)/shard_map/ppermute | solution.py:69
  201.5 4.2 %collective-permute-start.45 = (bf16[104,768]{1,0:T(8,128)(2,1)S(1)}, bf16[104,768]{1,0:T(8,128)(2,1)S(1)}, u32[]{:S(2)}, u32[]{:S(2)}) collective-permute-start(bf16[104,768]{1,0:T(8,128)(2,1)S(1)} %get-tuple-element.96), channel_id=1, source_target_pairs={{0,32},{1,33},{2,34},{3,35},{4,36},{5,37},{6,38},{7,39},{8,104},{9... | collective-permute-start | bytes 479240 | tf_op jit(solution)/shard_map/ppermute | solution.py:69
  201.6 5.4 %collective-permute-start.46 = (bf16[104,768]{1,0:T(8,128)(2,1)S(1)}, bf16[104,768]{1,0:T(8,128)(2,1)S(1)}, u32[]{:S(2)}, u32[]{:S(2)}) collective-permute-start(bf16[104,768]{1,0:T(8,128)(2,1)S(1)} %get-tuple-element.96), channel_id=1, source_target_pairs={{0,96},{1,97},{2,98},{3,99},{4,100},{5,101},{6,102},{7,103},{8,40}... | collective-permute-start | bytes 479240 | tf_op jit(solution)/shard_map/ppermute | solution.py:69
  203.1 7.8 %collective-permute-start.47 = (bf16[104,768]{1,0:T(8,128)(2,1)S(1)}, bf16[104,768]{1,0:T(8,128)(2,1)S(1)}, u32[]{:S(2)}, u32[]{:S(2)}) collective-permute-start(bf16[104,768]{1,0:T(8,128)(2,1)S(1)} %get-tuple-element.96), channel_id=1, source_target_pairs={{0,64},{1,65},{2,66},{3,67},{4,68},{5,69},{6,70},{7,71},{8,72},{9,... | collective-permute-start | bytes 479240 | tf_op jit(solution)/shard_map/ppermute | solution.py:69
  210.9 4.2 %collective-permute-start.48 = (bf16[416,768]{1,0:T(8,128)(2,1)S(1)}, bf16[416,768]{1,0:T(8,128)(2,1)S(1)}, u32[]{:S(2)}, u32[]{:S(2)}) collective-permute-start(bf16[416,768]{1,0:T(8,128)(2,1)S(1)} %constant_dynamic-update-slice_fusion.own), channel_id=1, source_target_pairs={{0,8},{1,9},{2,10},{3,11},{4,12},{5,13},{6,14},{7,15},{8,0},{9,1},... | collective-permute-start | bytes 1916936 | tf_op jit(solution)/shard_map/ppermute | solution.py:69

commit v12 on v11

--- a/solution.py
+++ b/solution.py
@@ -402,10 +402,19 @@
     )(*halves, *low_parts, *x_parts)
 
 
-def widen_kernel(own, others, out):
-    core, n = here()[0], CROSS // 2
-    out[:n, :] = jnp.where(core == 0, own[...], others[...]).astype(f32)
-    out[n:, :] = jnp.where(core == 0, others[...], own[...])[: NOCC - n].astype(f32)
+def widen_kernel(own, others, out, wide, sems):
+    core, n = here()[0], CROSS // 4
+    copies = []
+    for i in range(4):
+        low, high = i * n, min((i + 1) * n, NOCC)
+        rows = slice(low % (2 * n), low % (2 * n) + high - low)
+        mine, its = (own, others) if i < 2 else (others, own)
+        wide[low:high, :] = jnp.where(core == 0, mine[rows, :], its[rows, :]).astype(f32)
+        at = pl.ds(low, high - low)
+        copies.append(pltpu.make_async_copy(wide.at[at], out.at[at], sems.at[i]))
+        copies[-1].start()
+    for copy in copies:
+        copy.wait()
 
 
 def widen(own, others):
@@ -413,7 +422,8 @@
         widen_kernel,
         out_shape=jax.ShapeDtypeStruct((NOCC, ROWS), f32),
         in_specs=[pl.BlockSpec(memory_space=pltpu.VMEM)] * 2,
-        out_specs=pl.BlockSpec(memory_space=pltpu.VMEM),
+        out_specs=pl.BlockSpec(memory_space=pl.ANY),
+        scratch_shapes=[pltpu.VMEM((NOCC, ROWS), f32), pltpu.SemaphoreType.DMA((4,))],
         compiler_params=pltpu.CompilerParams(vmem_limit_bytes=16 * 1024 * 1024),
         name="widen",
     )(own, others)

time: 217 us -> 217 us (level)
  waiting for transfers between devices: 112 us -> 108 us
  starting transfers between devices: 66.9 us -> 69.4 us
    ppermute x49, waiting for transfers between devices: 112 us -> 108 us  [send(): return lax.ppermute(array, AXES, pairs)]
    ppermute x49, starting transfers between devices: 66.9 us -> 69.4 us  [send(): return lax.ppermute(array, AXES, pairs)]
  transfers between devices with their start and end apart: 49 -> 49, of which waited for: 37 -> 33; matrix products, arithmetic and copies ran while one was open for 1% -> 1% of each run, Pallas kernels for 10% -> 10%
where the time goes in v12:
time: 217 us
  waiting for transfers between devices  108 us (50%)
  starting transfers between devices  69.4 us (32%)
  Pallas kernels  33.5 us (15%)
  other arithmetic  2.57 us (1%)
    ppermute x49, waiting for transfers between devices, send(): return lax.ppermute(array, AXES, pairs)  108 us
    ppermute x49, starting transfers between devices, send(): return lax.ppermute(array, AXES, pairs)  69.4 us
    pallas_call x2, Pallas kernels, multiply(): pl.pallas_call(kernel, out_shape=jax.ShapeDtypeStruct((ROWS, WIDE), bf16)...  9.59 us
    pallas_call x1, Pallas kernels, exchange(): pl.pallas_call(exchange_kernel, out_shape=[jax.ShapeDtypeStruct((CROSS //...  5.73 us
    pallas_call x1, Pallas kernels, panels_and_slab(): pl.pallas_call(near_kernel, out_shape=held, in_specs=[anywhere] * 9, out_...  5.12 us
    pallas_call x1, Pallas kernels, plan(): pl.pallas_call(plan_kernel, out_shape=jax.ShapeDtypeStruct((2, MOST * FIE...  5.11 us
  transfers between devices with their start and end apart: 49, of which 33 were waited for; matrix products, arithmetic and copies ran while one was open for 1% of the time, Pallas kernels for 10%

profile of v12, /device:TPU:1, one launch (start us, length us, event | category | flops | bytes accessed | tf_op | source)
XLA Modules:
  0.0 217.0 jit_solution(2117296314435652741)
XLA Ops:
  0.9 1.5 collective-permute-start
  4.7 1.4 collective-permute-start.1
  6.8 1.9 collective-permute-start.2
  8.7 1.3 collective-permute-start.3
  10.9 0.9 bitcast_dynamic-update-slice_fusion.7
  11.8 1.1 collective-permute-done.2
  12.9 1.8 collective-permute-done.3
  14.9 3.8 %collective-permute-start.5 = (bf16[2,4,32,896]{3,2,1,0:T(8,128)(2,1)S(1)}, bf16[2,4,32,896]{3,2,1,0:T(8,128)(2,1)S(1)}, u32[]{:S(2)}, u32[]{:S(2)}) collective-permute-start(bf16[2,4,32,896]{3,2,1,0:T(8,128)(2,1)S(1)} %slice.39), channel_id=1, source_target_pairs={{0,1},{1,16},{2,3},{3,18},{4,5},{5,20},{6,7},{7,22},{8,25},{9,8},{... | collective-permute-start | bytes 1376264 | tf_op jit(solution)/shard_map/ppermute | solution.py:69
  18.9 5.2 %collective-permute-done.5 = bf16[2,4,32,896]{3,2,1,0:T(8,128)(2,1)S(1)} collective-permute-done((bf16[2,4,32,896]{3,2,1,0:T(8,128)(2,1)S(1)}, bf16[2,4,32,896]{3,2,1,0:T(8,128)(2,1)S(1)}, u32[]{:S(2)}, u32[]{:S(2)}) %collective-permute-start.5) | collective-permute-done | bytes 458784 | tf_op jit(solution)/shard_map/ppermute | solution.py:69
  24.1 2.5 %collective-permute-start.6 = (s32[1,256]{1,0:T(1,128)S(1)}, s32[1,256]{1,0:T(1,128)S(1)}, u32[]{:S(2)}, u32[]{:S(2)}) collective-permute-start(s32[1,256]{1,0:T(1,128)S(1)} %bitcast.73), channel_id=1, source_target_pairs={{0,8},{1,9},{2,10},{3,11},{4,12},{5,13},{6,14},{7,15},{8,0},{9,1},... | collective-permute-start | bytes 3080 | tf_op jit(solution)/shard_map/ppermute | solution.py:69
  26.6 2.7 %collective-permute-start.8 = (bf16[2,4,32,896]{3,2,1,0:T(8,128)(2,1)S(1)}, bf16[2,4,32,896]{3,2,1,0:T(8,128)(2,1)S(1)}, u32[]{:S(2)}, u32[]{:S(2)}) collective-permute-start(bf16[2,4,32,896]{3,2,1,0:T(8,128)(2,1)S(1)} %collective-permute-done.5), channel_id=1, source_target_pairs={{0,1},{1,16},{2,3},{3,18},{4,5},{5,20},{6,7},{7,22},{8,25},{9,8},{... | collective-permute-start | bytes 1376264 | tf_op jit(solution)/shard_map/ppermute | solution.py:69
  29.9 2.2 %collective-permute-start.10 = (bf16[2,4,16,896]{3,2,1,0:T(8,128)(2,1)S(1)}, bf16[2,4,16,896]{3,2,1,0:T(8,128)(2,1)S(1)}, u32[]{:S(2)}, u32[]{:S(2)}) collective-permute-start(bf16[2,4,16,896]{3,2,1,0:T(8,128)(2,1)S(1)} %slice.38), channel_id=1, source_target_pairs={{0,96},{1,97},{2,98},{3,99},{4,100},{5,101},{6,102},{7,103},{8,14}... | collective-permute-start | bytes 688136 | tf_op jit(solution)/shard_map/ppermute | solution.py:69
  32.5 3.3 %collective-permute-done.9 = bf16[2,4,16,896]{3,2,1,0:T(8,128)(2,1)S(1)} collective-permute-done((bf16[2,4,16,896]{3,2,1,0:T(8,128)(2,1)S(1)}, bf16[2,4,16,896]{3,2,1,0:T(8,128)(2,1)S(1)}, u32[]{:S(2)}, u32[]{:S(2)}) %collective-permute-start.9) | collective-permute-done | bytes 229408 | tf_op jit(solution)/shard_map/ppermute | solution.py:69
  35.8 1.7 collective-permute-done.10
  37.6 1.2 collective-permute-done.11
  39.2 2.1 collective-permute-start.14
  41.2 2.9 %collective-permute-start.15 = (bf16[2,4,4,16,896]{4,3,2,1,0:T(8,128)(2,1)S(1)}, bf16[2,4,4,16,896]{4,3,2,1,0:T(8,128)(2,1)S(1)}, u32[]{:S(2)}, u32[]{:S(2)}) collective-permute-start(bf16[2,4,4,16,896]{4,3,2,1,0:T(8,128)(2,1)S(1)} %bitcast_dynamic-update-slice_fusion.3.refs_2_), channel_id=1, source_target_pairs={{0,1},{1,16},{2,3},{3,18},{4,5},{5,20},{6,7},{7,22},{8,25},{9,8},{... | collective-permute-start | bytes 2752520 | tf_op jit(solution)/shard_map/ppermute | solution.py:69
  44.1 5.1 %plan.1.refs_0_ = s32[2,325]{1,0:T(2,128)S(1)} custom-call(s32[2,256]{1,0:T(2,128)S(1)} %pad_add_fusion.meta), custom_call_target="tpu_custom_call" | custom-call | flops 2147483648 | bytes 4096 | tf_op jit(solution)/shard_map/plan/pallas_call | solution.py:208
  49.2 2.6 %collective-permute-done.14.refs_7_ = bf16[2,2,4,32,896]{4,3,2,1,0:T(8,128)(2,1)S(1)} collective-permute-done((bf16[2,2,4,32,896]{4,3,2,1,0:T(8,128)(2,1)S(1)}, bf16[2,2,4,32,896]{4,3,2,1,0:T(8,128)(2,1)S(1)}, u32[]{:S(2)}, u32[]{:S(2)}) %collective-permute-start.14) | collective-permute-done | bytes 917536 | tf_op jit(solution)/shard_map/ppermute | solution.py:69
  51.8 3.2 %collective-permute-start.20 = (bf16[2,2,4,32,896]{4,3,2,1,0:T(8,128)(2,1)S(1)}, bf16[2,2,4,32,896]{4,3,2,1,0:T(8,128)(2,1)S(1)}, u32[]{:S(2)}, u32[]{:S(2)}) collective-permute-start(bf16[2,2,4,32,896]{4,3,2,1,0:T(8,128)(2,1)S(1)} %get-tuple-element.65.refs_0_), channel_id=1, source_target_pairs={{0,96},{1,97},{2,98},{3,99},{4,100},{5,101},{6,102},{7,103},{8,14}... | collective-permute-start | bytes 2752520 | tf_op jit(solution)/shard_map/ppermute | solution.py:69
  55.0 6.0 %collective-permute-done.15.refs_5_ = bf16[2,4,4,16,896]{4,3,2,1,0:T(8,128)(2,1)S(1)} collective-permute-done((bf16[2,4,4,16,896]{4,3,2,1,0:T(8,128)(2,1)S(1)}, bf16[2,4,4,16,896]{4,3,2,1,0:T(8,128)(2,1)S(1)}, u32[]{:S(2)}, u32[]{:S(2)}) %collective-permute-start.15) | collective-permute-done | bytes 917536 | tf_op jit(solution)/shard_map/ppermute | solution.py:69
  61.0 6.4 %collective-permute-done.17.refs_8_ = bf16[2,4,4,16,896]{4,3,2,1,0:T(8,128)(2,1)S(1)} collective-permute-done((bf16[2,4,4,16,896]{4,3,2,1,0:T(8,128)(2,1)S(1)}, bf16[2,4,4,16,896]{4,3,2,1,0:T(8,128)(2,1)S(1)}, u32[]{:S(2)}, u32[]{:S(2)}) %collective-permute-start.17) | collective-permute-done | bytes 917536 | tf_op jit(solution)/shard_map/ppermute | solution.py:69
  67.5 1.7 collective-permute-start.16
  69.2 5.1 %near.1 = bf16[4,2,2,4,2,48,896]{6,5,4,3,2,1,0:T(8,128)(2,1)S(1)} custom-call(bf16[2,2,4,32,896]{4,3,2,1,0:T(8,128)(2,1)S(1)} %get-tuple-element.65.refs_0_, bf16[2,2,4,32,896]{4,3,2,1,0:T(8,128)(2,1)S(1)} %get-tuple-element.64.refs_1_, bf16[2,4,4,16,896]{4,3,2,1,0:T(8,128)(2,1)S(1)} %bitcast_dynamic-update-slice_fusion.3.refs_2_, ...), custom_call_target="tpu_custom_call" | custom-call | tf_op jit(solution)/shard_map/near/pallas_call | solution.py:139
  74.3 5.7 %collective-permute-done.18.rest = bf16[2,4,4,16,896]{4,3,2,1,0:T(8,128)(2,1)S(1)} collective-permute-done((bf16[2,4,4,16,896]{4,3,2,1,0:T(8,128)(2,1)S(1)}, bf16[2,4,4,16,896]{4,3,2,1,0:T(8,128)(2,1)S(1)}, u32[]{:S(2)}, u32[]{:S(2)}) %collective-permute-start.18) | collective-permute-done | bytes 917536 | tf_op jit(solution)/shard_map/ppermute | solution.py:69
  80.0 2.9 %collective-permute-done.13.main0 = bf16[2,2,4,32,896]{4,3,2,1,0:T(8,128)(2,1)S(1)} collective-permute-done((bf16[2,2,4,32,896]{4,3,2,1,0:T(8,128)(2,1)S(1)}, bf16[2,2,4,32,896]{4,3,2,1,0:T(8,128)(2,1)S(1)}, u32[]{:S(2)}, u32[]{:S(2)}) %collective-permute-start.13) | collective-permute-done | bytes 917536 | tf_op jit(solution)/shard_map/ppermute | solution.py:69
  82.9 1.7 far.1
  84.7 2.6 %collective-permute-start.21 = (bf16[768,896]{1,0:T(8,128)(2,1)S(1)}, bf16[768,896]{1,0:T(8,128)(2,1)S(1)}, u32[]{:S(2)}, u32[]{:S(2)}) collective-permute-start(bf16[768,896]{1,0:T(8,128)(2,1)S(1)} %bitcast.70), channel_id=1, source_target_pairs={{0,8},{1,9},{2,10},{3,11},{4,12},{5,13},{6,14},{7,15},{8,0},{9,1},... | collective-permute-start | bytes 4128776 | tf_op jit(solution)/shard_map/ppermute | solution.py:69
  87.2 3.3 %multiply.2.refs_0_.refs_1_ = bf16[768,896]{1,0:T(8,128)(2,1)S(1)} custom-call(s32[2,325]{1,0:T(2,128)S(1)} %plan.1.refs_0_, bf16[96,128,128]{2,1,0:T(8,128)(2,1)S(1)} %collective-permute-done.4.refs_1_, bf16[4,2,2,4,2,48,896]{6,5,4,3,2,1,0:T(8,128)(2,1)S(1)} %get-tuple-element.70.refs_2_), custom_call_target="tpu_custom_call" | custom-call | flops 2818572288 | bytes 8388608 | tf_op jit(solution)/shard_map/multiply/pallas_call | solution.py:256
  90.6 2.0 cross.2
  92.6 1.1 collective-permute-start.22
  93.7 6.3 %multiply.3.refs_0_ = bf16[768,896]{1,0:T(8,128)(2,1)S(1)} custom-call(s32[2,325]{1,0:T(2,128)S(1)} %plan.1.refs_0_, bf16[96,128,128]{2,1,0:T(8,128)(2,1)S(1)} %bitcast.69, bf16[4,2,2,4,2,48,896]{6,5,4,3,2,1,0:T(8,128)(2,1)S(1)} %get-tuple-element.70.refs_2_), custom_call_target="tpu_custom_call" | custom-call | flops 2818572288 | bytes 8388608 | tf_op jit(solution)/shard_map/multiply/pallas_call | solution.py:256
  100.0 1.8 cross.3
  102.0 1.5 collective-permute-start.31
  104.2 3.5 %collective-permute-done.22.refs_1_ = bf16[416,896]{1,0:T(8,128)(2,1)S(1)} collective-permute-done((bf16[416,896]{1,0:T(8,128)(2,1)S(1)}, bf16[416,896]{1,0:T(8,128)(2,1)S(1)}, u32[]{:S(2)}, u32[]{:S(2)}) %collective-permute-start.22) | collective-permute-done | bytes 745504 | tf_op jit(solution)/shard_map/ppermute | solution.py:69
  108.0 5.8 %collective-permute-start.23 = (bf16[104,896]{1,0:T(8,128)(2,1)S(1)}, bf16[104,896]{1,0:T(8,128)(2,1)S(1)}, u32[]{:S(2)}, u32[]{:S(2)}) collective-permute-start(bf16[104,896]{1,0:T(8,128)(2,1)S(1)} %get-tuple-element.74), channel_id=1, source_target_pairs={{0,2},{1,3},{2,4},{3,5},{4,6},{5,7},{6,0},{7,1},{8,14},{9,15},{10,... | collective-permute-start | bytes 559112 | tf_op jit(solution)/shard_map/ppermute | solution.py:69
  113.8 1.6 collective-permute-start.25
  115.4 6.5 %collective-permute-done.31.refs_2_ = bf16[208,896]{1,0:T(8,128)(2,1)S(1)} collective-permute-done((bf16[208,896]{1,0:T(8,128)(2,1)S(1)}, bf16[208,896]{1,0:T(8,128)(2,1)S(1)}, u32[]{:S(2)}, u32[]{:S(2)}) %collective-permute-start.31) | collective-permute-done | bytes 372768 | tf_op jit(solution)/shard_map/ppermute | solution.py:69
  121.9 2.4 %collective-permute-done.23 = bf16[104,896]{1,0:T(8,128)(2,1)S(1)} collective-permute-done((bf16[104,896]{1,0:T(8,128)(2,1)S(1)}, bf16[104,896]{1,0:T(8,128)(2,1)S(1)}, u32[]{:S(2)}, u32[]{:S(2)}) %collective-permute-start.23) | collective-permute-done | bytes 186400 | tf_op jit(solution)/shard_map/ppermute | solution.py:69
  124.6 1.3 collective-permute-start.33
  125.9 3.4 %collective-permute-done.24 = bf16[104,896]{1,0:T(8,128)(2,1)S(1)} collective-permute-done((bf16[104,896]{1,0:T(8,128)(2,1)S(1)}, bf16[104,896]{1,0:T(8,128)(2,1)S(1)}, u32[]{:S(2)}, u32[]{:S(2)}) %collective-permute-start.24) | collective-permute-done | bytes 186400 | tf_op jit(solution)/shard_map/ppermute | solution.py:69
  129.6 6.4 %collective-permute-start.26 = (bf16[104,896]{1,0:T(8,128)(2,1)S(1)}, bf16[104,896]{1,0:T(8,128)(2,1)S(1)}, u32[]{:S(2)}, u32[]{:S(2)}) collective-permute-start(bf16[104,896]{1,0:T(8,128)(2,1)S(1)} %get-tuple-element.112), channel_id=1, source_target_pairs={{0,8},{1,9},{2,10},{3,11},{4,12},{5,13},{6,14},{7,15},{8,0},{9,1},... | collective-permute-start | bytes 559112 | tf_op jit(solution)/shard_map/ppermute | solution.py:69
  139.8 4.0 %collective-permute-done.35 = bf16[104,896]{1,0:T(8,128)(2,1)S(1)} collective-permute-done((bf16[104,896]{1,0:T(8,128)(2,1)S(1)}, bf16[104,896]{1,0:T(8,128)(2,1)S(1)}, u32[]{:S(2)}, u32[]{:S(2)}) %collective-permute-start.35) | collective-permute-done | bytes 186400 | tf_op jit(solution)/shard_map/ppermute | solution.py:69
  143.9 6.6 %collective-permute-done.28 = bf16[104,896]{1,0:T(8,128)(2,1)S(1)} collective-permute-done((bf16[104,896]{1,0:T(8,128)(2,1)S(1)}, bf16[104,896]{1,0:T(8,128)(2,1)S(1)}, u32[]{:S(2)}, u32[]{:S(2)}) %collective-permute-start.28) | collective-permute-done | bytes 186400 | tf_op jit(solution)/shard_map/ppermute | solution.py:69
  151.5 0.9 collective-permute-start.38
  152.4 1.0 collective-permute-start.39
  153.5 6.6 %collective-permute-done.37.refs_5_ = bf16[208,896]{1,0:T(8,128)(2,1)S(1)} collective-permute-done((bf16[208,896]{1,0:T(8,128)(2,1)S(1)}, bf16[208,896]{1,0:T(8,128)(2,1)S(1)}, u32[]{:S(2)}, u32[]{:S(2)}) %collective-permute-start.37) | collective-permute-done | bytes 372768 | tf_op jit(solution)/shard_map/ppermute | solution.py:69
  160.0 4.2 %collective-permute-done.38.refs_6_ = bf16[208,896]{1,0:T(8,128)(2,1)S(1)} collective-permute-done((bf16[208,896]{1,0:T(8,128)(2,1)S(1)}, bf16[208,896]{1,0:T(8,128)(2,1)S(1)}, u32[]{:S(2)}, u32[]{:S(2)}) %collective-permute-start.38) | collective-permute-done | bytes 372768 | tf_op jit(solution)/shard_map/ppermute | solution.py:69
  164.3 4.4 %collective-permute-done.39.refs_7_ = bf16[208,896]{1,0:T(8,128)(2,1)S(1)} collective-permute-done((bf16[208,896]{1,0:T(8,128)(2,1)S(1)}, bf16[208,896]{1,0:T(8,128)(2,1)S(1)}, u32[]{:S(2)}, u32[]{:S(2)}) %collective-permute-start.39) | collective-permute-done | bytes 372768 | tf_op jit(solution)/shard_map/ppermute | solution.py:69
  168.7 5.7 %exchange.1 = (f32[416,768]{1,0:T(8,128)S(1)}, f32[416,768]{1,0:T(8,128)S(1)}) custom-call(bf16[768,896]{1,0:T(8,128)(2,1)} %copy-done.2, bf16[768,896]{1,0:T(8,128)(2,1)} %copy-done.1, bf16[416,896]{1,0:T(8,128)(2,1)S(1)} %constant_dynamic-update-slice_fusion.6.refs_2_, bf16[416,896]{1,0:T(8,128)(2,1)S(1)} %collective-permute-done.36.refs_3_, ...), custom_call_target="tpu_custom_call" | custom-call | flops 2466250752 | bytes 8388608 | tf_op jit(solution)/shard_map/exchange/pallas_call | solution.py:388
  174.4 3.2 %collective-permute-start.40 = (f32[416,768]{1,0:T(8,128)S(1)}, f32[416,768]{1,0:T(8,128)S(1)}, u32[]{:S(2)}, u32[]{:S(2)}) collective-permute-start(f32[416,768]{1,0:T(8,128)S(1)} %get-tuple-element.90), channel_id=1, source_target_pairs={{0,8},{1,9},{2,10},{3,11},{4,12},{5,13},{6,14},{7,15},{8,0},{9,1},... | collective-permute-start | bytes 3833864 | tf_op jit(solution)/shard_map/ppermute | solution.py:69
  177.6 2.6 %collective-permute-done.40.refs_1_ = f32[416,768]{1,0:T(8,128)S(1)} collective-permute-done((f32[416,768]{1,0:T(8,128)S(1)}, f32[416,768]{1,0:T(8,128)S(1)}, u32[]{:S(2)}, u32[]{:S(2)}) %collective-permute-start.40) | collective-permute-done | bytes 1277984 | tf_op jit(solution)/shard_map/ppermute | solution.py:69
  180.5 1.5 collective-permute-start.42
  182.8 2.9 %collective-permute-done.41 = bf16[104,768]{1,0:T(8,128)(2,1)S(1)} collective-permute-done((bf16[104,768]{1,0:T(8,128)(2,1)S(1)}, bf16[104,768]{1,0:T(8,128)(2,1)S(1)}, u32[]{:S(2)}, u32[]{:S(2)}) %collective-permute-start.41) | collective-permute-done | bytes 159776 | tf_op jit(solution)/shard_map/ppermute | solution.py:69
  185.7 4.9 %collective-permute-done.42 = bf16[104,768]{1,0:T(8,128)(2,1)S(1)} collective-permute-done((bf16[104,768]{1,0:T(8,128)(2,1)S(1)}, bf16[104,768]{1,0:T(8,128)(2,1)S(1)}, u32[]{:S(2)}, u32[]{:S(2)}) %collective-permute-start.42) | collective-permute-done | bytes 159776 | tf_op jit(solution)/shard_map/ppermute | solution.py:69
  190.7 3.7 %collective-permute-start.44 = (f32[104,768]{1,0:T(8,128)S(1)}, f32[104,768]{1,0:T(8,128)S(1)}, u32[]{:S(2)}, u32[]{:S(2)}) collective-permute-start(f32[104,768]{1,0:T(8,128)S(1)} %add_add_fusion), channel_id=1, source_target_pairs={{0,16},{1,17},{2,18},{3,19},{4,20},{5,21},{6,22},{7,23},{8,24},{9,... | collective-permute-start | bytes 958472 | tf_op jit(solution)/shard_map/ppermute | solution.py:69
  194.4 6.8 %collective-permute-done.44 = f32[104,768]{1,0:T(8,128)S(1)} collective-permute-done((f32[104,768]{1,0:T(8,128)S(1)}, f32[104,768]{1,0:T(8,128)S(1)}, u32[]{:S(2)}, u32[]{:S(2)}) %collective-permute-start.44) | collective-permute-done | bytes 319520 | tf_op jit(solution)/shard_map/ppermute | solution.py:69
  201.4 1.5 collective-permute-start.46
  202.8 2.2 %collective-permute-start.47 = (bf16[104,768]{1,0:T(8,128)(2,1)S(1)}, bf16[104,768]{1,0:T(8,128)(2,1)S(1)}, u32[]{:S(2)}, u32[]{:S(2)}) collective-permute-start(bf16[104,768]{1,0:T(8,128)(2,1)S(1)} %get-tuple-element.96), channel_id=1, source_target_pairs={{0,64},{1,65},{2,66},{3,67},{4,68},{5,69},{6,70},{7,71},{8,72},{9,... | collective-permute-start | bytes 479240 | tf_op jit(solution)/shard_map/ppermute | solution.py:69
  205.5 1.3 collective-permute-done.46
  206.8 4.9 %collective-permute-done.47 = bf16[104,768]{1,0:T(8,128)(2,1)S(1)} collective-permute-done((bf16[104,768]{1,0:T(8,128)(2,1)S(1)}, bf16[104,768]{1,0:T(8,128)(2,1)S(1)}, u32[]{:S(2)}, u32[]{:S(2)}) %collective-permute-start.47) | collective-permute-done | bytes 159776 | tf_op jit(solution)/shard_map/ppermute | solution.py:69
  211.7 1.9 collective-permute-start.48
  213.6 1.7 collective-permute-done.48.others
  215.3 1.5 widen.1
  (99 shorter events, 14.4 us)
Async XLA Ops:
  0.0 10.8 %copy-start.4 = (s32[1,96]{1,0:T(1,128)S(1)}, s32[1,96]{1,0:T(1,128)}, u32[]{:S(2)}) copy-start(s32[1,96]{1,0:T(1,128)} %param.7) | copy-start | bytes 1156
  0.0 10.8 %copy-start.3 = (s32[1,96]{1,0:T(1,128)S(1)}, s32[1,96]{1,0:T(1,128)}, u32[]{:S(2)}) copy-start(s32[1,96]{1,0:T(1,128)} %param.8) | copy-start | bytes 1156
  0.9 2.4 %collective-permute-start = (bf16[48,800]{1,0:T(8,128)(2,1)S(1)}, bf16[48,800]{1,0:T(8,128)(2,1)S(1)}, u32[]{:S(2)}, u32[]{:S(2)}) collective-permute-start(bf16[48,800]{1,0:T(8,128)(2,1)S(1)} %broadcast_select_fusion.2), channel_id=1, source_target_pairs={{0,8},{1,9},{2,10},{3,11},{4,12},{5,13},{6,14},{7,15},{8,0},{9,1},... | collective-permute-start | bytes 230408 | tf_op jit(solution)/shard_map/ppermute | solution.py:69
  3.4 11.4 %collective-permute-start.4 = (bf16[96,128,128]{2,1,0:T(8,128)(2,1)}, bf16[96,128,128]{2,1,0:T(8,128)(2,1)S(1)}, u32[]{:S(2)}, u32[]{:S(2)}) collective-permute-start(bf16[96,128,128]{2,1,0:T(8,128)(2,1)} %bitcast.68), channel_id=1, source_target_pairs={{0,8},{1,9},{2,10},{3,11},{4,12},{5,13},{6,14},{7,15},{8,0},{9,1},... | collective-permute-start | bytes 9437192 | tf_op jit(solution)/shard_map/ppermute | solution.py:69
  4.7 6.1 %collective-permute-start.1 = (bf16[2,48,896]{2,1,0:T(8,128)(2,1)S(1)}, bf16[2,48,896]{2,1,0:T(8,128)(2,1)}, u32[]{:S(2)}, u32[]{:S(2)}) collective-permute-start(bf16[2,48,896]{2,1,0:T(8,128)(2,1)S(1)} %fusion.10), channel_id=1, source_target_pairs={{0,2},{1,3},{2,4},{3,5},{4,6},{5,7},{6,0},{7,1},{8,40},{9,41},{10,... | collective-permute-start | bytes 516104 | tf_op jit(solution)/shard_map/ppermute | solution.py:69
  6.8 6.1 %collective-permute-start.2 = (bf16[2,48,896]{2,1,0:T(8,128)(2,1)S(1)}, bf16[2,48,896]{2,1,0:T(8,128)(2,1)S(1)}, u32[]{:S(2)}, u32[]{:S(2)}) collective-permute-start(bf16[2,48,896]{2,1,0:T(8,128)(2,1)S(1)} %fusion.10), channel_id=1, source_target_pairs={{0,6},{1,7},{2,0},{3,1},{4,2},{5,3},{6,4},{7,5},{8,104},{9,105},{1... | collective-permute-start | bytes 516104 | tf_op jit(solution)/shard_map/ppermute | solution.py:69
  8.7 6.1 %collective-permute-start.3 = (bf16[2,48,896]{2,1,0:T(8,128)(2,1)S(1)}, bf16[2,48,896]{2,1,0:T(8,128)(2,1)S(1)}, u32[]{:S(2)}, u32[]{:S(2)}) collective-permute-start(bf16[2,48,896]{2,1,0:T(8,128)(2,1)S(1)} %fusion.10), channel_id=1, source_target_pairs={{0,4},{1,5},{2,6},{3,7},{4,0},{5,1},{6,2},{7,3},{8,72},{9,73},{10,... | collective-permute-start | bytes 516104 | tf_op jit(solution)/shard_map/ppermute | solution.py:69
  14.9 9.2 %collective-permute-start.5 = (bf16[2,4,32,896]{3,2,1,0:T(8,128)(2,1)S(1)}, bf16[2,4,32,896]{3,2,1,0:T(8,128)(2,1)S(1)}, u32[]{:S(2)}, u32[]{:S(2)}) collective-permute-start(bf16[2,4,32,896]{3,2,1,0:T(8,128)(2,1)S(1)} %slice.39), channel_id=1, source_target_pairs={{0,1},{1,16},{2,3},{3,18},{4,5},{5,20},{6,7},{7,22},{8,25},{9,8},{... | collective-permute-start | bytes 1376264 | tf_op jit(solution)/shard_map/ppermute | solution.py:69
  24.1 5.2 %collective-permute-start.6 = (s32[1,256]{1,0:T(1,128)S(1)}, s32[1,256]{1,0:T(1,128)S(1)}, u32[]{:S(2)}, u32[]{:S(2)}) collective-permute-start(s32[1,256]{1,0:T(1,128)S(1)} %bitcast.73), channel_id=1, source_target_pairs={{0,8},{1,9},{2,10},{3,11},{4,12},{5,13},{6,14},{7,15},{8,0},{9,1},... | collective-permute-start | bytes 3080 | tf_op jit(solution)/shard_map/ppermute | solution.py:69
  26.6 12.2 %collective-permute-start.7 = (bf16[2,4,32,896]{3,2,1,0:T(8,128)(2,1)S(1)}, bf16[2,4,32,896]{3,2,1,0:T(8,128)(2,1)S(1)}, u32[]{:S(2)}, u32[]{:S(2)}) collective-permute-start(bf16[2,4,32,896]{3,2,1,0:T(8,128)(2,1)S(1)} %slice.39), channel_id=1, source_target_pairs={{0,17},{1,0},{2,19},{3,2},{4,21},{5,4},{6,23},{7,6},{8,9},{9,24},{... | collective-permute-start | bytes 1376264 | tf_op jit(solution)/shard_map/ppermute | solution.py:69
  26.6 12.5 %collective-permute-start.8 = (bf16[2,4,32,896]{3,2,1,0:T(8,128)(2,1)S(1)}, bf16[2,4,32,896]{3,2,1,0:T(8,128)(2,1)S(1)}, u32[]{:S(2)}, u32[]{:S(2)}) collective-permute-start(bf16[2,4,32,896]{3,2,1,0:T(8,128)(2,1)S(1)} %collective-permute-done.5), channel_id=1, source_target_pairs={{0,1},{1,16},{2,3},{3,18},{4,5},{5,20},{6,7},{7,22},{8,25},{9,8},{... | collective-permute-start | bytes 1376264 | tf_op jit(solution)/shard_map/ppermute | solution.py:69
  29.3 6.4 %collective-permute-start.9 = (bf16[2,4,16,896]{3,2,1,0:T(8,128)(2,1)S(1)}, bf16[2,4,16,896]{3,2,1,0:T(8,128)(2,1)S(1)}, u32[]{:S(2)}, u32[]{:S(2)}) collective-permute-start(bf16[2,4,16,896]{3,2,1,0:T(8,128)(2,1)S(1)} %slice.38), channel_id=1, source_target_pairs={{0,32},{1,33},{2,34},{3,35},{4,36},{5,37},{6,38},{7,39},{8,10},{9,... | collective-permute-start | bytes 688136 | tf_op jit(solution)/shard_map/ppermute | solution.py:69
  29.9 7.7 %collective-permute-start.10 = (bf16[2,4,16,896]{3,2,1,0:T(8,128)(2,1)S(1)}, bf16[2,4,16,896]{3,2,1,0:T(8,128)(2,1)S(1)}, u32[]{:S(2)}, u32[]{:S(2)}) collective-permute-start(bf16[2,4,16,896]{3,2,1,0:T(8,128)(2,1)S(1)} %slice.38), channel_id=1, source_target_pairs={{0,96},{1,97},{2,98},{3,99},{4,100},{5,101},{6,102},{7,103},{8,14}... | collective-permute-start | bytes 688136 | tf_op jit(solution)/shard_map/ppermute | solution.py:69
  32.1 6.7 %collective-permute-start.11 = (bf16[2,4,16,896]{3,2,1,0:T(8,128)(2,1)S(1)}, bf16[2,4,16,896]{3,2,1,0:T(8,128)(2,1)S(1)}, u32[]{:S(2)}, u32[]{:S(2)}) collective-permute-start(bf16[2,4,16,896]{3,2,1,0:T(8,128)(2,1)S(1)} %slice.38), channel_id=1, source_target_pairs={{0,64},{1,65},{2,66},{3,67},{4,68},{5,69},{6,70},{7,71},{8,12},{9,... | collective-permute-start | bytes 688136 | tf_op jit(solution)/shard_map/ppermute | solution.py:69
  39.2 12.6 %collective-permute-start.14 = (bf16[2,2,4,32,896]{4,3,2,1,0:T(8,128)(2,1)S(1)}, bf16[2,2,4,32,896]{4,3,2,1,0:T(8,128)(2,1)S(1)}, u32[]{:S(2)}, u32[]{:S(2)}) collective-permute-start(bf16[2,2,4,32,896]{4,3,2,1,0:T(8,128)(2,1)S(1)} %get-tuple-element.64.refs_1_), channel_id=1, source_target_pairs={{0,96},{1,97},{2,98},{3,99},{4,100},{5,101},{6,102},{7,103},{8,14}... | collective-permute-start | bytes 2752520 | tf_op jit(solution)/shard_map/ppermute | solution.py:69
  41.2 13.8 %collective-permute-start.12 = (bf16[2,2,4,32,896]{4,3,2,1,0:T(8,128)(2,1)S(1)}, bf16[2,2,4,32,896]{4,3,2,1,0:T(8,128)(2,1)S(1)}, u32[]{:S(2)}, u32[]{:S(2)}) collective-permute-start(bf16[2,2,4,32,896]{4,3,2,1,0:T(8,128)(2,1)S(1)} %get-tuple-element.65.refs_0_), channel_id=1, source_target_pairs={{0,32},{1,33},{2,34},{3,35},{4,36},{5,37},{6,38},{7,39},{8,10},{9,... | collective-permute-start | bytes 2752520 | tf_op jit(solution)/shard_map/ppermute | solution.py:69
  41.2 19.8 %collective-permute-start.15 = (bf16[2,4,4,16,896]{4,3,2,1,0:T(8,128)(2,1)S(1)}, bf16[2,4,4,16,896]{4,3,2,1,0:T(8,128)(2,1)S(1)}, u32[]{:S(2)}, u32[]{:S(2)}) collective-permute-start(bf16[2,4,4,16,896]{4,3,2,1,0:T(8,128)(2,1)S(1)} %bitcast_dynamic-update-slice_fusion.3.refs_2_), channel_id=1, source_target_pairs={{0,1},{1,16},{2,3},{3,18},{4,5},{5,20},{6,7},{7,22},{8,25},{9,8},{... | collective-permute-start | bytes 2752520 | tf_op jit(solution)/shard_map/ppermute | solution.py:69
  44.1 23.4 %collective-permute-start.17 = (bf16[2,4,4,16,896]{4,3,2,1,0:T(8,128)(2,1)S(1)}, bf16[2,4,4,16,896]{4,3,2,1,0:T(8,128)(2,1)S(1)}, u32[]{:S(2)}, u32[]{:S(2)}) collective-permute-start(bf16[2,4,4,16,896]{4,3,2,1,0:T(8,128)(2,1)S(1)} %bitcast_dynamic-update-slice_fusion.3.refs_2_), channel_id=1, source_target_pairs={{0,17},{1,0},{2,19},{3,2},{4,21},{5,4},{6,23},{7,6},{8,9},{9,24},{... | collective-permute-start | bytes 2752520 | tf_op jit(solution)/shard_map/ppermute | solution.py:69
  51.8 17.4 %collective-permute-start.20 = (bf16[2,2,4,32,896]{4,3,2,1,0:T(8,128)(2,1)S(1)}, bf16[2,2,4,32,896]{4,3,2,1,0:T(8,128)(2,1)S(1)}, u32[]{:S(2)}, u32[]{:S(2)}) collective-permute-start(bf16[2,2,4,32,896]{4,3,2,1,0:T(8,128)(2,1)S(1)} %get-tuple-element.65.refs_0_), channel_id=1, source_target_pairs={{0,96},{1,97},{2,98},{3,99},{4,100},{5,101},{6,102},{7,103},{8,14}... | collective-permute-start | bytes 2752520 | tf_op jit(solution)/shard_map/ppermute | solution.py:69
  55.0 14.2 %collective-permute-start.19 = (bf16[2,2,4,32,896]{4,3,2,1,0:T(8,128)(2,1)S(1)}, bf16[2,2,4,32,896]{4,3,2,1,0:T(8,128)(2,1)S(1)}, u32[]{:S(2)}, u32[]{:S(2)}) collective-permute-start(bf16[2,2,4,32,896]{4,3,2,1,0:T(8,128)(2,1)S(1)} %get-tuple-element.64.refs_1_), channel_id=1, source_target_pairs={{0,32},{1,33},{2,34},{3,35},{4,36},{5,37},{6,38},{7,39},{8,10},{9,... | collective-permute-start | bytes 2752520 | tf_op jit(solution)/shard_map/ppermute | solution.py:69
  67.5 12.5 %collective-permute-start.18 = (bf16[2,4,4,16,896]{4,3,2,1,0:T(8,128)(2,1)S(1)}, bf16[2,4,4,16,896]{4,3,2,1,0:T(8,128)(2,1)S(1)}, u32[]{:S(2)}, u32[]{:S(2)}) collective-permute-start(bf16[2,4,4,16,896]{4,3,2,1,0:T(8,128)(2,1)S(1)} %collective-permute-done.15.refs_5_), channel_id=1, source_target_pairs={{0,1},{1,16},{2,3},{3,18},{4,5},{5,20},{6,7},{7,22},{8,25},{9,8},{... | collective-permute-start | bytes 2752520 | tf_op jit(solution)/shard_map/ppermute | solution.py:69
  67.5 12.5 %collective-permute-start.16 = (bf16[2,2,4,32,896]{4,3,2,1,0:T(8,128)(2,1)S(1)}, bf16[2,2,4,32,896]{4,3,2,1,0:T(8,128)(2,1)S(1)}, u32[]{:S(2)}, u32[]{:S(2)}) collective-permute-start(bf16[2,2,4,32,896]{4,3,2,1,0:T(8,128)(2,1)S(1)} %collective-permute-done.14.refs_7_), channel_id=1, source_target_pairs={{0,96},{1,97},{2,98},{3,99},{4,100},{5,101},{6,102},{7,103},{8,14}... | collective-permute-start | bytes 2752520 | tf_op jit(solution)/shard_map/ppermute | solution.py:69
  69.2 13.8 %collective-permute-start.13 = (bf16[2,2,4,32,896]{4,3,2,1,0:T(8,128)(2,1)S(1)}, bf16[2,2,4,32,896]{4,3,2,1,0:T(8,128)(2,1)S(1)}, u32[]{:S(2)}, u32[]{:S(2)}) collective-permute-start(bf16[2,2,4,32,896]{4,3,2,1,0:T(8,128)(2,1)S(1)} %collective-permute-done.12.refs_3_), channel_id=1, source_target_pairs={{0,32},{1,33},{2,34},{3,35},{4,36},{5,37},{6,38},{7,39},{8,10},{9,... | collective-permute-start | bytes 2752520 | tf_op jit(solution)/shard_map/ppermute | solution.py:69
  84.7 5.9 %collective-permute-start.21 = (bf16[768,896]{1,0:T(8,128)(2,1)S(1)}, bf16[768,896]{1,0:T(8,128)(2,1)S(1)}, u32[]{:S(2)}, u32[]{:S(2)}) collective-permute-start(bf16[768,896]{1,0:T(8,128)(2,1)S(1)} %bitcast.70), channel_id=1, source_target_pairs={{0,8},{1,9},{2,10},{3,11},{4,12},{5,13},{6,14},{7,15},{8,0},{9,1},... | collective-permute-start | bytes 4128776 | tf_op jit(solution)/shard_map/ppermute | solution.py:69
  90.6 2.1 copy-start.1
  90.6 3.2 %copy-start = (bf16[1,96,128,128]{3,2,1,0:T(8,128)(2,1)S(1)}, bf16[1,96,128,128]{3,2,1,0:T(8,128)(2,1)}, u32[]{:S(2)}) copy-start(bf16[1,96,128,128]{3,2,1,0:T(8,128)(2,1)} %param.6) | copy-start | bytes 9437188
  92.6 15.1 %collective-permute-start.22 = (bf16[416,896]{1,0:T(8,128)(2,1)S(1)}, bf16[416,896]{1,0:T(8,128)(2,1)S(1)}, u32[]{:S(2)}, u32[]{:S(2)}) collective-permute-start(bf16[416,896]{1,0:T(8,128)(2,1)S(1)} %get-tuple-element.72), channel_id=1, source_target_pairs={{0,1},{1,0},{2,3},{3,2},{4,5},{5,4},{6,7},{7,6},{8,9},{9,8},{10,11... | collective-permute-start | bytes 2236424 | tf_op jit(solution)/shard_map/ppermute | solution.py:69
  100.0 1.8 copy-start.2
  101.9 11.9 %collective-permute-start.30 = (bf16[208,896]{1,0:T(8,128)(2,1)S(1)}, bf16[208,896]{1,0:T(8,128)(2,1)S(1)}, u32[]{:S(2)}, u32[]{:S(2)}) collective-permute-start(bf16[208,896]{1,0:T(8,128)(2,1)S(1)} %get-tuple-element.78), channel_id=1, source_target_pairs={{0,2},{1,3},{2,4},{3,5},{4,6},{5,7},{6,0},{7,1},{8,14},{9,15},{10,... | collective-permute-start | bytes 1118216 | tf_op jit(solution)/shard_map/ppermute | solution.py:69
  102.0 20.0 %collective-permute-start.31 = (bf16[208,896]{1,0:T(8,128)(2,1)S(1)}, bf16[208,896]{1,0:T(8,128)(2,1)S(1)}, u32[]{:S(2)}, u32[]{:S(2)}) collective-permute-start(bf16[208,896]{1,0:T(8,128)(2,1)S(1)} %get-tuple-element.79), channel_id=1, source_target_pairs={{0,6},{1,7},{2,0},{3,1},{4,2},{5,3},{6,4},{7,5},{8,10},{9,11},{10,... | collective-permute-start | bytes 1118216 | tf_op jit(solution)/shard_map/ppermute | solution.py:69
  103.4 18.5 %collective-permute-start.32 = (bf16[208,896]{1,0:T(8,128)(2,1)S(1)}, bf16[208,896]{1,0:T(8,128)(2,1)S(1)}, u32[]{:S(2)}, u32[]{:S(2)}) collective-permute-start(bf16[208,896]{1,0:T(8,128)(2,1)S(1)} %get-tuple-element.80), channel_id=1, source_target_pairs={{0,4},{1,5},{2,6},{3,7},{4,0},{5,1},{6,2},{7,3},{8,12},{9,13},{10,... | collective-permute-start | bytes 1118216 | tf_op jit(solution)/shard_map/ppermute | solution.py:69
  108.0 16.3 %collective-permute-start.23 = (bf16[104,896]{1,0:T(8,128)(2,1)S(1)}, bf16[104,896]{1,0:T(8,128)(2,1)S(1)}, u32[]{:S(2)}, u32[]{:S(2)}) collective-permute-start(bf16[104,896]{1,0:T(8,128)(2,1)S(1)} %get-tuple-element.74), channel_id=1, source_target_pairs={{0,2},{1,3},{2,4},{3,5},{4,6},{5,7},{6,0},{7,1},{8,14},{9,15},{10,... | collective-permute-start | bytes 559112 | tf_op jit(solution)/shard_map/ppermute | solution.py:69
  113.8 15.5 %collective-permute-start.24 = (bf16[104,896]{1,0:T(8,128)(2,1)S(1)}, bf16[104,896]{1,0:T(8,128)(2,1)S(1)}, u32[]{:S(2)}, u32[]{:S(2)}) collective-permute-start(bf16[104,896]{1,0:T(8,128)(2,1)S(1)} %get-tuple-element.75), channel_id=1, source_target_pairs={{0,6},{1,7},{2,0},{3,1},{4,2},{5,3},{6,4},{7,5},{8,10},{9,11},{10,... | collective-permute-start | bytes 559112 | tf_op jit(solution)/shard_map/ppermute | solution.py:69
  113.8 15.5 %collective-permute-start.25 = (bf16[104,896]{1,0:T(8,128)(2,1)S(1)}, bf16[104,896]{1,0:T(8,128)(2,1)S(1)}, u32[]{:S(2)}, u32[]{:S(2)}) collective-permute-start(bf16[104,896]{1,0:T(8,128)(2,1)S(1)} %get-tuple-element.76), channel_id=1, source_target_pairs={{0,4},{1,5},{2,6},{3,7},{4,0},{5,1},{6,2},{7,3},{8,12},{9,13},{10,... | collective-permute-start | bytes 559112 | tf_op jit(solution)/shard_map/ppermute | solution.py:69
  124.6 4.7 %collective-permute-start.33 = (bf16[104,896]{1,0:T(8,128)(2,1)S(1)}, bf16[104,896]{1,0:T(8,128)(2,1)S(1)}, u32[]{:S(2)}, u32[]{:S(2)}) collective-permute-start(bf16[104,896]{1,0:T(8,128)(2,1)S(1)} %get-tuple-element.86), channel_id=1, source_target_pairs={{0,1},{1,0},{2,3},{3,2},{4,5},{5,4},{6,7},{7,6},{8,9},{9,8},{10,11... | collective-permute-start | bytes 559112 | tf_op jit(solution)/shard_map/ppermute | solution.py:69
  129.6 7.5 %collective-permute-start.26 = (bf16[104,896]{1,0:T(8,128)(2,1)S(1)}, bf16[104,896]{1,0:T(8,128)(2,1)S(1)}, u32[]{:S(2)}, u32[]{:S(2)}) collective-permute-start(bf16[104,896]{1,0:T(8,128)(2,1)S(1)} %get-tuple-element.112), channel_id=1, source_target_pairs={{0,8},{1,9},{2,10},{3,11},{4,12},{5,13},{6,14},{7,15},{8,0},{9,1},... | collective-permute-start | bytes 559112 | tf_op jit(solution)/shard_map/ppermute | solution.py:69
  136.0 1.4 collective-permute-start.34
  137.7 6.1 %collective-permute-start.35 = (bf16[104,896]{1,0:T(8,128)(2,1)S(1)}, bf16[104,896]{1,0:T(8,128)(2,1)S(1)}, u32[]{:S(2)}, u32[]{:S(2)}) collective-permute-start(bf16[104,896]{1,0:T(8,128)(2,1)S(1)} %get-tuple-element.98), channel_id=1, source_target_pairs={{0,1},{1,0},{2,3},{3,2},{4,5},{5,4},{6,7},{7,6},{8,9},{9,8},{10,11... | collective-permute-start | bytes 559112 | tf_op jit(solution)/shard_map/ppermute | solution.py:69
  137.8 6.0 %collective-permute-start.27 = (bf16[104,896]{1,0:T(8,128)(2,1)S(1)}, bf16[104,896]{1,0:T(8,128)(2,1)S(1)}, u32[]{:S(2)}, u32[]{:S(2)}) collective-permute-start(bf16[104,896]{1,0:T(8,128)(2,1)S(1)} %get-tuple-element.110), channel_id=1, source_target_pairs={{0,2},{1,3},{2,4},{3,5},{4,6},{5,7},{6,0},{7,1},{8,14},{9,15},{10,... | collective-permute-start | bytes 559112 | tf_op jit(solution)/shard_map/ppermute | solution.py:69
  138.6 11.9 %collective-permute-start.28 = (bf16[104,896]{1,0:T(8,128)(2,1)S(1)}, bf16[104,896]{1,0:T(8,128)(2,1)S(1)}, u32[]{:S(2)}, u32[]{:S(2)}) collective-permute-start(bf16[104,896]{1,0:T(8,128)(2,1)S(1)} %get-tuple-element.110), channel_id=1, source_target_pairs={{0,6},{1,7},{2,0},{3,1},{4,2},{5,3},{6,4},{7,5},{8,10},{9,11},{10,... | collective-permute-start | bytes 559112 | tf_op jit(solution)/shard_map/ppermute | solution.py:69
  139.3 11.2 %collective-permute-start.29 = (bf16[104,896]{1,0:T(8,128)(2,1)S(1)}, bf16[104,896]{1,0:T(8,128)(2,1)S(1)}, u32[]{:S(2)}, u32[]{:S(2)}) collective-permute-start(bf16[104,896]{1,0:T(8,128)(2,1)S(1)} %get-tuple-element.110), channel_id=1, source_target_pairs={{0,4},{1,5},{2,6},{3,7},{4,0},{5,1},{6,2},{7,3},{8,12},{9,13},{10,... | collective-permute-start | bytes 559112 | tf_op jit(solution)/shard_map/ppermute | solution.py:69
  150.6 18.1 %collective-permute-start.36 = (bf16[416,896]{1,0:T(8,128)(2,1)S(1)}, bf16[416,896]{1,0:T(8,128)(2,1)S(1)}, u32[]{:S(2)}, u32[]{:S(2)}) collective-permute-start(bf16[416,896]{1,0:T(8,128)(2,1)S(1)} %constant_dynamic-update-slice_fusion.6.refs_2_), channel_id=1, source_target_pairs={{0,1},{1,0},{2,3},{3,2},{4,5},{5,4},{6,7},{7,6},{8,9},{9,8},{10,11... | collective-permute-start | bytes 2236424 | tf_op jit(solution)/shard_map/ppermute | solution.py:69
  150.7 9.4 %collective-permute-start.37 = (bf16[208,896]{1,0:T(8,128)(2,1)S(1)}, bf16[208,896]{1,0:T(8,128)(2,1)S(1)}, u32[]{:S(2)}, u32[]{:S(2)}) collective-permute-start(bf16[208,896]{1,0:T(8,128)(2,1)S(1)} %constant_dynamic-update-slice_fusion.4.refs_4_), channel_id=1, source_target_pairs={{0,2},{1,3},{2,4},{3,5},{4,6},{5,7},{6,0},{7,1},{8,14},{9,15},{10,... | collective-permute-start | bytes 1118216 | tf_op jit(solution)/shard_map/ppermute | solution.py:69
  151.5 12.8 %collective-permute-start.38 = (bf16[208,896]{1,0:T(8,128)(2,1)S(1)}, bf16[208,896]{1,0:T(8,128)(2,1)S(1)}, u32[]{:S(2)}, u32[]{:S(2)}) collective-permute-start(bf16[208,896]{1,0:T(8,128)(2,1)S(1)} %constant_dynamic-update-slice_fusion.4.refs_4_), channel_id=1, source_target_pairs={{0,6},{1,7},{2,0},{3,1},{4,2},{5,3},{6,4},{7,5},{8,10},{9,11},{10,... | collective-permute-start | bytes 1118216 | tf_op jit(solution)/shard_map/ppermute | solution.py:69
  152.4 16.3 %collective-permute-start.39 = (bf16[208,896]{1,0:T(8,128)(2,1)S(1)}, bf16[208,896]{1,0:T(8,128)(2,1)S(1)}, u32[]{:S(2)}, u32[]{:S(2)}) collective-permute-start(bf16[208,896]{1,0:T(8,128)(2,1)S(1)} %constant_dynamic-update-slice_fusion.4.refs_4_), channel_id=1, source_target_pairs={{0,4},{1,5},{2,6},{3,7},{4,0},{5,1},{6,2},{7,3},{8,12},{9,13},{10,... | collective-permute-start | bytes 1118216 | tf_op jit(solution)/shard_map/ppermute | solution.py:69
  174.4 5.8 %collective-permute-start.40 = (f32[416,768]{1,0:T(8,128)S(1)}, f32[416,768]{1,0:T(8,128)S(1)}, u32[]{:S(2)}, u32[]{:S(2)}) collective-permute-start(f32[416,768]{1,0:T(8,128)S(1)} %get-tuple-element.90), channel_id=1, source_target_pairs={{0,8},{1,9},{2,10},{3,11},{4,12},{5,13},{6,14},{7,15},{8,0},{9,1},... | collective-permute-start | bytes 3833864 | tf_op jit(solution)/shard_map/ppermute | solution.py:69
  180.4 5.3 %collective-permute-start.41 = (bf16[104,768]{1,0:T(8,128)(2,1)S(1)}, bf16[104,768]{1,0:T(8,128)(2,1)S(1)}, u32[]{:S(2)}, u32[]{:S(2)}) collective-permute-start(bf16[104,768]{1,0:T(8,128)(2,1)S(1)} %get-tuple-element.92), channel_id=1, source_target_pairs={{0,32},{1,33},{2,34},{3,35},{4,36},{5,37},{6,38},{7,39},{8,104},{9... | collective-permute-start | bytes 479240 | tf_op jit(solution)/shard_map/ppermute | solution.py:69
  180.5 10.1 %collective-permute-start.42 = (bf16[104,768]{1,0:T(8,128)(2,1)S(1)}, bf16[104,768]{1,0:T(8,128)(2,1)S(1)}, u32[]{:S(2)}, u32[]{:S(2)}) collective-permute-start(bf16[104,768]{1,0:T(8,128)(2,1)S(1)} %get-tuple-element.93), channel_id=1, source_target_pairs={{0,96},{1,97},{2,98},{3,99},{4,100},{5,101},{6,102},{7,103},{8,40}... | collective-permute-start | bytes 479240 | tf_op jit(solution)/shard_map/ppermute | solution.py:69
  182.0 8.7 %collective-permute-start.43 = (bf16[104,768]{1,0:T(8,128)(2,1)S(1)}, bf16[104,768]{1,0:T(8,128)(2,1)S(1)}, u32[]{:S(2)}, u32[]{:S(2)}) collective-permute-start(bf16[104,768]{1,0:T(8,128)(2,1)S(1)} %get-tuple-element.94), channel_id=1, source_target_pairs={{0,64},{1,65},{2,66},{3,67},{4,68},{5,69},{6,70},{7,71},{8,72},{9,... | collective-permute-start | bytes 479240 | tf_op jit(solution)/shard_map/ppermute | solution.py:69
  190.7 10.5 %collective-permute-start.44 = (f32[104,768]{1,0:T(8,128)S(1)}, f32[104,768]{1,0:T(8,128)S(1)}, u32[]{:S(2)}, u32[]{:S(2)}) collective-permute-start(f32[104,768]{1,0:T(8,128)S(1)} %add_add_fusion), channel_id=1, source_target_pairs={{0,16},{1,17},{2,18},{3,19},{4,20},{5,21},{6,22},{7,23},{8,24},{9,... | collective-permute-start | bytes 958472 | tf_op jit(solution)/shard_map/ppermute | solution.py:69
  201.3 4.2 %collective-permute-start.45 = (bf16[104,768]{1,0:T(8,128)(2,1)S(1)}, bf16[104,768]{1,0:T(8,128)(2,1)S(1)}, u32[]{:S(2)}, u32[]{:S(2)}) collective-permute-start(bf16[104,768]{1,0:T(8,128)(2,1)S(1)} %get-tuple-element.96), channel_id=1, source_target_pairs={{0,32},{1,33},{2,34},{3,35},{4,36},{5,37},{6,38},{7,39},{8,104},{9... | collective-permute-start | bytes 479240 | tf_op jit(solution)/shard_map/ppermute | solution.py:69
  201.4 5.4 %collective-permute-start.46 = (bf16[104,768]{1,0:T(8,128)(2,1)S(1)}, bf16[104,768]{1,0:T(8,128)(2,1)S(1)}, u32[]{:S(2)}, u32[]{:S(2)}) collective-permute-start(bf16[104,768]{1,0:T(8,128)(2,1)S(1)} %get-tuple-element.96), channel_id=1, source_target_pairs={{0,96},{1,97},{2,98},{3,99},{4,100},{5,101},{6,102},{7,103},{8,40}... | collective-permute-start | bytes 479240 | tf_op jit(solution)/shard_map/ppermute | solution.py:69
  202.8 8.9 %collective-permute-start.47 = (bf16[104,768]{1,0:T(8,128)(2,1)S(1)}, bf16[104,768]{1,0:T(8,128)(2,1)S(1)}, u32[]{:S(2)}, u32[]{:S(2)}) collective-permute-start(bf16[104,768]{1,0:T(8,128)(2,1)S(1)} %get-tuple-element.96), channel_id=1, source_target_pairs={{0,64},{1,65},{2,66},{3,67},{4,68},{5,69},{6,70},{7,71},{8,72},{9,... | collective-permute-start | bytes 479240 | tf_op jit(solution)/shard_map/ppermute | solution.py:69
  211.7 3.6 %collective-permute-start.48 = (bf16[416,768]{1,0:T(8,128)(2,1)S(1)}, bf16[416,768]{1,0:T(8,128)(2,1)S(1)}, u32[]{:S(2)}, u32[]{:S(2)}) collective-permute-start(bf16[416,768]{1,0:T(8,128)(2,1)S(1)} %constant_dynamic-update-slice_fusion.own), channel_id=1, source_target_pairs={{0,8},{1,9},{2,10},{3,11},{4,12},{5,13},{6,14},{7,15},{8,0},{9,1},... | collective-permute-start | bytes 1916936 | tf_op jit(solution)/shard_map/ppermute | solution.py:69
